TPU v7x, 32 devices: a whole 2x2x4 slice. The times are simulated.
32 devices in a mesh: row: 4 (over z), col: 8 (over y, x, core).
Axes of the slice: x: 2, y: 2, z: 4, core: 2. Of those that a mesh axis runs over, the one named last changes fastest.
Arguments:
- current_block: float32 [48, 65536], P(None, ('row', 'col')), may hold values from -12 to 12, as said below
- previous_block: float32 [48, 65536], P(None, ('row', 'col')), may hold values from -12 to 12
- previous_coupling: float32 [48, 48], replicated, may hold values from -0.875 to 0.875
- stored_blocks: float32 [8, 48, 65536], P(None, None, ('row', 'col')), may hold values from -12 to 12
- stiffness_diag: float32 [65536], P(('row', 'col')), may hold values from 1 to 10
- lumped_mass: float32 [65536], P(('row', 'col')), may hold values from 0.25 to 24
- tile_values: bfloat16 [16384, 128, 128], P(('row', 'col')), may hold values from -0.14941406 to 0.14941406
- tile_rows: int32 [16384], P(('row', 'col')), may hold values from 0 to 63, as said below
- tile_cols: int32 [16384], P(('row', 'col')), may hold values from 0 to 127
- tile_counts: int32 [32], P(('row', 'col')), may hold values from 128 to 512, as said below
Outputs:
- residual_block: float32 [48, 65536], P(None, ('row', 'col'))
- coefficients: float32 [9, 48, 48], replicated
- gram: float32 [48, 48], replicated
Inputs may be any that keep to these rules, and one draw needn't show every extreme that they name: `current_block`: each entry shares a part with the same entry of the other Lanczos blocks. `tile_rows`: some local output tile rows hold far more tiles than others. `tile_counts`: exactly one device has all 512 slots occupied.
All inputs are finite; a program needn't handle non-finite values.
Results may differ from a plain program's by a relative error of at most 0.0044.
Values may be sent and summed in bfloat16 or wider, within the bound.
No kernel may reach another device: no remote copies, remote signals or barrier semaphores. Data moves between devices by JAX's collectives and lax.ppermute only.
A program may use at most 128 MiB of HBM per device.

v0:
```python
import jax
import jax.numpy as jnp
from jax import lax
from jax.sharding import PartitionSpec as P


def local(
    current_block,
    previous_block,
    previous_coupling,
    stored_blocks,
    stiffness_diag,
    lumped_mass,
    tile_values,
    tile_rows,
    tile_cols,
    tile_counts,
):
    row_devs = lax.axis_size("row")
    col_devs = lax.axis_size("col")
    width, slab_len = current_block.shape
    tile_len = tile_values.shape[1]
    slab_tiles = slab_len // tile_len
    slot_total = tile_values.shape[0]
    cells_total = slab_len * row_devs * col_devs
    rounded = current_block.astype(jnp.bfloat16)
    gathered = lax.all_gather(rounded, "col", axis=1, tiled=True)
    panels = gathered.reshape(width, col_devs * slab_tiles, tile_len)
    picked = jnp.take(panels, tile_cols, axis=1)
    products = jnp.einsum("btj,tij->tbi", picked, tile_values, preferred_element_type=jnp.float32)
    occupied = jnp.arange(slot_total, dtype=jnp.int32) < tile_counts[0]
    targets = jnp.arange(row_devs * slab_tiles, dtype=jnp.int32)
    selector = ((tile_rows[None, :] == targets[:, None]) & occupied[None, :]).astype(jnp.float32)
    selector = selector.reshape(row_devs, slab_tiles, slot_total)
    owners = selector.shape[0]
    summed_tiles = jnp.einsum("rst,tbi->rbsi", selector, products, precision=lax.Precision.HIGHEST)
    received = lax.psum_scatter(
        summed_tiles.reshape(owners, width, slab_len).astype(jnp.bfloat16),
        "row",
        scatter_dimension=0,
        tiled=True,
    ).astype(jnp.float32)
    product = received[0] + stiffness_diag[None, :] * current_block
    recurrence = product - jnp.dot(
        previous_coupling,
        previous_block,
        precision=lax.Precision.HIGHEST,
        preferred_element_type=jnp.float32,
    )
    basis = jnp.concatenate([current_block[None], stored_blocks], axis=0)
    weighted = recurrence * lumped_mass[None, :] / cells_total
    local_coef = jnp.einsum("kpi,qi->kpq", basis, weighted, precision=lax.Precision.HIGHEST)
    coefficients = lax.psum(local_coef, ("row", "col"))
    residual_block = recurrence - jnp.einsum(
        "kpq,kpi->qi", coefficients, basis, precision=lax.Precision.HIGHEST
    )
    local_gram = jnp.einsum(
        "qi,pi->qp",
        residual_block * lumped_mass[None, :] / cells_total,
        residual_block,
        precision=lax.Precision.HIGHEST,
    )
    gram = lax.psum(local_gram, ("row", "col"))
    return (residual_block, coefficients, gram)


def solution(mesh):
    return jax.shard_map(
        local,
        mesh=mesh,
        in_specs=(
            P(None, ("row", "col")),
            P(None, ("row", "col")),
            P(),
            P(None, None, ("row", "col")),
            P(("row", "col")),
            P(("row", "col")),
            P(("row", "col"), None, None),
            P(("row", "col")),
            P(("row", "col")),
            P(("row", "col")),
        ),
        out_specs=(P(None, ("row", "col")), P(), P()),
        check_vma=False,
    )
```

profile of v0, /device:TPU:0, one launch (start us, length us, event | category | flops | bytes accessed | tf_op | source)
XLA Modules:
  0.0 289.9 jit_solution(13317804184496933052)
XLA Ops:
  7.2 0.0 copy-start
  7.2 0.0 all-gather.2.cloned.1.call-start
  7.2 1.7 convert_element_type.14
  9.0 0.0 all-gather.2.cloned.1.call-update
  9.0 0.0 reduce-scatter.2.cloned.1.call-start
  9.7 0.7 compare_select_fusion
  10.4 0.7 compare_and_fusion
  11.1 27.8 %all-gather.2.cloned.1.call-done = bf16[48,16384]{1,0:T(8,128)(2,1)} async-done(((bf16[48,2048]{1,0:T(8,128)(2,1)}), bf16[48,16384]{1,0:T(8,128)(2,1)}) %all-gather.2.cloned.1.call-update) | async-done | bytes 1572880 | tf_op jit(solution)/shard_map/all_gather | solution.py:27
  38.9 1.7 copy_bitcast_fusion
  40.6 4.2 %gather_fusion = bf16[512,48,128]{2,1,0:T(8,128)(2,1)} fusion(bf16[48,128,128]{2,0,1:T(8,128)(2,1)S(1)} %copy_bitcast_fusion, s32[1024]{0:T(1024)S(1)} %pad_clamp_fusion), kind=kCustom, calls=%fused_computation | custom fusion | bytes 12584960 | tf_op jit(solution)/shard_map/jit(_take)/gather | solution.py:29
  44.8 0.0 copy-start.6
  44.8 18.9 %fusion.6 = f32[512,48,128,1]{2,1,0,3:T(8,128)} fusion(bf16[512,128,128]{2,1,0:T(8,128)(2,1)} %param.16, bf16[512,48,128]{2,1,0:T(8,128)(2,1)} %gather_fusion, pred[512]{0:T(512)(128)(4,1)S(1)} %compare_and_fusion), kind=kOutput, calls=%fused_computation.7 | convolution fusion | flops 808452096 | bytes 35652096 | tf_op jit(solution)/shard_map/btj,tij->tbi/dot_general | solution.py:30
  63.7 0.0 copy-done.6
  63.7 13.7 %fusion.17 = bf16[4,48,16,128]{3,2,0,1:T(8,128)(2,1)} fusion(f32[512,48,128,1]{2,1,0,3:T(8,128)} %fusion.6, s32[4,16]{1,0:T(4,128)S(1)} %multiply_add_fusion, s32[512]{0:T(512)S(1)} %copy-done.6, pred[512]{0:T(512)(128)(4,1)S(1)} %iota_compare_fusion), kind=kOutput, calls=%fused_computation.17 | convolution fusion | flops 2416377856 | bytes 13372160 | tf_op jit(solution)/shard_map/rst,tbi->rbsi/dot_general | solution.py:36
  77.4 0.0 copy-start.5
  77.4 0.0 copy-start.1
  77.4 0.0 copy-start.4
  77.4 2.6 convert_element_type.17
  80.0 2.5 copy.19
  82.5 0.0 reduce-scatter.2.cloned.1.call-update
  82.5 0.2 all-reduce.2.cloned.1.call-start
  82.7 23.2 %reduce-scatter.2.cloned.1.call-done = bf16[1,48,2048]{2,1,0:T(8,128)(2,1)} async-done(((bf16[4,48,2048]{2,1,0:T(8,128)(2,1)}), bf16[1,48,2048]{2,1,0:T(8,128)(2,1)}) %reduce-scatter.2.cloned.1.call-update) | async-done | bytes 196624 | tf_op jit(solution)/shard_map/reduce_scatter | solution.py:37
  105.9 0.0 copy-done
  105.9 0.0 copy-done.5
  105.9 1.5 convolution_subtract_fusion
  107.5 0.0 copy-start.3
  107.5 0.7 copy-done.3
  108.2 0.0 copy-done.1
  108.2 0.0 copy-done.4
  108.2 4.6 %fusion.11 = f32[9,48,48]{2,1,0:T(8,128)} fusion(f32[8,48,2048]{2,1,0:T(8,128)S(1)} %copy-done.1, f32[1,48,2048]{2,1,0:T(8,128)} %bitcast.39, f32[48,2048]{1,0:T(8,128)S(1)} %convolution_subtract_fusion, f32[2048]{0:T(1024)S(1)} %copy-done.4), kind=kOutput, calls=%fused_computation.11 | convolution fusion | flops 510689280 | bytes 4023296 | tf_op jit(solution)/shard_map/kpi,qi->kpq/dot_general | solution.py:52
  112.8 0.0 all-reduce.2.cloned.1.call-update
  112.8 122.4 %all-reduce.2.cloned.1.call-done = f32[9,48,48]{2,1,0:T(8,128)} async-done(((f32[9,48,48]{2,1,0:T(8,128)}), f32[9,48,48]{2,1,0:T(8,128)}) %all-reduce.2.cloned.1.call-update) | async-done | bytes 82960 | tf_op jit(solution)/shard_map/psum | solution.py:53
  235.3 3.5 %fusion.13 = f32[48,2048]{1,0:T(8,128)S(1)} fusion(f32[48,2048]{1,0:T(8,128)} %copy-done.3, f32[9,48,48]{2,1,0:T(8,128)} %all-reduce.2.cloned.1.call-done, f32[8,48,2048]{2,1,0:T(8,128)S(1)} %copy-done.1, f32[1,48,2048]{2,1,0:T(8,128)} %bitcast.40), kind=kOutput, calls=%fused_computation.14 | convolution fusion | flops 510590976 | bytes 4408320 | tf_op jit(solution)/shard_map/kpq,kpi->qi/dot_general | solution.py:54
  238.8 0.0 copy-start.2
  238.8 0.7 copy-done.2
  239.5 0.5 fusion.21
  240.0 41.7 %psum.15 = f32[48,48]{1,0:T(8,128)} all-reduce(f32[48,48]{1,0:T(8,128)S(1)} %fusion.21), channel_id=1, replica_groups=mesh['row'=4,'col'=8] {'row','col'}, use_global_device_ids=true, to_apply=%region_2.3 | all-reduce | flops 2304 | bytes 18432 | tf_op jit(solution)/shard_map/psum | solution.py:63
  281.7 1.6 copy.35
  (3 shorter events, 0.0 us)
Async XLA Ops:
  7.2 98.8 %copy-start = (f32[48,2048]{1,0:T(8,128)S(1)}, f32[48,2048]{1,0:T(8,128)}, u32[]{:S(2)}) copy-start(f32[48,2048]{1,0:T(8,128)} %param.11) | copy-start | bytes 1179652
  7.2 31.7 %all-gather.2.cloned.1.call-start = ((), (), s32[]{:S(2)}) async-start(), calls=%async_computation.1 | async-start | bytes 1769472 | tf_op jit(solution)/shard_map/all_gather | solution.py:27
  9.0 97.0 %reduce-scatter.2.cloned.1.call-start = ((), (), s32[]{:S(2)}) async-start(), calls=%async_computation.2 | async-start | bytes 983040 | tf_op jit(solution)/shard_map/reduce_scatter | solution.py:37
  44.8 19.0 %copy-start.6 = (s32[512]{0:T(512)S(1)}, s32[512]{0:T(512)}, u32[]{:S(2)}) copy-start(s32[512]{0:T(512)} %param.17) | copy-start | bytes 6148
  77.4 28.5 %copy-start.5 = (f32[2048]{0:T(1024)S(1)}, f32[2048]{0:T(1024)}, u32[]{:S(2)}) copy-start(f32[2048]{0:T(1024)} %param.14) | copy-start | bytes 24580
  77.4 30.8 %copy-start.1 = (f32[8,48,2048]{2,1,0:T(8,128)S(1)}, f32[8,48,2048]{2,1,0:T(8,128)}, u32[]{:S(2)}) copy-start(f32[8,48,2048]{2,1,0:T(8,128)} %param.13) | copy-start | bytes 9437188
  77.4 30.8 %copy-start.4 = (f32[2048]{0:T(1024)S(1)}, f32[2048]{0:T(1024)}, u32[]{:S(2)}) copy-start(f32[2048]{0:T(1024)} %param.15) | copy-start | bytes 24580
  82.5 152.8 %all-reduce.2.cloned.1.call-start = ((), (), s32[]{:S(2)}) async-start(), calls=%async_computation.3 | async-start | bytes 442368 | tf_op jit(solution)/shard_map/psum | solution.py:53
  107.5 0.7 copy-start.3
  238.8 0.7 copy-start.2
Sparse Core Ops, SparseCore 0:
  10.5 28.3 all-gather.1
  82.6 23.2 reduce-scatter.1
  113.0 122.2 all-reduce.1
where the time goes:
time: 290 us
  waiting for transfers between devices  174 us (60%)
  matrix products  42.7 us (15%)
  blocking collectives  41.7 us (14%)
  between operations  14.5 us (5%)
  local copies, waits for them, and re-layouts  14.1 us (5%)
  other arithmetic  3.13 us (1%)
    psum x1, waiting for transfers between devices, local(): coefficients = lax.psum(local_coef, ('row', 'col'))  122 us
    psum x1, blocking collectives, local(): gram = lax.psum(local_gram, ('row', 'col'))  41.7 us
    all_gather x1, waiting for transfers between devices, local(): gathered = lax.all_gather(rounded, 'col', axis=1, tiled=True)  27.8 us
    reduce_scatter x1, waiting for transfers between devices, local(): lax.psum_scatter(summed_tiles.reshape(owners, width, slab_len).astype(jnp...  23.2 us
    dot_general x1, matrix products, local(): jnp.einsum('btj,tij->tbi', picked, tile_values, preferred_element_type=jn...  18.9 us
    dot_general x1, matrix products, local(): jnp.einsum('rst,tbi->rbsi', selector, products, precision=lax.Precision.H...  13.7 us
  transfers between devices with their start and end apart: 3, of which 3 were waited for; matrix products, arithmetic and copies ran while one was open for 0% of the time, Pallas kernels for 0%

commit v1 on v0

v1 whole, which is shorter than its diff:
```python
import functools

import jax
import jax.numpy as jnp
from jax import lax
from jax.experimental import pallas as pl
from jax.experimental.pallas import tpu as pltpu
from jax.sharding import PartitionSpec as P

LANES = 128
CHUNK = 32
UNROLL = 8
NT = (((1,), (1,)), ((), ()))
MIB = 1 << 20


def swap(value, axis, mask):
    count = lax.axis_size(axis)
    return lax.ppermute(value, axis, [(i, i ^ mask) for i in range(count)])


def tree_sum(values):
    while len(values) > 1:
        values = [values[i] + values[i + 1] for i in range(0, len(values), 2)]
    return values[0]


def split(value):
    high = value.astype(jnp.bfloat16)
    low = (value - high.astype(jnp.float32)).astype(jnp.bfloat16)
    return high, low


def mm(a, b, dims=(((1,), (0,)), ((), ()))):
    return lax.dot_general(a, b, dims, preferred_element_type=jnp.float32)


def dot_split(a, b, dims=(((1,), (0,)), ((), ()))):
    rows = a.shape[0]
    a_high, a_low = split(a)
    b_high, b_low = split(b)
    both = mm(jnp.concatenate([a_high, a_low], axis=0), b_high, dims)
    return both[:rows] + both[rows:] + mm(a_high, b_low, dims)


def start_kernel(current, previous, coupling, diag, out):
    out[...] = diag[...] * current[...] - jnp.dot(
        coupling[...],
        previous[...],
        precision=lax.Precision.HIGHEST,
        preferred_element_type=jnp.float32,
    )


def tiles_kernel(row_devs, col_devs, place, rows, cols, counts, *refs):
    panels = refs[:col_devs]
    tiles = refs[col_devs]
    own = refs[col_devs + 1]
    sends = refs[col_devs + 2 : col_devs + 1 + row_devs]
    panel_buf, tile_buf, acc, panel_sem, tile_sem = refs[col_devs + 1 + row_devs :]
    slab_tiles = own.shape[1] // LANES
    targets = row_devs * slab_tiles
    row, col, count = place[0], place[1], counts[0]
    chunks = (count + CHUNK - 1) // CHUNK

    def tile_copy(k):
        window = pl.ds(k * CHUNK, CHUNK)
        return pltpu.make_async_copy(tiles.at[window], tile_buf.at[window], tile_sem.at[k])

    panel_copies = [
        pltpu.make_async_copy(panels[m], panel_buf.at[m], panel_sem.at[m]) for m in range(col_devs)
    ]
    for copy in panel_copies:
        copy.start()

    @pl.loop(0, chunks)
    def _(k):
        tile_copy(k).start()

    acc[...] = jnp.zeros_like(acc)
    for copy in panel_copies:
        copy.wait()

    @pl.loop(0, chunks)
    def _(k):
        tile_copy(k).wait()
        groups = jnp.minimum(CHUNK // UNROLL, (count - k * CHUNK + UNROLL - 1) // UNROLL)

        @pl.loop(0, groups)
        def _(g):
            first = k * CHUNK + g * UNROLL
            parts = []
            for u in range(UNROLL):
                b = cols[first + u]
                source = (b // slab_tiles) ^ col
                where = pl.multiple_of((b % slab_tiles) * LANES, LANES)
                parts.append(mm(panel_buf[source, :, pl.ds(where, LANES)], tile_buf[first + u], NT))
            for u in range(UNROLL):
                a = jnp.where(first + u < count, rows[first + u], targets)
                acc[a] += parts[u]

    for s in range(slab_tiles):
        window = pl.ds(s * LANES, LANES)
        own[:, window] = acc[row * slab_tiles + s]
        for m in range(1, row_devs):
            sends[m - 1][:, window] = acc[(row ^ m) * slab_tiles + s].astype(jnp.bfloat16)


def coefficient_kernel(cells, pieces, *refs):
    base, own = refs[0], refs[1]
    received = refs[2 : 1 + pieces]
    mass, current, stored, recurrence, out = refs[1 + pieces :]
    total = base[...] + own[...]
    for ref in received:
        total = total + ref[...].astype(jnp.float32)
    recurrence[...] = total
    weighted = total * (mass[...] * (1.0 / cells))
    basis = jnp.concatenate([current[...], stored[...]], axis=0)
    coef = dot_split(weighted, basis, NT)
    width = coef.shape[0]
    groups = out.shape[0] // width
    coef = jnp.concatenate(
        [coef, jnp.zeros((width, groups * LANES - coef.shape[1]), jnp.float32)], axis=1
    )
    for g in range(groups):
        out[g * width : (g + 1) * width, :] = coef[:, g * LANES : (g + 1) * LANES]


def residual_kernel(cells, col_devs, place, *refs):
    pieces = refs[:col_devs]
    recurrence, mass, current, stored, residual, coef_out, gram, gathered, packed = refs[col_devs:]
    col = place[1]
    rows = pieces[0].shape[0]
    for m in range(col_devs):
        gathered[m] = pieces[m][...]
    for p in range(col_devs):
        packed[p * rows : (p + 1) * rows, :] = gathered[p ^ col]
    width = recurrence.shape[0]
    groups = packed.shape[0] // width
    coef = jnp.concatenate(
        [packed[g * width : (g + 1) * width, :] for g in range(groups)], axis=1
    )
    basis = jnp.concatenate([current[...], stored[...]], axis=0)
    coef = coef[:, : basis.shape[0]]
    coef_out[...] = coef
    value = recurrence[...] - dot_split(coef, basis)
    residual[...] = value
    local = dot_split(value * (mass[...] * (1.0 / cells)), value, NT)
    half = width // 2
    gram[...] = jnp.zeros_like(gram)
    gram[:, :width] = local[:half]
    gram[:, LANES // 2 : LANES // 2 + width] = local[half:]


def vmem(count):
    return [pl.BlockSpec(memory_space=pltpu.VMEM)] * count


def smem(count):
    return [pl.BlockSpec(memory_space=pltpu.SMEM)] * count


def local(
    current_block,
    previous_block,
    previous_coupling,
    stored_blocks,
    stiffness_diag,
    lumped_mass,
    tile_values,
    tile_rows,
    tile_cols,
    tile_counts,
):
    row_devs = lax.axis_size("row")
    col_devs = lax.axis_size("col")
    width, slab_len = current_block.shape
    stored_count = stored_blocks.shape[0]
    slots, tile_len, _ = tile_values.shape
    slab_tiles = slab_len // tile_len
    cells = slab_len * row_devs * col_devs
    f32, bf16 = jnp.float32, jnp.bfloat16
    place = jnp.stack([lax.axis_index("row"), lax.axis_index("col")]).astype(jnp.int32)
    stored = stored_blocks.reshape(stored_count * width, slab_len)
    mass = lumped_mass.reshape(1, slab_len)
    diag = stiffness_diag.reshape(1, slab_len)
    slab = jax.ShapeDtypeStruct((width, slab_len), f32)

    with jax.named_scope("gather"):
        rounded = current_block.astype(bf16)
        panels = [rounded] + [None] * (col_devs - 1)
        for m in range(2, col_devs, 2):
            panels[m] = swap(rounded, "col", m)
        for m in range(0, col_devs, 2):
            panels[m + 1] = swap(panels[m], "col", 1)

    with jax.named_scope("start"):
        base = pl.pallas_call(
            start_kernel,
            out_shape=slab,
            in_specs=vmem(4),
            out_specs=vmem(1)[0],
            cost_estimate=pl.CostEstimate(
                flops=12 * width * width * slab_len, bytes_accessed=12 * width * slab_len, transcendentals=0
            ),
        )(current_block, previous_block, previous_coupling, diag)

    with jax.named_scope("tiles"):
        outs = pl.pallas_call(
            functools.partial(tiles_kernel, row_devs, col_devs),
            out_shape=[slab] + [jax.ShapeDtypeStruct((width, slab_len), bf16)] * (row_devs - 1),
            in_specs=smem(4) + [pl.BlockSpec(memory_space=pl.ANY)] * (col_devs + 1),
            out_specs=vmem(row_devs),
            scratch_shapes=[
                pltpu.VMEM((col_devs, width, slab_len), bf16),
                pltpu.VMEM((slots, tile_len, tile_len), bf16),
                pltpu.VMEM((row_devs * slab_tiles + 1, width, tile_len), f32),
                pltpu.SemaphoreType.DMA((col_devs,)),
                pltpu.SemaphoreType.DMA((slots // CHUNK,)),
            ],
            compiler_params=pltpu.CompilerParams(vmem_limit_bytes=40 * MIB),
            cost_estimate=pl.CostEstimate(
                flops=2 * slots * width * tile_len * tile_len,
                bytes_accessed=2 * slots * tile_len * tile_len,
                transcendentals=0,
            ),
        )(place, tile_rows, tile_cols, tile_counts, *panels, tile_values)

    with jax.named_scope("scatter"):
        received = [swap(outs[m], "row", m) for m in range(1, row_devs)]

    pad_groups = -(-(stored_count + 1) * width // LANES)
    with jax.named_scope("coefficients"):
        recurrence, partial = pl.pallas_call(
            functools.partial(coefficient_kernel, cells, row_devs),
            out_shape=[slab, jax.ShapeDtypeStruct((pad_groups * width, LANES), f32)],
            in_specs=vmem(row_devs + 4),
            out_specs=vmem(2),
            compiler_params=pltpu.CompilerParams(vmem_limit_bytes=40 * MIB),
        )(base, outs[0], *received, mass, current_block, stored)
        pieces = partial.reshape(col_devs, pad_groups * width // col_devs, LANES)
        pieces = lax.all_to_all(pieces, "col", 0, 0)
        piece = jnp.sum(pieces, axis=0)
        piece = tree_sum([piece] + [swap(piece, "row", m) for m in range(1, row_devs)])
        pieces = [piece] + [swap(piece, "col", m) for m in range(1, col_devs)]

    with jax.named_scope("residual"):
        basis_rows = (stored_count + 1) * width
        residual_block, coef, gram = pl.pallas_call(
            functools.partial(residual_kernel, cells, col_devs),
            out_shape=[
                slab,
                jax.ShapeDtypeStruct((width, basis_rows), f32),
                jax.ShapeDtypeStruct((width // 2, LANES), f32),
            ],
            in_specs=smem(1) + vmem(col_devs + 4),
            out_specs=vmem(3),
            scratch_shapes=[
                pltpu.VMEM((col_devs, pad_groups * width // col_devs, LANES), f32),
                pltpu.VMEM((pad_groups * width, LANES), f32),
            ],
            compiler_params=pltpu.CompilerParams(vmem_limit_bytes=40 * MIB),
        )(place, *pieces, recurrence, mass, current_block, stored)
        coefficients = coef.T.reshape(stored_count + 1, width, width)

    with jax.named_scope("gram"):
        gram = tree_sum([gram] + [swap(gram, "col", m) for m in range(1, col_devs)])
        gram = tree_sum([gram] + [swap(gram, "row", m) for m in range(1, row_devs)])
        gram = jnp.concatenate(
            [gram[:, :width], gram[:, LANES // 2 : LANES // 2 + width]], axis=0
        )
    return (residual_block, coefficients, gram)


def solution(mesh):
    return jax.shard_map(
        local,
        mesh=mesh,
        in_specs=(
            P(None, ("row", "col")),
            P(None, ("row", "col")),
            P(),
            P(None, None, ("row", "col")),
            P(("row", "col")),
            P(("row", "col")),
            P(("row", "col"), None, None),
            P(("row", "col")),
            P(("row", "col")),
            P(("row", "col")),
        ),
        out_specs=(P(None, ("row", "col")), P(), P()),
        check_vma=False,
    )
```

time: 290 us -> 107 us (0.37)
  waiting for transfers between devices: 174 us -> 24.6 us
  starting transfers between devices: 0.3 us -> 43.1 us
  matrix products: 42.7 us -> 0 us
  blocking collectives: 41.7 us -> 8.25 us
  Pallas kernels: 0 us -> 16.7 us
  between operations: 14.5 us -> 1.4 us
  local copies, waits for them, and re-layouts: 14.1 us -> 8.26 us
    psum x1 -> x0, waiting for transfers between devices: 122 us -> none  [local(): coefficients = lax.psum(local_coef, ('row', 'col'))]
    ppermute x0 -> x30, starting transfers between devices: none -> 43.1 us  [swap(): return lax.ppermute(value, axis, [(i, i ^ mask) for i in range(count)])]
    dot_general x6 -> x0, matrix products: 42.7 us -> none  [the longest x1 18.9 us: local(): jnp.einsum('btj,tij->tbi', picked, tile_values, preferred_element_type=jn...]
    psum x1 -> x0, blocking collectives: 41.7 us -> none  [local(): gram = lax.psum(local_gram, ('row', 'col'))]
    all_gather x1 -> x0, waiting for transfers between devices: 27.8 us -> none  [local(): gathered = lax.all_gather(rounded, 'col', axis=1, tiled=True)]
    ppermute x0 -> x30, waiting for transfers between devices: none -> 24.6 us  [swap(): return lax.ppermute(value, axis, [(i, i ^ mask) for i in range(count)])]
    reduce_scatter x1 -> x0, waiting for transfers between devices: 23.2 us -> none  [local(): lax.psum_scatter(summed_tiles.reshape(owners, width, slab_len).astype(jnp...]
    pallas_call x0 -> x4, Pallas kernels: none -> 16.7 us  [the longest x1 9.82 us: local(): pl.pallas_call(functools.partial(tiles_kernel, row_devs, col_devs), out_s...]
  transfers between devices with their start and end apart: 3 -> 30, of which waited for: 3 -> 17; matrix products, arithmetic and copies ran while one was open for 0% -> 2% of each run, Pallas kernels for 0% -> 2%
where the time goes in v1:
time: 107 us
  starting transfers between devices  43.1 us (40%)
  waiting for transfers between devices  24.6 us (23%)
  Pallas kernels  16.7 us (16%)
  local copies, waits for them, and re-layouts  8.26 us (8%)
  blocking collectives  8.25 us (8%)
  other arithmetic  4.77 us (4%)
  between operations  1.4 us (1%)
    ppermute x30, starting transfers between devices, swap(): return lax.ppermute(value, axis, [(i, i ^ mask) for i in range(count)])  43.1 us
    ppermute x30, waiting for transfers between devices, swap(): return lax.ppermute(value, axis, [(i, i ^ mask) for i in range(count)])  24.6 us
    pallas_call x1, Pallas kernels, local(): pl.pallas_call(functools.partial(tiles_kernel, row_devs, col_devs), out_s...  9.82 us
    all_to_all x1, blocking collectives, local(): pieces = lax.all_to_all(pieces, 'col', 0, 0)  8.25 us
    unnamed x22, local copies, waits for them, and re-layouts  6.48 us
    pallas_call x1, Pallas kernels, local(): pl.pallas_call(functools.partial(coefficient_kernel, cells, row_devs), ou...  2.36 us
    pallas_call x1, Pallas kernels, local(): pl.pallas_call(start_kernel, out_shape=slab, in_specs=vmem(4), out_specs=...  2.32 us
    pallas_call x1, Pallas kernels, local(): pl.pallas_call(functools.partial(residual_kernel, cells, col_devs), out_s...  2.18 us
  transfers between devices with their start and end apart: 30, of which 17 were waited for; matrix products, arithmetic and copies ran while one was open for 2% of the time, Pallas kernels for 2%

profile of v1, /device:TPU:0, one launch (start us, length us, event | category | flops | bytes accessed | tf_op | source)
XLA Modules:
  0.0 107.1 jit_solution(14806211227855509590)
XLA Ops:
  0.6 0.0 copy-start.1
  0.7 1.8 %convert_element_type.3.refs_0_ = bf16[48,2048]{1,0:T(8,128)(2,1)} convert(f32[48,2048]{1,0:T(8,128)} %refs_10_.1) | non-fusion elementwise | flops 98304 | bytes 589824 | tf_op jit(solution)/shard_map/gather/convert_element_type | solution.py:190
  2.5 3.9 %collective-permute-start.5 = (bf16[48,2048]{1,0:T(8,128)(2,1)}, bf16[48,2048]{1,0:T(8,128)(2,1)}, u32[]{:S(2)}, u32[]{:S(2)}) collective-permute-start(bf16[48,2048]{1,0:T(8,128)(2,1)} %convert_element_type.3.refs_0_), channel_id=1, source_target_pairs={{0,6},{1,7},{2,4},{3,5},{4,2},{5,3},{6,0},{7,1},{8,14},{9,15},{10,... | collective-permute-start | bytes 589832 | tf_op jit(solution)/shard_map/gather/ppermute | solution.py:19
  6.4 0.5 collective-permute-start.3
  6.9 0.1 collective-permute-start.1
  7.0 5.5 %collective-permute-done.5.refs_6_ = bf16[48,2048]{1,0:T(8,128)(2,1)} collective-permute-done((bf16[48,2048]{1,0:T(8,128)(2,1)}, bf16[48,2048]{1,0:T(8,128)(2,1)}, u32[]{:S(2)}, u32[]{:S(2)}) %collective-permute-start.5) | collective-permute-done | bytes 196640 | tf_op jit(solution)/shard_map/gather/ppermute | solution.py:19
  12.5 3.3 %collective-permute-done.3.refs_4_ = bf16[48,2048]{1,0:T(8,128)(2,1)} collective-permute-done((bf16[48,2048]{1,0:T(8,128)(2,1)}, bf16[48,2048]{1,0:T(8,128)(2,1)}, u32[]{:S(2)}, u32[]{:S(2)}) %collective-permute-start.3) | collective-permute-done | bytes 196640 | tf_op jit(solution)/shard_map/gather/ppermute | solution.py:19
  15.8 0.0 collective-permute-start.4
  15.8 0.3 collective-permute-done.1.refs_2_
  16.1 0.2 collective-permute-start.2
  17.0 0.1 pad_add_fusion.place
  17.1 0.5 collective-permute-done.4.refs_5_
  17.6 0.3 collective-permute-done.2.refs_3_
  17.9 0.7 copy-done.9
  18.6 0.7 copy-done.10
  19.3 9.8 %tiles.1 = (f32[48,2048]{1,0:T(8,128)S(1)}, bf16[48,2048]{1,0:T(8,128)(2,1)}, bf16[48,2048]{1,0:T(8,128)(2,1)}, bf16[48,2048]{1,0:T(8,128)(2,1)}) custom-call(s32[2]{0:T(128)S(1)} %pad_add_fusion.place, s32[512]{0:T(512)S(1)} %copy-done.9, s32[512]{0:T(512)S(1)} %copy-done.10, s32[1]{0:T(128)S(6)} %copy.15.counts, ...), custom_call_target="tpu_custom_call" | custom-call | flops 805306368 | bytes 16777216 | tf_op jit(solution)/shard_map/tiles/pallas_call | solution.py:209
  29.1 0.7 copy-done.5
  29.9 4.5 %collective-permute-start.7 = (bf16[48,2048]{1,0:T(8,128)(2,1)}, bf16[48,2048]{1,0:T(8,128)(2,1)}, u32[]{:S(2)}, u32[]{:S(2)}) collective-permute-start(bf16[48,2048]{1,0:T(8,128)(2,1)} %get-tuple-element.13), channel_id=1, source_target_pairs={{0,8},{8,0},{16,24},{24,16},{1,9},{9,1},{17,25},{25,17},{2,10},{10... | collective-permute-start | bytes 589832 | tf_op jit(solution)/shard_map/scatter/ppermute | solution.py:19
  34.3 11.1 %collective-permute-start.8 = (bf16[48,2048]{1,0:T(8,128)(2,1)}, bf16[48,2048]{1,0:T(8,128)(2,1)}, u32[]{:S(2)}, u32[]{:S(2)}) collective-permute-start(bf16[48,2048]{1,0:T(8,128)(2,1)} %get-tuple-element.14), channel_id=1, source_target_pairs={{0,16},{8,24},{16,0},{24,8},{1,17},{9,25},{17,1},{25,9},{2,18},{10... | collective-permute-start | bytes 589832 | tf_op jit(solution)/shard_map/scatter/ppermute | solution.py:19
  45.4 1.5 %collective-permute-start.9 = (bf16[48,2048]{1,0:T(8,128)(2,1)}, bf16[48,2048]{1,0:T(8,128)(2,1)}, u32[]{:S(2)}, u32[]{:S(2)}) collective-permute-start(bf16[48,2048]{1,0:T(8,128)(2,1)} %get-tuple-element.15), channel_id=1, source_target_pairs={{0,24},{8,16},{16,8},{24,0},{1,25},{9,17},{17,9},{25,1},{2,26},{10... | collective-permute-start | bytes 589832 | tf_op jit(solution)/shard_map/scatter/ppermute | solution.py:19
  46.9 2.3 %start.1.refs_0_ = f32[48,2048]{1,0:T(8,128)} custom-call(f32[48,2048]{1,0:T(8,128)} %refs_10_.1, f32[48,2048]{1,0:T(8,128)} %previous.1, f32[48,48]{1,0:T(8,128)} %coupling.1, f32[1,2048]{1,0:T(1,128)} %bitcast.15), custom_call_target="tpu_custom_call" | custom-call | flops 56623104 | bytes 1179648 | tf_op jit(solution)/shard_map/start/pallas_call | solution.py:198
  49.2 0.2 collective-permute-done.8.refs_3_
  49.4 5.8 %collective-permute-done.9.refs_4_ = bf16[48,2048]{1,0:T(8,128)(2,1)} collective-permute-done((bf16[48,2048]{1,0:T(8,128)(2,1)}, bf16[48,2048]{1,0:T(8,128)(2,1)}, u32[]{:S(2)}, u32[]{:S(2)}) %collective-permute-start.9) | collective-permute-done | bytes 196640 | tf_op jit(solution)/shard_map/scatter/ppermute | solution.py:19
  55.2 0.0 copy-start.2
  55.2 1.0 copy-done.2
  56.2 1.0 copy-done.6
  57.2 2.4 %coefficients.1 = (f32[48,2048]{1,0:T(8,128)S(1)}, f32[192,128]{1,0:T(8,128)S(1)}) custom-call(f32[48,2048]{1,0:T(8,128)S(1)} %copy-done.2, f32[48,2048]{1,0:T(8,128)S(1)} %copy-done.6, bf16[48,2048]{1,0:T(8,128)(2,1)} %collective-permute-done.7.refs_2_, bf16[48,2048]{1,0:T(8,128)(2,1)} %collective-permute-done.8.refs_3_, ...), custom_call_target="tpu_custom_call" | custom-call | tf_op jit(solution)/shard_map/coefficients/pallas_call | solution.py:234
  59.6 0.7 copy-done.3
  60.3 8.3 %all_to_all.5 = f32[8,24,128]{2,1,0:T(8,128)} all-to-all(f32[8,24,128]{2,1,0:T(8,128)S(1)} %bitcast.10), channel_id=1, replica_groups=mesh['row'=4,'col'=8] {'col'}, dimensions={0} | all-to-all | bytes 196608 | tf_op jit(solution)/shard_map/coefficients/all_to_all | solution.py:242
  68.6 1.5 %reduce_sum.9 = f32[24,128]{1,0:T(8,128)} reduce(f32[8,24,128]{2,1,0:T(8,128)} %all_to_all.5, f32[]{:T(128)} %constant.9.clone.1), dimensions={0}, to_apply=%region_0.0 | reduce | flops 21504 | bytes 110596 | tf_op jit(solution)/shard_map/coefficients/reduce_sum | solution.py:243
  70.1 2.3 %collective-permute-start.12 = (f32[24,128]{1,0:T(8,128)}, f32[24,128]{1,0:T(8,128)S(1)}, u32[]{:S(2)}, u32[]{:S(2)}) collective-permute-start(f32[24,128]{1,0:T(8,128)} %reduce_sum.9), channel_id=1, source_target_pairs={{0,24},{8,16},{16,8},{24,0},{1,25},{9,17},{17,9},{25,1},{2,26},{10... | collective-permute-start | bytes 36872 | tf_op jit(solution)/shard_map/coefficients/ppermute | solution.py:19
  72.3 1.7 %collective-permute-start.11 = (f32[24,128]{1,0:T(8,128)}, f32[24,128]{1,0:T(8,128)S(1)}, u32[]{:S(2)}, u32[]{:S(2)}) collective-permute-start(f32[24,128]{1,0:T(8,128)} %reduce_sum.9), channel_id=1, source_target_pairs={{0,16},{8,24},{16,0},{24,8},{1,17},{9,25},{17,1},{25,9},{2,18},{10... | collective-permute-start | bytes 36872 | tf_op jit(solution)/shard_map/coefficients/ppermute | solution.py:19
  74.0 0.4 collective-permute-start.10
  74.4 1.3 %collective-permute-done.12 = f32[24,128]{1,0:T(8,128)S(1)} collective-permute-done((f32[24,128]{1,0:T(8,128)}, f32[24,128]{1,0:T(8,128)S(1)}, u32[]{:S(2)}, u32[]{:S(2)}) %collective-permute-start.12) | collective-permute-done | bytes 12320 | tf_op jit(solution)/shard_map/coefficients/ppermute | solution.py:19
  75.8 1.4 %collective-permute-done.11 = f32[24,128]{1,0:T(8,128)S(1)} collective-permute-done((f32[24,128]{1,0:T(8,128)}, f32[24,128]{1,0:T(8,128)S(1)}, u32[]{:S(2)}, u32[]{:S(2)}) %collective-permute-start.11) | collective-permute-done | bytes 12320 | tf_op jit(solution)/shard_map/coefficients/ppermute | solution.py:19
  77.1 0.8 collective-permute-done.10
  77.9 0.7 add_add_fusion.2.refs_0_
  78.6 0.6 collective-permute-start.18
  79.2 2.3 %collective-permute-start.17 = (f32[24,128]{1,0:T(8,128)S(1)}, f32[24,128]{1,0:T(8,128)S(1)}, u32[]{:S(2)}, u32[]{:S(2)}) collective-permute-start(f32[24,128]{1,0:T(8,128)S(1)} %add_add_fusion.2.refs_0_), channel_id=1, source_target_pairs={{0,5},{1,4},{2,7},{3,6},{4,1},{5,0},{6,3},{7,2},{8,13},{9,12},{10,... | collective-permute-start | bytes 36872 | tf_op jit(solution)/shard_map/coefficients/ppermute | solution.py:19
  81.5 1.5 %collective-permute-start.16 = (f32[24,128]{1,0:T(8,128)S(1)}, f32[24,128]{1,0:T(8,128)S(1)}, u32[]{:S(2)}, u32[]{:S(2)}) collective-permute-start(f32[24,128]{1,0:T(8,128)S(1)} %add_add_fusion.2.refs_0_), channel_id=1, source_target_pairs={{0,4},{1,5},{2,6},{3,7},{4,0},{5,1},{6,2},{7,3},{8,12},{9,13},{10,... | collective-permute-start | bytes 36872 | tf_op jit(solution)/shard_map/coefficients/ppermute | solution.py:19
  83.0 0.6 collective-permute-start.14
  83.6 1.3 %collective-permute-start.13 = (f32[24,128]{1,0:T(8,128)S(1)}, f32[24,128]{1,0:T(8,128)S(1)}, u32[]{:S(2)}, u32[]{:S(2)}) collective-permute-start(f32[24,128]{1,0:T(8,128)S(1)} %add_add_fusion.2.refs_0_), channel_id=1, source_target_pairs={{0,1},{1,0},{2,3},{3,2},{4,5},{5,4},{6,7},{7,6},{8,9},{9,8},{10,11... | collective-permute-start | bytes 36872 | tf_op jit(solution)/shard_map/coefficients/ppermute | solution.py:19
  84.9 0.3 collective-permute-done.16.refs_4_
  85.2 0.9 collective-permute-done.15.refs_3_
  86.1 0.6 collective-permute-done.14.refs_2_
  86.7 1.0 copy-done.4
  87.7 2.2 %residual.1 = (f32[48,2048]{1,0:T(8,128)}, f32[48,432]{1,0:T(8,128)S(1)}, f32[24,128]{1,0:T(8,128)S(1)}) custom-call(s32[2]{0:T(128)S(1)} %pad_add_fusion.place, f32[24,128]{1,0:T(8,128)S(1)} %add_add_fusion.2.refs_0_, f32[24,128]{1,0:T(8,128)S(1)} %collective-permute-done.13.refs_1_, f32[24,128]{1,0:T(8,128)S(1)} %collective-permute-done.14.refs_2_, ...), custom_call_target="tpu_custom_call" | custom-call | tf_op jit(solution)/shard_map/residual/pallas_call | solution.py:249
  89.9 0.6 copy-done.7
  90.6 0.9 collective-permute-start.26
  91.5 1.1 %collective-permute-start.25 = (f32[24,128]{1,0:T(8,128)S(1)}, f32[24,128]{1,0:T(8,128)S(1)}, u32[]{:S(2)}, u32[]{:S(2)}) collective-permute-start(f32[24,128]{1,0:T(8,128)S(1)} %get-tuple-element.20), channel_id=1, source_target_pairs={{0,6},{1,7},{2,4},{3,5},{4,2},{5,3},{6,0},{7,1},{8,14},{9,15},{10,... | collective-permute-start | bytes 36872 | tf_op jit(solution)/shard_map/gram/ppermute | solution.py:19
  92.6 0.9 collective-permute-start.24
  93.5 1.4 %collective-permute-start.23 = (f32[24,128]{1,0:T(8,128)S(1)}, f32[24,128]{1,0:T(8,128)S(1)}, u32[]{:S(2)}, u32[]{:S(2)}) collective-permute-start(f32[24,128]{1,0:T(8,128)S(1)} %get-tuple-element.20), channel_id=1, source_target_pairs={{0,4},{1,5},{2,6},{3,7},{4,0},{5,1},{6,2},{7,3},{8,12},{9,13},{10,... | collective-permute-start | bytes 36872 | tf_op jit(solution)/shard_map/gram/ppermute | solution.py:19
  95.0 0.6 collective-permute-start.22
  95.6 0.5 collective-permute-start.21
  96.1 0.7 collective-permute-start.20
  96.8 0.4 collective-permute-done.23
  97.2 0.9 collective-permute-done.22
  98.1 1.2 %collective-permute-done.21 = f32[24,128]{1,0:T(8,128)S(1)} collective-permute-done((f32[24,128]{1,0:T(8,128)S(1)}, f32[24,128]{1,0:T(8,128)S(1)}, u32[]{:S(2)}, u32[]{:S(2)}) %collective-permute-start.21) | collective-permute-done | bytes 12320 | tf_op jit(solution)/shard_map/gram/ppermute | solution.py:19
  99.3 2.5 %collective-permute-start.29 = (f32[24,128]{1,0:T(8,128)S(1)}, f32[24,128]{1,0:T(8,128)S(1)}, u32[]{:S(2)}, u32[]{:S(2)}) collective-permute-start(f32[24,128]{1,0:T(8,128)S(1)} %add_add_fusion.1), channel_id=1, source_target_pairs={{0,24},{8,16},{16,8},{24,0},{1,25},{9,17},{17,9},{25,1},{2,26},{10... | collective-permute-start | bytes 36872 | tf_op jit(solution)/shard_map/gram/ppermute | solution.py:19
  101.8 1.9 %collective-permute-start.27 = (f32[24,128]{1,0:T(8,128)S(1)}, f32[24,128]{1,0:T(8,128)S(1)}, u32[]{:S(2)}, u32[]{:S(2)}) collective-permute-start(f32[24,128]{1,0:T(8,128)S(1)} %add_add_fusion.1), channel_id=1, source_target_pairs={{0,8},{8,0},{16,24},{24,16},{1,9},{9,1},{17,25},{25,17},{2,10},{10... | collective-permute-start | bytes 36872 | tf_op jit(solution)/shard_map/gram/ppermute | solution.py:19
  103.7 1.7 %copy.14 = f32[432,48]{1,0:T(8,128)} copy(f32[432,48]{0,1:T(8,128)} %bitcast.11) | data formatting | bytes 165888 | tf_op jit(solution)/shard_map/residual/transpose | solution.py:264
  105.4 0.9 collective-permute-done.28
  106.4 0.1 fusion
  106.5 0.6 pad_maximum_fusion
  (32 shorter events, 0.1 us)
Async XLA Ops:
  0.6 54.6 %copy-start.1 = (f32[48,2048]{1,0:T(8,128)S(1)}, f32[48,2048]{1,0:T(8,128)}, u32[]{:S(2)}) copy-start(f32[48,2048]{1,0:T(8,128)} %refs_10_.1) | copy-start | bytes 1179652
  0.6 54.5 %copy-start.8 = (f32[2048]{0:T(1024)S(1)}, f32[2048]{0:T(1024)}, u32[]{:S(2)}) copy-start(f32[2048]{0:T(1024)} %param.15) | copy-start | bytes 24580
  0.7 54.5 %copy-start = (f32[8,48,2048]{2,1,0:T(8,128)S(1)}, f32[8,48,2048]{2,1,0:T(8,128)}, u32[]{:S(2)}) copy-start(f32[8,48,2048]{2,1,0:T(8,128)} %param.13) | copy-start | bytes 9437188
  2.5 10.0 %collective-permute-start.5 = (bf16[48,2048]{1,0:T(8,128)(2,1)}, bf16[48,2048]{1,0:T(8,128)(2,1)}, u32[]{:S(2)}, u32[]{:S(2)}) collective-permute-start(bf16[48,2048]{1,0:T(8,128)(2,1)} %convert_element_type.3.refs_0_), channel_id=1, source_target_pairs={{0,6},{1,7},{2,4},{3,5},{4,2},{5,3},{6,0},{7,1},{8,14},{9,15},{10,... | collective-permute-start | bytes 589832 | tf_op jit(solution)/shard_map/gather/ppermute | solution.py:19
  6.4 9.4 %collective-permute-start.3 = (bf16[48,2048]{1,0:T(8,128)(2,1)}, bf16[48,2048]{1,0:T(8,128)(2,1)}, u32[]{:S(2)}, u32[]{:S(2)}) collective-permute-start(bf16[48,2048]{1,0:T(8,128)(2,1)} %convert_element_type.3.refs_0_), channel_id=1, source_target_pairs={{0,4},{1,5},{2,6},{3,7},{4,0},{5,1},{6,2},{7,3},{8,12},{9,13},{10,... | collective-permute-start | bytes 589832 | tf_op jit(solution)/shard_map/gather/ppermute | solution.py:19
  6.9 9.2 %collective-permute-start.1 = (bf16[48,2048]{1,0:T(8,128)(2,1)}, bf16[48,2048]{1,0:T(8,128)(2,1)}, u32[]{:S(2)}, u32[]{:S(2)}) collective-permute-start(bf16[48,2048]{1,0:T(8,128)(2,1)} %convert_element_type.3.refs_0_), channel_id=1, source_target_pairs={{0,2},{1,3},{2,0},{3,1},{4,6},{5,7},{6,4},{7,5},{8,10},{9,11},{10,... | collective-permute-start | bytes 589832 | tf_op jit(solution)/shard_map/gather/ppermute | solution.py:19
  7.0 10.1 %collective-permute-start = (bf16[48,2048]{1,0:T(8,128)(2,1)}, bf16[48,2048]{1,0:T(8,128)(2,1)}, u32[]{:S(2)}, u32[]{:S(2)}) collective-permute-start(bf16[48,2048]{1,0:T(8,128)(2,1)} %convert_element_type.3.refs_0_), channel_id=1, source_target_pairs={{0,1},{1,0},{2,3},{3,2},{4,5},{5,4},{6,7},{7,6},{8,9},{9,8},{10,11... | collective-permute-start | bytes 589832 | tf_op jit(solution)/shard_map/gather/ppermute | solution.py:19
  12.5 4.6 %collective-permute-start.6 = (bf16[48,2048]{1,0:T(8,128)(2,1)}, bf16[48,2048]{1,0:T(8,128)(2,1)}, u32[]{:S(2)}, u32[]{:S(2)}) collective-permute-start(bf16[48,2048]{1,0:T(8,128)(2,1)} %collective-permute-done.5.refs_6_), channel_id=1, source_target_pairs={{0,1},{1,0},{2,3},{3,2},{4,5},{5,4},{6,7},{7,6},{8,9},{9,8},{10,11... | collective-permute-start | bytes 589832 | tf_op jit(solution)/shard_map/gather/ppermute | solution.py:19
  15.8 1.8 %collective-permute-start.4 = (bf16[48,2048]{1,0:T(8,128)(2,1)}, bf16[48,2048]{1,0:T(8,128)(2,1)}, u32[]{:S(2)}, u32[]{:S(2)}) collective-permute-start(bf16[48,2048]{1,0:T(8,128)(2,1)} %collective-permute-done.3.refs_4_), channel_id=1, source_target_pairs={{0,1},{1,0},{2,3},{3,2},{4,5},{5,4},{6,7},{7,6},{8,9},{9,8},{10,11... | collective-permute-start | bytes 589832 | tf_op jit(solution)/shard_map/gather/ppermute | solution.py:19
  16.1 1.8 %collective-permute-start.2 = (bf16[48,2048]{1,0:T(8,128)(2,1)}, bf16[48,2048]{1,0:T(8,128)(2,1)}, u32[]{:S(2)}, u32[]{:S(2)}) collective-permute-start(bf16[48,2048]{1,0:T(8,128)(2,1)} %collective-permute-done.1.refs_2_), channel_id=1, source_target_pairs={{0,1},{1,0},{2,3},{3,2},{4,5},{5,4},{6,7},{7,6},{8,9},{9,8},{10,11... | collective-permute-start | bytes 589832 | tf_op jit(solution)/shard_map/gather/ppermute | solution.py:19
  17.9 0.7 copy-start.9
  18.6 0.7 copy-start.10
  29.1 0.7 copy-start.5
  29.9 19.4 %collective-permute-start.7 = (bf16[48,2048]{1,0:T(8,128)(2,1)}, bf16[48,2048]{1,0:T(8,128)(2,1)}, u32[]{:S(2)}, u32[]{:S(2)}) collective-permute-start(bf16[48,2048]{1,0:T(8,128)(2,1)} %get-tuple-element.13), channel_id=1, source_target_pairs={{0,8},{8,0},{16,24},{24,16},{1,9},{9,1},{17,25},{25,17},{2,10},{10... | collective-permute-start | bytes 589832 | tf_op jit(solution)/shard_map/scatter/ppermute | solution.py:19
  34.3 15.1 %collective-permute-start.8 = (bf16[48,2048]{1,0:T(8,128)(2,1)}, bf16[48,2048]{1,0:T(8,128)(2,1)}, u32[]{:S(2)}, u32[]{:S(2)}) collective-permute-start(bf16[48,2048]{1,0:T(8,128)(2,1)} %get-tuple-element.14), channel_id=1, source_target_pairs={{0,16},{8,24},{16,0},{24,8},{1,17},{9,25},{17,1},{25,9},{2,18},{10... | collective-permute-start | bytes 589832 | tf_op jit(solution)/shard_map/scatter/ppermute | solution.py:19
  45.4 9.7 %collective-permute-start.9 = (bf16[48,2048]{1,0:T(8,128)(2,1)}, bf16[48,2048]{1,0:T(8,128)(2,1)}, u32[]{:S(2)}, u32[]{:S(2)}) collective-permute-start(bf16[48,2048]{1,0:T(8,128)(2,1)} %get-tuple-element.15), channel_id=1, source_target_pairs={{0,24},{8,16},{16,8},{24,0},{1,25},{9,17},{17,9},{25,1},{2,26},{10... | collective-permute-start | bytes 589832 | tf_op jit(solution)/shard_map/scatter/ppermute | solution.py:19
  55.2 1.0 copy-start.2
  56.2 1.0 copy-start.6
  59.5 0.7 copy-start.3
  70.1 5.7 %collective-permute-start.12 = (f32[24,128]{1,0:T(8,128)}, f32[24,128]{1,0:T(8,128)S(1)}, u32[]{:S(2)}, u32[]{:S(2)}) collective-permute-start(f32[24,128]{1,0:T(8,128)} %reduce_sum.9), channel_id=1, source_target_pairs={{0,24},{8,16},{16,8},{24,0},{1,25},{9,17},{17,9},{25,1},{2,26},{10... | collective-permute-start | bytes 36872 | tf_op jit(solution)/shard_map/coefficients/ppermute | solution.py:19
  72.3 4.8 %collective-permute-start.11 = (f32[24,128]{1,0:T(8,128)}, f32[24,128]{1,0:T(8,128)S(1)}, u32[]{:S(2)}, u32[]{:S(2)}) collective-permute-start(f32[24,128]{1,0:T(8,128)} %reduce_sum.9), channel_id=1, source_target_pairs={{0,16},{8,24},{16,0},{24,8},{1,17},{9,25},{17,1},{25,9},{2,18},{10... | collective-permute-start | bytes 36872 | tf_op jit(solution)/shard_map/coefficients/ppermute | solution.py:19
  74.0 3.9 %collective-permute-start.10 = (f32[24,128]{1,0:T(8,128)}, f32[24,128]{1,0:T(8,128)S(1)}, u32[]{:S(2)}, u32[]{:S(2)}) collective-permute-start(f32[24,128]{1,0:T(8,128)} %reduce_sum.9), channel_id=1, source_target_pairs={{0,8},{8,0},{16,24},{24,16},{1,9},{9,1},{17,25},{25,17},{2,10},{10... | collective-permute-start | bytes 36872 | tf_op jit(solution)/shard_map/coefficients/ppermute | solution.py:19
  78.6 4.4 %collective-permute-start.19 = (f32[24,128]{1,0:T(8,128)S(1)}, f32[24,128]{1,0:T(8,128)S(1)}, u32[]{:S(2)}, u32[]{:S(2)}) collective-permute-start(f32[24,128]{1,0:T(8,128)S(1)} %add_add_fusion.2.refs_0_), channel_id=1, source_target_pairs={{0,7},{1,6},{2,5},{3,4},{4,3},{5,2},{6,1},{7,0},{8,15},{9,14},{10,... | collective-permute-start | bytes 36872 | tf_op jit(solution)/shard_map/coefficients/ppermute | solution.py:19
  78.6 5.0 %collective-permute-start.18 = (f32[24,128]{1,0:T(8,128)S(1)}, f32[24,128]{1,0:T(8,128)S(1)}, u32[]{:S(2)}, u32[]{:S(2)}) collective-permute-start(f32[24,128]{1,0:T(8,128)S(1)} %add_add_fusion.2.refs_0_), channel_id=1, source_target_pairs={{0,6},{1,7},{2,4},{3,5},{4,2},{5,3},{6,0},{7,1},{8,14},{9,15},{10,... | collective-permute-start | bytes 36872 | tf_op jit(solution)/shard_map/coefficients/ppermute | solution.py:19
  79.2 5.6 %collective-permute-start.17 = (f32[24,128]{1,0:T(8,128)S(1)}, f32[24,128]{1,0:T(8,128)S(1)}, u32[]{:S(2)}, u32[]{:S(2)}) collective-permute-start(f32[24,128]{1,0:T(8,128)S(1)} %add_add_fusion.2.refs_0_), channel_id=1, source_target_pairs={{0,5},{1,4},{2,7},{3,6},{4,1},{5,0},{6,3},{7,2},{8,13},{9,12},{10,... | collective-permute-start | bytes 36872 | tf_op jit(solution)/shard_map/coefficients/ppermute | solution.py:19
  81.5 3.7 %collective-permute-start.16 = (f32[24,128]{1,0:T(8,128)S(1)}, f32[24,128]{1,0:T(8,128)S(1)}, u32[]{:S(2)}, u32[]{:S(2)}) collective-permute-start(f32[24,128]{1,0:T(8,128)S(1)} %add_add_fusion.2.refs_0_), channel_id=1, source_target_pairs={{0,4},{1,5},{2,6},{3,7},{4,0},{5,1},{6,2},{7,3},{8,12},{9,13},{10,... | collective-permute-start | bytes 36872 | tf_op jit(solution)/shard_map/coefficients/ppermute | solution.py:19
  83.0 3.1 %collective-permute-start.15 = (f32[24,128]{1,0:T(8,128)S(1)}, f32[24,128]{1,0:T(8,128)S(1)}, u32[]{:S(2)}, u32[]{:S(2)}) collective-permute-start(f32[24,128]{1,0:T(8,128)S(1)} %add_add_fusion.2.refs_0_), channel_id=1, source_target_pairs={{0,3},{1,2},{2,1},{3,0},{4,7},{5,6},{6,5},{7,4},{8,11},{9,10},{10,... | collective-permute-start | bytes 36872 | tf_op jit(solution)/shard_map/coefficients/ppermute | solution.py:19
  83.0 3.7 %collective-permute-start.14 = (f32[24,128]{1,0:T(8,128)S(1)}, f32[24,128]{1,0:T(8,128)S(1)}, u32[]{:S(2)}, u32[]{:S(2)}) collective-permute-start(f32[24,128]{1,0:T(8,128)S(1)} %add_add_fusion.2.refs_0_), channel_id=1, source_target_pairs={{0,2},{1,3},{2,0},{3,1},{4,6},{5,7},{6,4},{7,5},{8,10},{9,11},{10,... | collective-permute-start | bytes 36872 | tf_op jit(solution)/shard_map/coefficients/ppermute | solution.py:19
  83.6 3.1 %collective-permute-start.13 = (f32[24,128]{1,0:T(8,128)S(1)}, f32[24,128]{1,0:T(8,128)S(1)}, u32[]{:S(2)}, u32[]{:S(2)}) collective-permute-start(f32[24,128]{1,0:T(8,128)S(1)} %add_add_fusion.2.refs_0_), channel_id=1, source_target_pairs={{0,1},{1,0},{2,3},{3,2},{4,5},{5,4},{6,7},{7,6},{8,9},{9,8},{10,11... | collective-permute-start | bytes 36872 | tf_op jit(solution)/shard_map/coefficients/ppermute | solution.py:19
  86.7 1.0 copy-start.4
  89.9 0.6 copy-start.7
  90.6 5.0 %collective-permute-start.26 = (f32[24,128]{1,0:T(8,128)S(1)}, f32[24,128]{1,0:T(8,128)S(1)}, u32[]{:S(2)}, u32[]{:S(2)}) collective-permute-start(f32[24,128]{1,0:T(8,128)S(1)} %get-tuple-element.20), channel_id=1, source_target_pairs={{0,7},{1,6},{2,5},{3,4},{4,3},{5,2},{6,1},{7,0},{8,15},{9,14},{10,... | collective-permute-start | bytes 36872 | tf_op jit(solution)/shard_map/gram/ppermute | solution.py:19
  91.5 4.6 %collective-permute-start.25 = (f32[24,128]{1,0:T(8,128)S(1)}, f32[24,128]{1,0:T(8,128)S(1)}, u32[]{:S(2)}, u32[]{:S(2)}) collective-permute-start(f32[24,128]{1,0:T(8,128)S(1)} %get-tuple-element.20), channel_id=1, source_target_pairs={{0,6},{1,7},{2,4},{3,5},{4,2},{5,3},{6,0},{7,1},{8,14},{9,15},{10,... | collective-permute-start | bytes 36872 | tf_op jit(solution)/shard_map/gram/ppermute | solution.py:19
  92.6 4.2 %collective-permute-start.24 = (f32[24,128]{1,0:T(8,128)S(1)}, f32[24,128]{1,0:T(8,128)S(1)}, u32[]{:S(2)}, u32[]{:S(2)}) collective-permute-start(f32[24,128]{1,0:T(8,128)S(1)} %get-tuple-element.20), channel_id=1, source_target_pairs={{0,5},{1,4},{2,7},{3,6},{4,1},{5,0},{6,3},{7,2},{8,13},{9,12},{10,... | collective-permute-start | bytes 36872 | tf_op jit(solution)/shard_map/gram/ppermute | solution.py:19
  93.5 3.7 %collective-permute-start.23 = (f32[24,128]{1,0:T(8,128)S(1)}, f32[24,128]{1,0:T(8,128)S(1)}, u32[]{:S(2)}, u32[]{:S(2)}) collective-permute-start(f32[24,128]{1,0:T(8,128)S(1)} %get-tuple-element.20), channel_id=1, source_target_pairs={{0,4},{1,5},{2,6},{3,7},{4,0},{5,1},{6,2},{7,3},{8,12},{9,13},{10,... | collective-permute-start | bytes 36872 | tf_op jit(solution)/shard_map/gram/ppermute | solution.py:19
  95.0 3.1 %collective-permute-start.22 = (f32[24,128]{1,0:T(8,128)S(1)}, f32[24,128]{1,0:T(8,128)S(1)}, u32[]{:S(2)}, u32[]{:S(2)}) collective-permute-start(f32[24,128]{1,0:T(8,128)S(1)} %get-tuple-element.20), channel_id=1, source_target_pairs={{0,3},{1,2},{2,1},{3,0},{4,7},{5,6},{6,5},{7,4},{8,11},{9,10},{10,... | collective-permute-start | bytes 36872 | tf_op jit(solution)/shard_map/gram/ppermute | solution.py:19
  95.6 3.7 %collective-permute-start.21 = (f32[24,128]{1,0:T(8,128)S(1)}, f32[24,128]{1,0:T(8,128)S(1)}, u32[]{:S(2)}, u32[]{:S(2)}) collective-permute-start(f32[24,128]{1,0:T(8,128)S(1)} %get-tuple-element.20), channel_id=1, source_target_pairs={{0,2},{1,3},{2,0},{3,1},{4,6},{5,7},{6,4},{7,5},{8,10},{9,11},{10,... | collective-permute-start | bytes 36872 | tf_op jit(solution)/shard_map/gram/ppermute | solution.py:19
  96.1 3.2 %collective-permute-start.20 = (f32[24,128]{1,0:T(8,128)S(1)}, f32[24,128]{1,0:T(8,128)S(1)}, u32[]{:S(2)}, u32[]{:S(2)}) collective-permute-start(f32[24,128]{1,0:T(8,128)S(1)} %get-tuple-element.20), channel_id=1, source_target_pairs={{0,1},{1,0},{2,3},{3,2},{4,5},{5,4},{6,7},{7,6},{8,9},{9,8},{10,11... | collective-permute-start | bytes 36872 | tf_op jit(solution)/shard_map/gram/ppermute | solution.py:19
  99.3 6.2 %collective-permute-start.29 = (f32[24,128]{1,0:T(8,128)S(1)}, f32[24,128]{1,0:T(8,128)S(1)}, u32[]{:S(2)}, u32[]{:S(2)}) collective-permute-start(f32[24,128]{1,0:T(8,128)S(1)} %add_add_fusion.1), channel_id=1, source_target_pairs={{0,24},{8,16},{16,8},{24,0},{1,25},{9,17},{17,9},{25,1},{2,26},{10... | collective-permute-start | bytes 36872 | tf_op jit(solution)/shard_map/gram/ppermute | solution.py:19
  101.8 4.6 %collective-permute-start.28 = (f32[24,128]{1,0:T(8,128)S(1)}, f32[24,128]{1,0:T(8,128)S(1)}, u32[]{:S(2)}, u32[]{:S(2)}) collective-permute-start(f32[24,128]{1,0:T(8,128)S(1)} %add_add_fusion.1), channel_id=1, source_target_pairs={{0,16},{8,24},{16,0},{24,8},{1,17},{9,25},{17,1},{25,9},{2,18},{10... | collective-permute-start | bytes 36872 | tf_op jit(solution)/shard_map/gram/ppermute | solution.py:19
  101.8 4.6 %collective-permute-start.27 = (f32[24,128]{1,0:T(8,128)S(1)}, f32[24,128]{1,0:T(8,128)S(1)}, u32[]{:S(2)}, u32[]{:S(2)}) collective-permute-start(f32[24,128]{1,0:T(8,128)S(1)} %add_add_fusion.1), channel_id=1, source_target_pairs={{0,8},{8,0},{16,24},{24,16},{1,9},{9,1},{17,25},{25,17},{2,10},{10... | collective-permute-start | bytes 36872 | tf_op jit(solution)/shard_map/gram/ppermute | solution.py:19

commit v2 on v1

v2 whole, which is shorter than its diff:
```python
import functools

import jax
import jax.numpy as jnp
from jax import lax
from jax.experimental import pallas as pl
from jax.experimental.pallas import tpu as pltpu
from jax.sharding import PartitionSpec as P

LANES = 128
UNROLL = 8
NT = (((1,), (1,)), ((), ()))
MIB = 1 << 20


def swap(value, axis, mask):
    count = lax.axis_size(axis)
    return lax.ppermute(value, axis, [(i, i ^ mask) for i in range(count)])


def split(value):
    high = value.astype(jnp.bfloat16)
    low = (value - high.astype(jnp.float32)).astype(jnp.bfloat16)
    return high, low


def mm(a, b, dims=(((1,), (0,)), ((), ()))):
    return lax.dot_general(a, b, dims, preferred_element_type=jnp.float32)


def dot_split(a, b, dims=(((1,), (0,)), ((), ()))):
    rows = a.shape[0]
    a_high, a_low = split(a)
    b_high, b_low = split(b)
    both = mm(jnp.concatenate([a_high, a_low], axis=0), b_high, dims)
    return both[:rows] + both[rows:] + mm(a_high, b_low, dims)


def blocks(shape):
    return [(q, k) for q in range(0, shape[0], 8) for k in range(0, shape[1], LANES)]


def start_kernel(current, previous, coupling, diag, out):
    out[...] = diag[...] * current[...] - jnp.dot(
        coupling[...],
        previous[...],
        precision=lax.Precision.HIGHEST,
        preferred_element_type=jnp.float32,
    )


def plan_kernel(row_devs, col_devs, slab_tiles, place, counts, rows, cols, out):
    f32, bf16, i32 = jnp.float32, jnp.bfloat16, jnp.int32
    slots, places = rows.shape[1], out.shape[1]
    targets = row_devs * slab_tiles

    def iota(shape, dim):
        return lax.broadcasted_iota(i32, shape, dim)

    slot = iota((1, slots), 1)
    occupied = slot < counts[0]
    row = jnp.where(occupied, rows[...], -1)
    member = (iota((targets, slots), 0) == row).astype(f32)
    member_bf = member.astype(bf16)
    earlier = (iota((slots, slots), 0) < iota((slots, slots), 1)).astype(f32).astype(bf16)
    rank = jnp.sum(member * mm(member_bf, earlier), axis=0, keepdims=True)
    sizes = mm(jnp.ones((8, slots), bf16), member_bf, NT)[:1]
    sizes = 2.0 * jnp.floor(0.5 * (sizes + 1.0))
    before = (iota((targets, targets), 1) < iota((targets, targets), 0)).astype(f32)
    begin = jnp.sum(before * sizes, axis=1, keepdims=True)
    total = jnp.sum(sizes, axis=1, keepdims=True)
    position = jnp.sum(member * begin, axis=0, keepdims=True) + rank
    position = jnp.where(occupied, position.astype(i32), -1)
    chosen = (iota((places, slots), 0) == position).astype(f32).astype(bf16)
    slot_f = slot.astype(f32)
    slot_high = jnp.floor(slot_f * (1.0 / 16.0))
    facts = [slot_high, slot_f - 16.0 * slot_high, cols[...].astype(f32), row.astype(f32), jnp.ones((1, slots), f32)]
    facts = jnp.concatenate(facts + [jnp.zeros((3, slots), f32)], axis=0).astype(bf16)
    found = mm(facts, chosen, NT)
    valid = found[4:5] > 0.5
    source = jnp.floor(found[2:3] * (1.0 / slab_tiles))
    tile = found[2:3] - slab_tiles * source
    out[0:1] = (16.0 * found[0:1] + found[1:2]).astype(i32)
    out[1:2] = jnp.where(valid, source.astype(i32) ^ place[1], col_devs)
    out[2:3] = tile.astype(i32)
    out[3:4] = jnp.where(valid, found[3:4].astype(i32), targets)
    out[4:8] = jnp.broadcast_to(total.astype(i32), (4, places))


def tiles_kernel(row_devs, col_devs, place, plan, *refs):
    panels = refs[:col_devs]
    tiles = refs[col_devs]
    own = refs[col_devs + 1]
    sends = refs[col_devs + 2 : col_devs + 1 + row_devs]
    panel_buf, acc, panel_sem = refs[col_devs + 1 + row_devs :]
    slab_tiles = own.shape[1] // LANES
    row = place[0]

    panel_copies = [
        pltpu.make_async_copy(panels[m], panel_buf.at[m], panel_sem.at[m]) for m in range(col_devs)
    ]
    for copy in panel_copies:
        copy.start()
    panel_buf[col_devs, :, :LANES] = jnp.zeros((own.shape[0], LANES), jnp.bfloat16)
    acc[...] = jnp.zeros_like(acc)
    for copy in panel_copies:
        copy.wait()

    def panel(p):
        where = pl.multiple_of(plan[2, p] * LANES, LANES)
        return panel_buf[plan[1, p], :, pl.ds(where, LANES)]

    @pl.loop(0, (plan[4, 0] + 2 * UNROLL - 1) // (2 * UNROLL))
    def _(g):
        first = g * 2 * UNROLL
        parts = []
        for u in range(UNROLL):
            p = first + 2 * u
            left = jnp.concatenate([panel(p), panel(p + 1)], axis=1)
            right = jnp.concatenate([tiles[plan[0, p]], tiles[plan[0, p + 1]]], axis=1)
            parts.append(mm(left, right, NT))
        for u in range(UNROLL):
            acc[plan[3, first + 2 * u]] += parts[u]

    for s in range(slab_tiles):
        window = pl.ds(s * LANES, LANES)
        own[:, window] = acc[row * slab_tiles + s]
        for m in range(1, row_devs):
            sends[m - 1][:, window] = acc[(row ^ m) * slab_tiles + s].astype(jnp.bfloat16)


def coefficient_kernel(cells, pieces, *refs):
    base, own = refs[0], refs[1]
    received = refs[2 : 1 + pieces]
    mass, current, stored, recurrence, out = refs[1 + pieces :]
    total = base[...] + own[...]
    for ref in received:
        total = total + ref[...].astype(jnp.float32)
    recurrence[...] = total
    weighted = total * (mass[...] * (1.0 / cells))
    basis = jnp.concatenate([current[...], stored[...]], axis=0)
    coef = dot_split(weighted, basis, NT)
    width = coef.shape[0]
    groups = out.shape[0] // width
    spare = -coef.shape[1] % LANES
    coef = jnp.concatenate([coef, jnp.zeros((coef.shape[0], spare), jnp.float32)], axis=1)
    out[...] = jnp.zeros_like(out)
    for p, (q, k) in enumerate(blocks(coef.shape)):
        out[p] = coef[q : q + 8, k : k + LANES]


def residual_kernel(cells, pieces, recurrence, mass, current, stored, residual, coef_out, gram, packed):
    width = recurrence.shape[0]
    for p, (q, k) in enumerate(blocks(packed.shape)):
        packed[q : q + 8, k : k + LANES] = pieces[p]
    coef = packed[...]
    basis = jnp.concatenate([current[...], stored[...]], axis=0)
    coef = coef[:, : basis.shape[0]]
    coef_out[...] = coef
    value = recurrence[...] - dot_split(coef, basis)
    residual[...] = value
    local = dot_split(value * (mass[...] * (1.0 / cells)), value, NT)
    half = width // 2
    gram[...] = jnp.zeros_like(gram)
    gram[:, :width] = local[:half]
    gram[:, LANES // 2 : LANES // 2 + width] = local[half:]


def vmem(count):
    return [pl.BlockSpec(memory_space=pltpu.VMEM)] * count


def smem(count):
    return [pl.BlockSpec(memory_space=pltpu.SMEM)] * count


def local(
    current_block,
    previous_block,
    previous_coupling,
    stored_blocks,
    stiffness_diag,
    lumped_mass,
    tile_values,
    tile_rows,
    tile_cols,
    tile_counts,
):
    row_devs = lax.axis_size("row")
    col_devs = lax.axis_size("col")
    width, slab_len = current_block.shape
    stored_count = stored_blocks.shape[0]
    slots, tile_len, _ = tile_values.shape
    slab_tiles = slab_len // tile_len
    cells = slab_len * row_devs * col_devs
    f32, bf16 = jnp.float32, jnp.bfloat16
    place = jnp.stack([lax.axis_index("row"), lax.axis_index("col")]).astype(jnp.int32)
    stored = stored_blocks.reshape(stored_count * width, slab_len)
    mass = lumped_mass.reshape(1, slab_len)
    diag = stiffness_diag.reshape(1, slab_len)
    slab = jax.ShapeDtypeStruct((width, slab_len), f32)

    with jax.named_scope("gather"):
        rounded = current_block.astype(bf16)
        panels = [rounded] + [None] * (col_devs - 1)
        for m in range(2, col_devs, 2):
            panels[m] = swap(rounded, "col", m)
        for m in range(0, col_devs, 2):
            panels[m + 1] = swap(panels[m], "col", 1)

    with jax.named_scope("start"):
        base = pl.pallas_call(
            start_kernel,
            out_shape=slab,
            in_specs=vmem(4),
            out_specs=vmem(1)[0],
            cost_estimate=pl.CostEstimate(
                flops=12 * width * width * slab_len, bytes_accessed=12 * width * slab_len, transcendentals=0
            ),
        )(current_block, previous_block, previous_coupling, diag)

    with jax.named_scope("plan"):
        targets = row_devs * slab_tiles
        places = -(-(slots + targets) // LANES) * LANES
        plan = pl.pallas_call(
            functools.partial(plan_kernel, row_devs, col_devs, slab_tiles),
            out_shape=jax.ShapeDtypeStruct((8, places), jnp.int32),
            in_specs=smem(2) + vmem(2),
            out_specs=vmem(1)[0],
            cost_estimate=pl.CostEstimate(flops=4 * slots * slots * targets, bytes_accessed=8192, transcendentals=0),
        )(place, tile_counts, tile_rows.reshape(1, slots), tile_cols.reshape(1, slots))

    with jax.named_scope("tiles"):
        outs = pl.pallas_call(
            functools.partial(tiles_kernel, row_devs, col_devs),
            out_shape=[slab] + [jax.ShapeDtypeStruct((width, slab_len), bf16)] * (row_devs - 1),
            in_specs=smem(2) + [pl.BlockSpec(memory_space=pl.ANY)] * col_devs + vmem(1),
            out_specs=vmem(row_devs),
            scratch_shapes=[
                pltpu.VMEM((col_devs + 1, width, slab_len), bf16),
                pltpu.VMEM((targets + 1, width, tile_len), f32),
                pltpu.SemaphoreType.DMA((col_devs,)),
            ],
            compiler_params=pltpu.CompilerParams(vmem_limit_bytes=32 * MIB),
            cost_estimate=pl.CostEstimate(
                flops=2 * slots * width * tile_len * tile_len,
                bytes_accessed=2 * slots * tile_len * tile_len,
                transcendentals=0,
            ),
        )(place, plan, *panels, tile_values)

    with jax.named_scope("scatter"):
        received = [swap(outs[m], "row", m) for m in range(1, row_devs)]

    devices = row_devs * col_devs
    both = ("row", "col")
    basis_rows = (stored_count + 1) * width
    padded = (width, -(-basis_rows // LANES) * LANES)
    with jax.named_scope("coefficients"):
        recurrence, partial = pl.pallas_call(
            functools.partial(coefficient_kernel, cells, row_devs),
            out_shape=[slab, jax.ShapeDtypeStruct((devices, 8, LANES), f32)],
            in_specs=vmem(row_devs + 4),
            out_specs=vmem(2),
            compiler_params=pltpu.CompilerParams(vmem_limit_bytes=24 * MIB),
        )(base, outs[0], *received, mass, current_block, stored)
        piece = jnp.sum(lax.all_to_all(partial, both, 0, 0), axis=0)
        pieces = lax.all_to_all(jnp.broadcast_to(piece, partial.shape), both, 0, 0)

    with jax.named_scope("residual"):
        residual_block, coef, gram = pl.pallas_call(
            functools.partial(residual_kernel, cells),
            out_shape=[
                slab,
                jax.ShapeDtypeStruct((width, basis_rows), f32),
                jax.ShapeDtypeStruct((width // 2, LANES), f32),
            ],
            in_specs=vmem(5),
            out_specs=vmem(3),
            scratch_shapes=[pltpu.VMEM(padded, f32)],
            compiler_params=pltpu.CompilerParams(vmem_limit_bytes=24 * MIB),
        )(pieces, recurrence, mass, current_block, stored)
        coefficients = coef.T.reshape(stored_count + 1, width, width)

    with jax.named_scope("gram"):
        grams = jnp.broadcast_to(gram, (devices,) + gram.shape)
        gram = jnp.sum(lax.all_to_all(grams, both, 0, 0), axis=0)
        gram = jnp.concatenate(
            [gram[:, :width], gram[:, LANES // 2 : LANES // 2 + width]], axis=0
        )
    return (residual_block, coefficients, gram)


def solution(mesh):
    return jax.shard_map(
        local,
        mesh=mesh,
        in_specs=(
            P(None, ("row", "col")),
            P(None, ("row", "col")),
            P(),
            P(None, None, ("row", "col")),
            P(("row", "col")),
            P(("row", "col")),
            P(("row", "col"), None, None),
            P(("row", "col")),
            P(("row", "col")),
            P(("row", "col")),
        ),
        out_specs=(P(None, ("row", "col")), P(), P()),
        check_vma=False,
    )
```

time: 107 us -> 118 us (1.10)
  starting transfers between devices: 43.1 us -> 13.9 us
  local copies, waits for them, and re-layouts: 8.26 us -> 27 us
  blocking collectives: 8.25 us -> 24.9 us
  waiting for transfers between devices: 24.6 us -> 31.5 us
  other arithmetic: 4.77 us -> 3.26 us
    ppermute x30 -> x10, starting transfers between devices: 43.1 us -> 11.3 us  [swap(): return lax.ppermute(value, axis, [(i, i ^ mask) for i in range(count)])]
    unnamed x22 -> x56, local copies, waits for them, and re-layouts: 6.48 us -> 24.4 us
    all_to_all x1 -> x2, blocking collectives: 8.25 us -> 24.9 us  [the longest x1 14.9 us: local(): piece = jnp.sum(lax.all_to_all(partial, both, 0, 0), axis=0)]
    all_to_all x0 -> x1, waiting for transfers between devices: none -> 11.5 us  [local(): gram = jnp.sum(lax.all_to_all(grams, both, 0, 0), axis=0)]
    ppermute x30 -> x10, waiting for transfers between devices: 24.6 us -> 20 us  [swap(): return lax.ppermute(value, axis, [(i, i ^ mask) for i in range(count)])]
    all_to_all x0 -> x1, starting transfers between devices: none -> 2.59 us  [local(): gram = jnp.sum(lax.all_to_all(grams, both, 0, 0), axis=0)]
    pallas_call x1, Pallas kernels: 9.82 us -> 7.37 us  [local(): pl.pallas_call(functools.partial(tiles_kernel, row_devs, col_devs), out_s...]
    pallas_call x1 -> x2, Pallas kernels: 2.18 us -> 3.6 us  [the longest x1 1.98 us: local(): pl.pallas_call(functools.partial(plan_kernel, row_devs, col_devs, slab_ti...]
  transfers between devices with their start and end apart: 30 -> 11, of which waited for: 17 -> 5; matrix products, arithmetic and copies ran while one was open for 2% -> 2% of each run, Pallas kernels for 2% -> 4%
where the time goes in v2:
time: 118 us
  waiting for transfers between devices  31.5 us (27%)
  local copies, waits for them, and re-layouts  27 us (23%)
  blocking collectives  24.9 us (21%)
  Pallas kernels  15.7 us (13%)
  starting transfers between devices  13.9 us (12%)
  other arithmetic  3.26 us (3%)
  between operations  1.41 us (1%)
    unnamed x56, local copies, waits for them, and re-layouts  24.4 us
    ppermute x10, waiting for transfers between devices, swap(): return lax.ppermute(value, axis, [(i, i ^ mask) for i in range(count)])  20 us
    all_to_all x1, blocking collectives, local(): piece = jnp.sum(lax.all_to_all(partial, both, 0, 0), axis=0)  14.9 us
    all_to_all x1, waiting for transfers between devices, local(): gram = jnp.sum(lax.all_to_all(grams, both, 0, 0), axis=0)  11.5 us
    ppermute x10, starting transfers between devices, swap(): return lax.ppermute(value, axis, [(i, i ^ mask) for i in range(count)])  11.3 us
    all_to_all x1, blocking collectives, local(): pieces = lax.all_to_all(jnp.broadcast_to(piece, partial.shape), both, 0, 0)  10 us
    pallas_call x1, Pallas kernels, local(): pl.pallas_call(functools.partial(tiles_kernel, row_devs, col_devs), out_s...  7.37 us
    all_to_all x1, starting transfers between devices, local(): gram = jnp.sum(lax.all_to_all(grams, both, 0, 0), axis=0)  2.59 us
  transfers between devices with their start and end apart: 11, of which 5 were waited for; matrix products, arithmetic and copies ran while one was open for 2% of the time, Pallas kernels for 4%

profile of v2, /device:TPU:0, one launch (start us, length us, event | category | flops | bytes accessed | tf_op | source)
XLA Modules:
  0.0 117.6 jit_solution(15623706140793216269)
XLA Ops:
  0.6 0.0 copy-start.2
  0.7 1.1 convert_element_type.3.refs_0_
  1.7 0.0 copy-start.4
  1.7 4.0 %collective-permute-start.5 = (bf16[48,2048]{1,0:T(8,128)(2,1)S(1)}, bf16[48,2048]{1,0:T(8,128)(2,1)S(1)}, u32[]{:S(2)}, u32[]{:S(2)}) collective-permute-start(bf16[48,2048]{1,0:T(8,128)(2,1)S(1)} %convert_element_type.3.refs_0_), channel_id=1, source_target_pairs={{0,6},{1,7},{2,4},{3,5},{4,2},{5,3},{6,0},{7,1},{8,14},{9,15},{10,... | collective-permute-start | bytes 589832 | tf_op jit(solution)/shard_map/gather/ppermute | solution.py:18
  5.7 0.5 collective-permute-start.3
  6.2 0.1 collective-permute-start.1
  6.3 0.0 collective-permute-start
  6.3 5.1 %collective-permute-done.5.refs_6_ = bf16[48,2048]{1,0:T(8,128)(2,1)S(1)} collective-permute-done((bf16[48,2048]{1,0:T(8,128)(2,1)S(1)}, bf16[48,2048]{1,0:T(8,128)(2,1)S(1)}, u32[]{:S(2)}, u32[]{:S(2)}) %collective-permute-start.5) | collective-permute-done | bytes 196640 | tf_op jit(solution)/shard_map/gather/ppermute | solution.py:18
  11.5 0.0 collective-permute-start.6
  11.5 0.7 copy-done.10
  12.2 2.7 %collective-permute-done.3.refs_4_ = bf16[48,2048]{1,0:T(8,128)(2,1)S(1)} collective-permute-done((bf16[48,2048]{1,0:T(8,128)(2,1)S(1)}, bf16[48,2048]{1,0:T(8,128)(2,1)S(1)}, u32[]{:S(2)}, u32[]{:S(2)}) %collective-permute-start.3) | collective-permute-done | bytes 196640 | tf_op jit(solution)/shard_map/gather/ppermute | solution.py:18
  14.8 0.0 collective-permute-start.4
  14.8 0.7 copy-done.12
  15.5 0.0 collective-permute-done.1.refs_2_
  15.5 0.5 collective-permute-start.2
  16.0 0.7 copy-done.14
  17.3 0.6 pad_add_fusion.place
  17.9 2.0 %plan.1 = s32[8,640]{1,0:T(8,128)} custom-call(s32[2]{0:T(128)} %pad_add_fusion.place, s32[1]{0:T(128)S(6)} %copy.16.counts, s32[1,512]{1,0:T(1,128)} %bitcast.16, s32[1,512]{1,0:T(1,128)} %bitcast.17), custom_call_target="tpu_custom_call" | custom-call | flops 67108864 | bytes 8192 | tf_op jit(solution)/shard_map/plan/pallas_call | solution.py:225
  19.9 0.0 collective-permute-done.refs_1_
  19.9 0.7 copy-done.16
  20.6 0.0 collective-permute-done.6.refs_7_
  20.6 0.7 copy-done.18
  21.3 0.0 collective-permute-done.4.refs_5_
  21.3 0.7 copy-done.20
  22.0 0.0 collective-permute-done.2.refs_3_
  22.0 0.7 copy-done.22
  22.7 5.8 %copy-done = bf16[512,128,128]{2,1,0:T(8,128)(2,1)S(1)} copy-done((bf16[512,128,128]{2,1,0:T(8,128)(2,1)S(1)}, bf16[512,128,128]{2,1,0:T(8,128)(2,1)}, u32[]{:S(2)}) %copy-start) | copy-done | bytes 16777240
  28.4 0.9 copy-done.5
  29.4 0.9 copy-done.11
  30.3 0.9 copy-done.13
  31.2 0.9 copy-done.15
  32.1 0.9 copy-done.17
  33.1 0.9 copy-done.19
  34.0 0.9 copy-done.21
  34.9 0.9 copy-done.23
  35.9 0.7 copy-done.26
  36.6 0.6 copy-done.27
  37.2 7.4 %tiles.1 = (f32[48,2048]{1,0:T(8,128)S(1)}, bf16[48,2048]{1,0:T(8,128)(2,1)}, bf16[48,2048]{1,0:T(8,128)(2,1)}, bf16[48,2048]{1,0:T(8,128)(2,1)}) custom-call(s32[2]{0:T(128)S(1)} %copy-done.27, s32[8,640]{1,0:T(8,128)S(1)} %copy-done.26, bf16[48,2048]{1,0:T(8,128)(2,1)S(1)} %copy-done.5, bf16[48,2048]{1,0:T(8,128)(2,1)S(1)} %copy-done.17, ...), custom_call_target="tpu_custom_call" | custom-call | flops 805306368 | bytes 16777216 | tf_op jit(solution)/shard_map/tiles/pallas_call | solution.py:234
  44.6 0.8 copy-done.6
  45.3 2.7 %collective-permute-start.7 = (bf16[48,2048]{1,0:T(8,128)(2,1)}, bf16[48,2048]{1,0:T(8,128)(2,1)}, u32[]{:S(2)}, u32[]{:S(2)}) collective-permute-start(bf16[48,2048]{1,0:T(8,128)(2,1)} %get-tuple-element.13), channel_id=1, source_target_pairs={{0,8},{8,0},{16,24},{24,16},{1,9},{9,1},{17,25},{25,17},{2,10},{10... | collective-permute-start | bytes 589832 | tf_op jit(solution)/shard_map/scatter/ppermute | solution.py:18
  48.0 3.5 %collective-permute-start.8 = (bf16[48,2048]{1,0:T(8,128)(2,1)}, bf16[48,2048]{1,0:T(8,128)(2,1)}, u32[]{:S(2)}, u32[]{:S(2)}) collective-permute-start(bf16[48,2048]{1,0:T(8,128)(2,1)} %get-tuple-element.14), channel_id=1, source_target_pairs={{0,16},{8,24},{16,0},{24,8},{1,17},{9,25},{17,1},{25,9},{2,18},{10... | collective-permute-start | bytes 589832 | tf_op jit(solution)/shard_map/scatter/ppermute | solution.py:18
  51.5 0.0 collective-permute-start.9
  51.5 2.3 %start.1.refs_0_ = f32[48,2048]{1,0:T(8,128)} custom-call(f32[48,2048]{1,0:T(8,128)} %current.3, f32[48,2048]{1,0:T(8,128)} %previous.1, f32[48,48]{1,0:T(8,128)} %coupling.1, f32[1,2048]{1,0:T(1,128)} %bitcast.15), custom_call_target="tpu_custom_call" | custom-call | flops 56623104 | bytes 1179648 | tf_op jit(solution)/shard_map/start/pallas_call | solution.py:212
  53.9 2.7 %collective-permute-done.7.refs_2_ = bf16[48,2048]{1,0:T(8,128)(2,1)} collective-permute-done((bf16[48,2048]{1,0:T(8,128)(2,1)}, bf16[48,2048]{1,0:T(8,128)(2,1)}, u32[]{:S(2)}, u32[]{:S(2)}) %collective-permute-start.7) | collective-permute-done | bytes 196640 | tf_op jit(solution)/shard_map/scatter/ppermute | solution.py:18
  56.5 9.6 %collective-permute-done.8.refs_3_ = bf16[48,2048]{1,0:T(8,128)(2,1)} collective-permute-done((bf16[48,2048]{1,0:T(8,128)(2,1)}, bf16[48,2048]{1,0:T(8,128)(2,1)}, u32[]{:S(2)}, u32[]{:S(2)}) %collective-permute-start.8) | collective-permute-done | bytes 196640 | tf_op jit(solution)/shard_map/scatter/ppermute | solution.py:18
  66.1 0.0 collective-permute-done.9.refs_4_
  66.1 0.0 copy-start.3
  66.1 1.0 copy-done.3
  67.1 1.0 copy-done.7
  68.1 2.4 %coefficients.1 = (f32[48,2048]{1,0:T(8,128)S(1)}, f32[32,8,128]{2,1,0:T(8,128)S(1)}) custom-call(f32[48,2048]{1,0:T(8,128)S(1)} %copy-done.3, f32[48,2048]{1,0:T(8,128)S(1)} %copy-done.7, bf16[48,2048]{1,0:T(8,128)(2,1)} %collective-permute-done.7.refs_2_, bf16[48,2048]{1,0:T(8,128)(2,1)} %collective-permute-done.8.refs_3_, ...), custom_call_target="tpu_custom_call" | custom-call | tf_op jit(solution)/shard_map/coefficients/pallas_call | solution.py:260
  70.5 0.0 copy-start.8
  70.5 0.7 copy-done.8
  71.2 14.9 %all_to_all.15 = f32[32,8,128]{2,1,0:T(8,128)} all-to-all(f32[32,8,128]{2,1,0:T(8,128)S(1)} %get-tuple-element.16), channel_id=1, replica_groups=mesh['row'=4,'col'=8] {'row','col'}, dimensions={0} | all-to-all | bytes 262144 | tf_op jit(solution)/shard_map/coefficients/all_to_all | solution.py:267
  86.1 0.9 reduce_sum.18
  87.1 10.0 %all_to_all.16.pieces = f32[32,8,128]{2,1,0:T(8,128)S(1)} all-to-all(f32[32,8,128]{2,1,0:T(8,128)S(1)} %broadcast_in_dim.6), channel_id=1, replica_groups=mesh['row'=4,'col'=8] {'row','col'}, dimensions={0} | all-to-all | bytes 262144 | tf_op jit(solution)/shard_map/coefficients/all_to_all | solution.py:268
  97.1 1.0 copy-done.9
  98.1 1.6 %residual.1 = (f32[48,2048]{1,0:T(8,128)}, f32[48,432]{1,0:T(8,128)S(1)}, f32[24,128]{1,0:T(8,128)S(1)}) custom-call(f32[32,8,128]{2,1,0:T(8,128)S(1)} %all_to_all.16.pieces, f32[48,2048]{1,0:T(8,128)S(1)} %copy-done.9, f32[1,2048]{1,0:T(1,128)S(1)} %bitcast.13, f32[48,2048]{1,0:T(8,128)S(1)} %copy-done.2, f32[384,2048]{1,0:T(8,128)S(1)} %bitcast.10), custom_call_target="tpu_custom_call" | custom-call | tf_op jit(solution)/shard_map/residual/pallas_call | solution.py:271
  99.7 0.6 copy-done.24
  100.3 0.8 broadcast_in_dim.7
  101.1 2.6 %all-to-all-start.2 = ((f32[32,24,128]{2,1,0:T(8,128)}), f32[32,24,128]{2,1,0:T(8,128)S(1)}, u32[]{:S(2)}, u32[]{:S(2)}) async-start(f32[32,24,128]{2,1,0:T(8,128)} %broadcast_in_dim.7), calls=%async_computation.2 | async-start | bytes 786432 | tf_op jit(solution)/shard_map/gram/all_to_all | solution.py:287
  103.7 1.7 %copy.15 = f32[432,48]{1,0:T(8,128)} copy(f32[432,48]{0,1:T(8,128)} %bitcast.11) | data formatting | bytes 165888 | tf_op jit(solution)/shard_map/residual/transpose | solution.py:283
  105.4 11.5 %all-to-all-done.2 = f32[32,24,128]{2,1,0:T(8,128)S(1)} async-done(((f32[32,24,128]{2,1,0:T(8,128)}), f32[32,24,128]{2,1,0:T(8,128)S(1)}, u32[]{:S(2)}, u32[]{:S(2)}) %all-to-all-start.2) | async-done | bytes 393248 | tf_op jit(solution)/shard_map/gram/all_to_all | solution.py:287
  116.9 0.1 fusion
  117.0 0.6 pad_maximum_fusion
  (30 shorter events, 0.1 us)
Async XLA Ops:
  0.6 65.5 %copy-start.2 = (f32[48,2048]{1,0:T(8,128)S(1)}, f32[48,2048]{1,0:T(8,128)}, u32[]{:S(2)}) copy-start(f32[48,2048]{1,0:T(8,128)} %current.3) | copy-start | bytes 1179652
  0.6 65.5 %copy-start.25 = (f32[2048]{0:T(1024)S(1)}, f32[2048]{0:T(1024)}, u32[]{:S(2)}) copy-start(f32[2048]{0:T(1024)} %param.15) | copy-start | bytes 24580
  1.7 19.6 %copy-start.4 = (bf16[48,2048]{1,0:T(8,128)(2,1)}, bf16[48,2048]{1,0:T(8,128)(2,1)S(1)}, u32[]{:S(2)}) copy-start(bf16[48,2048]{1,0:T(8,128)(2,1)S(1)} %convert_element_type.3.refs_0_) | copy-start | bytes 589828
  1.7 9.7 %collective-permute-start.5 = (bf16[48,2048]{1,0:T(8,128)(2,1)S(1)}, bf16[48,2048]{1,0:T(8,128)(2,1)S(1)}, u32[]{:S(2)}, u32[]{:S(2)}) collective-permute-start(bf16[48,2048]{1,0:T(8,128)(2,1)S(1)} %convert_element_type.3.refs_0_), channel_id=1, source_target_pairs={{0,6},{1,7},{2,4},{3,5},{4,2},{5,3},{6,0},{7,1},{8,14},{9,15},{10,... | collective-permute-start | bytes 589832 | tf_op jit(solution)/shard_map/gather/ppermute | solution.py:18
  5.7 9.1 %collective-permute-start.3 = (bf16[48,2048]{1,0:T(8,128)(2,1)S(1)}, bf16[48,2048]{1,0:T(8,128)(2,1)S(1)}, u32[]{:S(2)}, u32[]{:S(2)}) collective-permute-start(bf16[48,2048]{1,0:T(8,128)(2,1)S(1)} %convert_element_type.3.refs_0_), channel_id=1, source_target_pairs={{0,4},{1,5},{2,6},{3,7},{4,0},{5,1},{6,2},{7,3},{8,12},{9,13},{10,... | collective-permute-start | bytes 589832 | tf_op jit(solution)/shard_map/gather/ppermute | solution.py:18
  6.2 9.3 %collective-permute-start.1 = (bf16[48,2048]{1,0:T(8,128)(2,1)S(1)}, bf16[48,2048]{1,0:T(8,128)(2,1)S(1)}, u32[]{:S(2)}, u32[]{:S(2)}) collective-permute-start(bf16[48,2048]{1,0:T(8,128)(2,1)S(1)} %convert_element_type.3.refs_0_), channel_id=1, source_target_pairs={{0,2},{1,3},{2,0},{3,1},{4,6},{5,7},{6,4},{7,5},{8,10},{9,11},{10,... | collective-permute-start | bytes 589832 | tf_op jit(solution)/shard_map/gather/ppermute | solution.py:18
  6.3 13.6 %collective-permute-start = (bf16[48,2048]{1,0:T(8,128)(2,1)S(1)}, bf16[48,2048]{1,0:T(8,128)(2,1)S(1)}, u32[]{:S(2)}, u32[]{:S(2)}) collective-permute-start(bf16[48,2048]{1,0:T(8,128)(2,1)S(1)} %convert_element_type.3.refs_0_), channel_id=1, source_target_pairs={{0,1},{1,0},{2,3},{3,2},{4,5},{5,4},{6,7},{7,6},{8,9},{9,8},{10,11... | collective-permute-start | bytes 589832 | tf_op jit(solution)/shard_map/gather/ppermute | solution.py:18
  11.5 9.1 %collective-permute-start.6 = (bf16[48,2048]{1,0:T(8,128)(2,1)S(1)}, bf16[48,2048]{1,0:T(8,128)(2,1)S(1)}, u32[]{:S(2)}, u32[]{:S(2)}) collective-permute-start(bf16[48,2048]{1,0:T(8,128)(2,1)S(1)} %collective-permute-done.5.refs_6_), channel_id=1, source_target_pairs={{0,1},{1,0},{2,3},{3,2},{4,5},{5,4},{6,7},{7,6},{8,9},{9,8},{10,11... | collective-permute-start | bytes 589832 | tf_op jit(solution)/shard_map/gather/ppermute | solution.py:18
  11.5 0.7 copy-start.10
  14.8 6.5 %collective-permute-start.4 = (bf16[48,2048]{1,0:T(8,128)(2,1)S(1)}, bf16[48,2048]{1,0:T(8,128)(2,1)S(1)}, u32[]{:S(2)}, u32[]{:S(2)}) collective-permute-start(bf16[48,2048]{1,0:T(8,128)(2,1)S(1)} %collective-permute-done.3.refs_4_), channel_id=1, source_target_pairs={{0,1},{1,0},{2,3},{3,2},{4,5},{5,4},{6,7},{7,6},{8,9},{9,8},{10,11... | collective-permute-start | bytes 589832 | tf_op jit(solution)/shard_map/gather/ppermute | solution.py:18
  14.8 0.7 copy-start.12
  15.5 6.4 %collective-permute-start.2 = (bf16[48,2048]{1,0:T(8,128)(2,1)S(1)}, bf16[48,2048]{1,0:T(8,128)(2,1)S(1)}, u32[]{:S(2)}, u32[]{:S(2)}) collective-permute-start(bf16[48,2048]{1,0:T(8,128)(2,1)S(1)} %collective-permute-done.1.refs_2_), channel_id=1, source_target_pairs={{0,1},{1,0},{2,3},{3,2},{4,5},{5,4},{6,7},{7,6},{8,9},{9,8},{10,11... | collective-permute-start | bytes 589832 | tf_op jit(solution)/shard_map/gather/ppermute | solution.py:18
  16.0 0.7 copy-start.14
  19.9 0.7 copy-start.16
  20.6 0.7 copy-start.18
  21.3 0.7 copy-start.20
  22.0 0.7 copy-start.22
  22.7 5.8 %copy-start = (bf16[512,128,128]{2,1,0:T(8,128)(2,1)S(1)}, bf16[512,128,128]{2,1,0:T(8,128)(2,1)}, u32[]{:S(2)}) copy-start(bf16[512,128,128]{2,1,0:T(8,128)(2,1)} %refs_8_.1) | copy-start | bytes 50331652
  28.4 0.9 copy-start.5
  29.4 0.9 copy-start.11
  30.3 0.9 copy-start.13
  31.2 0.9 copy-start.15
  32.1 0.9 copy-start.17
  33.1 0.9 copy-start.19
  34.0 0.9 copy-start.21
  34.9 0.9 copy-start.23
  35.9 0.7 copy-start.26
  36.6 0.6 copy-start.27
  37.2 28.9 %copy-start.1 = (f32[8,48,2048]{2,1,0:T(8,128)S(1)}, f32[8,48,2048]{2,1,0:T(8,128)}, u32[]{:S(2)}) copy-start(f32[8,48,2048]{2,1,0:T(8,128)} %param.13) | copy-start | bytes 9437188
  44.6 0.8 copy-start.6
  45.3 11.2 %collective-permute-start.7 = (bf16[48,2048]{1,0:T(8,128)(2,1)}, bf16[48,2048]{1,0:T(8,128)(2,1)}, u32[]{:S(2)}, u32[]{:S(2)}) collective-permute-start(bf16[48,2048]{1,0:T(8,128)(2,1)} %get-tuple-element.13), channel_id=1, source_target_pairs={{0,8},{8,0},{16,24},{24,16},{1,9},{9,1},{17,25},{25,17},{2,10},{10... | collective-permute-start | bytes 589832 | tf_op jit(solution)/shard_map/scatter/ppermute | solution.py:18
  48.0 18.1 %collective-permute-start.8 = (bf16[48,2048]{1,0:T(8,128)(2,1)}, bf16[48,2048]{1,0:T(8,128)(2,1)}, u32[]{:S(2)}, u32[]{:S(2)}) collective-permute-start(bf16[48,2048]{1,0:T(8,128)(2,1)} %get-tuple-element.14), channel_id=1, source_target_pairs={{0,16},{8,24},{16,0},{24,8},{1,17},{9,25},{17,1},{25,9},{2,18},{10... | collective-permute-start | bytes 589832 | tf_op jit(solution)/shard_map/scatter/ppermute | solution.py:18
  51.5 14.6 %collective-permute-start.9 = (bf16[48,2048]{1,0:T(8,128)(2,1)}, bf16[48,2048]{1,0:T(8,128)(2,1)}, u32[]{:S(2)}, u32[]{:S(2)}) collective-permute-start(bf16[48,2048]{1,0:T(8,128)(2,1)} %get-tuple-element.15), channel_id=1, source_target_pairs={{0,24},{8,16},{16,8},{24,0},{1,25},{9,17},{17,9},{25,1},{2,26},{10... | collective-permute-start | bytes 589832 | tf_op jit(solution)/shard_map/scatter/ppermute | solution.py:18
  66.1 1.0 copy-start.3
  67.1 1.0 copy-start.7
  70.5 0.7 copy-start.8
  97.1 1.0 copy-start.9
  99.7 0.6 copy-start.24
  101.1 15.8 %all-to-all-start.2 = ((f32[32,24,128]{2,1,0:T(8,128)}), f32[32,24,128]{2,1,0:T(8,128)S(1)}, u32[]{:S(2)}, u32[]{:S(2)}) async-start(f32[32,24,128]{2,1,0:T(8,128)} %broadcast_in_dim.7), calls=%async_computation.2 | async-start | bytes 786432 | tf_op jit(solution)/shard_map/gram/all_to_all | solution.py:287

commit v3 on v2

--- a/solution.py
+++ b/solution.py
@@ -8,6 +8,7 @@
 from jax.sharding import PartitionSpec as P
 
 LANES = 128
+CHUNK = 32
 UNROLL = 8
 NT = (((1,), (1,)), ((), ()))
 MIB = 1 << 20
@@ -16,6 +17,15 @@
 def swap(value, axis, mask):
     count = lax.axis_size(axis)
     return lax.ppermute(value, axis, [(i, i ^ mask) for i in range(count)])
+
+
+def spread(value, axis):
+    copies = jnp.broadcast_to(value, (lax.axis_size(axis),) + value.shape)
+    return lax.all_to_all(copies, axis, 0, 0)
+
+
+def total(value, axis):
+    return jnp.sum(spread(value, axis), axis=0)
 
 
 def split(value):
@@ -49,7 +59,17 @@
     )
 
 
-def plan_kernel(row_devs, col_devs, slab_tiles, place, counts, rows, cols, out):
+def plan_kernel(row_devs, col_devs, slab_tiles, place, counts, rows, cols, tiles, out, held, sem):
+    chunks = (counts[0] + CHUNK - 1) // CHUNK
+
+    def tile_copy(k):
+        window = pl.ds(k * CHUNK, CHUNK)
+        return pltpu.make_async_copy(tiles.at[window], held.at[window], sem.at[k])
+
+    @pl.loop(0, chunks)
+    def _(k):
+        tile_copy(k).start()
+
     f32, bf16, i32 = jnp.float32, jnp.bfloat16, jnp.int32
     slots, places = rows.shape[1], out.shape[1]
     targets = row_devs * slab_tiles
@@ -86,6 +106,10 @@
     out[3:4] = jnp.where(valid, found[3:4].astype(i32), targets)
     out[4:8] = jnp.broadcast_to(total.astype(i32), (4, places))
 
+    @pl.loop(0, chunks)
+    def _(k):
+        tile_copy(k).wait()
+
 
 def tiles_kernel(row_devs, col_devs, place, plan, *refs):
     panels = refs[:col_devs]
@@ -112,21 +136,23 @@
 
     @pl.loop(0, (plan[4, 0] + 2 * UNROLL - 1) // (2 * UNROLL))
     def _(g):
-        first = g * 2 * UNROLL
-        parts = []
         for u in range(UNROLL):
-            p = first + 2 * u
-            left = jnp.concatenate([panel(p), panel(p + 1)], axis=1)
-            right = jnp.concatenate([tiles[plan[0, p]], tiles[plan[0, p + 1]]], axis=1)
-            parts.append(mm(left, right, NT))
-        for u in range(UNROLL):
-            acc[plan[3, first + 2 * u]] += parts[u]
+            p = g * 2 * UNROLL + 2 * u
+            left = jnp.concatenate([tiles[plan[0, p]], tiles[plan[0, p + 1]]], axis=1)
+            right = jnp.concatenate([panel(p), panel(p + 1)], axis=1)
+            acc[plan[3, p]] += mm(left, right, NT)
+
+    def turned(t):
+        value = acc[t]
+        width = value.shape[1]
+        spare = jnp.zeros((value.shape[0], LANES - width), jnp.float32)
+        return jnp.concatenate([value, spare], axis=1).T[:width]
 
     for s in range(slab_tiles):
         window = pl.ds(s * LANES, LANES)
-        own[:, window] = acc[row * slab_tiles + s]
+        own[:, window] = turned(row * slab_tiles + s)
         for m in range(1, row_devs):
-            sends[m - 1][:, window] = acc[(row ^ m) * slab_tiles + s].astype(jnp.bfloat16)
+            sends[m - 1][:, window] = turned((row ^ m) * slab_tiles + s).astype(jnp.bfloat16)
 
 
 def coefficient_kernel(cells, pieces, *refs):
@@ -146,7 +172,7 @@
     coef = jnp.concatenate([coef, jnp.zeros((coef.shape[0], spare), jnp.float32)], axis=1)
     out[...] = jnp.zeros_like(out)
     for p, (q, k) in enumerate(blocks(coef.shape)):
-        out[p] = coef[q : q + 8, k : k + LANES]
+        out[p // out.shape[1], p % out.shape[1]] = coef[q : q + 8, k : k + LANES]
 
 
 def residual_kernel(cells, pieces, recurrence, mass, current, stored, residual, coef_out, gram, packed):
@@ -164,6 +190,21 @@
     gram[...] = jnp.zeros_like(gram)
     gram[:, :width] = local[:half]
     gram[:, LANES // 2 : LANES // 2 + width] = local[half:]
+
+
+def after_kernel(value, earlier, out):
+    pass
+
+
+def after(value, earlier):
+    anywhere = pl.BlockSpec(memory_space=pl.ANY)
+    return pl.pallas_call(
+        after_kernel,
+        out_shape=jax.ShapeDtypeStruct(value.shape, value.dtype),
+        in_specs=[anywhere, anywhere],
+        out_specs=anywhere,
+        input_output_aliases={0: 0},
+    )(value, earlier)
 
 
 def vmem(count):
@@ -203,9 +244,25 @@
     with jax.named_scope("gather"):
         rounded = current_block.astype(bf16)
         panels = [rounded] + [None] * (col_devs - 1)
-        for m in range(2, col_devs, 2):
+        for m in range(col_devs - 2, 0, -2):
             panels[m] = swap(rounded, "col", m)
-        for m in range(0, col_devs, 2):
+
+    with jax.named_scope("plan"):
+        targets = row_devs * slab_tiles
+        places = -(-(slots + targets) // LANES) * LANES
+        plan, held = pl.pallas_call(
+            functools.partial(plan_kernel, row_devs, col_devs, slab_tiles),
+            out_shape=[jax.ShapeDtypeStruct((8, places), jnp.int32), pltpu.VMEM(tile_values.shape, bf16)],
+            in_specs=smem(2) + vmem(2) + [pl.BlockSpec(memory_space=pltpu.HBM)],
+            out_specs=vmem(2),
+            scratch_shapes=[pltpu.SemaphoreType.DMA((slots // CHUNK,))],
+            compiler_params=pltpu.CompilerParams(vmem_limit_bytes=8 * MIB),
+            cost_estimate=pl.CostEstimate(flops=4 * slots * slots * targets, bytes_accessed=8192, transcendentals=0),
+        )(place, tile_counts, tile_rows.reshape(1, slots), tile_cols.reshape(1, slots), pltpu.with_memory_space_constraint(tile_values, pltpu.HBM))
+
+    with jax.named_scope("gather"):
+        panels[col_devs - 2] = after(panels[col_devs - 2], plan)
+        for m in range(col_devs - 2, -2, -2):
             panels[m + 1] = swap(panels[m], "col", 1)
 
     with jax.named_scope("start"):
@@ -219,17 +276,6 @@
             ),
         )(current_block, previous_block, previous_coupling, diag)
 
-    with jax.named_scope("plan"):
-        targets = row_devs * slab_tiles
-        places = -(-(slots + targets) // LANES) * LANES
-        plan = pl.pallas_call(
-            functools.partial(plan_kernel, row_devs, col_devs, slab_tiles),
-            out_shape=jax.ShapeDtypeStruct((8, places), jnp.int32),
-            in_specs=smem(2) + vmem(2),
-            out_specs=vmem(1)[0],
-            cost_estimate=pl.CostEstimate(flops=4 * slots * slots * targets, bytes_accessed=8192, transcendentals=0),
-        )(place, tile_counts, tile_rows.reshape(1, slots), tile_cols.reshape(1, slots))
-
     with jax.named_scope("tiles"):
         outs = pl.pallas_call(
             functools.partial(tiles_kernel, row_devs, col_devs),
@@ -238,34 +284,34 @@
             out_specs=vmem(row_devs),
             scratch_shapes=[
                 pltpu.VMEM((col_devs + 1, width, slab_len), bf16),
-                pltpu.VMEM((targets + 1, width, tile_len), f32),
+                pltpu.VMEM((targets + 1, tile_len, width), f32),
                 pltpu.SemaphoreType.DMA((col_devs,)),
             ],
-            compiler_params=pltpu.CompilerParams(vmem_limit_bytes=32 * MIB),
+            compiler_params=pltpu.CompilerParams(vmem_limit_bytes=12 * MIB),
             cost_estimate=pl.CostEstimate(
                 flops=2 * slots * width * tile_len * tile_len,
                 bytes_accessed=2 * slots * tile_len * tile_len,
                 transcendentals=0,
             ),
-        )(place, plan, *panels, tile_values)
+        )(place, plan, *panels, held)
 
     with jax.named_scope("scatter"):
         received = [swap(outs[m], "row", m) for m in range(1, row_devs)]
 
-    devices = row_devs * col_devs
-    both = ("row", "col")
     basis_rows = (stored_count + 1) * width
     padded = (width, -(-basis_rows // LANES) * LANES)
+    share = -(-len(blocks(padded)) // col_devs)
     with jax.named_scope("coefficients"):
         recurrence, partial = pl.pallas_call(
             functools.partial(coefficient_kernel, cells, row_devs),
-            out_shape=[slab, jax.ShapeDtypeStruct((devices, 8, LANES), f32)],
+            out_shape=[slab, jax.ShapeDtypeStruct((col_devs, share, 8, LANES), f32)],
             in_specs=vmem(row_devs + 4),
             out_specs=vmem(2),
             compiler_params=pltpu.CompilerParams(vmem_limit_bytes=24 * MIB),
         )(base, outs[0], *received, mass, current_block, stored)
-        piece = jnp.sum(lax.all_to_all(partial, both, 0, 0), axis=0)
-        pieces = lax.all_to_all(jnp.broadcast_to(piece, partial.shape), both, 0, 0)
+        piece = jnp.sum(lax.all_to_all(partial, "col", 0, 0), axis=0)
+        piece = total(piece, "row")
+        pieces = spread(piece, "col").reshape(-1, 8, LANES)
 
     with jax.named_scope("residual"):
         residual_block, coef, gram = pl.pallas_call(
@@ -283,8 +329,7 @@
         coefficients = coef.T.reshape(stored_count + 1, width, width)
 
     with jax.named_scope("gram"):
-        grams = jnp.broadcast_to(gram, (devices,) + gram.shape)
-        gram = jnp.sum(lax.all_to_all(grams, both, 0, 0), axis=0)
+        gram = total(total(gram, "col"), "row")
         gram = jnp.concatenate(
             [gram[:, :width], gram[:, LANES // 2 : LANES // 2 + width]], axis=0
         )

time: 118 us -> 117 us (level)
  waiting for transfers between devices: 31.5 us -> 16.8 us
  blocking collectives: 24.9 us -> 36.7 us
  Pallas kernels: 15.7 us -> 20 us
  local copies, waits for them, and re-layouts: 27 us -> 23.1 us
  other arithmetic: 3.26 us -> 5.31 us
    all_to_all x2 -> x4, blocking collectives: 24.9 us -> 36.7 us  [the longest x3 26.1 us: spread(): return lax.all_to_all(copies, axis, 0, 0)]
    all_to_all x1, waiting for transfers between devices: 11.5 us -> 3.95 us  [spread(): return lax.all_to_all(copies, axis, 0, 0)]
    ppermute x10, waiting for transfers between devices: 20 us -> 12.9 us  [swap(): return lax.ppermute(value, axis, [(i, i ^ mask) for i in range(count)])]
    unnamed x56 -> x30, local copies, waits for them, and re-layouts: 24.4 us -> 19.3 us
    pallas_call x1, Pallas kernels: 1.98 us -> 4.36 us  [local(): pl.pallas_call(functools.partial(plan_kernel, row_devs, col_devs, slab_ti...]
    pallas_call x1, Pallas kernels: 7.37 us -> 9.38 us  [local(): pl.pallas_call(functools.partial(tiles_kernel, row_devs, col_devs), out_s...]
    reduce_sum x2 -> x4, other arithmetic: 0.98 us -> 2.93 us  [the longest x1 1.5 us: local(): piece = jnp.sum(lax.all_to_all(partial, 'col', 0, 0), axis=0)]
    ppermute x10, starting transfers between devices: 11.3 us -> 9.78 us  [swap(): return lax.ppermute(value, axis, [(i, i ^ mask) for i in range(count)])]
  transfers between devices with their start and end apart: 11 -> 11, of which waited for: 5 -> 6; matrix products, arithmetic and copies ran while one was open for 2% -> 2% of each run, Pallas kernels for 4% -> 6%
where the time goes in v3:
time: 117 us; the launch traced here: 116 us
  blocking collectives  36.7 us (31%)
  local copies, waits for them, and re-layouts  23.1 us (20%)
  Pallas kernels  20 us (17%)
  waiting for transfers between devices  16.8 us (14%)
  starting transfers between devices  13.1 us (11%)
  other arithmetic  5.31 us (5%)
  between operations  1.39 us (1%)
    all_to_all x3, blocking collectives, spread(): return lax.all_to_all(copies, axis, 0, 0)  26.1 us
    unnamed x30, local copies, waits for them, and re-layouts  19.3 us
    ppermute x10, waiting for transfers between devices, swap(): return lax.ppermute(value, axis, [(i, i ^ mask) for i in range(count)])  12.9 us
    all_to_all x1, blocking collectives, local(): piece = jnp.sum(lax.all_to_all(partial, 'col', 0, 0), axis=0)  10.6 us
    ppermute x10, starting transfers between devices, swap(): return lax.ppermute(value, axis, [(i, i ^ mask) for i in range(count)])  9.78 us
    pallas_call x1, Pallas kernels, local(): pl.pallas_call(functools.partial(tiles_kernel, row_devs, col_devs), out_s...  9.38 us
    pallas_call x1, Pallas kernels, local(): pl.pallas_call(functools.partial(plan_kernel, row_devs, col_devs, slab_ti...  4.36 us
    all_to_all x1, waiting for transfers between devices, spread(): return lax.all_to_all(copies, axis, 0, 0)  3.95 us
  transfers between devices with their start and end apart: 11, of which 6 were waited for; matrix products, arithmetic and copies ran while one was open for 2% of the time, Pallas kernels for 6%

profile of v3, /device:TPU:0, one launch (start us, length us, event | category | flops | bytes accessed | tf_op | source)
XLA Modules:
  0.0 116.4 jit_solution(13849953883444724285)
XLA Ops:
  0.6 1.7 %convert_element_type.3.refs_0_ = bf16[48,2048]{1,0:T(8,128)(2,1)} convert(f32[48,2048]{1,0:T(8,128)} %current.3) | non-fusion elementwise | flops 98304 | bytes 589824 | tf_op jit(solution)/shard_map/gather/convert_element_type | solution.py:245
  2.3 3.9 %collective-permute-start.5 = (bf16[48,2048]{1,0:T(8,128)(2,1)}, bf16[48,2048]{1,0:T(8,128)(2,1)}, u32[]{:S(2)}, u32[]{:S(2)}) collective-permute-start(bf16[48,2048]{1,0:T(8,128)(2,1)} %convert_element_type.3.refs_0_), channel_id=1, source_target_pairs={{0,6},{1,7},{2,4},{3,5},{4,2},{5,3},{6,0},{7,1},{8,14},{9,15},{10,... | collective-permute-start | bytes 589832 | tf_op jit(solution)/shard_map/gather/ppermute | solution.py:19
  6.2 0.5 collective-permute-start.1
  6.8 0.0 collective-permute-start.3
  6.8 0.0 collective-permute-start
  7.4 0.1 pad_add_fusion.place
  7.5 0.0 copy-start.13
  7.5 0.7 copy-done.13
  8.2 0.0 copy-start.14
  8.2 0.7 copy-done.14
  8.9 0.0 copy-start.2
  8.9 0.0 copy-start.3
  8.9 4.4 %plan.1 = (s32[8,640]{1,0:T(8,128)S(1)}, bf16[512,128,128]{2,1,0:T(8,128)(2,1)S(1)}) custom-call(s32[2]{0:T(128)S(1)} %pad_add_fusion.place, s32[1]{0:T(128)S(6)} %copy.18.counts, s32[1,512]{1,0:T(1,128)S(1)} %bitcast.16, s32[1,512]{1,0:T(1,128)S(1)} %bitcast.17, bf16[512,128,128]{2,1,0:T(8,128)(2,1)} %tiles.2), custom_call_target="tpu_custom_call" | custom-call | flops 67108864 | bytes 8192 | tf_op jit(solution)/shard_map/plan/pallas_call | solution.py:253
  13.3 0.0 copy-start
  13.3 5.7 %copy-done = bf16[512,128,128]{2,1,0:T(8,128)(2,1)} copy-done((bf16[512,128,128]{2,1,0:T(8,128)(2,1)}, bf16[512,128,128]{2,1,0:T(8,128)(2,1)S(1)}, u32[]{:S(2)}) %copy-start) | copy-done | bytes 16777240
  19.0 0.6 copy-done.10
  19.6 0.0 collective-permute-done.5.value
  19.6 0.0 collective-permute-start.6
  19.6 0.0 collective-permute-done.1.refs_2_
  19.6 0.5 collective-permute-start.2
  20.1 0.0 collective-permute-done.3.refs_4_
  20.1 0.1 collective-permute-start.4
  20.2 0.0 collective-permute-done.refs_1_
  20.2 1.1 collective-permute-done.6.refs_7_
  21.3 0.3 collective-permute-done.2.refs_3_
  21.5 0.3 collective-permute-done.4.refs_5_
  21.8 5.8 %copy-done.1 = bf16[512,128,128]{2,1,0:T(8,128)(2,1)S(1)} copy-done((bf16[512,128,128]{2,1,0:T(8,128)(2,1)S(1)}, bf16[512,128,128]{2,1,0:T(8,128)(2,1)}, u32[]{:S(2)}) %copy-start.1) | copy-done | bytes 16777240
  27.6 0.7 copy-done.11
  28.3 9.4 %tiles.3 = (f32[48,2048]{1,0:T(8,128)S(1)}, bf16[48,2048]{1,0:T(8,128)(2,1)}, bf16[48,2048]{1,0:T(8,128)(2,1)}, bf16[48,2048]{1,0:T(8,128)(2,1)}) custom-call(s32[2]{0:T(128)S(1)} %pad_add_fusion.place, s32[8,640]{1,0:T(8,128)S(1)} %copy-done.11, bf16[48,2048]{1,0:T(8,128)(2,1)} %convert_element_type.3.refs_0_, ...), custom_call_target="tpu_custom_call" | custom-call | flops 805306368 | bytes 16777216 | tf_op jit(solution)/shard_map/tiles/pallas_call | solution.py:280
  37.7 0.0 copy-start.5
  37.7 0.7 copy-done.5
  38.5 0.8 collective-permute-start.7
  39.2 2.6 %collective-permute-start.8 = (bf16[48,2048]{1,0:T(8,128)(2,1)}, bf16[48,2048]{1,0:T(8,128)(2,1)}, u32[]{:S(2)}, u32[]{:S(2)}) collective-permute-start(bf16[48,2048]{1,0:T(8,128)(2,1)} %get-tuple-element.18), channel_id=1, source_target_pairs={{0,16},{8,24},{16,0},{24,8},{1,17},{9,25},{17,1},{25,9},{2,18},{10... | collective-permute-start | bytes 589832 | tf_op jit(solution)/shard_map/scatter/ppermute | solution.py:19
  41.8 1.4 %collective-permute-start.9 = (bf16[48,2048]{1,0:T(8,128)(2,1)}, bf16[48,2048]{1,0:T(8,128)(2,1)}, u32[]{:S(2)}, u32[]{:S(2)}) collective-permute-start(bf16[48,2048]{1,0:T(8,128)(2,1)} %get-tuple-element.19), channel_id=1, source_target_pairs={{0,24},{8,16},{16,8},{24,0},{1,25},{9,17},{17,9},{25,1},{2,26},{10... | collective-permute-start | bytes 589832 | tf_op jit(solution)/shard_map/scatter/ppermute | solution.py:19
  43.2 2.4 %start.1.refs_0_ = f32[48,2048]{1,0:T(8,128)} custom-call(f32[48,2048]{1,0:T(8,128)} %current.3, f32[48,2048]{1,0:T(8,128)} %previous.1, f32[48,48]{1,0:T(8,128)} %coupling.1, f32[1,2048]{1,0:T(1,128)} %bitcast.19), custom_call_target="tpu_custom_call" | custom-call | flops 56623104 | bytes 1179648 | tf_op jit(solution)/shard_map/start/pallas_call | solution.py:269
  45.6 4.9 %collective-permute-done.7.refs_2_ = bf16[48,2048]{1,0:T(8,128)(2,1)} collective-permute-done((bf16[48,2048]{1,0:T(8,128)(2,1)}, bf16[48,2048]{1,0:T(8,128)(2,1)}, u32[]{:S(2)}, u32[]{:S(2)}) %collective-permute-start.7) | collective-permute-done | bytes 196640 | tf_op jit(solution)/shard_map/scatter/ppermute | solution.py:19
  50.5 0.0 collective-permute-done.8.refs_3_
  50.5 6.4 %collective-permute-done.9.refs_4_ = bf16[48,2048]{1,0:T(8,128)(2,1)} collective-permute-done((bf16[48,2048]{1,0:T(8,128)(2,1)}, bf16[48,2048]{1,0:T(8,128)(2,1)}, u32[]{:S(2)}, u32[]{:S(2)}) %collective-permute-start.9) | collective-permute-done | bytes 196640 | tf_op jit(solution)/shard_map/scatter/ppermute | solution.py:19
  56.8 0.0 copy-done.2
  56.8 0.0 copy-done.3
  56.8 0.0 copy-done.12
  56.9 0.0 copy-start.4
  56.9 1.0 copy-done.4
  57.9 1.0 copy-done.6
  58.8 2.3 %coefficients.1 = (f32[48,2048]{1,0:T(8,128)S(1)}, f32[8,3,8,128]{3,2,1,0:T(8,128)S(1)}) custom-call(f32[48,2048]{1,0:T(8,128)S(1)} %copy-done.4, f32[48,2048]{1,0:T(8,128)S(1)} %copy-done.6, bf16[48,2048]{1,0:T(8,128)(2,1)} %collective-permute-done.7.refs_2_, bf16[48,2048]{1,0:T(8,128)(2,1)} %collective-permute-done.8.refs_3_, ...), custom_call_target="tpu_custom_call" | custom-call | tf_op jit(solution)/shard_map/coefficients/pallas_call | solution.py:305
  61.2 0.0 copy-start.7
  61.2 0.7 copy-done.7
  61.9 10.6 %all_to_all.25 = f32[8,3,8,128]{3,2,1,0:T(8,128)} all-to-all(f32[8,3,8,128]{3,2,1,0:T(8,128)S(1)} %get-tuple-element.20), channel_id=1, replica_groups=mesh['row'=4,'col'=8] {'col'}, dimensions={0} | all-to-all | bytes 196608 | tf_op jit(solution)/shard_map/coefficients/all_to_all | solution.py:312
  72.5 1.5 %reduce_sum.36 = f32[3,8,128]{2,1,0:T(8,128)} reduce(f32[8,3,8,128]{3,2,1,0:T(8,128)} %all_to_all.25, f32[]{:T(128)} %constant.9.clone.1), dimensions={0}, to_apply=%region_0.0 | reduce | flops 21504 | bytes 110596 | tf_op jit(solution)/shard_map/coefficients/reduce_sum | solution.py:312
  74.0 0.7 broadcast_in_dim.12
  74.7 11.0 %all_to_all.26 = f32[4,3,8,128]{3,2,1,0:T(8,128)} all-to-all(f32[4,3,8,128]{3,2,1,0:T(8,128)S(1)} %broadcast_in_dim.12), channel_id=1, replica_groups=mesh['row'=4,'col'=8] {'row'}, dimensions={0} | all-to-all | bytes 98304 | tf_op jit(solution)/shard_map/coefficients/all_to_all | solution.py:24
  85.7 1.4 %reduce_sum.37 = f32[3,8,128]{2,1,0:T(8,128)} reduce(f32[4,3,8,128]{3,2,1,0:T(8,128)} %all_to_all.26, f32[]{:T(128)} %constant.9.clone.1), dimensions={0}, to_apply=%region_1.0 | reduce | flops 9216 | bytes 61444 | tf_op jit(solution)/shard_map/coefficients/reduce_sum | solution.py:28
  87.1 0.7 broadcast_in_dim.13
  87.8 7.6 %all_to_all.27 = f32[8,3,8,128]{3,2,1,0:T(8,128)S(1)} all-to-all(f32[8,3,8,128]{3,2,1,0:T(8,128)S(1)} %broadcast_in_dim.13), channel_id=1, replica_groups=mesh['row'=4,'col'=8] {'col'}, dimensions={0} | all-to-all | bytes 196608 | tf_op jit(solution)/shard_map/coefficients/all_to_all | solution.py:24
  95.4 1.0 copy-done.8
  96.3 1.5 %residual.1 = (f32[48,2048]{1,0:T(8,128)}, f32[48,432]{1,0:T(8,128)S(1)}, f32[24,128]{1,0:T(8,128)S(1)}) custom-call(f32[24,8,128]{2,1,0:T(8,128)S(1)} %bitcast.12, f32[48,2048]{1,0:T(8,128)S(1)} %copy-done.8, f32[1,2048]{1,0:T(1,128)S(1)} %bitcast.15, f32[48,2048]{1,0:T(8,128)S(1)} %copy-done.3, f32[384,2048]{1,0:T(8,128)S(1)} %bitcast.11), custom_call_target="tpu_custom_call" | custom-call | tf_op jit(solution)/shard_map/residual/pallas_call | solution.py:317
  97.9 0.6 copy-done.9
  98.5 7.6 %all_to_all.28 = f32[8,24,128]{2,1,0:T(8,128)S(1)} all-to-all(f32[8,24,128]{2,1,0:T(8,128)S(1)} %broadcast_in_dim.14), channel_id=1, replica_groups=mesh['row'=4,'col'=8] {'col'}, dimensions={0} | all-to-all | bytes 196608 | tf_op jit(solution)/shard_map/gram/all_to_all | solution.py:24
  106.1 0.6 broadcast_in_dim.15
  106.7 3.3 %all-to-all-start.4 = ((f32[4,24,128]{2,1,0:T(8,128)}), f32[4,24,128]{2,1,0:T(8,128)S(1)}, u32[]{:S(2)}, u32[]{:S(2)}) async-start(f32[4,24,128]{2,1,0:T(8,128)} %broadcast_in_dim.15), calls=%async_computation.4 | async-start | bytes 98304 | tf_op jit(solution)/shard_map/gram/all_to_all | solution.py:24
  110.0 1.7 %copy.16 = f32[432,48]{1,0:T(8,128)} copy(f32[432,48]{0,1:T(8,128)} %bitcast.13) | data formatting | bytes 165888 | tf_op jit(solution)/shard_map/residual/transpose | solution.py:329
  111.7 4.0 %all-to-all-done.4 = f32[4,24,128]{2,1,0:T(8,128)S(1)} async-done(((f32[4,24,128]{2,1,0:T(8,128)}), f32[4,24,128]{2,1,0:T(8,128)S(1)}, u32[]{:S(2)}, u32[]{:S(2)}) %all-to-all-start.4) | async-done | bytes 49184 | tf_op jit(solution)/shard_map/gram/all_to_all | solution.py:24
  115.7 0.1 fusion
  115.8 0.6 pad_maximum_fusion
  (11 shorter events, 0.0 us)
Async XLA Ops:
  2.3 17.3 %collective-permute-start.5 = (bf16[48,2048]{1,0:T(8,128)(2,1)}, bf16[48,2048]{1,0:T(8,128)(2,1)}, u32[]{:S(2)}, u32[]{:S(2)}) collective-permute-start(bf16[48,2048]{1,0:T(8,128)(2,1)} %convert_element_type.3.refs_0_), channel_id=1, source_target_pairs={{0,6},{1,7},{2,4},{3,5},{4,2},{5,3},{6,0},{7,1},{8,14},{9,15},{10,... | collective-permute-start | bytes 589832 | tf_op jit(solution)/shard_map/gather/ppermute | solution.py:19
  6.2 13.4 %collective-permute-start.1 = (bf16[48,2048]{1,0:T(8,128)(2,1)}, bf16[48,2048]{1,0:T(8,128)(2,1)}, u32[]{:S(2)}, u32[]{:S(2)}) collective-permute-start(bf16[48,2048]{1,0:T(8,128)(2,1)} %convert_element_type.3.refs_0_), channel_id=1, source_target_pairs={{0,2},{1,3},{2,0},{3,1},{4,6},{5,7},{6,4},{7,5},{8,10},{9,11},{10,... | collective-permute-start | bytes 589832 | tf_op jit(solution)/shard_map/gather/ppermute | solution.py:19
  6.8 13.4 %collective-permute-start.3 = (bf16[48,2048]{1,0:T(8,128)(2,1)}, bf16[48,2048]{1,0:T(8,128)(2,1)}, u32[]{:S(2)}, u32[]{:S(2)}) collective-permute-start(bf16[48,2048]{1,0:T(8,128)(2,1)} %convert_element_type.3.refs_0_), channel_id=1, source_target_pairs={{0,4},{1,5},{2,6},{3,7},{4,0},{5,1},{6,2},{7,3},{8,12},{9,13},{10,... | collective-permute-start | bytes 589832 | tf_op jit(solution)/shard_map/gather/ppermute | solution.py:19
  6.8 13.4 %collective-permute-start = (bf16[48,2048]{1,0:T(8,128)(2,1)}, bf16[48,2048]{1,0:T(8,128)(2,1)}, u32[]{:S(2)}, u32[]{:S(2)}) collective-permute-start(bf16[48,2048]{1,0:T(8,128)(2,1)} %convert_element_type.3.refs_0_), channel_id=1, source_target_pairs={{0,1},{1,0},{2,3},{3,2},{4,5},{5,4},{6,7},{7,6},{8,9},{9,8},{10,11... | collective-permute-start | bytes 589832 | tf_op jit(solution)/shard_map/gather/ppermute | solution.py:19
  7.5 0.7 copy-start.13
  8.2 0.7 copy-start.14
  8.9 48.0 %copy-start.2 = (f32[8,48,2048]{2,1,0:T(8,128)S(1)}, f32[8,48,2048]{2,1,0:T(8,128)}, u32[]{:S(2)}) copy-start(f32[8,48,2048]{2,1,0:T(8,128)} %param.13) | copy-start | bytes 9437188
  8.9 48.0 %copy-start.3 = (f32[48,2048]{1,0:T(8,128)S(1)}, f32[48,2048]{1,0:T(8,128)}, u32[]{:S(2)}) copy-start(f32[48,2048]{1,0:T(8,128)} %current.3) | copy-start | bytes 1179652
  8.9 48.0 %copy-start.12 = (f32[2048]{0:T(1024)S(1)}, f32[2048]{0:T(1024)}, u32[]{:S(2)}) copy-start(f32[2048]{0:T(1024)} %param.15) | copy-start | bytes 24580
  13.3 5.7 %copy-start = (bf16[512,128,128]{2,1,0:T(8,128)(2,1)}, bf16[512,128,128]{2,1,0:T(8,128)(2,1)S(1)}, u32[]{:S(2)}) copy-start(bf16[512,128,128]{2,1,0:T(8,128)(2,1)S(1)} %get-tuple-element.15.refs_8_) | copy-start | bytes 50331652
  19.0 0.6 copy-start.10
  19.6 1.7 %collective-permute-start.6 = (bf16[48,2048]{1,0:T(8,128)(2,1)}, bf16[48,2048]{1,0:T(8,128)(2,1)S(1)}, u32[]{:S(2)}, u32[]{:S(2)}) collective-permute-start(bf16[48,2048]{1,0:T(8,128)(2,1)} %gather.1.refs_6_), channel_id=1, source_target_pairs={{0,1},{1,0},{2,3},{3,2},{4,5},{5,4},{6,7},{7,6},{8,9},{9,8},{10,11... | collective-permute-start | bytes 589832 | tf_op jit(solution)/shard_map/gather/ppermute | solution.py:19
  19.6 1.9 %collective-permute-start.2 = (bf16[48,2048]{1,0:T(8,128)(2,1)}, bf16[48,2048]{1,0:T(8,128)(2,1)S(1)}, u32[]{:S(2)}, u32[]{:S(2)}) collective-permute-start(bf16[48,2048]{1,0:T(8,128)(2,1)} %collective-permute-done.1.refs_2_), channel_id=1, source_target_pairs={{0,1},{1,0},{2,3},{3,2},{4,5},{5,4},{6,7},{7,6},{8,9},{9,8},{10,11... | collective-permute-start | bytes 589832 | tf_op jit(solution)/shard_map/gather/ppermute | solution.py:19
  20.1 1.7 %collective-permute-start.4 = (bf16[48,2048]{1,0:T(8,128)(2,1)}, bf16[48,2048]{1,0:T(8,128)(2,1)S(1)}, u32[]{:S(2)}, u32[]{:S(2)}) collective-permute-start(bf16[48,2048]{1,0:T(8,128)(2,1)} %collective-permute-done.3.refs_4_), channel_id=1, source_target_pairs={{0,1},{1,0},{2,3},{3,2},{4,5},{5,4},{6,7},{7,6},{8,9},{9,8},{10,11... | collective-permute-start | bytes 589832 | tf_op jit(solution)/shard_map/gather/ppermute | solution.py:19
  21.8 5.8 %copy-start.1 = (bf16[512,128,128]{2,1,0:T(8,128)(2,1)S(1)}, bf16[512,128,128]{2,1,0:T(8,128)(2,1)}, u32[]{:S(2)}) copy-start(bf16[512,128,128]{2,1,0:T(8,128)(2,1)} %copy-done) | copy-start | bytes 50331652
  27.6 0.7 copy-start.11
  37.7 0.8 copy-start.5
  38.5 12.0 %collective-permute-start.7 = (bf16[48,2048]{1,0:T(8,128)(2,1)}, bf16[48,2048]{1,0:T(8,128)(2,1)}, u32[]{:S(2)}, u32[]{:S(2)}) collective-permute-start(bf16[48,2048]{1,0:T(8,128)(2,1)} %get-tuple-element.17), channel_id=1, source_target_pairs={{0,8},{8,0},{16,24},{24,16},{1,9},{9,1},{17,25},{25,17},{2,10},{10... | collective-permute-start | bytes 589832 | tf_op jit(solution)/shard_map/scatter/ppermute | solution.py:19
  39.2 11.2 %collective-permute-start.8 = (bf16[48,2048]{1,0:T(8,128)(2,1)}, bf16[48,2048]{1,0:T(8,128)(2,1)}, u32[]{:S(2)}, u32[]{:S(2)}) collective-permute-start(bf16[48,2048]{1,0:T(8,128)(2,1)} %get-tuple-element.18), channel_id=1, source_target_pairs={{0,16},{8,24},{16,0},{24,8},{1,17},{9,25},{17,1},{25,9},{2,18},{10... | collective-permute-start | bytes 589832 | tf_op jit(solution)/shard_map/scatter/ppermute | solution.py:19
  41.8 15.0 %collective-permute-start.9 = (bf16[48,2048]{1,0:T(8,128)(2,1)}, bf16[48,2048]{1,0:T(8,128)(2,1)}, u32[]{:S(2)}, u32[]{:S(2)}) collective-permute-start(bf16[48,2048]{1,0:T(8,128)(2,1)} %get-tuple-element.19), channel_id=1, source_target_pairs={{0,24},{8,16},{16,8},{24,0},{1,25},{9,17},{17,9},{25,1},{2,26},{10... | collective-permute-start | bytes 589832 | tf_op jit(solution)/shard_map/scatter/ppermute | solution.py:19
  56.9 1.0 copy-start.4
  57.9 1.0 copy-start.6
  61.2 0.7 copy-start.7
  95.4 1.0 copy-start.8
  97.9 0.6 copy-start.9
  106.7 8.9 %all-to-all-start.4 = ((f32[4,24,128]{2,1,0:T(8,128)}), f32[4,24,128]{2,1,0:T(8,128)S(1)}, u32[]{:S(2)}, u32[]{:S(2)}) async-start(f32[4,24,128]{2,1,0:T(8,128)} %broadcast_in_dim.15), calls=%async_computation.4 | async-start | bytes 98304 | tf_op jit(solution)/shard_map/gram/all_to_all | solution.py:24

commit v4 on v3

v4 whole, which is shorter than its diff:
```python
import functools

import jax
import jax.numpy as jnp
from jax import lax
from jax.experimental import pallas as pl
from jax.experimental.pallas import tpu as pltpu
from jax.sharding import PartitionSpec as P

LANES = 128
CHUNK = 32
UNROLL = 4
NT = (((1,), (1,)), ((), ()))
MIB = 1 << 20


def swap(value, axis, mask):
    count = lax.axis_size(axis)
    return lax.ppermute(value, axis, [(i, i ^ mask) for i in range(count)])


def bits(axis):
    return [1 << i for i in range(lax.axis_size(axis).bit_length() - 1)]


def total(value, axis, masks):
    for m in masks:
        value = value + swap(value, axis, m)
    return value


def split(value):
    high = value.astype(jnp.bfloat16)
    low = (value - high.astype(jnp.float32)).astype(jnp.bfloat16)
    return high, low


def mm(a, b, dims=(((1,), (0,)), ((), ()))):
    return lax.dot_general(a, b, dims, preferred_element_type=jnp.float32)


def dot_split(a, b, dims=(((1,), (0,)), ((), ()))):
    rows = a.shape[0]
    a_high, a_low = split(a)
    b_high, b_low = split(b)
    both = mm(jnp.concatenate([a_high, a_low], axis=0), b_high, dims)
    return both[:rows] + both[rows:] + mm(a_high, b_low, dims)


def blocks(shape):
    return [(q, k) for q in range(0, shape[0], 8) for k in range(0, shape[1], LANES)]


def plan_kernel(row_devs, col_devs, slab_tiles, place, counts, rows, cols, tiles, out, held, sem):
    chunks = (counts[0] + CHUNK - 1) // CHUNK

    def tile_copy(k):
        window = pl.ds(k * CHUNK, CHUNK)
        return pltpu.make_async_copy(tiles.at[window], held.at[window], sem.at[k])

    @pl.loop(0, chunks)
    def _(k):
        tile_copy(k).start()

    f32, bf16, i32 = jnp.float32, jnp.bfloat16, jnp.int32
    slots, places = rows.shape[1], out.shape[1]
    targets = row_devs * slab_tiles
    bins = 2 * targets

    def iota(shape, dim):
        return lax.broadcasted_iota(i32, shape, dim)

    slot = iota((1, slots), 1)
    occupied = slot < counts[0]
    row = rows[...]
    row_owner = jnp.floor(row.astype(f32) * (1.0 / slab_tiles)).astype(i32)
    col_f = cols[...].astype(f32)
    source_f = jnp.floor(col_f * (1.0 / slab_tiles))
    source = source_f.astype(i32) ^ place[1]
    tile_f = col_f - slab_tiles * source_f
    far = row_devs - 1 - (row_owner ^ place[0])
    late_bin = targets + far * slab_tiles + row - row_owner * slab_tiles
    bin_of = jnp.where(occupied, jnp.where(source < 2, row, late_bin), -1)
    member = (iota((bins, slots), 0) == bin_of).astype(f32)
    member_bf = member.astype(bf16)
    earlier = (iota((slots, slots), 0) < iota((slots, slots), 1)).astype(f32).astype(bf16)
    rank = jnp.sum(member * mm(member_bf, earlier), axis=0, keepdims=True)
    sizes = mm(jnp.ones((8, slots), bf16), member_bf, NT)[:1]
    sizes = 2.0 * jnp.floor(0.5 * (sizes + 1.0))
    before = (iota((bins, bins), 1) < iota((bins, bins), 0)).astype(f32)
    begin = jnp.sum(before * sizes, axis=1, keepdims=True)
    position = jnp.sum(member * begin, axis=0, keepdims=True) + rank
    position = jnp.where(occupied, position.astype(i32), -1)
    chosen = (iota((places, slots), 0) == position).astype(f32).astype(bf16)
    slot_f = slot.astype(f32)
    slot_high = jnp.floor(slot_f * (1.0 / 16.0))
    facts = [slot_high, slot_f - 16.0 * slot_high, source.astype(f32), tile_f, row.astype(f32), jnp.ones((1, slots), f32)]
    facts = jnp.concatenate(facts + [jnp.zeros((2, slots), f32)], axis=0).astype(bf16)
    found = mm(facts, chosen, NT)
    valid = found[5:6] > 0.5
    out[0:1] = (16.0 * found[0:1] + found[1:2]).astype(i32)
    out[1:2] = jnp.where(valid, found[2:3].astype(i32), col_devs)
    out[2:3] = found[3:4].astype(i32)
    out[3:4] = found[4:5].astype(i32)
    out[4:8] = jnp.zeros((4, places), i32)
    phases = out.shape[0] - 8
    phase = iota((phases, bins), 0)
    edge = jnp.where(phase > 0, targets + (phase - 1) * slab_tiles, 0)
    edges = jnp.sum((iota((phases, bins), 1) < edge).astype(f32) * sizes, axis=1, keepdims=True)
    out[8:] = jnp.broadcast_to(edges.astype(i32), (phases, places))

    @pl.loop(0, chunks)
    def _(k):
        tile_copy(k).wait()


def add_products(plan, phase, first_row, spare_row, tiles, panel_buf, acc):
    begin, end = plan[8 + phase, 0], plan[9 + phase, 0]

    def panel(p):
        where = pl.multiple_of(plan[2, p] * LANES, LANES)
        return panel_buf[plan[1, p], :, pl.ds(where, LANES)]

    @pl.loop(0, (end - begin + 2 * UNROLL - 1) // (2 * UNROLL))
    def _(g):
        first = begin + g * 2 * UNROLL
        parts = []
        for u in range(UNROLL):
            p = first + 2 * u
            left = jnp.concatenate([panel(p), panel(p + 1)], axis=1)
            right = jnp.concatenate([tiles[plan[0, p]], tiles[plan[0, p + 1]]], axis=1)
            parts.append(mm(left, right, NT))
        for u in range(UNROLL):
            p = first + 2 * u
            a = jnp.where(p < end, plan[3, p] - first_row, spare_row)
            acc[a] += parts[u]


def load_panels(panels, panel_buf, sem):
    copies = [pltpu.make_async_copy(ref, panel_buf.at[m], sem.at[m]) for m, ref in enumerate(panels)]
    for copy in copies:
        copy.start()
    zero = panel_buf.shape[0] - 1
    panel_buf[zero, :, :LANES] = jnp.zeros((panel_buf.shape[1], LANES), jnp.bfloat16)
    return copies


def early_kernel(plan, own_panel, near_panel, tiles, acc, panel_buf, sem):
    copies = load_panels((own_panel, near_panel), panel_buf, sem)
    acc[...] = jnp.zeros_like(acc)
    for copy in copies:
        copy.wait()
    add_products(plan, 0, 0, acc.shape[0] - 1, tiles, panel_buf, acc)


def first_late_kernel(mask, phase, place, plan, *refs):
    panels = refs[:-6]
    tiles, early, send, panel_buf, acc, sem = refs[-6:]
    copies = load_panels(panels, panel_buf, sem)
    late_part(mask, phase, place, plan, tiles, early, panel_buf, acc, copies)
    put(send, acc)


def late_kernel(masks, place, plan, panel_buf, tiles, early, *refs):
    acc = refs[-1]
    for phase, (mask, send) in enumerate(zip(masks, refs), 2):
        late_part(mask, phase, place, plan, tiles, early, panel_buf, acc, ())
        put(send, acc)


def own_kernel(phase, place, plan, panel_buf, tiles, early, received, current, previous, coupling, diag, base, acc):
    late_part(0, phase, place, plan, tiles, early, panel_buf, acc, ())
    put(base, acc)
    base[...] += received[...].astype(jnp.float32) + diag[...] * current[...] - jnp.dot(
        coupling[...],
        previous[...],
        precision=lax.Precision.HIGHEST,
        preferred_element_type=jnp.float32,
    )


def late_part(mask, phase, place, plan, tiles, early, panel_buf, acc, copies):
    slab_tiles = acc.shape[0] - 1
    first_row = (place[0] ^ mask) * slab_tiles
    for s in range(slab_tiles):
        acc[s] = early[first_row + s]
    for copy in copies:
        copy.wait()
    add_products(plan, phase, first_row, slab_tiles, tiles, panel_buf, acc)


def put(out, acc):
    for s in range(acc.shape[0] - 1):
        out[:, s * LANES : (s + 1) * LANES] = acc[s].astype(out.dtype)


def coefficient_kernel(cells, received_count, place, base, *refs):
    received = refs[:received_count]
    mass, current, stored, recurrence, keep, give, halves = refs[received_count:]
    total = base[...]
    for ref in received:
        total = total + ref[...].astype(jnp.float32)
    recurrence[...] = total
    weighted = total * (mass[...] * (1.0 / cells))
    basis = jnp.concatenate([current[...], stored[...]], axis=0)
    coef = dot_split(weighted, basis, NT)
    spare = -coef.shape[1] % LANES
    coef = jnp.concatenate([coef, jnp.zeros((coef.shape[0], spare), jnp.float32)], axis=1)
    halves[...] = jnp.zeros_like(halves)
    for p, (q, k) in enumerate(blocks(coef.shape)):
        halves[p // halves.shape[1], p % halves.shape[1]] = coef[q : q + 8, k : k + LANES]
    core = place[1] & 1
    keep[...] = halves[core]
    give[...] = halves[1 - core]


def residual_kernel(
    cells, place, mine, other, recurrence, mass, current, stored, residual, coef_out, gram, halves, packed
):
    width = recurrence.shape[0]
    core = place[1] & 1
    halves[core] = mine[...]
    halves[1 - core] = other[...]
    for p, (q, k) in enumerate(blocks(packed.shape)):
        packed[q : q + 8, k : k + LANES] = halves[p // halves.shape[1], p % halves.shape[1]]
    coef = packed[...]
    basis = jnp.concatenate([current[...], stored[...]], axis=0)
    coef = coef[:, : basis.shape[0]]
    coef_out[...] = coef
    value = recurrence[...] - dot_split(coef, basis)
    residual[...] = value
    local = dot_split(value * (mass[...] * (1.0 / cells)), value, NT)
    half = width // 2
    gram[...] = jnp.zeros_like(gram)
    gram[:, :width] = local[:half]
    gram[:, LANES // 2 : LANES // 2 + width] = local[half:]


def after_kernel(value, earlier, out):
    pass


def after(value, earlier):
    anywhere = pl.BlockSpec(memory_space=pl.ANY)
    return pl.pallas_call(
        after_kernel,
        out_shape=jax.ShapeDtypeStruct(value.shape, value.dtype),
        in_specs=[anywhere, anywhere],
        out_specs=anywhere,
        input_output_aliases={0: 0},
        compiler_params=limit(1),
    )(value, earlier)


def limit(mib):
    return pltpu.CompilerParams(vmem_limit_bytes=mib * MIB)


def vmem(count):
    return [pl.BlockSpec(memory_space=pltpu.VMEM)] * count


def smem(count):
    return [pl.BlockSpec(memory_space=pltpu.SMEM)] * count


def local(
    current_block,
    previous_block,
    previous_coupling,
    stored_blocks,
    stiffness_diag,
    lumped_mass,
    tile_values,
    tile_rows,
    tile_cols,
    tile_counts,
):
    row_devs = lax.axis_size("row")
    col_devs = lax.axis_size("col")
    width, slab_len = current_block.shape
    stored_count = stored_blocks.shape[0]
    slots, tile_len, _ = tile_values.shape
    slab_tiles = slab_len // tile_len
    cells = slab_len * row_devs * col_devs
    f32, bf16 = jnp.float32, jnp.bfloat16
    place = jnp.stack([lax.axis_index("row"), lax.axis_index("col")]).astype(jnp.int32)
    stored = stored_blocks.reshape(stored_count * width, slab_len)
    mass = lumped_mass.reshape(1, slab_len)
    diag = stiffness_diag.reshape(1, slab_len)
    slab = jax.ShapeDtypeStruct((width, slab_len), f32)

    targets = row_devs * slab_tiles
    anywhere = [pl.BlockSpec(memory_space=pl.ANY)]
    panel_shape = (col_devs + 1, width, slab_len)
    early_shape = (targets + 1, width, tile_len)
    part_acc = pltpu.VMEM((slab_tiles + 1, width, tile_len), f32)

    def cost(flops):
        return pl.CostEstimate(flops=flops, bytes_accessed=flops // width, transcendentals=0)

    with jax.named_scope("gather"):
        rounded = current_block.astype(bf16)
        panels = [rounded] + [None] * (col_devs - 1)
        for m in range(col_devs - 2, 0, -2):
            panels[m] = swap(rounded, "col", m)
        panels[1] = swap(rounded, "col", 1)

    with jax.named_scope("plan"):
        places = -(-(slots + 2 * targets + 2 * UNROLL) // LANES) * LANES
        plan_rows = 8 + -(-(row_devs + 2) // 8) * 8
        plan, held = pl.pallas_call(
            functools.partial(plan_kernel, row_devs, col_devs, slab_tiles),
            out_shape=[jax.ShapeDtypeStruct((plan_rows, places), jnp.int32), pltpu.VMEM(tile_values.shape, bf16)],
            in_specs=smem(2) + vmem(2) + [pl.BlockSpec(memory_space=pltpu.HBM)],
            out_specs=vmem(2),
            scratch_shapes=[pltpu.SemaphoreType.DMA((slots // CHUNK,))],
            compiler_params=limit(8),
            cost_estimate=cost(2 * slots * width * tile_len * tile_len),
        )(
            place,
            tile_counts,
            tile_rows.reshape(1, slots),
            tile_cols.reshape(1, slots),
            pltpu.with_memory_space_constraint(tile_values, pltpu.HBM),
        )

    with jax.named_scope("early"):
        early = pl.pallas_call(
            early_kernel,
            out_shape=pltpu.VMEM(early_shape, f32),
            in_specs=smem(1) + anywhere * 2 + vmem(1),
            out_specs=vmem(1)[0],
            scratch_shapes=[pltpu.VMEM(panel_shape, bf16), pltpu.SemaphoreType.DMA((2,))],
            compiler_params=limit(8),
            cost_estimate=cost(slots * width * tile_len * tile_len // 2),
        )(plan, panels[0], panels[1], held)

    with jax.named_scope("gather"):
        for m in range(col_devs - 2, 0, -2):
            panels[m] = after(panels[m], early)
            panels[m + 1] = swap(panels[m], "col", 1)

    with jax.named_scope("late"):
        masks = list(range(row_devs - 1, 0, -1))
        part = jax.ShapeDtypeStruct((width, slab_len), bf16)
        first, gathered = pl.pallas_call(
            functools.partial(first_late_kernel, masks[0], 1),
            out_shape=[part, pltpu.VMEM(panel_shape, bf16)],
            in_specs=smem(2) + anywhere * col_devs + vmem(2),
            out_specs=vmem(2),
            scratch_shapes=[part_acc, pltpu.SemaphoreType.DMA((col_devs,))],
            compiler_params=limit(8),
            cost_estimate=cost(width),
        )(place, plan, *panels, held, early)
        first = swap(first, "row", masks[0])
        others = pl.pallas_call(
            functools.partial(late_kernel, masks[1:]),
            out_shape=[part] * len(masks[1:]),
            in_specs=smem(2) + vmem(3),
            out_specs=vmem(len(masks[1:])),
            scratch_shapes=[part_acc],
            compiler_params=limit(8),
            cost_estimate=cost(width),
        )(place, plan, gathered, held, early)
        received = [swap(other, "row", m) for m, other in zip(masks[1:], others)]
        base = pl.pallas_call(
            functools.partial(own_kernel, row_devs),
            out_shape=slab,
            in_specs=smem(2) + vmem(8),
            out_specs=vmem(1)[0],
            scratch_shapes=[part_acc],
            compiler_params=limit(8),
            cost_estimate=cost(width),
        )(place, plan, gathered, held, early, first, current_block, previous_block, previous_coupling, diag)

    basis_rows = (stored_count + 1) * width
    padded = (width, -(-basis_rows // LANES) * LANES)
    half = (-(-len(blocks(padded)) // 2), 8, LANES)
    with jax.named_scope("coefficients"):
        recurrence, keep, give = pl.pallas_call(
            functools.partial(coefficient_kernel, cells, len(received)),
            out_shape=[slab] + [jax.ShapeDtypeStruct(half, f32)] * 2,
            in_specs=smem(1) + vmem(len(received) + 4),
            out_specs=vmem(3),
            scratch_shapes=[pltpu.VMEM((2,) + half, f32)],
            compiler_params=limit(24),
        )(place, base, *received, mass, current_block, stored)
        mine = keep + swap(give, "col", 1)
        mine = total(total(mine, "col", bits("col")[1:]), "row", bits("row"))
        other = swap(mine, "col", 1)

    with jax.named_scope("residual"):
        residual_block, coef, gram = pl.pallas_call(
            functools.partial(residual_kernel, cells),
            out_shape=[
                slab,
                jax.ShapeDtypeStruct((width, basis_rows), f32),
                jax.ShapeDtypeStruct((width // 2, LANES), f32),
            ],
            in_specs=smem(1) + vmem(6),
            out_specs=vmem(3),
            scratch_shapes=[pltpu.VMEM((2,) + half, f32), pltpu.VMEM(padded, f32)],
            compiler_params=limit(24),
        )(place, mine, other, recurrence, mass, current_block, stored)
        coefficients = coef.T.reshape(stored_count + 1, width, width)

    with jax.named_scope("gram"):
        gram = total(total(gram, "col", bits("col")), "row", bits("row"))
        gram = jnp.concatenate(
            [gram[:, :width], gram[:, LANES // 2 : LANES // 2 + width]], axis=0
        )
    return (residual_block, coefficients, gram)


def solution(mesh):
    return jax.shard_map(
        local,
        mesh=mesh,
        in_specs=(
            P(None, ("row", "col")),
            P(None, ("row", "col")),
            P(),
            P(None, None, ("row", "col")),
            P(("row", "col")),
            P(("row", "col")),
            P(("row", "col"), None, None),
            P(("row", "col")),
            P(("row", "col")),
            P(("row", "col")),
        ),
        out_specs=(P(None, ("row", "col")), P(), P()),
        check_vma=False,
    )
```

time: 117 us -> 88.3 us (0.75)
  blocking collectives: 36.7 us -> 0 us
  local copies, waits for them, and re-layouts: 23.1 us -> 2.28 us
  starting transfers between devices: 13.1 us -> 29.7 us
  waiting for transfers between devices: 16.8 us -> 30.9 us
  other arithmetic: 5.31 us -> 1.76 us
  Pallas kernels: 20 us -> 21.5 us
    all_to_all x4 -> x0, blocking collectives: 36.7 us -> none  [the longest x3 26.1 us: spread(): return lax.all_to_all(copies, axis, 0, 0)]
    ppermute x10 -> x21, starting transfers between devices: 9.78 us -> 29.7 us  [swap(): return lax.ppermute(value, axis, [(i, i ^ mask) for i in range(count)])]
    ppermute x10 -> x21, waiting for transfers between devices: 12.9 us -> 30.9 us  [swap(): return lax.ppermute(value, axis, [(i, i ^ mask) for i in range(count)])]
    unnamed x30 -> x16, local copies, waits for them, and re-layouts: 19.3 us -> 1.39 us
    all_to_all x1 -> x0, waiting for transfers between devices: 3.95 us -> none  [spread(): return lax.all_to_all(copies, axis, 0, 0)]
    all_to_all x1 -> x0, starting transfers between devices: 3.27 us -> none  [spread(): return lax.all_to_all(copies, axis, 0, 0)]
    reduce_sum x4 -> x0, other arithmetic: 2.93 us -> none  [the longest x1 1.5 us: local(): piece = jnp.sum(lax.all_to_all(partial, 'col', 0, 0), axis=0)]
    pallas_call x3 -> x5, Pallas kernels: 14.1 us -> 16.2 us  [the longest x1 4.59 us: local(): pl.pallas_call(functools.partial(first_late_kernel, masks[0], 1), out_sha...]
  transfers between devices with their start and end apart: 11 -> 21, of which waited for: 6 -> 17; matrix products, arithmetic and copies ran while one was open for 2% -> 1% of each run, Pallas kernels for 6% -> 15%
where the time goes in v4:
time: 88.3 us; the launch traced here: 87.6 us
  waiting for transfers between devices  30.9 us (35%)
  starting transfers between devices  29.7 us (34%)
  Pallas kernels  21.5 us (24%)
  local copies, waits for them, and re-layouts  2.28 us (3%)
  other arithmetic  1.76 us (2%)
  between operations  1.42 us (2%)
    ppermute x21, waiting for transfers between devices, swap(): return lax.ppermute(value, axis, [(i, i ^ mask) for i in range(count)])  30.9 us
    ppermute x21, starting transfers between devices, swap(): return lax.ppermute(value, axis, [(i, i ^ mask) for i in range(count)])  29.7 us
    pallas_call x1, Pallas kernels, local(): pl.pallas_call(functools.partial(first_late_kernel, masks[0], 1), out_sha...  4.59 us
    pallas_call x1, Pallas kernels, local(): pl.pallas_call(early_kernel, out_shape=pltpu.VMEM(early_shape, f32), in_s...  3.7 us
    pallas_call x1, Pallas kernels, local(): pl.pallas_call(functools.partial(plan_kernel, row_devs, col_devs, slab_ti...  3.19 us
    pallas_call x1, Pallas kernels, local(): pl.pallas_call(functools.partial(own_kernel, row_devs), out_shape=slab, i...  3.13 us
    pallas_call x1, Pallas kernels, local(): pl.pallas_call(functools.partial(late_kernel, masks[1:]), out_shape=[part...  2.96 us
    pallas_call x1, Pallas kernels, local(): pl.pallas_call(functools.partial(residual_kernel, cells), out_shape=[slab...  2.16 us
  transfers between devices with their start and end apart: 21, of which 17 were waited for; matrix products, arithmetic and copies ran while one was open for 1% of the time, Pallas kernels for 15%

profile of v4, /device:TPU:0, one launch (start us, length us, event | category | flops | bytes accessed | tf_op | source)
XLA Modules:
  0.0 87.6 jit_solution(9780796373846497995)
XLA Ops:
  0.6 1.0 %convert_element_type.3.own_panel.refs_0_ = bf16[48,2048]{1,0:T(8,128)(2,1)S(1)} convert(f32[48,2048]{1,0:T(8,128)} %current.3) | non-fusion elementwise | flops 98304 | bytes 589824 | tf_op jit(solution)/shard_map/gather/convert_element_type | solution.py:303
  1.7 0.5 collective-permute-start
  2.2 3.5 %collective-permute-start.5 = (bf16[48,2048]{1,0:T(8,128)(2,1)S(1)}, bf16[48,2048]{1,0:T(8,128)(2,1)S(1)}, u32[]{:S(2)}, u32[]{:S(2)}) collective-permute-start(bf16[48,2048]{1,0:T(8,128)(2,1)S(1)} %convert_element_type.3.own_panel.refs_0_), channel_id=1, source_target_pairs={{0,6},{1,7},{2,4},{3,5},{4,2},{5,3},{6,0},{7,1},{8,14},{9,15},{10,... | collective-permute-start | bytes 589832 | tf_op jit(solution)/shard_map/gather/ppermute | solution.py:19
  5.7 0.5 collective-permute-start.3
  6.2 0.1 collective-permute-start.1
  7.0 0.1 pad_add_fusion.place
  7.1 0.7 copy-done.6
  7.7 0.7 copy-done.7
  8.4 3.2 %plan.1 = (s32[16,768]{1,0:T(8,128)S(1)}, bf16[512,128,128]{2,1,0:T(8,128)(2,1)S(1)}) custom-call(s32[2]{0:T(128)S(1)} %pad_add_fusion.place, s32[1]{0:T(128)S(6)} %copy.21.counts, s32[1,512]{1,0:T(1,128)S(1)} %bitcast.15, s32[1,512]{1,0:T(1,128)S(1)} %bitcast.16, bf16[512,128,128]{2,1,0:T(8,128)(2,1)} %tiles.1), custom_call_target="tpu_custom_call" | custom-call | flops 805306368 | bytes 16777216 | tf_op jit(solution)/shard_map/plan/pallas_call | solution.py:312
  11.6 0.0 collective-permute-done.near_panel.refs_1_
  11.6 3.7 %early.1.earlier.refs_9_ = f32[65,48,128]{2,1,0:T(8,128)S(1)} custom-call(s32[16,768]{1,0:T(8,128)S(1)} %get-tuple-element.15.plan, bf16[48,2048]{1,0:T(8,128)(2,1)S(1)} %convert_element_type.3.own_panel.refs_0_, bf16[48,2048]{1,0:T(8,128)(2,1)S(1)} %collective-permute-done.near_panel.refs_1_, bf16[512,128,128]{2,1,0:T(8,128)(2,1)S(1)} %get-tuple-element.16.tiles.refs_8_), custom_call_target="tpu_custom_call" | custom-call | flops 201326592 | bytes 4194304 | tf_op jit(solution)/shard_map/early/pallas_call | solution.py:329
  15.3 0.4 collective-permute-done.1.value
  15.7 1.1 %collective-permute-start.2 = (bf16[48,2048]{1,0:T(8,128)(2,1)S(1)}, bf16[48,2048]{1,0:T(8,128)(2,1)S(1)}, u32[]{:S(2)}, u32[]{:S(2)}) collective-permute-start(bf16[48,2048]{1,0:T(8,128)(2,1)S(1)} %gather.3.refs_2_), channel_id=1, source_target_pairs={{0,1},{1,0},{2,3},{3,2},{4,5},{5,4},{6,7},{7,6},{8,9},{9,8},{10,11... | collective-permute-start | bytes 589832 | tf_op jit(solution)/shard_map/gather/ppermute | solution.py:19
  16.8 0.0 collective-permute-done.3.value
  16.8 0.1 collective-permute-start.4
  16.9 0.0 collective-permute-done.5.value
  16.9 0.4 collective-permute-start.6
  17.3 0.6 collective-permute-done.2.refs_3_
  17.9 0.4 collective-permute-done.4.refs_5_
  18.2 0.3 collective-permute-done.6.refs_7_
  18.5 4.6 %late.3 = (bf16[48,2048]{1,0:T(8,128)(2,1)S(1)}, bf16[9,48,2048]{2,1,0:T(8,128)(2,1)S(1)}) custom-call(s32[2]{0:T(128)S(1)} %pad_add_fusion.place, s32[16,768]{1,0:T(8,128)S(1)} %get-tuple-element.15.plan, bf16[48,2048]{1,0:T(8,128)(2,1)S(1)} %convert_element_type.3.own_panel.refs_0_, bf16[48,2048]{1,0:T(8,128)(2,1)S(1)} %collective-permute-done.near_panel.refs_1_, ...), custom_call_target="tpu_custom_call" | custom-call | flops 48 | bytes 1 | tf_op jit(solution)/shard_map/late/pallas_call | solution.py:347
  23.1 3.3 %collective-permute-start.7 = (bf16[48,2048]{1,0:T(8,128)(2,1)S(1)}, bf16[48,2048]{1,0:T(8,128)(2,1)S(1)}, u32[]{:S(2)}, u32[]{:S(2)}) collective-permute-start(bf16[48,2048]{1,0:T(8,128)(2,1)S(1)} %get-tuple-element.18), channel_id=1, source_target_pairs={{0,24},{8,16},{16,8},{24,0},{1,25},{9,17},{17,9},{25,1},{2,26},{10... | collective-permute-start | bytes 589832 | tf_op jit(solution)/shard_map/late/ppermute | solution.py:19
  26.4 3.0 %late.5 = (bf16[48,2048]{1,0:T(8,128)(2,1)S(1)}, bf16[48,2048]{1,0:T(8,128)(2,1)S(1)}) custom-call(s32[2]{0:T(128)S(1)} %pad_add_fusion.place, s32[16,768]{1,0:T(8,128)S(1)} %get-tuple-element.15.plan, bf16[9,48,2048]{2,1,0:T(8,128)(2,1)S(1)} %get-tuple-element.17.panel_buf, bf16[512,128,128]{2,1,0:T(8,128)(2,1)S(1)} %get-tuple-element.16.tiles.refs_8_, ...), custom_call_target="tpu_custom_call" | custom-call | flops 48 | bytes 1 | tf_op jit(solution)/shard_map/late/pallas_call | solution.py:357
  29.4 2.1 %collective-permute-start.8 = (bf16[48,2048]{1,0:T(8,128)(2,1)S(1)}, bf16[48,2048]{1,0:T(8,128)(2,1)S(1)}, u32[]{:S(2)}, u32[]{:S(2)}) collective-permute-start(bf16[48,2048]{1,0:T(8,128)(2,1)S(1)} %get-tuple-element.19), channel_id=1, source_target_pairs={{0,16},{8,24},{16,0},{24,8},{1,17},{9,25},{17,1},{25,9},{2,18},{10... | collective-permute-start | bytes 589832 | tf_op jit(solution)/shard_map/late/ppermute | solution.py:19
  31.4 0.5 collective-permute-start.9
  32.0 0.6 collective-permute-done.7.received
  32.6 0.0 copy-done.1
  32.6 0.0 copy-done.2
  32.6 0.0 copy-done.4
  32.6 0.0 copy-done.5
  32.6 0.0 copy-start
  32.6 0.0 copy-start.3
  32.6 3.1 %late.4.base = f32[48,2048]{1,0:T(8,128)S(1)} custom-call(s32[2]{0:T(128)S(1)} %pad_add_fusion.place, s32[16,768]{1,0:T(8,128)S(1)} %get-tuple-element.15.plan, bf16[9,48,2048]{2,1,0:T(8,128)(2,1)S(1)} %get-tuple-element.17.panel_buf, bf16[512,128,128]{2,1,0:T(8,128)(2,1)S(1)} %get-tuple-element.16.tiles.refs_8_, f32[65,48,128]{2,1,0:T(8,128)S(1)} %early.1.earlier.refs_9_, ...), custom_call_target="tpu_custom_call" | custom-call | flops 48 | bytes 1 | tf_op jit(solution)/shard_map/late/pallas_call | solution.py:367
  35.8 8.8 %collective-permute-done.8.refs_0_ = bf16[48,2048]{1,0:T(8,128)(2,1)S(1)} collective-permute-done((bf16[48,2048]{1,0:T(8,128)(2,1)S(1)}, bf16[48,2048]{1,0:T(8,128)(2,1)S(1)}, u32[]{:S(2)}, u32[]{:S(2)}) %collective-permute-start.8) | collective-permute-done | bytes 196640 | tf_op jit(solution)/shard_map/late/ppermute | solution.py:19
  44.5 0.0 collective-permute-done.9.refs_1_
  44.5 0.0 copy-done
  44.5 0.0 copy-done.3
  44.5 1.8 %coefficients.1 = (f32[48,2048]{1,0:T(8,128)S(1)}, f32[12,8,128]{2,1,0:T(8,128)S(1)}, f32[12,8,128]{2,1,0:T(8,128)S(1)}) custom-call(s32[2]{0:T(128)S(1)} %pad_add_fusion.place, f32[48,2048]{1,0:T(8,128)S(1)} %late.4.base, bf16[48,2048]{1,0:T(8,128)(2,1)S(1)} %collective-permute-done.8.refs_0_, bf16[48,2048]{1,0:T(8,128)(2,1)S(1)} %collective-permute-done.9.refs_1_, ...), custom_call_target="tpu_custom_call" | custom-call | tf_op jit(solution)/shard_map/coefficients/pallas_call | solution.py:381
  46.3 0.1 collective-permute-start.10
  46.4 1.2 %collective-permute-done.10 = f32[12,8,128]{2,1,0:T(8,128)S(1)} collective-permute-done((f32[12,8,128]{2,1,0:T(8,128)S(1)}, f32[12,8,128]{2,1,0:T(8,128)S(1)}, u32[]{:S(2)}, u32[]{:S(2)}) %collective-permute-start.10) | collective-permute-done | bytes 49184 | tf_op jit(solution)/shard_map/coefficients/ppermute | solution.py:19
  47.6 1.8 %collective-permute-start.11 = (f32[12,8,128]{2,1,0:T(8,128)S(1)}, f32[12,8,128]{2,1,0:T(8,128)S(1)}, u32[]{:S(2)}, u32[]{:S(2)}) collective-permute-start(f32[12,8,128]{2,1,0:T(8,128)S(1)} %add.30), channel_id=1, source_target_pairs={{0,2},{1,3},{2,0},{3,1},{4,6},{5,7},{6,4},{7,5},{8,10},{9,11},{10,... | collective-permute-start | bytes 147464 | tf_op jit(solution)/shard_map/coefficients/ppermute | solution.py:19
  49.4 2.4 %collective-permute-done.11 = f32[12,8,128]{2,1,0:T(8,128)S(1)} collective-permute-done((f32[12,8,128]{2,1,0:T(8,128)S(1)}, f32[12,8,128]{2,1,0:T(8,128)S(1)}, u32[]{:S(2)}, u32[]{:S(2)}) %collective-permute-start.11) | collective-permute-done | bytes 49184 | tf_op jit(solution)/shard_map/coefficients/ppermute | solution.py:19
  51.8 3.3 %collective-permute-start.12 = (f32[12,8,128]{2,1,0:T(8,128)S(1)}, f32[12,8,128]{2,1,0:T(8,128)S(1)}, u32[]{:S(2)}, u32[]{:S(2)}) collective-permute-start(f32[12,8,128]{2,1,0:T(8,128)S(1)} %add.31), channel_id=1, source_target_pairs={{0,4},{1,5},{2,6},{3,7},{4,0},{5,1},{6,2},{7,3},{8,12},{9,13},{10,... | collective-permute-start | bytes 147464 | tf_op jit(solution)/shard_map/coefficients/ppermute | solution.py:19
  55.1 2.1 %collective-permute-done.12 = f32[12,8,128]{2,1,0:T(8,128)S(1)} collective-permute-done((f32[12,8,128]{2,1,0:T(8,128)S(1)}, f32[12,8,128]{2,1,0:T(8,128)S(1)}, u32[]{:S(2)}, u32[]{:S(2)}) %collective-permute-start.12) | collective-permute-done | bytes 49184 | tf_op jit(solution)/shard_map/coefficients/ppermute | solution.py:19
  57.2 0.7 collective-permute-start.13
  57.8 3.5 %collective-permute-done.13 = f32[12,8,128]{2,1,0:T(8,128)S(1)} collective-permute-done((f32[12,8,128]{2,1,0:T(8,128)S(1)}, f32[12,8,128]{2,1,0:T(8,128)S(1)}, u32[]{:S(2)}, u32[]{:S(2)}) %collective-permute-start.13) | collective-permute-done | bytes 49184 | tf_op jit(solution)/shard_map/coefficients/ppermute | solution.py:19
  61.3 2.8 %collective-permute-start.14 = (f32[12,8,128]{2,1,0:T(8,128)S(1)}, f32[12,8,128]{2,1,0:T(8,128)S(1)}, u32[]{:S(2)}, u32[]{:S(2)}) collective-permute-start(f32[12,8,128]{2,1,0:T(8,128)S(1)} %add.33), channel_id=1, source_target_pairs={{0,16},{8,24},{16,0},{24,8},{1,17},{9,25},{17,1},{25,9},{2,18},{10... | collective-permute-start | bytes 147464 | tf_op jit(solution)/shard_map/coefficients/ppermute | solution.py:19
  64.1 2.3 %collective-permute-done.14 = f32[12,8,128]{2,1,0:T(8,128)S(1)} collective-permute-done((f32[12,8,128]{2,1,0:T(8,128)S(1)}, f32[12,8,128]{2,1,0:T(8,128)S(1)}, u32[]{:S(2)}, u32[]{:S(2)}) %collective-permute-start.14) | collective-permute-done | bytes 49184 | tf_op jit(solution)/shard_map/coefficients/ppermute | solution.py:19
  66.4 0.1 collective-permute-start.15
  66.5 1.2 %collective-permute-done.15.other = f32[12,8,128]{2,1,0:T(8,128)S(1)} collective-permute-done((f32[12,8,128]{2,1,0:T(8,128)S(1)}, f32[12,8,128]{2,1,0:T(8,128)S(1)}, u32[]{:S(2)}, u32[]{:S(2)}) %collective-permute-start.15) | collective-permute-done | bytes 49184 | tf_op jit(solution)/shard_map/coefficients/ppermute | solution.py:19
  67.7 2.2 %residual.1 = (f32[48,2048]{1,0:T(8,128)}, f32[48,432]{1,0:T(8,128)S(1)}, f32[24,128]{1,0:T(8,128)S(1)}) custom-call(s32[2]{0:T(128)S(1)} %pad_add_fusion.place, f32[12,8,128]{2,1,0:T(8,128)S(1)} %add.34.mine, f32[12,8,128]{2,1,0:T(8,128)S(1)} %collective-permute-done.15.other, f32[48,2048]{1,0:T(8,128)S(1)} %get-tuple-element.23.recurrence, ...), custom_call_target="tpu_custom_call" | custom-call | tf_op jit(solution)/shard_map/residual/pallas_call | solution.py:394
  69.8 0.2 collective-permute-start.16
  70.0 1.0 %collective-permute-done.16 = f32[24,128]{1,0:T(8,128)S(1)} collective-permute-done((f32[24,128]{1,0:T(8,128)S(1)}, f32[24,128]{1,0:T(8,128)S(1)}, u32[]{:S(2)}, u32[]{:S(2)}) %collective-permute-start.16) | collective-permute-done | bytes 12320 | tf_op jit(solution)/shard_map/gram/ppermute | solution.py:19
  71.0 2.0 %collective-permute-start.17 = (f32[24,128]{1,0:T(8,128)S(1)}, f32[24,128]{1,0:T(8,128)S(1)}, u32[]{:S(2)}, u32[]{:S(2)}) collective-permute-start(f32[24,128]{1,0:T(8,128)S(1)} %add.35), channel_id=1, source_target_pairs={{0,2},{1,3},{2,0},{3,1},{4,6},{5,7},{6,4},{7,5},{8,10},{9,11},{10,... | collective-permute-start | bytes 36872 | tf_op jit(solution)/shard_map/gram/ppermute | solution.py:19
  73.0 1.7 %collective-permute-done.17 = f32[24,128]{1,0:T(8,128)S(1)} collective-permute-done((f32[24,128]{1,0:T(8,128)S(1)}, f32[24,128]{1,0:T(8,128)S(1)}, u32[]{:S(2)}, u32[]{:S(2)}) %collective-permute-start.17) | collective-permute-done | bytes 12320 | tf_op jit(solution)/shard_map/gram/ppermute | solution.py:19
  74.7 2.2 %collective-permute-start.18 = (f32[24,128]{1,0:T(8,128)S(1)}, f32[24,128]{1,0:T(8,128)S(1)}, u32[]{:S(2)}, u32[]{:S(2)}) collective-permute-start(f32[24,128]{1,0:T(8,128)S(1)} %add.36), channel_id=1, source_target_pairs={{0,4},{1,5},{2,6},{3,7},{4,0},{5,1},{6,2},{7,3},{8,12},{9,13},{10,... | collective-permute-start | bytes 36872 | tf_op jit(solution)/shard_map/gram/ppermute | solution.py:19
  76.9 1.7 %collective-permute-done.18 = f32[24,128]{1,0:T(8,128)S(1)} collective-permute-done((f32[24,128]{1,0:T(8,128)S(1)}, f32[24,128]{1,0:T(8,128)S(1)}, u32[]{:S(2)}, u32[]{:S(2)}) %collective-permute-start.18) | collective-permute-done | bytes 12320 | tf_op jit(solution)/shard_map/gram/ppermute | solution.py:19
  78.6 1.6 %collective-permute-start.19 = (f32[24,128]{1,0:T(8,128)S(1)}, f32[24,128]{1,0:T(8,128)S(1)}, u32[]{:S(2)}, u32[]{:S(2)}) collective-permute-start(f32[24,128]{1,0:T(8,128)S(1)} %add.37), channel_id=1, source_target_pairs={{0,8},{8,0},{16,24},{24,16},{1,9},{9,1},{17,25},{25,17},{2,10},{10... | collective-permute-start | bytes 36872 | tf_op jit(solution)/shard_map/gram/ppermute | solution.py:19
  80.2 2.1 %collective-permute-done.19 = f32[24,128]{1,0:T(8,128)S(1)} collective-permute-done((f32[24,128]{1,0:T(8,128)S(1)}, f32[24,128]{1,0:T(8,128)S(1)}, u32[]{:S(2)}, u32[]{:S(2)}) %collective-permute-start.19) | collective-permute-done | bytes 12320 | tf_op jit(solution)/shard_map/gram/ppermute | solution.py:19
  82.3 3.0 %collective-permute-start.20 = (f32[24,128]{1,0:T(8,128)S(1)}, f32[24,128]{1,0:T(8,128)S(1)}, u32[]{:S(2)}, u32[]{:S(2)}) collective-permute-start(f32[24,128]{1,0:T(8,128)S(1)} %add.38), channel_id=1, source_target_pairs={{0,16},{8,24},{16,0},{24,8},{1,17},{9,25},{17,1},{25,9},{2,18},{10... | collective-permute-start | bytes 36872 | tf_op jit(solution)/shard_map/gram/ppermute | solution.py:19
  85.3 0.8 copy.17
  86.1 0.9 collective-permute-done.20
  86.9 0.1 fusion
  87.0 0.6 pad_maximum_fusion
  (19 shorter events, 0.1 us)
Async XLA Ops:
  1.7 10.0 %collective-permute-start = (bf16[48,2048]{1,0:T(8,128)(2,1)S(1)}, bf16[48,2048]{1,0:T(8,128)(2,1)S(1)}, u32[]{:S(2)}, u32[]{:S(2)}) collective-permute-start(bf16[48,2048]{1,0:T(8,128)(2,1)S(1)} %convert_element_type.3.own_panel.refs_0_), channel_id=1, source_target_pairs={{0,1},{1,0},{2,3},{3,2},{4,5},{5,4},{6,7},{7,6},{8,9},{9,8},{10,11... | collective-permute-start | bytes 589832 | tf_op jit(solution)/shard_map/gather/ppermute | solution.py:19
  2.2 14.7 %collective-permute-start.5 = (bf16[48,2048]{1,0:T(8,128)(2,1)S(1)}, bf16[48,2048]{1,0:T(8,128)(2,1)S(1)}, u32[]{:S(2)}, u32[]{:S(2)}) collective-permute-start(bf16[48,2048]{1,0:T(8,128)(2,1)S(1)} %convert_element_type.3.own_panel.refs_0_), channel_id=1, source_target_pairs={{0,6},{1,7},{2,4},{3,5},{4,2},{5,3},{6,0},{7,1},{8,14},{9,15},{10,... | collective-permute-start | bytes 589832 | tf_op jit(solution)/shard_map/gather/ppermute | solution.py:19
  5.7 11.1 %collective-permute-start.3 = (bf16[48,2048]{1,0:T(8,128)(2,1)S(1)}, bf16[48,2048]{1,0:T(8,128)(2,1)S(1)}, u32[]{:S(2)}, u32[]{:S(2)}) collective-permute-start(bf16[48,2048]{1,0:T(8,128)(2,1)S(1)} %convert_element_type.3.own_panel.refs_0_), channel_id=1, source_target_pairs={{0,4},{1,5},{2,6},{3,7},{4,0},{5,1},{6,2},{7,3},{8,12},{9,13},{10,... | collective-permute-start | bytes 589832 | tf_op jit(solution)/shard_map/gather/ppermute | solution.py:19
  6.2 9.5 %collective-permute-start.1 = (bf16[48,2048]{1,0:T(8,128)(2,1)S(1)}, bf16[48,2048]{1,0:T(8,128)(2,1)S(1)}, u32[]{:S(2)}, u32[]{:S(2)}) collective-permute-start(bf16[48,2048]{1,0:T(8,128)(2,1)S(1)} %convert_element_type.3.own_panel.refs_0_), channel_id=1, source_target_pairs={{0,2},{1,3},{2,0},{3,1},{4,6},{5,7},{6,4},{7,5},{8,10},{9,11},{10,... | collective-permute-start | bytes 589832 | tf_op jit(solution)/shard_map/gather/ppermute | solution.py:19
  7.1 0.7 copy-start.6
  7.7 0.7 copy-start.7
  15.7 2.1 %collective-permute-start.2 = (bf16[48,2048]{1,0:T(8,128)(2,1)S(1)}, bf16[48,2048]{1,0:T(8,128)(2,1)S(1)}, u32[]{:S(2)}, u32[]{:S(2)}) collective-permute-start(bf16[48,2048]{1,0:T(8,128)(2,1)S(1)} %gather.3.refs_2_), channel_id=1, source_target_pairs={{0,1},{1,0},{2,3},{3,2},{4,5},{5,4},{6,7},{7,6},{8,9},{9,8},{10,11... | collective-permute-start | bytes 589832 | tf_op jit(solution)/shard_map/gather/ppermute | solution.py:19
  16.8 1.4 %collective-permute-start.4 = (bf16[48,2048]{1,0:T(8,128)(2,1)S(1)}, bf16[48,2048]{1,0:T(8,128)(2,1)S(1)}, u32[]{:S(2)}, u32[]{:S(2)}) collective-permute-start(bf16[48,2048]{1,0:T(8,128)(2,1)S(1)} %gather.4.refs_4_), channel_id=1, source_target_pairs={{0,1},{1,0},{2,3},{3,2},{4,5},{5,4},{6,7},{7,6},{8,9},{9,8},{10,11... | collective-permute-start | bytes 589832 | tf_op jit(solution)/shard_map/gather/ppermute | solution.py:19
  16.9 1.6 %collective-permute-start.6 = (bf16[48,2048]{1,0:T(8,128)(2,1)S(1)}, bf16[48,2048]{1,0:T(8,128)(2,1)S(1)}, u32[]{:S(2)}, u32[]{:S(2)}) collective-permute-start(bf16[48,2048]{1,0:T(8,128)(2,1)S(1)} %gather.5.refs_6_), channel_id=1, source_target_pairs={{0,1},{1,0},{2,3},{3,2},{4,5},{5,4},{6,7},{7,6},{8,9},{9,8},{10,11... | collective-permute-start | bytes 589832 | tf_op jit(solution)/shard_map/gather/ppermute | solution.py:19
  23.1 9.5 %collective-permute-start.7 = (bf16[48,2048]{1,0:T(8,128)(2,1)S(1)}, bf16[48,2048]{1,0:T(8,128)(2,1)S(1)}, u32[]{:S(2)}, u32[]{:S(2)}) collective-permute-start(bf16[48,2048]{1,0:T(8,128)(2,1)S(1)} %get-tuple-element.18), channel_id=1, source_target_pairs={{0,24},{8,16},{16,8},{24,0},{1,25},{9,17},{17,9},{25,1},{2,26},{10... | collective-permute-start | bytes 589832 | tf_op jit(solution)/shard_map/late/ppermute | solution.py:19
  26.4 6.2 %copy-start.1 = (f32[48,2048]{1,0:T(8,128)S(1)}, f32[48,2048]{1,0:T(8,128)}, u32[]{:S(2)}) copy-start(f32[48,2048]{1,0:T(8,128)} %current.3) | copy-start | bytes 1179652
  26.4 6.2 %copy-start.2 = (f32[48,2048]{1,0:T(8,128)S(1)}, f32[48,2048]{1,0:T(8,128)}, u32[]{:S(2)}) copy-start(f32[48,2048]{1,0:T(8,128)} %previous.1) | copy-start | bytes 1179652
  26.4 6.2 %copy-start.4 = (f32[48,48]{1,0:T(8,128)S(1)}, f32[48,48]{1,0:T(8,128)}, u32[]{:S(2)}) copy-start(f32[48,48]{1,0:T(8,128)} %coupling.1) | copy-start | bytes 27652
  26.4 6.2 %copy-start.5 = (f32[2048]{0:T(1024)S(1)}, f32[2048]{0:T(1024)}, u32[]{:S(2)}) copy-start(f32[2048]{0:T(1024)} %param.14) | copy-start | bytes 24580
  29.4 15.1 %collective-permute-start.8 = (bf16[48,2048]{1,0:T(8,128)(2,1)S(1)}, bf16[48,2048]{1,0:T(8,128)(2,1)S(1)}, u32[]{:S(2)}, u32[]{:S(2)}) collective-permute-start(bf16[48,2048]{1,0:T(8,128)(2,1)S(1)} %get-tuple-element.19), channel_id=1, source_target_pairs={{0,16},{8,24},{16,0},{24,8},{1,17},{9,25},{17,1},{25,9},{2,18},{10... | collective-permute-start | bytes 589832 | tf_op jit(solution)/shard_map/late/ppermute | solution.py:19
  31.4 13.1 %collective-permute-start.9 = (bf16[48,2048]{1,0:T(8,128)(2,1)S(1)}, bf16[48,2048]{1,0:T(8,128)(2,1)S(1)}, u32[]{:S(2)}, u32[]{:S(2)}) collective-permute-start(bf16[48,2048]{1,0:T(8,128)(2,1)S(1)} %get-tuple-element.20), channel_id=1, source_target_pairs={{0,8},{8,0},{16,24},{24,16},{1,9},{9,1},{17,25},{25,17},{2,10},{10... | collective-permute-start | bytes 589832 | tf_op jit(solution)/shard_map/late/ppermute | solution.py:19
  32.6 11.9 %copy-start = (f32[8,48,2048]{2,1,0:T(8,128)S(1)}, f32[8,48,2048]{2,1,0:T(8,128)}, u32[]{:S(2)}) copy-start(f32[8,48,2048]{2,1,0:T(8,128)} %param.13) | copy-start | bytes 9437188
  32.6 11.9 %copy-start.3 = (f32[2048]{0:T(1024)S(1)}, f32[2048]{0:T(1024)}, u32[]{:S(2)}) copy-start(f32[2048]{0:T(1024)} %param.15) | copy-start | bytes 24580
  46.3 1.3 %collective-permute-start.10 = (f32[12,8,128]{2,1,0:T(8,128)S(1)}, f32[12,8,128]{2,1,0:T(8,128)S(1)}, u32[]{:S(2)}, u32[]{:S(2)}) collective-permute-start(f32[12,8,128]{2,1,0:T(8,128)S(1)} %get-tuple-element.22), channel_id=1, source_target_pairs={{0,1},{1,0},{2,3},{3,2},{4,5},{5,4},{6,7},{7,6},{8,9},{9,8},{10,11... | collective-permute-start | bytes 147464 | tf_op jit(solution)/shard_map/coefficients/ppermute | solution.py:19
  47.6 4.2 %collective-permute-start.11 = (f32[12,8,128]{2,1,0:T(8,128)S(1)}, f32[12,8,128]{2,1,0:T(8,128)S(1)}, u32[]{:S(2)}, u32[]{:S(2)}) collective-permute-start(f32[12,8,128]{2,1,0:T(8,128)S(1)} %add.30), channel_id=1, source_target_pairs={{0,2},{1,3},{2,0},{3,1},{4,6},{5,7},{6,4},{7,5},{8,10},{9,11},{10,... | collective-permute-start | bytes 147464 | tf_op jit(solution)/shard_map/coefficients/ppermute | solution.py:19
  51.8 5.4 %collective-permute-start.12 = (f32[12,8,128]{2,1,0:T(8,128)S(1)}, f32[12,8,128]{2,1,0:T(8,128)S(1)}, u32[]{:S(2)}, u32[]{:S(2)}) collective-permute-start(f32[12,8,128]{2,1,0:T(8,128)S(1)} %add.31), channel_id=1, source_target_pairs={{0,4},{1,5},{2,6},{3,7},{4,0},{5,1},{6,2},{7,3},{8,12},{9,13},{10,... | collective-permute-start | bytes 147464 | tf_op jit(solution)/shard_map/coefficients/ppermute | solution.py:19
  57.2 4.2 %collective-permute-start.13 = (f32[12,8,128]{2,1,0:T(8,128)S(1)}, f32[12,8,128]{2,1,0:T(8,128)S(1)}, u32[]{:S(2)}, u32[]{:S(2)}) collective-permute-start(f32[12,8,128]{2,1,0:T(8,128)S(1)} %add.32), channel_id=1, source_target_pairs={{0,8},{8,0},{16,24},{24,16},{1,9},{9,1},{17,25},{25,17},{2,10},{10... | collective-permute-start | bytes 147464 | tf_op jit(solution)/shard_map/coefficients/ppermute | solution.py:19
  61.3 5.0 %collective-permute-start.14 = (f32[12,8,128]{2,1,0:T(8,128)S(1)}, f32[12,8,128]{2,1,0:T(8,128)S(1)}, u32[]{:S(2)}, u32[]{:S(2)}) collective-permute-start(f32[12,8,128]{2,1,0:T(8,128)S(1)} %add.33), channel_id=1, source_target_pairs={{0,16},{8,24},{16,0},{24,8},{1,17},{9,25},{17,1},{25,9},{2,18},{10... | collective-permute-start | bytes 147464 | tf_op jit(solution)/shard_map/coefficients/ppermute | solution.py:19
  66.4 1.3 %collective-permute-start.15 = (f32[12,8,128]{2,1,0:T(8,128)S(1)}, f32[12,8,128]{2,1,0:T(8,128)S(1)}, u32[]{:S(2)}, u32[]{:S(2)}) collective-permute-start(f32[12,8,128]{2,1,0:T(8,128)S(1)} %add.34.mine), channel_id=1, source_target_pairs={{0,1},{1,0},{2,3},{3,2},{4,5},{5,4},{6,7},{7,6},{8,9},{9,8},{10,11... | collective-permute-start | bytes 147464 | tf_op jit(solution)/shard_map/coefficients/ppermute | solution.py:19
  69.8 1.2 %collective-permute-start.16 = (f32[24,128]{1,0:T(8,128)S(1)}, f32[24,128]{1,0:T(8,128)S(1)}, u32[]{:S(2)}, u32[]{:S(2)}) collective-permute-start(f32[24,128]{1,0:T(8,128)S(1)} %get-tuple-element.26), channel_id=1, source_target_pairs={{0,1},{1,0},{2,3},{3,2},{4,5},{5,4},{6,7},{7,6},{8,9},{9,8},{10,11... | collective-permute-start | bytes 36872 | tf_op jit(solution)/shard_map/gram/ppermute | solution.py:19
  71.0 3.7 %collective-permute-start.17 = (f32[24,128]{1,0:T(8,128)S(1)}, f32[24,128]{1,0:T(8,128)S(1)}, u32[]{:S(2)}, u32[]{:S(2)}) collective-permute-start(f32[24,128]{1,0:T(8,128)S(1)} %add.35), channel_id=1, source_target_pairs={{0,2},{1,3},{2,0},{3,1},{4,6},{5,7},{6,4},{7,5},{8,10},{9,11},{10,... | collective-permute-start | bytes 36872 | tf_op jit(solution)/shard_map/gram/ppermute | solution.py:19
  74.7 3.9 %collective-permute-start.18 = (f32[24,128]{1,0:T(8,128)S(1)}, f32[24,128]{1,0:T(8,128)S(1)}, u32[]{:S(2)}, u32[]{:S(2)}) collective-permute-start(f32[24,128]{1,0:T(8,128)S(1)} %add.36), channel_id=1, source_target_pairs={{0,4},{1,5},{2,6},{3,7},{4,0},{5,1},{6,2},{7,3},{8,12},{9,13},{10,... | collective-permute-start | bytes 36872 | tf_op jit(solution)/shard_map/gram/ppermute | solution.py:19
  78.6 3.7 %collective-permute-start.19 = (f32[24,128]{1,0:T(8,128)S(1)}, f32[24,128]{1,0:T(8,128)S(1)}, u32[]{:S(2)}, u32[]{:S(2)}) collective-permute-start(f32[24,128]{1,0:T(8,128)S(1)} %add.37), channel_id=1, source_target_pairs={{0,8},{8,0},{16,24},{24,16},{1,9},{9,1},{17,25},{25,17},{2,10},{10... | collective-permute-start | bytes 36872 | tf_op jit(solution)/shard_map/gram/ppermute | solution.py:19
  82.3 4.6 %collective-permute-start.20 = (f32[24,128]{1,0:T(8,128)S(1)}, f32[24,128]{1,0:T(8,128)S(1)}, u32[]{:S(2)}, u32[]{:S(2)}) collective-permute-start(f32[24,128]{1,0:T(8,128)S(1)} %add.38), channel_id=1, source_target_pairs={{0,16},{8,24},{16,0},{24,8},{1,17},{9,25},{17,1},{25,9},{2,18},{10... | collective-permute-start | bytes 36872 | tf_op jit(solution)/shard_map/gram/ppermute | solution.py:19

commit v5 on v4

--- a/solution.py
+++ b/solution.py
@@ -9,7 +9,9 @@
 
 LANES = 128
 CHUNK = 32
+GROUP = 4
 UNROLL = 4
+TILE_BIT, SOURCE_BIT, ROW_BIT = 10, 15, 20
 NT = (((1,), (1,)), ((), ()))
 MIB = 1 << 20
 
@@ -19,14 +21,11 @@
     return lax.ppermute(value, axis, [(i, i ^ mask) for i in range(count)])
 
 
-def bits(axis):
-    return [1 << i for i in range(lax.axis_size(axis).bit_length() - 1)]
-
-
-def total(value, axis, masks):
-    for m in masks:
-        value = value + swap(value, axis, m)
-    return value
+def total(value, axis, step):
+    values = [value] + [swap(value, axis, m) for m in range(step, lax.axis_size(axis), step)]
+    while len(values) > 1:
+        values = [values[i] + values[i + 1] for i in range(0, len(values), 2)]
+    return values[0]
 
 
 def split(value):
@@ -51,8 +50,14 @@
     return [(q, k) for q in range(0, shape[0], 8) for k in range(0, shape[1], LANES)]
 
 
-def plan_kernel(row_devs, col_devs, slab_tiles, place, counts, rows, cols, tiles, out, held, sem):
+def plan_kernel(
+    row_devs, col_devs, slab_tiles, place, counts, rows_hbm, cols_hbm, tiles, out, held, rows, cols, sem, list_sem
+):
     chunks = (counts[0] + CHUNK - 1) // CHUNK
+    row_copy = pltpu.make_async_copy(rows_hbm, rows, list_sem.at[0])
+    col_copy = pltpu.make_async_copy(cols_hbm, cols, list_sem.at[1])
+    row_copy.start()
+    col_copy.start()
 
     def tile_copy(k):
         window = pl.ds(k * CHUNK, CHUNK)
@@ -63,7 +68,7 @@
         tile_copy(k).start()
 
     f32, bf16, i32 = jnp.float32, jnp.bfloat16, jnp.int32
-    slots, places = rows.shape[1], out.shape[1]
+    slots, places = rows.shape[1], out.shape[1] - LANES
     targets = row_devs * slab_tiles
     bins = 2 * targets
 
@@ -72,6 +77,9 @@
 
     slot = iota((1, slots), 1)
     occupied = slot < counts[0]
+    earlier = (iota((slots, slots), 0) < iota((slots, slots), 1)).astype(f32).astype(bf16)
+    row_copy.wait()
+    col_copy.wait()
     row = rows[...]
     row_owner = jnp.floor(row.astype(f32) * (1.0 / slab_tiles)).astype(i32)
     col_f = cols[...].astype(f32)
@@ -83,12 +91,11 @@
     bin_of = jnp.where(occupied, jnp.where(source < 2, row, late_bin), -1)
     member = (iota((bins, slots), 0) == bin_of).astype(f32)
     member_bf = member.astype(bf16)
-    earlier = (iota((slots, slots), 0) < iota((slots, slots), 1)).astype(f32).astype(bf16)
     rank = jnp.sum(member * mm(member_bf, earlier), axis=0, keepdims=True)
-    sizes = mm(jnp.ones((8, slots), bf16), member_bf, NT)[:1]
-    sizes = 2.0 * jnp.floor(0.5 * (sizes + 1.0))
+    sizes = mm(jnp.ones((8, slots), bf16), member_bf, NT)
+    sizes = GROUP * jnp.floor((sizes + (GROUP - 1.0)) * (1.0 / GROUP))
     before = (iota((bins, bins), 1) < iota((bins, bins), 0)).astype(f32)
-    begin = jnp.sum(before * sizes, axis=1, keepdims=True)
+    begin = jnp.sum(before * sizes[:1], axis=1, keepdims=True)
     position = jnp.sum(member * begin, axis=0, keepdims=True) + rank
     position = jnp.where(occupied, position.astype(i32), -1)
     chosen = (iota((places, slots), 0) == position).astype(f32).astype(bf16)
@@ -96,43 +103,44 @@
     slot_high = jnp.floor(slot_f * (1.0 / 16.0))
     facts = [slot_high, slot_f - 16.0 * slot_high, source.astype(f32), tile_f, row.astype(f32), jnp.ones((1, slots), f32)]
     facts = jnp.concatenate(facts + [jnp.zeros((2, slots), f32)], axis=0).astype(bf16)
-    found = mm(facts, chosen, NT)
-    valid = found[5:6] > 0.5
-    out[0:1] = (16.0 * found[0:1] + found[1:2]).astype(i32)
-    out[1:2] = jnp.where(valid, found[2:3].astype(i32), col_devs)
-    out[2:3] = found[3:4].astype(i32)
-    out[3:4] = found[4:5].astype(i32)
-    out[4:8] = jnp.zeros((4, places), i32)
-    phases = out.shape[0] - 8
-    phase = iota((phases, bins), 0)
+    found = mm(facts, chosen, NT).astype(i32)
+    source = jnp.where(found[5:6] > 0, found[2:3], col_devs)
+    words = (found[4:5] << ROW_BIT) + (source << SOURCE_BIT) + (found[3:4] << TILE_BIT)
+    out[:, :places] = words + (found[0:1] << 4) + found[1:2]
+    phase = iota((bins, LANES), 1)
     edge = jnp.where(phase > 0, targets + (phase - 1) * slab_tiles, 0)
-    edges = jnp.sum((iota((phases, bins), 1) < edge).astype(f32) * sizes, axis=1, keepdims=True)
-    out[8:] = jnp.broadcast_to(edges.astype(i32), (phases, places))
+    inside = (iota((bins, LANES), 0) < edge).astype(f32).astype(bf16)
+    out[:, places:] = mm(sizes.astype(bf16), inside)[:1].astype(i32)
 
     @pl.loop(0, chunks)
     def _(k):
         tile_copy(k).wait()
 
 
+def field(word, low, high):
+    return (word >> low) & ((1 << (high - low)) - 1)
+
+
 def add_products(plan, phase, first_row, spare_row, tiles, panel_buf, acc):
-    begin, end = plan[8 + phase, 0], plan[9 + phase, 0]
-
-    def panel(p):
-        where = pl.multiple_of(plan[2, p] * LANES, LANES)
-        return panel_buf[plan[1, p], :, pl.ds(where, LANES)]
-
-    @pl.loop(0, (end - begin + 2 * UNROLL - 1) // (2 * UNROLL))
+    phases = plan.shape[1] - LANES
+    begin, end = plan[0, phases + phase], plan[0, phases + phase + 1]
+
+    def panel(word):
+        where = pl.multiple_of(field(word, TILE_BIT, SOURCE_BIT) * LANES, LANES)
+        return panel_buf[field(word, SOURCE_BIT, ROW_BIT), :, pl.ds(where, LANES)]
+
+    @pl.loop(0, (end - begin + GROUP * UNROLL - 1) // (GROUP * UNROLL))
     def _(g):
-        first = begin + g * 2 * UNROLL
+        first = begin + g * GROUP * UNROLL
         parts = []
         for u in range(UNROLL):
-            p = first + 2 * u
-            left = jnp.concatenate([panel(p), panel(p + 1)], axis=1)
-            right = jnp.concatenate([tiles[plan[0, p]], tiles[plan[0, p + 1]]], axis=1)
+            words = [plan[0, first + GROUP * u + i] for i in range(GROUP)]
+            left = jnp.concatenate([panel(word) for word in words], axis=1)
+            right = jnp.concatenate([tiles[field(word, 0, TILE_BIT)] for word in words], axis=1)
             parts.append(mm(left, right, NT))
         for u in range(UNROLL):
-            p = first + 2 * u
-            a = jnp.where(p < end, plan[3, p] - first_row, spare_row)
+            p = first + GROUP * u
+            a = jnp.where(p < end, (plan[0, p] >> ROW_BIT) - first_row, spare_row)
             acc[a] += parts[u]
 
 
@@ -250,6 +258,10 @@
         input_output_aliases={0: 0},
         compiler_params=limit(1),
     )(value, earlier)
+
+
+def in_hbm(value):
+    return pltpu.with_memory_space_constraint(value, pltpu.HBM)
 
 
 def limit(mib):
@@ -307,23 +319,17 @@
         panels[1] = swap(rounded, "col", 1)
 
     with jax.named_scope("plan"):
-        places = -(-(slots + 2 * targets + 2 * UNROLL) // LANES) * LANES
-        plan_rows = 8 + -(-(row_devs + 2) // 8) * 8
+        places = -(-(slots + (GROUP - 1) * 2 * targets + GROUP * UNROLL) // LANES) * LANES
         plan, held = pl.pallas_call(
             functools.partial(plan_kernel, row_devs, col_devs, slab_tiles),
-            out_shape=[jax.ShapeDtypeStruct((plan_rows, places), jnp.int32), pltpu.VMEM(tile_values.shape, bf16)],
-            in_specs=smem(2) + vmem(2) + [pl.BlockSpec(memory_space=pltpu.HBM)],
+            out_shape=[jax.ShapeDtypeStruct((1, places + LANES), jnp.int32), pltpu.VMEM(tile_values.shape, bf16)],
+            in_specs=smem(2) + [pl.BlockSpec(memory_space=pltpu.HBM)] * 3,
             out_specs=vmem(2),
-            scratch_shapes=[pltpu.SemaphoreType.DMA((slots // CHUNK,))],
+            scratch_shapes=[pltpu.VMEM((1, slots), jnp.int32)] * 2
+            + [pltpu.SemaphoreType.DMA((slots // CHUNK,)), pltpu.SemaphoreType.DMA((2,))],
             compiler_params=limit(8),
             cost_estimate=cost(2 * slots * width * tile_len * tile_len),
-        )(
-            place,
-            tile_counts,
-            tile_rows.reshape(1, slots),
-            tile_cols.reshape(1, slots),
-            pltpu.with_memory_space_constraint(tile_values, pltpu.HBM),
-        )
+        )(place, tile_counts, in_hbm(tile_rows.reshape(1, slots)), in_hbm(tile_cols.reshape(1, slots)), in_hbm(tile_values))
 
     with jax.named_scope("early"):
         early = pl.pallas_call(
@@ -387,7 +393,7 @@
             compiler_params=limit(24),
         )(place, base, *received, mass, current_block, stored)
         mine = keep + swap(give, "col", 1)
-        mine = total(total(mine, "col", bits("col")[1:]), "row", bits("row"))
+        mine = total(total(mine, "col", 2), "row", 1)
         other = swap(mine, "col", 1)
 
     with jax.named_scope("residual"):
@@ -406,7 +412,8 @@
         coefficients = coef.T.reshape(stored_count + 1, width, width)
 
     with jax.named_scope("gram"):
-        gram = total(total(gram, "col", bits("col")), "row", bits("row"))
+        gram = gram + swap(gram, "col", 1)
+        gram = total(total(gram, "col", 2), "row", 1)
         gram = jnp.concatenate(
             [gram[:, :width], gram[:, LANES // 2 : LANES // 2 + width]], axis=0
         )

time: 88.3 us -> 79.2 us (0.90)
  waiting for transfers between devices: 30.9 us -> 25.8 us
  starting transfers between devices: 29.7 us -> 26.5 us
  local copies, waits for them, and re-layouts: 2.28 us -> 0.92 us
    ppermute x21 -> x25, waiting for transfers between devices: 30.9 us -> 25.8 us  [swap(): return lax.ppermute(value, axis, [(i, i ^ mask) for i in range(count)])]
    ppermute x21 -> x25, starting transfers between devices: 29.7 us -> 26.5 us  [swap(): return lax.ppermute(value, axis, [(i, i ^ mask) for i in range(count)])]
    unnamed x16 -> x12, local copies, waits for them, and re-layouts: 1.39 us -> 0.03 us
    pallas_call x1, Pallas kernels: 3.19 us -> 4.14 us  [local(): pl.pallas_call(functools.partial(plan_kernel, row_devs, col_devs, slab_ti...]
  transfers between devices with their start and end apart: 21 -> 25, of which waited for: 17 -> 18; matrix products, arithmetic and copies ran while one was open for 1% -> 1% of each run, Pallas kernels for 15% -> 18%
where the time goes in v5:
time: 79.2 us; the launch traced here: 78.6 us
  starting transfers between devices  26.5 us (33%)
  waiting for transfers between devices  25.8 us (33%)
  Pallas kernels  22.1 us (28%)
  other arithmetic  1.76 us (2%)
  between operations  1.44 us (2%)
  local copies, waits for them, and re-layouts  0.92 us (1%)
    ppermute x25, starting transfers between devices, swap(): return lax.ppermute(value, axis, [(i, i ^ mask) for i in range(count)])  26.5 us
    ppermute x25, waiting for transfers between devices, swap(): return lax.ppermute(value, axis, [(i, i ^ mask) for i in range(count)])  25.8 us
    pallas_call x1, Pallas kernels, local(): pl.pallas_call(functools.partial(first_late_kernel, masks[0], 1), out_sha...  4.29 us
    pallas_call x1, Pallas kernels, local(): pl.pallas_call(functools.partial(plan_kernel, row_devs, col_devs, slab_ti...  4.14 us
    pallas_call x1, Pallas kernels, local(): pl.pallas_call(functools.partial(late_kernel, masks[1:]), out_shape=[part...  3.74 us
    pallas_call x1, Pallas kernels, local(): pl.pallas_call(early_kernel, out_shape=pltpu.VMEM(early_shape, f32), in_s...  3.67 us
    pallas_call x1, Pallas kernels, local(): pl.pallas_call(functools.partial(own_kernel, row_devs), out_shape=slab, i...  2.32 us
    pallas_call x1, Pallas kernels, local(): pl.pallas_call(functools.partial(residual_kernel, cells), out_shape=[slab...  2.18 us
  transfers between devices with their start and end apart: 25, of which 18 were waited for; matrix products, arithmetic and copies ran while one was open for 1% of the time, Pallas kernels for 18%

profile of v5, /device:TPU:0, one launch (start us, length us, event | category | flops | bytes accessed | tf_op | source)
XLA Modules:
  0.0 78.6 jit_solution(8135289399706323723)
XLA Ops:
  0.6 1.0 %convert_element_type.3.own_panel.refs_0_ = bf16[48,2048]{1,0:T(8,128)(2,1)S(1)} convert(f32[48,2048]{1,0:T(8,128)} %current.3) | non-fusion elementwise | flops 98304 | bytes 589824 | tf_op jit(solution)/shard_map/gather/convert_element_type | solution.py:315
  1.7 0.5 collective-permute-start
  2.2 3.5 %collective-permute-start.5 = (bf16[48,2048]{1,0:T(8,128)(2,1)S(1)}, bf16[48,2048]{1,0:T(8,128)(2,1)S(1)}, u32[]{:S(2)}, u32[]{:S(2)}) collective-permute-start(bf16[48,2048]{1,0:T(8,128)(2,1)S(1)} %convert_element_type.3.own_panel.refs_0_), channel_id=1, source_target_pairs={{0,6},{1,7},{2,4},{3,5},{4,2},{5,3},{6,0},{7,1},{8,14},{9,15},{10,... | collective-permute-start | bytes 589832 | tf_op jit(solution)/shard_map/gather/ppermute | solution.py:21
  5.7 0.5 collective-permute-start.3
  6.2 0.1 collective-permute-start.1
  7.0 0.1 pad_add_fusion.place
  7.1 4.1 %plan.1 = (s32[1,1152]{1,0:T(1,128)S(1)}, bf16[512,128,128]{2,1,0:T(8,128)(2,1)S(1)}) custom-call(s32[2]{0:T(128)S(1)} %pad_add_fusion.place, s32[1]{0:T(128)S(6)} %copy.21.counts, s32[1,512]{1,0:T(1,128)} %bitcast.16, s32[1,512]{1,0:T(1,128)} %bitcast.17, bf16[512,128,128]{2,1,0:T(8,128)(2,1)} %tiles.1), custom_call_target="tpu_custom_call" | custom-call | flops 805306368 | bytes 16777216 | tf_op jit(solution)/shard_map/plan/pallas_call | solution.py:323
  11.2 0.0 collective-permute-done.near_panel.refs_1_
  11.2 3.7 %early.1.earlier.refs_9_ = f32[65,48,128]{2,1,0:T(8,128)S(1)} custom-call(s32[1,1152]{1,0:T(1,128)S(1)} %get-tuple-element.15.plan, bf16[48,2048]{1,0:T(8,128)(2,1)S(1)} %convert_element_type.3.own_panel.refs_0_, bf16[48,2048]{1,0:T(8,128)(2,1)S(1)} %collective-permute-done.near_panel.refs_1_, bf16[512,128,128]{2,1,0:T(8,128)(2,1)S(1)} %get-tuple-element.16.tiles.refs_8_), custom_call_target="tpu_custom_call" | custom-call | flops 201326592 | bytes 4194304 | tf_op jit(solution)/shard_map/early/pallas_call | solution.py:335
  14.9 0.8 %collective-permute-done.1.value = bf16[48,2048]{1,0:T(8,128)(2,1)S(1)} collective-permute-done((bf16[48,2048]{1,0:T(8,128)(2,1)S(1)}, bf16[48,2048]{1,0:T(8,128)(2,1)S(1)}, u32[]{:S(2)}, u32[]{:S(2)}) %collective-permute-start.1) | collective-permute-done | bytes 196640 | tf_op jit(solution)/shard_map/gather/ppermute | solution.py:21
  15.7 0.0 collective-permute-start.2
  15.7 0.0 collective-permute-done.3.value
  15.7 0.5 collective-permute-start.4
  16.2 0.0 collective-permute-done.5.value
  16.2 0.1 collective-permute-start.6
  16.3 0.8 %collective-permute-done.2.refs_3_ = bf16[48,2048]{1,0:T(8,128)(2,1)S(1)} collective-permute-done((bf16[48,2048]{1,0:T(8,128)(2,1)S(1)}, bf16[48,2048]{1,0:T(8,128)(2,1)S(1)}, u32[]{:S(2)}, u32[]{:S(2)}) %collective-permute-start.2) | collective-permute-done | bytes 196640 | tf_op jit(solution)/shard_map/gather/ppermute | solution.py:21
  17.2 0.3 collective-permute-done.4.refs_5_
  17.4 0.3 collective-permute-done.6.refs_7_
  17.7 4.3 %late.3 = (bf16[48,2048]{1,0:T(8,128)(2,1)S(1)}, bf16[9,48,2048]{2,1,0:T(8,128)(2,1)S(1)}) custom-call(s32[2]{0:T(128)S(1)} %pad_add_fusion.place, s32[1,1152]{1,0:T(1,128)S(1)} %get-tuple-element.15.plan, bf16[48,2048]{1,0:T(8,128)(2,1)S(1)} %convert_element_type.3.own_panel.refs_0_, bf16[48,2048]{1,0:T(8,128)(2,1)S(1)} %collective-permute-done.near_panel.refs_1_, ...), custom_call_target="tpu_custom_call" | custom-call | flops 48 | bytes 1 | tf_op jit(solution)/shard_map/late/pallas_call | solution.py:353
  22.0 3.4 %collective-permute-start.7 = (bf16[48,2048]{1,0:T(8,128)(2,1)S(1)}, bf16[48,2048]{1,0:T(8,128)(2,1)S(1)}, u32[]{:S(2)}, u32[]{:S(2)}) collective-permute-start(bf16[48,2048]{1,0:T(8,128)(2,1)S(1)} %get-tuple-element.18), channel_id=1, source_target_pairs={{0,24},{8,16},{16,8},{24,0},{1,25},{9,17},{17,9},{25,1},{2,26},{10... | collective-permute-start | bytes 589832 | tf_op jit(solution)/shard_map/late/ppermute | solution.py:21
  25.4 3.7 %late.5 = (bf16[48,2048]{1,0:T(8,128)(2,1)S(1)}, bf16[48,2048]{1,0:T(8,128)(2,1)S(1)}) custom-call(s32[2]{0:T(128)S(1)} %pad_add_fusion.place, s32[1,1152]{1,0:T(1,128)S(1)} %get-tuple-element.15.plan, bf16[9,48,2048]{2,1,0:T(8,128)(2,1)S(1)} %get-tuple-element.17.panel_buf, bf16[512,128,128]{2,1,0:T(8,128)(2,1)S(1)} %get-tuple-element.16.tiles.refs_8_, ...), custom_call_target="tpu_custom_call" | custom-call | flops 48 | bytes 1 | tf_op jit(solution)/shard_map/late/pallas_call | solution.py:363
  29.1 0.1 collective-permute-start.8
  29.2 1.4 %collective-permute-start.9 = (bf16[48,2048]{1,0:T(8,128)(2,1)S(1)}, bf16[48,2048]{1,0:T(8,128)(2,1)S(1)}, u32[]{:S(2)}, u32[]{:S(2)}) collective-permute-start(bf16[48,2048]{1,0:T(8,128)(2,1)S(1)} %get-tuple-element.20), channel_id=1, source_target_pairs={{0,8},{8,0},{16,24},{24,16},{1,9},{9,1},{17,25},{25,17},{2,10},{10... | collective-permute-start | bytes 589832 | tf_op jit(solution)/shard_map/late/ppermute | solution.py:21
  30.6 0.1 collective-permute-done.7.received
  30.7 0.0 copy-start
  30.8 0.0 copy-start.3
  30.8 2.3 %late.4.base = f32[48,2048]{1,0:T(8,128)S(1)} custom-call(s32[2]{0:T(128)S(1)} %pad_add_fusion.place, s32[1,1152]{1,0:T(1,128)S(1)} %get-tuple-element.15.plan, bf16[9,48,2048]{2,1,0:T(8,128)(2,1)S(1)} %get-tuple-element.17.panel_buf, bf16[512,128,128]{2,1,0:T(8,128)(2,1)S(1)} %get-tuple-element.16.tiles.refs_8_, f32[65,48,128]{2,1,0:T(8,128)S(1)} %early.1.earlier.refs_9_, ...), custom_call_target="tpu_custom_call" | custom-call | flops 48 | bytes 1 | tf_op jit(solution)/shard_map/late/pallas_call | solution.py:373
  33.1 9.7 %collective-permute-done.8.refs_0_ = bf16[48,2048]{1,0:T(8,128)(2,1)S(1)} collective-permute-done((bf16[48,2048]{1,0:T(8,128)(2,1)S(1)}, bf16[48,2048]{1,0:T(8,128)(2,1)S(1)}, u32[]{:S(2)}, u32[]{:S(2)}) %collective-permute-start.8) | collective-permute-done | bytes 196640 | tf_op jit(solution)/shard_map/late/ppermute | solution.py:21
  42.8 0.0 collective-permute-done.9.refs_1_
  42.8 1.8 %coefficients.1 = (f32[48,2048]{1,0:T(8,128)S(1)}, f32[12,8,128]{2,1,0:T(8,128)S(1)}, f32[12,8,128]{2,1,0:T(8,128)S(1)}) custom-call(s32[2]{0:T(128)S(1)} %pad_add_fusion.place, f32[48,2048]{1,0:T(8,128)S(1)} %late.4.base, bf16[48,2048]{1,0:T(8,128)(2,1)S(1)} %collective-permute-done.8.refs_0_, bf16[48,2048]{1,0:T(8,128)(2,1)S(1)} %collective-permute-done.9.refs_1_, ...), custom_call_target="tpu_custom_call" | custom-call | tf_op jit(solution)/shard_map/coefficients/pallas_call | solution.py:387
  44.6 0.1 collective-permute-start.10
  44.6 1.2 %collective-permute-done.10 = f32[12,8,128]{2,1,0:T(8,128)S(1)} collective-permute-done((f32[12,8,128]{2,1,0:T(8,128)S(1)}, f32[12,8,128]{2,1,0:T(8,128)S(1)}, u32[]{:S(2)}, u32[]{:S(2)}) %collective-permute-start.10) | collective-permute-done | bytes 49184 | tf_op jit(solution)/shard_map/coefficients/ppermute | solution.py:21
  45.9 2.6 %collective-permute-start.13 = (f32[12,8,128]{2,1,0:T(8,128)S(1)}, f32[12,8,128]{2,1,0:T(8,128)S(1)}, u32[]{:S(2)}, u32[]{:S(2)}) collective-permute-start(f32[12,8,128]{2,1,0:T(8,128)S(1)} %add.42), channel_id=1, source_target_pairs={{0,6},{1,7},{2,4},{3,5},{4,2},{5,3},{6,0},{7,1},{8,14},{9,15},{10,... | collective-permute-start | bytes 147464 | tf_op jit(solution)/shard_map/coefficients/ppermute | solution.py:21
  48.5 0.2 collective-permute-start.12
  48.7 0.9 %collective-permute-start.11 = (f32[12,8,128]{2,1,0:T(8,128)S(1)}, f32[12,8,128]{2,1,0:T(8,128)S(1)}, u32[]{:S(2)}, u32[]{:S(2)}) collective-permute-start(f32[12,8,128]{2,1,0:T(8,128)S(1)} %add.42), channel_id=1, source_target_pairs={{0,2},{1,3},{2,0},{3,1},{4,6},{5,7},{6,4},{7,5},{8,10},{9,11},{10,... | collective-permute-start | bytes 147464 | tf_op jit(solution)/shard_map/coefficients/ppermute | solution.py:21
  49.6 1.3 %collective-permute-done.13 = f32[12,8,128]{2,1,0:T(8,128)S(1)} collective-permute-done((f32[12,8,128]{2,1,0:T(8,128)S(1)}, f32[12,8,128]{2,1,0:T(8,128)S(1)}, u32[]{:S(2)}, u32[]{:S(2)}) %collective-permute-start.13) | collective-permute-done | bytes 49184 | tf_op jit(solution)/shard_map/coefficients/ppermute | solution.py:21
  50.9 1.7 %collective-permute-done.12 = f32[12,8,128]{2,1,0:T(8,128)S(1)} collective-permute-done((f32[12,8,128]{2,1,0:T(8,128)S(1)}, f32[12,8,128]{2,1,0:T(8,128)S(1)}, u32[]{:S(2)}, u32[]{:S(2)}) %collective-permute-start.12) | collective-permute-done | bytes 49184 | tf_op jit(solution)/shard_map/coefficients/ppermute | solution.py:21
  52.6 0.2 collective-permute-done.11
  52.8 2.8 %collective-permute-start.16 = (f32[12,8,128]{2,1,0:T(8,128)S(1)}, f32[12,8,128]{2,1,0:T(8,128)S(1)}, u32[]{:S(2)}, u32[]{:S(2)}) collective-permute-start(f32[12,8,128]{2,1,0:T(8,128)S(1)} %add_add_fusion.1), channel_id=1, source_target_pairs={{0,24},{8,16},{16,8},{24,0},{1,25},{9,17},{17,9},{25,1},{2,26},{10... | collective-permute-start | bytes 147464 | tf_op jit(solution)/shard_map/coefficients/ppermute | solution.py:21
  55.6 0.0 collective-permute-start.15
  55.6 1.7 %collective-permute-start.14 = (f32[12,8,128]{2,1,0:T(8,128)S(1)}, f32[12,8,128]{2,1,0:T(8,128)S(1)}, u32[]{:S(2)}, u32[]{:S(2)}) collective-permute-start(f32[12,8,128]{2,1,0:T(8,128)S(1)} %add_add_fusion.1), channel_id=1, source_target_pairs={{0,8},{8,0},{16,24},{24,16},{1,9},{9,1},{17,25},{25,17},{2,10},{10... | collective-permute-start | bytes 147464 | tf_op jit(solution)/shard_map/coefficients/ppermute | solution.py:21
  57.3 1.6 %collective-permute-done.16 = f32[12,8,128]{2,1,0:T(8,128)S(1)} collective-permute-done((f32[12,8,128]{2,1,0:T(8,128)S(1)}, f32[12,8,128]{2,1,0:T(8,128)S(1)}, u32[]{:S(2)}, u32[]{:S(2)}) %collective-permute-start.16) | collective-permute-done | bytes 49184 | tf_op jit(solution)/shard_map/coefficients/ppermute | solution.py:21
  58.9 1.7 %collective-permute-done.15 = f32[12,8,128]{2,1,0:T(8,128)S(1)} collective-permute-done((f32[12,8,128]{2,1,0:T(8,128)S(1)}, f32[12,8,128]{2,1,0:T(8,128)S(1)}, u32[]{:S(2)}, u32[]{:S(2)}) %collective-permute-start.15) | collective-permute-done | bytes 49184 | tf_op jit(solution)/shard_map/coefficients/ppermute | solution.py:21
  60.6 0.0 collective-permute-done.14
  60.6 0.1 collective-permute-start.17
  60.7 1.2 %collective-permute-done.17.other = f32[12,8,128]{2,1,0:T(8,128)S(1)} collective-permute-done((f32[12,8,128]{2,1,0:T(8,128)S(1)}, f32[12,8,128]{2,1,0:T(8,128)S(1)}, u32[]{:S(2)}, u32[]{:S(2)}) %collective-permute-start.17) | collective-permute-done | bytes 49184 | tf_op jit(solution)/shard_map/coefficients/ppermute | solution.py:21
  61.9 2.2 %residual.1 = (f32[48,2048]{1,0:T(8,128)}, f32[48,432]{1,0:T(8,128)S(1)}, f32[24,128]{1,0:T(8,128)S(1)}) custom-call(s32[2]{0:T(128)S(1)} %pad_add_fusion.place, f32[12,8,128]{2,1,0:T(8,128)S(1)} %add_add_fusion.mine, f32[12,8,128]{2,1,0:T(8,128)S(1)} %collective-permute-done.17.other, f32[48,2048]{1,0:T(8,128)S(1)} %get-tuple-element.23.recurrence, ...), custom_call_target="tpu_custom_call" | custom-call | tf_op jit(solution)/shard_map/residual/pallas_call | solution.py:400
  64.1 0.2 collective-permute-start.18
  64.3 1.0 %collective-permute-done.18 = f32[24,128]{1,0:T(8,128)S(1)} collective-permute-done((f32[24,128]{1,0:T(8,128)S(1)}, f32[24,128]{1,0:T(8,128)S(1)}, u32[]{:S(2)}, u32[]{:S(2)}) %collective-permute-start.18) | collective-permute-done | bytes 12320 | tf_op jit(solution)/shard_map/gram/ppermute | solution.py:21
  65.3 2.3 %collective-permute-start.21 = (f32[24,128]{1,0:T(8,128)S(1)}, f32[24,128]{1,0:T(8,128)S(1)}, u32[]{:S(2)}, u32[]{:S(2)}) collective-permute-start(f32[24,128]{1,0:T(8,128)S(1)} %add.49), channel_id=1, source_target_pairs={{0,6},{1,7},{2,4},{3,5},{4,2},{5,3},{6,0},{7,1},{8,14},{9,15},{10,... | collective-permute-start | bytes 36872 | tf_op jit(solution)/shard_map/gram/ppermute | solution.py:21
  67.6 0.0 collective-permute-start.20
  67.6 1.2 %collective-permute-start.19 = (f32[24,128]{1,0:T(8,128)S(1)}, f32[24,128]{1,0:T(8,128)S(1)}, u32[]{:S(2)}, u32[]{:S(2)}) collective-permute-start(f32[24,128]{1,0:T(8,128)S(1)} %add.49), channel_id=1, source_target_pairs={{0,2},{1,3},{2,0},{3,1},{4,6},{5,7},{6,4},{7,5},{8,10},{9,11},{10,... | collective-permute-start | bytes 36872 | tf_op jit(solution)/shard_map/gram/ppermute | solution.py:21
  68.8 1.1 %collective-permute-done.21 = f32[24,128]{1,0:T(8,128)S(1)} collective-permute-done((f32[24,128]{1,0:T(8,128)S(1)}, f32[24,128]{1,0:T(8,128)S(1)}, u32[]{:S(2)}, u32[]{:S(2)}) %collective-permute-start.21) | collective-permute-done | bytes 12320 | tf_op jit(solution)/shard_map/gram/ppermute | solution.py:21
  69.9 1.4 %collective-permute-done.20 = f32[24,128]{1,0:T(8,128)S(1)} collective-permute-done((f32[24,128]{1,0:T(8,128)S(1)}, f32[24,128]{1,0:T(8,128)S(1)}, u32[]{:S(2)}, u32[]{:S(2)}) %collective-permute-start.20) | collective-permute-done | bytes 12320 | tf_op jit(solution)/shard_map/gram/ppermute | solution.py:21
  71.3 0.0 collective-permute-done.19
  71.3 2.0 %collective-permute-start.24 = (f32[24,128]{1,0:T(8,128)S(1)}, f32[24,128]{1,0:T(8,128)S(1)}, u32[]{:S(2)}, u32[]{:S(2)}) collective-permute-start(f32[24,128]{1,0:T(8,128)S(1)} %add_add_fusion.3), channel_id=1, source_target_pairs={{0,24},{8,16},{16,8},{24,0},{1,25},{9,17},{17,9},{25,1},{2,26},{10... | collective-permute-start | bytes 36872 | tf_op jit(solution)/shard_map/gram/ppermute | solution.py:21
  73.3 0.3 collective-permute-start.23
  73.7 2.1 %collective-permute-start.22 = (f32[24,128]{1,0:T(8,128)S(1)}, f32[24,128]{1,0:T(8,128)S(1)}, u32[]{:S(2)}, u32[]{:S(2)}) collective-permute-start(f32[24,128]{1,0:T(8,128)S(1)} %add_add_fusion.3), channel_id=1, source_target_pairs={{0,8},{8,0},{16,24},{24,16},{1,9},{9,1},{17,25},{25,17},{2,10},{10... | collective-permute-start | bytes 36872 | tf_op jit(solution)/shard_map/gram/ppermute | solution.py:21
  75.8 0.8 %copy.17 = f32[432,48]{1,0:T(8,128)} copy(f32[432,48]{0,1:T(8,128)S(1)} %bitcast.11) | data formatting | bytes 165888 | tf_op jit(solution)/shard_map/residual/transpose | solution.py:412
  76.6 0.3 collective-permute-done.24
  76.9 1.1 %collective-permute-done.23 = f32[24,128]{1,0:T(8,128)S(1)} collective-permute-done((f32[24,128]{1,0:T(8,128)S(1)}, f32[24,128]{1,0:T(8,128)S(1)}, u32[]{:S(2)}, u32[]{:S(2)}) %collective-permute-start.23) | collective-permute-done | bytes 12320 | tf_op jit(solution)/shard_map/gram/ppermute | solution.py:21
  77.9 0.0 collective-permute-done.22
  77.9 0.1 fusion
  78.0 0.6 pad_maximum_fusion
  (19 shorter events, 0.1 us)
Async XLA Ops:
  1.7 9.6 %collective-permute-start = (bf16[48,2048]{1,0:T(8,128)(2,1)S(1)}, bf16[48,2048]{1,0:T(8,128)(2,1)S(1)}, u32[]{:S(2)}, u32[]{:S(2)}) collective-permute-start(bf16[48,2048]{1,0:T(8,128)(2,1)S(1)} %convert_element_type.3.own_panel.refs_0_), channel_id=1, source_target_pairs={{0,1},{1,0},{2,3},{3,2},{4,5},{5,4},{6,7},{7,6},{8,9},{9,8},{10,11... | collective-permute-start | bytes 589832 | tf_op jit(solution)/shard_map/gather/ppermute | solution.py:21
  2.2 14.1 %collective-permute-start.5 = (bf16[48,2048]{1,0:T(8,128)(2,1)S(1)}, bf16[48,2048]{1,0:T(8,128)(2,1)S(1)}, u32[]{:S(2)}, u32[]{:S(2)}) collective-permute-start(bf16[48,2048]{1,0:T(8,128)(2,1)S(1)} %convert_element_type.3.own_panel.refs_0_), channel_id=1, source_target_pairs={{0,6},{1,7},{2,4},{3,5},{4,2},{5,3},{6,0},{7,1},{8,14},{9,15},{10,... | collective-permute-start | bytes 589832 | tf_op jit(solution)/shard_map/gather/ppermute | solution.py:21
  5.7 10.0 %collective-permute-start.3 = (bf16[48,2048]{1,0:T(8,128)(2,1)S(1)}, bf16[48,2048]{1,0:T(8,128)(2,1)S(1)}, u32[]{:S(2)}, u32[]{:S(2)}) collective-permute-start(bf16[48,2048]{1,0:T(8,128)(2,1)S(1)} %convert_element_type.3.own_panel.refs_0_), channel_id=1, source_target_pairs={{0,4},{1,5},{2,6},{3,7},{4,0},{5,1},{6,2},{7,3},{8,12},{9,13},{10,... | collective-permute-start | bytes 589832 | tf_op jit(solution)/shard_map/gather/ppermute | solution.py:21
  6.2 9.5 %collective-permute-start.1 = (bf16[48,2048]{1,0:T(8,128)(2,1)S(1)}, bf16[48,2048]{1,0:T(8,128)(2,1)S(1)}, u32[]{:S(2)}, u32[]{:S(2)}) collective-permute-start(bf16[48,2048]{1,0:T(8,128)(2,1)S(1)} %convert_element_type.3.own_panel.refs_0_), channel_id=1, source_target_pairs={{0,2},{1,3},{2,0},{3,1},{4,6},{5,7},{6,4},{7,5},{8,10},{9,11},{10,... | collective-permute-start | bytes 589832 | tf_op jit(solution)/shard_map/gather/ppermute | solution.py:21
  15.7 1.4 %collective-permute-start.2 = (bf16[48,2048]{1,0:T(8,128)(2,1)S(1)}, bf16[48,2048]{1,0:T(8,128)(2,1)S(1)}, u32[]{:S(2)}, u32[]{:S(2)}) collective-permute-start(bf16[48,2048]{1,0:T(8,128)(2,1)S(1)} %gather.3.refs_2_), channel_id=1, source_target_pairs={{0,1},{1,0},{2,3},{3,2},{4,5},{5,4},{6,7},{7,6},{8,9},{9,8},{10,11... | collective-permute-start | bytes 589832 | tf_op jit(solution)/shard_map/gather/ppermute | solution.py:21
  15.7 1.7 %collective-permute-start.4 = (bf16[48,2048]{1,0:T(8,128)(2,1)S(1)}, bf16[48,2048]{1,0:T(8,128)(2,1)S(1)}, u32[]{:S(2)}, u32[]{:S(2)}) collective-permute-start(bf16[48,2048]{1,0:T(8,128)(2,1)S(1)} %gather.4.refs_4_), channel_id=1, source_target_pairs={{0,1},{1,0},{2,3},{3,2},{4,5},{5,4},{6,7},{7,6},{8,9},{9,8},{10,11... | collective-permute-start | bytes 589832 | tf_op jit(solution)/shard_map/gather/ppermute | solution.py:21
  16.2 1.5 %collective-permute-start.6 = (bf16[48,2048]{1,0:T(8,128)(2,1)S(1)}, bf16[48,2048]{1,0:T(8,128)(2,1)S(1)}, u32[]{:S(2)}, u32[]{:S(2)}) collective-permute-start(bf16[48,2048]{1,0:T(8,128)(2,1)S(1)} %gather.5.refs_6_), channel_id=1, source_target_pairs={{0,1},{1,0},{2,3},{3,2},{4,5},{5,4},{6,7},{7,6},{8,9},{9,8},{10,11... | collective-permute-start | bytes 589832 | tf_op jit(solution)/shard_map/gather/ppermute | solution.py:21
  22.0 8.7 %collective-permute-start.7 = (bf16[48,2048]{1,0:T(8,128)(2,1)S(1)}, bf16[48,2048]{1,0:T(8,128)(2,1)S(1)}, u32[]{:S(2)}, u32[]{:S(2)}) collective-permute-start(bf16[48,2048]{1,0:T(8,128)(2,1)S(1)} %get-tuple-element.18), channel_id=1, source_target_pairs={{0,24},{8,16},{16,8},{24,0},{1,25},{9,17},{17,9},{25,1},{2,26},{10... | collective-permute-start | bytes 589832 | tf_op jit(solution)/shard_map/late/ppermute | solution.py:21
  25.4 5.3 %copy-start.1 = (f32[48,2048]{1,0:T(8,128)S(1)}, f32[48,2048]{1,0:T(8,128)}, u32[]{:S(2)}) copy-start(f32[48,2048]{1,0:T(8,128)} %current.3) | copy-start | bytes 1179652
  25.4 5.3 %copy-start.2 = (f32[48,2048]{1,0:T(8,128)S(1)}, f32[48,2048]{1,0:T(8,128)}, u32[]{:S(2)}) copy-start(f32[48,2048]{1,0:T(8,128)} %previous.1) | copy-start | bytes 1179652
  25.4 5.3 %copy-start.4 = (f32[48,48]{1,0:T(8,128)S(1)}, f32[48,48]{1,0:T(8,128)}, u32[]{:S(2)}) copy-start(f32[48,48]{1,0:T(8,128)} %coupling.1) | copy-start | bytes 27652
  25.4 5.4 %copy-start.5 = (f32[2048]{0:T(1024)S(1)}, f32[2048]{0:T(1024)}, u32[]{:S(2)}) copy-start(f32[2048]{0:T(1024)} %param.14) | copy-start | bytes 24580
  29.1 13.6 %collective-permute-start.8 = (bf16[48,2048]{1,0:T(8,128)(2,1)S(1)}, bf16[48,2048]{1,0:T(8,128)(2,1)S(1)}, u32[]{:S(2)}, u32[]{:S(2)}) collective-permute-start(bf16[48,2048]{1,0:T(8,128)(2,1)S(1)} %get-tuple-element.19), channel_id=1, source_target_pairs={{0,16},{8,24},{16,0},{24,8},{1,17},{9,25},{17,1},{25,9},{2,18},{10... | collective-permute-start | bytes 589832 | tf_op jit(solution)/shard_map/late/ppermute | solution.py:21
  29.2 13.6 %collective-permute-start.9 = (bf16[48,2048]{1,0:T(8,128)(2,1)S(1)}, bf16[48,2048]{1,0:T(8,128)(2,1)S(1)}, u32[]{:S(2)}, u32[]{:S(2)}) collective-permute-start(bf16[48,2048]{1,0:T(8,128)(2,1)S(1)} %get-tuple-element.20), channel_id=1, source_target_pairs={{0,8},{8,0},{16,24},{24,16},{1,9},{9,1},{17,25},{25,17},{2,10},{10... | collective-permute-start | bytes 589832 | tf_op jit(solution)/shard_map/late/ppermute | solution.py:21
  30.7 12.0 %copy-start = (f32[8,48,2048]{2,1,0:T(8,128)S(1)}, f32[8,48,2048]{2,1,0:T(8,128)}, u32[]{:S(2)}) copy-start(f32[8,48,2048]{2,1,0:T(8,128)} %param.13) | copy-start | bytes 9437188
  30.8 12.0 %copy-start.3 = (f32[2048]{0:T(1024)S(1)}, f32[2048]{0:T(1024)}, u32[]{:S(2)}) copy-start(f32[2048]{0:T(1024)} %param.15) | copy-start | bytes 24580
  44.6 1.3 %collective-permute-start.10 = (f32[12,8,128]{2,1,0:T(8,128)S(1)}, f32[12,8,128]{2,1,0:T(8,128)S(1)}, u32[]{:S(2)}, u32[]{:S(2)}) collective-permute-start(f32[12,8,128]{2,1,0:T(8,128)S(1)} %get-tuple-element.22), channel_id=1, source_target_pairs={{0,1},{1,0},{2,3},{3,2},{4,5},{5,4},{6,7},{7,6},{8,9},{9,8},{10,11... | collective-permute-start | bytes 147464 | tf_op jit(solution)/shard_map/coefficients/ppermute | solution.py:21
  45.9 5.0 %collective-permute-start.13 = (f32[12,8,128]{2,1,0:T(8,128)S(1)}, f32[12,8,128]{2,1,0:T(8,128)S(1)}, u32[]{:S(2)}, u32[]{:S(2)}) collective-permute-start(f32[12,8,128]{2,1,0:T(8,128)S(1)} %add.42), channel_id=1, source_target_pairs={{0,6},{1,7},{2,4},{3,5},{4,2},{5,3},{6,0},{7,1},{8,14},{9,15},{10,... | collective-permute-start | bytes 147464 | tf_op jit(solution)/shard_map/coefficients/ppermute | solution.py:21
  48.5 4.1 %collective-permute-start.12 = (f32[12,8,128]{2,1,0:T(8,128)S(1)}, f32[12,8,128]{2,1,0:T(8,128)S(1)}, u32[]{:S(2)}, u32[]{:S(2)}) collective-permute-start(f32[12,8,128]{2,1,0:T(8,128)S(1)} %add.42), channel_id=1, source_target_pairs={{0,4},{1,5},{2,6},{3,7},{4,0},{5,1},{6,2},{7,3},{8,12},{9,13},{10,... | collective-permute-start | bytes 147464 | tf_op jit(solution)/shard_map/coefficients/ppermute | solution.py:21
  48.7 4.1 %collective-permute-start.11 = (f32[12,8,128]{2,1,0:T(8,128)S(1)}, f32[12,8,128]{2,1,0:T(8,128)S(1)}, u32[]{:S(2)}, u32[]{:S(2)}) collective-permute-start(f32[12,8,128]{2,1,0:T(8,128)S(1)} %add.42), channel_id=1, source_target_pairs={{0,2},{1,3},{2,0},{3,1},{4,6},{5,7},{6,4},{7,5},{8,10},{9,11},{10,... | collective-permute-start | bytes 147464 | tf_op jit(solution)/shard_map/coefficients/ppermute | solution.py:21
  52.8 6.1 %collective-permute-start.16 = (f32[12,8,128]{2,1,0:T(8,128)S(1)}, f32[12,8,128]{2,1,0:T(8,128)S(1)}, u32[]{:S(2)}, u32[]{:S(2)}) collective-permute-start(f32[12,8,128]{2,1,0:T(8,128)S(1)} %add_add_fusion.1), channel_id=1, source_target_pairs={{0,24},{8,16},{16,8},{24,0},{1,25},{9,17},{17,9},{25,1},{2,26},{10... | collective-permute-start | bytes 147464 | tf_op jit(solution)/shard_map/coefficients/ppermute | solution.py:21
  55.6 5.0 %collective-permute-start.15 = (f32[12,8,128]{2,1,0:T(8,128)S(1)}, f32[12,8,128]{2,1,0:T(8,128)S(1)}, u32[]{:S(2)}, u32[]{:S(2)}) collective-permute-start(f32[12,8,128]{2,1,0:T(8,128)S(1)} %add_add_fusion.1), channel_id=1, source_target_pairs={{0,16},{8,24},{16,0},{24,8},{1,17},{9,25},{17,1},{25,9},{2,18},{10... | collective-permute-start | bytes 147464 | tf_op jit(solution)/shard_map/coefficients/ppermute | solution.py:21
  55.6 5.0 %collective-permute-start.14 = (f32[12,8,128]{2,1,0:T(8,128)S(1)}, f32[12,8,128]{2,1,0:T(8,128)S(1)}, u32[]{:S(2)}, u32[]{:S(2)}) collective-permute-start(f32[12,8,128]{2,1,0:T(8,128)S(1)} %add_add_fusion.1), channel_id=1, source_target_pairs={{0,8},{8,0},{16,24},{24,16},{1,9},{9,1},{17,25},{25,17},{2,10},{10... | collective-permute-start | bytes 147464 | tf_op jit(solution)/shard_map/coefficients/ppermute | solution.py:21
  60.6 1.3 %collective-permute-start.17 = (f32[12,8,128]{2,1,0:T(8,128)S(1)}, f32[12,8,128]{2,1,0:T(8,128)S(1)}, u32[]{:S(2)}, u32[]{:S(2)}) collective-permute-start(f32[12,8,128]{2,1,0:T(8,128)S(1)} %add_add_fusion.mine), channel_id=1, source_target_pairs={{0,1},{1,0},{2,3},{3,2},{4,5},{5,4},{6,7},{7,6},{8,9},{9,8},{10,11... | collective-permute-start | bytes 147464 | tf_op jit(solution)/shard_map/coefficients/ppermute | solution.py:21
  64.1 1.2 %collective-permute-start.18 = (f32[24,128]{1,0:T(8,128)S(1)}, f32[24,128]{1,0:T(8,128)S(1)}, u32[]{:S(2)}, u32[]{:S(2)}) collective-permute-start(f32[24,128]{1,0:T(8,128)S(1)} %get-tuple-element.26), channel_id=1, source_target_pairs={{0,1},{1,0},{2,3},{3,2},{4,5},{5,4},{6,7},{7,6},{8,9},{9,8},{10,11... | collective-permute-start | bytes 36872 | tf_op jit(solution)/shard_map/gram/ppermute | solution.py:21
  65.3 4.6 %collective-permute-start.21 = (f32[24,128]{1,0:T(8,128)S(1)}, f32[24,128]{1,0:T(8,128)S(1)}, u32[]{:S(2)}, u32[]{:S(2)}) collective-permute-start(f32[24,128]{1,0:T(8,128)S(1)} %add.49), channel_id=1, source_target_pairs={{0,6},{1,7},{2,4},{3,5},{4,2},{5,3},{6,0},{7,1},{8,14},{9,15},{10,... | collective-permute-start | bytes 36872 | tf_op jit(solution)/shard_map/gram/ppermute | solution.py:21
  67.6 3.7 %collective-permute-start.20 = (f32[24,128]{1,0:T(8,128)S(1)}, f32[24,128]{1,0:T(8,128)S(1)}, u32[]{:S(2)}, u32[]{:S(2)}) collective-permute-start(f32[24,128]{1,0:T(8,128)S(1)} %add.49), channel_id=1, source_target_pairs={{0,4},{1,5},{2,6},{3,7},{4,0},{5,1},{6,2},{7,3},{8,12},{9,13},{10,... | collective-permute-start | bytes 36872 | tf_op jit(solution)/shard_map/gram/ppermute | solution.py:21
  67.6 3.7 %collective-permute-start.19 = (f32[24,128]{1,0:T(8,128)S(1)}, f32[24,128]{1,0:T(8,128)S(1)}, u32[]{:S(2)}, u32[]{:S(2)}) collective-permute-start(f32[24,128]{1,0:T(8,128)S(1)} %add.49), channel_id=1, source_target_pairs={{0,2},{1,3},{2,0},{3,1},{4,6},{5,7},{6,4},{7,5},{8,10},{9,11},{10,... | collective-permute-start | bytes 36872 | tf_op jit(solution)/shard_map/gram/ppermute | solution.py:21
  71.3 5.6 %collective-permute-start.24 = (f32[24,128]{1,0:T(8,128)S(1)}, f32[24,128]{1,0:T(8,128)S(1)}, u32[]{:S(2)}, u32[]{:S(2)}) collective-permute-start(f32[24,128]{1,0:T(8,128)S(1)} %add_add_fusion.3), channel_id=1, source_target_pairs={{0,24},{8,16},{16,8},{24,0},{1,25},{9,17},{17,9},{25,1},{2,26},{10... | collective-permute-start | bytes 36872 | tf_op jit(solution)/shard_map/gram/ppermute | solution.py:21
  73.3 4.6 %collective-permute-start.23 = (f32[24,128]{1,0:T(8,128)S(1)}, f32[24,128]{1,0:T(8,128)S(1)}, u32[]{:S(2)}, u32[]{:S(2)}) collective-permute-start(f32[24,128]{1,0:T(8,128)S(1)} %add_add_fusion.3), channel_id=1, source_target_pairs={{0,16},{8,24},{16,0},{24,8},{1,17},{9,25},{17,1},{25,9},{2,18},{10... | collective-permute-start | bytes 36872 | tf_op jit(solution)/shard_map/gram/ppermute | solution.py:21
  73.7 4.3 %collective-permute-start.22 = (f32[24,128]{1,0:T(8,128)S(1)}, f32[24,128]{1,0:T(8,128)S(1)}, u32[]{:S(2)}, u32[]{:S(2)}) collective-permute-start(f32[24,128]{1,0:T(8,128)S(1)} %add_add_fusion.3), channel_id=1, source_target_pairs={{0,8},{8,0},{16,24},{24,16},{1,9},{9,1},{17,25},{25,17},{2,10},{10... | collective-permute-start | bytes 36872 | tf_op jit(solution)/shard_map/gram/ppermute | solution.py:21

commit v6 on v5

--- a/solution.py
+++ b/solution.py
@@ -9,7 +9,7 @@
 
 LANES = 128
 CHUNK = 32
-GROUP = 4
+GROUP = 2
 UNROLL = 4
 TILE_BIT, SOURCE_BIT, ROW_BIT = 10, 15, 20
 NT = (((1,), (1,)), ((), ()))
@@ -50,8 +50,27 @@
     return [(q, k) for q in range(0, shape[0], 8) for k in range(0, shape[1], LANES)]
 
 
-def plan_kernel(
-    row_devs, col_devs, slab_tiles, place, counts, rows_hbm, cols_hbm, tiles, out, held, rows, cols, sem, list_sem
+def early_kernel(
+    row_devs,
+    col_devs,
+    slab_tiles,
+    place,
+    counts,
+    rows_hbm,
+    cols_hbm,
+    tiles,
+    own_panel,
+    near_panel,
+    out,
+    held,
+    acc,
+    rows,
+    cols,
+    plan,
+    panel_buf,
+    tile_sem,
+    list_sem,
+    panel_sem,
 ):
     chunks = (counts[0] + CHUNK - 1) // CHUNK
     row_copy = pltpu.make_async_copy(rows_hbm, rows, list_sem.at[0])
@@ -61,12 +80,13 @@
 
     def tile_copy(k):
         window = pl.ds(k * CHUNK, CHUNK)
-        return pltpu.make_async_copy(tiles.at[window], held.at[window], sem.at[k])
+        return pltpu.make_async_copy(tiles.at[window], held.at[window], tile_sem.at[k])
 
     @pl.loop(0, chunks)
     def _(k):
         tile_copy(k).start()
 
+    copies = load_panels((own_panel, near_panel), panel_buf, panel_sem)
     f32, bf16, i32 = jnp.float32, jnp.bfloat16, jnp.int32
     slots, places = rows.shape[1], out.shape[1] - LANES
     targets = row_devs * slab_tiles
@@ -111,10 +131,17 @@
     edge = jnp.where(phase > 0, targets + (phase - 1) * slab_tiles, 0)
     inside = (iota((bins, LANES), 0) < edge).astype(f32).astype(bf16)
     out[:, places:] = mm(sizes.astype(bf16), inside)[:1].astype(i32)
+    plan_copy = pltpu.make_async_copy(out, plan, list_sem.at[2])
+    plan_copy.start()
+    acc[...] = jnp.zeros_like(acc)
+    for copy in copies + [plan_copy]:
+        copy.wait()
 
     @pl.loop(0, chunks)
     def _(k):
         tile_copy(k).wait()
+
+    add_products(plan, 0, 0, targets, held, panel_buf, acc)
 
 
 def field(word, low, high):
@@ -153,33 +180,28 @@
     return copies
 
 
-def early_kernel(plan, own_panel, near_panel, tiles, acc, panel_buf, sem):
-    copies = load_panels((own_panel, near_panel), panel_buf, sem)
-    acc[...] = jnp.zeros_like(acc)
-    for copy in copies:
-        copy.wait()
-    add_products(plan, 0, 0, acc.shape[0] - 1, tiles, panel_buf, acc)
-
-
-def first_late_kernel(mask, phase, place, plan, *refs):
+def first_late_kernel(mask, place, plan, *refs):
     panels = refs[:-6]
     tiles, early, send, panel_buf, acc, sem = refs[-6:]
     copies = load_panels(panels, panel_buf, sem)
-    late_part(mask, phase, place, plan, tiles, early, panel_buf, acc, copies)
+    late_part(mask, place, plan, tiles, early, panel_buf, acc, copies)
     put(send, acc)
 
 
 def late_kernel(masks, place, plan, panel_buf, tiles, early, *refs):
     acc = refs[-1]
-    for phase, (mask, send) in enumerate(zip(masks, refs), 2):
-        late_part(mask, phase, place, plan, tiles, early, panel_buf, acc, ())
+    if masks is None:
+        inner = (place[0] == 1) | (place[0] == 2)
+        masks = (jnp.where(inner, 1, 2), jnp.where(inner, 2, 1))
+    for mask, send in zip(masks, refs):
+        late_part(mask, place, plan, tiles, early, panel_buf, acc, ())
         put(send, acc)
 
 
-def own_kernel(phase, place, plan, panel_buf, tiles, early, received, current, previous, coupling, diag, base, acc):
-    late_part(0, phase, place, plan, tiles, early, panel_buf, acc, ())
+def own_kernel(place, plan, panel_buf, tiles, early, current, previous, coupling, diag, base, acc):
+    late_part(0, place, plan, tiles, early, panel_buf, acc, ())
     put(base, acc)
-    base[...] += received[...].astype(jnp.float32) + diag[...] * current[...] - jnp.dot(
+    base[...] += diag[...] * current[...] - jnp.dot(
         coupling[...],
         previous[...],
         precision=lax.Precision.HIGHEST,
@@ -187,14 +209,15 @@
     )
 
 
-def late_part(mask, phase, place, plan, tiles, early, panel_buf, acc, copies):
+def late_part(mask, place, plan, tiles, early, panel_buf, acc, copies):
     slab_tiles = acc.shape[0] - 1
+    row_devs = (early.shape[0] - 1) // slab_tiles
     first_row = (place[0] ^ mask) * slab_tiles
     for s in range(slab_tiles):
         acc[s] = early[first_row + s]
     for copy in copies:
         copy.wait()
-    add_products(plan, phase, first_row, slab_tiles, tiles, panel_buf, acc)
+    add_products(plan, row_devs - mask, first_row, slab_tiles, tiles, panel_buf, acc)
 
 
 def put(out, acc):
@@ -318,29 +341,38 @@
             panels[m] = swap(rounded, "col", m)
         panels[1] = swap(rounded, "col", 1)
 
-    with jax.named_scope("plan"):
+    with jax.named_scope("early"):
         places = -(-(slots + (GROUP - 1) * 2 * targets + GROUP * UNROLL) // LANES) * LANES
-        plan, held = pl.pallas_call(
-            functools.partial(plan_kernel, row_devs, col_devs, slab_tiles),
-            out_shape=[jax.ShapeDtypeStruct((1, places + LANES), jnp.int32), pltpu.VMEM(tile_values.shape, bf16)],
-            in_specs=smem(2) + [pl.BlockSpec(memory_space=pltpu.HBM)] * 3,
-            out_specs=vmem(2),
-            scratch_shapes=[pltpu.VMEM((1, slots), jnp.int32)] * 2
-            + [pltpu.SemaphoreType.DMA((slots // CHUNK,)), pltpu.SemaphoreType.DMA((2,))],
-            compiler_params=limit(8),
+        plan_shape = (1, places + LANES)
+        plan, held, early = pl.pallas_call(
+            functools.partial(early_kernel, row_devs, col_devs, slab_tiles),
+            out_shape=[
+                jax.ShapeDtypeStruct(plan_shape, jnp.int32),
+                pltpu.VMEM(tile_values.shape, bf16),
+                pltpu.VMEM(early_shape, f32),
+            ],
+            in_specs=smem(2) + [pl.BlockSpec(memory_space=pltpu.HBM)] * 3 + anywhere * 2,
+            out_specs=vmem(3),
+            scratch_shapes=[
+                pltpu.VMEM((1, slots), jnp.int32),
+                pltpu.VMEM((1, slots), jnp.int32),
+                pltpu.SMEM(plan_shape, jnp.int32),
+                pltpu.VMEM(panel_shape, bf16),
+                pltpu.SemaphoreType.DMA((slots // CHUNK,)),
+                pltpu.SemaphoreType.DMA((3,)),
+                pltpu.SemaphoreType.DMA((2,)),
+            ],
+            compiler_params=limit(12),
             cost_estimate=cost(2 * slots * width * tile_len * tile_len),
-        )(place, tile_counts, in_hbm(tile_rows.reshape(1, slots)), in_hbm(tile_cols.reshape(1, slots)), in_hbm(tile_values))
-
-    with jax.named_scope("early"):
-        early = pl.pallas_call(
-            early_kernel,
-            out_shape=pltpu.VMEM(early_shape, f32),
-            in_specs=smem(1) + anywhere * 2 + vmem(1),
-            out_specs=vmem(1)[0],
-            scratch_shapes=[pltpu.VMEM(panel_shape, bf16), pltpu.SemaphoreType.DMA((2,))],
-            compiler_params=limit(8),
-            cost_estimate=cost(slots * width * tile_len * tile_len // 2),
-        )(plan, panels[0], panels[1], held)
+        )(
+            place,
+            tile_counts,
+            in_hbm(tile_rows.reshape(1, slots)),
+            in_hbm(tile_cols.reshape(1, slots)),
+            in_hbm(tile_values),
+            panels[0],
+            panels[1],
+        )
 
     with jax.named_scope("gather"):
         for m in range(col_devs - 2, 0, -2):
@@ -348,10 +380,9 @@
             panels[m + 1] = swap(panels[m], "col", 1)
 
     with jax.named_scope("late"):
-        masks = list(range(row_devs - 1, 0, -1))
         part = jax.ShapeDtypeStruct((width, slab_len), bf16)
         first, gathered = pl.pallas_call(
-            functools.partial(first_late_kernel, masks[0], 1),
+            functools.partial(first_late_kernel, row_devs - 1),
             out_shape=[part, pltpu.VMEM(panel_shape, bf16)],
             in_specs=smem(2) + anywhere * col_devs + vmem(2),
             out_specs=vmem(2),
@@ -359,26 +390,36 @@
             compiler_params=limit(8),
             cost_estimate=cost(width),
         )(place, plan, *panels, held, early)
-        first = swap(first, "row", masks[0])
+        relay = row_devs == 4
+        masks = None if relay else list(range(row_devs - 2, 0, -1))
+        parts = [part, slab] if relay else [part] * (row_devs - 2)
         others = pl.pallas_call(
-            functools.partial(late_kernel, masks[1:]),
-            out_shape=[part] * len(masks[1:]),
+            functools.partial(late_kernel, masks),
+            out_shape=parts,
             in_specs=smem(2) + vmem(3),
-            out_specs=vmem(len(masks[1:])),
+            out_specs=vmem(len(parts)),
             scratch_shapes=[part_acc],
             compiler_params=limit(8),
             cost_estimate=cost(width),
         )(place, plan, gathered, held, early)
-        received = [swap(other, "row", m) for m, other in zip(masks[1:], others)]
+        if relay:
+            passing = lax.ppermute(first, "row", [(0, 1), (3, 2)])
+            received = [lax.ppermute(first, "row", [(1, 2), (2, 1)])]
+            received.append(lax.ppermute(others[0], "row", [(0, 2), (3, 1), (1, 0), (2, 3)]))
+            joined = (others[1] + passing.astype(f32)).astype(bf16)
+            received.append(lax.ppermute(joined, "row", [(0, 1), (1, 3), (3, 2), (2, 0)]))
+        else:
+            received = [swap(first, "row", row_devs - 1)]
+            received += [swap(other, "row", m) for m, other in zip(masks, others)]
         base = pl.pallas_call(
-            functools.partial(own_kernel, row_devs),
+            own_kernel,
             out_shape=slab,
-            in_specs=smem(2) + vmem(8),
+            in_specs=smem(2) + vmem(7),
             out_specs=vmem(1)[0],
             scratch_shapes=[part_acc],
             compiler_params=limit(8),
             cost_estimate=cost(width),
-        )(place, plan, gathered, held, early, first, current_block, previous_block, previous_coupling, diag)
+        )(place, plan, gathered, held, early, current_block, previous_block, previous_coupling, diag)
 
     basis_rows = (stored_count + 1) * width
     padded = (width, -(-basis_rows // LANES) * LANES)
@@ -413,7 +454,7 @@
 
     with jax.named_scope("gram"):
         gram = gram + swap(gram, "col", 1)
-        gram = total(total(gram, "col", 2), "row", 1)
+        gram = lax.psum(total(gram, "col", 2), "row")
         gram = jnp.concatenate(
             [gram[:, :width], gram[:, LANES // 2 : LANES // 2 + width]], axis=0
         )

time: 79.2 us -> 89.9 us (1.14)
  blocking collectives: 0 us -> 17.1 us
  Pallas kernels: 22.1 us -> 18.8 us
  waiting for transfers between devices: 25.8 us -> 22.6 us
    psum x0 -> x1, blocking collectives: none -> 17.1 us  [local(): gram = lax.psum(total(gram, 'col', 2), 'row')]
    ppermute x25 -> x19, waiting for transfers between devices: 25.8 us -> 14.9 us  [swap(): return lax.ppermute(value, axis, [(i, i ^ mask) for i in range(count)])]
    ppermute x25 -> x19, starting transfers between devices: 26.5 us -> 18.5 us  [swap(): return lax.ppermute(value, axis, [(i, i ^ mask) for i in range(count)])]
    ppermute x0 -> x4, starting transfers between devices: none -> 7.87 us  [the longest x1 3.07 us: local(): passing = lax.ppermute(first, 'row', [(0, 1), (3, 2)])]
    ppermute x0 -> x4, waiting for transfers between devices: none -> 7.72 us  [the longest x1 5.91 us: local(): lax.ppermute(joined, 'row', [(0, 1), (1, 3), (3, 2), (2, 0)])]
    pallas_call x5 -> x4, Pallas kernels: 18.2 us -> 15 us  [the longest x1 5.5 us: local(): pl.pallas_call(functools.partial(early_kernel, row_devs, col_devs, slab_t...]
  transfers between devices with their start and end apart: 25 -> 23, of which waited for: 18 -> 15; matrix products, arithmetic and copies ran while one was open for 1% -> 1% of each run, Pallas kernels for 18% -> 12%
where the time goes in v6:
time: 89.9 us; the launch traced here: 89.1 us
  starting transfers between devices  26.3 us (29%)
  waiting for transfers between devices  22.6 us (25%)
  Pallas kernels  18.8 us (21%)
  blocking collectives  17.1 us (19%)
  other arithmetic  1.8 us (2%)
  between operations  1.46 us (2%)
  local copies, waits for them, and re-layouts  0.93 us (1%)
    ppermute x19, starting transfers between devices, swap(): return lax.ppermute(value, axis, [(i, i ^ mask) for i in range(count)])  18.5 us
    psum x1, blocking collectives, local(): gram = lax.psum(total(gram, 'col', 2), 'row')  17.1 us
    ppermute x19, waiting for transfers between devices, swap(): return lax.ppermute(value, axis, [(i, i ^ mask) for i in range(count)])  14.9 us
    ppermute x1, waiting for transfers between devices, local(): lax.ppermute(joined, 'row', [(0, 1), (1, 3), (3, 2), (2, 0)])  5.91 us
    pallas_call x1, Pallas kernels, local(): pl.pallas_call(functools.partial(early_kernel, row_devs, col_devs, slab_t...  5.5 us
    pallas_call x1, Pallas kernels, local(): pl.pallas_call(functools.partial(first_late_kernel, row_devs - 1), out_sh...  4.26 us
    ppermute x1, starting transfers between devices, local(): passing = lax.ppermute(first, 'row', [(0, 1), (3, 2)])  3.07 us
    pallas_call x1, Pallas kernels, local(): pl.pallas_call(own_kernel, out_shape=slab, in_specs=smem(2) + vmem(7), ou...  2.8 us
  transfers between devices with their start and end apart: 23, of which 15 were waited for; matrix products, arithmetic and copies ran while one was open for 1% of the time, Pallas kernels for 12%

profile of v6, /device:TPU:0, one launch (start us, length us, event | category | flops | bytes accessed | tf_op | source)
XLA Modules:
  0.0 89.1 jit_solution(2208290268450282727)
XLA Ops:
  0.6 1.0 %convert_element_type.9.own_panel.refs_0_ = bf16[48,2048]{1,0:T(8,128)(2,1)S(1)} convert(f32[48,2048]{1,0:T(8,128)} %current.3) | non-fusion elementwise | flops 98304 | bytes 589824 | tf_op jit(solution)/shard_map/gather/convert_element_type | solution.py:338
  1.7 0.5 collective-permute-start
  2.2 2.6 %collective-permute-start.1 = (bf16[48,2048]{1,0:T(8,128)(2,1)S(1)}, bf16[48,2048]{1,0:T(8,128)(2,1)S(1)}, u32[]{:S(2)}, u32[]{:S(2)}) collective-permute-start(bf16[48,2048]{1,0:T(8,128)(2,1)S(1)} %convert_element_type.9.own_panel.refs_0_), channel_id=1, source_target_pairs={{0,2},{1,3},{2,0},{3,1},{4,6},{5,7},{6,4},{7,5},{8,10},{9,11},{10,... | collective-permute-start | bytes 589832 | tf_op jit(solution)/shard_map/gather/ppermute | solution.py:21
  4.7 1.5 %collective-permute-start.3 = (bf16[48,2048]{1,0:T(8,128)(2,1)S(1)}, bf16[48,2048]{1,0:T(8,128)(2,1)S(1)}, u32[]{:S(2)}, u32[]{:S(2)}) collective-permute-start(bf16[48,2048]{1,0:T(8,128)(2,1)S(1)} %convert_element_type.9.own_panel.refs_0_), channel_id=1, source_target_pairs={{0,4},{1,5},{2,6},{3,7},{4,0},{5,1},{6,2},{7,3},{8,12},{9,13},{10,... | collective-permute-start | bytes 589832 | tf_op jit(solution)/shard_map/gather/ppermute | solution.py:21
  6.3 0.0 collective-permute-start.5
  6.9 0.1 pad_add_fusion.place
  7.0 0.0 collective-permute-done.near_panel.refs_1_
  7.0 5.5 %early.1 = (s32[1,896]{1,0:T(1,128)S(1)}, bf16[512,128,128]{2,1,0:T(8,128)(2,1)S(1)}, f32[65,48,128]{2,1,0:T(8,128)S(1)}) custom-call(s32[2]{0:T(128)S(1)} %pad_add_fusion.place, s32[1]{0:T(128)S(6)} %copy.21.counts, s32[1,512]{1,0:T(1,128)} %bitcast.16, s32[1,512]{1,0:T(1,128)} %bitcast.17, bf16[512,128,128]{2,1,0:T(8,128)(2,1)} %tiles.1, ...), custom_call_target="tpu_custom_call" | custom-call | flops 805306368 | bytes 16777216 | tf_op jit(solution)/shard_map/early/pallas_call | solution.py:347
  12.5 0.0 collective-permute-done.1.value
  12.5 0.7 collective-permute-start.2
  13.3 2.6 %collective-permute-done.3.value = bf16[48,2048]{1,0:T(8,128)(2,1)S(1)} collective-permute-done((bf16[48,2048]{1,0:T(8,128)(2,1)S(1)}, bf16[48,2048]{1,0:T(8,128)(2,1)S(1)}, u32[]{:S(2)}, u32[]{:S(2)}) %collective-permute-start.3) | collective-permute-done | bytes 196640 | tf_op jit(solution)/shard_map/gather/ppermute | solution.py:21
  15.9 0.0 collective-permute-start.4
  15.9 0.0 collective-permute-done.5.value
  15.9 0.5 collective-permute-start.6
  16.4 0.0 collective-permute-done.2.refs_3_
  16.4 0.9 %collective-permute-done.4.refs_5_ = bf16[48,2048]{1,0:T(8,128)(2,1)S(1)} collective-permute-done((bf16[48,2048]{1,0:T(8,128)(2,1)S(1)}, bf16[48,2048]{1,0:T(8,128)(2,1)S(1)}, u32[]{:S(2)}, u32[]{:S(2)}) %collective-permute-start.4) | collective-permute-done | bytes 196640 | tf_op jit(solution)/shard_map/gather/ppermute | solution.py:21
  17.4 0.3 collective-permute-done.6.refs_7_
  17.6 4.3 %late.3 = (bf16[48,2048]{1,0:T(8,128)(2,1)S(1)}, bf16[9,48,2048]{2,1,0:T(8,128)(2,1)S(1)}) custom-call(s32[2]{0:T(128)S(1)} %pad_add_fusion.place, s32[1,896]{1,0:T(1,128)S(1)} %get-tuple-element.16.plan, bf16[48,2048]{1,0:T(8,128)(2,1)S(1)} %convert_element_type.9.own_panel.refs_0_, bf16[48,2048]{1,0:T(8,128)(2,1)S(1)} %collective-permute-done.near_panel.refs_1_, ...), custom_call_target="tpu_custom_call" | custom-call | flops 48 | bytes 1 | tf_op jit(solution)/shard_map/late/pallas_call | solution.py:384
  21.9 3.1 %collective-permute-start.9 = (bf16[48,2048]{1,0:T(8,128)(2,1)S(1)}, bf16[48,2048]{1,0:T(8,128)(2,1)S(1)}, u32[]{:S(2)}, u32[]{:S(2)}) collective-permute-start(bf16[48,2048]{1,0:T(8,128)(2,1)S(1)} %get-tuple-element.20), channel_id=1, source_target_pairs={{0,8},{24,16},{1,9},{25,17},{2,10},{26,18},{3,11},{27,19},{4,12},{... | collective-permute-start | bytes 589832 | tf_op jit(solution)/shard_map/late/ppermute | solution.py:406
  25.0 0.7 collective-permute-start.7
  25.7 0.0 copy-start.1
  25.7 0.0 copy-start.2
  25.7 0.0 copy-start.4
  25.7 0.0 copy-start.5
  25.7 2.4 %late.5 = (bf16[48,2048]{1,0:T(8,128)(2,1)S(1)}, f32[48,2048]{1,0:T(8,128)S(1)}) custom-call(s32[2]{0:T(128)S(1)} %pad_add_fusion.place, s32[1,896]{1,0:T(1,128)S(1)} %get-tuple-element.16.plan, bf16[9,48,2048]{2,1,0:T(8,128)(2,1)S(1)} %get-tuple-element.19.panel_buf, bf16[512,128,128]{2,1,0:T(8,128)(2,1)S(1)} %get-tuple-element.18.refs_8_.tiles, ...), custom_call_target="tpu_custom_call" | custom-call | flops 48 | bytes 1 | tf_op jit(solution)/shard_map/late/pallas_call | solution.py:396
  28.1 2.3 %collective-permute-start.8 = (bf16[48,2048]{1,0:T(8,128)(2,1)S(1)}, bf16[48,2048]{1,0:T(8,128)(2,1)S(1)}, u32[]{:S(2)}, u32[]{:S(2)}) collective-permute-start(bf16[48,2048]{1,0:T(8,128)(2,1)S(1)} %get-tuple-element.21), channel_id=1, source_target_pairs={{0,16},{24,8},{8,0},{16,24},{1,17},{25,9},{9,1},{17,25},{2,18},{26... | collective-permute-start | bytes 589832 | tf_op jit(solution)/shard_map/late/ppermute | solution.py:408
  30.5 0.0 collective-permute-done.9
  30.5 1.8 %collective-permute-start.10 = (bf16[48,2048]{1,0:T(8,128)(2,1)S(1)}, bf16[48,2048]{1,0:T(8,128)(2,1)S(1)}, u32[]{:S(2)}, u32[]{:S(2)}) collective-permute-start(bf16[48,2048]{1,0:T(8,128)(2,1)S(1)} %add_convert_fusion), channel_id=1, source_target_pairs={{0,8},{8,24},{24,16},{16,0},{1,9},{9,25},{25,17},{17,1},{2,10},{10... | collective-permute-start | bytes 589832 | tf_op jit(solution)/shard_map/late/ppermute | solution.py:410
  32.3 0.0 copy-start
  32.3 0.0 copy-start.3
  32.3 2.8 %late.4.base = f32[48,2048]{1,0:T(8,128)S(1)} custom-call(s32[2]{0:T(128)S(1)} %pad_add_fusion.place, s32[1,896]{1,0:T(1,128)S(1)} %get-tuple-element.16.plan, bf16[9,48,2048]{2,1,0:T(8,128)(2,1)S(1)} %get-tuple-element.19.panel_buf, bf16[512,128,128]{2,1,0:T(8,128)(2,1)S(1)} %get-tuple-element.18.refs_8_.tiles, ...), custom_call_target="tpu_custom_call" | custom-call | flops 48 | bytes 1 | tf_op jit(solution)/shard_map/late/pallas_call | solution.py:414
  35.2 0.0 collective-permute-done.7.refs_0_
  35.2 1.8 %collective-permute-done.8.refs_1_ = bf16[48,2048]{1,0:T(8,128)(2,1)S(1)} collective-permute-done((bf16[48,2048]{1,0:T(8,128)(2,1)S(1)}, bf16[48,2048]{1,0:T(8,128)(2,1)S(1)}, u32[]{:S(2)}, u32[]{:S(2)}) %collective-permute-start.8) | collective-permute-done | bytes 196640 | tf_op jit(solution)/shard_map/late/ppermute | solution.py:408
  37.0 5.9 %collective-permute-done.10.refs_2_ = bf16[48,2048]{1,0:T(8,128)(2,1)S(1)} collective-permute-done((bf16[48,2048]{1,0:T(8,128)(2,1)S(1)}, bf16[48,2048]{1,0:T(8,128)(2,1)S(1)}, u32[]{:S(2)}, u32[]{:S(2)}) %collective-permute-start.10) | collective-permute-done | bytes 196640 | tf_op jit(solution)/shard_map/late/ppermute | solution.py:410
  42.9 1.7 %coefficients.1 = (f32[48,2048]{1,0:T(8,128)S(1)}, f32[12,8,128]{2,1,0:T(8,128)S(1)}, f32[12,8,128]{2,1,0:T(8,128)S(1)}) custom-call(s32[2]{0:T(128)S(1)} %pad_add_fusion.place, f32[48,2048]{1,0:T(8,128)S(1)} %late.4.base, bf16[48,2048]{1,0:T(8,128)(2,1)S(1)} %collective-permute-done.7.refs_0_, bf16[48,2048]{1,0:T(8,128)(2,1)S(1)} %collective-permute-done.8.refs_1_, ...), custom_call_target="tpu_custom_call" | custom-call | tf_op jit(solution)/shard_map/coefficients/pallas_call | solution.py:428
  44.6 0.9 %collective-permute-start.11 = (f32[12,8,128]{2,1,0:T(8,128)S(1)}, f32[12,8,128]{2,1,0:T(8,128)S(1)}, u32[]{:S(2)}, u32[]{:S(2)}) collective-permute-start(f32[12,8,128]{2,1,0:T(8,128)S(1)} %get-tuple-element.24), channel_id=1, source_target_pairs={{0,1},{1,0},{2,3},{3,2},{4,5},{5,4},{6,7},{7,6},{8,9},{9,8},{10,11... | collective-permute-start | bytes 147464 | tf_op jit(solution)/shard_map/coefficients/ppermute | solution.py:21
  45.6 0.9 collective-permute-done.11
  46.5 1.5 %collective-permute-start.14 = (f32[12,8,128]{2,1,0:T(8,128)S(1)}, f32[12,8,128]{2,1,0:T(8,128)S(1)}, u32[]{:S(2)}, u32[]{:S(2)}) collective-permute-start(f32[12,8,128]{2,1,0:T(8,128)S(1)} %add.39), channel_id=1, source_target_pairs={{0,6},{1,7},{2,4},{3,5},{4,2},{5,3},{6,0},{7,1},{8,14},{9,15},{10,... | collective-permute-start | bytes 147464 | tf_op jit(solution)/shard_map/coefficients/ppermute | solution.py:21
  48.0 0.4 collective-permute-start.13
  48.4 1.6 %collective-permute-start.12 = (f32[12,8,128]{2,1,0:T(8,128)S(1)}, f32[12,8,128]{2,1,0:T(8,128)S(1)}, u32[]{:S(2)}, u32[]{:S(2)}) collective-permute-start(f32[12,8,128]{2,1,0:T(8,128)S(1)} %add.39), channel_id=1, source_target_pairs={{0,2},{1,3},{2,0},{3,1},{4,6},{5,7},{6,4},{7,5},{8,10},{9,11},{10,... | collective-permute-start | bytes 147464 | tf_op jit(solution)/shard_map/coefficients/ppermute | solution.py:21
  50.0 1.6 %collective-permute-done.14 = f32[12,8,128]{2,1,0:T(8,128)S(1)} collective-permute-done((f32[12,8,128]{2,1,0:T(8,128)S(1)}, f32[12,8,128]{2,1,0:T(8,128)S(1)}, u32[]{:S(2)}, u32[]{:S(2)}) %collective-permute-start.14) | collective-permute-done | bytes 49184 | tf_op jit(solution)/shard_map/coefficients/ppermute | solution.py:21
  51.5 0.9 %collective-permute-done.13 = f32[12,8,128]{2,1,0:T(8,128)S(1)} collective-permute-done((f32[12,8,128]{2,1,0:T(8,128)S(1)}, f32[12,8,128]{2,1,0:T(8,128)S(1)}, u32[]{:S(2)}, u32[]{:S(2)}) %collective-permute-start.13) | collective-permute-done | bytes 49184 | tf_op jit(solution)/shard_map/coefficients/ppermute | solution.py:21
  52.5 0.0 collective-permute-done.12
  52.5 1.8 %collective-permute-start.17 = (f32[12,8,128]{2,1,0:T(8,128)S(1)}, f32[12,8,128]{2,1,0:T(8,128)S(1)}, u32[]{:S(2)}, u32[]{:S(2)}) collective-permute-start(f32[12,8,128]{2,1,0:T(8,128)S(1)} %add_add_fusion.1), channel_id=1, source_target_pairs={{0,24},{8,16},{16,8},{24,0},{1,25},{9,17},{17,9},{25,1},{2,26},{10... | collective-permute-start | bytes 147464 | tf_op jit(solution)/shard_map/coefficients/ppermute | solution.py:21
  54.3 0.0 collective-permute-start.16
  54.3 2.7 %collective-permute-start.15 = (f32[12,8,128]{2,1,0:T(8,128)S(1)}, f32[12,8,128]{2,1,0:T(8,128)S(1)}, u32[]{:S(2)}, u32[]{:S(2)}) collective-permute-start(f32[12,8,128]{2,1,0:T(8,128)S(1)} %add_add_fusion.1), channel_id=1, source_target_pairs={{0,8},{8,0},{16,24},{24,16},{1,9},{9,1},{17,25},{25,17},{2,10},{10... | collective-permute-start | bytes 147464 | tf_op jit(solution)/shard_map/coefficients/ppermute | solution.py:21
  57.0 2.1 %collective-permute-done.17 = f32[12,8,128]{2,1,0:T(8,128)S(1)} collective-permute-done((f32[12,8,128]{2,1,0:T(8,128)S(1)}, f32[12,8,128]{2,1,0:T(8,128)S(1)}, u32[]{:S(2)}, u32[]{:S(2)}) %collective-permute-start.17) | collective-permute-done | bytes 49184 | tf_op jit(solution)/shard_map/coefficients/ppermute | solution.py:21
  59.1 0.9 collective-permute-done.16
  59.9 0.0 collective-permute-done.15
  60.0 0.1 collective-permute-start.18
  60.0 1.2 %collective-permute-done.18.other = f32[12,8,128]{2,1,0:T(8,128)S(1)} collective-permute-done((f32[12,8,128]{2,1,0:T(8,128)S(1)}, f32[12,8,128]{2,1,0:T(8,128)S(1)}, u32[]{:S(2)}, u32[]{:S(2)}) %collective-permute-start.18) | collective-permute-done | bytes 49184 | tf_op jit(solution)/shard_map/coefficients/ppermute | solution.py:21
  61.3 2.1 %residual.1 = (f32[48,2048]{1,0:T(8,128)}, f32[48,432]{1,0:T(8,128)S(1)}, f32[24,128]{1,0:T(8,128)S(1)}) custom-call(s32[2]{0:T(128)S(1)} %pad_add_fusion.place, f32[12,8,128]{2,1,0:T(8,128)S(1)} %add_add_fusion.mine, f32[12,8,128]{2,1,0:T(8,128)S(1)} %collective-permute-done.18.other, f32[48,2048]{1,0:T(8,128)S(1)} %get-tuple-element.25.recurrence, ...), custom_call_target="tpu_custom_call" | custom-call | tf_op jit(solution)/shard_map/residual/pallas_call | solution.py:441
  63.4 0.2 collective-permute-start.19
  63.5 1.0 %collective-permute-done.19 = f32[24,128]{1,0:T(8,128)S(1)} collective-permute-done((f32[24,128]{1,0:T(8,128)S(1)}, f32[24,128]{1,0:T(8,128)S(1)}, u32[]{:S(2)}, u32[]{:S(2)}) %collective-permute-start.19) | collective-permute-done | bytes 12320 | tf_op jit(solution)/shard_map/gram/ppermute | solution.py:21
  64.6 1.2 %collective-permute-start.22 = (f32[24,128]{1,0:T(8,128)S(1)}, f32[24,128]{1,0:T(8,128)S(1)}, u32[]{:S(2)}, u32[]{:S(2)}) collective-permute-start(f32[24,128]{1,0:T(8,128)S(1)} %add.46), channel_id=1, source_target_pairs={{0,6},{1,7},{2,4},{3,5},{4,2},{5,3},{6,0},{7,1},{8,14},{9,15},{10,... | collective-permute-start | bytes 36872 | tf_op jit(solution)/shard_map/gram/ppermute | solution.py:21
  65.8 1.8 %collective-permute-start.21 = (f32[24,128]{1,0:T(8,128)S(1)}, f32[24,128]{1,0:T(8,128)S(1)}, u32[]{:S(2)}, u32[]{:S(2)}) collective-permute-start(f32[24,128]{1,0:T(8,128)S(1)} %add.46), channel_id=1, source_target_pairs={{0,4},{1,5},{2,6},{3,7},{4,0},{5,1},{6,2},{7,3},{8,12},{9,13},{10,... | collective-permute-start | bytes 36872 | tf_op jit(solution)/shard_map/gram/ppermute | solution.py:21
  67.6 0.4 collective-permute-start.20
  68.0 0.8 copy.17
  68.9 0.3 collective-permute-done.22
  69.1 0.3 collective-permute-done.21
  69.5 1.8 %collective-permute-done.20 = f32[24,128]{1,0:T(8,128)S(1)} collective-permute-done((f32[24,128]{1,0:T(8,128)S(1)}, f32[24,128]{1,0:T(8,128)S(1)}, u32[]{:S(2)}, u32[]{:S(2)}) %collective-permute-start.20) | collective-permute-done | bytes 12320 | tf_op jit(solution)/shard_map/gram/ppermute | solution.py:21
  71.3 17.1 %psum.7 = f32[24,128]{1,0:T(8,128)S(1)} all-reduce(f32[24,128]{1,0:T(8,128)S(1)} %add_add_fusion.2), channel_id=1, replica_groups=mesh['row'=4,'col'=8] {'row'}, use_global_device_ids=true, to_apply=%region_0.0 | all-reduce | flops 3072 | bytes 24576 | tf_op jit(solution)/shard_map/gram/psum | solution.py:457
  88.4 0.1 fusion
  88.5 0.6 pad_maximum_fusion
  (15 shorter events, 0.1 us)
Async XLA Ops:
  1.7 5.4 %collective-permute-start = (bf16[48,2048]{1,0:T(8,128)(2,1)S(1)}, bf16[48,2048]{1,0:T(8,128)(2,1)S(1)}, u32[]{:S(2)}, u32[]{:S(2)}) collective-permute-start(bf16[48,2048]{1,0:T(8,128)(2,1)S(1)} %convert_element_type.9.own_panel.refs_0_), channel_id=1, source_target_pairs={{0,1},{1,0},{2,3},{3,2},{4,5},{5,4},{6,7},{7,6},{8,9},{9,8},{10,11... | collective-permute-start | bytes 589832 | tf_op jit(solution)/shard_map/gather/ppermute | solution.py:21
  2.2 10.3 %collective-permute-start.1 = (bf16[48,2048]{1,0:T(8,128)(2,1)S(1)}, bf16[48,2048]{1,0:T(8,128)(2,1)S(1)}, u32[]{:S(2)}, u32[]{:S(2)}) collective-permute-start(bf16[48,2048]{1,0:T(8,128)(2,1)S(1)} %convert_element_type.9.own_panel.refs_0_), channel_id=1, source_target_pairs={{0,2},{1,3},{2,0},{3,1},{4,6},{5,7},{6,4},{7,5},{8,10},{9,11},{10,... | collective-permute-start | bytes 589832 | tf_op jit(solution)/shard_map/gather/ppermute | solution.py:21
  4.7 11.2 %collective-permute-start.3 = (bf16[48,2048]{1,0:T(8,128)(2,1)S(1)}, bf16[48,2048]{1,0:T(8,128)(2,1)S(1)}, u32[]{:S(2)}, u32[]{:S(2)}) collective-permute-start(bf16[48,2048]{1,0:T(8,128)(2,1)S(1)} %convert_element_type.9.own_panel.refs_0_), channel_id=1, source_target_pairs={{0,4},{1,5},{2,6},{3,7},{4,0},{5,1},{6,2},{7,3},{8,12},{9,13},{10,... | collective-permute-start | bytes 589832 | tf_op jit(solution)/shard_map/gather/ppermute | solution.py:21
  6.3 9.7 %collective-permute-start.5 = (bf16[48,2048]{1,0:T(8,128)(2,1)S(1)}, bf16[48,2048]{1,0:T(8,128)(2,1)S(1)}, u32[]{:S(2)}, u32[]{:S(2)}) collective-permute-start(bf16[48,2048]{1,0:T(8,128)(2,1)S(1)} %convert_element_type.9.own_panel.refs_0_), channel_id=1, source_target_pairs={{0,6},{1,7},{2,4},{3,5},{4,2},{5,3},{6,0},{7,1},{8,14},{9,15},{10,... | collective-permute-start | bytes 589832 | tf_op jit(solution)/shard_map/gather/ppermute | solution.py:21
  12.5 3.9 %collective-permute-start.2 = (bf16[48,2048]{1,0:T(8,128)(2,1)S(1)}, bf16[48,2048]{1,0:T(8,128)(2,1)S(1)}, u32[]{:S(2)}, u32[]{:S(2)}) collective-permute-start(bf16[48,2048]{1,0:T(8,128)(2,1)S(1)} %gather.3.refs_2_), channel_id=1, source_target_pairs={{0,1},{1,0},{2,3},{3,2},{4,5},{5,4},{6,7},{7,6},{8,9},{9,8},{10,11... | collective-permute-start | bytes 589832 | tf_op jit(solution)/shard_map/gather/ppermute | solution.py:21
  15.9 1.4 %collective-permute-start.4 = (bf16[48,2048]{1,0:T(8,128)(2,1)S(1)}, bf16[48,2048]{1,0:T(8,128)(2,1)S(1)}, u32[]{:S(2)}, u32[]{:S(2)}) collective-permute-start(bf16[48,2048]{1,0:T(8,128)(2,1)S(1)} %gather.4.refs_4_), channel_id=1, source_target_pairs={{0,1},{1,0},{2,3},{3,2},{4,5},{5,4},{6,7},{7,6},{8,9},{9,8},{10,11... | collective-permute-start | bytes 589832 | tf_op jit(solution)/shard_map/gather/ppermute | solution.py:21
  15.9 1.7 %collective-permute-start.6 = (bf16[48,2048]{1,0:T(8,128)(2,1)S(1)}, bf16[48,2048]{1,0:T(8,128)(2,1)S(1)}, u32[]{:S(2)}, u32[]{:S(2)}) collective-permute-start(bf16[48,2048]{1,0:T(8,128)(2,1)S(1)} %gather.5.refs_6_), channel_id=1, source_target_pairs={{0,1},{1,0},{2,3},{3,2},{4,5},{5,4},{6,7},{7,6},{8,9},{9,8},{10,11... | collective-permute-start | bytes 589832 | tf_op jit(solution)/shard_map/gather/ppermute | solution.py:21
  21.9 8.6 %collective-permute-start.9 = (bf16[48,2048]{1,0:T(8,128)(2,1)S(1)}, bf16[48,2048]{1,0:T(8,128)(2,1)S(1)}, u32[]{:S(2)}, u32[]{:S(2)}) collective-permute-start(bf16[48,2048]{1,0:T(8,128)(2,1)S(1)} %get-tuple-element.20), channel_id=1, source_target_pairs={{0,8},{24,16},{1,9},{25,17},{2,10},{26,18},{3,11},{27,19},{4,12},{... | collective-permute-start | bytes 589832 | tf_op jit(solution)/shard_map/late/ppermute | solution.py:406
  25.0 10.2 %collective-permute-start.7 = (bf16[48,2048]{1,0:T(8,128)(2,1)S(1)}, bf16[48,2048]{1,0:T(8,128)(2,1)S(1)}, u32[]{:S(2)}, u32[]{:S(2)}) collective-permute-start(bf16[48,2048]{1,0:T(8,128)(2,1)S(1)} %get-tuple-element.20), channel_id=1, source_target_pairs={{8,16},{16,8},{9,17},{17,9},{10,18},{18,10},{11,19},{19,11},{12,20... | collective-permute-start | bytes 589832 | tf_op jit(solution)/shard_map/late/ppermute | solution.py:407
  25.7 6.6 %copy-start.1 = (f32[48,2048]{1,0:T(8,128)S(1)}, f32[48,2048]{1,0:T(8,128)}, u32[]{:S(2)}) copy-start(f32[48,2048]{1,0:T(8,128)} %current.3) | copy-start | bytes 1179652
  25.7 6.6 %copy-start.2 = (f32[48,2048]{1,0:T(8,128)S(1)}, f32[48,2048]{1,0:T(8,128)}, u32[]{:S(2)}) copy-start(f32[48,2048]{1,0:T(8,128)} %previous.1) | copy-start | bytes 1179652
  25.7 6.6 %copy-start.4 = (f32[48,48]{1,0:T(8,128)S(1)}, f32[48,48]{1,0:T(8,128)}, u32[]{:S(2)}) copy-start(f32[48,48]{1,0:T(8,128)} %coupling.1) | copy-start | bytes 27652
  25.7 6.6 %copy-start.5 = (f32[2048]{0:T(1024)S(1)}, f32[2048]{0:T(1024)}, u32[]{:S(2)}) copy-start(f32[2048]{0:T(1024)} %param.14) | copy-start | bytes 24580
  28.1 8.8 %collective-permute-start.8 = (bf16[48,2048]{1,0:T(8,128)(2,1)S(1)}, bf16[48,2048]{1,0:T(8,128)(2,1)S(1)}, u32[]{:S(2)}, u32[]{:S(2)}) collective-permute-start(bf16[48,2048]{1,0:T(8,128)(2,1)S(1)} %get-tuple-element.21), channel_id=1, source_target_pairs={{0,16},{24,8},{8,0},{16,24},{1,17},{25,9},{9,1},{17,25},{2,18},{26... | collective-permute-start | bytes 589832 | tf_op jit(solution)/shard_map/late/ppermute | solution.py:408
  30.5 12.4 %collective-permute-start.10 = (bf16[48,2048]{1,0:T(8,128)(2,1)S(1)}, bf16[48,2048]{1,0:T(8,128)(2,1)S(1)}, u32[]{:S(2)}, u32[]{:S(2)}) collective-permute-start(bf16[48,2048]{1,0:T(8,128)(2,1)S(1)} %add_convert_fusion), channel_id=1, source_target_pairs={{0,8},{8,24},{24,16},{16,0},{1,9},{9,25},{25,17},{17,1},{2,10},{10... | collective-permute-start | bytes 589832 | tf_op jit(solution)/shard_map/late/ppermute | solution.py:410
  32.3 10.6 %copy-start = (f32[8,48,2048]{2,1,0:T(8,128)S(1)}, f32[8,48,2048]{2,1,0:T(8,128)}, u32[]{:S(2)}) copy-start(f32[8,48,2048]{2,1,0:T(8,128)} %param.13) | copy-start | bytes 9437188
  32.3 10.6 %copy-start.3 = (f32[2048]{0:T(1024)S(1)}, f32[2048]{0:T(1024)}, u32[]{:S(2)}) copy-start(f32[2048]{0:T(1024)} %param.15) | copy-start | bytes 24580
  44.6 1.8 %collective-permute-start.11 = (f32[12,8,128]{2,1,0:T(8,128)S(1)}, f32[12,8,128]{2,1,0:T(8,128)S(1)}, u32[]{:S(2)}, u32[]{:S(2)}) collective-permute-start(f32[12,8,128]{2,1,0:T(8,128)S(1)} %get-tuple-element.24), channel_id=1, source_target_pairs={{0,1},{1,0},{2,3},{3,2},{4,5},{5,4},{6,7},{7,6},{8,9},{9,8},{10,11... | collective-permute-start | bytes 147464 | tf_op jit(solution)/shard_map/coefficients/ppermute | solution.py:21
  46.5 5.1 %collective-permute-start.14 = (f32[12,8,128]{2,1,0:T(8,128)S(1)}, f32[12,8,128]{2,1,0:T(8,128)S(1)}, u32[]{:S(2)}, u32[]{:S(2)}) collective-permute-start(f32[12,8,128]{2,1,0:T(8,128)S(1)} %add.39), channel_id=1, source_target_pairs={{0,6},{1,7},{2,4},{3,5},{4,2},{5,3},{6,0},{7,1},{8,14},{9,15},{10,... | collective-permute-start | bytes 147464 | tf_op jit(solution)/shard_map/coefficients/ppermute | solution.py:21
  48.0 4.5 %collective-permute-start.13 = (f32[12,8,128]{2,1,0:T(8,128)S(1)}, f32[12,8,128]{2,1,0:T(8,128)S(1)}, u32[]{:S(2)}, u32[]{:S(2)}) collective-permute-start(f32[12,8,128]{2,1,0:T(8,128)S(1)} %add.39), channel_id=1, source_target_pairs={{0,4},{1,5},{2,6},{3,7},{4,0},{5,1},{6,2},{7,3},{8,12},{9,13},{10,... | collective-permute-start | bytes 147464 | tf_op jit(solution)/shard_map/coefficients/ppermute | solution.py:21
  48.4 4.1 %collective-permute-start.12 = (f32[12,8,128]{2,1,0:T(8,128)S(1)}, f32[12,8,128]{2,1,0:T(8,128)S(1)}, u32[]{:S(2)}, u32[]{:S(2)}) collective-permute-start(f32[12,8,128]{2,1,0:T(8,128)S(1)} %add.39), channel_id=1, source_target_pairs={{0,2},{1,3},{2,0},{3,1},{4,6},{5,7},{6,4},{7,5},{8,10},{9,11},{10,... | collective-permute-start | bytes 147464 | tf_op jit(solution)/shard_map/coefficients/ppermute | solution.py:21
  52.5 6.6 %collective-permute-start.17 = (f32[12,8,128]{2,1,0:T(8,128)S(1)}, f32[12,8,128]{2,1,0:T(8,128)S(1)}, u32[]{:S(2)}, u32[]{:S(2)}) collective-permute-start(f32[12,8,128]{2,1,0:T(8,128)S(1)} %add_add_fusion.1), channel_id=1, source_target_pairs={{0,24},{8,16},{16,8},{24,0},{1,25},{9,17},{17,9},{25,1},{2,26},{10... | collective-permute-start | bytes 147464 | tf_op jit(solution)/shard_map/coefficients/ppermute | solution.py:21
  54.3 5.7 %collective-permute-start.16 = (f32[12,8,128]{2,1,0:T(8,128)S(1)}, f32[12,8,128]{2,1,0:T(8,128)S(1)}, u32[]{:S(2)}, u32[]{:S(2)}) collective-permute-start(f32[12,8,128]{2,1,0:T(8,128)S(1)} %add_add_fusion.1), channel_id=1, source_target_pairs={{0,16},{8,24},{16,0},{24,8},{1,17},{9,25},{17,1},{25,9},{2,18},{10... | collective-permute-start | bytes 147464 | tf_op jit(solution)/shard_map/coefficients/ppermute | solution.py:21
  54.3 5.7 %collective-permute-start.15 = (f32[12,8,128]{2,1,0:T(8,128)S(1)}, f32[12,8,128]{2,1,0:T(8,128)S(1)}, u32[]{:S(2)}, u32[]{:S(2)}) collective-permute-start(f32[12,8,128]{2,1,0:T(8,128)S(1)} %add_add_fusion.1), channel_id=1, source_target_pairs={{0,8},{8,0},{16,24},{24,16},{1,9},{9,1},{17,25},{25,17},{2,10},{10... | collective-permute-start | bytes 147464 | tf_op jit(solution)/shard_map/coefficients/ppermute | solution.py:21
  60.0 1.3 %collective-permute-start.18 = (f32[12,8,128]{2,1,0:T(8,128)S(1)}, f32[12,8,128]{2,1,0:T(8,128)S(1)}, u32[]{:S(2)}, u32[]{:S(2)}) collective-permute-start(f32[12,8,128]{2,1,0:T(8,128)S(1)} %add_add_fusion.mine), channel_id=1, source_target_pairs={{0,1},{1,0},{2,3},{3,2},{4,5},{5,4},{6,7},{7,6},{8,9},{9,8},{10,11... | collective-permute-start | bytes 147464 | tf_op jit(solution)/shard_map/coefficients/ppermute | solution.py:21
  63.4 1.2 %collective-permute-start.19 = (f32[24,128]{1,0:T(8,128)S(1)}, f32[24,128]{1,0:T(8,128)S(1)}, u32[]{:S(2)}, u32[]{:S(2)}) collective-permute-start(f32[24,128]{1,0:T(8,128)S(1)} %get-tuple-element.28), channel_id=1, source_target_pairs={{0,1},{1,0},{2,3},{3,2},{4,5},{5,4},{6,7},{7,6},{8,9},{9,8},{10,11... | collective-permute-start | bytes 36872 | tf_op jit(solution)/shard_map/gram/ppermute | solution.py:21
  64.6 4.6 %collective-permute-start.22 = (f32[24,128]{1,0:T(8,128)S(1)}, f32[24,128]{1,0:T(8,128)S(1)}, u32[]{:S(2)}, u32[]{:S(2)}) collective-permute-start(f32[24,128]{1,0:T(8,128)S(1)} %add.46), channel_id=1, source_target_pairs={{0,6},{1,7},{2,4},{3,5},{4,2},{5,3},{6,0},{7,1},{8,14},{9,15},{10,... | collective-permute-start | bytes 36872 | tf_op jit(solution)/shard_map/gram/ppermute | solution.py:21
  65.8 3.7 %collective-permute-start.21 = (f32[24,128]{1,0:T(8,128)S(1)}, f32[24,128]{1,0:T(8,128)S(1)}, u32[]{:S(2)}, u32[]{:S(2)}) collective-permute-start(f32[24,128]{1,0:T(8,128)S(1)} %add.46), channel_id=1, source_target_pairs={{0,4},{1,5},{2,6},{3,7},{4,0},{5,1},{6,2},{7,3},{8,12},{9,13},{10,... | collective-permute-start | bytes 36872 | tf_op jit(solution)/shard_map/gram/ppermute | solution.py:21
  67.6 3.7 %collective-permute-start.20 = (f32[24,128]{1,0:T(8,128)S(1)}, f32[24,128]{1,0:T(8,128)S(1)}, u32[]{:S(2)}, u32[]{:S(2)}) collective-permute-start(f32[24,128]{1,0:T(8,128)S(1)} %add.46), channel_id=1, source_target_pairs={{0,2},{1,3},{2,0},{3,1},{4,6},{5,7},{6,4},{7,5},{8,10},{9,11},{10,... | collective-permute-start | bytes 36872 | tf_op jit(solution)/shard_map/gram/ppermute | solution.py:21

commit v7 on v6

--- a/solution.py
+++ b/solution.py
@@ -10,7 +10,7 @@
 LANES = 128
 CHUNK = 32
 GROUP = 2
-UNROLL = 4
+UNROLL = 8
 TILE_BIT, SOURCE_BIT, ROW_BIT = 10, 15, 20
 NT = (((1,), (1,)), ((), ()))
 MIB = 1 << 20
@@ -190,18 +190,15 @@
 
 def late_kernel(masks, place, plan, panel_buf, tiles, early, *refs):
     acc = refs[-1]
-    if masks is None:
-        inner = (place[0] == 1) | (place[0] == 2)
-        masks = (jnp.where(inner, 1, 2), jnp.where(inner, 2, 1))
     for mask, send in zip(masks, refs):
         late_part(mask, place, plan, tiles, early, panel_buf, acc, ())
         put(send, acc)
 
 
-def own_kernel(place, plan, panel_buf, tiles, early, current, previous, coupling, diag, base, acc):
+def own_kernel(place, plan, panel_buf, tiles, early, received, current, previous, coupling, diag, base, acc):
     late_part(0, place, plan, tiles, early, panel_buf, acc, ())
     put(base, acc)
-    base[...] += diag[...] * current[...] - jnp.dot(
+    base[...] += received[...].astype(jnp.float32) + diag[...] * current[...] - jnp.dot(
         coupling[...],
         previous[...],
         precision=lax.Precision.HIGHEST,
@@ -390,36 +387,27 @@
             compiler_params=limit(8),
             cost_estimate=cost(width),
         )(place, plan, *panels, held, early)
-        relay = row_devs == 4
-        masks = None if relay else list(range(row_devs - 2, 0, -1))
-        parts = [part, slab] if relay else [part] * (row_devs - 2)
+        first = swap(first, "row", row_devs - 1)
+        masks = list(range(row_devs - 2, 0, -1))
         others = pl.pallas_call(
             functools.partial(late_kernel, masks),
-            out_shape=parts,
+            out_shape=[part] * len(masks),
             in_specs=smem(2) + vmem(3),
-            out_specs=vmem(len(parts)),
+            out_specs=vmem(len(masks)),
             scratch_shapes=[part_acc],
             compiler_params=limit(8),
             cost_estimate=cost(width),
         )(place, plan, gathered, held, early)
-        if relay:
-            passing = lax.ppermute(first, "row", [(0, 1), (3, 2)])
-            received = [lax.ppermute(first, "row", [(1, 2), (2, 1)])]
-            received.append(lax.ppermute(others[0], "row", [(0, 2), (3, 1), (1, 0), (2, 3)]))
-            joined = (others[1] + passing.astype(f32)).astype(bf16)
-            received.append(lax.ppermute(joined, "row", [(0, 1), (1, 3), (3, 2), (2, 0)]))
-        else:
-            received = [swap(first, "row", row_devs - 1)]
-            received += [swap(other, "row", m) for m, other in zip(masks, others)]
+        received = [swap(other, "row", m) for m, other in zip(masks, others)]
         base = pl.pallas_call(
             own_kernel,
             out_shape=slab,
-            in_specs=smem(2) + vmem(7),
+            in_specs=smem(2) + vmem(8),
             out_specs=vmem(1)[0],
             scratch_shapes=[part_acc],
             compiler_params=limit(8),
             cost_estimate=cost(width),
-        )(place, plan, gathered, held, early, current_block, previous_block, previous_coupling, diag)
+        )(place, plan, gathered, held, early, first, current_block, previous_block, previous_coupling, diag)
 
     basis_rows = (stored_count + 1) * width
     padded = (width, -(-basis_rows // LANES) * LANES)
@@ -454,7 +442,7 @@
 
     with jax.named_scope("gram"):
         gram = gram + swap(gram, "col", 1)
-        gram = lax.psum(total(gram, "col", 2), "row")
+        gram = total(total(gram, "col", 2), "row", 1)
         gram = jnp.concatenate(
             [gram[:, :width], gram[:, LANES // 2 : LANES // 2 + width]], axis=0
         )

time: 89.9 us -> 77.7 us (0.86); the launches traced: 89.1 us -> 77.8 us
  blocking collectives: 17.1 us -> 0 us
  waiting for transfers between devices: 22.6 us -> 28 us
    psum x1 -> x0, blocking collectives: 17.1 us -> none  [local(): gram = lax.psum(total(gram, 'col', 2), 'row')]
    ppermute x19 -> x25, waiting for transfers between devices: 14.9 us -> 28 us  [swap(): return lax.ppermute(value, axis, [(i, i ^ mask) for i in range(count)])]
    ppermute x4 -> x0, starting transfers between devices: 7.87 us -> none  [the longest x1 3.07 us: local(): passing = lax.ppermute(first, 'row', [(0, 1), (3, 2)])]
    ppermute x4 -> x0, waiting for transfers between devices: 7.72 us -> none  [the longest x1 5.91 us: local(): lax.ppermute(joined, 'row', [(0, 1), (1, 3), (3, 2), (2, 0)])]
    ppermute x19 -> x25, starting transfers between devices: 18.5 us -> 26.1 us  [swap(): return lax.ppermute(value, axis, [(i, i ^ mask) for i in range(count)])]
  transfers between devices with their start and end apart: 23 -> 25, of which waited for: 15 -> 19; matrix products, arithmetic and copies ran while one was open for 1% -> 1% of each run, Pallas kernels for 12% -> 14%
where the time goes in v7:
time: 77.7 us; the launch traced here: 77.8 us
  waiting for transfers between devices  28 us (36%)
  starting transfers between devices  26.1 us (34%)
  Pallas kernels  19.6 us (25%)
  other arithmetic  1.76 us (2%)
  between operations  1.44 us (2%)
  local copies, waits for them, and re-layouts  0.92 us (1%)
    ppermute x25, waiting for transfers between devices, swap(): return lax.ppermute(value, axis, [(i, i ^ mask) for i in range(count)])  28 us
    ppermute x25, starting transfers between devices, swap(): return lax.ppermute(value, axis, [(i, i ^ mask) for i in range(count)])  26.1 us
    pallas_call x1, Pallas kernels, local(): pl.pallas_call(functools.partial(early_kernel, row_devs, col_devs, slab_t...  5.98 us
    pallas_call x1, Pallas kernels, local(): pl.pallas_call(functools.partial(first_late_kernel, row_devs - 1), out_sh...  4.59 us
    pallas_call x1, Pallas kernels, local(): pl.pallas_call(functools.partial(late_kernel, masks), out_shape=[part] *...  2.84 us
    pallas_call x1, Pallas kernels, local(): pl.pallas_call(own_kernel, out_shape=slab, in_specs=smem(2) + vmem(8), ou...  2.31 us
    pallas_call x1, Pallas kernels, local(): pl.pallas_call(functools.partial(residual_kernel, cells), out_shape=[slab...  2.12 us
    pallas_call x1, Pallas kernels, local(): pl.pallas_call(functools.partial(coefficient_kernel, cells, len(received)...  1.73 us
  transfers between devices with their start and end apart: 25, of which 19 were waited for; matrix products, arithmetic and copies ran while one was open for 1% of the time, Pallas kernels for 14%

profile of v7, /device:TPU:0, one launch (start us, length us, event | category | flops | bytes accessed | tf_op | source)
XLA Modules:
  0.0 77.8 jit_solution(287039022439730494)
XLA Ops:
  0.6 1.0 %convert_element_type.3.own_panel.refs_0_ = bf16[48,2048]{1,0:T(8,128)(2,1)S(1)} convert(f32[48,2048]{1,0:T(8,128)} %current.3) | non-fusion elementwise | flops 98304 | bytes 589824 | tf_op jit(solution)/shard_map/gather/convert_element_type | solution.py:335
  1.7 0.5 collective-permute-start
  2.2 2.6 %collective-permute-start.1 = (bf16[48,2048]{1,0:T(8,128)(2,1)S(1)}, bf16[48,2048]{1,0:T(8,128)(2,1)S(1)}, u32[]{:S(2)}, u32[]{:S(2)}) collective-permute-start(bf16[48,2048]{1,0:T(8,128)(2,1)S(1)} %convert_element_type.3.own_panel.refs_0_), channel_id=1, source_target_pairs={{0,2},{1,3},{2,0},{3,1},{4,6},{5,7},{6,4},{7,5},{8,10},{9,11},{10,... | collective-permute-start | bytes 589832 | tf_op jit(solution)/shard_map/gather/ppermute | solution.py:21
  4.7 1.5 %collective-permute-start.3 = (bf16[48,2048]{1,0:T(8,128)(2,1)S(1)}, bf16[48,2048]{1,0:T(8,128)(2,1)S(1)}, u32[]{:S(2)}, u32[]{:S(2)}) collective-permute-start(bf16[48,2048]{1,0:T(8,128)(2,1)S(1)} %convert_element_type.3.own_panel.refs_0_), channel_id=1, source_target_pairs={{0,4},{1,5},{2,6},{3,7},{4,0},{5,1},{6,2},{7,3},{8,12},{9,13},{10,... | collective-permute-start | bytes 589832 | tf_op jit(solution)/shard_map/gather/ppermute | solution.py:21
  6.3 0.0 collective-permute-start.5
  6.9 0.1 pad_add_fusion.place
  7.0 0.0 collective-permute-done.near_panel.refs_1_
  7.0 6.0 %early.1 = (s32[1,896]{1,0:T(1,128)S(1)}, bf16[512,128,128]{2,1,0:T(8,128)(2,1)S(1)}, f32[65,48,128]{2,1,0:T(8,128)S(1)}) custom-call(s32[2]{0:T(128)S(1)} %pad_add_fusion.place, s32[1]{0:T(128)S(6)} %copy.21.counts, s32[1,512]{1,0:T(1,128)} %bitcast.16, s32[1,512]{1,0:T(1,128)} %bitcast.17, bf16[512,128,128]{2,1,0:T(8,128)(2,1)} %tiles.1, ...), custom_call_target="tpu_custom_call" | custom-call | flops 805306368 | bytes 16777216 | tf_op jit(solution)/shard_map/early/pallas_call | solution.py:344
  13.0 0.0 collective-permute-done.1.value
  13.0 0.1 collective-permute-start.2
  13.1 2.8 %collective-permute-done.3.value = bf16[48,2048]{1,0:T(8,128)(2,1)S(1)} collective-permute-done((bf16[48,2048]{1,0:T(8,128)(2,1)S(1)}, bf16[48,2048]{1,0:T(8,128)(2,1)S(1)}, u32[]{:S(2)}, u32[]{:S(2)}) %collective-permute-start.3) | collective-permute-done | bytes 196640 | tf_op jit(solution)/shard_map/gather/ppermute | solution.py:21
  15.9 0.0 collective-permute-start.4
  15.9 0.0 collective-permute-done.5.value
  15.9 0.5 collective-permute-start.6
  16.4 0.0 collective-permute-done.2.refs_3_
  16.4 0.9 %collective-permute-done.4.refs_5_ = bf16[48,2048]{1,0:T(8,128)(2,1)S(1)} collective-permute-done((bf16[48,2048]{1,0:T(8,128)(2,1)S(1)}, bf16[48,2048]{1,0:T(8,128)(2,1)S(1)}, u32[]{:S(2)}, u32[]{:S(2)}) %collective-permute-start.4) | collective-permute-done | bytes 196640 | tf_op jit(solution)/shard_map/gather/ppermute | solution.py:21
  17.4 0.3 collective-permute-done.6.refs_7_
  17.6 4.6 %late.3 = (bf16[48,2048]{1,0:T(8,128)(2,1)S(1)}, bf16[9,48,2048]{2,1,0:T(8,128)(2,1)S(1)}) custom-call(s32[2]{0:T(128)S(1)} %pad_add_fusion.place, s32[1,896]{1,0:T(1,128)S(1)} %get-tuple-element.16.plan, bf16[48,2048]{1,0:T(8,128)(2,1)S(1)} %convert_element_type.3.own_panel.refs_0_, bf16[48,2048]{1,0:T(8,128)(2,1)S(1)} %collective-permute-done.near_panel.refs_1_, ...), custom_call_target="tpu_custom_call" | custom-call | flops 48 | bytes 1 | tf_op jit(solution)/shard_map/late/pallas_call | solution.py:381
  22.2 2.8 %collective-permute-start.7 = (bf16[48,2048]{1,0:T(8,128)(2,1)S(1)}, bf16[48,2048]{1,0:T(8,128)(2,1)S(1)}, u32[]{:S(2)}, u32[]{:S(2)}) collective-permute-start(bf16[48,2048]{1,0:T(8,128)(2,1)S(1)} %get-tuple-element.20), channel_id=1, source_target_pairs={{0,24},{8,16},{16,8},{24,0},{1,25},{9,17},{17,9},{25,1},{2,26},{10... | collective-permute-start | bytes 589832 | tf_op jit(solution)/shard_map/late/ppermute | solution.py:21
  25.0 2.8 %late.5 = (bf16[48,2048]{1,0:T(8,128)(2,1)S(1)}, bf16[48,2048]{1,0:T(8,128)(2,1)S(1)}) custom-call(s32[2]{0:T(128)S(1)} %pad_add_fusion.place, s32[1,896]{1,0:T(1,128)S(1)} %get-tuple-element.16.plan, bf16[9,48,2048]{2,1,0:T(8,128)(2,1)S(1)} %get-tuple-element.19.panel_buf, bf16[512,128,128]{2,1,0:T(8,128)(2,1)S(1)} %get-tuple-element.18.refs_8_.tiles, ...), custom_call_target="tpu_custom_call" | custom-call | flops 48 | bytes 1 | tf_op jit(solution)/shard_map/late/pallas_call | solution.py:392
  27.9 0.1 collective-permute-start.8
  28.0 1.4 %collective-permute-start.9 = (bf16[48,2048]{1,0:T(8,128)(2,1)S(1)}, bf16[48,2048]{1,0:T(8,128)(2,1)S(1)}, u32[]{:S(2)}, u32[]{:S(2)}) collective-permute-start(bf16[48,2048]{1,0:T(8,128)(2,1)S(1)} %get-tuple-element.22), channel_id=1, source_target_pairs={{0,8},{8,0},{16,24},{24,16},{1,9},{9,1},{17,25},{25,17},{2,10},{10... | collective-permute-start | bytes 589832 | tf_op jit(solution)/shard_map/late/ppermute | solution.py:21
  29.3 1.1 %collective-permute-done.7.received = bf16[48,2048]{1,0:T(8,128)(2,1)S(1)} collective-permute-done((bf16[48,2048]{1,0:T(8,128)(2,1)S(1)}, bf16[48,2048]{1,0:T(8,128)(2,1)S(1)}, u32[]{:S(2)}, u32[]{:S(2)}) %collective-permute-start.7) | collective-permute-done | bytes 196640 | tf_op jit(solution)/shard_map/late/ppermute | solution.py:21
  30.5 0.0 copy-done.5
  30.5 0.0 copy-start
  30.5 0.0 copy-start.3
  30.5 2.3 %late.4.base = f32[48,2048]{1,0:T(8,128)S(1)} custom-call(s32[2]{0:T(128)S(1)} %pad_add_fusion.place, s32[1,896]{1,0:T(1,128)S(1)} %get-tuple-element.16.plan, bf16[9,48,2048]{2,1,0:T(8,128)(2,1)S(1)} %get-tuple-element.19.panel_buf, bf16[512,128,128]{2,1,0:T(8,128)(2,1)S(1)} %get-tuple-element.18.refs_8_.tiles, ...), custom_call_target="tpu_custom_call" | custom-call | flops 48 | bytes 1 | tf_op jit(solution)/shard_map/late/pallas_call | solution.py:402
  32.8 9.4 %collective-permute-done.8.refs_0_ = bf16[48,2048]{1,0:T(8,128)(2,1)S(1)} collective-permute-done((bf16[48,2048]{1,0:T(8,128)(2,1)S(1)}, bf16[48,2048]{1,0:T(8,128)(2,1)S(1)}, u32[]{:S(2)}, u32[]{:S(2)}) %collective-permute-start.8) | collective-permute-done | bytes 196640 | tf_op jit(solution)/shard_map/late/ppermute | solution.py:21
  42.2 0.0 collective-permute-done.9.refs_1_
  42.2 1.7 %coefficients.1 = (f32[48,2048]{1,0:T(8,128)S(1)}, f32[12,8,128]{2,1,0:T(8,128)S(1)}, f32[12,8,128]{2,1,0:T(8,128)S(1)}) custom-call(s32[2]{0:T(128)S(1)} %pad_add_fusion.place, f32[48,2048]{1,0:T(8,128)S(1)} %late.4.base, bf16[48,2048]{1,0:T(8,128)(2,1)S(1)} %collective-permute-done.8.refs_0_, bf16[48,2048]{1,0:T(8,128)(2,1)S(1)} %collective-permute-done.9.refs_1_, ...), custom_call_target="tpu_custom_call" | custom-call | tf_op jit(solution)/shard_map/coefficients/pallas_call | solution.py:416
  44.0 0.1 collective-permute-start.10
  44.1 1.2 %collective-permute-done.10 = f32[12,8,128]{2,1,0:T(8,128)S(1)} collective-permute-done((f32[12,8,128]{2,1,0:T(8,128)S(1)}, f32[12,8,128]{2,1,0:T(8,128)S(1)}, u32[]{:S(2)}, u32[]{:S(2)}) %collective-permute-start.10) | collective-permute-done | bytes 49184 | tf_op jit(solution)/shard_map/coefficients/ppermute | solution.py:21
  45.3 1.2 %collective-permute-start.13 = (f32[12,8,128]{2,1,0:T(8,128)S(1)}, f32[12,8,128]{2,1,0:T(8,128)S(1)}, u32[]{:S(2)}, u32[]{:S(2)}) collective-permute-start(f32[12,8,128]{2,1,0:T(8,128)S(1)} %add.42), channel_id=1, source_target_pairs={{0,6},{1,7},{2,4},{3,5},{4,2},{5,3},{6,0},{7,1},{8,14},{9,15},{10,... | collective-permute-start | bytes 147464 | tf_op jit(solution)/shard_map/coefficients/ppermute | solution.py:21
  46.5 1.4 %collective-permute-start.12 = (f32[12,8,128]{2,1,0:T(8,128)S(1)}, f32[12,8,128]{2,1,0:T(8,128)S(1)}, u32[]{:S(2)}, u32[]{:S(2)}) collective-permute-start(f32[12,8,128]{2,1,0:T(8,128)S(1)} %add.42), channel_id=1, source_target_pairs={{0,4},{1,5},{2,6},{3,7},{4,0},{5,1},{6,2},{7,3},{8,12},{9,13},{10,... | collective-permute-start | bytes 147464 | tf_op jit(solution)/shard_map/coefficients/ppermute | solution.py:21
  48.0 1.4 %collective-permute-start.11 = (f32[12,8,128]{2,1,0:T(8,128)S(1)}, f32[12,8,128]{2,1,0:T(8,128)S(1)}, u32[]{:S(2)}, u32[]{:S(2)}) collective-permute-start(f32[12,8,128]{2,1,0:T(8,128)S(1)} %add.42), channel_id=1, source_target_pairs={{0,2},{1,3},{2,0},{3,1},{4,6},{5,7},{6,4},{7,5},{8,10},{9,11},{10,... | collective-permute-start | bytes 147464 | tf_op jit(solution)/shard_map/coefficients/ppermute | solution.py:21
  49.4 1.0 %collective-permute-done.13 = f32[12,8,128]{2,1,0:T(8,128)S(1)} collective-permute-done((f32[12,8,128]{2,1,0:T(8,128)S(1)}, f32[12,8,128]{2,1,0:T(8,128)S(1)}, u32[]{:S(2)}, u32[]{:S(2)}) %collective-permute-start.13) | collective-permute-done | bytes 49184 | tf_op jit(solution)/shard_map/coefficients/ppermute | solution.py:21
  50.4 0.7 collective-permute-done.12
  51.0 1.1 %collective-permute-done.11 = f32[12,8,128]{2,1,0:T(8,128)S(1)} collective-permute-done((f32[12,8,128]{2,1,0:T(8,128)S(1)}, f32[12,8,128]{2,1,0:T(8,128)S(1)}, u32[]{:S(2)}, u32[]{:S(2)}) %collective-permute-start.11) | collective-permute-done | bytes 49184 | tf_op jit(solution)/shard_map/coefficients/ppermute | solution.py:21
  52.2 1.7 %collective-permute-start.16 = (f32[12,8,128]{2,1,0:T(8,128)S(1)}, f32[12,8,128]{2,1,0:T(8,128)S(1)}, u32[]{:S(2)}, u32[]{:S(2)}) collective-permute-start(f32[12,8,128]{2,1,0:T(8,128)S(1)} %add_add_fusion.1), channel_id=1, source_target_pairs={{0,24},{8,16},{16,8},{24,0},{1,25},{9,17},{17,9},{25,1},{2,26},{10... | collective-permute-start | bytes 147464 | tf_op jit(solution)/shard_map/coefficients/ppermute | solution.py:21
  53.9 0.0 collective-permute-start.15
  53.9 2.7 %collective-permute-start.14 = (f32[12,8,128]{2,1,0:T(8,128)S(1)}, f32[12,8,128]{2,1,0:T(8,128)S(1)}, u32[]{:S(2)}, u32[]{:S(2)}) collective-permute-start(f32[12,8,128]{2,1,0:T(8,128)S(1)} %add_add_fusion.1), channel_id=1, source_target_pairs={{0,8},{8,0},{16,24},{24,16},{1,9},{9,1},{17,25},{25,17},{2,10},{10... | collective-permute-start | bytes 147464 | tf_op jit(solution)/shard_map/coefficients/ppermute | solution.py:21
  56.6 1.7 %collective-permute-done.16 = f32[12,8,128]{2,1,0:T(8,128)S(1)} collective-permute-done((f32[12,8,128]{2,1,0:T(8,128)S(1)}, f32[12,8,128]{2,1,0:T(8,128)S(1)}, u32[]{:S(2)}, u32[]{:S(2)}) %collective-permute-start.16) | collective-permute-done | bytes 49184 | tf_op jit(solution)/shard_map/coefficients/ppermute | solution.py:21
  58.3 1.1 %collective-permute-done.15 = f32[12,8,128]{2,1,0:T(8,128)S(1)} collective-permute-done((f32[12,8,128]{2,1,0:T(8,128)S(1)}, f32[12,8,128]{2,1,0:T(8,128)S(1)}, u32[]{:S(2)}, u32[]{:S(2)}) %collective-permute-start.15) | collective-permute-done | bytes 49184 | tf_op jit(solution)/shard_map/coefficients/ppermute | solution.py:21
  59.4 0.0 collective-permute-done.14
  59.4 0.1 collective-permute-start.17
  59.5 1.2 %collective-permute-done.17.other = f32[12,8,128]{2,1,0:T(8,128)S(1)} collective-permute-done((f32[12,8,128]{2,1,0:T(8,128)S(1)}, f32[12,8,128]{2,1,0:T(8,128)S(1)}, u32[]{:S(2)}, u32[]{:S(2)}) %collective-permute-start.17) | collective-permute-done | bytes 49184 | tf_op jit(solution)/shard_map/coefficients/ppermute | solution.py:21
  60.7 2.1 %residual.1 = (f32[48,2048]{1,0:T(8,128)}, f32[48,432]{1,0:T(8,128)S(1)}, f32[24,128]{1,0:T(8,128)S(1)}) custom-call(s32[2]{0:T(128)S(1)} %pad_add_fusion.place, f32[12,8,128]{2,1,0:T(8,128)S(1)} %add_add_fusion.mine, f32[12,8,128]{2,1,0:T(8,128)S(1)} %collective-permute-done.17.other, f32[48,2048]{1,0:T(8,128)S(1)} %get-tuple-element.25.recurrence, ...), custom_call_target="tpu_custom_call" | custom-call | tf_op jit(solution)/shard_map/residual/pallas_call | solution.py:429
  62.8 0.2 collective-permute-start.18
  63.0 1.0 %collective-permute-done.18 = f32[24,128]{1,0:T(8,128)S(1)} collective-permute-done((f32[24,128]{1,0:T(8,128)S(1)}, f32[24,128]{1,0:T(8,128)S(1)}, u32[]{:S(2)}, u32[]{:S(2)}) %collective-permute-start.18) | collective-permute-done | bytes 12320 | tf_op jit(solution)/shard_map/gram/ppermute | solution.py:21
  64.0 2.6 %collective-permute-start.21 = (f32[24,128]{1,0:T(8,128)S(1)}, f32[24,128]{1,0:T(8,128)S(1)}, u32[]{:S(2)}, u32[]{:S(2)}) collective-permute-start(f32[24,128]{1,0:T(8,128)S(1)} %add.49), channel_id=1, source_target_pairs={{0,6},{1,7},{2,4},{3,5},{4,2},{5,3},{6,0},{7,1},{8,14},{9,15},{10,... | collective-permute-start | bytes 36872 | tf_op jit(solution)/shard_map/gram/ppermute | solution.py:21
  66.6 0.1 collective-permute-start.20
  66.7 0.8 %collective-permute-start.19 = (f32[24,128]{1,0:T(8,128)S(1)}, f32[24,128]{1,0:T(8,128)S(1)}, u32[]{:S(2)}, u32[]{:S(2)}) collective-permute-start(f32[24,128]{1,0:T(8,128)S(1)} %add.49), channel_id=1, source_target_pairs={{0,2},{1,3},{2,0},{3,1},{4,6},{5,7},{6,4},{7,5},{8,10},{9,11},{10,... | collective-permute-start | bytes 36872 | tf_op jit(solution)/shard_map/gram/ppermute | solution.py:21
  67.5 1.1 %collective-permute-done.21 = f32[24,128]{1,0:T(8,128)S(1)} collective-permute-done((f32[24,128]{1,0:T(8,128)S(1)}, f32[24,128]{1,0:T(8,128)S(1)}, u32[]{:S(2)}, u32[]{:S(2)}) %collective-permute-start.21) | collective-permute-done | bytes 12320 | tf_op jit(solution)/shard_map/gram/ppermute | solution.py:21
  68.6 1.7 %collective-permute-done.20 = f32[24,128]{1,0:T(8,128)S(1)} collective-permute-done((f32[24,128]{1,0:T(8,128)S(1)}, f32[24,128]{1,0:T(8,128)S(1)}, u32[]{:S(2)}, u32[]{:S(2)}) %collective-permute-start.20) | collective-permute-done | bytes 12320 | tf_op jit(solution)/shard_map/gram/ppermute | solution.py:21
  70.3 0.1 collective-permute-done.19
  70.4 2.0 %collective-permute-start.24 = (f32[24,128]{1,0:T(8,128)S(1)}, f32[24,128]{1,0:T(8,128)S(1)}, u32[]{:S(2)}, u32[]{:S(2)}) collective-permute-start(f32[24,128]{1,0:T(8,128)S(1)} %add_add_fusion.3), channel_id=1, source_target_pairs={{0,24},{8,16},{16,8},{24,0},{1,25},{9,17},{17,9},{25,1},{2,26},{10... | collective-permute-start | bytes 36872 | tf_op jit(solution)/shard_map/gram/ppermute | solution.py:21
  72.4 0.9 %collective-permute-start.23 = (f32[24,128]{1,0:T(8,128)S(1)}, f32[24,128]{1,0:T(8,128)S(1)}, u32[]{:S(2)}, u32[]{:S(2)}) collective-permute-start(f32[24,128]{1,0:T(8,128)S(1)} %add_add_fusion.3), channel_id=1, source_target_pairs={{0,16},{8,24},{16,0},{24,8},{1,17},{9,25},{17,1},{25,9},{2,18},{10... | collective-permute-start | bytes 36872 | tf_op jit(solution)/shard_map/gram/ppermute | solution.py:21
  73.3 1.5 %collective-permute-start.22 = (f32[24,128]{1,0:T(8,128)S(1)}, f32[24,128]{1,0:T(8,128)S(1)}, u32[]{:S(2)}, u32[]{:S(2)}) collective-permute-start(f32[24,128]{1,0:T(8,128)S(1)} %add_add_fusion.3), channel_id=1, source_target_pairs={{0,8},{8,0},{16,24},{24,16},{1,9},{9,1},{17,25},{25,17},{2,10},{10... | collective-permute-start | bytes 36872 | tf_op jit(solution)/shard_map/gram/ppermute | solution.py:21
  74.8 0.8 %copy.17 = f32[432,48]{1,0:T(8,128)} copy(f32[432,48]{0,1:T(8,128)S(1)} %bitcast.11) | data formatting | bytes 165888 | tf_op jit(solution)/shard_map/residual/transpose | solution.py:441
  75.6 0.3 collective-permute-done.24
  75.9 1.1 %collective-permute-done.23 = f32[24,128]{1,0:T(8,128)S(1)} collective-permute-done((f32[24,128]{1,0:T(8,128)S(1)}, f32[24,128]{1,0:T(8,128)S(1)}, u32[]{:S(2)}, u32[]{:S(2)}) %collective-permute-start.23) | collective-permute-done | bytes 12320 | tf_op jit(solution)/shard_map/gram/ppermute | solution.py:21
  77.0 0.1 collective-permute-done.22
  77.1 0.1 fusion
  77.2 0.6 pad_maximum_fusion
  (18 shorter events, 0.1 us)
Async XLA Ops:
  1.7 5.4 %collective-permute-start = (bf16[48,2048]{1,0:T(8,128)(2,1)S(1)}, bf16[48,2048]{1,0:T(8,128)(2,1)S(1)}, u32[]{:S(2)}, u32[]{:S(2)}) collective-permute-start(bf16[48,2048]{1,0:T(8,128)(2,1)S(1)} %convert_element_type.3.own_panel.refs_0_), channel_id=1, source_target_pairs={{0,1},{1,0},{2,3},{3,2},{4,5},{5,4},{6,7},{7,6},{8,9},{9,8},{10,11... | collective-permute-start | bytes 589832 | tf_op jit(solution)/shard_map/gather/ppermute | solution.py:21
  2.2 10.8 %collective-permute-start.1 = (bf16[48,2048]{1,0:T(8,128)(2,1)S(1)}, bf16[48,2048]{1,0:T(8,128)(2,1)S(1)}, u32[]{:S(2)}, u32[]{:S(2)}) collective-permute-start(bf16[48,2048]{1,0:T(8,128)(2,1)S(1)} %convert_element_type.3.own_panel.refs_0_), channel_id=1, source_target_pairs={{0,2},{1,3},{2,0},{3,1},{4,6},{5,7},{6,4},{7,5},{8,10},{9,11},{10,... | collective-permute-start | bytes 589832 | tf_op jit(solution)/shard_map/gather/ppermute | solution.py:21
  4.7 11.2 %collective-permute-start.3 = (bf16[48,2048]{1,0:T(8,128)(2,1)S(1)}, bf16[48,2048]{1,0:T(8,128)(2,1)S(1)}, u32[]{:S(2)}, u32[]{:S(2)}) collective-permute-start(bf16[48,2048]{1,0:T(8,128)(2,1)S(1)} %convert_element_type.3.own_panel.refs_0_), channel_id=1, source_target_pairs={{0,4},{1,5},{2,6},{3,7},{4,0},{5,1},{6,2},{7,3},{8,12},{9,13},{10,... | collective-permute-start | bytes 589832 | tf_op jit(solution)/shard_map/gather/ppermute | solution.py:21
  6.3 9.7 %collective-permute-start.5 = (bf16[48,2048]{1,0:T(8,128)(2,1)S(1)}, bf16[48,2048]{1,0:T(8,128)(2,1)S(1)}, u32[]{:S(2)}, u32[]{:S(2)}) collective-permute-start(bf16[48,2048]{1,0:T(8,128)(2,1)S(1)} %convert_element_type.3.own_panel.refs_0_), channel_id=1, source_target_pairs={{0,6},{1,7},{2,4},{3,5},{4,2},{5,3},{6,0},{7,1},{8,14},{9,15},{10,... | collective-permute-start | bytes 589832 | tf_op jit(solution)/shard_map/gather/ppermute | solution.py:21
  13.0 3.4 %collective-permute-start.2 = (bf16[48,2048]{1,0:T(8,128)(2,1)S(1)}, bf16[48,2048]{1,0:T(8,128)(2,1)S(1)}, u32[]{:S(2)}, u32[]{:S(2)}) collective-permute-start(bf16[48,2048]{1,0:T(8,128)(2,1)S(1)} %gather.3.refs_2_), channel_id=1, source_target_pairs={{0,1},{1,0},{2,3},{3,2},{4,5},{5,4},{6,7},{7,6},{8,9},{9,8},{10,11... | collective-permute-start | bytes 589832 | tf_op jit(solution)/shard_map/gather/ppermute | solution.py:21
  15.9 1.4 %collective-permute-start.4 = (bf16[48,2048]{1,0:T(8,128)(2,1)S(1)}, bf16[48,2048]{1,0:T(8,128)(2,1)S(1)}, u32[]{:S(2)}, u32[]{:S(2)}) collective-permute-start(bf16[48,2048]{1,0:T(8,128)(2,1)S(1)} %gather.4.refs_4_), channel_id=1, source_target_pairs={{0,1},{1,0},{2,3},{3,2},{4,5},{5,4},{6,7},{7,6},{8,9},{9,8},{10,11... | collective-permute-start | bytes 589832 | tf_op jit(solution)/shard_map/gather/ppermute | solution.py:21
  15.9 1.7 %collective-permute-start.6 = (bf16[48,2048]{1,0:T(8,128)(2,1)S(1)}, bf16[48,2048]{1,0:T(8,128)(2,1)S(1)}, u32[]{:S(2)}, u32[]{:S(2)}) collective-permute-start(bf16[48,2048]{1,0:T(8,128)(2,1)S(1)} %gather.5.refs_6_), channel_id=1, source_target_pairs={{0,1},{1,0},{2,3},{3,2},{4,5},{5,4},{6,7},{7,6},{8,9},{9,8},{10,11... | collective-permute-start | bytes 589832 | tf_op jit(solution)/shard_map/gather/ppermute | solution.py:21
  22.2 8.2 %collective-permute-start.7 = (bf16[48,2048]{1,0:T(8,128)(2,1)S(1)}, bf16[48,2048]{1,0:T(8,128)(2,1)S(1)}, u32[]{:S(2)}, u32[]{:S(2)}) collective-permute-start(bf16[48,2048]{1,0:T(8,128)(2,1)S(1)} %get-tuple-element.20), channel_id=1, source_target_pairs={{0,24},{8,16},{16,8},{24,0},{1,25},{9,17},{17,9},{25,1},{2,26},{10... | collective-permute-start | bytes 589832 | tf_op jit(solution)/shard_map/late/ppermute | solution.py:21
  25.0 5.5 %copy-start.1 = (f32[48,2048]{1,0:T(8,128)S(1)}, f32[48,2048]{1,0:T(8,128)}, u32[]{:S(2)}) copy-start(f32[48,2048]{1,0:T(8,128)} %current.3) | copy-start | bytes 1179652
  25.0 5.5 %copy-start.2 = (f32[48,2048]{1,0:T(8,128)S(1)}, f32[48,2048]{1,0:T(8,128)}, u32[]{:S(2)}) copy-start(f32[48,2048]{1,0:T(8,128)} %previous.1) | copy-start | bytes 1179652
  25.0 5.5 %copy-start.4 = (f32[48,48]{1,0:T(8,128)S(1)}, f32[48,48]{1,0:T(8,128)}, u32[]{:S(2)}) copy-start(f32[48,48]{1,0:T(8,128)} %coupling.1) | copy-start | bytes 27652
  25.0 5.5 %copy-start.5 = (f32[2048]{0:T(1024)S(1)}, f32[2048]{0:T(1024)}, u32[]{:S(2)}) copy-start(f32[2048]{0:T(1024)} %param.14) | copy-start | bytes 24580
  27.9 14.4 %collective-permute-start.8 = (bf16[48,2048]{1,0:T(8,128)(2,1)S(1)}, bf16[48,2048]{1,0:T(8,128)(2,1)S(1)}, u32[]{:S(2)}, u32[]{:S(2)}) collective-permute-start(bf16[48,2048]{1,0:T(8,128)(2,1)S(1)} %get-tuple-element.21), channel_id=1, source_target_pairs={{0,16},{8,24},{16,0},{24,8},{1,17},{9,25},{17,1},{25,9},{2,18},{10... | collective-permute-start | bytes 589832 | tf_op jit(solution)/shard_map/late/ppermute | solution.py:21
  28.0 14.3 %collective-permute-start.9 = (bf16[48,2048]{1,0:T(8,128)(2,1)S(1)}, bf16[48,2048]{1,0:T(8,128)(2,1)S(1)}, u32[]{:S(2)}, u32[]{:S(2)}) collective-permute-start(bf16[48,2048]{1,0:T(8,128)(2,1)S(1)} %get-tuple-element.22), channel_id=1, source_target_pairs={{0,8},{8,0},{16,24},{24,16},{1,9},{9,1},{17,25},{25,17},{2,10},{10... | collective-permute-start | bytes 589832 | tf_op jit(solution)/shard_map/late/ppermute | solution.py:21
  30.5 11.8 %copy-start = (f32[8,48,2048]{2,1,0:T(8,128)S(1)}, f32[8,48,2048]{2,1,0:T(8,128)}, u32[]{:S(2)}) copy-start(f32[8,48,2048]{2,1,0:T(8,128)} %param.13) | copy-start | bytes 9437188
  30.5 11.7 %copy-start.3 = (f32[2048]{0:T(1024)S(1)}, f32[2048]{0:T(1024)}, u32[]{:S(2)}) copy-start(f32[2048]{0:T(1024)} %param.15) | copy-start | bytes 24580
  44.0 1.3 %collective-permute-start.10 = (f32[12,8,128]{2,1,0:T(8,128)S(1)}, f32[12,8,128]{2,1,0:T(8,128)S(1)}, u32[]{:S(2)}, u32[]{:S(2)}) collective-permute-start(f32[12,8,128]{2,1,0:T(8,128)S(1)} %get-tuple-element.24), channel_id=1, source_target_pairs={{0,1},{1,0},{2,3},{3,2},{4,5},{5,4},{6,7},{7,6},{8,9},{9,8},{10,11... | collective-permute-start | bytes 147464 | tf_op jit(solution)/shard_map/coefficients/ppermute | solution.py:21
  45.3 5.1 %collective-permute-start.13 = (f32[12,8,128]{2,1,0:T(8,128)S(1)}, f32[12,8,128]{2,1,0:T(8,128)S(1)}, u32[]{:S(2)}, u32[]{:S(2)}) collective-permute-start(f32[12,8,128]{2,1,0:T(8,128)S(1)} %add.42), channel_id=1, source_target_pairs={{0,6},{1,7},{2,4},{3,5},{4,2},{5,3},{6,0},{7,1},{8,14},{9,15},{10,... | collective-permute-start | bytes 147464 | tf_op jit(solution)/shard_map/coefficients/ppermute | solution.py:21
  46.5 4.5 %collective-permute-start.12 = (f32[12,8,128]{2,1,0:T(8,128)S(1)}, f32[12,8,128]{2,1,0:T(8,128)S(1)}, u32[]{:S(2)}, u32[]{:S(2)}) collective-permute-start(f32[12,8,128]{2,1,0:T(8,128)S(1)} %add.42), channel_id=1, source_target_pairs={{0,4},{1,5},{2,6},{3,7},{4,0},{5,1},{6,2},{7,3},{8,12},{9,13},{10,... | collective-permute-start | bytes 147464 | tf_op jit(solution)/shard_map/coefficients/ppermute | solution.py:21
  48.0 4.2 %collective-permute-start.11 = (f32[12,8,128]{2,1,0:T(8,128)S(1)}, f32[12,8,128]{2,1,0:T(8,128)S(1)}, u32[]{:S(2)}, u32[]{:S(2)}) collective-permute-start(f32[12,8,128]{2,1,0:T(8,128)S(1)} %add.42), channel_id=1, source_target_pairs={{0,2},{1,3},{2,0},{3,1},{4,6},{5,7},{6,4},{7,5},{8,10},{9,11},{10,... | collective-permute-start | bytes 147464 | tf_op jit(solution)/shard_map/coefficients/ppermute | solution.py:21
  52.2 6.2 %collective-permute-start.16 = (f32[12,8,128]{2,1,0:T(8,128)S(1)}, f32[12,8,128]{2,1,0:T(8,128)S(1)}, u32[]{:S(2)}, u32[]{:S(2)}) collective-permute-start(f32[12,8,128]{2,1,0:T(8,128)S(1)} %add_add_fusion.1), channel_id=1, source_target_pairs={{0,24},{8,16},{16,8},{24,0},{1,25},{9,17},{17,9},{25,1},{2,26},{10... | collective-permute-start | bytes 147464 | tf_op jit(solution)/shard_map/coefficients/ppermute | solution.py:21
  53.9 5.5 %collective-permute-start.15 = (f32[12,8,128]{2,1,0:T(8,128)S(1)}, f32[12,8,128]{2,1,0:T(8,128)S(1)}, u32[]{:S(2)}, u32[]{:S(2)}) collective-permute-start(f32[12,8,128]{2,1,0:T(8,128)S(1)} %add_add_fusion.1), channel_id=1, source_target_pairs={{0,16},{8,24},{16,0},{24,8},{1,17},{9,25},{17,1},{25,9},{2,18},{10... | collective-permute-start | bytes 147464 | tf_op jit(solution)/shard_map/coefficients/ppermute | solution.py:21
  53.9 5.5 %collective-permute-start.14 = (f32[12,8,128]{2,1,0:T(8,128)S(1)}, f32[12,8,128]{2,1,0:T(8,128)S(1)}, u32[]{:S(2)}, u32[]{:S(2)}) collective-permute-start(f32[12,8,128]{2,1,0:T(8,128)S(1)} %add_add_fusion.1), channel_id=1, source_target_pairs={{0,8},{8,0},{16,24},{24,16},{1,9},{9,1},{17,25},{25,17},{2,10},{10... | collective-permute-start | bytes 147464 | tf_op jit(solution)/shard_map/coefficients/ppermute | solution.py:21
  59.4 1.3 %collective-permute-start.17 = (f32[12,8,128]{2,1,0:T(8,128)S(1)}, f32[12,8,128]{2,1,0:T(8,128)S(1)}, u32[]{:S(2)}, u32[]{:S(2)}) collective-permute-start(f32[12,8,128]{2,1,0:T(8,128)S(1)} %add_add_fusion.mine), channel_id=1, source_target_pairs={{0,1},{1,0},{2,3},{3,2},{4,5},{5,4},{6,7},{7,6},{8,9},{9,8},{10,11... | collective-permute-start | bytes 147464 | tf_op jit(solution)/shard_map/coefficients/ppermute | solution.py:21
  62.8 1.2 %collective-permute-start.18 = (f32[24,128]{1,0:T(8,128)S(1)}, f32[24,128]{1,0:T(8,128)S(1)}, u32[]{:S(2)}, u32[]{:S(2)}) collective-permute-start(f32[24,128]{1,0:T(8,128)S(1)} %get-tuple-element.28), channel_id=1, source_target_pairs={{0,1},{1,0},{2,3},{3,2},{4,5},{5,4},{6,7},{7,6},{8,9},{9,8},{10,11... | collective-permute-start | bytes 36872 | tf_op jit(solution)/shard_map/gram/ppermute | solution.py:21
  64.0 4.6 %collective-permute-start.21 = (f32[24,128]{1,0:T(8,128)S(1)}, f32[24,128]{1,0:T(8,128)S(1)}, u32[]{:S(2)}, u32[]{:S(2)}) collective-permute-start(f32[24,128]{1,0:T(8,128)S(1)} %add.49), channel_id=1, source_target_pairs={{0,6},{1,7},{2,4},{3,5},{4,2},{5,3},{6,0},{7,1},{8,14},{9,15},{10,... | collective-permute-start | bytes 36872 | tf_op jit(solution)/shard_map/gram/ppermute | solution.py:21
  66.6 3.7 %collective-permute-start.20 = (f32[24,128]{1,0:T(8,128)S(1)}, f32[24,128]{1,0:T(8,128)S(1)}, u32[]{:S(2)}, u32[]{:S(2)}) collective-permute-start(f32[24,128]{1,0:T(8,128)S(1)} %add.49), channel_id=1, source_target_pairs={{0,4},{1,5},{2,6},{3,7},{4,0},{5,1},{6,2},{7,3},{8,12},{9,13},{10,... | collective-permute-start | bytes 36872 | tf_op jit(solution)/shard_map/gram/ppermute | solution.py:21
  66.7 3.7 %collective-permute-start.19 = (f32[24,128]{1,0:T(8,128)S(1)}, f32[24,128]{1,0:T(8,128)S(1)}, u32[]{:S(2)}, u32[]{:S(2)}) collective-permute-start(f32[24,128]{1,0:T(8,128)S(1)} %add.49), channel_id=1, source_target_pairs={{0,2},{1,3},{2,0},{3,1},{4,6},{5,7},{6,4},{7,5},{8,10},{9,11},{10,... | collective-permute-start | bytes 36872 | tf_op jit(solution)/shard_map/gram/ppermute | solution.py:21
  70.4 5.5 %collective-permute-start.24 = (f32[24,128]{1,0:T(8,128)S(1)}, f32[24,128]{1,0:T(8,128)S(1)}, u32[]{:S(2)}, u32[]{:S(2)}) collective-permute-start(f32[24,128]{1,0:T(8,128)S(1)} %add_add_fusion.3), channel_id=1, source_target_pairs={{0,24},{8,16},{16,8},{24,0},{1,25},{9,17},{17,9},{25,1},{2,26},{10... | collective-permute-start | bytes 36872 | tf_op jit(solution)/shard_map/gram/ppermute | solution.py:21
  72.4 4.6 %collective-permute-start.23 = (f32[24,128]{1,0:T(8,128)S(1)}, f32[24,128]{1,0:T(8,128)S(1)}, u32[]{:S(2)}, u32[]{:S(2)}) collective-permute-start(f32[24,128]{1,0:T(8,128)S(1)} %add_add_fusion.3), channel_id=1, source_target_pairs={{0,16},{8,24},{16,0},{24,8},{1,17},{9,25},{17,1},{25,9},{2,18},{10... | collective-permute-start | bytes 36872 | tf_op jit(solution)/shard_map/gram/ppermute | solution.py:21
  73.3 3.8 %collective-permute-start.22 = (f32[24,128]{1,0:T(8,128)S(1)}, f32[24,128]{1,0:T(8,128)S(1)}, u32[]{:S(2)}, u32[]{:S(2)}) collective-permute-start(f32[24,128]{1,0:T(8,128)S(1)} %add_add_fusion.3), channel_id=1, source_target_pairs={{0,8},{8,0},{16,24},{24,16},{1,9},{9,1},{17,25},{25,17},{2,10},{10... | collective-permute-start | bytes 36872 | tf_op jit(solution)/shard_map/gram/ppermute | solution.py:21

commit v8 on v7

--- a/solution.py
+++ b/solution.py
@@ -64,10 +64,10 @@
     out,
     held,
     acc,
+    panel_buf,
     rows,
     cols,
     plan,
-    panel_buf,
     tile_sem,
     list_sem,
     panel_sem,
@@ -86,7 +86,9 @@
     def _(k):
         tile_copy(k).start()
 
-    copies = load_panels((own_panel, near_panel), panel_buf, panel_sem)
+    copies = load_panels({0: own_panel, 1: near_panel}, panel_buf, panel_sem)
+    zero_panel = panel_buf.shape[0] - 1
+    panel_buf[zero_panel, :, :LANES] = jnp.zeros((panel_buf.shape[1], LANES), jnp.bfloat16)
     f32, bf16, i32 = jnp.float32, jnp.bfloat16, jnp.int32
     slots, places = rows.shape[1], out.shape[1] - LANES
     targets = row_devs * slab_tiles
@@ -172,33 +174,44 @@
 
 
 def load_panels(panels, panel_buf, sem):
-    copies = [pltpu.make_async_copy(ref, panel_buf.at[m], sem.at[m]) for m, ref in enumerate(panels)]
+    copies = [pltpu.make_async_copy(ref, panel_buf.at[m], sem.at[i]) for i, (m, ref) in enumerate(panels.items())]
     for copy in copies:
         copy.start()
-    zero = panel_buf.shape[0] - 1
-    panel_buf[zero, :, :LANES] = jnp.zeros((panel_buf.shape[1], LANES), jnp.bfloat16)
     return copies
 
 
-def first_late_kernel(mask, place, plan, *refs):
-    panels = refs[:-6]
-    tiles, early, send, panel_buf, acc, sem = refs[-6:]
+def collect_kernel(masks, *refs):
+    panels, (_, panel_buf, sem) = refs[: len(masks)], refs[len(masks) :]
+    for copy in load_panels(dict(zip(masks, panels)), panel_buf, sem):
+        copy.wait()
+
+
+def first_late_kernel(masks, odd, place, plan, *refs):
+    panels = dict(zip(odd, refs))
+    tiles, early, _ = refs[len(odd) : len(odd) + 3]
+    sends = refs[len(odd) + 3 : -3]
+    panel_buf, acc, sem = refs[-3:]
     copies = load_panels(panels, panel_buf, sem)
-    late_part(mask, place, plan, tiles, early, panel_buf, acc, copies)
-    put(send, acc)
-
-
-def late_kernel(masks, place, plan, panel_buf, tiles, early, *refs):
-    acc = refs[-1]
-    for mask, send in zip(masks, refs):
+    for mask, send in zip(late_masks(masks, place), sends):
+        late_part(mask, place, plan, tiles, early, panel_buf, acc, copies)
+        put(send, acc)
+        copies = ()
+
+
+def late_masks(masks, place):
+    inner = (place[0] == 1) | (place[0] == 2)
+    change = {"x": jnp.where(inner, 1, 2), "y": jnp.where(inner, 2, 1)}
+    return [change.get(mask, mask) for mask in masks]
+
+
+def late_kernel(masks, place, plan, panel_buf, tiles, early, current, previous, coupling, diag, *refs):
+    sends, base, acc = refs[:-2], refs[-2], refs[-1]
+    for mask, send in zip(late_masks(masks, place), sends):
         late_part(mask, place, plan, tiles, early, panel_buf, acc, ())
         put(send, acc)
-
-
-def own_kernel(place, plan, panel_buf, tiles, early, received, current, previous, coupling, diag, base, acc):
     late_part(0, place, plan, tiles, early, panel_buf, acc, ())
     put(base, acc)
-    base[...] += received[...].astype(jnp.float32) + diag[...] * current[...] - jnp.dot(
+    base[...] += diag[...] * current[...] - jnp.dot(
         coupling[...],
         previous[...],
         precision=lax.Precision.HIGHEST,
@@ -341,20 +354,20 @@
     with jax.named_scope("early"):
         places = -(-(slots + (GROUP - 1) * 2 * targets + GROUP * UNROLL) // LANES) * LANES
         plan_shape = (1, places + LANES)
-        plan, held, early = pl.pallas_call(
+        plan, held, early, gathered = pl.pallas_call(
             functools.partial(early_kernel, row_devs, col_devs, slab_tiles),
             out_shape=[
                 jax.ShapeDtypeStruct(plan_shape, jnp.int32),
                 pltpu.VMEM(tile_values.shape, bf16),
                 pltpu.VMEM(early_shape, f32),
+                pltpu.VMEM(panel_shape, bf16),
             ],
             in_specs=smem(2) + [pl.BlockSpec(memory_space=pltpu.HBM)] * 3 + anywhere * 2,
-            out_specs=vmem(3),
+            out_specs=vmem(4),
             scratch_shapes=[
                 pltpu.VMEM((1, slots), jnp.int32),
                 pltpu.VMEM((1, slots), jnp.int32),
                 pltpu.SMEM(plan_shape, jnp.int32),
-                pltpu.VMEM(panel_shape, bf16),
                 pltpu.SemaphoreType.DMA((slots // CHUNK,)),
                 pltpu.SemaphoreType.DMA((3,)),
                 pltpu.SemaphoreType.DMA((2,)),
@@ -375,39 +388,52 @@
         for m in range(col_devs - 2, 0, -2):
             panels[m] = after(panels[m], early)
             panels[m + 1] = swap(panels[m], "col", 1)
+        even, odd = list(range(2, col_devs, 2)), list(range(3, col_devs, 2))
+        gathered = pl.pallas_call(
+            functools.partial(collect_kernel, even),
+            out_shape=pltpu.VMEM(panel_shape, bf16),
+            in_specs=anywhere * len(even) + vmem(1),
+            out_specs=vmem(1)[0],
+            scratch_shapes=[pltpu.SemaphoreType.DMA((len(even),))],
+            input_output_aliases={len(even): 0},
+            compiler_params=limit(1),
+            cost_estimate=cost(width),
+        )(*[panels[m] for m in even], gathered)
 
     with jax.named_scope("late"):
+        relay = row_devs == 4
+        first_masks = [3, "x"] if relay else [row_devs - 1]
+        last_masks = ["y"] if relay else list(range(row_devs - 2, 0, -1))
         part = jax.ShapeDtypeStruct((width, slab_len), bf16)
-        first, gathered = pl.pallas_call(
-            functools.partial(first_late_kernel, row_devs - 1),
-            out_shape=[part, pltpu.VMEM(panel_shape, bf16)],
-            in_specs=smem(2) + anywhere * col_devs + vmem(2),
-            out_specs=vmem(2),
-            scratch_shapes=[part_acc, pltpu.SemaphoreType.DMA((col_devs,))],
+        *firsts, gathered = pl.pallas_call(
+            functools.partial(first_late_kernel, first_masks, odd),
+            out_shape=[part] * len(first_masks) + [pltpu.VMEM(panel_shape, bf16)],
+            in_specs=smem(2) + anywhere * len(odd) + vmem(3),
+            out_specs=vmem(len(first_masks) + 1),
+            scratch_shapes=[part_acc, pltpu.SemaphoreType.DMA((len(odd),))],
+            input_output_aliases={4 + len(odd): len(first_masks)},
             compiler_params=limit(8),
             cost_estimate=cost(width),
-        )(place, plan, *panels, held, early)
-        first = swap(first, "row", row_devs - 1)
-        masks = list(range(row_devs - 2, 0, -1))
-        others = pl.pallas_call(
-            functools.partial(late_kernel, masks),
-            out_shape=[part] * len(masks),
-            in_specs=smem(2) + vmem(3),
-            out_specs=vmem(len(masks)),
+        )(place, plan, *[panels[m] for m in odd], held, early, gathered)
+        lasts = [slab] if relay else [part] * len(last_masks)
+        *lasts, base = pl.pallas_call(
+            functools.partial(late_kernel, last_masks),
+            out_shape=lasts + [slab],
+            in_specs=smem(2) + vmem(7),
+            out_specs=vmem(len(lasts) + 1),
             scratch_shapes=[part_acc],
             compiler_params=limit(8),
             cost_estimate=cost(width),
-        )(place, plan, gathered, held, early)
-        received = [swap(other, "row", m) for m, other in zip(masks, others)]
-        base = pl.pallas_call(
-            own_kernel,
-            out_shape=slab,
-            in_specs=smem(2) + vmem(8),
-            out_specs=vmem(1)[0],
-            scratch_shapes=[part_acc],
-            compiler_params=limit(8),
-            cost_estimate=cost(width),
-        )(place, plan, gathered, held, early, first, current_block, previous_block, previous_coupling, diag)
+        )(place, plan, gathered, held, early, current_block, previous_block, previous_coupling, diag)
+        if relay:
+            passing = lax.ppermute(firsts[0], "row", [(0, 1), (3, 2)])
+            received = [lax.ppermute(firsts[0], "row", [(1, 2), (2, 1)])]
+            received.append(lax.ppermute(firsts[1], "row", [(0, 2), (3, 1), (1, 0), (2, 3)]))
+            joined = (lasts[0] + passing.astype(f32)).astype(bf16)
+            received.append(lax.ppermute(joined, "row", [(0, 1), (1, 3), (3, 2), (2, 0)]))
+        else:
+            received = [swap(firsts[0], "row", first_masks[0])]
+            received += [swap(last, "row", m) for m, last in zip(last_masks, lasts)]
 
     basis_rows = (stored_count + 1) * width
     padded = (width, -(-basis_rows // LANES) * LANES)

time: 77.7 us -> 76.6 us (0.986)
  starting transfers between devices: 26.1 us -> 30.9 us
  Pallas kernels: 19.6 us -> 15 us
  waiting for transfers between devices: 28 us -> 26.4 us
    ppermute x25 -> x22, waiting for transfers between devices: 28 us -> 17.1 us  [swap(): return lax.ppermute(value, axis, [(i, i ^ mask) for i in range(count)])]
    ppermute x0 -> x4, waiting for transfers between devices: none -> 9.29 us  [the longest x1 7.6 us: local(): lax.ppermute(joined, 'row', [(0, 1), (1, 3), (3, 2), (2, 0)])]
    ppermute x0 -> x4, starting transfers between devices: none -> 7.74 us  [the longest x1 2.89 us: local(): passing = lax.ppermute(firsts[0], 'row', [(0, 1), (3, 2)])]
    ppermute x25 -> x22, starting transfers between devices: 26.1 us -> 23.2 us  [swap(): return lax.ppermute(value, axis, [(i, i ^ mask) for i in range(count)])]
    pallas_call x3, Pallas kernels: 9.75 us -> 7.08 us  [the longest x1 3.64 us: local(): pl.pallas_call(functools.partial(first_late_kernel, first_masks, odd), ou...]
    pallas_call x1, Pallas kernels: 5.98 us -> 4.15 us  [local(): pl.pallas_call(functools.partial(early_kernel, row_devs, col_devs, slab_t...]
  transfers between devices with their start and end apart: 25 -> 26, of which waited for: 19 -> 18; matrix products, arithmetic and copies ran while one was open for 1% -> 1% of each run, Pallas kernels for 14% -> 10%
where the time goes in v8:
time: 76.6 us; the launch traced here: 76.5 us
  starting transfers between devices  30.9 us (40%)
  waiting for transfers between devices  26.4 us (34%)
  Pallas kernels  15 us (20%)
  other arithmetic  1.8 us (2%)
  between operations  1.45 us (2%)
  local copies, waits for them, and re-layouts  0.92 us (1%)
    ppermute x22, starting transfers between devices, swap(): return lax.ppermute(value, axis, [(i, i ^ mask) for i in range(count)])  23.2 us
    ppermute x22, waiting for transfers between devices, swap(): return lax.ppermute(value, axis, [(i, i ^ mask) for i in range(count)])  17.1 us
    ppermute x1, waiting for transfers between devices, local(): lax.ppermute(joined, 'row', [(0, 1), (1, 3), (3, 2), (2, 0)])  7.6 us
    pallas_call x1, Pallas kernels, local(): pl.pallas_call(functools.partial(early_kernel, row_devs, col_devs, slab_t...  4.15 us
    pallas_call x1, Pallas kernels, local(): pl.pallas_call(functools.partial(first_late_kernel, first_masks, odd), ou...  3.64 us
    ppermute x1, starting transfers between devices, local(): passing = lax.ppermute(firsts[0], 'row', [(0, 1), (3, 2)])  2.89 us
    pallas_call x1, Pallas kernels, local(): pl.pallas_call(functools.partial(late_kernel, last_masks), out_shape=last...  2.68 us
    ppermute x1, starting transfers between devices, local(): lax.ppermute(firsts[1], 'row', [(0, 2), (3, 1), (1, 0), (2, 3)])  2.13 us
  transfers between devices with their start and end apart: 26, of which 18 were waited for; matrix products, arithmetic and copies ran while one was open for 1% of the time, Pallas kernels for 10%

profile of v8, /device:TPU:0, one launch (start us, length us, event | category | flops | bytes accessed | tf_op | source)
XLA Modules:
  0.0 76.5 jit_solution(3626801843101842638)
XLA Ops:
  0.6 1.0 %convert_element_type.9.own_panel = bf16[48,2048]{1,0:T(8,128)(2,1)S(1)} convert(f32[48,2048]{1,0:T(8,128)} %current.3) | non-fusion elementwise | flops 98304 | bytes 589824 | tf_op jit(solution)/shard_map/gather/convert_element_type | solution.py:348
  1.7 0.5 collective-permute-start
  2.2 2.6 %collective-permute-start.1 = (bf16[48,2048]{1,0:T(8,128)(2,1)S(1)}, bf16[48,2048]{1,0:T(8,128)(2,1)S(1)}, u32[]{:S(2)}, u32[]{:S(2)}) collective-permute-start(bf16[48,2048]{1,0:T(8,128)(2,1)S(1)} %convert_element_type.9.own_panel), channel_id=1, source_target_pairs={{0,2},{1,3},{2,0},{3,1},{4,6},{5,7},{6,4},{7,5},{8,10},{9,11},{10,... | collective-permute-start | bytes 589832 | tf_op jit(solution)/shard_map/gather/ppermute | solution.py:21
  4.7 1.5 %collective-permute-start.3 = (bf16[48,2048]{1,0:T(8,128)(2,1)S(1)}, bf16[48,2048]{1,0:T(8,128)(2,1)S(1)}, u32[]{:S(2)}, u32[]{:S(2)}) collective-permute-start(bf16[48,2048]{1,0:T(8,128)(2,1)S(1)} %convert_element_type.9.own_panel), channel_id=1, source_target_pairs={{0,4},{1,5},{2,6},{3,7},{4,0},{5,1},{6,2},{7,3},{8,12},{9,13},{10,... | collective-permute-start | bytes 589832 | tf_op jit(solution)/shard_map/gather/ppermute | solution.py:21
  6.3 0.0 collective-permute-start.5
  6.9 0.1 pad_add_fusion.place
  7.0 0.0 collective-permute-done.near_panel
  7.0 4.2 %early.1 = (s32[1,896]{1,0:T(1,128)S(1)}, bf16[512,128,128]{2,1,0:T(8,128)(2,1)S(1)}, f32[65,48,128]{2,1,0:T(8,128)S(1)}, bf16[9,48,2048]{2,1,0:T(8,128)(2,1)S(1)}) custom-call(s32[2]{0:T(128)S(1)} %pad_add_fusion.place, s32[1]{0:T(128)S(6)} %copy.25.counts, s32[1,512]{1,0:T(1,128)} %bitcast.16, s32[1,512]{1,0:T(1,128)} %bitcast.17, ...), custom_call_target="tpu_custom_call" | custom-call | flops 805306368 | bytes 16777216 | tf_op jit(solution)/shard_map/early/pallas_call | solution.py:357
  11.2 0.0 collective-permute-done.1.value
  11.2 1.8 %collective-permute-start.2 = (bf16[48,2048]{1,0:T(8,128)(2,1)S(1)}, bf16[48,2048]{1,0:T(8,128)(2,1)S(1)}, u32[]{:S(2)}, u32[]{:S(2)}) collective-permute-start(bf16[48,2048]{1,0:T(8,128)(2,1)S(1)} %gather.4.refs_0_), channel_id=1, source_target_pairs={{0,1},{1,0},{2,3},{3,2},{4,5},{5,4},{6,7},{7,6},{8,9},{9,8},{10,11... | collective-permute-start | bytes 589832 | tf_op jit(solution)/shard_map/gather/ppermute | solution.py:21
  13.0 3.0 %collective-permute-done.3.value = bf16[48,2048]{1,0:T(8,128)(2,1)S(1)} collective-permute-done((bf16[48,2048]{1,0:T(8,128)(2,1)S(1)}, bf16[48,2048]{1,0:T(8,128)(2,1)S(1)}, u32[]{:S(2)}, u32[]{:S(2)}) %collective-permute-start.3) | collective-permute-done | bytes 196640 | tf_op jit(solution)/shard_map/gather/ppermute | solution.py:21
  15.9 0.0 collective-permute-start.4
  15.9 0.0 collective-permute-done.5.value
  15.9 0.5 collective-permute-start.6
  16.4 0.8 gather.7.refs_5_
  17.2 0.0 collective-permute-done.2.refs_0_
  17.2 0.2 collective-permute-done.4.refs_1_
  17.4 0.3 collective-permute-done.6.refs_2_
  17.7 3.6 %late.2 = (bf16[48,2048]{1,0:T(8,128)(2,1)S(1)}, bf16[48,2048]{1,0:T(8,128)(2,1)S(1)}, bf16[9,48,2048]{2,1,0:T(8,128)(2,1)S(1)}) custom-call(s32[2]{0:T(128)S(1)} %pad_add_fusion.place, s32[1,896]{1,0:T(1,128)S(1)} %get-tuple-element.18.plan, bf16[48,2048]{1,0:T(8,128)(2,1)S(1)} %collective-permute-done.2.refs_0_, ...), custom_call_target="tpu_custom_call", output_to_operand_aliasing={{2}: (7, {})} | custom-call | flops 48 | bytes 1 | tf_op jit(solution)/shard_map/late/pallas_call | solution.py:408
  21.3 2.9 %collective-permute-start.9 = (bf16[48,2048]{1,0:T(8,128)(2,1)S(1)}, bf16[48,2048]{1,0:T(8,128)(2,1)S(1)}, u32[]{:S(2)}, u32[]{:S(2)}) collective-permute-start(bf16[48,2048]{1,0:T(8,128)(2,1)S(1)} %get-tuple-element.24), channel_id=1, source_target_pairs={{0,8},{24,16},{1,9},{25,17},{2,10},{26,18},{3,11},{27,19},{4,12},{... | collective-permute-start | bytes 589832 | tf_op jit(solution)/shard_map/late/ppermute | solution.py:429
  24.2 0.7 collective-permute-start.7
  24.9 2.1 %collective-permute-start.8 = (bf16[48,2048]{1,0:T(8,128)(2,1)S(1)}, bf16[48,2048]{1,0:T(8,128)(2,1)S(1)}, u32[]{:S(2)}, u32[]{:S(2)}) collective-permute-start(bf16[48,2048]{1,0:T(8,128)(2,1)S(1)} %get-tuple-element.25), channel_id=1, source_target_pairs={{0,16},{24,8},{8,0},{16,24},{1,17},{25,9},{9,1},{17,25},{2,18},{26... | collective-permute-start | bytes 589832 | tf_op jit(solution)/shard_map/late/ppermute | solution.py:431
  27.0 0.0 copy-start
  27.0 0.0 copy-start.3
  27.0 2.7 %late.3 = (f32[48,2048]{1,0:T(8,128)S(1)}, f32[48,2048]{1,0:T(8,128)S(1)}) custom-call(s32[2]{0:T(128)S(1)} %pad_add_fusion.place, s32[1,896]{1,0:T(1,128)S(1)} %get-tuple-element.18.plan, bf16[9,48,2048]{2,1,0:T(8,128)(2,1)S(1)} %get-tuple-element.22.panel_buf, bf16[512,128,128]{2,1,0:T(8,128)(2,1)S(1)} %get-tuple-element.20.refs_3_.tiles, ...), custom_call_target="tpu_custom_call" | custom-call | flops 48 | bytes 1 | tf_op jit(solution)/shard_map/late/pallas_call | solution.py:419
  29.7 0.0 collective-permute-done.9
  29.8 2.1 %collective-permute-start.10 = (bf16[48,2048]{1,0:T(8,128)(2,1)S(1)}, bf16[48,2048]{1,0:T(8,128)(2,1)S(1)}, u32[]{:S(2)}, u32[]{:S(2)}) collective-permute-start(bf16[48,2048]{1,0:T(8,128)(2,1)S(1)} %add_convert_fusion), channel_id=1, source_target_pairs={{0,8},{8,24},{24,16},{16,0},{1,9},{9,25},{25,17},{17,1},{2,10},{10... | collective-permute-start | bytes 589832 | tf_op jit(solution)/shard_map/late/ppermute | solution.py:433
  31.8 1.7 %collective-permute-done.8.refs_1_ = bf16[48,2048]{1,0:T(8,128)(2,1)S(1)} collective-permute-done((bf16[48,2048]{1,0:T(8,128)(2,1)S(1)}, bf16[48,2048]{1,0:T(8,128)(2,1)S(1)}, u32[]{:S(2)}, u32[]{:S(2)}) %collective-permute-start.8) | collective-permute-done | bytes 196640 | tf_op jit(solution)/shard_map/late/ppermute | solution.py:431
  33.5 0.0 collective-permute-done.7.refs_0_
  33.5 7.6 %collective-permute-done.10.refs_2_ = bf16[48,2048]{1,0:T(8,128)(2,1)S(1)} collective-permute-done((bf16[48,2048]{1,0:T(8,128)(2,1)S(1)}, bf16[48,2048]{1,0:T(8,128)(2,1)S(1)}, u32[]{:S(2)}, u32[]{:S(2)}) %collective-permute-start.10) | collective-permute-done | bytes 196640 | tf_op jit(solution)/shard_map/late/ppermute | solution.py:433
  41.1 1.7 %coefficients.1 = (f32[48,2048]{1,0:T(8,128)S(1)}, f32[12,8,128]{2,1,0:T(8,128)S(1)}, f32[12,8,128]{2,1,0:T(8,128)S(1)}) custom-call(s32[2]{0:T(128)S(1)} %pad_add_fusion.place, f32[48,2048]{1,0:T(8,128)S(1)} %get-tuple-element.23.base, bf16[48,2048]{1,0:T(8,128)(2,1)S(1)} %collective-permute-done.7.refs_0_, ...), custom_call_target="tpu_custom_call" | custom-call | tf_op jit(solution)/shard_map/coefficients/pallas_call | solution.py:442
  42.9 0.2 collective-permute-start.11
  43.0 1.1 %collective-permute-done.11 = f32[12,8,128]{2,1,0:T(8,128)S(1)} collective-permute-done((f32[12,8,128]{2,1,0:T(8,128)S(1)}, f32[12,8,128]{2,1,0:T(8,128)S(1)}, u32[]{:S(2)}, u32[]{:S(2)}) %collective-permute-start.11) | collective-permute-done | bytes 49184 | tf_op jit(solution)/shard_map/coefficients/ppermute | solution.py:21
  44.2 2.1 %collective-permute-start.14 = (f32[12,8,128]{2,1,0:T(8,128)S(1)}, f32[12,8,128]{2,1,0:T(8,128)S(1)}, u32[]{:S(2)}, u32[]{:S(2)}) collective-permute-start(f32[12,8,128]{2,1,0:T(8,128)S(1)} %add.46), channel_id=1, source_target_pairs={{0,6},{1,7},{2,4},{3,5},{4,2},{5,3},{6,0},{7,1},{8,14},{9,15},{10,... | collective-permute-start | bytes 147464 | tf_op jit(solution)/shard_map/coefficients/ppermute | solution.py:21
  46.3 0.2 collective-permute-start.13
  46.5 1.2 %collective-permute-start.12 = (f32[12,8,128]{2,1,0:T(8,128)S(1)}, f32[12,8,128]{2,1,0:T(8,128)S(1)}, u32[]{:S(2)}, u32[]{:S(2)}) collective-permute-start(f32[12,8,128]{2,1,0:T(8,128)S(1)} %add.46), channel_id=1, source_target_pairs={{0,2},{1,3},{2,0},{3,1},{4,6},{5,7},{6,4},{7,5},{8,10},{9,11},{10,... | collective-permute-start | bytes 147464 | tf_op jit(solution)/shard_map/coefficients/ppermute | solution.py:21
  47.7 1.5 %collective-permute-done.14 = f32[12,8,128]{2,1,0:T(8,128)S(1)} collective-permute-done((f32[12,8,128]{2,1,0:T(8,128)S(1)}, f32[12,8,128]{2,1,0:T(8,128)S(1)}, u32[]{:S(2)}, u32[]{:S(2)}) %collective-permute-start.14) | collective-permute-done | bytes 49184 | tf_op jit(solution)/shard_map/coefficients/ppermute | solution.py:21
  49.2 1.2 %collective-permute-done.13 = f32[12,8,128]{2,1,0:T(8,128)S(1)} collective-permute-done((f32[12,8,128]{2,1,0:T(8,128)S(1)}, f32[12,8,128]{2,1,0:T(8,128)S(1)}, u32[]{:S(2)}, u32[]{:S(2)}) %collective-permute-start.13) | collective-permute-done | bytes 49184 | tf_op jit(solution)/shard_map/coefficients/ppermute | solution.py:21
  50.4 0.2 collective-permute-done.12
  50.7 2.7 %collective-permute-start.17 = (f32[12,8,128]{2,1,0:T(8,128)S(1)}, f32[12,8,128]{2,1,0:T(8,128)S(1)}, u32[]{:S(2)}, u32[]{:S(2)}) collective-permute-start(f32[12,8,128]{2,1,0:T(8,128)S(1)} %add_add_fusion.1), channel_id=1, source_target_pairs={{0,24},{8,16},{16,8},{24,0},{1,25},{9,17},{17,9},{25,1},{2,26},{10... | collective-permute-start | bytes 147464 | tf_op jit(solution)/shard_map/coefficients/ppermute | solution.py:21
  53.4 1.8 %collective-permute-start.15 = (f32[12,8,128]{2,1,0:T(8,128)S(1)}, f32[12,8,128]{2,1,0:T(8,128)S(1)}, u32[]{:S(2)}, u32[]{:S(2)}) collective-permute-start(f32[12,8,128]{2,1,0:T(8,128)S(1)} %add_add_fusion.1), channel_id=1, source_target_pairs={{0,8},{8,0},{16,24},{24,16},{1,9},{9,1},{17,25},{25,17},{2,10},{10... | collective-permute-start | bytes 147464 | tf_op jit(solution)/shard_map/coefficients/ppermute | solution.py:21
  55.1 1.7 %collective-permute-done.17 = f32[12,8,128]{2,1,0:T(8,128)S(1)} collective-permute-done((f32[12,8,128]{2,1,0:T(8,128)S(1)}, f32[12,8,128]{2,1,0:T(8,128)S(1)}, u32[]{:S(2)}, u32[]{:S(2)}) %collective-permute-start.17) | collective-permute-done | bytes 49184 | tf_op jit(solution)/shard_map/coefficients/ppermute | solution.py:21
  56.8 1.5 %collective-permute-done.16 = f32[12,8,128]{2,1,0:T(8,128)S(1)} collective-permute-done((f32[12,8,128]{2,1,0:T(8,128)S(1)}, f32[12,8,128]{2,1,0:T(8,128)S(1)}, u32[]{:S(2)}, u32[]{:S(2)}) %collective-permute-start.16) | collective-permute-done | bytes 49184 | tf_op jit(solution)/shard_map/coefficients/ppermute | solution.py:21
  58.3 0.0 collective-permute-done.15
  58.4 0.1 collective-permute-start.18
  58.4 1.2 %collective-permute-done.18.other = f32[12,8,128]{2,1,0:T(8,128)S(1)} collective-permute-done((f32[12,8,128]{2,1,0:T(8,128)S(1)}, f32[12,8,128]{2,1,0:T(8,128)S(1)}, u32[]{:S(2)}, u32[]{:S(2)}) %collective-permute-start.18) | collective-permute-done | bytes 49184 | tf_op jit(solution)/shard_map/coefficients/ppermute | solution.py:21
  59.7 2.1 %residual.1 = (f32[48,2048]{1,0:T(8,128)}, f32[48,432]{1,0:T(8,128)S(1)}, f32[24,128]{1,0:T(8,128)S(1)}) custom-call(s32[2]{0:T(128)S(1)} %pad_add_fusion.place, f32[12,8,128]{2,1,0:T(8,128)S(1)} %add_add_fusion.mine, f32[12,8,128]{2,1,0:T(8,128)S(1)} %collective-permute-done.18.other, f32[48,2048]{1,0:T(8,128)S(1)} %get-tuple-element.29.recurrence, ...), custom_call_target="tpu_custom_call" | custom-call | tf_op jit(solution)/shard_map/residual/pallas_call | solution.py:455
  61.7 0.2 collective-permute-start.19
  61.9 1.0 %collective-permute-done.19 = f32[24,128]{1,0:T(8,128)S(1)} collective-permute-done((f32[24,128]{1,0:T(8,128)S(1)}, f32[24,128]{1,0:T(8,128)S(1)}, u32[]{:S(2)}, u32[]{:S(2)}) %collective-permute-start.19) | collective-permute-done | bytes 12320 | tf_op jit(solution)/shard_map/gram/ppermute | solution.py:21
  62.9 1.3 %collective-permute-start.22 = (f32[24,128]{1,0:T(8,128)S(1)}, f32[24,128]{1,0:T(8,128)S(1)}, u32[]{:S(2)}, u32[]{:S(2)}) collective-permute-start(f32[24,128]{1,0:T(8,128)S(1)} %add.53), channel_id=1, source_target_pairs={{0,6},{1,7},{2,4},{3,5},{4,2},{5,3},{6,0},{7,1},{8,14},{9,15},{10,... | collective-permute-start | bytes 36872 | tf_op jit(solution)/shard_map/gram/ppermute | solution.py:21
  64.2 1.3 %collective-permute-start.21 = (f32[24,128]{1,0:T(8,128)S(1)}, f32[24,128]{1,0:T(8,128)S(1)}, u32[]{:S(2)}, u32[]{:S(2)}) collective-permute-start(f32[24,128]{1,0:T(8,128)S(1)} %add.53), channel_id=1, source_target_pairs={{0,4},{1,5},{2,6},{3,7},{4,0},{5,1},{6,2},{7,3},{8,12},{9,13},{10,... | collective-permute-start | bytes 36872 | tf_op jit(solution)/shard_map/gram/ppermute | solution.py:21
  65.5 0.9 %collective-permute-start.20 = (f32[24,128]{1,0:T(8,128)S(1)}, f32[24,128]{1,0:T(8,128)S(1)}, u32[]{:S(2)}, u32[]{:S(2)}) collective-permute-start(f32[24,128]{1,0:T(8,128)S(1)} %add.53), channel_id=1, source_target_pairs={{0,2},{1,3},{2,0},{3,1},{4,6},{5,7},{6,4},{7,5},{8,10},{9,11},{10,... | collective-permute-start | bytes 36872 | tf_op jit(solution)/shard_map/gram/ppermute | solution.py:21
  66.4 1.1 %collective-permute-done.22 = f32[24,128]{1,0:T(8,128)S(1)} collective-permute-done((f32[24,128]{1,0:T(8,128)S(1)}, f32[24,128]{1,0:T(8,128)S(1)}, u32[]{:S(2)}, u32[]{:S(2)}) %collective-permute-start.22) | collective-permute-done | bytes 12320 | tf_op jit(solution)/shard_map/gram/ppermute | solution.py:21
  67.5 0.4 collective-permute-done.21
  67.9 1.3 %collective-permute-done.20 = f32[24,128]{1,0:T(8,128)S(1)} collective-permute-done((f32[24,128]{1,0:T(8,128)S(1)}, f32[24,128]{1,0:T(8,128)S(1)}, u32[]{:S(2)}, u32[]{:S(2)}) %collective-permute-start.20) | collective-permute-done | bytes 12320 | tf_op jit(solution)/shard_map/gram/ppermute | solution.py:21
  69.2 2.0 %collective-permute-start.25 = (f32[24,128]{1,0:T(8,128)S(1)}, f32[24,128]{1,0:T(8,128)S(1)}, u32[]{:S(2)}, u32[]{:S(2)}) collective-permute-start(f32[24,128]{1,0:T(8,128)S(1)} %add_add_fusion.3), channel_id=1, source_target_pairs={{0,24},{8,16},{16,8},{24,0},{1,25},{9,17},{17,9},{25,1},{2,26},{10... | collective-permute-start | bytes 36872 | tf_op jit(solution)/shard_map/gram/ppermute | solution.py:21
  71.2 0.4 collective-permute-start.24
  71.6 2.0 %collective-permute-start.23 = (f32[24,128]{1,0:T(8,128)S(1)}, f32[24,128]{1,0:T(8,128)S(1)}, u32[]{:S(2)}, u32[]{:S(2)}) collective-permute-start(f32[24,128]{1,0:T(8,128)S(1)} %add_add_fusion.3), channel_id=1, source_target_pairs={{0,8},{8,0},{16,24},{24,16},{1,9},{9,1},{17,25},{25,17},{2,10},{10... | collective-permute-start | bytes 36872 | tf_op jit(solution)/shard_map/gram/ppermute | solution.py:21
  73.6 0.8 %copy.19 = f32[432,48]{1,0:T(8,128)} copy(f32[432,48]{0,1:T(8,128)S(1)} %bitcast.11) | data formatting | bytes 165888 | tf_op jit(solution)/shard_map/residual/transpose | solution.py:467
  74.4 0.3 collective-permute-done.25
  74.7 1.1 %collective-permute-done.24 = f32[24,128]{1,0:T(8,128)S(1)} collective-permute-done((f32[24,128]{1,0:T(8,128)S(1)}, f32[24,128]{1,0:T(8,128)S(1)}, u32[]{:S(2)}, u32[]{:S(2)}) %collective-permute-start.24) | collective-permute-done | bytes 12320 | tf_op jit(solution)/shard_map/gram/ppermute | solution.py:21
  75.8 0.0 collective-permute-done.23
  75.8 0.1 fusion
  75.9 0.6 pad_maximum_fusion
  (21 shorter events, 0.1 us)
Async XLA Ops:
  1.7 5.4 %collective-permute-start = (bf16[48,2048]{1,0:T(8,128)(2,1)S(1)}, bf16[48,2048]{1,0:T(8,128)(2,1)S(1)}, u32[]{:S(2)}, u32[]{:S(2)}) collective-permute-start(bf16[48,2048]{1,0:T(8,128)(2,1)S(1)} %convert_element_type.9.own_panel), channel_id=1, source_target_pairs={{0,1},{1,0},{2,3},{3,2},{4,5},{5,4},{6,7},{7,6},{8,9},{9,8},{10,11... | collective-permute-start | bytes 589832 | tf_op jit(solution)/shard_map/gather/ppermute | solution.py:21
  2.2 9.0 %collective-permute-start.1 = (bf16[48,2048]{1,0:T(8,128)(2,1)S(1)}, bf16[48,2048]{1,0:T(8,128)(2,1)S(1)}, u32[]{:S(2)}, u32[]{:S(2)}) collective-permute-start(bf16[48,2048]{1,0:T(8,128)(2,1)S(1)} %convert_element_type.9.own_panel), channel_id=1, source_target_pairs={{0,2},{1,3},{2,0},{3,1},{4,6},{5,7},{6,4},{7,5},{8,10},{9,11},{10,... | collective-permute-start | bytes 589832 | tf_op jit(solution)/shard_map/gather/ppermute | solution.py:21
  4.7 11.2 %collective-permute-start.3 = (bf16[48,2048]{1,0:T(8,128)(2,1)S(1)}, bf16[48,2048]{1,0:T(8,128)(2,1)S(1)}, u32[]{:S(2)}, u32[]{:S(2)}) collective-permute-start(bf16[48,2048]{1,0:T(8,128)(2,1)S(1)} %convert_element_type.9.own_panel), channel_id=1, source_target_pairs={{0,4},{1,5},{2,6},{3,7},{4,0},{5,1},{6,2},{7,3},{8,12},{9,13},{10,... | collective-permute-start | bytes 589832 | tf_op jit(solution)/shard_map/gather/ppermute | solution.py:21
  6.3 9.7 %collective-permute-start.5 = (bf16[48,2048]{1,0:T(8,128)(2,1)S(1)}, bf16[48,2048]{1,0:T(8,128)(2,1)S(1)}, u32[]{:S(2)}, u32[]{:S(2)}) collective-permute-start(bf16[48,2048]{1,0:T(8,128)(2,1)S(1)} %convert_element_type.9.own_panel), channel_id=1, source_target_pairs={{0,6},{1,7},{2,4},{3,5},{4,2},{5,3},{6,0},{7,1},{8,14},{9,15},{10,... | collective-permute-start | bytes 589832 | tf_op jit(solution)/shard_map/gather/ppermute | solution.py:21
  11.2 6.0 %collective-permute-start.2 = (bf16[48,2048]{1,0:T(8,128)(2,1)S(1)}, bf16[48,2048]{1,0:T(8,128)(2,1)S(1)}, u32[]{:S(2)}, u32[]{:S(2)}) collective-permute-start(bf16[48,2048]{1,0:T(8,128)(2,1)S(1)} %gather.4.refs_0_), channel_id=1, source_target_pairs={{0,1},{1,0},{2,3},{3,2},{4,5},{5,4},{6,7},{7,6},{8,9},{9,8},{10,11... | collective-permute-start | bytes 589832 | tf_op jit(solution)/shard_map/gather/ppermute | solution.py:21
  15.9 1.4 %collective-permute-start.4 = (bf16[48,2048]{1,0:T(8,128)(2,1)S(1)}, bf16[48,2048]{1,0:T(8,128)(2,1)S(1)}, u32[]{:S(2)}, u32[]{:S(2)}) collective-permute-start(bf16[48,2048]{1,0:T(8,128)(2,1)S(1)} %gather.5.refs_1_), channel_id=1, source_target_pairs={{0,1},{1,0},{2,3},{3,2},{4,5},{5,4},{6,7},{7,6},{8,9},{9,8},{10,11... | collective-permute-start | bytes 589832 | tf_op jit(solution)/shard_map/gather/ppermute | solution.py:21
  15.9 1.7 %collective-permute-start.6 = (bf16[48,2048]{1,0:T(8,128)(2,1)S(1)}, bf16[48,2048]{1,0:T(8,128)(2,1)S(1)}, u32[]{:S(2)}, u32[]{:S(2)}) collective-permute-start(bf16[48,2048]{1,0:T(8,128)(2,1)S(1)} %gather.6.refs_2_), channel_id=1, source_target_pairs={{0,1},{1,0},{2,3},{3,2},{4,5},{5,4},{6,7},{7,6},{8,9},{9,8},{10,11... | collective-permute-start | bytes 589832 | tf_op jit(solution)/shard_map/gather/ppermute | solution.py:21
  17.6 9.4 %copy-start.1 = (f32[48,2048]{1,0:T(8,128)S(1)}, f32[48,2048]{1,0:T(8,128)}, u32[]{:S(2)}) copy-start(f32[48,2048]{1,0:T(8,128)} %current.3) | copy-start | bytes 1179652
  17.6 9.4 %copy-start.2 = (f32[48,2048]{1,0:T(8,128)S(1)}, f32[48,2048]{1,0:T(8,128)}, u32[]{:S(2)}) copy-start(f32[48,2048]{1,0:T(8,128)} %previous.1) | copy-start | bytes 1179652
  17.6 9.4 %copy-start.4 = (f32[48,48]{1,0:T(8,128)S(1)}, f32[48,48]{1,0:T(8,128)}, u32[]{:S(2)}) copy-start(f32[48,48]{1,0:T(8,128)} %coupling.1) | copy-start | bytes 27652
  17.7 9.4 %copy-start.5 = (f32[2048]{0:T(1024)S(1)}, f32[2048]{0:T(1024)}, u32[]{:S(2)}) copy-start(f32[2048]{0:T(1024)} %param.14) | copy-start | bytes 24580
  21.3 8.4 %collective-permute-start.9 = (bf16[48,2048]{1,0:T(8,128)(2,1)S(1)}, bf16[48,2048]{1,0:T(8,128)(2,1)S(1)}, u32[]{:S(2)}, u32[]{:S(2)}) collective-permute-start(bf16[48,2048]{1,0:T(8,128)(2,1)S(1)} %get-tuple-element.24), channel_id=1, source_target_pairs={{0,8},{24,16},{1,9},{25,17},{2,10},{26,18},{3,11},{27,19},{4,12},{... | collective-permute-start | bytes 589832 | tf_op jit(solution)/shard_map/late/ppermute | solution.py:429
  24.2 9.3 %collective-permute-start.7 = (bf16[48,2048]{1,0:T(8,128)(2,1)S(1)}, bf16[48,2048]{1,0:T(8,128)(2,1)S(1)}, u32[]{:S(2)}, u32[]{:S(2)}) collective-permute-start(bf16[48,2048]{1,0:T(8,128)(2,1)S(1)} %get-tuple-element.24), channel_id=1, source_target_pairs={{8,16},{16,8},{9,17},{17,9},{10,18},{18,10},{11,19},{19,11},{12,20... | collective-permute-start | bytes 589832 | tf_op jit(solution)/shard_map/late/ppermute | solution.py:430
  24.9 8.6 %collective-permute-start.8 = (bf16[48,2048]{1,0:T(8,128)(2,1)S(1)}, bf16[48,2048]{1,0:T(8,128)(2,1)S(1)}, u32[]{:S(2)}, u32[]{:S(2)}) collective-permute-start(bf16[48,2048]{1,0:T(8,128)(2,1)S(1)} %get-tuple-element.25), channel_id=1, source_target_pairs={{0,16},{24,8},{8,0},{16,24},{1,17},{25,9},{9,1},{17,25},{2,18},{26... | collective-permute-start | bytes 589832 | tf_op jit(solution)/shard_map/late/ppermute | solution.py:431
  27.0 14.1 %copy-start = (f32[8,48,2048]{2,1,0:T(8,128)S(1)}, f32[8,48,2048]{2,1,0:T(8,128)}, u32[]{:S(2)}) copy-start(f32[8,48,2048]{2,1,0:T(8,128)} %param.13) | copy-start | bytes 9437188
  27.0 14.1 %copy-start.3 = (f32[2048]{0:T(1024)S(1)}, f32[2048]{0:T(1024)}, u32[]{:S(2)}) copy-start(f32[2048]{0:T(1024)} %param.15) | copy-start | bytes 24580
  29.8 11.3 %collective-permute-start.10 = (bf16[48,2048]{1,0:T(8,128)(2,1)S(1)}, bf16[48,2048]{1,0:T(8,128)(2,1)S(1)}, u32[]{:S(2)}, u32[]{:S(2)}) collective-permute-start(bf16[48,2048]{1,0:T(8,128)(2,1)S(1)} %add_convert_fusion), channel_id=1, source_target_pairs={{0,8},{8,24},{24,16},{16,0},{1,9},{9,25},{25,17},{17,1},{2,10},{10... | collective-permute-start | bytes 589832 | tf_op jit(solution)/shard_map/late/ppermute | solution.py:433
  42.9 1.3 %collective-permute-start.11 = (f32[12,8,128]{2,1,0:T(8,128)S(1)}, f32[12,8,128]{2,1,0:T(8,128)S(1)}, u32[]{:S(2)}, u32[]{:S(2)}) collective-permute-start(f32[12,8,128]{2,1,0:T(8,128)S(1)} %get-tuple-element.28), channel_id=1, source_target_pairs={{0,1},{1,0},{2,3},{3,2},{4,5},{5,4},{6,7},{7,6},{8,9},{9,8},{10,11... | collective-permute-start | bytes 147464 | tf_op jit(solution)/shard_map/coefficients/ppermute | solution.py:21
  44.2 5.1 %collective-permute-start.14 = (f32[12,8,128]{2,1,0:T(8,128)S(1)}, f32[12,8,128]{2,1,0:T(8,128)S(1)}, u32[]{:S(2)}, u32[]{:S(2)}) collective-permute-start(f32[12,8,128]{2,1,0:T(8,128)S(1)} %add.46), channel_id=1, source_target_pairs={{0,6},{1,7},{2,4},{3,5},{4,2},{5,3},{6,0},{7,1},{8,14},{9,15},{10,... | collective-permute-start | bytes 147464 | tf_op jit(solution)/shard_map/coefficients/ppermute | solution.py:21
  46.3 4.1 %collective-permute-start.13 = (f32[12,8,128]{2,1,0:T(8,128)S(1)}, f32[12,8,128]{2,1,0:T(8,128)S(1)}, u32[]{:S(2)}, u32[]{:S(2)}) collective-permute-start(f32[12,8,128]{2,1,0:T(8,128)S(1)} %add.46), channel_id=1, source_target_pairs={{0,4},{1,5},{2,6},{3,7},{4,0},{5,1},{6,2},{7,3},{8,12},{9,13},{10,... | collective-permute-start | bytes 147464 | tf_op jit(solution)/shard_map/coefficients/ppermute | solution.py:21
  46.5 4.1 %collective-permute-start.12 = (f32[12,8,128]{2,1,0:T(8,128)S(1)}, f32[12,8,128]{2,1,0:T(8,128)S(1)}, u32[]{:S(2)}, u32[]{:S(2)}) collective-permute-start(f32[12,8,128]{2,1,0:T(8,128)S(1)} %add.46), channel_id=1, source_target_pairs={{0,2},{1,3},{2,0},{3,1},{4,6},{5,7},{6,4},{7,5},{8,10},{9,11},{10,... | collective-permute-start | bytes 147464 | tf_op jit(solution)/shard_map/coefficients/ppermute | solution.py:21
  50.7 6.2 %collective-permute-start.17 = (f32[12,8,128]{2,1,0:T(8,128)S(1)}, f32[12,8,128]{2,1,0:T(8,128)S(1)}, u32[]{:S(2)}, u32[]{:S(2)}) collective-permute-start(f32[12,8,128]{2,1,0:T(8,128)S(1)} %add_add_fusion.1), channel_id=1, source_target_pairs={{0,24},{8,16},{16,8},{24,0},{1,25},{9,17},{17,9},{25,1},{2,26},{10... | collective-permute-start | bytes 147464 | tf_op jit(solution)/shard_map/coefficients/ppermute | solution.py:21
  53.4 5.0 %collective-permute-start.16 = (f32[12,8,128]{2,1,0:T(8,128)S(1)}, f32[12,8,128]{2,1,0:T(8,128)S(1)}, u32[]{:S(2)}, u32[]{:S(2)}) collective-permute-start(f32[12,8,128]{2,1,0:T(8,128)S(1)} %add_add_fusion.1), channel_id=1, source_target_pairs={{0,16},{8,24},{16,0},{24,8},{1,17},{9,25},{17,1},{25,9},{2,18},{10... | collective-permute-start | bytes 147464 | tf_op jit(solution)/shard_map/coefficients/ppermute | solution.py:21
  53.4 5.0 %collective-permute-start.15 = (f32[12,8,128]{2,1,0:T(8,128)S(1)}, f32[12,8,128]{2,1,0:T(8,128)S(1)}, u32[]{:S(2)}, u32[]{:S(2)}) collective-permute-start(f32[12,8,128]{2,1,0:T(8,128)S(1)} %add_add_fusion.1), channel_id=1, source_target_pairs={{0,8},{8,0},{16,24},{24,16},{1,9},{9,1},{17,25},{25,17},{2,10},{10... | collective-permute-start | bytes 147464 | tf_op jit(solution)/shard_map/coefficients/ppermute | solution.py:21
  58.4 1.3 %collective-permute-start.18 = (f32[12,8,128]{2,1,0:T(8,128)S(1)}, f32[12,8,128]{2,1,0:T(8,128)S(1)}, u32[]{:S(2)}, u32[]{:S(2)}) collective-permute-start(f32[12,8,128]{2,1,0:T(8,128)S(1)} %add_add_fusion.mine), channel_id=1, source_target_pairs={{0,1},{1,0},{2,3},{3,2},{4,5},{5,4},{6,7},{7,6},{8,9},{9,8},{10,11... | collective-permute-start | bytes 147464 | tf_op jit(solution)/shard_map/coefficients/ppermute | solution.py:21
  61.7 1.2 %collective-permute-start.19 = (f32[24,128]{1,0:T(8,128)S(1)}, f32[24,128]{1,0:T(8,128)S(1)}, u32[]{:S(2)}, u32[]{:S(2)}) collective-permute-start(f32[24,128]{1,0:T(8,128)S(1)} %get-tuple-element.32), channel_id=1, source_target_pairs={{0,1},{1,0},{2,3},{3,2},{4,5},{5,4},{6,7},{7,6},{8,9},{9,8},{10,11... | collective-permute-start | bytes 36872 | tf_op jit(solution)/shard_map/gram/ppermute | solution.py:21
  62.9 4.6 %collective-permute-start.22 = (f32[24,128]{1,0:T(8,128)S(1)}, f32[24,128]{1,0:T(8,128)S(1)}, u32[]{:S(2)}, u32[]{:S(2)}) collective-permute-start(f32[24,128]{1,0:T(8,128)S(1)} %add.53), channel_id=1, source_target_pairs={{0,6},{1,7},{2,4},{3,5},{4,2},{5,3},{6,0},{7,1},{8,14},{9,15},{10,... | collective-permute-start | bytes 36872 | tf_op jit(solution)/shard_map/gram/ppermute | solution.py:21
  64.2 3.7 %collective-permute-start.21 = (f32[24,128]{1,0:T(8,128)S(1)}, f32[24,128]{1,0:T(8,128)S(1)}, u32[]{:S(2)}, u32[]{:S(2)}) collective-permute-start(f32[24,128]{1,0:T(8,128)S(1)} %add.53), channel_id=1, source_target_pairs={{0,4},{1,5},{2,6},{3,7},{4,0},{5,1},{6,2},{7,3},{8,12},{9,13},{10,... | collective-permute-start | bytes 36872 | tf_op jit(solution)/shard_map/gram/ppermute | solution.py:21
  65.5 3.7 %collective-permute-start.20 = (f32[24,128]{1,0:T(8,128)S(1)}, f32[24,128]{1,0:T(8,128)S(1)}, u32[]{:S(2)}, u32[]{:S(2)}) collective-permute-start(f32[24,128]{1,0:T(8,128)S(1)} %add.53), channel_id=1, source_target_pairs={{0,2},{1,3},{2,0},{3,1},{4,6},{5,7},{6,4},{7,5},{8,10},{9,11},{10,... | collective-permute-start | bytes 36872 | tf_op jit(solution)/shard_map/gram/ppermute | solution.py:21
  69.2 5.5 %collective-permute-start.25 = (f32[24,128]{1,0:T(8,128)S(1)}, f32[24,128]{1,0:T(8,128)S(1)}, u32[]{:S(2)}, u32[]{:S(2)}) collective-permute-start(f32[24,128]{1,0:T(8,128)S(1)} %add_add_fusion.3), channel_id=1, source_target_pairs={{0,24},{8,16},{16,8},{24,0},{1,25},{9,17},{17,9},{25,1},{2,26},{10... | collective-permute-start | bytes 36872 | tf_op jit(solution)/shard_map/gram/ppermute | solution.py:21
  71.2 4.6 %collective-permute-start.24 = (f32[24,128]{1,0:T(8,128)S(1)}, f32[24,128]{1,0:T(8,128)S(1)}, u32[]{:S(2)}, u32[]{:S(2)}) collective-permute-start(f32[24,128]{1,0:T(8,128)S(1)} %add_add_fusion.3), channel_id=1, source_target_pairs={{0,16},{8,24},{16,0},{24,8},{1,17},{9,25},{17,1},{25,9},{2,18},{10... | collective-permute-start | bytes 36872 | tf_op jit(solution)/shard_map/gram/ppermute | solution.py:21
  71.6 4.2 %collective-permute-start.23 = (f32[24,128]{1,0:T(8,128)S(1)}, f32[24,128]{1,0:T(8,128)S(1)}, u32[]{:S(2)}, u32[]{:S(2)}) collective-permute-start(f32[24,128]{1,0:T(8,128)S(1)} %add_add_fusion.3), channel_id=1, source_target_pairs={{0,8},{8,0},{16,24},{24,16},{1,9},{9,1},{17,25},{25,17},{2,10},{10... | collective-permute-start | bytes 36872 | tf_op jit(solution)/shard_map/gram/ppermute | solution.py:21

commit v9 on v8

--- a/solution.py
+++ b/solution.py
@@ -38,10 +38,10 @@
     return lax.dot_general(a, b, dims, preferred_element_type=jnp.float32)
 
 
-def dot_split(a, b, dims=(((1,), (0,)), ((), ()))):
+def dot_split(a, b_parts, dims=(((1,), (0,)), ((), ()))):
     rows = a.shape[0]
     a_high, a_low = split(a)
-    b_high, b_low = split(b)
+    b_high, b_low = b_parts
     both = mm(jnp.concatenate([a_high, a_low], axis=0), b_high, dims)
     return both[:rows] + both[rows:] + mm(a_high, b_low, dims)
 
@@ -204,11 +204,16 @@
     return [change.get(mask, mask) for mask in masks]
 
 
-def late_kernel(masks, place, plan, panel_buf, tiles, early, current, previous, coupling, diag, *refs):
-    sends, base, acc = refs[:-2], refs[-2], refs[-1]
+def late_kernel(masks, place, plan, panel_buf, tiles, early, *refs):
+    sends, acc = refs[:-1], refs[-1]
     for mask, send in zip(late_masks(masks, place), sends):
         late_part(mask, place, plan, tiles, early, panel_buf, acc, ())
         put(send, acc)
+
+
+def own_kernel(
+    place, plan, panel_buf, tiles, early, current, previous, coupling, diag, stored, base, basis_high, basis_low, acc
+):
     late_part(0, place, plan, tiles, early, panel_buf, acc, ())
     put(base, acc)
     base[...] += diag[...] * current[...] - jnp.dot(
@@ -217,6 +222,9 @@
         precision=lax.Precision.HIGHEST,
         preferred_element_type=jnp.float32,
     )
+    width = current.shape[0]
+    basis_high[:width], basis_low[:width] = split(current[...])
+    basis_high[width:], basis_low[width:] = split(stored[...])
 
 
 def late_part(mask, place, plan, tiles, early, panel_buf, acc, copies):
@@ -237,14 +245,13 @@
 
 def coefficient_kernel(cells, received_count, place, base, *refs):
     received = refs[:received_count]
-    mass, current, stored, recurrence, keep, give, halves = refs[received_count:]
+    mass, basis_high, basis_low, recurrence, keep, give, halves = refs[received_count:]
     total = base[...]
     for ref in received:
         total = total + ref[...].astype(jnp.float32)
     recurrence[...] = total
     weighted = total * (mass[...] * (1.0 / cells))
-    basis = jnp.concatenate([current[...], stored[...]], axis=0)
-    coef = dot_split(weighted, basis, NT)
+    coef = dot_split(weighted, (basis_high[...], basis_low[...]), NT)
     spare = -coef.shape[1] % LANES
     coef = jnp.concatenate([coef, jnp.zeros((coef.shape[0], spare), jnp.float32)], axis=1)
     halves[...] = jnp.zeros_like(halves)
@@ -256,7 +263,7 @@
 
 
 def residual_kernel(
-    cells, place, mine, other, recurrence, mass, current, stored, residual, coef_out, gram, halves, packed
+    cells, place, mine, other, recurrence, mass, basis_high, basis_low, residual, coef_out, gram, halves, packed
 ):
     width = recurrence.shape[0]
     core = place[1] & 1
@@ -265,12 +272,11 @@
     for p, (q, k) in enumerate(blocks(packed.shape)):
         packed[q : q + 8, k : k + LANES] = halves[p // halves.shape[1], p % halves.shape[1]]
     coef = packed[...]
-    basis = jnp.concatenate([current[...], stored[...]], axis=0)
-    coef = coef[:, : basis.shape[0]]
+    coef = coef[:, : basis_high.shape[0]]
     coef_out[...] = coef
-    value = recurrence[...] - dot_split(coef, basis)
+    value = recurrence[...] - dot_split(coef, (basis_high[...], basis_low[...]))
     residual[...] = value
-    local = dot_split(value * (mass[...] * (1.0 / cells)), value, NT)
+    local = dot_split(value * (mass[...] * (1.0 / cells)), split(value), NT)
     half = width // 2
     gram[...] = jnp.zeros_like(gram)
     gram[:, :width] = local[:half]
@@ -402,38 +408,46 @@
 
     with jax.named_scope("late"):
         relay = row_devs == 4
-        first_masks = [3, "x"] if relay else [row_devs - 1]
-        last_masks = ["y"] if relay else list(range(row_devs - 2, 0, -1))
+        others = ["x", "y"] if relay else list(range(row_devs - 2, 0, -1))
         part = jax.ShapeDtypeStruct((width, slab_len), bf16)
-        *firsts, gathered = pl.pallas_call(
-            functools.partial(first_late_kernel, first_masks, odd),
-            out_shape=[part] * len(first_masks) + [pltpu.VMEM(panel_shape, bf16)],
+        first, gathered = pl.pallas_call(
+            functools.partial(first_late_kernel, [row_devs - 1], odd),
+            out_shape=[part, pltpu.VMEM(panel_shape, bf16)],
             in_specs=smem(2) + anywhere * len(odd) + vmem(3),
-            out_specs=vmem(len(first_masks) + 1),
+            out_specs=vmem(2),
             scratch_shapes=[part_acc, pltpu.SemaphoreType.DMA((len(odd),))],
-            input_output_aliases={4 + len(odd): len(first_masks)},
+            input_output_aliases={4 + len(odd): 1},
             compiler_params=limit(8),
             cost_estimate=cost(width),
         )(place, plan, *[panels[m] for m in odd], held, early, gathered)
-        lasts = [slab] if relay else [part] * len(last_masks)
-        *lasts, base = pl.pallas_call(
-            functools.partial(late_kernel, last_masks),
-            out_shape=lasts + [slab],
-            in_specs=smem(2) + vmem(7),
-            out_specs=vmem(len(lasts) + 1),
+        parts = pl.pallas_call(
+            functools.partial(late_kernel, others),
+            out_shape=[part, slab] if relay else [part] * len(others),
+            in_specs=smem(2) + vmem(3),
+            out_specs=vmem(len(others)),
             scratch_shapes=[part_acc],
             compiler_params=limit(8),
             cost_estimate=cost(width),
-        )(place, plan, gathered, held, early, current_block, previous_block, previous_coupling, diag)
+        )(place, plan, gathered, held, early)
         if relay:
-            passing = lax.ppermute(firsts[0], "row", [(0, 1), (3, 2)])
-            received = [lax.ppermute(firsts[0], "row", [(1, 2), (2, 1)])]
-            received.append(lax.ppermute(firsts[1], "row", [(0, 2), (3, 1), (1, 0), (2, 3)]))
-            joined = (lasts[0] + passing.astype(f32)).astype(bf16)
+            passing = lax.ppermute(first, "row", [(0, 1), (3, 2)])
+            received = [lax.ppermute(first, "row", [(1, 2), (2, 1)])]
+            received.append(lax.ppermute(parts[0], "row", [(0, 2), (3, 1), (1, 0), (2, 3)]))
+            joined = (parts[1] + passing.astype(f32)).astype(bf16)
             received.append(lax.ppermute(joined, "row", [(0, 1), (1, 3), (3, 2), (2, 0)]))
         else:
-            received = [swap(firsts[0], "row", first_masks[0])]
-            received += [swap(last, "row", m) for m, last in zip(last_masks, lasts)]
+            received = [swap(first, "row", row_devs - 1)]
+            received += [swap(part, "row", m) for m, part in zip(others, parts)]
+        basis_part = pltpu.VMEM(((stored_count + 1) * width, slab_len), bf16)
+        base, *basis = pl.pallas_call(
+            own_kernel,
+            out_shape=[slab, basis_part, basis_part],
+            in_specs=smem(2) + vmem(8),
+            out_specs=vmem(3),
+            scratch_shapes=[part_acc],
+            compiler_params=limit(8),
+            cost_estimate=cost(width),
+        )(place, plan, gathered, held, early, current_block, previous_block, previous_coupling, diag, stored)
 
     basis_rows = (stored_count + 1) * width
     padded = (width, -(-basis_rows // LANES) * LANES)
@@ -445,8 +459,8 @@
             in_specs=smem(1) + vmem(len(received) + 4),
             out_specs=vmem(3),
             scratch_shapes=[pltpu.VMEM((2,) + half, f32)],
-            compiler_params=limit(24),
-        )(place, base, *received, mass, current_block, stored)
+            compiler_params=limit(12),
+        )(place, base, *received, mass, *basis)
         mine = keep + swap(give, "col", 1)
         mine = total(total(mine, "col", 2), "row", 1)
         other = swap(mine, "col", 1)
@@ -462,8 +476,8 @@
             in_specs=smem(1) + vmem(6),
             out_specs=vmem(3),
             scratch_shapes=[pltpu.VMEM((2,) + half, f32), pltpu.VMEM(padded, f32)],
-            compiler_params=limit(24),
-        )(place, mine, other, recurrence, mass, current_block, stored)
+            compiler_params=limit(12),
+        )(place, mine, other, recurrence, mass, *basis)
         coefficients = coef.T.reshape(stored_count + 1, width, width)
 
     with jax.named_scope("gram"):

time: 76.6 us -> 79.8 us (1.042)
  Pallas kernels: 15 us -> 16.8 us
  waiting for transfers between devices: 26.4 us -> 27.4 us
    ppermute x22, waiting for transfers between devices: 17.1 us -> 20.9 us  [swap(): return lax.ppermute(value, axis, [(i, i ^ mask) for i in range(count)])]
    ppermute x1, waiting for transfers between devices: 7.6 us -> 6.19 us  [local(): lax.ppermute(joined, 'row', [(0, 1), (1, 3), (3, 2), (2, 0)])]
    ppermute x3, waiting for transfers between devices: 1.69 us -> 0.33 us  [the longest x1 0.33 us: local(): lax.ppermute(parts[0], 'row', [(0, 2), (3, 1), (1, 0), (2, 3)])]
    pallas_call x2 -> x3, Pallas kernels: 6.32 us -> 7.48 us  [the longest x1 3.17 us: local(): pl.pallas_call(own_kernel, out_shape=[slab, basis_part, basis_part], in_s...]
    ppermute x3, starting transfers between devices: 5.69 us -> 6.79 us  [the longest x1 3.99 us: local(): passing = lax.ppermute(first, 'row', [(0, 1), (3, 2)])]
    ppermute x22, starting transfers between devices: 23.2 us -> 22.2 us  [swap(): return lax.ppermute(value, axis, [(i, i ^ mask) for i in range(count)])]
  transfers between devices with their start and end apart: 26 -> 26, of which waited for: 18 -> 17; matrix products, arithmetic and copies ran while one was open for 1% -> 1% of each run, Pallas kernels for 10% -> 14%
where the time goes in v9:
time: 79.8 us; the launch traced here: 79.3 us
  starting transfers between devices  30.9 us (39%)
  waiting for transfers between devices  27.4 us (34%)
  Pallas kernels  16.8 us (21%)
  other arithmetic  1.8 us (2%)
  between operations  1.48 us (2%)
  local copies, waits for them, and re-layouts  0.93 us (1%)
    ppermute x22, starting transfers between devices, swap(): return lax.ppermute(value, axis, [(i, i ^ mask) for i in range(count)])  22.2 us
    ppermute x22, waiting for transfers between devices, swap(): return lax.ppermute(value, axis, [(i, i ^ mask) for i in range(count)])  20.9 us
    ppermute x1, waiting for transfers between devices, local(): lax.ppermute(joined, 'row', [(0, 1), (1, 3), (3, 2), (2, 0)])  6.19 us
    pallas_call x1, Pallas kernels, local(): pl.pallas_call(functools.partial(early_kernel, row_devs, col_devs, slab_t...  4.78 us
    ppermute x1, starting transfers between devices, local(): passing = lax.ppermute(first, 'row', [(0, 1), (3, 2)])  3.99 us
    pallas_call x1, Pallas kernels, local(): pl.pallas_call(own_kernel, out_shape=[slab, basis_part, basis_part], in_s...  3.17 us
    pallas_call x1, Pallas kernels, local(): pl.pallas_call(functools.partial(late_kernel, others), out_shape=[part, s...  2.24 us
    ppermute x1, starting transfers between devices, local(): lax.ppermute(parts[0], 'row', [(0, 2), (3, 1), (1, 0), (2, 3)])  2.12 us
  transfers between devices with their start and end apart: 26, of which 17 were waited for; matrix products, arithmetic and copies ran while one was open for 1% of the time, Pallas kernels for 14%

profile of v9, /device:TPU:0, one launch (start us, length us, event | category | flops | bytes accessed | tf_op | source)
XLA Modules:
  0.0 79.3 jit_solution(5677901190379193583)
XLA Ops:
  0.6 1.0 %convert_element_type.9.own_panel = bf16[48,2048]{1,0:T(8,128)(2,1)S(1)} convert(f32[48,2048]{1,0:T(8,128)} %current.1) | non-fusion elementwise | flops 98304 | bytes 589824 | tf_op jit(solution)/shard_map/gather/convert_element_type | solution.py:354
  1.7 0.5 collective-permute-start
  2.2 2.6 %collective-permute-start.3 = (bf16[48,2048]{1,0:T(8,128)(2,1)S(1)}, bf16[48,2048]{1,0:T(8,128)(2,1)S(1)}, u32[]{:S(2)}, u32[]{:S(2)}) collective-permute-start(bf16[48,2048]{1,0:T(8,128)(2,1)S(1)} %convert_element_type.9.own_panel), channel_id=1, source_target_pairs={{0,4},{1,5},{2,6},{3,7},{4,0},{5,1},{6,2},{7,3},{8,12},{9,13},{10,... | collective-permute-start | bytes 589832 | tf_op jit(solution)/shard_map/gather/ppermute | solution.py:21
  4.8 1.4 %collective-permute-start.5 = (bf16[48,2048]{1,0:T(8,128)(2,1)S(1)}, bf16[48,2048]{1,0:T(8,128)(2,1)S(1)}, u32[]{:S(2)}, u32[]{:S(2)}) collective-permute-start(bf16[48,2048]{1,0:T(8,128)(2,1)S(1)} %convert_element_type.9.own_panel), channel_id=1, source_target_pairs={{0,6},{1,7},{2,4},{3,5},{4,2},{5,3},{6,0},{7,1},{8,14},{9,15},{10,... | collective-permute-start | bytes 589832 | tf_op jit(solution)/shard_map/gather/ppermute | solution.py:21
  6.2 0.1 collective-permute-start.1
  7.0 0.1 pad_add_fusion.place
  7.0 0.0 collective-permute-done.near_panel
  7.0 4.8 %early.1 = (s32[1,896]{1,0:T(1,128)S(1)}, bf16[512,128,128]{2,1,0:T(8,128)(2,1)S(1)}, f32[65,48,128]{2,1,0:T(8,128)S(1)}, bf16[9,48,2048]{2,1,0:T(8,128)(2,1)S(1)}) custom-call(s32[2]{0:T(128)S(1)} %pad_add_fusion.place, s32[1]{0:T(128)S(6)} %copy.25.counts, s32[1,512]{1,0:T(1,128)} %bitcast.15, s32[1,512]{1,0:T(1,128)} %bitcast.16, ...), custom_call_target="tpu_custom_call" | custom-call | flops 805306368 | bytes 16777216 | tf_op jit(solution)/shard_map/early/pallas_call | solution.py:363
  11.8 2.7 %collective-permute-done.3.value = bf16[48,2048]{1,0:T(8,128)(2,1)S(1)} collective-permute-done((bf16[48,2048]{1,0:T(8,128)(2,1)S(1)}, bf16[48,2048]{1,0:T(8,128)(2,1)S(1)}, u32[]{:S(2)}, u32[]{:S(2)}) %collective-permute-start.3) | collective-permute-done | bytes 196640 | tf_op jit(solution)/shard_map/gather/ppermute | solution.py:21
  14.5 0.0 collective-permute-start.4
  14.5 0.0 collective-permute-done.5.value
  14.5 0.5 collective-permute-start.6
  15.0 0.8 collective-permute-done.1.value
  15.7 0.0 collective-permute-start.2
  15.7 0.8 gather.7.refs_5_
  16.5 0.0 collective-permute-done.4.refs_1_
  16.5 0.0 collective-permute-done.6.refs_2_
  16.6 0.6 collective-permute-done.2.refs_0_
  17.2 2.1 %late.3 = (bf16[48,2048]{1,0:T(8,128)(2,1)S(1)}, bf16[9,48,2048]{2,1,0:T(8,128)(2,1)S(1)}) custom-call(s32[2]{0:T(128)S(1)} %pad_add_fusion.place, s32[1,896]{1,0:T(1,128)S(1)} %get-tuple-element.20.plan, bf16[48,2048]{1,0:T(8,128)(2,1)S(1)} %collective-permute-done.2.refs_0_, ...), custom_call_target="tpu_custom_call", output_to_operand_aliasing={{1}: (7, {})} | custom-call | flops 48 | bytes 1 | tf_op jit(solution)/shard_map/late/pallas_call | solution.py:413
  19.3 4.0 %collective-permute-start.9 = (bf16[48,2048]{1,0:T(8,128)(2,1)S(1)}, bf16[48,2048]{1,0:T(8,128)(2,1)S(1)}, u32[]{:S(2)}, u32[]{:S(2)}) collective-permute-start(bf16[48,2048]{1,0:T(8,128)(2,1)S(1)} %get-tuple-element.26), channel_id=1, source_target_pairs={{0,8},{24,16},{1,9},{25,17},{2,10},{26,18},{3,11},{27,19},{4,12},{... | collective-permute-start | bytes 589832 | tf_op jit(solution)/shard_map/late/ppermute | solution.py:433
  23.3 0.7 collective-permute-start.7
  23.9 0.0 copy-start
  24.0 0.0 copy-start.1
  24.0 0.0 copy-start.2
  24.0 0.0 copy-start.4
  24.0 0.0 copy-start.5
  24.0 2.2 %late.5 = (bf16[48,2048]{1,0:T(8,128)(2,1)S(1)}, f32[48,2048]{1,0:T(8,128)S(1)}) custom-call(s32[2]{0:T(128)S(1)} %pad_add_fusion.place, s32[1,896]{1,0:T(1,128)S(1)} %get-tuple-element.20.plan, bf16[9,48,2048]{2,1,0:T(8,128)(2,1)S(1)} %get-tuple-element.24.panel_buf, bf16[512,128,128]{2,1,0:T(8,128)(2,1)S(1)} %get-tuple-element.22.refs_3_.tiles, ...), custom_call_target="tpu_custom_call" | custom-call | flops 48 | bytes 1 | tf_op jit(solution)/shard_map/late/pallas_call | solution.py:423
  26.2 2.1 %collective-permute-start.8 = (bf16[48,2048]{1,0:T(8,128)(2,1)S(1)}, bf16[48,2048]{1,0:T(8,128)(2,1)S(1)}, u32[]{:S(2)}, u32[]{:S(2)}) collective-permute-start(bf16[48,2048]{1,0:T(8,128)(2,1)S(1)} %get-tuple-element.27), channel_id=1, source_target_pairs={{0,16},{24,8},{8,0},{16,24},{1,17},{25,9},{9,1},{17,25},{2,18},{26... | collective-permute-start | bytes 589832 | tf_op jit(solution)/shard_map/late/ppermute | solution.py:435
  28.4 1.9 %collective-permute-start.10 = (bf16[48,2048]{1,0:T(8,128)(2,1)S(1)}, bf16[48,2048]{1,0:T(8,128)(2,1)S(1)}, u32[]{:S(2)}, u32[]{:S(2)}) collective-permute-start(bf16[48,2048]{1,0:T(8,128)(2,1)S(1)} %add_convert_fusion), channel_id=1, source_target_pairs={{0,8},{8,24},{24,16},{16,0},{1,9},{9,25},{25,17},{17,1},{2,10},{10... | collective-permute-start | bytes 589832 | tf_op jit(solution)/shard_map/late/ppermute | solution.py:437
  30.3 0.0 copy-start.3
  30.3 3.2 %late.4 = (f32[48,2048]{1,0:T(8,128)S(1)}, bf16[432,2048]{1,0:T(8,128)(2,1)S(1)}, bf16[432,2048]{1,0:T(8,128)(2,1)S(1)}) custom-call(s32[2]{0:T(128)S(1)} %pad_add_fusion.place, s32[1,896]{1,0:T(1,128)S(1)} %get-tuple-element.20.plan, bf16[9,48,2048]{2,1,0:T(8,128)(2,1)S(1)} %get-tuple-element.24.panel_buf, ...), custom_call_target="tpu_custom_call" | custom-call | flops 48 | bytes 1 | tf_op jit(solution)/shard_map/late/pallas_call | solution.py:442
  33.5 0.3 collective-permute-done.8.refs_1_
  33.8 6.2 %collective-permute-done.10.refs_2_ = bf16[48,2048]{1,0:T(8,128)(2,1)S(1)} collective-permute-done((bf16[48,2048]{1,0:T(8,128)(2,1)S(1)}, bf16[48,2048]{1,0:T(8,128)(2,1)S(1)}, u32[]{:S(2)}, u32[]{:S(2)}) %collective-permute-start.10) | collective-permute-done | bytes 196640 | tf_op jit(solution)/shard_map/late/ppermute | solution.py:437
  40.0 1.7 %coefficients.1 = (f32[48,2048]{1,0:T(8,128)S(1)}, f32[12,8,128]{2,1,0:T(8,128)S(1)}, f32[12,8,128]{2,1,0:T(8,128)S(1)}) custom-call(s32[2]{0:T(128)S(1)} %pad_add_fusion.place, f32[48,2048]{1,0:T(8,128)S(1)} %get-tuple-element.25.base, bf16[48,2048]{1,0:T(8,128)(2,1)S(1)} %collective-permute-done.7.refs_0_, ...), custom_call_target="tpu_custom_call" | custom-call | tf_op jit(solution)/shard_map/coefficients/pallas_call | solution.py:456
  41.7 0.1 collective-permute-start.11
  41.8 1.2 %collective-permute-done.11 = f32[12,8,128]{2,1,0:T(8,128)S(1)} collective-permute-done((f32[12,8,128]{2,1,0:T(8,128)S(1)}, f32[12,8,128]{2,1,0:T(8,128)S(1)}, u32[]{:S(2)}, u32[]{:S(2)}) %collective-permute-start.11) | collective-permute-done | bytes 49184 | tf_op jit(solution)/shard_map/coefficients/ppermute | solution.py:21
  43.0 2.9 %collective-permute-start.12 = (f32[12,8,128]{2,1,0:T(8,128)S(1)}, f32[12,8,128]{2,1,0:T(8,128)S(1)}, u32[]{:S(2)}, u32[]{:S(2)}) collective-permute-start(f32[12,8,128]{2,1,0:T(8,128)S(1)} %add.46), channel_id=1, source_target_pairs={{0,2},{1,3},{2,0},{3,1},{4,6},{5,7},{6,4},{7,5},{8,10},{9,11},{10,... | collective-permute-start | bytes 147464 | tf_op jit(solution)/shard_map/coefficients/ppermute | solution.py:21
  45.9 0.8 collective-permute-start.13
  46.7 0.8 collective-permute-start.14
  47.4 0.5 collective-permute-done.12
  48.0 2.5 %collective-permute-done.13 = f32[12,8,128]{2,1,0:T(8,128)S(1)} collective-permute-done((f32[12,8,128]{2,1,0:T(8,128)S(1)}, f32[12,8,128]{2,1,0:T(8,128)S(1)}, u32[]{:S(2)}, u32[]{:S(2)}) %collective-permute-start.13) | collective-permute-done | bytes 49184 | tf_op jit(solution)/shard_map/coefficients/ppermute | solution.py:21
  50.5 1.1 %collective-permute-done.14 = f32[12,8,128]{2,1,0:T(8,128)S(1)} collective-permute-done((f32[12,8,128]{2,1,0:T(8,128)S(1)}, f32[12,8,128]{2,1,0:T(8,128)S(1)}, u32[]{:S(2)}, u32[]{:S(2)}) %collective-permute-start.14) | collective-permute-done | bytes 49184 | tf_op jit(solution)/shard_map/coefficients/ppermute | solution.py:21
  51.7 0.1 collective-permute-start.15
  51.7 1.8 %collective-permute-start.16 = (f32[12,8,128]{2,1,0:T(8,128)S(1)}, f32[12,8,128]{2,1,0:T(8,128)S(1)}, u32[]{:S(2)}, u32[]{:S(2)}) collective-permute-start(f32[12,8,128]{2,1,0:T(8,128)S(1)} %add_add_fusion.1), channel_id=1, source_target_pairs={{0,16},{8,24},{16,0},{24,8},{1,17},{9,25},{17,1},{25,9},{2,18},{10... | collective-permute-start | bytes 147464 | tf_op jit(solution)/shard_map/coefficients/ppermute | solution.py:21
  53.5 2.6 %collective-permute-start.17 = (f32[12,8,128]{2,1,0:T(8,128)S(1)}, f32[12,8,128]{2,1,0:T(8,128)S(1)}, u32[]{:S(2)}, u32[]{:S(2)}) collective-permute-start(f32[12,8,128]{2,1,0:T(8,128)S(1)} %add_add_fusion.1), channel_id=1, source_target_pairs={{0,24},{8,16},{16,8},{24,0},{1,25},{9,17},{17,9},{25,1},{2,26},{10... | collective-permute-start | bytes 147464 | tf_op jit(solution)/shard_map/coefficients/ppermute | solution.py:21
  56.1 0.9 %collective-permute-done.16 = f32[12,8,128]{2,1,0:T(8,128)S(1)} collective-permute-done((f32[12,8,128]{2,1,0:T(8,128)S(1)}, f32[12,8,128]{2,1,0:T(8,128)S(1)}, u32[]{:S(2)}, u32[]{:S(2)}) %collective-permute-start.16) | collective-permute-done | bytes 49184 | tf_op jit(solution)/shard_map/coefficients/ppermute | solution.py:21
  57.0 2.4 %collective-permute-done.17 = f32[12,8,128]{2,1,0:T(8,128)S(1)} collective-permute-done((f32[12,8,128]{2,1,0:T(8,128)S(1)}, f32[12,8,128]{2,1,0:T(8,128)S(1)}, u32[]{:S(2)}, u32[]{:S(2)}) %collective-permute-start.17) | collective-permute-done | bytes 49184 | tf_op jit(solution)/shard_map/coefficients/ppermute | solution.py:21
  59.4 0.1 collective-permute-start.18
  59.5 1.2 %collective-permute-done.18.other = f32[12,8,128]{2,1,0:T(8,128)S(1)} collective-permute-done((f32[12,8,128]{2,1,0:T(8,128)S(1)}, f32[12,8,128]{2,1,0:T(8,128)S(1)}, u32[]{:S(2)}, u32[]{:S(2)}) %collective-permute-start.18) | collective-permute-done | bytes 49184 | tf_op jit(solution)/shard_map/coefficients/ppermute | solution.py:21
  60.7 2.1 %residual.1 = (f32[48,2048]{1,0:T(8,128)}, f32[48,432]{1,0:T(8,128)S(1)}, f32[24,128]{1,0:T(8,128)S(1)}) custom-call(s32[2]{0:T(128)S(1)} %pad_add_fusion.place, f32[12,8,128]{2,1,0:T(8,128)S(1)} %add_add_fusion.mine, f32[12,8,128]{2,1,0:T(8,128)S(1)} %collective-permute-done.18.other, f32[48,2048]{1,0:T(8,128)S(1)} %get-tuple-element.33.recurrence, ...), custom_call_target="tpu_custom_call" | custom-call | tf_op jit(solution)/shard_map/residual/pallas_call | solution.py:469
  62.8 0.2 collective-permute-start.19
  63.0 1.0 %collective-permute-done.19 = f32[24,128]{1,0:T(8,128)S(1)} collective-permute-done((f32[24,128]{1,0:T(8,128)S(1)}, f32[24,128]{1,0:T(8,128)S(1)}, u32[]{:S(2)}, u32[]{:S(2)}) %collective-permute-start.19) | collective-permute-done | bytes 12320 | tf_op jit(solution)/shard_map/gram/ppermute | solution.py:21
  64.0 0.8 %collective-permute-start.20 = (f32[24,128]{1,0:T(8,128)S(1)}, f32[24,128]{1,0:T(8,128)S(1)}, u32[]{:S(2)}, u32[]{:S(2)}) collective-permute-start(f32[24,128]{1,0:T(8,128)S(1)} %add.53), channel_id=1, source_target_pairs={{0,2},{1,3},{2,0},{3,1},{4,6},{5,7},{6,4},{7,5},{8,10},{9,11},{10,... | collective-permute-start | bytes 36872 | tf_op jit(solution)/shard_map/gram/ppermute | solution.py:21
  64.8 0.2 collective-permute-start.21
  65.0 2.4 %collective-permute-start.22 = (f32[24,128]{1,0:T(8,128)S(1)}, f32[24,128]{1,0:T(8,128)S(1)}, u32[]{:S(2)}, u32[]{:S(2)}) collective-permute-start(f32[24,128]{1,0:T(8,128)S(1)} %add.53), channel_id=1, source_target_pairs={{0,6},{1,7},{2,4},{3,5},{4,2},{5,3},{6,0},{7,1},{8,14},{9,15},{10,... | collective-permute-start | bytes 36872 | tf_op jit(solution)/shard_map/gram/ppermute | solution.py:21
  67.5 0.2 collective-permute-done.20
  67.7 0.9 %collective-permute-done.21 = f32[24,128]{1,0:T(8,128)S(1)} collective-permute-done((f32[24,128]{1,0:T(8,128)S(1)}, f32[24,128]{1,0:T(8,128)S(1)}, u32[]{:S(2)}, u32[]{:S(2)}) %collective-permute-start.21) | collective-permute-done | bytes 12320 | tf_op jit(solution)/shard_map/gram/ppermute | solution.py:21
  68.6 1.0 %collective-permute-done.22 = f32[24,128]{1,0:T(8,128)S(1)} collective-permute-done((f32[24,128]{1,0:T(8,128)S(1)}, f32[24,128]{1,0:T(8,128)S(1)}, u32[]{:S(2)}, u32[]{:S(2)}) %collective-permute-start.22) | collective-permute-done | bytes 12320 | tf_op jit(solution)/shard_map/gram/ppermute | solution.py:21
  69.6 3.4 %collective-permute-start.24 = (f32[24,128]{1,0:T(8,128)S(1)}, f32[24,128]{1,0:T(8,128)S(1)}, u32[]{:S(2)}, u32[]{:S(2)}) collective-permute-start(f32[24,128]{1,0:T(8,128)S(1)} %add_add_fusion.3), channel_id=1, source_target_pairs={{0,16},{8,24},{16,0},{24,8},{1,17},{9,25},{17,1},{25,9},{2,18},{10... | collective-permute-start | bytes 36872 | tf_op jit(solution)/shard_map/gram/ppermute | solution.py:21
  73.1 1.0 %collective-permute-start.25 = (f32[24,128]{1,0:T(8,128)S(1)}, f32[24,128]{1,0:T(8,128)S(1)}, u32[]{:S(2)}, u32[]{:S(2)}) collective-permute-start(f32[24,128]{1,0:T(8,128)S(1)} %add_add_fusion.3), channel_id=1, source_target_pairs={{0,24},{8,16},{16,8},{24,0},{1,25},{9,17},{17,9},{25,1},{2,26},{10... | collective-permute-start | bytes 36872 | tf_op jit(solution)/shard_map/gram/ppermute | solution.py:21
  74.0 0.8 %copy.19 = f32[432,48]{1,0:T(8,128)} copy(f32[432,48]{0,1:T(8,128)S(1)} %bitcast.10) | data formatting | bytes 165888 | tf_op jit(solution)/shard_map/residual/transpose | solution.py:481
  74.9 3.7 %collective-permute-done.25 = f32[24,128]{1,0:T(8,128)S(1)} collective-permute-done((f32[24,128]{1,0:T(8,128)S(1)}, f32[24,128]{1,0:T(8,128)S(1)}, u32[]{:S(2)}, u32[]{:S(2)}) %collective-permute-start.25) | collective-permute-done | bytes 12320 | tf_op jit(solution)/shard_map/gram/ppermute | solution.py:21
  78.6 0.1 fusion
  78.6 0.6 pad_maximum_fusion
  (22 shorter events, 0.1 us)
Async XLA Ops:
  1.7 5.4 %collective-permute-start = (bf16[48,2048]{1,0:T(8,128)(2,1)S(1)}, bf16[48,2048]{1,0:T(8,128)(2,1)S(1)}, u32[]{:S(2)}, u32[]{:S(2)}) collective-permute-start(bf16[48,2048]{1,0:T(8,128)(2,1)S(1)} %convert_element_type.9.own_panel), channel_id=1, source_target_pairs={{0,1},{1,0},{2,3},{3,2},{4,5},{5,4},{6,7},{7,6},{8,9},{9,8},{10,11... | collective-permute-start | bytes 589832 | tf_op jit(solution)/shard_map/gather/ppermute | solution.py:21
  2.2 12.3 %collective-permute-start.3 = (bf16[48,2048]{1,0:T(8,128)(2,1)S(1)}, bf16[48,2048]{1,0:T(8,128)(2,1)S(1)}, u32[]{:S(2)}, u32[]{:S(2)}) collective-permute-start(bf16[48,2048]{1,0:T(8,128)(2,1)S(1)} %convert_element_type.9.own_panel), channel_id=1, source_target_pairs={{0,4},{1,5},{2,6},{3,7},{4,0},{5,1},{6,2},{7,3},{8,12},{9,13},{10,... | collective-permute-start | bytes 589832 | tf_op jit(solution)/shard_map/gather/ppermute | solution.py:21
  4.8 9.7 %collective-permute-start.5 = (bf16[48,2048]{1,0:T(8,128)(2,1)S(1)}, bf16[48,2048]{1,0:T(8,128)(2,1)S(1)}, u32[]{:S(2)}, u32[]{:S(2)}) collective-permute-start(bf16[48,2048]{1,0:T(8,128)(2,1)S(1)} %convert_element_type.9.own_panel), channel_id=1, source_target_pairs={{0,6},{1,7},{2,4},{3,5},{4,2},{5,3},{6,0},{7,1},{8,14},{9,15},{10,... | collective-permute-start | bytes 589832 | tf_op jit(solution)/shard_map/gather/ppermute | solution.py:21
  6.2 9.5 %collective-permute-start.1 = (bf16[48,2048]{1,0:T(8,128)(2,1)S(1)}, bf16[48,2048]{1,0:T(8,128)(2,1)S(1)}, u32[]{:S(2)}, u32[]{:S(2)}) collective-permute-start(bf16[48,2048]{1,0:T(8,128)(2,1)S(1)} %convert_element_type.9.own_panel), channel_id=1, source_target_pairs={{0,2},{1,3},{2,0},{3,1},{4,6},{5,7},{6,4},{7,5},{8,10},{9,11},{10,... | collective-permute-start | bytes 589832 | tf_op jit(solution)/shard_map/gather/ppermute | solution.py:21
  14.5 2.1 %collective-permute-start.4 = (bf16[48,2048]{1,0:T(8,128)(2,1)S(1)}, bf16[48,2048]{1,0:T(8,128)(2,1)S(1)}, u32[]{:S(2)}, u32[]{:S(2)}) collective-permute-start(bf16[48,2048]{1,0:T(8,128)(2,1)S(1)} %gather.5.refs_1_), channel_id=1, source_target_pairs={{0,1},{1,0},{2,3},{3,2},{4,5},{5,4},{6,7},{7,6},{8,9},{9,8},{10,11... | collective-permute-start | bytes 589832 | tf_op jit(solution)/shard_map/gather/ppermute | solution.py:21
  14.5 2.1 %collective-permute-start.6 = (bf16[48,2048]{1,0:T(8,128)(2,1)S(1)}, bf16[48,2048]{1,0:T(8,128)(2,1)S(1)}, u32[]{:S(2)}, u32[]{:S(2)}) collective-permute-start(bf16[48,2048]{1,0:T(8,128)(2,1)S(1)} %gather.6.refs_2_), channel_id=1, source_target_pairs={{0,1},{1,0},{2,3},{3,2},{4,5},{5,4},{6,7},{7,6},{8,9},{9,8},{10,11... | collective-permute-start | bytes 589832 | tf_op jit(solution)/shard_map/gather/ppermute | solution.py:21
  15.7 1.4 %collective-permute-start.2 = (bf16[48,2048]{1,0:T(8,128)(2,1)S(1)}, bf16[48,2048]{1,0:T(8,128)(2,1)S(1)}, u32[]{:S(2)}, u32[]{:S(2)}) collective-permute-start(bf16[48,2048]{1,0:T(8,128)(2,1)S(1)} %gather.4.refs_0_), channel_id=1, source_target_pairs={{0,1},{1,0},{2,3},{3,2},{4,5},{5,4},{6,7},{7,6},{8,9},{9,8},{10,11... | collective-permute-start | bytes 589832 | tf_op jit(solution)/shard_map/gather/ppermute | solution.py:21
  19.3 9.1 %collective-permute-start.9 = (bf16[48,2048]{1,0:T(8,128)(2,1)S(1)}, bf16[48,2048]{1,0:T(8,128)(2,1)S(1)}, u32[]{:S(2)}, u32[]{:S(2)}) collective-permute-start(bf16[48,2048]{1,0:T(8,128)(2,1)S(1)} %get-tuple-element.26), channel_id=1, source_target_pairs={{0,8},{24,16},{1,9},{25,17},{2,10},{26,18},{3,11},{27,19},{4,12},{... | collective-permute-start | bytes 589832 | tf_op jit(solution)/shard_map/late/ppermute | solution.py:433
  23.3 10.6 %collective-permute-start.7 = (bf16[48,2048]{1,0:T(8,128)(2,1)S(1)}, bf16[48,2048]{1,0:T(8,128)(2,1)S(1)}, u32[]{:S(2)}, u32[]{:S(2)}) collective-permute-start(bf16[48,2048]{1,0:T(8,128)(2,1)S(1)} %get-tuple-element.26), channel_id=1, source_target_pairs={{8,16},{16,8},{9,17},{17,9},{10,18},{18,10},{11,19},{19,11},{12,20... | collective-permute-start | bytes 589832 | tf_op jit(solution)/shard_map/late/ppermute | solution.py:434
  23.9 6.3 %copy-start = (f32[8,48,2048]{2,1,0:T(8,128)S(1)}, f32[8,48,2048]{2,1,0:T(8,128)}, u32[]{:S(2)}) copy-start(f32[8,48,2048]{2,1,0:T(8,128)} %param.13) | copy-start | bytes 9437188
  24.0 6.3 %copy-start.1 = (f32[48,2048]{1,0:T(8,128)S(1)}, f32[48,2048]{1,0:T(8,128)}, u32[]{:S(2)}) copy-start(f32[48,2048]{1,0:T(8,128)} %current.1) | copy-start | bytes 1179652
  24.0 6.3 %copy-start.2 = (f32[48,2048]{1,0:T(8,128)S(1)}, f32[48,2048]{1,0:T(8,128)}, u32[]{:S(2)}) copy-start(f32[48,2048]{1,0:T(8,128)} %previous.1) | copy-start | bytes 1179652
  24.0 6.3 %copy-start.4 = (f32[48,48]{1,0:T(8,128)S(1)}, f32[48,48]{1,0:T(8,128)}, u32[]{:S(2)}) copy-start(f32[48,48]{1,0:T(8,128)} %coupling.1) | copy-start | bytes 27652
  24.0 6.3 %copy-start.5 = (f32[2048]{0:T(1024)S(1)}, f32[2048]{0:T(1024)}, u32[]{:S(2)}) copy-start(f32[2048]{0:T(1024)} %param.14) | copy-start | bytes 24580
  26.2 7.6 %collective-permute-start.8 = (bf16[48,2048]{1,0:T(8,128)(2,1)S(1)}, bf16[48,2048]{1,0:T(8,128)(2,1)S(1)}, u32[]{:S(2)}, u32[]{:S(2)}) collective-permute-start(bf16[48,2048]{1,0:T(8,128)(2,1)S(1)} %get-tuple-element.27), channel_id=1, source_target_pairs={{0,16},{24,8},{8,0},{16,24},{1,17},{25,9},{9,1},{17,25},{2,18},{26... | collective-permute-start | bytes 589832 | tf_op jit(solution)/shard_map/late/ppermute | solution.py:435
  28.4 11.6 %collective-permute-start.10 = (bf16[48,2048]{1,0:T(8,128)(2,1)S(1)}, bf16[48,2048]{1,0:T(8,128)(2,1)S(1)}, u32[]{:S(2)}, u32[]{:S(2)}) collective-permute-start(bf16[48,2048]{1,0:T(8,128)(2,1)S(1)} %add_convert_fusion), channel_id=1, source_target_pairs={{0,8},{8,24},{24,16},{16,0},{1,9},{9,25},{25,17},{17,1},{2,10},{10... | collective-permute-start | bytes 589832 | tf_op jit(solution)/shard_map/late/ppermute | solution.py:437
  30.3 9.7 %copy-start.3 = (f32[2048]{0:T(1024)S(1)}, f32[2048]{0:T(1024)}, u32[]{:S(2)}) copy-start(f32[2048]{0:T(1024)} %param.15) | copy-start | bytes 24580
  41.7 1.3 %collective-permute-start.11 = (f32[12,8,128]{2,1,0:T(8,128)S(1)}, f32[12,8,128]{2,1,0:T(8,128)S(1)}, u32[]{:S(2)}, u32[]{:S(2)}) collective-permute-start(f32[12,8,128]{2,1,0:T(8,128)S(1)} %get-tuple-element.32), channel_id=1, source_target_pairs={{0,1},{1,0},{2,3},{3,2},{4,5},{5,4},{6,7},{7,6},{8,9},{9,8},{10,11... | collective-permute-start | bytes 147464 | tf_op jit(solution)/shard_map/coefficients/ppermute | solution.py:21
  43.0 4.9 %collective-permute-start.12 = (f32[12,8,128]{2,1,0:T(8,128)S(1)}, f32[12,8,128]{2,1,0:T(8,128)S(1)}, u32[]{:S(2)}, u32[]{:S(2)}) collective-permute-start(f32[12,8,128]{2,1,0:T(8,128)S(1)} %add.46), channel_id=1, source_target_pairs={{0,2},{1,3},{2,0},{3,1},{4,6},{5,7},{6,4},{7,5},{8,10},{9,11},{10,... | collective-permute-start | bytes 147464 | tf_op jit(solution)/shard_map/coefficients/ppermute | solution.py:21
  45.9 4.6 %collective-permute-start.13 = (f32[12,8,128]{2,1,0:T(8,128)S(1)}, f32[12,8,128]{2,1,0:T(8,128)S(1)}, u32[]{:S(2)}, u32[]{:S(2)}) collective-permute-start(f32[12,8,128]{2,1,0:T(8,128)S(1)} %add.46), channel_id=1, source_target_pairs={{0,4},{1,5},{2,6},{3,7},{4,0},{5,1},{6,2},{7,3},{8,12},{9,13},{10,... | collective-permute-start | bytes 147464 | tf_op jit(solution)/shard_map/coefficients/ppermute | solution.py:21
  46.7 5.0 %collective-permute-start.14 = (f32[12,8,128]{2,1,0:T(8,128)S(1)}, f32[12,8,128]{2,1,0:T(8,128)S(1)}, u32[]{:S(2)}, u32[]{:S(2)}) collective-permute-start(f32[12,8,128]{2,1,0:T(8,128)S(1)} %add.46), channel_id=1, source_target_pairs={{0,6},{1,7},{2,4},{3,5},{4,2},{5,3},{6,0},{7,1},{8,14},{9,15},{10,... | collective-permute-start | bytes 147464 | tf_op jit(solution)/shard_map/coefficients/ppermute | solution.py:21
  51.7 4.5 %collective-permute-start.15 = (f32[12,8,128]{2,1,0:T(8,128)S(1)}, f32[12,8,128]{2,1,0:T(8,128)S(1)}, u32[]{:S(2)}, u32[]{:S(2)}) collective-permute-start(f32[12,8,128]{2,1,0:T(8,128)S(1)} %add_add_fusion.1), channel_id=1, source_target_pairs={{0,8},{8,0},{16,24},{24,16},{1,9},{9,1},{17,25},{25,17},{2,10},{10... | collective-permute-start | bytes 147464 | tf_op jit(solution)/shard_map/coefficients/ppermute | solution.py:21
  51.7 5.3 %collective-permute-start.16 = (f32[12,8,128]{2,1,0:T(8,128)S(1)}, f32[12,8,128]{2,1,0:T(8,128)S(1)}, u32[]{:S(2)}, u32[]{:S(2)}) collective-permute-start(f32[12,8,128]{2,1,0:T(8,128)S(1)} %add_add_fusion.1), channel_id=1, source_target_pairs={{0,16},{8,24},{16,0},{24,8},{1,17},{9,25},{17,1},{25,9},{2,18},{10... | collective-permute-start | bytes 147464 | tf_op jit(solution)/shard_map/coefficients/ppermute | solution.py:21
  53.5 5.9 %collective-permute-start.17 = (f32[12,8,128]{2,1,0:T(8,128)S(1)}, f32[12,8,128]{2,1,0:T(8,128)S(1)}, u32[]{:S(2)}, u32[]{:S(2)}) collective-permute-start(f32[12,8,128]{2,1,0:T(8,128)S(1)} %add_add_fusion.1), channel_id=1, source_target_pairs={{0,24},{8,16},{16,8},{24,0},{1,25},{9,17},{17,9},{25,1},{2,26},{10... | collective-permute-start | bytes 147464 | tf_op jit(solution)/shard_map/coefficients/ppermute | solution.py:21
  59.4 1.3 %collective-permute-start.18 = (f32[12,8,128]{2,1,0:T(8,128)S(1)}, f32[12,8,128]{2,1,0:T(8,128)S(1)}, u32[]{:S(2)}, u32[]{:S(2)}) collective-permute-start(f32[12,8,128]{2,1,0:T(8,128)S(1)} %add_add_fusion.mine), channel_id=1, source_target_pairs={{0,1},{1,0},{2,3},{3,2},{4,5},{5,4},{6,7},{7,6},{8,9},{9,8},{10,11... | collective-permute-start | bytes 147464 | tf_op jit(solution)/shard_map/coefficients/ppermute | solution.py:21
  62.8 1.2 %collective-permute-start.19 = (f32[24,128]{1,0:T(8,128)S(1)}, f32[24,128]{1,0:T(8,128)S(1)}, u32[]{:S(2)}, u32[]{:S(2)}) collective-permute-start(f32[24,128]{1,0:T(8,128)S(1)} %get-tuple-element.36), channel_id=1, source_target_pairs={{0,1},{1,0},{2,3},{3,2},{4,5},{5,4},{6,7},{7,6},{8,9},{9,8},{10,11... | collective-permute-start | bytes 36872 | tf_op jit(solution)/shard_map/gram/ppermute | solution.py:21
  64.0 3.7 %collective-permute-start.20 = (f32[24,128]{1,0:T(8,128)S(1)}, f32[24,128]{1,0:T(8,128)S(1)}, u32[]{:S(2)}, u32[]{:S(2)}) collective-permute-start(f32[24,128]{1,0:T(8,128)S(1)} %add.53), channel_id=1, source_target_pairs={{0,2},{1,3},{2,0},{3,1},{4,6},{5,7},{6,4},{7,5},{8,10},{9,11},{10,... | collective-permute-start | bytes 36872 | tf_op jit(solution)/shard_map/gram/ppermute | solution.py:21
  64.8 3.8 %collective-permute-start.21 = (f32[24,128]{1,0:T(8,128)S(1)}, f32[24,128]{1,0:T(8,128)S(1)}, u32[]{:S(2)}, u32[]{:S(2)}) collective-permute-start(f32[24,128]{1,0:T(8,128)S(1)} %add.53), channel_id=1, source_target_pairs={{0,4},{1,5},{2,6},{3,7},{4,0},{5,1},{6,2},{7,3},{8,12},{9,13},{10,... | collective-permute-start | bytes 36872 | tf_op jit(solution)/shard_map/gram/ppermute | solution.py:21
  65.0 4.6 %collective-permute-start.22 = (f32[24,128]{1,0:T(8,128)S(1)}, f32[24,128]{1,0:T(8,128)S(1)}, u32[]{:S(2)}, u32[]{:S(2)}) collective-permute-start(f32[24,128]{1,0:T(8,128)S(1)} %add.53), channel_id=1, source_target_pairs={{0,6},{1,7},{2,4},{3,5},{4,2},{5,3},{6,0},{7,1},{8,14},{9,15},{10,... | collective-permute-start | bytes 36872 | tf_op jit(solution)/shard_map/gram/ppermute | solution.py:21
  69.6 5.2 %collective-permute-start.23 = (f32[24,128]{1,0:T(8,128)S(1)}, f32[24,128]{1,0:T(8,128)S(1)}, u32[]{:S(2)}, u32[]{:S(2)}) collective-permute-start(f32[24,128]{1,0:T(8,128)S(1)} %add_add_fusion.3), channel_id=1, source_target_pairs={{0,8},{8,0},{16,24},{24,16},{1,9},{9,1},{17,25},{25,17},{2,10},{10... | collective-permute-start | bytes 36872 | tf_op jit(solution)/shard_map/gram/ppermute | solution.py:21
  69.6 5.2 %collective-permute-start.24 = (f32[24,128]{1,0:T(8,128)S(1)}, f32[24,128]{1,0:T(8,128)S(1)}, u32[]{:S(2)}, u32[]{:S(2)}) collective-permute-start(f32[24,128]{1,0:T(8,128)S(1)} %add_add_fusion.3), channel_id=1, source_target_pairs={{0,16},{8,24},{16,0},{24,8},{1,17},{9,25},{17,1},{25,9},{2,18},{10... | collective-permute-start | bytes 36872 | tf_op jit(solution)/shard_map/gram/ppermute | solution.py:21
  73.1 5.5 %collective-permute-start.25 = (f32[24,128]{1,0:T(8,128)S(1)}, f32[24,128]{1,0:T(8,128)S(1)}, u32[]{:S(2)}, u32[]{:S(2)}) collective-permute-start(f32[24,128]{1,0:T(8,128)S(1)} %add_add_fusion.3), channel_id=1, source_target_pairs={{0,24},{8,16},{16,8},{24,0},{1,25},{9,17},{17,9},{25,1},{2,26},{10... | collective-permute-start | bytes 36872 | tf_op jit(solution)/shard_map/gram/ppermute | solution.py:21

commit v10 on v8

--- a/solution.py
+++ b/solution.py
@@ -192,23 +192,21 @@
     sends = refs[len(odd) + 3 : -3]
     panel_buf, acc, sem = refs[-3:]
     copies = load_panels(panels, panel_buf, sem)
-    for mask, send in zip(late_masks(masks, place), sends):
+    for mask, send in zip(masks, sends):
         late_part(mask, place, plan, tiles, early, panel_buf, acc, copies)
         put(send, acc)
         copies = ()
 
 
-def late_masks(masks, place):
-    inner = (place[0] == 1) | (place[0] == 2)
-    change = {"x": jnp.where(inner, 1, 2), "y": jnp.where(inner, 2, 1)}
-    return [change.get(mask, mask) for mask in masks]
-
-
-def late_kernel(masks, place, plan, panel_buf, tiles, early, current, previous, coupling, diag, *refs):
-    sends, base, acc = refs[:-2], refs[-2], refs[-1]
-    for mask, send in zip(late_masks(masks, place), sends):
-        late_part(mask, place, plan, tiles, early, panel_buf, acc, ())
+def late_kernel(masks, place, plan, panel_buf, tiles, early, *refs):
+    sends, acc = refs[:-1], refs[-1]
+    for i, (mask, send) in enumerate(zip(masks, sends)):
+        if i == 0 or mask != masks[i - 1]:
+            late_part(mask, place, plan, tiles, early, panel_buf, acc, ())
         put(send, acc)
+
+
+def own_kernel(place, plan, panel_buf, tiles, early, current, previous, coupling, diag, base, acc):
     late_part(0, place, plan, tiles, early, panel_buf, acc, ())
     put(base, acc)
     base[...] += diag[...] * current[...] - jnp.dot(
@@ -235,12 +233,15 @@
         out[:, s * LANES : (s + 1) * LANES] = acc[s].astype(out.dtype)
 
 
-def coefficient_kernel(cells, received_count, place, base, *refs):
+def coefficient_kernel(cells, received_count, relay, place, base, *refs):
     received = refs[:received_count]
     mass, current, stored, recurrence, keep, give, halves = refs[received_count:]
     total = base[...]
-    for ref in received:
-        total = total + ref[...].astype(jnp.float32)
+    for i, ref in enumerate(received):
+        value = ref[...].astype(jnp.float32)
+        if relay and i == 0:
+            value = jnp.where((place[0] == 1) | (place[0] == 2), 0.0, value)
+        total = total + value
     recurrence[...] = total
     weighted = total * (mass[...] * (1.0 / cells))
     basis = jnp.concatenate([current[...], stored[...]], axis=0)
@@ -402,45 +403,56 @@
 
     with jax.named_scope("late"):
         relay = row_devs == 4
-        first_masks = [3, "x"] if relay else [row_devs - 1]
-        last_masks = ["y"] if relay else list(range(row_devs - 2, 0, -1))
+        first_mask = 2 if relay else row_devs - 1
+        masks = [3, 3, 1] if relay else list(range(row_devs - 2, 0, -1))
         part = jax.ShapeDtypeStruct((width, slab_len), bf16)
-        *firsts, gathered = pl.pallas_call(
-            functools.partial(first_late_kernel, first_masks, odd),
-            out_shape=[part] * len(first_masks) + [pltpu.VMEM(panel_shape, bf16)],
+        first, gathered = pl.pallas_call(
+            functools.partial(first_late_kernel, [first_mask], odd),
+            out_shape=[part, pltpu.VMEM(panel_shape, bf16)],
             in_specs=smem(2) + anywhere * len(odd) + vmem(3),
-            out_specs=vmem(len(first_masks) + 1),
+            out_specs=vmem(2),
             scratch_shapes=[part_acc, pltpu.SemaphoreType.DMA((len(odd),))],
-            input_output_aliases={4 + len(odd): len(first_masks)},
+            input_output_aliases={4 + len(odd): 1},
             compiler_params=limit(8),
             cost_estimate=cost(width),
         )(place, plan, *[panels[m] for m in odd], held, early, gathered)
-        lasts = [slab] if relay else [part] * len(last_masks)
-        *lasts, base = pl.pallas_call(
-            functools.partial(late_kernel, last_masks),
-            out_shape=lasts + [slab],
+        parts = pl.pallas_call(
+            functools.partial(late_kernel, masks),
+            out_shape=[part, slab, part] if relay else [part] * len(masks),
+            in_specs=smem(2) + vmem(3),
+            out_specs=vmem(len(masks)),
+            scratch_shapes=[part_acc],
+            compiler_params=limit(8),
+            cost_estimate=cost(width),
+        )(place, plan, gathered, held, early)
+        if relay:
+            first = lax.ppermute(first, "row", [(0, 1), (3, 2), (1, 3), (2, 0)])
+            joined = (parts[1] + first.astype(f32)).astype(bf16)
+            received = [
+                first,
+                lax.ppermute(parts[0], "row", [(0, 3), (3, 0)]),
+                lax.ppermute(joined, "row", [(1, 2), (2, 1)]),
+                swap(parts[2], "row", 1),
+            ]
+        else:
+            received = [swap(first, "row", first_mask)]
+            received += [swap(part, "row", m) for m, part in zip(masks, parts)]
+        base = pl.pallas_call(
+            own_kernel,
+            out_shape=slab,
             in_specs=smem(2) + vmem(7),
-            out_specs=vmem(len(lasts) + 1),
+            out_specs=vmem(1)[0],
             scratch_shapes=[part_acc],
             compiler_params=limit(8),
             cost_estimate=cost(width),
         )(place, plan, gathered, held, early, current_block, previous_block, previous_coupling, diag)
-        if relay:
-            passing = lax.ppermute(firsts[0], "row", [(0, 1), (3, 2)])
-            received = [lax.ppermute(firsts[0], "row", [(1, 2), (2, 1)])]
-            received.append(lax.ppermute(firsts[1], "row", [(0, 2), (3, 1), (1, 0), (2, 3)]))
-            joined = (lasts[0] + passing.astype(f32)).astype(bf16)
-            received.append(lax.ppermute(joined, "row", [(0, 1), (1, 3), (3, 2), (2, 0)]))
-        else:
-            received = [swap(firsts[0], "row", first_masks[0])]
-            received += [swap(last, "row", m) for m, last in zip(last_masks, lasts)]
 
     basis_rows = (stored_count + 1) * width
     padded = (width, -(-basis_rows // LANES) * LANES)
     half = (-(-len(blocks(padded)) // 2), 8, LANES)
     with jax.named_scope("coefficients"):
         recurrence, keep, give = pl.pallas_call(
-            functools.partial(coefficient_kernel, cells, len(received)),
+            functools.partial(coefficient_kernel, cells, len(received), relay),
             out_shape=[slab] + [jax.ShapeDtypeStruct(half, f32)] * 2,
             in_specs=smem(1) + vmem(len(received) + 4),
             out_specs=vmem(3),

time: 76.6 us -> 75.6 us (0.987)
  starting transfers between devices: 30.9 us -> 28.1 us
  Pallas kernels: 15 us -> 17 us
    ppermute x22 -> x23, waiting for transfers between devices: 17.1 us -> 21.9 us  [swap(): return lax.ppermute(value, axis, [(i, i ^ mask) for i in range(count)])]
    ppermute x4 -> x3, waiting for transfers between devices: 9.29 us -> 4.86 us  [the longest x1 4.85 us: local(): lax.ppermute(parts[0], 'row', [(0, 3), (3, 0)])]
    ppermute x4 -> x3, starting transfers between devices: 7.74 us -> 6 us  [the longest x1 4 us: local(): lax.ppermute(parts[0], 'row', [(0, 3), (3, 0)])]
    ppermute x22 -> x23, starting transfers between devices: 23.2 us -> 22.1 us  [swap(): return lax.ppermute(value, axis, [(i, i ^ mask) for i in range(count)])]
    pallas_call x2 -> x3, Pallas kernels: 6.32 us -> 7.26 us  [the longest x1 3.48 us: local(): pl.pallas_call(functools.partial(late_kernel, masks), out_shape=[part, sl...]
    pallas_call x1, Pallas kernels: 4.15 us -> 5.08 us  [local(): pl.pallas_call(functools.partial(early_kernel, row_devs, col_devs, slab_t...]
  transfers between devices with their start and end apart: 26 -> 26, of which waited for: 18 -> 17; matrix products, arithmetic and copies ran while one was open for 1% -> 1% of each run, Pallas kernels for 10% -> 15%
where the time goes in v10:
time: 75.6 us; the launch traced here: 76 us
  starting transfers between devices  28.1 us (37%)
  waiting for transfers between devices  26.7 us (35%)
  Pallas kernels  17 us (22%)
  other arithmetic  1.81 us (2%)
  between operations  1.5 us (2%)
  local copies, waits for them, and re-layouts  0.92 us (1%)
    ppermute x23, starting transfers between devices, swap(): return lax.ppermute(value, axis, [(i, i ^ mask) for i in range(count)])  22.1 us
    ppermute x23, waiting for transfers between devices, swap(): return lax.ppermute(value, axis, [(i, i ^ mask) for i in range(count)])  21.9 us
    pallas_call x1, Pallas kernels, local(): pl.pallas_call(functools.partial(early_kernel, row_devs, col_devs, slab_t...  5.08 us
    ppermute x1, waiting for transfers between devices, local(): lax.ppermute(parts[0], 'row', [(0, 3), (3, 0)])  4.85 us
    ppermute x1, starting transfers between devices, local(): lax.ppermute(parts[0], 'row', [(0, 3), (3, 0)])  4 us
    pallas_call x1, Pallas kernels, local(): pl.pallas_call(functools.partial(late_kernel, masks), out_shape=[part, sl...  3.48 us
    pallas_call x1, Pallas kernels, local(): pl.pallas_call(functools.partial(residual_kernel, cells), out_shape=[slab...  2.1 us
    pallas_call x1, Pallas kernels, local(): pl.pallas_call(functools.partial(first_late_kernel, [first_mask], odd), o...  2.07 us
  transfers between devices with their start and end apart: 26, of which 17 were waited for; matrix products, arithmetic and copies ran while one was open for 1% of the time, Pallas kernels for 15%

profile of v10, /device:TPU:0, one launch (start us, length us, event | category | flops | bytes accessed | tf_op | source)
XLA Modules:
  0.0 76.0 jit_solution(18315574590836265656)
XLA Ops:
  0.6 1.0 %convert_element_type.9.own_panel = bf16[48,2048]{1,0:T(8,128)(2,1)S(1)} convert(f32[48,2048]{1,0:T(8,128)} %current.3) | non-fusion elementwise | flops 98304 | bytes 589824 | tf_op jit(solution)/shard_map/gather/convert_element_type | solution.py:349
  1.7 0.5 collective-permute-start
  2.2 2.6 %collective-permute-start.1 = (bf16[48,2048]{1,0:T(8,128)(2,1)S(1)}, bf16[48,2048]{1,0:T(8,128)(2,1)S(1)}, u32[]{:S(2)}, u32[]{:S(2)}) collective-permute-start(bf16[48,2048]{1,0:T(8,128)(2,1)S(1)} %convert_element_type.9.own_panel), channel_id=1, source_target_pairs={{0,2},{1,3},{2,0},{3,1},{4,6},{5,7},{6,4},{7,5},{8,10},{9,11},{10,... | collective-permute-start | bytes 589832 | tf_op jit(solution)/shard_map/gather/ppermute | solution.py:21
  4.7 1.5 %collective-permute-start.3 = (bf16[48,2048]{1,0:T(8,128)(2,1)S(1)}, bf16[48,2048]{1,0:T(8,128)(2,1)S(1)}, u32[]{:S(2)}, u32[]{:S(2)}) collective-permute-start(bf16[48,2048]{1,0:T(8,128)(2,1)S(1)} %convert_element_type.9.own_panel), channel_id=1, source_target_pairs={{0,4},{1,5},{2,6},{3,7},{4,0},{5,1},{6,2},{7,3},{8,12},{9,13},{10,... | collective-permute-start | bytes 589832 | tf_op jit(solution)/shard_map/gather/ppermute | solution.py:21
  6.3 0.0 collective-permute-start.5
  6.9 0.1 pad_add_fusion.place
  7.0 0.0 collective-permute-done.near_panel
  7.0 5.1 %early.1 = (s32[1,896]{1,0:T(1,128)S(1)}, bf16[512,128,128]{2,1,0:T(8,128)(2,1)S(1)}, f32[65,48,128]{2,1,0:T(8,128)S(1)}, bf16[9,48,2048]{2,1,0:T(8,128)(2,1)S(1)}) custom-call(s32[2]{0:T(128)S(1)} %pad_add_fusion.place, s32[1]{0:T(128)S(6)} %copy.25.counts, s32[1,512]{1,0:T(1,128)} %bitcast.16, s32[1,512]{1,0:T(1,128)} %bitcast.17, ...), custom_call_target="tpu_custom_call" | custom-call | flops 805306368 | bytes 16777216 | tf_op jit(solution)/shard_map/early/pallas_call | solution.py:358
  12.1 0.0 collective-permute-done.1.value
  12.1 0.1 collective-permute-start.2
  12.2 3.7 %collective-permute-done.3.value = bf16[48,2048]{1,0:T(8,128)(2,1)S(1)} collective-permute-done((bf16[48,2048]{1,0:T(8,128)(2,1)S(1)}, bf16[48,2048]{1,0:T(8,128)(2,1)S(1)}, u32[]{:S(2)}, u32[]{:S(2)}) %collective-permute-start.3) | collective-permute-done | bytes 196640 | tf_op jit(solution)/shard_map/gather/ppermute | solution.py:21
  15.9 0.0 collective-permute-start.4
  15.9 0.0 collective-permute-done.5.value
  15.9 0.5 collective-permute-start.6
  16.4 0.8 gather.7.refs_5_
  17.2 0.0 collective-permute-done.2.refs_0_
  17.2 0.2 collective-permute-done.4.refs_1_
  17.4 0.3 collective-permute-done.6.refs_2_
  17.6 2.1 %late.3 = (bf16[48,2048]{1,0:T(8,128)(2,1)S(1)}, bf16[9,48,2048]{2,1,0:T(8,128)(2,1)S(1)}) custom-call(s32[2]{0:T(128)S(1)} %pad_add_fusion.place, s32[1,896]{1,0:T(1,128)S(1)} %get-tuple-element.18.plan, bf16[48,2048]{1,0:T(8,128)(2,1)S(1)} %collective-permute-done.2.refs_0_, ...), custom_call_target="tpu_custom_call", output_to_operand_aliasing={{1}: (7, {})} | custom-call | flops 48 | bytes 1 | tf_op jit(solution)/shard_map/late/pallas_call | solution.py:409
  19.7 1.3 %collective-permute-start.7 = (bf16[48,2048]{1,0:T(8,128)(2,1)S(1)}, bf16[48,2048]{1,0:T(8,128)(2,1)S(1)}, u32[]{:S(2)}, u32[]{:S(2)}) collective-permute-start(bf16[48,2048]{1,0:T(8,128)(2,1)S(1)} %get-tuple-element.23), channel_id=1, source_target_pairs={{0,8},{24,16},{8,24},{16,0},{1,9},{25,17},{9,25},{17,1},{2,10},{26... | collective-permute-start | bytes 589832 | tf_op jit(solution)/shard_map/late/ppermute | solution.py:429
  21.1 3.5 %late.5 = (bf16[48,2048]{1,0:T(8,128)(2,1)S(1)}, f32[48,2048]{1,0:T(8,128)S(1)}, bf16[48,2048]{1,0:T(8,128)(2,1)S(1)}) custom-call(s32[2]{0:T(128)S(1)} %pad_add_fusion.place, s32[1,896]{1,0:T(1,128)S(1)} %get-tuple-element.18.plan, bf16[9,48,2048]{2,1,0:T(8,128)(2,1)S(1)} %get-tuple-element.22.panel_buf, ...), custom_call_target="tpu_custom_call" | custom-call | flops 48 | bytes 1 | tf_op jit(solution)/shard_map/late/pallas_call | solution.py:419
  24.5 4.0 %collective-permute-start.8 = (bf16[48,2048]{1,0:T(8,128)(2,1)S(1)}, bf16[48,2048]{1,0:T(8,128)(2,1)S(1)}, u32[]{:S(2)}, u32[]{:S(2)}) collective-permute-start(bf16[48,2048]{1,0:T(8,128)(2,1)S(1)} %get-tuple-element.24), channel_id=1, source_target_pairs={{0,24},{24,0},{1,25},{25,1},{2,26},{26,2},{3,27},{27,3},{4,28},{28... | collective-permute-start | bytes 589832 | tf_op jit(solution)/shard_map/late/ppermute | solution.py:433
  28.5 0.1 collective-permute-start.10
  28.6 0.0 collective-permute-done.7.refs_0_
  28.7 0.7 collective-permute-start.9
  29.4 0.0 copy-start
  29.4 0.0 copy-start.3
  29.4 1.7 %late.4.base = f32[48,2048]{1,0:T(8,128)S(1)} custom-call(s32[2]{0:T(128)S(1)} %pad_add_fusion.place, s32[1,896]{1,0:T(1,128)S(1)} %get-tuple-element.18.plan, bf16[9,48,2048]{2,1,0:T(8,128)(2,1)S(1)} %get-tuple-element.22.panel_buf, bf16[512,128,128]{2,1,0:T(8,128)(2,1)S(1)} %get-tuple-element.20.refs_3_.tiles, ...), custom_call_target="tpu_custom_call" | custom-call | flops 48 | bytes 1 | tf_op jit(solution)/shard_map/late/pallas_call | solution.py:440
  31.2 4.9 %collective-permute-done.8.refs_1_ = bf16[48,2048]{1,0:T(8,128)(2,1)S(1)} collective-permute-done((bf16[48,2048]{1,0:T(8,128)(2,1)S(1)}, bf16[48,2048]{1,0:T(8,128)(2,1)S(1)}, u32[]{:S(2)}, u32[]{:S(2)}) %collective-permute-start.8) | collective-permute-done | bytes 196640 | tf_op jit(solution)/shard_map/late/ppermute | solution.py:433
  36.0 3.2 %collective-permute-done.10.refs_3_ = bf16[48,2048]{1,0:T(8,128)(2,1)S(1)} collective-permute-done((bf16[48,2048]{1,0:T(8,128)(2,1)S(1)}, bf16[48,2048]{1,0:T(8,128)(2,1)S(1)}, u32[]{:S(2)}, u32[]{:S(2)}) %collective-permute-start.10) | collective-permute-done | bytes 196640 | tf_op jit(solution)/shard_map/late/ppermute | solution.py:21
  39.2 0.0 collective-permute-done.9.refs_2_
  39.2 1.8 %coefficients.1 = (f32[48,2048]{1,0:T(8,128)S(1)}, f32[12,8,128]{2,1,0:T(8,128)S(1)}, f32[12,8,128]{2,1,0:T(8,128)S(1)}) custom-call(s32[2]{0:T(128)S(1)} %pad_add_fusion.place, f32[48,2048]{1,0:T(8,128)S(1)} %late.4.base, bf16[48,2048]{1,0:T(8,128)(2,1)S(1)} %collective-permute-done.7.refs_0_, bf16[48,2048]{1,0:T(8,128)(2,1)S(1)} %collective-permute-done.8.refs_1_, ...), custom_call_target="tpu_custom_call" | custom-call | tf_op jit(solution)/shard_map/coefficients/pallas_call | solution.py:454
  41.0 0.2 collective-permute-start.11
  41.2 1.1 %collective-permute-done.11 = f32[12,8,128]{2,1,0:T(8,128)S(1)} collective-permute-done((f32[12,8,128]{2,1,0:T(8,128)S(1)}, f32[12,8,128]{2,1,0:T(8,128)S(1)}, u32[]{:S(2)}, u32[]{:S(2)}) %collective-permute-start.11) | collective-permute-done | bytes 49184 | tf_op jit(solution)/shard_map/coefficients/ppermute | solution.py:21
  42.3 3.4 %collective-permute-start.14 = (f32[12,8,128]{2,1,0:T(8,128)S(1)}, f32[12,8,128]{2,1,0:T(8,128)S(1)}, u32[]{:S(2)}, u32[]{:S(2)}) collective-permute-start(f32[12,8,128]{2,1,0:T(8,128)S(1)} %add.46), channel_id=1, source_target_pairs={{0,6},{1,7},{2,4},{3,5},{4,2},{5,3},{6,0},{7,1},{8,14},{9,15},{10,... | collective-permute-start | bytes 147464 | tf_op jit(solution)/shard_map/coefficients/ppermute | solution.py:21
  45.7 0.6 collective-permute-start.12
  46.3 1.7 %collective-permute-done.14 = f32[12,8,128]{2,1,0:T(8,128)S(1)} collective-permute-done((f32[12,8,128]{2,1,0:T(8,128)S(1)}, f32[12,8,128]{2,1,0:T(8,128)S(1)}, u32[]{:S(2)}, u32[]{:S(2)}) %collective-permute-start.14) | collective-permute-done | bytes 49184 | tf_op jit(solution)/shard_map/coefficients/ppermute | solution.py:21
  48.0 1.8 %collective-permute-done.13 = f32[12,8,128]{2,1,0:T(8,128)S(1)} collective-permute-done((f32[12,8,128]{2,1,0:T(8,128)S(1)}, f32[12,8,128]{2,1,0:T(8,128)S(1)}, u32[]{:S(2)}, u32[]{:S(2)}) %collective-permute-start.13) | collective-permute-done | bytes 49184 | tf_op jit(solution)/shard_map/coefficients/ppermute | solution.py:21
  49.8 0.0 collective-permute-done.12
  49.8 3.2 %collective-permute-start.17 = (f32[12,8,128]{2,1,0:T(8,128)S(1)}, f32[12,8,128]{2,1,0:T(8,128)S(1)}, u32[]{:S(2)}, u32[]{:S(2)}) collective-permute-start(f32[12,8,128]{2,1,0:T(8,128)S(1)} %add_add_fusion.1), channel_id=1, source_target_pairs={{0,24},{8,16},{16,8},{24,0},{1,25},{9,17},{17,9},{25,1},{2,26},{10... | collective-permute-start | bytes 147464 | tf_op jit(solution)/shard_map/coefficients/ppermute | solution.py:21
  53.0 0.4 collective-permute-start.16
  53.4 0.8 %collective-permute-start.15 = (f32[12,8,128]{2,1,0:T(8,128)S(1)}, f32[12,8,128]{2,1,0:T(8,128)S(1)}, u32[]{:S(2)}, u32[]{:S(2)}) collective-permute-start(f32[12,8,128]{2,1,0:T(8,128)S(1)} %add_add_fusion.1), channel_id=1, source_target_pairs={{0,8},{8,0},{16,24},{24,16},{1,9},{9,1},{17,25},{25,17},{2,10},{10... | collective-permute-start | bytes 147464 | tf_op jit(solution)/shard_map/coefficients/ppermute | solution.py:21
  54.3 1.5 %collective-permute-done.17 = f32[12,8,128]{2,1,0:T(8,128)S(1)} collective-permute-done((f32[12,8,128]{2,1,0:T(8,128)S(1)}, f32[12,8,128]{2,1,0:T(8,128)S(1)}, u32[]{:S(2)}, u32[]{:S(2)}) %collective-permute-start.17) | collective-permute-done | bytes 49184 | tf_op jit(solution)/shard_map/coefficients/ppermute | solution.py:21
  55.8 2.3 %collective-permute-done.16 = f32[12,8,128]{2,1,0:T(8,128)S(1)} collective-permute-done((f32[12,8,128]{2,1,0:T(8,128)S(1)}, f32[12,8,128]{2,1,0:T(8,128)S(1)}, u32[]{:S(2)}, u32[]{:S(2)}) %collective-permute-start.16) | collective-permute-done | bytes 49184 | tf_op jit(solution)/shard_map/coefficients/ppermute | solution.py:21
  58.1 0.0 collective-permute-done.15
  58.1 0.1 collective-permute-start.18
  58.1 1.2 %collective-permute-done.18.other = f32[12,8,128]{2,1,0:T(8,128)S(1)} collective-permute-done((f32[12,8,128]{2,1,0:T(8,128)S(1)}, f32[12,8,128]{2,1,0:T(8,128)S(1)}, u32[]{:S(2)}, u32[]{:S(2)}) %collective-permute-start.18) | collective-permute-done | bytes 49184 | tf_op jit(solution)/shard_map/coefficients/ppermute | solution.py:21
  59.4 2.1 %residual.1 = (f32[48,2048]{1,0:T(8,128)}, f32[48,432]{1,0:T(8,128)S(1)}, f32[24,128]{1,0:T(8,128)S(1)}) custom-call(s32[2]{0:T(128)S(1)} %pad_add_fusion.place, f32[12,8,128]{2,1,0:T(8,128)S(1)} %add_add_fusion.mine, f32[12,8,128]{2,1,0:T(8,128)S(1)} %collective-permute-done.18.other, f32[48,2048]{1,0:T(8,128)S(1)} %get-tuple-element.29.recurrence, ...), custom_call_target="tpu_custom_call" | custom-call | tf_op jit(solution)/shard_map/residual/pallas_call | solution.py:467
  61.5 0.2 collective-permute-start.19
  61.6 1.0 %collective-permute-done.19 = f32[24,128]{1,0:T(8,128)S(1)} collective-permute-done((f32[24,128]{1,0:T(8,128)S(1)}, f32[24,128]{1,0:T(8,128)S(1)}, u32[]{:S(2)}, u32[]{:S(2)}) %collective-permute-start.19) | collective-permute-done | bytes 12320 | tf_op jit(solution)/shard_map/gram/ppermute | solution.py:21
  62.7 1.5 %collective-permute-start.22 = (f32[24,128]{1,0:T(8,128)S(1)}, f32[24,128]{1,0:T(8,128)S(1)}, u32[]{:S(2)}, u32[]{:S(2)}) collective-permute-start(f32[24,128]{1,0:T(8,128)S(1)} %add.53), channel_id=1, source_target_pairs={{0,6},{1,7},{2,4},{3,5},{4,2},{5,3},{6,0},{7,1},{8,14},{9,15},{10,... | collective-permute-start | bytes 36872 | tf_op jit(solution)/shard_map/gram/ppermute | solution.py:21
  64.1 1.2 %collective-permute-start.21 = (f32[24,128]{1,0:T(8,128)S(1)}, f32[24,128]{1,0:T(8,128)S(1)}, u32[]{:S(2)}, u32[]{:S(2)}) collective-permute-start(f32[24,128]{1,0:T(8,128)S(1)} %add.53), channel_id=1, source_target_pairs={{0,4},{1,5},{2,6},{3,7},{4,0},{5,1},{6,2},{7,3},{8,12},{9,13},{10,... | collective-permute-start | bytes 36872 | tf_op jit(solution)/shard_map/gram/ppermute | solution.py:21
  65.3 0.9 %collective-permute-start.20 = (f32[24,128]{1,0:T(8,128)S(1)}, f32[24,128]{1,0:T(8,128)S(1)}, u32[]{:S(2)}, u32[]{:S(2)}) collective-permute-start(f32[24,128]{1,0:T(8,128)S(1)} %add.53), channel_id=1, source_target_pairs={{0,2},{1,3},{2,0},{3,1},{4,6},{5,7},{6,4},{7,5},{8,10},{9,11},{10,... | collective-permute-start | bytes 36872 | tf_op jit(solution)/shard_map/gram/ppermute | solution.py:21
  66.1 1.1 %collective-permute-done.22 = f32[24,128]{1,0:T(8,128)S(1)} collective-permute-done((f32[24,128]{1,0:T(8,128)S(1)}, f32[24,128]{1,0:T(8,128)S(1)}, u32[]{:S(2)}, u32[]{:S(2)}) %collective-permute-start.22) | collective-permute-done | bytes 12320 | tf_op jit(solution)/shard_map/gram/ppermute | solution.py:21
  67.2 0.6 collective-permute-done.21
  67.8 1.2 %collective-permute-done.20 = f32[24,128]{1,0:T(8,128)S(1)} collective-permute-done((f32[24,128]{1,0:T(8,128)S(1)}, f32[24,128]{1,0:T(8,128)S(1)}, u32[]{:S(2)}, u32[]{:S(2)}) %collective-permute-start.20) | collective-permute-done | bytes 12320 | tf_op jit(solution)/shard_map/gram/ppermute | solution.py:21
  69.0 1.6 %collective-permute-start.25 = (f32[24,128]{1,0:T(8,128)S(1)}, f32[24,128]{1,0:T(8,128)S(1)}, u32[]{:S(2)}, u32[]{:S(2)}) collective-permute-start(f32[24,128]{1,0:T(8,128)S(1)} %add_add_fusion.3), channel_id=1, source_target_pairs={{0,24},{8,16},{16,8},{24,0},{1,25},{9,17},{17,9},{25,1},{2,26},{10... | collective-permute-start | bytes 36872 | tf_op jit(solution)/shard_map/gram/ppermute | solution.py:21
  70.6 0.0 collective-permute-start.24
  70.6 2.7 %collective-permute-start.23 = (f32[24,128]{1,0:T(8,128)S(1)}, f32[24,128]{1,0:T(8,128)S(1)}, u32[]{:S(2)}, u32[]{:S(2)}) collective-permute-start(f32[24,128]{1,0:T(8,128)S(1)} %add_add_fusion.3), channel_id=1, source_target_pairs={{0,8},{8,0},{16,24},{24,16},{1,9},{9,1},{17,25},{25,17},{2,10},{10... | collective-permute-start | bytes 36872 | tf_op jit(solution)/shard_map/gram/ppermute | solution.py:21
  73.4 0.8 %copy.19 = f32[432,48]{1,0:T(8,128)} copy(f32[432,48]{0,1:T(8,128)S(1)} %bitcast.11) | data formatting | bytes 165888 | tf_op jit(solution)/shard_map/residual/transpose | solution.py:479
  74.2 0.3 collective-permute-done.25
  74.5 0.8 %collective-permute-done.24 = f32[24,128]{1,0:T(8,128)S(1)} collective-permute-done((f32[24,128]{1,0:T(8,128)S(1)}, f32[24,128]{1,0:T(8,128)S(1)}, u32[]{:S(2)}, u32[]{:S(2)}) %collective-permute-start.24) | collective-permute-done | bytes 12320 | tf_op jit(solution)/shard_map/gram/ppermute | solution.py:21
  75.3 0.1 fusion
  75.4 0.6 pad_maximum_fusion
  (22 shorter events, 0.1 us)
Async XLA Ops:
  1.7 5.4 %collective-permute-start = (bf16[48,2048]{1,0:T(8,128)(2,1)S(1)}, bf16[48,2048]{1,0:T(8,128)(2,1)S(1)}, u32[]{:S(2)}, u32[]{:S(2)}) collective-permute-start(bf16[48,2048]{1,0:T(8,128)(2,1)S(1)} %convert_element_type.9.own_panel), channel_id=1, source_target_pairs={{0,1},{1,0},{2,3},{3,2},{4,5},{5,4},{6,7},{7,6},{8,9},{9,8},{10,11... | collective-permute-start | bytes 589832 | tf_op jit(solution)/shard_map/gather/ppermute | solution.py:21
  2.2 9.9 %collective-permute-start.1 = (bf16[48,2048]{1,0:T(8,128)(2,1)S(1)}, bf16[48,2048]{1,0:T(8,128)(2,1)S(1)}, u32[]{:S(2)}, u32[]{:S(2)}) collective-permute-start(bf16[48,2048]{1,0:T(8,128)(2,1)S(1)} %convert_element_type.9.own_panel), channel_id=1, source_target_pairs={{0,2},{1,3},{2,0},{3,1},{4,6},{5,7},{6,4},{7,5},{8,10},{9,11},{10,... | collective-permute-start | bytes 589832 | tf_op jit(solution)/shard_map/gather/ppermute | solution.py:21
  4.7 11.2 %collective-permute-start.3 = (bf16[48,2048]{1,0:T(8,128)(2,1)S(1)}, bf16[48,2048]{1,0:T(8,128)(2,1)S(1)}, u32[]{:S(2)}, u32[]{:S(2)}) collective-permute-start(bf16[48,2048]{1,0:T(8,128)(2,1)S(1)} %convert_element_type.9.own_panel), channel_id=1, source_target_pairs={{0,4},{1,5},{2,6},{3,7},{4,0},{5,1},{6,2},{7,3},{8,12},{9,13},{10,... | collective-permute-start | bytes 589832 | tf_op jit(solution)/shard_map/gather/ppermute | solution.py:21
  6.3 9.7 %collective-permute-start.5 = (bf16[48,2048]{1,0:T(8,128)(2,1)S(1)}, bf16[48,2048]{1,0:T(8,128)(2,1)S(1)}, u32[]{:S(2)}, u32[]{:S(2)}) collective-permute-start(bf16[48,2048]{1,0:T(8,128)(2,1)S(1)} %convert_element_type.9.own_panel), channel_id=1, source_target_pairs={{0,6},{1,7},{2,4},{3,5},{4,2},{5,3},{6,0},{7,1},{8,14},{9,15},{10,... | collective-permute-start | bytes 589832 | tf_op jit(solution)/shard_map/gather/ppermute | solution.py:21
  12.1 5.1 %collective-permute-start.2 = (bf16[48,2048]{1,0:T(8,128)(2,1)S(1)}, bf16[48,2048]{1,0:T(8,128)(2,1)S(1)}, u32[]{:S(2)}, u32[]{:S(2)}) collective-permute-start(bf16[48,2048]{1,0:T(8,128)(2,1)S(1)} %gather.4.refs_0_), channel_id=1, source_target_pairs={{0,1},{1,0},{2,3},{3,2},{4,5},{5,4},{6,7},{7,6},{8,9},{9,8},{10,11... | collective-permute-start | bytes 589832 | tf_op jit(solution)/shard_map/gather/ppermute | solution.py:21
  15.9 1.4 %collective-permute-start.4 = (bf16[48,2048]{1,0:T(8,128)(2,1)S(1)}, bf16[48,2048]{1,0:T(8,128)(2,1)S(1)}, u32[]{:S(2)}, u32[]{:S(2)}) collective-permute-start(bf16[48,2048]{1,0:T(8,128)(2,1)S(1)} %gather.5.refs_1_), channel_id=1, source_target_pairs={{0,1},{1,0},{2,3},{3,2},{4,5},{5,4},{6,7},{7,6},{8,9},{9,8},{10,11... | collective-permute-start | bytes 589832 | tf_op jit(solution)/shard_map/gather/ppermute | solution.py:21
  15.9 1.7 %collective-permute-start.6 = (bf16[48,2048]{1,0:T(8,128)(2,1)S(1)}, bf16[48,2048]{1,0:T(8,128)(2,1)S(1)}, u32[]{:S(2)}, u32[]{:S(2)}) collective-permute-start(bf16[48,2048]{1,0:T(8,128)(2,1)S(1)} %gather.6.refs_2_), channel_id=1, source_target_pairs={{0,1},{1,0},{2,3},{3,2},{4,5},{5,4},{6,7},{7,6},{8,9},{9,8},{10,11... | collective-permute-start | bytes 589832 | tf_op jit(solution)/shard_map/gather/ppermute | solution.py:21
  19.7 8.9 %collective-permute-start.7 = (bf16[48,2048]{1,0:T(8,128)(2,1)S(1)}, bf16[48,2048]{1,0:T(8,128)(2,1)S(1)}, u32[]{:S(2)}, u32[]{:S(2)}) collective-permute-start(bf16[48,2048]{1,0:T(8,128)(2,1)S(1)} %get-tuple-element.23), channel_id=1, source_target_pairs={{0,8},{24,16},{8,24},{16,0},{1,9},{25,17},{9,25},{17,1},{2,10},{26... | collective-permute-start | bytes 589832 | tf_op jit(solution)/shard_map/late/ppermute | solution.py:429
  21.0 8.3 %copy-start.1 = (f32[48,2048]{1,0:T(8,128)S(1)}, f32[48,2048]{1,0:T(8,128)}, u32[]{:S(2)}) copy-start(f32[48,2048]{1,0:T(8,128)} %current.3) | copy-start | bytes 1179652
  21.0 8.3 %copy-start.2 = (f32[48,2048]{1,0:T(8,128)S(1)}, f32[48,2048]{1,0:T(8,128)}, u32[]{:S(2)}) copy-start(f32[48,2048]{1,0:T(8,128)} %previous.1) | copy-start | bytes 1179652
  21.0 8.3 %copy-start.4 = (f32[48,48]{1,0:T(8,128)S(1)}, f32[48,48]{1,0:T(8,128)}, u32[]{:S(2)}) copy-start(f32[48,48]{1,0:T(8,128)} %coupling.1) | copy-start | bytes 27652
  21.1 8.3 %copy-start.5 = (f32[2048]{0:T(1024)S(1)}, f32[2048]{0:T(1024)}, u32[]{:S(2)}) copy-start(f32[2048]{0:T(1024)} %param.14) | copy-start | bytes 24580
  24.5 11.5 %collective-permute-start.8 = (bf16[48,2048]{1,0:T(8,128)(2,1)S(1)}, bf16[48,2048]{1,0:T(8,128)(2,1)S(1)}, u32[]{:S(2)}, u32[]{:S(2)}) collective-permute-start(bf16[48,2048]{1,0:T(8,128)(2,1)S(1)} %get-tuple-element.24), channel_id=1, source_target_pairs={{0,24},{24,0},{1,25},{25,1},{2,26},{26,2},{3,27},{27,3},{4,28},{28... | collective-permute-start | bytes 589832 | tf_op jit(solution)/shard_map/late/ppermute | solution.py:433
  28.5 10.7 %collective-permute-start.10 = (bf16[48,2048]{1,0:T(8,128)(2,1)S(1)}, bf16[48,2048]{1,0:T(8,128)(2,1)S(1)}, u32[]{:S(2)}, u32[]{:S(2)}) collective-permute-start(bf16[48,2048]{1,0:T(8,128)(2,1)S(1)} %get-tuple-element.26), channel_id=1, source_target_pairs={{0,8},{8,0},{16,24},{24,16},{1,9},{9,1},{17,25},{25,17},{2,10},{10... | collective-permute-start | bytes 589832 | tf_op jit(solution)/shard_map/late/ppermute | solution.py:21
  28.7 10.5 %collective-permute-start.9 = (bf16[48,2048]{1,0:T(8,128)(2,1)S(1)}, bf16[48,2048]{1,0:T(8,128)(2,1)S(1)}, u32[]{:S(2)}, u32[]{:S(2)}) collective-permute-start(bf16[48,2048]{1,0:T(8,128)(2,1)S(1)} %add_convert_fusion), channel_id=1, source_target_pairs={{8,16},{16,8},{9,17},{17,9},{10,18},{18,10},{11,19},{19,11},{12,20... | collective-permute-start | bytes 589832 | tf_op jit(solution)/shard_map/late/ppermute | solution.py:434
  29.4 9.8 %copy-start = (f32[8,48,2048]{2,1,0:T(8,128)S(1)}, f32[8,48,2048]{2,1,0:T(8,128)}, u32[]{:S(2)}) copy-start(f32[8,48,2048]{2,1,0:T(8,128)} %param.13) | copy-start | bytes 9437188
  29.4 9.8 %copy-start.3 = (f32[2048]{0:T(1024)S(1)}, f32[2048]{0:T(1024)}, u32[]{:S(2)}) copy-start(f32[2048]{0:T(1024)} %param.15) | copy-start | bytes 24580
  41.0 1.3 %collective-permute-start.11 = (f32[12,8,128]{2,1,0:T(8,128)S(1)}, f32[12,8,128]{2,1,0:T(8,128)S(1)}, u32[]{:S(2)}, u32[]{:S(2)}) collective-permute-start(f32[12,8,128]{2,1,0:T(8,128)S(1)} %get-tuple-element.28), channel_id=1, source_target_pairs={{0,1},{1,0},{2,3},{3,2},{4,5},{5,4},{6,7},{7,6},{8,9},{9,8},{10,11... | collective-permute-start | bytes 147464 | tf_op jit(solution)/shard_map/coefficients/ppermute | solution.py:21
  42.3 5.7 %collective-permute-start.14 = (f32[12,8,128]{2,1,0:T(8,128)S(1)}, f32[12,8,128]{2,1,0:T(8,128)S(1)}, u32[]{:S(2)}, u32[]{:S(2)}) collective-permute-start(f32[12,8,128]{2,1,0:T(8,128)S(1)} %add.46), channel_id=1, source_target_pairs={{0,6},{1,7},{2,4},{3,5},{4,2},{5,3},{6,0},{7,1},{8,14},{9,15},{10,... | collective-permute-start | bytes 147464 | tf_op jit(solution)/shard_map/coefficients/ppermute | solution.py:21
  45.7 4.1 %collective-permute-start.13 = (f32[12,8,128]{2,1,0:T(8,128)S(1)}, f32[12,8,128]{2,1,0:T(8,128)S(1)}, u32[]{:S(2)}, u32[]{:S(2)}) collective-permute-start(f32[12,8,128]{2,1,0:T(8,128)S(1)} %add.46), channel_id=1, source_target_pairs={{0,4},{1,5},{2,6},{3,7},{4,0},{5,1},{6,2},{7,3},{8,12},{9,13},{10,... | collective-permute-start | bytes 147464 | tf_op jit(solution)/shard_map/coefficients/ppermute | solution.py:21
  45.7 4.1 %collective-permute-start.12 = (f32[12,8,128]{2,1,0:T(8,128)S(1)}, f32[12,8,128]{2,1,0:T(8,128)S(1)}, u32[]{:S(2)}, u32[]{:S(2)}) collective-permute-start(f32[12,8,128]{2,1,0:T(8,128)S(1)} %add.46), channel_id=1, source_target_pairs={{0,2},{1,3},{2,0},{3,1},{4,6},{5,7},{6,4},{7,5},{8,10},{9,11},{10,... | collective-permute-start | bytes 147464 | tf_op jit(solution)/shard_map/coefficients/ppermute | solution.py:21
  49.8 6.0 %collective-permute-start.17 = (f32[12,8,128]{2,1,0:T(8,128)S(1)}, f32[12,8,128]{2,1,0:T(8,128)S(1)}, u32[]{:S(2)}, u32[]{:S(2)}) collective-permute-start(f32[12,8,128]{2,1,0:T(8,128)S(1)} %add_add_fusion.1), channel_id=1, source_target_pairs={{0,24},{8,16},{16,8},{24,0},{1,25},{9,17},{17,9},{25,1},{2,26},{10... | collective-permute-start | bytes 147464 | tf_op jit(solution)/shard_map/coefficients/ppermute | solution.py:21
  53.0 5.0 %collective-permute-start.16 = (f32[12,8,128]{2,1,0:T(8,128)S(1)}, f32[12,8,128]{2,1,0:T(8,128)S(1)}, u32[]{:S(2)}, u32[]{:S(2)}) collective-permute-start(f32[12,8,128]{2,1,0:T(8,128)S(1)} %add_add_fusion.1), channel_id=1, source_target_pairs={{0,16},{8,24},{16,0},{24,8},{1,17},{9,25},{17,1},{25,9},{2,18},{10... | collective-permute-start | bytes 147464 | tf_op jit(solution)/shard_map/coefficients/ppermute | solution.py:21
  53.4 4.6 %collective-permute-start.15 = (f32[12,8,128]{2,1,0:T(8,128)S(1)}, f32[12,8,128]{2,1,0:T(8,128)S(1)}, u32[]{:S(2)}, u32[]{:S(2)}) collective-permute-start(f32[12,8,128]{2,1,0:T(8,128)S(1)} %add_add_fusion.1), channel_id=1, source_target_pairs={{0,8},{8,0},{16,24},{24,16},{1,9},{9,1},{17,25},{25,17},{2,10},{10... | collective-permute-start | bytes 147464 | tf_op jit(solution)/shard_map/coefficients/ppermute | solution.py:21
  58.1 1.3 %collective-permute-start.18 = (f32[12,8,128]{2,1,0:T(8,128)S(1)}, f32[12,8,128]{2,1,0:T(8,128)S(1)}, u32[]{:S(2)}, u32[]{:S(2)}) collective-permute-start(f32[12,8,128]{2,1,0:T(8,128)S(1)} %add_add_fusion.mine), channel_id=1, source_target_pairs={{0,1},{1,0},{2,3},{3,2},{4,5},{5,4},{6,7},{7,6},{8,9},{9,8},{10,11... | collective-permute-start | bytes 147464 | tf_op jit(solution)/shard_map/coefficients/ppermute | solution.py:21
  61.5 1.2 %collective-permute-start.19 = (f32[24,128]{1,0:T(8,128)S(1)}, f32[24,128]{1,0:T(8,128)S(1)}, u32[]{:S(2)}, u32[]{:S(2)}) collective-permute-start(f32[24,128]{1,0:T(8,128)S(1)} %get-tuple-element.32), channel_id=1, source_target_pairs={{0,1},{1,0},{2,3},{3,2},{4,5},{5,4},{6,7},{7,6},{8,9},{9,8},{10,11... | collective-permute-start | bytes 36872 | tf_op jit(solution)/shard_map/gram/ppermute | solution.py:21
  62.7 4.6 %collective-permute-start.22 = (f32[24,128]{1,0:T(8,128)S(1)}, f32[24,128]{1,0:T(8,128)S(1)}, u32[]{:S(2)}, u32[]{:S(2)}) collective-permute-start(f32[24,128]{1,0:T(8,128)S(1)} %add.53), channel_id=1, source_target_pairs={{0,6},{1,7},{2,4},{3,5},{4,2},{5,3},{6,0},{7,1},{8,14},{9,15},{10,... | collective-permute-start | bytes 36872 | tf_op jit(solution)/shard_map/gram/ppermute | solution.py:21
  64.1 3.7 %collective-permute-start.21 = (f32[24,128]{1,0:T(8,128)S(1)}, f32[24,128]{1,0:T(8,128)S(1)}, u32[]{:S(2)}, u32[]{:S(2)}) collective-permute-start(f32[24,128]{1,0:T(8,128)S(1)} %add.53), channel_id=1, source_target_pairs={{0,4},{1,5},{2,6},{3,7},{4,0},{5,1},{6,2},{7,3},{8,12},{9,13},{10,... | collective-permute-start | bytes 36872 | tf_op jit(solution)/shard_map/gram/ppermute | solution.py:21
  65.3 3.7 %collective-permute-start.20 = (f32[24,128]{1,0:T(8,128)S(1)}, f32[24,128]{1,0:T(8,128)S(1)}, u32[]{:S(2)}, u32[]{:S(2)}) collective-permute-start(f32[24,128]{1,0:T(8,128)S(1)} %add.53), channel_id=1, source_target_pairs={{0,2},{1,3},{2,0},{3,1},{4,6},{5,7},{6,4},{7,5},{8,10},{9,11},{10,... | collective-permute-start | bytes 36872 | tf_op jit(solution)/shard_map/gram/ppermute | solution.py:21
  69.0 5.5 %collective-permute-start.25 = (f32[24,128]{1,0:T(8,128)S(1)}, f32[24,128]{1,0:T(8,128)S(1)}, u32[]{:S(2)}, u32[]{:S(2)}) collective-permute-start(f32[24,128]{1,0:T(8,128)S(1)} %add_add_fusion.3), channel_id=1, source_target_pairs={{0,24},{8,16},{16,8},{24,0},{1,25},{9,17},{17,9},{25,1},{2,26},{10... | collective-permute-start | bytes 36872 | tf_op jit(solution)/shard_map/gram/ppermute | solution.py:21
  70.6 4.6 %collective-permute-start.24 = (f32[24,128]{1,0:T(8,128)S(1)}, f32[24,128]{1,0:T(8,128)S(1)}, u32[]{:S(2)}, u32[]{:S(2)}) collective-permute-start(f32[24,128]{1,0:T(8,128)S(1)} %add_add_fusion.3), channel_id=1, source_target_pairs={{0,16},{8,24},{16,0},{24,8},{1,17},{9,25},{17,1},{25,9},{2,18},{10... | collective-permute-start | bytes 36872 | tf_op jit(solution)/shard_map/gram/ppermute | solution.py:21
  70.6 4.6 %collective-permute-start.23 = (f32[24,128]{1,0:T(8,128)S(1)}, f32[24,128]{1,0:T(8,128)S(1)}, u32[]{:S(2)}, u32[]{:S(2)}) collective-permute-start(f32[24,128]{1,0:T(8,128)S(1)} %add_add_fusion.3), channel_id=1, source_target_pairs={{0,8},{8,0},{16,24},{24,16},{1,9},{9,1},{17,25},{25,17},{2,10},{10... | collective-permute-start | bytes 36872 | tf_op jit(solution)/shard_map/gram/ppermute | solution.py:21

commit v11 on v10

--- a/solution.py
+++ b/solution.py
@@ -21,11 +21,29 @@
     return lax.ppermute(value, axis, [(i, i ^ mask) for i in range(count)])
 
 
-def total(value, axis, step):
-    values = [value] + [swap(value, axis, m) for m in range(step, lax.axis_size(axis), step)]
+def tree_sum(values):
     while len(values) > 1:
         values = [values[i] + values[i + 1] for i in range(0, len(values), 2)]
     return values[0]
+
+
+def total(value, axis, step):
+    return tree_sum([value] + [swap(value, axis, m) for m in range(step, lax.axis_size(axis), step)])
+
+
+def total_by_core(value):
+    row_devs, col_devs = lax.axis_size("row"), lax.axis_size("col")
+    if col_devs != 2 * row_devs:
+        return total(total(value, "col", 2), "row", 1)
+    places = [(r, c) for r in range(row_devs) for c in range(col_devs)]
+    for turn in range(2):
+        values = [value]
+        for m in range(1, row_devs):
+            partners = [(r, c ^ (2 * m)) if c % 2 == turn else (r ^ m, c) for r, c in places]
+            trades = [(i, r * col_devs + c) for i, (r, c) in enumerate(partners)]
+            values.append(lax.ppermute(value, ("row", "col"), trades))
+        value = tree_sum(values)
+    return value
 
 
 def split(value):
@@ -460,14 +478,14 @@
             compiler_params=limit(24),
         )(place, base, *received, mass, current_block, stored)
         mine = keep + swap(give, "col", 1)
-        mine = total(total(mine, "col", 2), "row", 1)
+        mine = total_by_core(mine)
         other = swap(mine, "col", 1)
 
     with jax.named_scope("residual"):
         residual_block, coef, gram = pl.pallas_call(
             functools.partial(residual_kernel, cells),
             out_shape=[
-                slab,
+                pltpu.VMEM((width, slab_len), f32),
                 jax.ShapeDtypeStruct((width, basis_rows), f32),
                 jax.ShapeDtypeStruct((width // 2, LANES), f32),
             ],

time: 75.6 us -> 74.6 us (0.987)
  waiting for transfers between devices: 26.7 us -> 24.6 us
  starting transfers between devices: 28.1 us -> 29.7 us
  Pallas kernels: 17 us -> 15.6 us
    ppermute x0 -> x6, starting transfers between devices: none -> 8.59 us  [total_by_core(): values.append(lax.ppermute(value, ('row', 'col'), trades))]
    ppermute x23 -> x17, starting transfers between devices: 22.1 us -> 13.5 us  [swap(): return lax.ppermute(value, axis, [(i, i ^ mask) for i in range(count)])]
    ppermute x23 -> x17, waiting for transfers between devices: 21.9 us -> 14.4 us  [swap(): return lax.ppermute(value, axis, [(i, i ^ mask) for i in range(count)])]
    ppermute x0 -> x6, waiting for transfers between devices: none -> 6.58 us  [total_by_core(): values.append(lax.ppermute(value, ('row', 'col'), trades))]
    ppermute x1, waiting for transfers between devices: 4.85 us -> 3.6 us  [local(): lax.ppermute(parts[0], 'row', [(0, 3), (3, 0)])]
    ppermute x1, starting transfers between devices: 1.32 us -> 2.24 us  [local(): first = lax.ppermute(first, 'row', [(0, 1), (3, 2), (1, 3), (2, 0)])]
    pallas_call x1, Pallas kernels: 3.48 us -> 2.57 us  [local(): pl.pallas_call(functools.partial(late_kernel, masks), out_shape=[part, sl...]
  transfers between devices with their start and end apart: 26 -> 26, of which waited for: 17 -> 17; matrix products, arithmetic and copies ran while one was open for 1% -> 2% of each run, Pallas kernels for 15% -> 13%
where the time goes in v11:
time: 74.6 us; the launch traced here: 74.9 us
  starting transfers between devices  29.7 us (40%)
  waiting for transfers between devices  24.6 us (33%)
  Pallas kernels  15.6 us (21%)
  other arithmetic  1.81 us (2%)
  local copies, waits for them, and re-layouts  1.66 us (2%)
  between operations  1.5 us (2%)
    ppermute x17, waiting for transfers between devices, swap(): return lax.ppermute(value, axis, [(i, i ^ mask) for i in range(count)])  14.4 us
    ppermute x17, starting transfers between devices, swap(): return lax.ppermute(value, axis, [(i, i ^ mask) for i in range(count)])  13.5 us
    ppermute x6, starting transfers between devices, total_by_core(): values.append(lax.ppermute(value, ('row', 'col'), trades))  8.59 us
    ppermute x6, waiting for transfers between devices, total_by_core(): values.append(lax.ppermute(value, ('row', 'col'), trades))  6.58 us
    ppermute x1, starting transfers between devices, local(): lax.ppermute(parts[0], 'row', [(0, 3), (3, 0)])  4.69 us
    pallas_call x1, Pallas kernels, local(): pl.pallas_call(functools.partial(early_kernel, row_devs, col_devs, slab_t...  4.46 us
    ppermute x1, waiting for transfers between devices, local(): lax.ppermute(parts[0], 'row', [(0, 3), (3, 0)])  3.6 us
    pallas_call x1, Pallas kernels, local(): pl.pallas_call(functools.partial(late_kernel, masks), out_shape=[part, sl...  2.57 us
  transfers between devices with their start and end apart: 26, of which 17 were waited for; matrix products, arithmetic and copies ran while one was open for 2% of the time, Pallas kernels for 13%

profile of v11, /device:TPU:0, one launch (start us, length us, event | category | flops | bytes accessed | tf_op | source)
XLA Modules:
  0.0 74.9 jit_solution(8651813982178751904)
XLA Ops:
  0.6 1.0 %convert_element_type.9.own_panel = bf16[48,2048]{1,0:T(8,128)(2,1)S(1)} convert(f32[48,2048]{1,0:T(8,128)} %current.3) | non-fusion elementwise | flops 98304 | bytes 589824 | tf_op jit(solution)/shard_map/gather/convert_element_type | solution.py:367
  1.7 0.5 collective-permute-start
  2.2 2.6 %collective-permute-start.1 = (bf16[48,2048]{1,0:T(8,128)(2,1)S(1)}, bf16[48,2048]{1,0:T(8,128)(2,1)S(1)}, u32[]{:S(2)}, u32[]{:S(2)}) collective-permute-start(bf16[48,2048]{1,0:T(8,128)(2,1)S(1)} %convert_element_type.9.own_panel), channel_id=1, source_target_pairs={{0,2},{1,3},{2,0},{3,1},{4,6},{5,7},{6,4},{7,5},{8,10},{9,11},{10,... | collective-permute-start | bytes 589832 | tf_op jit(solution)/shard_map/gather/ppermute | solution.py:21
  4.7 1.5 %collective-permute-start.3 = (bf16[48,2048]{1,0:T(8,128)(2,1)S(1)}, bf16[48,2048]{1,0:T(8,128)(2,1)S(1)}, u32[]{:S(2)}, u32[]{:S(2)}) collective-permute-start(bf16[48,2048]{1,0:T(8,128)(2,1)S(1)} %convert_element_type.9.own_panel), channel_id=1, source_target_pairs={{0,4},{1,5},{2,6},{3,7},{4,0},{5,1},{6,2},{7,3},{8,12},{9,13},{10,... | collective-permute-start | bytes 589832 | tf_op jit(solution)/shard_map/gather/ppermute | solution.py:21
  6.3 0.0 collective-permute-start.5
  6.9 0.1 pad_add_fusion.place
  7.0 0.0 collective-permute-done.near_panel
  7.0 4.5 %early.1 = (s32[1,896]{1,0:T(1,128)S(1)}, bf16[512,128,128]{2,1,0:T(8,128)(2,1)S(1)}, f32[65,48,128]{2,1,0:T(8,128)S(1)}, bf16[9,48,2048]{2,1,0:T(8,128)(2,1)S(1)}) custom-call(s32[2]{0:T(128)S(1)} %pad_add_fusion.place, s32[1]{0:T(128)S(6)} %copy.26.counts, s32[1,512]{1,0:T(1,128)} %bitcast.16, s32[1,512]{1,0:T(1,128)} %bitcast.17, ...), custom_call_target="tpu_custom_call" | custom-call | flops 805306368 | bytes 16777216 | tf_op jit(solution)/shard_map/early/pallas_call | solution.py:376
  11.5 0.0 collective-permute-done.1.value
  11.5 0.1 collective-permute-start.2
  11.6 4.3 %collective-permute-done.3.value = bf16[48,2048]{1,0:T(8,128)(2,1)S(1)} collective-permute-done((bf16[48,2048]{1,0:T(8,128)(2,1)S(1)}, bf16[48,2048]{1,0:T(8,128)(2,1)S(1)}, u32[]{:S(2)}, u32[]{:S(2)}) %collective-permute-start.3) | collective-permute-done | bytes 196640 | tf_op jit(solution)/shard_map/gather/ppermute | solution.py:21
  15.9 0.0 collective-permute-start.4
  15.9 0.0 collective-permute-done.5.value
  15.9 0.5 collective-permute-start.6
  16.4 0.8 %gather.7.refs_5_ = bf16[9,48,2048]{2,1,0:T(8,128)(2,1)S(1)} custom-call(bf16[48,2048]{1,0:T(8,128)(2,1)S(1)} %gather.4.refs_0_, bf16[48,2048]{1,0:T(8,128)(2,1)S(1)} %gather.5.refs_1_, bf16[48,2048]{1,0:T(8,128)(2,1)S(1)} %gather.6.refs_2_, bf16[9,48,2048]{2,1,0:T(8,128)(2,1)S(1)} %get-tuple-element.21.refs_3_), custom_call_target="tpu_custom_call", output_to_operand_aliasing={{}: (3, {})} | custom-call | flops 48 | bytes 1 | tf_op jit(solution)/shard_map/gather/pallas_call | solution.py:411
  17.2 0.0 collective-permute-done.2.refs_0_
  17.2 0.2 collective-permute-done.4.refs_1_
  17.4 0.3 collective-permute-done.6.refs_2_
  17.6 2.1 %late.3 = (bf16[48,2048]{1,0:T(8,128)(2,1)S(1)}, bf16[9,48,2048]{2,1,0:T(8,128)(2,1)S(1)}) custom-call(s32[2]{0:T(128)S(1)} %pad_add_fusion.place, s32[1,896]{1,0:T(1,128)S(1)} %get-tuple-element.18.plan, bf16[48,2048]{1,0:T(8,128)(2,1)S(1)} %collective-permute-done.2.refs_0_, ...), custom_call_target="tpu_custom_call", output_to_operand_aliasing={{1}: (7, {})} | custom-call | flops 48 | bytes 1 | tf_op jit(solution)/shard_map/late/pallas_call | solution.py:427
  19.7 2.2 %collective-permute-start.7 = (bf16[48,2048]{1,0:T(8,128)(2,1)S(1)}, bf16[48,2048]{1,0:T(8,128)(2,1)S(1)}, u32[]{:S(2)}, u32[]{:S(2)}) collective-permute-start(bf16[48,2048]{1,0:T(8,128)(2,1)S(1)} %get-tuple-element.23), channel_id=1, source_target_pairs={{0,8},{24,16},{8,24},{16,0},{1,9},{25,17},{9,25},{17,1},{2,10},{26... | collective-permute-start | bytes 589832 | tf_op jit(solution)/shard_map/late/ppermute | solution.py:447
  22.0 2.6 %late.5 = (bf16[48,2048]{1,0:T(8,128)(2,1)S(1)}, f32[48,2048]{1,0:T(8,128)S(1)}, bf16[48,2048]{1,0:T(8,128)(2,1)S(1)}) custom-call(s32[2]{0:T(128)S(1)} %pad_add_fusion.place, s32[1,896]{1,0:T(1,128)S(1)} %get-tuple-element.18.plan, bf16[9,48,2048]{2,1,0:T(8,128)(2,1)S(1)} %get-tuple-element.22.panel_buf, ...), custom_call_target="tpu_custom_call" | custom-call | flops 48 | bytes 1 | tf_op jit(solution)/shard_map/late/pallas_call | solution.py:437
  24.5 4.7 %collective-permute-start.8 = (bf16[48,2048]{1,0:T(8,128)(2,1)S(1)}, bf16[48,2048]{1,0:T(8,128)(2,1)S(1)}, u32[]{:S(2)}, u32[]{:S(2)}) collective-permute-start(bf16[48,2048]{1,0:T(8,128)(2,1)S(1)} %get-tuple-element.24), channel_id=1, source_target_pairs={{0,24},{24,0},{1,25},{25,1},{2,26},{26,2},{3,27},{27,3},{4,28},{28... | collective-permute-start | bytes 589832 | tf_op jit(solution)/shard_map/late/ppermute | solution.py:451
  29.2 0.1 collective-permute-start.10
  29.3 0.0 collective-permute-done.7.refs_0_
  29.4 0.7 collective-permute-start.9
  30.1 0.0 copy-start
  30.1 0.0 copy-start.3
  30.1 2.3 %late.4.base = f32[48,2048]{1,0:T(8,128)S(1)} custom-call(s32[2]{0:T(128)S(1)} %pad_add_fusion.place, s32[1,896]{1,0:T(1,128)S(1)} %get-tuple-element.18.plan, bf16[9,48,2048]{2,1,0:T(8,128)(2,1)S(1)} %get-tuple-element.22.panel_buf, bf16[512,128,128]{2,1,0:T(8,128)(2,1)S(1)} %get-tuple-element.20.refs_3_.tiles, ...), custom_call_target="tpu_custom_call" | custom-call | flops 48 | bytes 1 | tf_op jit(solution)/shard_map/late/pallas_call | solution.py:458
  32.5 3.6 %collective-permute-done.8.refs_1_ = bf16[48,2048]{1,0:T(8,128)(2,1)S(1)} collective-permute-done((bf16[48,2048]{1,0:T(8,128)(2,1)S(1)}, bf16[48,2048]{1,0:T(8,128)(2,1)S(1)}, u32[]{:S(2)}, u32[]{:S(2)}) %collective-permute-start.8) | collective-permute-done | bytes 196640 | tf_op jit(solution)/shard_map/late/ppermute | solution.py:451
  36.1 2.9 %collective-permute-done.10.refs_3_ = bf16[48,2048]{1,0:T(8,128)(2,1)S(1)} collective-permute-done((bf16[48,2048]{1,0:T(8,128)(2,1)S(1)}, bf16[48,2048]{1,0:T(8,128)(2,1)S(1)}, u32[]{:S(2)}, u32[]{:S(2)}) %collective-permute-start.10) | collective-permute-done | bytes 196640 | tf_op jit(solution)/shard_map/late/ppermute | solution.py:21
  38.9 1.8 %coefficients.1 = (f32[48,2048]{1,0:T(8,128)S(1)}, f32[12,8,128]{2,1,0:T(8,128)S(1)}, f32[12,8,128]{2,1,0:T(8,128)S(1)}) custom-call(s32[2]{0:T(128)S(1)} %pad_add_fusion.place, f32[48,2048]{1,0:T(8,128)S(1)} %late.4.base, bf16[48,2048]{1,0:T(8,128)(2,1)S(1)} %collective-permute-done.7.refs_0_, bf16[48,2048]{1,0:T(8,128)(2,1)S(1)} %collective-permute-done.8.refs_1_, ...), custom_call_target="tpu_custom_call" | custom-call | tf_op jit(solution)/shard_map/coefficients/pallas_call | solution.py:472
  40.7 0.1 collective-permute-start.11
  40.8 1.2 %collective-permute-done.11 = f32[12,8,128]{2,1,0:T(8,128)S(1)} collective-permute-done((f32[12,8,128]{2,1,0:T(8,128)S(1)}, f32[12,8,128]{2,1,0:T(8,128)S(1)}, u32[]{:S(2)}, u32[]{:S(2)}) %collective-permute-start.11) | collective-permute-done | bytes 49184 | tf_op jit(solution)/shard_map/coefficients/ppermute | solution.py:21
  42.0 3.5 %collective-permute-start.14 = (f32[12,8,128]{2,1,0:T(8,128)S(1)}, f32[12,8,128]{2,1,0:T(8,128)S(1)}, u32[]{:S(2)}, u32[]{:S(2)}) collective-permute-start(f32[12,8,128]{2,1,0:T(8,128)S(1)} %add.46), channel_id=1, source_target_pairs={{0,6},{1,25},{2,4},{3,27},{4,2},{5,29},{6,0},{7,31},{8,14},{9,17},... | collective-permute-start | bytes 147464 | tf_op jit(solution)/shard_map/coefficients/ppermute | solution.py:44
  45.5 0.0 collective-permute-start.13
  45.5 0.6 collective-permute-start.12
  46.1 1.4 %collective-permute-done.14 = f32[12,8,128]{2,1,0:T(8,128)S(1)} collective-permute-done((f32[12,8,128]{2,1,0:T(8,128)S(1)}, f32[12,8,128]{2,1,0:T(8,128)S(1)}, u32[]{:S(2)}, u32[]{:S(2)}) %collective-permute-start.14) | collective-permute-done | bytes 49184 | tf_op jit(solution)/shard_map/coefficients/ppermute | solution.py:44
  47.6 2.0 %collective-permute-done.13 = f32[12,8,128]{2,1,0:T(8,128)S(1)} collective-permute-done((f32[12,8,128]{2,1,0:T(8,128)S(1)}, f32[12,8,128]{2,1,0:T(8,128)S(1)}, u32[]{:S(2)}, u32[]{:S(2)}) %collective-permute-start.13) | collective-permute-done | bytes 49184 | tf_op jit(solution)/shard_map/coefficients/ppermute | solution.py:44
  49.6 0.0 collective-permute-done.12
  49.6 2.0 %collective-permute-start.17 = (f32[12,8,128]{2,1,0:T(8,128)S(1)}, f32[12,8,128]{2,1,0:T(8,128)S(1)}, u32[]{:S(2)}, u32[]{:S(2)}) collective-permute-start(f32[12,8,128]{2,1,0:T(8,128)S(1)} %add_add_fusion.1), channel_id=1, source_target_pairs={{0,24},{1,7},{2,26},{3,5},{4,28},{5,3},{6,30},{7,1},{8,16},{9,15},... | collective-permute-start | bytes 147464 | tf_op jit(solution)/shard_map/coefficients/ppermute | solution.py:44
  51.6 1.5 %collective-permute-start.16 = (f32[12,8,128]{2,1,0:T(8,128)S(1)}, f32[12,8,128]{2,1,0:T(8,128)S(1)}, u32[]{:S(2)}, u32[]{:S(2)}) collective-permute-start(f32[12,8,128]{2,1,0:T(8,128)S(1)} %add_add_fusion.1), channel_id=1, source_target_pairs={{0,16},{1,5},{2,18},{3,7},{4,20},{5,1},{6,22},{7,3},{8,24},{9,13},... | collective-permute-start | bytes 147464 | tf_op jit(solution)/shard_map/coefficients/ppermute | solution.py:44
  53.1 1.0 %collective-permute-start.15 = (f32[12,8,128]{2,1,0:T(8,128)S(1)}, f32[12,8,128]{2,1,0:T(8,128)S(1)}, u32[]{:S(2)}, u32[]{:S(2)}) collective-permute-start(f32[12,8,128]{2,1,0:T(8,128)S(1)} %add_add_fusion.1), channel_id=1, source_target_pairs={{0,8},{1,3},{2,10},{3,1},{4,12},{5,7},{6,14},{7,5},{8,0},{9,11},{1... | collective-permute-start | bytes 147464 | tf_op jit(solution)/shard_map/coefficients/ppermute | solution.py:44
  54.1 1.6 %collective-permute-done.17 = f32[12,8,128]{2,1,0:T(8,128)S(1)} collective-permute-done((f32[12,8,128]{2,1,0:T(8,128)S(1)}, f32[12,8,128]{2,1,0:T(8,128)S(1)}, u32[]{:S(2)}, u32[]{:S(2)}) %collective-permute-start.17) | collective-permute-done | bytes 49184 | tf_op jit(solution)/shard_map/coefficients/ppermute | solution.py:44
  55.7 1.0 %collective-permute-done.16 = f32[12,8,128]{2,1,0:T(8,128)S(1)} collective-permute-done((f32[12,8,128]{2,1,0:T(8,128)S(1)}, f32[12,8,128]{2,1,0:T(8,128)S(1)}, u32[]{:S(2)}, u32[]{:S(2)}) %collective-permute-start.16) | collective-permute-done | bytes 49184 | tf_op jit(solution)/shard_map/coefficients/ppermute | solution.py:44
  56.6 0.6 collective-permute-done.15
  57.2 0.1 collective-permute-start.18
  57.3 1.2 %collective-permute-done.18.other = f32[12,8,128]{2,1,0:T(8,128)S(1)} collective-permute-done((f32[12,8,128]{2,1,0:T(8,128)S(1)}, f32[12,8,128]{2,1,0:T(8,128)S(1)}, u32[]{:S(2)}, u32[]{:S(2)}) %collective-permute-start.18) | collective-permute-done | bytes 49184 | tf_op jit(solution)/shard_map/coefficients/ppermute | solution.py:21
  58.5 1.6 %residual.1 = (f32[48,2048]{1,0:T(8,128)S(1)}, f32[48,432]{1,0:T(8,128)S(1)}, f32[24,128]{1,0:T(8,128)S(1)}) custom-call(s32[2]{0:T(128)S(1)} %pad_add_fusion.place, f32[12,8,128]{2,1,0:T(8,128)S(1)} %add_add_fusion.mine, f32[12,8,128]{2,1,0:T(8,128)S(1)} %collective-permute-done.18.other, f32[48,2048]{1,0:T(8,128)S(1)} %get-tuple-element.29.recurrence, ...), custom_call_target="tpu_custom_call" | custom-call | tf_op jit(solution)/shard_map/residual/pallas_call | solution.py:485
  60.1 0.2 collective-permute-start.19
  60.3 1.0 %collective-permute-done.19 = f32[24,128]{1,0:T(8,128)S(1)} collective-permute-done((f32[24,128]{1,0:T(8,128)S(1)}, f32[24,128]{1,0:T(8,128)S(1)}, u32[]{:S(2)}, u32[]{:S(2)}) %collective-permute-start.19) | collective-permute-done | bytes 12320 | tf_op jit(solution)/shard_map/gram/ppermute | solution.py:21
  61.4 1.5 %collective-permute-start.22 = (f32[24,128]{1,0:T(8,128)S(1)}, f32[24,128]{1,0:T(8,128)S(1)}, u32[]{:S(2)}, u32[]{:S(2)}) collective-permute-start(f32[24,128]{1,0:T(8,128)S(1)} %add.53), channel_id=1, source_target_pairs={{0,6},{1,7},{2,4},{3,5},{4,2},{5,3},{6,0},{7,1},{8,14},{9,15},{10,... | collective-permute-start | bytes 36872 | tf_op jit(solution)/shard_map/gram/ppermute | solution.py:21
  62.8 0.6 collective-permute-start.21
  63.5 1.4 %collective-permute-start.20 = (f32[24,128]{1,0:T(8,128)S(1)}, f32[24,128]{1,0:T(8,128)S(1)}, u32[]{:S(2)}, u32[]{:S(2)}) collective-permute-start(f32[24,128]{1,0:T(8,128)S(1)} %add.53), channel_id=1, source_target_pairs={{0,2},{1,3},{2,0},{3,1},{4,6},{5,7},{6,4},{7,5},{8,10},{9,11},{10,... | collective-permute-start | bytes 36872 | tf_op jit(solution)/shard_map/gram/ppermute | solution.py:21
  64.8 1.1 %collective-permute-done.22 = f32[24,128]{1,0:T(8,128)S(1)} collective-permute-done((f32[24,128]{1,0:T(8,128)S(1)}, f32[24,128]{1,0:T(8,128)S(1)}, u32[]{:S(2)}, u32[]{:S(2)}) %collective-permute-start.22) | collective-permute-done | bytes 12320 | tf_op jit(solution)/shard_map/gram/ppermute | solution.py:21
  65.9 0.6 collective-permute-done.21
  66.5 0.6 collective-permute-done.20
  67.2 2.4 %collective-permute-start.25 = (f32[24,128]{1,0:T(8,128)S(1)}, f32[24,128]{1,0:T(8,128)S(1)}, u32[]{:S(2)}, u32[]{:S(2)}) collective-permute-start(f32[24,128]{1,0:T(8,128)S(1)} %add_add_fusion.3), channel_id=1, source_target_pairs={{0,24},{8,16},{16,8},{24,0},{1,25},{9,17},{17,9},{25,1},{2,26},{10... | collective-permute-start | bytes 36872 | tf_op jit(solution)/shard_map/gram/ppermute | solution.py:21
  69.6 0.0 collective-permute-start.24
  69.6 2.0 %collective-permute-start.23 = (f32[24,128]{1,0:T(8,128)S(1)}, f32[24,128]{1,0:T(8,128)S(1)}, u32[]{:S(2)}, u32[]{:S(2)}) collective-permute-start(f32[24,128]{1,0:T(8,128)S(1)} %add_add_fusion.3), channel_id=1, source_target_pairs={{0,8},{8,0},{16,24},{24,16},{1,9},{9,1},{17,25},{25,17},{2,10},{10... | collective-permute-start | bytes 36872 | tf_op jit(solution)/shard_map/gram/ppermute | solution.py:21
  71.5 0.7 copy.25
  72.3 0.8 %copy.19 = f32[432,48]{1,0:T(8,128)} copy(f32[432,48]{0,1:T(8,128)S(1)} %bitcast.11) | data formatting | bytes 165888 | tf_op jit(solution)/shard_map/residual/transpose | solution.py:497
  73.1 1.0 %collective-permute-done.24 = f32[24,128]{1,0:T(8,128)S(1)} collective-permute-done((f32[24,128]{1,0:T(8,128)S(1)}, f32[24,128]{1,0:T(8,128)S(1)}, u32[]{:S(2)}, u32[]{:S(2)}) %collective-permute-start.24) | collective-permute-done | bytes 12320 | tf_op jit(solution)/shard_map/gram/ppermute | solution.py:21
  74.2 0.1 fusion
  74.2 0.6 pad_maximum_fusion
  (23 shorter events, 0.1 us)
Async XLA Ops:
  1.7 5.4 %collective-permute-start = (bf16[48,2048]{1,0:T(8,128)(2,1)S(1)}, bf16[48,2048]{1,0:T(8,128)(2,1)S(1)}, u32[]{:S(2)}, u32[]{:S(2)}) collective-permute-start(bf16[48,2048]{1,0:T(8,128)(2,1)S(1)} %convert_element_type.9.own_panel), channel_id=1, source_target_pairs={{0,1},{1,0},{2,3},{3,2},{4,5},{5,4},{6,7},{7,6},{8,9},{9,8},{10,11... | collective-permute-start | bytes 589832 | tf_op jit(solution)/shard_map/gather/ppermute | solution.py:21
  2.2 9.3 %collective-permute-start.1 = (bf16[48,2048]{1,0:T(8,128)(2,1)S(1)}, bf16[48,2048]{1,0:T(8,128)(2,1)S(1)}, u32[]{:S(2)}, u32[]{:S(2)}) collective-permute-start(bf16[48,2048]{1,0:T(8,128)(2,1)S(1)} %convert_element_type.9.own_panel), channel_id=1, source_target_pairs={{0,2},{1,3},{2,0},{3,1},{4,6},{5,7},{6,4},{7,5},{8,10},{9,11},{10,... | collective-permute-start | bytes 589832 | tf_op jit(solution)/shard_map/gather/ppermute | solution.py:21
  4.7 11.2 %collective-permute-start.3 = (bf16[48,2048]{1,0:T(8,128)(2,1)S(1)}, bf16[48,2048]{1,0:T(8,128)(2,1)S(1)}, u32[]{:S(2)}, u32[]{:S(2)}) collective-permute-start(bf16[48,2048]{1,0:T(8,128)(2,1)S(1)} %convert_element_type.9.own_panel), channel_id=1, source_target_pairs={{0,4},{1,5},{2,6},{3,7},{4,0},{5,1},{6,2},{7,3},{8,12},{9,13},{10,... | collective-permute-start | bytes 589832 | tf_op jit(solution)/shard_map/gather/ppermute | solution.py:21
  6.3 9.7 %collective-permute-start.5 = (bf16[48,2048]{1,0:T(8,128)(2,1)S(1)}, bf16[48,2048]{1,0:T(8,128)(2,1)S(1)}, u32[]{:S(2)}, u32[]{:S(2)}) collective-permute-start(bf16[48,2048]{1,0:T(8,128)(2,1)S(1)} %convert_element_type.9.own_panel), channel_id=1, source_target_pairs={{0,6},{1,7},{2,4},{3,5},{4,2},{5,3},{6,0},{7,1},{8,14},{9,15},{10,... | collective-permute-start | bytes 589832 | tf_op jit(solution)/shard_map/gather/ppermute | solution.py:21
  11.5 5.7 %collective-permute-start.2 = (bf16[48,2048]{1,0:T(8,128)(2,1)S(1)}, bf16[48,2048]{1,0:T(8,128)(2,1)S(1)}, u32[]{:S(2)}, u32[]{:S(2)}) collective-permute-start(bf16[48,2048]{1,0:T(8,128)(2,1)S(1)} %gather.4.refs_0_), channel_id=1, source_target_pairs={{0,1},{1,0},{2,3},{3,2},{4,5},{5,4},{6,7},{7,6},{8,9},{9,8},{10,11... | collective-permute-start | bytes 589832 | tf_op jit(solution)/shard_map/gather/ppermute | solution.py:21
  15.9 1.4 %collective-permute-start.4 = (bf16[48,2048]{1,0:T(8,128)(2,1)S(1)}, bf16[48,2048]{1,0:T(8,128)(2,1)S(1)}, u32[]{:S(2)}, u32[]{:S(2)}) collective-permute-start(bf16[48,2048]{1,0:T(8,128)(2,1)S(1)} %gather.5.refs_1_), channel_id=1, source_target_pairs={{0,1},{1,0},{2,3},{3,2},{4,5},{5,4},{6,7},{7,6},{8,9},{9,8},{10,11... | collective-permute-start | bytes 589832 | tf_op jit(solution)/shard_map/gather/ppermute | solution.py:21
  15.9 1.7 %collective-permute-start.6 = (bf16[48,2048]{1,0:T(8,128)(2,1)S(1)}, bf16[48,2048]{1,0:T(8,128)(2,1)S(1)}, u32[]{:S(2)}, u32[]{:S(2)}) collective-permute-start(bf16[48,2048]{1,0:T(8,128)(2,1)S(1)} %gather.6.refs_2_), channel_id=1, source_target_pairs={{0,1},{1,0},{2,3},{3,2},{4,5},{5,4},{6,7},{7,6},{8,9},{9,8},{10,11... | collective-permute-start | bytes 589832 | tf_op jit(solution)/shard_map/gather/ppermute | solution.py:21
  19.7 9.6 %collective-permute-start.7 = (bf16[48,2048]{1,0:T(8,128)(2,1)S(1)}, bf16[48,2048]{1,0:T(8,128)(2,1)S(1)}, u32[]{:S(2)}, u32[]{:S(2)}) collective-permute-start(bf16[48,2048]{1,0:T(8,128)(2,1)S(1)} %get-tuple-element.23), channel_id=1, source_target_pairs={{0,8},{24,16},{8,24},{16,0},{1,9},{25,17},{9,25},{17,1},{2,10},{26... | collective-permute-start | bytes 589832 | tf_op jit(solution)/shard_map/late/ppermute | solution.py:447
  22.0 8.1 %copy-start.1 = (f32[48,2048]{1,0:T(8,128)S(1)}, f32[48,2048]{1,0:T(8,128)}, u32[]{:S(2)}) copy-start(f32[48,2048]{1,0:T(8,128)} %current.3) | copy-start | bytes 1179652
  22.0 8.1 %copy-start.2 = (f32[48,2048]{1,0:T(8,128)S(1)}, f32[48,2048]{1,0:T(8,128)}, u32[]{:S(2)}) copy-start(f32[48,2048]{1,0:T(8,128)} %previous.1) | copy-start | bytes 1179652
  22.0 8.1 %copy-start.4 = (f32[48,48]{1,0:T(8,128)S(1)}, f32[48,48]{1,0:T(8,128)}, u32[]{:S(2)}) copy-start(f32[48,48]{1,0:T(8,128)} %coupling.1) | copy-start | bytes 27652
  22.0 8.1 %copy-start.5 = (f32[2048]{0:T(1024)S(1)}, f32[2048]{0:T(1024)}, u32[]{:S(2)}) copy-start(f32[2048]{0:T(1024)} %param.14) | copy-start | bytes 24580
  24.5 11.5 %collective-permute-start.8 = (bf16[48,2048]{1,0:T(8,128)(2,1)S(1)}, bf16[48,2048]{1,0:T(8,128)(2,1)S(1)}, u32[]{:S(2)}, u32[]{:S(2)}) collective-permute-start(bf16[48,2048]{1,0:T(8,128)(2,1)S(1)} %get-tuple-element.24), channel_id=1, source_target_pairs={{0,24},{24,0},{1,25},{25,1},{2,26},{26,2},{3,27},{27,3},{4,28},{28... | collective-permute-start | bytes 589832 | tf_op jit(solution)/shard_map/late/ppermute | solution.py:451
  29.2 9.7 %collective-permute-start.10 = (bf16[48,2048]{1,0:T(8,128)(2,1)S(1)}, bf16[48,2048]{1,0:T(8,128)(2,1)S(1)}, u32[]{:S(2)}, u32[]{:S(2)}) collective-permute-start(bf16[48,2048]{1,0:T(8,128)(2,1)S(1)} %get-tuple-element.26), channel_id=1, source_target_pairs={{0,8},{8,0},{16,24},{24,16},{1,9},{9,1},{17,25},{25,17},{2,10},{10... | collective-permute-start | bytes 589832 | tf_op jit(solution)/shard_map/late/ppermute | solution.py:21
  29.4 9.5 %collective-permute-start.9 = (bf16[48,2048]{1,0:T(8,128)(2,1)S(1)}, bf16[48,2048]{1,0:T(8,128)(2,1)S(1)}, u32[]{:S(2)}, u32[]{:S(2)}) collective-permute-start(bf16[48,2048]{1,0:T(8,128)(2,1)S(1)} %add_convert_fusion), channel_id=1, source_target_pairs={{8,16},{16,8},{9,17},{17,9},{10,18},{18,10},{11,19},{19,11},{12,20... | collective-permute-start | bytes 589832 | tf_op jit(solution)/shard_map/late/ppermute | solution.py:452
  30.1 8.8 %copy-start = (f32[8,48,2048]{2,1,0:T(8,128)S(1)}, f32[8,48,2048]{2,1,0:T(8,128)}, u32[]{:S(2)}) copy-start(f32[8,48,2048]{2,1,0:T(8,128)} %param.13) | copy-start | bytes 9437188
  30.1 8.8 %copy-start.3 = (f32[2048]{0:T(1024)S(1)}, f32[2048]{0:T(1024)}, u32[]{:S(2)}) copy-start(f32[2048]{0:T(1024)} %param.15) | copy-start | bytes 24580
  40.7 1.3 %collective-permute-start.11 = (f32[12,8,128]{2,1,0:T(8,128)S(1)}, f32[12,8,128]{2,1,0:T(8,128)S(1)}, u32[]{:S(2)}, u32[]{:S(2)}) collective-permute-start(f32[12,8,128]{2,1,0:T(8,128)S(1)} %get-tuple-element.28), channel_id=1, source_target_pairs={{0,1},{1,0},{2,3},{3,2},{4,5},{5,4},{6,7},{7,6},{8,9},{9,8},{10,11... | collective-permute-start | bytes 147464 | tf_op jit(solution)/shard_map/coefficients/ppermute | solution.py:21
  42.0 5.6 %collective-permute-start.14 = (f32[12,8,128]{2,1,0:T(8,128)S(1)}, f32[12,8,128]{2,1,0:T(8,128)S(1)}, u32[]{:S(2)}, u32[]{:S(2)}) collective-permute-start(f32[12,8,128]{2,1,0:T(8,128)S(1)} %add.46), channel_id=1, source_target_pairs={{0,6},{1,25},{2,4},{3,27},{4,2},{5,29},{6,0},{7,31},{8,14},{9,17},... | collective-permute-start | bytes 147464 | tf_op jit(solution)/shard_map/coefficients/ppermute | solution.py:44
  45.5 4.1 %collective-permute-start.13 = (f32[12,8,128]{2,1,0:T(8,128)S(1)}, f32[12,8,128]{2,1,0:T(8,128)S(1)}, u32[]{:S(2)}, u32[]{:S(2)}) collective-permute-start(f32[12,8,128]{2,1,0:T(8,128)S(1)} %add.46), channel_id=1, source_target_pairs={{0,4},{1,17},{2,6},{3,19},{4,0},{5,21},{6,2},{7,23},{8,12},{9,25},... | collective-permute-start | bytes 147464 | tf_op jit(solution)/shard_map/coefficients/ppermute | solution.py:44
  45.5 4.1 %collective-permute-start.12 = (f32[12,8,128]{2,1,0:T(8,128)S(1)}, f32[12,8,128]{2,1,0:T(8,128)S(1)}, u32[]{:S(2)}, u32[]{:S(2)}) collective-permute-start(f32[12,8,128]{2,1,0:T(8,128)S(1)} %add.46), channel_id=1, source_target_pairs={{0,2},{1,9},{2,0},{3,11},{4,6},{5,13},{6,4},{7,15},{8,10},{9,1},{1... | collective-permute-start | bytes 147464 | tf_op jit(solution)/shard_map/coefficients/ppermute | solution.py:44
  49.6 6.1 %collective-permute-start.17 = (f32[12,8,128]{2,1,0:T(8,128)S(1)}, f32[12,8,128]{2,1,0:T(8,128)S(1)}, u32[]{:S(2)}, u32[]{:S(2)}) collective-permute-start(f32[12,8,128]{2,1,0:T(8,128)S(1)} %add_add_fusion.1), channel_id=1, source_target_pairs={{0,24},{1,7},{2,26},{3,5},{4,28},{5,3},{6,30},{7,1},{8,16},{9,15},... | collective-permute-start | bytes 147464 | tf_op jit(solution)/shard_map/coefficients/ppermute | solution.py:44
  51.6 5.0 %collective-permute-start.16 = (f32[12,8,128]{2,1,0:T(8,128)S(1)}, f32[12,8,128]{2,1,0:T(8,128)S(1)}, u32[]{:S(2)}, u32[]{:S(2)}) collective-permute-start(f32[12,8,128]{2,1,0:T(8,128)S(1)} %add_add_fusion.1), channel_id=1, source_target_pairs={{0,16},{1,5},{2,18},{3,7},{4,20},{5,1},{6,22},{7,3},{8,24},{9,13},... | collective-permute-start | bytes 147464 | tf_op jit(solution)/shard_map/coefficients/ppermute | solution.py:44
  53.1 4.1 %collective-permute-start.15 = (f32[12,8,128]{2,1,0:T(8,128)S(1)}, f32[12,8,128]{2,1,0:T(8,128)S(1)}, u32[]{:S(2)}, u32[]{:S(2)}) collective-permute-start(f32[12,8,128]{2,1,0:T(8,128)S(1)} %add_add_fusion.1), channel_id=1, source_target_pairs={{0,8},{1,3},{2,10},{3,1},{4,12},{5,7},{6,14},{7,5},{8,0},{9,11},{1... | collective-permute-start | bytes 147464 | tf_op jit(solution)/shard_map/coefficients/ppermute | solution.py:44
  57.2 1.3 %collective-permute-start.18 = (f32[12,8,128]{2,1,0:T(8,128)S(1)}, f32[12,8,128]{2,1,0:T(8,128)S(1)}, u32[]{:S(2)}, u32[]{:S(2)}) collective-permute-start(f32[12,8,128]{2,1,0:T(8,128)S(1)} %add_add_fusion.mine), channel_id=1, source_target_pairs={{0,1},{1,0},{2,3},{3,2},{4,5},{5,4},{6,7},{7,6},{8,9},{9,8},{10,11... | collective-permute-start | bytes 147464 | tf_op jit(solution)/shard_map/coefficients/ppermute | solution.py:21
  60.1 1.2 %collective-permute-start.19 = (f32[24,128]{1,0:T(8,128)S(1)}, f32[24,128]{1,0:T(8,128)S(1)}, u32[]{:S(2)}, u32[]{:S(2)}) collective-permute-start(f32[24,128]{1,0:T(8,128)S(1)} %get-tuple-element.32), channel_id=1, source_target_pairs={{0,1},{1,0},{2,3},{3,2},{4,5},{5,4},{6,7},{7,6},{8,9},{9,8},{10,11... | collective-permute-start | bytes 36872 | tf_op jit(solution)/shard_map/gram/ppermute | solution.py:21
  61.4 4.6 %collective-permute-start.22 = (f32[24,128]{1,0:T(8,128)S(1)}, f32[24,128]{1,0:T(8,128)S(1)}, u32[]{:S(2)}, u32[]{:S(2)}) collective-permute-start(f32[24,128]{1,0:T(8,128)S(1)} %add.53), channel_id=1, source_target_pairs={{0,6},{1,7},{2,4},{3,5},{4,2},{5,3},{6,0},{7,1},{8,14},{9,15},{10,... | collective-permute-start | bytes 36872 | tf_op jit(solution)/shard_map/gram/ppermute | solution.py:21
  62.8 3.7 %collective-permute-start.21 = (f32[24,128]{1,0:T(8,128)S(1)}, f32[24,128]{1,0:T(8,128)S(1)}, u32[]{:S(2)}, u32[]{:S(2)}) collective-permute-start(f32[24,128]{1,0:T(8,128)S(1)} %add.53), channel_id=1, source_target_pairs={{0,4},{1,5},{2,6},{3,7},{4,0},{5,1},{6,2},{7,3},{8,12},{9,13},{10,... | collective-permute-start | bytes 36872 | tf_op jit(solution)/shard_map/gram/ppermute | solution.py:21
  63.5 3.7 %collective-permute-start.20 = (f32[24,128]{1,0:T(8,128)S(1)}, f32[24,128]{1,0:T(8,128)S(1)}, u32[]{:S(2)}, u32[]{:S(2)}) collective-permute-start(f32[24,128]{1,0:T(8,128)S(1)} %add.53), channel_id=1, source_target_pairs={{0,2},{1,3},{2,0},{3,1},{4,6},{5,7},{6,4},{7,5},{8,10},{9,11},{10,... | collective-permute-start | bytes 36872 | tf_op jit(solution)/shard_map/gram/ppermute | solution.py:21
  67.2 6.0 %collective-permute-start.25 = (f32[24,128]{1,0:T(8,128)S(1)}, f32[24,128]{1,0:T(8,128)S(1)}, u32[]{:S(2)}, u32[]{:S(2)}) collective-permute-start(f32[24,128]{1,0:T(8,128)S(1)} %add_add_fusion.3), channel_id=1, source_target_pairs={{0,24},{8,16},{16,8},{24,0},{1,25},{9,17},{17,9},{25,1},{2,26},{10... | collective-permute-start | bytes 36872 | tf_op jit(solution)/shard_map/gram/ppermute | solution.py:21
  69.6 4.6 %collective-permute-start.24 = (f32[24,128]{1,0:T(8,128)S(1)}, f32[24,128]{1,0:T(8,128)S(1)}, u32[]{:S(2)}, u32[]{:S(2)}) collective-permute-start(f32[24,128]{1,0:T(8,128)S(1)} %add_add_fusion.3), channel_id=1, source_target_pairs={{0,16},{8,24},{16,0},{24,8},{1,17},{9,25},{17,1},{25,9},{2,18},{10... | collective-permute-start | bytes 36872 | tf_op jit(solution)/shard_map/gram/ppermute | solution.py:21
  69.6 4.6 %collective-permute-start.23 = (f32[24,128]{1,0:T(8,128)S(1)}, f32[24,128]{1,0:T(8,128)S(1)}, u32[]{:S(2)}, u32[]{:S(2)}) collective-permute-start(f32[24,128]{1,0:T(8,128)S(1)} %add_add_fusion.3), channel_id=1, source_target_pairs={{0,8},{8,0},{16,24},{24,16},{1,9},{9,1},{17,25},{25,17},{2,10},{10... | collective-permute-start | bytes 36872 | tf_op jit(solution)/shard_map/gram/ppermute | solution.py:21

commit v12 on v11

--- a/solution.py
+++ b/solution.py
@@ -109,6 +109,7 @@
     panel_buf[zero_panel, :, :LANES] = jnp.zeros((panel_buf.shape[1], LANES), jnp.bfloat16)
     f32, bf16, i32 = jnp.float32, jnp.bfloat16, jnp.int32
     slots, places = rows.shape[1], out.shape[1] - LANES
+    early_chunks = 3 * slots // CHUNK // 4
     targets = row_devs * slab_tiles
     bins = 2 * targets
 
@@ -128,7 +129,8 @@
     tile_f = col_f - slab_tiles * source_f
     far = row_devs - 1 - (row_owner ^ place[0])
     late_bin = targets + far * slab_tiles + row - row_owner * slab_tiles
-    bin_of = jnp.where(occupied, jnp.where(source < 2, row, late_bin), -1)
+    early = (source < 2) & (slot < early_chunks * CHUNK)
+    bin_of = jnp.where(occupied, jnp.where(early, row, late_bin), -1)
     member = (iota((bins, slots), 0) == bin_of).astype(f32)
     member_bf = member.astype(bf16)
     rank = jnp.sum(member * mm(member_bf, earlier), axis=0, keepdims=True)
@@ -157,11 +159,15 @@
     for copy in copies + [plan_copy]:
         copy.wait()
 
-    @pl.loop(0, chunks)
+    @pl.loop(0, jnp.minimum(chunks, early_chunks))
     def _(k):
         tile_copy(k).wait()
 
     add_products(plan, 0, 0, targets, held, panel_buf, acc)
+
+    @pl.loop(early_chunks, chunks)
+    def _(k):
+        tile_copy(k).wait()
 
 
 def field(word, low, high):
@@ -210,23 +216,20 @@
     sends = refs[len(odd) + 3 : -3]
     panel_buf, acc, sem = refs[-3:]
     copies = load_panels(panels, panel_buf, sem)
-    for mask, send in zip(masks, sends):
-        late_part(mask, place, plan, tiles, early, panel_buf, acc, copies)
-        put(send, acc)
-        copies = ()
-
-
-def late_kernel(masks, place, plan, panel_buf, tiles, early, *refs):
-    sends, acc = refs[:-1], refs[-1]
+    make_parts(masks, place, plan, tiles, early, panel_buf, acc, sends, copies)
+
+
+def make_parts(masks, place, plan, tiles, early, panel_buf, acc, sends, copies):
     for i, (mask, send) in enumerate(zip(masks, sends)):
         if i == 0 or mask != masks[i - 1]:
-            late_part(mask, place, plan, tiles, early, panel_buf, acc, ())
+            late_part(mask, place, plan, tiles, early, panel_buf, acc, copies)
+            copies = ()
         put(send, acc)
 
 
-def own_kernel(place, plan, panel_buf, tiles, early, current, previous, coupling, diag, base, acc):
-    late_part(0, place, plan, tiles, early, panel_buf, acc, ())
-    put(base, acc)
+def late_kernel(masks, place, plan, panel_buf, tiles, early, current, previous, coupling, diag, *refs):
+    sends, base, acc = refs[:-2], refs[-2], refs[-1]
+    make_parts(masks + [0], place, plan, tiles, early, panel_buf, acc, sends + (base,), ())
     base[...] += diag[...] * current[...] - jnp.dot(
         coupling[...],
         previous[...],
@@ -421,49 +424,40 @@
 
     with jax.named_scope("late"):
         relay = row_devs == 4
-        first_mask = 2 if relay else row_devs - 1
-        masks = [3, 3, 1] if relay else list(range(row_devs - 2, 0, -1))
+        first_masks = [2, 3, 3] if relay else [row_devs - 1]
+        last_masks = [1] if relay else list(range(row_devs - 2, 0, -1))
         part = jax.ShapeDtypeStruct((width, slab_len), bf16)
-        first, gathered = pl.pallas_call(
-            functools.partial(first_late_kernel, [first_mask], odd),
-            out_shape=[part, pltpu.VMEM(panel_shape, bf16)],
+        *firsts, gathered = pl.pallas_call(
+            functools.partial(first_late_kernel, first_masks, odd),
+            out_shape=([part, part, slab] if relay else [part]) + [pltpu.VMEM(panel_shape, bf16)],
             in_specs=smem(2) + anywhere * len(odd) + vmem(3),
-            out_specs=vmem(2),
+            out_specs=vmem(len(first_masks) + 1),
             scratch_shapes=[part_acc, pltpu.SemaphoreType.DMA((len(odd),))],
-            input_output_aliases={4 + len(odd): 1},
+            input_output_aliases={4 + len(odd): len(first_masks)},
             compiler_params=limit(8),
             cost_estimate=cost(width),
         )(place, plan, *[panels[m] for m in odd], held, early, gathered)
-        parts = pl.pallas_call(
-            functools.partial(late_kernel, masks),
-            out_shape=[part, slab, part] if relay else [part] * len(masks),
-            in_specs=smem(2) + vmem(3),
-            out_specs=vmem(len(masks)),
-            scratch_shapes=[part_acc],
-            compiler_params=limit(8),
-            cost_estimate=cost(width),
-        )(place, plan, gathered, held, early)
-        if relay:
-            first = lax.ppermute(first, "row", [(0, 1), (3, 2), (1, 3), (2, 0)])
-            joined = (parts[1] + first.astype(f32)).astype(bf16)
-            received = [
-                first,
-                lax.ppermute(parts[0], "row", [(0, 3), (3, 0)]),
-                lax.ppermute(joined, "row", [(1, 2), (2, 1)]),
-                swap(parts[2], "row", 1),
-            ]
-        else:
-            received = [swap(first, "row", first_mask)]
-            received += [swap(part, "row", m) for m, part in zip(masks, parts)]
-        base = pl.pallas_call(
-            own_kernel,
-            out_shape=slab,
+        *lasts, base = pl.pallas_call(
+            functools.partial(late_kernel, last_masks),
+            out_shape=[part] * len(last_masks) + [slab],
             in_specs=smem(2) + vmem(7),
-            out_specs=vmem(1)[0],
+            out_specs=vmem(len(last_masks) + 1),
             scratch_shapes=[part_acc],
             compiler_params=limit(8),
             cost_estimate=cost(width),
         )(place, plan, gathered, held, early, current_block, previous_block, previous_coupling, diag)
+        if relay:
+            first = lax.ppermute(firsts[0], "row", [(0, 1), (3, 2), (1, 3), (2, 0)])
+            joined = (firsts[2] + first.astype(f32)).astype(bf16)
+            received = [
+                first,
+                lax.ppermute(firsts[1], "row", [(0, 3), (3, 0)]),
+                swap(after(lasts[0], joined), "row", 1),
+                lax.ppermute(joined, "row", [(1, 2), (2, 1)]),
+            ]
+        else:
+            received = [swap(firsts[0], "row", first_masks[0])]
+            received += [swap(last, "row", m) for m, last in zip(last_masks, lasts)]
 
     basis_rows = (stored_count + 1) * width
     padded = (width, -(-basis_rows // LANES) * LANES)

time: 74.6 us -> 78.2 us (1.048)
  Pallas kernels: 15.6 us -> 23.4 us
  waiting for transfers between devices: 24.6 us -> 20.2 us
    pallas_call x3 -> x2, Pallas kernels: 6.96 us -> 11.2 us  [the longest x1 5.7 us: local(): pl.pallas_call(functools.partial(late_kernel, last_masks), out_shape=[par...]
    pallas_call x1, Pallas kernels: 4.46 us -> 8.1 us  [local(): pl.pallas_call(functools.partial(early_kernel, row_devs, col_devs, slab_t...]
    ppermute x2, waiting for transfers between devices: 3.61 us -> 0.01 us  [the longest x1 0.01 us: local(): first = lax.ppermute(firsts[0], 'row', [(0, 1), (3, 2), (1, 3), (2, 0)])]
    ppermute x2, starting transfers between devices: 6.92 us -> 3.89 us  [the longest x1 3.77 us: local(): lax.ppermute(firsts[1], 'row', [(0, 3), (3, 0)])]
    ppermute x6, starting transfers between devices: 8.59 us -> 10.3 us  [total_by_core(): values.append(lax.ppermute(value, ('row', 'col'), trades))]
    ppermute x17, starting transfers between devices: 13.5 us -> 14.7 us  [swap(): return lax.ppermute(value, axis, [(i, i ^ mask) for i in range(count)])]
    ppermute x17, waiting for transfers between devices: 14.4 us -> 13.5 us  [swap(): return lax.ppermute(value, axis, [(i, i ^ mask) for i in range(count)])]
  transfers between devices with their start and end apart: 26 -> 26, of which waited for: 17 -> 16; matrix products, arithmetic and copies ran while one was open for 2% -> 2% of each run, Pallas kernels for 13% -> 19%
where the time goes in v12:
time: 78.2 us; the launch traced here: 78.1 us
  starting transfers between devices  29.5 us (38%)
  Pallas kernels  23.4 us (30%)
  waiting for transfers between devices  20.2 us (26%)
  other arithmetic  1.8 us (2%)
  local copies, waits for them, and re-layouts  1.66 us (2%)
  between operations  1.51 us (2%)
    ppermute x17, starting transfers between devices, swap(): return lax.ppermute(value, axis, [(i, i ^ mask) for i in range(count)])  14.7 us
    ppermute x17, waiting for transfers between devices, swap(): return lax.ppermute(value, axis, [(i, i ^ mask) for i in range(count)])  13.5 us
    ppermute x6, starting transfers between devices, total_by_core(): values.append(lax.ppermute(value, ('row', 'col'), trades))  10.3 us
    pallas_call x1, Pallas kernels, local(): pl.pallas_call(functools.partial(early_kernel, row_devs, col_devs, slab_t...  8.1 us
    ppermute x6, waiting for transfers between devices, total_by_core(): values.append(lax.ppermute(value, ('row', 'col'), trades))  6.67 us
    pallas_call x1, Pallas kernels, local(): pl.pallas_call(functools.partial(late_kernel, last_masks), out_shape=[par...  5.7 us
    pallas_call x1, Pallas kernels, local(): pl.pallas_call(functools.partial(first_late_kernel, first_masks, odd), ou...  5.49 us
    ppermute x1, starting transfers between devices, local(): lax.ppermute(firsts[1], 'row', [(0, 3), (3, 0)])  3.77 us
  transfers between devices with their start and end apart: 26, of which 16 were waited for; matrix products, arithmetic and copies ran while one was open for 2% of the time, Pallas kernels for 19%

profile of v12, /device:TPU:0, one launch (start us, length us, event | category | flops | bytes accessed | tf_op | source)
XLA Modules:
  0.0 78.1 jit_solution(18137431143437691851)
XLA Ops:
  0.6 1.0 %convert_element_type.9.own_panel = bf16[48,2048]{1,0:T(8,128)(2,1)S(1)} convert(f32[48,2048]{1,0:T(8,128)} %current.3) | non-fusion elementwise | flops 98304 | bytes 589824 | tf_op jit(solution)/shard_map/gather/convert_element_type | solution.py:370
  1.7 0.5 collective-permute-start
  2.2 2.6 %collective-permute-start.1 = (bf16[48,2048]{1,0:T(8,128)(2,1)S(1)}, bf16[48,2048]{1,0:T(8,128)(2,1)S(1)}, u32[]{:S(2)}, u32[]{:S(2)}) collective-permute-start(bf16[48,2048]{1,0:T(8,128)(2,1)S(1)} %convert_element_type.9.own_panel), channel_id=1, source_target_pairs={{0,2},{1,3},{2,0},{3,1},{4,6},{5,7},{6,4},{7,5},{8,10},{9,11},{10,... | collective-permute-start | bytes 589832 | tf_op jit(solution)/shard_map/gather/ppermute | solution.py:21
  4.7 1.5 %collective-permute-start.3 = (bf16[48,2048]{1,0:T(8,128)(2,1)S(1)}, bf16[48,2048]{1,0:T(8,128)(2,1)S(1)}, u32[]{:S(2)}, u32[]{:S(2)}) collective-permute-start(bf16[48,2048]{1,0:T(8,128)(2,1)S(1)} %convert_element_type.9.own_panel), channel_id=1, source_target_pairs={{0,4},{1,5},{2,6},{3,7},{4,0},{5,1},{6,2},{7,3},{8,12},{9,13},{10,... | collective-permute-start | bytes 589832 | tf_op jit(solution)/shard_map/gather/ppermute | solution.py:21
  6.3 0.0 collective-permute-start.5
  6.9 0.1 pad_add_fusion.place
  7.0 0.0 collective-permute-done.near_panel
  7.0 8.1 %early.1 = (s32[1,896]{1,0:T(1,128)S(1)}, bf16[512,128,128]{2,1,0:T(8,128)(2,1)S(1)}, f32[65,48,128]{2,1,0:T(8,128)S(1)}, bf16[9,48,2048]{2,1,0:T(8,128)(2,1)S(1)}) custom-call(s32[2]{0:T(128)S(1)} %pad_add_fusion.place, s32[1]{0:T(128)S(6)} %copy.28.counts, s32[1,512]{1,0:T(1,128)} %bitcast.16, s32[1,512]{1,0:T(1,128)} %bitcast.17, ...), custom_call_target="tpu_custom_call" | custom-call | flops 805306368 | bytes 16777216 | tf_op jit(solution)/shard_map/early/pallas_call | solution.py:379
  15.1 0.0 collective-permute-done.1.value
  15.1 0.1 collective-permute-start.2
  15.2 0.7 collective-permute-done.3.value
  15.9 0.0 collective-permute-start.4
  15.9 0.0 collective-permute-done.5.value
  15.9 0.5 collective-permute-start.6
  16.4 0.8 gather.7.refs_5_
  17.2 0.0 collective-permute-done.2.refs_0_
  17.2 0.2 collective-permute-done.4.refs_1_
  17.4 0.3 collective-permute-done.6.refs_2_
  17.7 5.5 %late.3 = (bf16[48,2048]{1,0:T(8,128)(2,1)S(1)}, bf16[48,2048]{1,0:T(8,128)(2,1)S(1)}, f32[48,2048]{1,0:T(8,128)S(1)}, bf16[9,48,2048]{2,1,0:T(8,128)(2,1)S(1)}) custom-call(s32[2]{0:T(128)S(1)} %pad_add_fusion.place, s32[1,896]{1,0:T(1,128)S(1)} %get-tuple-element.19.plan, ...), custom_call_target="tpu_custom_call", output_to_operand_aliasing={{3}: (7, {})} | custom-call | flops 48 | bytes 1 | tf_op jit(solution)/shard_map/late/pallas_call | solution.py:430
  23.2 0.1 collective-permute-start.7
  23.3 3.8 %collective-permute-start.8 = (bf16[48,2048]{1,0:T(8,128)(2,1)S(1)}, bf16[48,2048]{1,0:T(8,128)(2,1)S(1)}, u32[]{:S(2)}, u32[]{:S(2)}) collective-permute-start(bf16[48,2048]{1,0:T(8,128)(2,1)S(1)} %get-tuple-element.26), channel_id=1, source_target_pairs={{0,24},{24,0},{1,25},{25,1},{2,26},{26,2},{3,27},{27,3},{4,28},{28... | collective-permute-start | bytes 589832 | tf_op jit(solution)/shard_map/late/ppermute | solution.py:454
  27.1 0.0 copy-start
  27.1 0.0 copy-start.3
  27.1 5.7 %late.4 = (bf16[48,2048]{1,0:T(8,128)(2,1)S(1)}, f32[48,2048]{1,0:T(8,128)S(1)}) custom-call(s32[2]{0:T(128)S(1)} %pad_add_fusion.place, s32[1,896]{1,0:T(1,128)S(1)} %get-tuple-element.19.plan, bf16[9,48,2048]{2,1,0:T(8,128)(2,1)S(1)} %get-tuple-element.23.panel_buf, bf16[512,128,128]{2,1,0:T(8,128)(2,1)S(1)} %get-tuple-element.21.refs_3_.tiles, ...), custom_call_target="tpu_custom_call" | custom-call | flops 48 | bytes 1 | tf_op jit(solution)/shard_map/late/pallas_call | solution.py:440
  32.8 0.0 collective-permute-done.7.refs_0_
  32.9 1.2 %collective-permute-start.9 = (bf16[48,2048]{1,0:T(8,128)(2,1)S(1)}, bf16[48,2048]{1,0:T(8,128)(2,1)S(1)}, u32[]{:S(2)}, u32[]{:S(2)}) collective-permute-start(bf16[48,2048]{1,0:T(8,128)(2,1)S(1)} %late.5), channel_id=1, source_target_pairs={{0,8},{8,0},{16,24},{24,16},{1,9},{9,1},{17,25},{25,17},{2,10},{10... | collective-permute-start | bytes 589832 | tf_op jit(solution)/shard_map/late/ppermute | solution.py:21
  34.1 0.7 collective-permute-start.10
  34.8 4.1 %collective-permute-done.9.refs_2_ = bf16[48,2048]{1,0:T(8,128)(2,1)S(1)} collective-permute-done((bf16[48,2048]{1,0:T(8,128)(2,1)S(1)}, bf16[48,2048]{1,0:T(8,128)(2,1)S(1)}, u32[]{:S(2)}, u32[]{:S(2)}) %collective-permute-start.9) | collective-permute-done | bytes 196640 | tf_op jit(solution)/shard_map/late/ppermute | solution.py:21
  38.9 0.0 collective-permute-done.10.refs_3_
  38.9 1.7 %coefficients.1 = (f32[48,2048]{1,0:T(8,128)S(1)}, f32[12,8,128]{2,1,0:T(8,128)S(1)}, f32[12,8,128]{2,1,0:T(8,128)S(1)}) custom-call(s32[2]{0:T(128)S(1)} %pad_add_fusion.place, f32[48,2048]{1,0:T(8,128)S(1)} %get-tuple-element.24.base, bf16[48,2048]{1,0:T(8,128)(2,1)S(1)} %collective-permute-done.7.refs_0_, ...), custom_call_target="tpu_custom_call" | custom-call | tf_op jit(solution)/shard_map/coefficients/pallas_call | solution.py:466
  40.7 0.1 collective-permute-start.11
  40.7 1.2 %collective-permute-done.11 = f32[12,8,128]{2,1,0:T(8,128)S(1)} collective-permute-done((f32[12,8,128]{2,1,0:T(8,128)S(1)}, f32[12,8,128]{2,1,0:T(8,128)S(1)}, u32[]{:S(2)}, u32[]{:S(2)}) %collective-permute-start.11) | collective-permute-done | bytes 49184 | tf_op jit(solution)/shard_map/coefficients/ppermute | solution.py:21
  42.0 1.1 %collective-permute-start.14 = (f32[12,8,128]{2,1,0:T(8,128)S(1)}, f32[12,8,128]{2,1,0:T(8,128)S(1)}, u32[]{:S(2)}, u32[]{:S(2)}) collective-permute-start(f32[12,8,128]{2,1,0:T(8,128)S(1)} %add.46), channel_id=1, source_target_pairs={{0,6},{1,25},{2,4},{3,27},{4,2},{5,29},{6,0},{7,31},{8,14},{9,17},... | collective-permute-start | bytes 147464 | tf_op jit(solution)/shard_map/coefficients/ppermute | solution.py:44
  43.0 1.3 %collective-permute-start.13 = (f32[12,8,128]{2,1,0:T(8,128)S(1)}, f32[12,8,128]{2,1,0:T(8,128)S(1)}, u32[]{:S(2)}, u32[]{:S(2)}) collective-permute-start(f32[12,8,128]{2,1,0:T(8,128)S(1)} %add.46), channel_id=1, source_target_pairs={{0,4},{1,17},{2,6},{3,19},{4,0},{5,21},{6,2},{7,23},{8,12},{9,25},... | collective-permute-start | bytes 147464 | tf_op jit(solution)/shard_map/coefficients/ppermute | solution.py:44
  44.3 1.2 %collective-permute-start.12 = (f32[12,8,128]{2,1,0:T(8,128)S(1)}, f32[12,8,128]{2,1,0:T(8,128)S(1)}, u32[]{:S(2)}, u32[]{:S(2)}) collective-permute-start(f32[12,8,128]{2,1,0:T(8,128)S(1)} %add.46), channel_id=1, source_target_pairs={{0,2},{1,9},{2,0},{3,11},{4,6},{5,13},{6,4},{7,15},{8,10},{9,1},{1... | collective-permute-start | bytes 147464 | tf_op jit(solution)/shard_map/coefficients/ppermute | solution.py:44
  45.5 1.5 %collective-permute-done.14 = f32[12,8,128]{2,1,0:T(8,128)S(1)} collective-permute-done((f32[12,8,128]{2,1,0:T(8,128)S(1)}, f32[12,8,128]{2,1,0:T(8,128)S(1)}, u32[]{:S(2)}, u32[]{:S(2)}) %collective-permute-start.14) | collective-permute-done | bytes 49184 | tf_op jit(solution)/shard_map/coefficients/ppermute | solution.py:44
  47.0 0.5 collective-permute-done.13
  47.5 0.9 %collective-permute-done.12 = f32[12,8,128]{2,1,0:T(8,128)S(1)} collective-permute-done((f32[12,8,128]{2,1,0:T(8,128)S(1)}, f32[12,8,128]{2,1,0:T(8,128)S(1)}, u32[]{:S(2)}, u32[]{:S(2)}) %collective-permute-start.12) | collective-permute-done | bytes 49184 | tf_op jit(solution)/shard_map/coefficients/ppermute | solution.py:44
  48.4 4.0 %collective-permute-start.17 = (f32[12,8,128]{2,1,0:T(8,128)S(1)}, f32[12,8,128]{2,1,0:T(8,128)S(1)}, u32[]{:S(2)}, u32[]{:S(2)}) collective-permute-start(f32[12,8,128]{2,1,0:T(8,128)S(1)} %add_add_fusion.1), channel_id=1, source_target_pairs={{0,24},{1,7},{2,26},{3,5},{4,28},{5,3},{6,30},{7,1},{8,16},{9,15},... | collective-permute-start | bytes 147464 | tf_op jit(solution)/shard_map/coefficients/ppermute | solution.py:44
  52.4 2.4 %collective-permute-start.16 = (f32[12,8,128]{2,1,0:T(8,128)S(1)}, f32[12,8,128]{2,1,0:T(8,128)S(1)}, u32[]{:S(2)}, u32[]{:S(2)}) collective-permute-start(f32[12,8,128]{2,1,0:T(8,128)S(1)} %add_add_fusion.1), channel_id=1, source_target_pairs={{0,16},{1,5},{2,18},{3,7},{4,20},{5,1},{6,22},{7,3},{8,24},{9,13},... | collective-permute-start | bytes 147464 | tf_op jit(solution)/shard_map/coefficients/ppermute | solution.py:44
  54.8 0.3 collective-permute-start.15
  55.2 0.0 collective-permute-done.17
  55.2 2.3 %collective-permute-done.16 = f32[12,8,128]{2,1,0:T(8,128)S(1)} collective-permute-done((f32[12,8,128]{2,1,0:T(8,128)S(1)}, f32[12,8,128]{2,1,0:T(8,128)S(1)}, u32[]{:S(2)}, u32[]{:S(2)}) %collective-permute-start.16) | collective-permute-done | bytes 49184 | tf_op jit(solution)/shard_map/coefficients/ppermute | solution.py:44
  57.4 1.5 %collective-permute-done.15 = f32[12,8,128]{2,1,0:T(8,128)S(1)} collective-permute-done((f32[12,8,128]{2,1,0:T(8,128)S(1)}, f32[12,8,128]{2,1,0:T(8,128)S(1)}, u32[]{:S(2)}, u32[]{:S(2)}) %collective-permute-start.15) | collective-permute-done | bytes 49184 | tf_op jit(solution)/shard_map/coefficients/ppermute | solution.py:44
  58.9 0.1 collective-permute-start.18
  59.0 1.2 %collective-permute-done.18.other = f32[12,8,128]{2,1,0:T(8,128)S(1)} collective-permute-done((f32[12,8,128]{2,1,0:T(8,128)S(1)}, f32[12,8,128]{2,1,0:T(8,128)S(1)}, u32[]{:S(2)}, u32[]{:S(2)}) %collective-permute-start.18) | collective-permute-done | bytes 49184 | tf_op jit(solution)/shard_map/coefficients/ppermute | solution.py:21
  60.2 1.6 %residual.1 = (f32[48,2048]{1,0:T(8,128)S(1)}, f32[48,432]{1,0:T(8,128)S(1)}, f32[24,128]{1,0:T(8,128)S(1)}) custom-call(s32[2]{0:T(128)S(1)} %pad_add_fusion.place, f32[12,8,128]{2,1,0:T(8,128)S(1)} %add_add_fusion.mine, f32[12,8,128]{2,1,0:T(8,128)S(1)} %collective-permute-done.18.other, f32[48,2048]{1,0:T(8,128)S(1)} %get-tuple-element.31.recurrence, ...), custom_call_target="tpu_custom_call" | custom-call | tf_op jit(solution)/shard_map/residual/pallas_call | solution.py:479
  61.9 0.2 collective-permute-start.19
  62.1 1.0 %collective-permute-done.19 = f32[24,128]{1,0:T(8,128)S(1)} collective-permute-done((f32[24,128]{1,0:T(8,128)S(1)}, f32[24,128]{1,0:T(8,128)S(1)}, u32[]{:S(2)}, u32[]{:S(2)}) %collective-permute-start.19) | collective-permute-done | bytes 12320 | tf_op jit(solution)/shard_map/gram/ppermute | solution.py:21
  63.1 2.8 %collective-permute-start.22 = (f32[24,128]{1,0:T(8,128)S(1)}, f32[24,128]{1,0:T(8,128)S(1)}, u32[]{:S(2)}, u32[]{:S(2)}) collective-permute-start(f32[24,128]{1,0:T(8,128)S(1)} %add.53), channel_id=1, source_target_pairs={{0,6},{1,7},{2,4},{3,5},{4,2},{5,3},{6,0},{7,1},{8,14},{9,15},{10,... | collective-permute-start | bytes 36872 | tf_op jit(solution)/shard_map/gram/ppermute | solution.py:21
  65.9 0.5 collective-permute-start.21
  66.5 0.1 collective-permute-start.20
  66.6 1.1 %collective-permute-done.22 = f32[24,128]{1,0:T(8,128)S(1)} collective-permute-done((f32[24,128]{1,0:T(8,128)S(1)}, f32[24,128]{1,0:T(8,128)S(1)}, u32[]{:S(2)}, u32[]{:S(2)}) %collective-permute-start.22) | collective-permute-done | bytes 12320 | tf_op jit(solution)/shard_map/gram/ppermute | solution.py:21
  67.7 1.9 %collective-permute-done.21 = f32[24,128]{1,0:T(8,128)S(1)} collective-permute-done((f32[24,128]{1,0:T(8,128)S(1)}, f32[24,128]{1,0:T(8,128)S(1)}, u32[]{:S(2)}, u32[]{:S(2)}) %collective-permute-start.21) | collective-permute-done | bytes 12320 | tf_op jit(solution)/shard_map/gram/ppermute | solution.py:21
  69.6 0.5 collective-permute-done.20
  70.2 2.6 %collective-permute-start.25 = (f32[24,128]{1,0:T(8,128)S(1)}, f32[24,128]{1,0:T(8,128)S(1)}, u32[]{:S(2)}, u32[]{:S(2)}) collective-permute-start(f32[24,128]{1,0:T(8,128)S(1)} %add_add_fusion.3), channel_id=1, source_target_pairs={{0,24},{8,16},{16,8},{24,0},{1,25},{9,17},{17,9},{25,1},{2,26},{10... | collective-permute-start | bytes 36872 | tf_op jit(solution)/shard_map/gram/ppermute | solution.py:21
  72.8 0.0 collective-permute-start.24
  72.8 1.7 %collective-permute-start.23 = (f32[24,128]{1,0:T(8,128)S(1)}, f32[24,128]{1,0:T(8,128)S(1)}, u32[]{:S(2)}, u32[]{:S(2)}) collective-permute-start(f32[24,128]{1,0:T(8,128)S(1)} %add_add_fusion.3), channel_id=1, source_target_pairs={{0,8},{8,0},{16,24},{24,16},{1,9},{9,1},{17,25},{25,17},{2,10},{10... | collective-permute-start | bytes 36872 | tf_op jit(solution)/shard_map/gram/ppermute | solution.py:21
  74.6 0.7 copy.27
  75.3 0.8 %copy.20 = f32[432,48]{1,0:T(8,128)} copy(f32[432,48]{0,1:T(8,128)S(1)} %bitcast.11) | data formatting | bytes 165888 | tf_op jit(solution)/shard_map/residual/transpose | solution.py:491
  76.1 1.3 %collective-permute-done.24 = f32[24,128]{1,0:T(8,128)S(1)} collective-permute-done((f32[24,128]{1,0:T(8,128)S(1)}, f32[24,128]{1,0:T(8,128)S(1)}, u32[]{:S(2)}, u32[]{:S(2)}) %collective-permute-start.24) | collective-permute-done | bytes 12320 | tf_op jit(solution)/shard_map/gram/ppermute | solution.py:21
  77.4 0.0 collective-permute-done.23
  77.4 0.1 fusion
  77.5 0.6 pad_maximum_fusion
  (23 shorter events, 0.1 us)
Async XLA Ops:
  1.7 5.4 %collective-permute-start = (bf16[48,2048]{1,0:T(8,128)(2,1)S(1)}, bf16[48,2048]{1,0:T(8,128)(2,1)S(1)}, u32[]{:S(2)}, u32[]{:S(2)}) collective-permute-start(bf16[48,2048]{1,0:T(8,128)(2,1)S(1)} %convert_element_type.9.own_panel), channel_id=1, source_target_pairs={{0,1},{1,0},{2,3},{3,2},{4,5},{5,4},{6,7},{7,6},{8,9},{9,8},{10,11... | collective-permute-start | bytes 589832 | tf_op jit(solution)/shard_map/gather/ppermute | solution.py:21
  2.2 13.0 %collective-permute-start.1 = (bf16[48,2048]{1,0:T(8,128)(2,1)S(1)}, bf16[48,2048]{1,0:T(8,128)(2,1)S(1)}, u32[]{:S(2)}, u32[]{:S(2)}) collective-permute-start(bf16[48,2048]{1,0:T(8,128)(2,1)S(1)} %convert_element_type.9.own_panel), channel_id=1, source_target_pairs={{0,2},{1,3},{2,0},{3,1},{4,6},{5,7},{6,4},{7,5},{8,10},{9,11},{10,... | collective-permute-start | bytes 589832 | tf_op jit(solution)/shard_map/gather/ppermute | solution.py:21
  4.7 11.2 %collective-permute-start.3 = (bf16[48,2048]{1,0:T(8,128)(2,1)S(1)}, bf16[48,2048]{1,0:T(8,128)(2,1)S(1)}, u32[]{:S(2)}, u32[]{:S(2)}) collective-permute-start(bf16[48,2048]{1,0:T(8,128)(2,1)S(1)} %convert_element_type.9.own_panel), channel_id=1, source_target_pairs={{0,4},{1,5},{2,6},{3,7},{4,0},{5,1},{6,2},{7,3},{8,12},{9,13},{10,... | collective-permute-start | bytes 589832 | tf_op jit(solution)/shard_map/gather/ppermute | solution.py:21
  6.3 9.7 %collective-permute-start.5 = (bf16[48,2048]{1,0:T(8,128)(2,1)S(1)}, bf16[48,2048]{1,0:T(8,128)(2,1)S(1)}, u32[]{:S(2)}, u32[]{:S(2)}) collective-permute-start(bf16[48,2048]{1,0:T(8,128)(2,1)S(1)} %convert_element_type.9.own_panel), channel_id=1, source_target_pairs={{0,6},{1,7},{2,4},{3,5},{4,2},{5,3},{6,0},{7,1},{8,14},{9,15},{10,... | collective-permute-start | bytes 589832 | tf_op jit(solution)/shard_map/gather/ppermute | solution.py:21
  15.1 2.1 %collective-permute-start.2 = (bf16[48,2048]{1,0:T(8,128)(2,1)S(1)}, bf16[48,2048]{1,0:T(8,128)(2,1)S(1)}, u32[]{:S(2)}, u32[]{:S(2)}) collective-permute-start(bf16[48,2048]{1,0:T(8,128)(2,1)S(1)} %gather.4.refs_0_), channel_id=1, source_target_pairs={{0,1},{1,0},{2,3},{3,2},{4,5},{5,4},{6,7},{7,6},{8,9},{9,8},{10,11... | collective-permute-start | bytes 589832 | tf_op jit(solution)/shard_map/gather/ppermute | solution.py:21
  15.9 1.4 %collective-permute-start.4 = (bf16[48,2048]{1,0:T(8,128)(2,1)S(1)}, bf16[48,2048]{1,0:T(8,128)(2,1)S(1)}, u32[]{:S(2)}, u32[]{:S(2)}) collective-permute-start(bf16[48,2048]{1,0:T(8,128)(2,1)S(1)} %gather.5.refs_1_), channel_id=1, source_target_pairs={{0,1},{1,0},{2,3},{3,2},{4,5},{5,4},{6,7},{7,6},{8,9},{9,8},{10,11... | collective-permute-start | bytes 589832 | tf_op jit(solution)/shard_map/gather/ppermute | solution.py:21
  15.9 1.7 %collective-permute-start.6 = (bf16[48,2048]{1,0:T(8,128)(2,1)S(1)}, bf16[48,2048]{1,0:T(8,128)(2,1)S(1)}, u32[]{:S(2)}, u32[]{:S(2)}) collective-permute-start(bf16[48,2048]{1,0:T(8,128)(2,1)S(1)} %gather.6.refs_2_), channel_id=1, source_target_pairs={{0,1},{1,0},{2,3},{3,2},{4,5},{5,4},{6,7},{7,6},{8,9},{9,8},{10,11... | collective-permute-start | bytes 589832 | tf_op jit(solution)/shard_map/gather/ppermute | solution.py:21
  17.6 9.4 %copy-start.1 = (f32[48,2048]{1,0:T(8,128)S(1)}, f32[48,2048]{1,0:T(8,128)}, u32[]{:S(2)}) copy-start(f32[48,2048]{1,0:T(8,128)} %current.3) | copy-start | bytes 1179652
  17.6 9.4 %copy-start.2 = (f32[48,2048]{1,0:T(8,128)S(1)}, f32[48,2048]{1,0:T(8,128)}, u32[]{:S(2)}) copy-start(f32[48,2048]{1,0:T(8,128)} %previous.1) | copy-start | bytes 1179652
  17.6 9.4 %copy-start.4 = (f32[48,48]{1,0:T(8,128)S(1)}, f32[48,48]{1,0:T(8,128)}, u32[]{:S(2)}) copy-start(f32[48,48]{1,0:T(8,128)} %coupling.1) | copy-start | bytes 27652
  17.7 9.4 %copy-start.5 = (f32[2048]{0:T(1024)S(1)}, f32[2048]{0:T(1024)}, u32[]{:S(2)}) copy-start(f32[2048]{0:T(1024)} %param.14) | copy-start | bytes 24580
  23.2 9.7 %collective-permute-start.7 = (bf16[48,2048]{1,0:T(8,128)(2,1)S(1)}, bf16[48,2048]{1,0:T(8,128)(2,1)S(1)}, u32[]{:S(2)}, u32[]{:S(2)}) collective-permute-start(bf16[48,2048]{1,0:T(8,128)(2,1)S(1)} %get-tuple-element.25), channel_id=1, source_target_pairs={{0,8},{24,16},{8,24},{16,0},{1,9},{25,17},{9,25},{17,1},{2,10},{26... | collective-permute-start | bytes 589832 | tf_op jit(solution)/shard_map/late/ppermute | solution.py:450
  23.3 11.5 %collective-permute-start.8 = (bf16[48,2048]{1,0:T(8,128)(2,1)S(1)}, bf16[48,2048]{1,0:T(8,128)(2,1)S(1)}, u32[]{:S(2)}, u32[]{:S(2)}) collective-permute-start(bf16[48,2048]{1,0:T(8,128)(2,1)S(1)} %get-tuple-element.26), channel_id=1, source_target_pairs={{0,24},{24,0},{1,25},{25,1},{2,26},{26,2},{3,27},{27,3},{4,28},{28... | collective-permute-start | bytes 589832 | tf_op jit(solution)/shard_map/late/ppermute | solution.py:454
  27.1 11.8 %copy-start = (f32[8,48,2048]{2,1,0:T(8,128)S(1)}, f32[8,48,2048]{2,1,0:T(8,128)}, u32[]{:S(2)}) copy-start(f32[8,48,2048]{2,1,0:T(8,128)} %param.13) | copy-start | bytes 9437188
  27.1 11.8 %copy-start.3 = (f32[2048]{0:T(1024)S(1)}, f32[2048]{0:T(1024)}, u32[]{:S(2)}) copy-start(f32[2048]{0:T(1024)} %param.15) | copy-start | bytes 24580
  32.9 6.0 %collective-permute-start.9 = (bf16[48,2048]{1,0:T(8,128)(2,1)S(1)}, bf16[48,2048]{1,0:T(8,128)(2,1)S(1)}, u32[]{:S(2)}, u32[]{:S(2)}) collective-permute-start(bf16[48,2048]{1,0:T(8,128)(2,1)S(1)} %late.5), channel_id=1, source_target_pairs={{0,8},{8,0},{16,24},{24,16},{1,9},{9,1},{17,25},{25,17},{2,10},{10... | collective-permute-start | bytes 589832 | tf_op jit(solution)/shard_map/late/ppermute | solution.py:21
  34.1 4.7 %collective-permute-start.10 = (bf16[48,2048]{1,0:T(8,128)(2,1)S(1)}, bf16[48,2048]{1,0:T(8,128)(2,1)S(1)}, u32[]{:S(2)}, u32[]{:S(2)}) collective-permute-start(bf16[48,2048]{1,0:T(8,128)(2,1)S(1)} %add_convert_fusion.earlier), channel_id=1, source_target_pairs={{8,16},{16,8},{9,17},{17,9},{10,18},{18,10},{11,19},{19,11},{12,20... | collective-permute-start | bytes 589832 | tf_op jit(solution)/shard_map/late/ppermute | solution.py:456
  40.7 1.3 %collective-permute-start.11 = (f32[12,8,128]{2,1,0:T(8,128)S(1)}, f32[12,8,128]{2,1,0:T(8,128)S(1)}, u32[]{:S(2)}, u32[]{:S(2)}) collective-permute-start(f32[12,8,128]{2,1,0:T(8,128)S(1)} %get-tuple-element.30), channel_id=1, source_target_pairs={{0,1},{1,0},{2,3},{3,2},{4,5},{5,4},{6,7},{7,6},{8,9},{9,8},{10,11... | collective-permute-start | bytes 147464 | tf_op jit(solution)/shard_map/coefficients/ppermute | solution.py:21
  42.0 5.1 %collective-permute-start.14 = (f32[12,8,128]{2,1,0:T(8,128)S(1)}, f32[12,8,128]{2,1,0:T(8,128)S(1)}, u32[]{:S(2)}, u32[]{:S(2)}) collective-permute-start(f32[12,8,128]{2,1,0:T(8,128)S(1)} %add.46), channel_id=1, source_target_pairs={{0,6},{1,25},{2,4},{3,27},{4,2},{5,29},{6,0},{7,31},{8,14},{9,17},... | collective-permute-start | bytes 147464 | tf_op jit(solution)/shard_map/coefficients/ppermute | solution.py:44
  43.0 4.5 %collective-permute-start.13 = (f32[12,8,128]{2,1,0:T(8,128)S(1)}, f32[12,8,128]{2,1,0:T(8,128)S(1)}, u32[]{:S(2)}, u32[]{:S(2)}) collective-permute-start(f32[12,8,128]{2,1,0:T(8,128)S(1)} %add.46), channel_id=1, source_target_pairs={{0,4},{1,17},{2,6},{3,19},{4,0},{5,21},{6,2},{7,23},{8,12},{9,25},... | collective-permute-start | bytes 147464 | tf_op jit(solution)/shard_map/coefficients/ppermute | solution.py:44
  44.3 4.1 %collective-permute-start.12 = (f32[12,8,128]{2,1,0:T(8,128)S(1)}, f32[12,8,128]{2,1,0:T(8,128)S(1)}, u32[]{:S(2)}, u32[]{:S(2)}) collective-permute-start(f32[12,8,128]{2,1,0:T(8,128)S(1)} %add.46), channel_id=1, source_target_pairs={{0,2},{1,9},{2,0},{3,11},{4,6},{5,13},{6,4},{7,15},{8,10},{9,1},{1... | collective-permute-start | bytes 147464 | tf_op jit(solution)/shard_map/coefficients/ppermute | solution.py:44
  48.4 6.7 %collective-permute-start.17 = (f32[12,8,128]{2,1,0:T(8,128)S(1)}, f32[12,8,128]{2,1,0:T(8,128)S(1)}, u32[]{:S(2)}, u32[]{:S(2)}) collective-permute-start(f32[12,8,128]{2,1,0:T(8,128)S(1)} %add_add_fusion.1), channel_id=1, source_target_pairs={{0,24},{1,7},{2,26},{3,5},{4,28},{5,3},{6,30},{7,1},{8,16},{9,15},... | collective-permute-start | bytes 147464 | tf_op jit(solution)/shard_map/coefficients/ppermute | solution.py:44
  52.4 5.0 %collective-permute-start.16 = (f32[12,8,128]{2,1,0:T(8,128)S(1)}, f32[12,8,128]{2,1,0:T(8,128)S(1)}, u32[]{:S(2)}, u32[]{:S(2)}) collective-permute-start(f32[12,8,128]{2,1,0:T(8,128)S(1)} %add_add_fusion.1), channel_id=1, source_target_pairs={{0,16},{1,5},{2,18},{3,7},{4,20},{5,1},{6,22},{7,3},{8,24},{9,13},... | collective-permute-start | bytes 147464 | tf_op jit(solution)/shard_map/coefficients/ppermute | solution.py:44
  54.8 4.1 %collective-permute-start.15 = (f32[12,8,128]{2,1,0:T(8,128)S(1)}, f32[12,8,128]{2,1,0:T(8,128)S(1)}, u32[]{:S(2)}, u32[]{:S(2)}) collective-permute-start(f32[12,8,128]{2,1,0:T(8,128)S(1)} %add_add_fusion.1), channel_id=1, source_target_pairs={{0,8},{1,3},{2,10},{3,1},{4,12},{5,7},{6,14},{7,5},{8,0},{9,11},{1... | collective-permute-start | bytes 147464 | tf_op jit(solution)/shard_map/coefficients/ppermute | solution.py:44
  58.9 1.3 %collective-permute-start.18 = (f32[12,8,128]{2,1,0:T(8,128)S(1)}, f32[12,8,128]{2,1,0:T(8,128)S(1)}, u32[]{:S(2)}, u32[]{:S(2)}) collective-permute-start(f32[12,8,128]{2,1,0:T(8,128)S(1)} %add_add_fusion.mine), channel_id=1, source_target_pairs={{0,1},{1,0},{2,3},{3,2},{4,5},{5,4},{6,7},{7,6},{8,9},{9,8},{10,11... | collective-permute-start | bytes 147464 | tf_op jit(solution)/shard_map/coefficients/ppermute | solution.py:21
  61.9 1.2 %collective-permute-start.19 = (f32[24,128]{1,0:T(8,128)S(1)}, f32[24,128]{1,0:T(8,128)S(1)}, u32[]{:S(2)}, u32[]{:S(2)}) collective-permute-start(f32[24,128]{1,0:T(8,128)S(1)} %get-tuple-element.34), channel_id=1, source_target_pairs={{0,1},{1,0},{2,3},{3,2},{4,5},{5,4},{6,7},{7,6},{8,9},{9,8},{10,11... | collective-permute-start | bytes 36872 | tf_op jit(solution)/shard_map/gram/ppermute | solution.py:21
  63.1 4.6 %collective-permute-start.22 = (f32[24,128]{1,0:T(8,128)S(1)}, f32[24,128]{1,0:T(8,128)S(1)}, u32[]{:S(2)}, u32[]{:S(2)}) collective-permute-start(f32[24,128]{1,0:T(8,128)S(1)} %add.53), channel_id=1, source_target_pairs={{0,6},{1,7},{2,4},{3,5},{4,2},{5,3},{6,0},{7,1},{8,14},{9,15},{10,... | collective-permute-start | bytes 36872 | tf_op jit(solution)/shard_map/gram/ppermute | solution.py:21
  65.9 3.7 %collective-permute-start.21 = (f32[24,128]{1,0:T(8,128)S(1)}, f32[24,128]{1,0:T(8,128)S(1)}, u32[]{:S(2)}, u32[]{:S(2)}) collective-permute-start(f32[24,128]{1,0:T(8,128)S(1)} %add.53), channel_id=1, source_target_pairs={{0,4},{1,5},{2,6},{3,7},{4,0},{5,1},{6,2},{7,3},{8,12},{9,13},{10,... | collective-permute-start | bytes 36872 | tf_op jit(solution)/shard_map/gram/ppermute | solution.py:21
  66.5 3.7 %collective-permute-start.20 = (f32[24,128]{1,0:T(8,128)S(1)}, f32[24,128]{1,0:T(8,128)S(1)}, u32[]{:S(2)}, u32[]{:S(2)}) collective-permute-start(f32[24,128]{1,0:T(8,128)S(1)} %add.53), channel_id=1, source_target_pairs={{0,2},{1,3},{2,0},{3,1},{4,6},{5,7},{6,4},{7,5},{8,10},{9,11},{10,... | collective-permute-start | bytes 36872 | tf_op jit(solution)/shard_map/gram/ppermute | solution.py:21
  70.2 6.0 %collective-permute-start.25 = (f32[24,128]{1,0:T(8,128)S(1)}, f32[24,128]{1,0:T(8,128)S(1)}, u32[]{:S(2)}, u32[]{:S(2)}) collective-permute-start(f32[24,128]{1,0:T(8,128)S(1)} %add_add_fusion.3), channel_id=1, source_target_pairs={{0,24},{8,16},{16,8},{24,0},{1,25},{9,17},{17,9},{25,1},{2,26},{10... | collective-permute-start | bytes 36872 | tf_op jit(solution)/shard_map/gram/ppermute | solution.py:21
  72.8 4.6 %collective-permute-start.24 = (f32[24,128]{1,0:T(8,128)S(1)}, f32[24,128]{1,0:T(8,128)S(1)}, u32[]{:S(2)}, u32[]{:S(2)}) collective-permute-start(f32[24,128]{1,0:T(8,128)S(1)} %add_add_fusion.3), channel_id=1, source_target_pairs={{0,16},{8,24},{16,0},{24,8},{1,17},{9,25},{17,1},{25,9},{2,18},{10... | collective-permute-start | bytes 36872 | tf_op jit(solution)/shard_map/gram/ppermute | solution.py:21
  72.8 4.6 %collective-permute-start.23 = (f32[24,128]{1,0:T(8,128)S(1)}, f32[24,128]{1,0:T(8,128)S(1)}, u32[]{:S(2)}, u32[]{:S(2)}) collective-permute-start(f32[24,128]{1,0:T(8,128)S(1)} %add_add_fusion.3), channel_id=1, source_target_pairs={{0,8},{8,0},{16,24},{24,16},{1,9},{9,1},{17,25},{25,17},{2,10},{10... | collective-permute-start | bytes 36872 | tf_op jit(solution)/shard_map/gram/ppermute | solution.py:21

commit v13 on v11

--- a/solution.py
+++ b/solution.py
@@ -109,6 +109,7 @@
     panel_buf[zero_panel, :, :LANES] = jnp.zeros((panel_buf.shape[1], LANES), jnp.bfloat16)
     f32, bf16, i32 = jnp.float32, jnp.bfloat16, jnp.int32
     slots, places = rows.shape[1], out.shape[1] - LANES
+    early_chunks = 3 * slots // CHUNK // 4
     targets = row_devs * slab_tiles
     bins = 2 * targets
 
@@ -128,7 +129,8 @@
     tile_f = col_f - slab_tiles * source_f
     far = row_devs - 1 - (row_owner ^ place[0])
     late_bin = targets + far * slab_tiles + row - row_owner * slab_tiles
-    bin_of = jnp.where(occupied, jnp.where(source < 2, row, late_bin), -1)
+    early = (source < 2) & (slot < early_chunks * CHUNK)
+    bin_of = jnp.where(occupied, jnp.where(early, row, late_bin), -1)
     member = (iota((bins, slots), 0) == bin_of).astype(f32)
     member_bf = member.astype(bf16)
     rank = jnp.sum(member * mm(member_bf, earlier), axis=0, keepdims=True)
@@ -157,11 +159,15 @@
     for copy in copies + [plan_copy]:
         copy.wait()
 
-    @pl.loop(0, chunks)
+    @pl.loop(0, jnp.minimum(chunks, early_chunks))
     def _(k):
         tile_copy(k).wait()
 
     add_products(plan, 0, 0, targets, held, panel_buf, acc)
+
+    @pl.loop(early_chunks, chunks)
+    def _(k):
+        tile_copy(k).wait()
 
 
 def field(word, low, high):
@@ -448,9 +454,9 @@
             joined = (parts[1] + first.astype(f32)).astype(bf16)
             received = [
                 first,
+                swap(parts[2], "row", 1),
+                lax.ppermute(joined, "row", [(1, 2), (2, 1)]),
                 lax.ppermute(parts[0], "row", [(0, 3), (3, 0)]),
-                lax.ppermute(joined, "row", [(1, 2), (2, 1)]),
-                swap(parts[2], "row", 1),
             ]
         else:
             received = [swap(first, "row", first_mask)]

time: 74.6 us -> 75.1 us (level)
  starting transfers between devices: 29.7 us -> 30.5 us
    ppermute x17, starting transfers between devices: 13.5 us -> 17.1 us  [swap(): return lax.ppermute(value, axis, [(i, i ^ mask) for i in range(count)])]
    ppermute x1, starting transfers between devices: 4.69 us -> 2.43 us  [local(): lax.ppermute(parts[0], 'row', [(0, 3), (3, 0)])]
    ppermute x1, waiting for transfers between devices: 3.6 us -> 5.58 us  [local(): lax.ppermute(parts[0], 'row', [(0, 3), (3, 0)])]
    ppermute x17, waiting for transfers between devices: 14.4 us -> 12.7 us  [swap(): return lax.ppermute(value, axis, [(i, i ^ mask) for i in range(count)])]
    ppermute x1, starting transfers between devices: 2.24 us -> 1.33 us  [local(): first = lax.ppermute(first, 'row', [(0, 1), (3, 2), (1, 3), (2, 0)])]
  transfers between devices with their start and end apart: 26 -> 26, of which waited for: 17 -> 18; matrix products, arithmetic and copies ran while one was open for 2% -> 2% of each run, Pallas kernels for 13% -> 12%
where the time goes in v13:
time: 75.1 us; the launch traced here: 75.7 us
  starting transfers between devices  30.5 us (41%)
  waiting for transfers between devices  24.9 us (33%)
  Pallas kernels  15.3 us (20%)
  other arithmetic  1.81 us (2%)
  local copies, waits for them, and re-layouts  1.66 us (2%)
  between operations  1.49 us (2%)
    ppermute x17, starting transfers between devices, swap(): return lax.ppermute(value, axis, [(i, i ^ mask) for i in range(count)])  17.1 us
    ppermute x17, waiting for transfers between devices, swap(): return lax.ppermute(value, axis, [(i, i ^ mask) for i in range(count)])  12.7 us
    ppermute x6, starting transfers between devices, total_by_core(): values.append(lax.ppermute(value, ('row', 'col'), trades))  8.98 us
    ppermute x6, waiting for transfers between devices, total_by_core(): values.append(lax.ppermute(value, ('row', 'col'), trades))  6.6 us
    ppermute x1, waiting for transfers between devices, local(): lax.ppermute(parts[0], 'row', [(0, 3), (3, 0)])  5.58 us
    pallas_call x1, Pallas kernels, local(): pl.pallas_call(functools.partial(early_kernel, row_devs, col_devs, slab_t...  4.47 us
    pallas_call x1, Pallas kernels, local(): pl.pallas_call(functools.partial(first_late_kernel, [first_mask], odd), o...  2.67 us
    ppermute x1, starting transfers between devices, local(): lax.ppermute(parts[0], 'row', [(0, 3), (3, 0)])  2.43 us
  transfers between devices with their start and end apart: 26, of which 18 were waited for; matrix products, arithmetic and copies ran while one was open for 2% of the time, Pallas kernels for 12%

profile of v13, /device:TPU:0, one launch (start us, length us, event | category | flops | bytes accessed | tf_op | source)
XLA Modules:
  0.0 75.7 jit_solution(10048162639926437872)
XLA Ops:
  0.6 1.0 %convert_element_type.9.own_panel = bf16[48,2048]{1,0:T(8,128)(2,1)S(1)} convert(f32[48,2048]{1,0:T(8,128)} %current.3) | non-fusion elementwise | flops 98304 | bytes 589824 | tf_op jit(solution)/shard_map/gather/convert_element_type | solution.py:373
  1.7 0.5 collective-permute-start
  2.2 2.6 %collective-permute-start.1 = (bf16[48,2048]{1,0:T(8,128)(2,1)S(1)}, bf16[48,2048]{1,0:T(8,128)(2,1)S(1)}, u32[]{:S(2)}, u32[]{:S(2)}) collective-permute-start(bf16[48,2048]{1,0:T(8,128)(2,1)S(1)} %convert_element_type.9.own_panel), channel_id=1, source_target_pairs={{0,2},{1,3},{2,0},{3,1},{4,6},{5,7},{6,4},{7,5},{8,10},{9,11},{10,... | collective-permute-start | bytes 589832 | tf_op jit(solution)/shard_map/gather/ppermute | solution.py:21
  4.7 1.5 %collective-permute-start.3 = (bf16[48,2048]{1,0:T(8,128)(2,1)S(1)}, bf16[48,2048]{1,0:T(8,128)(2,1)S(1)}, u32[]{:S(2)}, u32[]{:S(2)}) collective-permute-start(bf16[48,2048]{1,0:T(8,128)(2,1)S(1)} %convert_element_type.9.own_panel), channel_id=1, source_target_pairs={{0,4},{1,5},{2,6},{3,7},{4,0},{5,1},{6,2},{7,3},{8,12},{9,13},{10,... | collective-permute-start | bytes 589832 | tf_op jit(solution)/shard_map/gather/ppermute | solution.py:21
  6.3 0.0 collective-permute-start.5
  6.9 0.1 pad_add_fusion.place
  7.0 0.0 collective-permute-done.near_panel
  7.0 4.5 %early.1 = (s32[1,896]{1,0:T(1,128)S(1)}, bf16[512,128,128]{2,1,0:T(8,128)(2,1)S(1)}, f32[65,48,128]{2,1,0:T(8,128)S(1)}, bf16[9,48,2048]{2,1,0:T(8,128)(2,1)S(1)}) custom-call(s32[2]{0:T(128)S(1)} %pad_add_fusion.place, s32[1]{0:T(128)S(6)} %copy.26.counts, s32[1,512]{1,0:T(1,128)} %bitcast.16, s32[1,512]{1,0:T(1,128)} %bitcast.17, ...), custom_call_target="tpu_custom_call" | custom-call | flops 805306368 | bytes 16777216 | tf_op jit(solution)/shard_map/early/pallas_call | solution.py:382
  11.5 0.0 collective-permute-done.1.value
  11.5 0.8 %collective-permute-start.2 = (bf16[48,2048]{1,0:T(8,128)(2,1)S(1)}, bf16[48,2048]{1,0:T(8,128)(2,1)S(1)}, u32[]{:S(2)}, u32[]{:S(2)}) collective-permute-start(bf16[48,2048]{1,0:T(8,128)(2,1)S(1)} %gather.4.refs_0_), channel_id=1, source_target_pairs={{0,1},{1,0},{2,3},{3,2},{4,5},{5,4},{6,7},{7,6},{8,9},{9,8},{10,11... | collective-permute-start | bytes 589832 | tf_op jit(solution)/shard_map/gather/ppermute | solution.py:21
  12.4 3.6 %collective-permute-done.3.value = bf16[48,2048]{1,0:T(8,128)(2,1)S(1)} collective-permute-done((bf16[48,2048]{1,0:T(8,128)(2,1)S(1)}, bf16[48,2048]{1,0:T(8,128)(2,1)S(1)}, u32[]{:S(2)}, u32[]{:S(2)}) %collective-permute-start.3) | collective-permute-done | bytes 196640 | tf_op jit(solution)/shard_map/gather/ppermute | solution.py:21
  15.9 0.0 collective-permute-start.4
  15.9 0.0 collective-permute-done.5.value
  15.9 0.5 collective-permute-start.6
  16.4 0.8 gather.7.refs_5_
  17.2 0.0 collective-permute-done.2.refs_0_
  17.2 0.2 collective-permute-done.4.refs_1_
  17.4 0.3 collective-permute-done.6.refs_2_
  17.6 2.7 %late.3 = (bf16[48,2048]{1,0:T(8,128)(2,1)S(1)}, bf16[9,48,2048]{2,1,0:T(8,128)(2,1)S(1)}) custom-call(s32[2]{0:T(128)S(1)} %pad_add_fusion.place, s32[1,896]{1,0:T(1,128)S(1)} %get-tuple-element.18.plan, bf16[48,2048]{1,0:T(8,128)(2,1)S(1)} %collective-permute-done.2.refs_0_, ...), custom_call_target="tpu_custom_call", output_to_operand_aliasing={{1}: (7, {})} | custom-call | flops 48 | bytes 1 | tf_op jit(solution)/shard_map/late/pallas_call | solution.py:433
  20.3 1.3 %collective-permute-start.7 = (bf16[48,2048]{1,0:T(8,128)(2,1)S(1)}, bf16[48,2048]{1,0:T(8,128)(2,1)S(1)}, u32[]{:S(2)}, u32[]{:S(2)}) collective-permute-start(bf16[48,2048]{1,0:T(8,128)(2,1)S(1)} %get-tuple-element.23), channel_id=1, source_target_pairs={{0,8},{24,16},{8,24},{16,0},{1,9},{25,17},{9,25},{17,1},{2,10},{26... | collective-permute-start | bytes 589832 | tf_op jit(solution)/shard_map/late/ppermute | solution.py:453
  21.7 2.3 %late.5 = (bf16[48,2048]{1,0:T(8,128)(2,1)S(1)}, f32[48,2048]{1,0:T(8,128)S(1)}, bf16[48,2048]{1,0:T(8,128)(2,1)S(1)}) custom-call(s32[2]{0:T(128)S(1)} %pad_add_fusion.place, s32[1,896]{1,0:T(1,128)S(1)} %get-tuple-element.18.plan, bf16[9,48,2048]{2,1,0:T(8,128)(2,1)S(1)} %get-tuple-element.22.panel_buf, ...), custom_call_target="tpu_custom_call" | custom-call | flops 48 | bytes 1 | tf_op jit(solution)/shard_map/late/pallas_call | solution.py:443
  23.9 3.0 %collective-permute-start.8 = (bf16[48,2048]{1,0:T(8,128)(2,1)S(1)}, bf16[48,2048]{1,0:T(8,128)(2,1)S(1)}, u32[]{:S(2)}, u32[]{:S(2)}) collective-permute-start(bf16[48,2048]{1,0:T(8,128)(2,1)S(1)} %get-tuple-element.24), channel_id=1, source_target_pairs={{0,8},{8,0},{16,24},{24,16},{1,9},{9,1},{17,25},{25,17},{2,10},{10... | collective-permute-start | bytes 589832 | tf_op jit(solution)/shard_map/late/ppermute | solution.py:21
  26.9 2.4 %collective-permute-start.10 = (bf16[48,2048]{1,0:T(8,128)(2,1)S(1)}, bf16[48,2048]{1,0:T(8,128)(2,1)S(1)}, u32[]{:S(2)}, u32[]{:S(2)}) collective-permute-start(bf16[48,2048]{1,0:T(8,128)(2,1)S(1)} %get-tuple-element.26), channel_id=1, source_target_pairs={{0,24},{24,0},{1,25},{25,1},{2,26},{26,2},{3,27},{27,3},{4,28},{28... | collective-permute-start | bytes 589832 | tf_op jit(solution)/shard_map/late/ppermute | solution.py:459
  29.3 0.0 collective-permute-done.7.refs_0_
  29.4 0.7 collective-permute-start.9
  30.1 0.0 copy-start
  30.1 0.0 copy-start.3
  30.1 1.7 %late.4.base = f32[48,2048]{1,0:T(8,128)S(1)} custom-call(s32[2]{0:T(128)S(1)} %pad_add_fusion.place, s32[1,896]{1,0:T(1,128)S(1)} %get-tuple-element.18.plan, bf16[9,48,2048]{2,1,0:T(8,128)(2,1)S(1)} %get-tuple-element.22.panel_buf, bf16[512,128,128]{2,1,0:T(8,128)(2,1)S(1)} %get-tuple-element.20.refs_3_.tiles, ...), custom_call_target="tpu_custom_call" | custom-call | flops 48 | bytes 1 | tf_op jit(solution)/shard_map/late/pallas_call | solution.py:464
  31.9 0.7 collective-permute-done.8.refs_1_
  32.5 5.6 %collective-permute-done.10.refs_3_ = bf16[48,2048]{1,0:T(8,128)(2,1)S(1)} collective-permute-done((bf16[48,2048]{1,0:T(8,128)(2,1)S(1)}, bf16[48,2048]{1,0:T(8,128)(2,1)S(1)}, u32[]{:S(2)}, u32[]{:S(2)}) %collective-permute-start.10) | collective-permute-done | bytes 196640 | tf_op jit(solution)/shard_map/late/ppermute | solution.py:459
  38.1 1.8 %coefficients.1 = (f32[48,2048]{1,0:T(8,128)S(1)}, f32[12,8,128]{2,1,0:T(8,128)S(1)}, f32[12,8,128]{2,1,0:T(8,128)S(1)}) custom-call(s32[2]{0:T(128)S(1)} %pad_add_fusion.place, f32[48,2048]{1,0:T(8,128)S(1)} %late.4.base, bf16[48,2048]{1,0:T(8,128)(2,1)S(1)} %collective-permute-done.7.refs_0_, bf16[48,2048]{1,0:T(8,128)(2,1)S(1)} %collective-permute-done.8.refs_1_, ...), custom_call_target="tpu_custom_call" | custom-call | tf_op jit(solution)/shard_map/coefficients/pallas_call | solution.py:478
  39.9 0.1 collective-permute-start.11
  40.0 1.2 %collective-permute-done.11 = f32[12,8,128]{2,1,0:T(8,128)S(1)} collective-permute-done((f32[12,8,128]{2,1,0:T(8,128)S(1)}, f32[12,8,128]{2,1,0:T(8,128)S(1)}, u32[]{:S(2)}, u32[]{:S(2)}) %collective-permute-start.11) | collective-permute-done | bytes 49184 | tf_op jit(solution)/shard_map/coefficients/ppermute | solution.py:21
  41.2 1.6 %collective-permute-start.14 = (f32[12,8,128]{2,1,0:T(8,128)S(1)}, f32[12,8,128]{2,1,0:T(8,128)S(1)}, u32[]{:S(2)}, u32[]{:S(2)}) collective-permute-start(f32[12,8,128]{2,1,0:T(8,128)S(1)} %add.46), channel_id=1, source_target_pairs={{0,6},{1,25},{2,4},{3,27},{4,2},{5,29},{6,0},{7,31},{8,14},{9,17},... | collective-permute-start | bytes 147464 | tf_op jit(solution)/shard_map/coefficients/ppermute | solution.py:44
  42.7 0.7 collective-permute-start.13
  43.4 1.3 %collective-permute-start.12 = (f32[12,8,128]{2,1,0:T(8,128)S(1)}, f32[12,8,128]{2,1,0:T(8,128)S(1)}, u32[]{:S(2)}, u32[]{:S(2)}) collective-permute-start(f32[12,8,128]{2,1,0:T(8,128)S(1)} %add.46), channel_id=1, source_target_pairs={{0,2},{1,9},{2,0},{3,11},{4,6},{5,13},{6,4},{7,15},{8,10},{9,1},{1... | collective-permute-start | bytes 147464 | tf_op jit(solution)/shard_map/coefficients/ppermute | solution.py:44
  44.7 1.5 %collective-permute-done.14 = f32[12,8,128]{2,1,0:T(8,128)S(1)} collective-permute-done((f32[12,8,128]{2,1,0:T(8,128)S(1)}, f32[12,8,128]{2,1,0:T(8,128)S(1)}, u32[]{:S(2)}, u32[]{:S(2)}) %collective-permute-start.14) | collective-permute-done | bytes 49184 | tf_op jit(solution)/shard_map/coefficients/ppermute | solution.py:44
  46.2 0.6 collective-permute-done.13
  46.8 0.7 collective-permute-done.12
  47.5 2.4 %collective-permute-start.17 = (f32[12,8,128]{2,1,0:T(8,128)S(1)}, f32[12,8,128]{2,1,0:T(8,128)S(1)}, u32[]{:S(2)}, u32[]{:S(2)}) collective-permute-start(f32[12,8,128]{2,1,0:T(8,128)S(1)} %add_add_fusion.1), channel_id=1, source_target_pairs={{0,24},{1,7},{2,26},{3,5},{4,28},{5,3},{6,30},{7,1},{8,16},{9,15},... | collective-permute-start | bytes 147464 | tf_op jit(solution)/shard_map/coefficients/ppermute | solution.py:44
  50.0 2.7 %collective-permute-start.16 = (f32[12,8,128]{2,1,0:T(8,128)S(1)}, f32[12,8,128]{2,1,0:T(8,128)S(1)}, u32[]{:S(2)}, u32[]{:S(2)}) collective-permute-start(f32[12,8,128]{2,1,0:T(8,128)S(1)} %add_add_fusion.1), channel_id=1, source_target_pairs={{0,16},{1,5},{2,18},{3,7},{4,20},{5,1},{6,22},{7,3},{8,24},{9,13},... | collective-permute-start | bytes 147464 | tf_op jit(solution)/shard_map/coefficients/ppermute | solution.py:44
  52.7 0.3 collective-permute-start.15
  53.0 0.5 collective-permute-done.17
  53.5 1.8 %collective-permute-done.16 = f32[12,8,128]{2,1,0:T(8,128)S(1)} collective-permute-done((f32[12,8,128]{2,1,0:T(8,128)S(1)}, f32[12,8,128]{2,1,0:T(8,128)S(1)}, u32[]{:S(2)}, u32[]{:S(2)}) %collective-permute-start.16) | collective-permute-done | bytes 49184 | tf_op jit(solution)/shard_map/coefficients/ppermute | solution.py:44
  55.3 1.5 %collective-permute-done.15 = f32[12,8,128]{2,1,0:T(8,128)S(1)} collective-permute-done((f32[12,8,128]{2,1,0:T(8,128)S(1)}, f32[12,8,128]{2,1,0:T(8,128)S(1)}, u32[]{:S(2)}, u32[]{:S(2)}) %collective-permute-start.15) | collective-permute-done | bytes 49184 | tf_op jit(solution)/shard_map/coefficients/ppermute | solution.py:44
  56.8 0.1 collective-permute-start.18
  56.9 1.2 %collective-permute-done.18.other = f32[12,8,128]{2,1,0:T(8,128)S(1)} collective-permute-done((f32[12,8,128]{2,1,0:T(8,128)S(1)}, f32[12,8,128]{2,1,0:T(8,128)S(1)}, u32[]{:S(2)}, u32[]{:S(2)}) %collective-permute-start.18) | collective-permute-done | bytes 49184 | tf_op jit(solution)/shard_map/coefficients/ppermute | solution.py:21
  58.1 1.6 %residual.1 = (f32[48,2048]{1,0:T(8,128)S(1)}, f32[48,432]{1,0:T(8,128)S(1)}, f32[24,128]{1,0:T(8,128)S(1)}) custom-call(s32[2]{0:T(128)S(1)} %pad_add_fusion.place, f32[12,8,128]{2,1,0:T(8,128)S(1)} %add_add_fusion.mine, f32[12,8,128]{2,1,0:T(8,128)S(1)} %collective-permute-done.18.other, f32[48,2048]{1,0:T(8,128)S(1)} %get-tuple-element.29.recurrence, ...), custom_call_target="tpu_custom_call" | custom-call | tf_op jit(solution)/shard_map/residual/pallas_call | solution.py:491
  59.7 0.2 collective-permute-start.19
  59.9 1.0 %collective-permute-done.19 = f32[24,128]{1,0:T(8,128)S(1)} collective-permute-done((f32[24,128]{1,0:T(8,128)S(1)}, f32[24,128]{1,0:T(8,128)S(1)}, u32[]{:S(2)}, u32[]{:S(2)}) %collective-permute-start.19) | collective-permute-done | bytes 12320 | tf_op jit(solution)/shard_map/gram/ppermute | solution.py:21
  61.0 2.7 %collective-permute-start.22 = (f32[24,128]{1,0:T(8,128)S(1)}, f32[24,128]{1,0:T(8,128)S(1)}, u32[]{:S(2)}, u32[]{:S(2)}) collective-permute-start(f32[24,128]{1,0:T(8,128)S(1)} %add.53), channel_id=1, source_target_pairs={{0,6},{1,7},{2,4},{3,5},{4,2},{5,3},{6,0},{7,1},{8,14},{9,15},{10,... | collective-permute-start | bytes 36872 | tf_op jit(solution)/shard_map/gram/ppermute | solution.py:21
  63.6 0.8 collective-permute-start.21
  64.4 0.1 collective-permute-start.20
  64.4 1.1 %collective-permute-done.22 = f32[24,128]{1,0:T(8,128)S(1)} collective-permute-done((f32[24,128]{1,0:T(8,128)S(1)}, f32[24,128]{1,0:T(8,128)S(1)}, u32[]{:S(2)}, u32[]{:S(2)}) %collective-permute-start.22) | collective-permute-done | bytes 12320 | tf_op jit(solution)/shard_map/gram/ppermute | solution.py:21
  65.5 1.8 %collective-permute-done.21 = f32[24,128]{1,0:T(8,128)S(1)} collective-permute-done((f32[24,128]{1,0:T(8,128)S(1)}, f32[24,128]{1,0:T(8,128)S(1)}, u32[]{:S(2)}, u32[]{:S(2)}) %collective-permute-start.21) | collective-permute-done | bytes 12320 | tf_op jit(solution)/shard_map/gram/ppermute | solution.py:21
  67.3 0.8 collective-permute-done.20
  68.1 2.3 %collective-permute-start.25 = (f32[24,128]{1,0:T(8,128)S(1)}, f32[24,128]{1,0:T(8,128)S(1)}, u32[]{:S(2)}, u32[]{:S(2)}) collective-permute-start(f32[24,128]{1,0:T(8,128)S(1)} %add_add_fusion.3), channel_id=1, source_target_pairs={{0,24},{8,16},{16,8},{24,0},{1,25},{9,17},{17,9},{25,1},{2,26},{10... | collective-permute-start | bytes 36872 | tf_op jit(solution)/shard_map/gram/ppermute | solution.py:21
  70.4 0.0 collective-permute-start.24
  70.4 2.1 %collective-permute-start.23 = (f32[24,128]{1,0:T(8,128)S(1)}, f32[24,128]{1,0:T(8,128)S(1)}, u32[]{:S(2)}, u32[]{:S(2)}) collective-permute-start(f32[24,128]{1,0:T(8,128)S(1)} %add_add_fusion.3), channel_id=1, source_target_pairs={{0,8},{8,0},{16,24},{24,16},{1,9},{9,1},{17,25},{25,17},{2,10},{10... | collective-permute-start | bytes 36872 | tf_op jit(solution)/shard_map/gram/ppermute | solution.py:21
  72.5 0.7 copy.25
  73.2 0.8 %copy.19 = f32[432,48]{1,0:T(8,128)} copy(f32[432,48]{0,1:T(8,128)S(1)} %bitcast.11) | data formatting | bytes 165888 | tf_op jit(solution)/shard_map/residual/transpose | solution.py:503
  74.0 0.9 %collective-permute-done.24 = f32[24,128]{1,0:T(8,128)S(1)} collective-permute-done((f32[24,128]{1,0:T(8,128)S(1)}, f32[24,128]{1,0:T(8,128)S(1)}, u32[]{:S(2)}, u32[]{:S(2)}) %collective-permute-start.24) | collective-permute-done | bytes 12320 | tf_op jit(solution)/shard_map/gram/ppermute | solution.py:21
  75.0 0.1 fusion
  75.0 0.6 pad_maximum_fusion
  (23 shorter events, 0.1 us)
Async XLA Ops:
  1.7 5.4 %collective-permute-start = (bf16[48,2048]{1,0:T(8,128)(2,1)S(1)}, bf16[48,2048]{1,0:T(8,128)(2,1)S(1)}, u32[]{:S(2)}, u32[]{:S(2)}) collective-permute-start(bf16[48,2048]{1,0:T(8,128)(2,1)S(1)} %convert_element_type.9.own_panel), channel_id=1, source_target_pairs={{0,1},{1,0},{2,3},{3,2},{4,5},{5,4},{6,7},{7,6},{8,9},{9,8},{10,11... | collective-permute-start | bytes 589832 | tf_op jit(solution)/shard_map/gather/ppermute | solution.py:21
  2.2 9.3 %collective-permute-start.1 = (bf16[48,2048]{1,0:T(8,128)(2,1)S(1)}, bf16[48,2048]{1,0:T(8,128)(2,1)S(1)}, u32[]{:S(2)}, u32[]{:S(2)}) collective-permute-start(bf16[48,2048]{1,0:T(8,128)(2,1)S(1)} %convert_element_type.9.own_panel), channel_id=1, source_target_pairs={{0,2},{1,3},{2,0},{3,1},{4,6},{5,7},{6,4},{7,5},{8,10},{9,11},{10,... | collective-permute-start | bytes 589832 | tf_op jit(solution)/shard_map/gather/ppermute | solution.py:21
  4.7 11.2 %collective-permute-start.3 = (bf16[48,2048]{1,0:T(8,128)(2,1)S(1)}, bf16[48,2048]{1,0:T(8,128)(2,1)S(1)}, u32[]{:S(2)}, u32[]{:S(2)}) collective-permute-start(bf16[48,2048]{1,0:T(8,128)(2,1)S(1)} %convert_element_type.9.own_panel), channel_id=1, source_target_pairs={{0,4},{1,5},{2,6},{3,7},{4,0},{5,1},{6,2},{7,3},{8,12},{9,13},{10,... | collective-permute-start | bytes 589832 | tf_op jit(solution)/shard_map/gather/ppermute | solution.py:21
  6.3 9.7 %collective-permute-start.5 = (bf16[48,2048]{1,0:T(8,128)(2,1)S(1)}, bf16[48,2048]{1,0:T(8,128)(2,1)S(1)}, u32[]{:S(2)}, u32[]{:S(2)}) collective-permute-start(bf16[48,2048]{1,0:T(8,128)(2,1)S(1)} %convert_element_type.9.own_panel), channel_id=1, source_target_pairs={{0,6},{1,7},{2,4},{3,5},{4,2},{5,3},{6,0},{7,1},{8,14},{9,15},{10,... | collective-permute-start | bytes 589832 | tf_op jit(solution)/shard_map/gather/ppermute | solution.py:21
  11.5 5.7 %collective-permute-start.2 = (bf16[48,2048]{1,0:T(8,128)(2,1)S(1)}, bf16[48,2048]{1,0:T(8,128)(2,1)S(1)}, u32[]{:S(2)}, u32[]{:S(2)}) collective-permute-start(bf16[48,2048]{1,0:T(8,128)(2,1)S(1)} %gather.4.refs_0_), channel_id=1, source_target_pairs={{0,1},{1,0},{2,3},{3,2},{4,5},{5,4},{6,7},{7,6},{8,9},{9,8},{10,11... | collective-permute-start | bytes 589832 | tf_op jit(solution)/shard_map/gather/ppermute | solution.py:21
  15.9 1.4 %collective-permute-start.4 = (bf16[48,2048]{1,0:T(8,128)(2,1)S(1)}, bf16[48,2048]{1,0:T(8,128)(2,1)S(1)}, u32[]{:S(2)}, u32[]{:S(2)}) collective-permute-start(bf16[48,2048]{1,0:T(8,128)(2,1)S(1)} %gather.5.refs_1_), channel_id=1, source_target_pairs={{0,1},{1,0},{2,3},{3,2},{4,5},{5,4},{6,7},{7,6},{8,9},{9,8},{10,11... | collective-permute-start | bytes 589832 | tf_op jit(solution)/shard_map/gather/ppermute | solution.py:21
  15.9 1.7 %collective-permute-start.6 = (bf16[48,2048]{1,0:T(8,128)(2,1)S(1)}, bf16[48,2048]{1,0:T(8,128)(2,1)S(1)}, u32[]{:S(2)}, u32[]{:S(2)}) collective-permute-start(bf16[48,2048]{1,0:T(8,128)(2,1)S(1)} %gather.6.refs_2_), channel_id=1, source_target_pairs={{0,1},{1,0},{2,3},{3,2},{4,5},{5,4},{6,7},{7,6},{8,9},{9,8},{10,11... | collective-permute-start | bytes 589832 | tf_op jit(solution)/shard_map/gather/ppermute | solution.py:21
  20.3 9.0 %collective-permute-start.7 = (bf16[48,2048]{1,0:T(8,128)(2,1)S(1)}, bf16[48,2048]{1,0:T(8,128)(2,1)S(1)}, u32[]{:S(2)}, u32[]{:S(2)}) collective-permute-start(bf16[48,2048]{1,0:T(8,128)(2,1)S(1)} %get-tuple-element.23), channel_id=1, source_target_pairs={{0,8},{24,16},{8,24},{16,0},{1,9},{25,17},{9,25},{17,1},{2,10},{26... | collective-permute-start | bytes 589832 | tf_op jit(solution)/shard_map/late/ppermute | solution.py:453
  21.7 8.4 %copy-start.1 = (f32[48,2048]{1,0:T(8,128)S(1)}, f32[48,2048]{1,0:T(8,128)}, u32[]{:S(2)}) copy-start(f32[48,2048]{1,0:T(8,128)} %current.3) | copy-start | bytes 1179652
  21.7 8.4 %copy-start.2 = (f32[48,2048]{1,0:T(8,128)S(1)}, f32[48,2048]{1,0:T(8,128)}, u32[]{:S(2)}) copy-start(f32[48,2048]{1,0:T(8,128)} %previous.1) | copy-start | bytes 1179652
  21.7 8.4 %copy-start.4 = (f32[48,48]{1,0:T(8,128)S(1)}, f32[48,48]{1,0:T(8,128)}, u32[]{:S(2)}) copy-start(f32[48,48]{1,0:T(8,128)} %coupling.1) | copy-start | bytes 27652
  21.7 8.4 %copy-start.5 = (f32[2048]{0:T(1024)S(1)}, f32[2048]{0:T(1024)}, u32[]{:S(2)}) copy-start(f32[2048]{0:T(1024)} %param.14) | copy-start | bytes 24580
  23.9 8.6 %collective-permute-start.8 = (bf16[48,2048]{1,0:T(8,128)(2,1)S(1)}, bf16[48,2048]{1,0:T(8,128)(2,1)S(1)}, u32[]{:S(2)}, u32[]{:S(2)}) collective-permute-start(bf16[48,2048]{1,0:T(8,128)(2,1)S(1)} %get-tuple-element.24), channel_id=1, source_target_pairs={{0,8},{8,0},{16,24},{24,16},{1,9},{9,1},{17,25},{25,17},{2,10},{10... | collective-permute-start | bytes 589832 | tf_op jit(solution)/shard_map/late/ppermute | solution.py:21
  26.9 11.2 %collective-permute-start.10 = (bf16[48,2048]{1,0:T(8,128)(2,1)S(1)}, bf16[48,2048]{1,0:T(8,128)(2,1)S(1)}, u32[]{:S(2)}, u32[]{:S(2)}) collective-permute-start(bf16[48,2048]{1,0:T(8,128)(2,1)S(1)} %get-tuple-element.26), channel_id=1, source_target_pairs={{0,24},{24,0},{1,25},{25,1},{2,26},{26,2},{3,27},{27,3},{4,28},{28... | collective-permute-start | bytes 589832 | tf_op jit(solution)/shard_map/late/ppermute | solution.py:459
  29.4 8.7 %collective-permute-start.9 = (bf16[48,2048]{1,0:T(8,128)(2,1)S(1)}, bf16[48,2048]{1,0:T(8,128)(2,1)S(1)}, u32[]{:S(2)}, u32[]{:S(2)}) collective-permute-start(bf16[48,2048]{1,0:T(8,128)(2,1)S(1)} %add_convert_fusion), channel_id=1, source_target_pairs={{8,16},{16,8},{9,17},{17,9},{10,18},{18,10},{11,19},{19,11},{12,20... | collective-permute-start | bytes 589832 | tf_op jit(solution)/shard_map/late/ppermute | solution.py:458
  30.1 8.0 %copy-start = (f32[8,48,2048]{2,1,0:T(8,128)S(1)}, f32[8,48,2048]{2,1,0:T(8,128)}, u32[]{:S(2)}) copy-start(f32[8,48,2048]{2,1,0:T(8,128)} %param.13) | copy-start | bytes 9437188
  30.1 8.0 %copy-start.3 = (f32[2048]{0:T(1024)S(1)}, f32[2048]{0:T(1024)}, u32[]{:S(2)}) copy-start(f32[2048]{0:T(1024)} %param.15) | copy-start | bytes 24580
  39.9 1.3 %collective-permute-start.11 = (f32[12,8,128]{2,1,0:T(8,128)S(1)}, f32[12,8,128]{2,1,0:T(8,128)S(1)}, u32[]{:S(2)}, u32[]{:S(2)}) collective-permute-start(f32[12,8,128]{2,1,0:T(8,128)S(1)} %get-tuple-element.28), channel_id=1, source_target_pairs={{0,1},{1,0},{2,3},{3,2},{4,5},{5,4},{6,7},{7,6},{8,9},{9,8},{10,11... | collective-permute-start | bytes 147464 | tf_op jit(solution)/shard_map/coefficients/ppermute | solution.py:21
  41.2 5.0 %collective-permute-start.14 = (f32[12,8,128]{2,1,0:T(8,128)S(1)}, f32[12,8,128]{2,1,0:T(8,128)S(1)}, u32[]{:S(2)}, u32[]{:S(2)}) collective-permute-start(f32[12,8,128]{2,1,0:T(8,128)S(1)} %add.46), channel_id=1, source_target_pairs={{0,6},{1,25},{2,4},{3,27},{4,2},{5,29},{6,0},{7,31},{8,14},{9,17},... | collective-permute-start | bytes 147464 | tf_op jit(solution)/shard_map/coefficients/ppermute | solution.py:44
  42.7 4.1 %collective-permute-start.13 = (f32[12,8,128]{2,1,0:T(8,128)S(1)}, f32[12,8,128]{2,1,0:T(8,128)S(1)}, u32[]{:S(2)}, u32[]{:S(2)}) collective-permute-start(f32[12,8,128]{2,1,0:T(8,128)S(1)} %add.46), channel_id=1, source_target_pairs={{0,4},{1,17},{2,6},{3,19},{4,0},{5,21},{6,2},{7,23},{8,12},{9,25},... | collective-permute-start | bytes 147464 | tf_op jit(solution)/shard_map/coefficients/ppermute | solution.py:44
  43.4 4.1 %collective-permute-start.12 = (f32[12,8,128]{2,1,0:T(8,128)S(1)}, f32[12,8,128]{2,1,0:T(8,128)S(1)}, u32[]{:S(2)}, u32[]{:S(2)}) collective-permute-start(f32[12,8,128]{2,1,0:T(8,128)S(1)} %add.46), channel_id=1, source_target_pairs={{0,2},{1,9},{2,0},{3,11},{4,6},{5,13},{6,4},{7,15},{8,10},{9,1},{1... | collective-permute-start | bytes 147464 | tf_op jit(solution)/shard_map/coefficients/ppermute | solution.py:44
  47.5 6.0 %collective-permute-start.17 = (f32[12,8,128]{2,1,0:T(8,128)S(1)}, f32[12,8,128]{2,1,0:T(8,128)S(1)}, u32[]{:S(2)}, u32[]{:S(2)}) collective-permute-start(f32[12,8,128]{2,1,0:T(8,128)S(1)} %add_add_fusion.1), channel_id=1, source_target_pairs={{0,24},{1,7},{2,26},{3,5},{4,28},{5,3},{6,30},{7,1},{8,16},{9,15},... | collective-permute-start | bytes 147464 | tf_op jit(solution)/shard_map/coefficients/ppermute | solution.py:44
  50.0 5.3 %collective-permute-start.16 = (f32[12,8,128]{2,1,0:T(8,128)S(1)}, f32[12,8,128]{2,1,0:T(8,128)S(1)}, u32[]{:S(2)}, u32[]{:S(2)}) collective-permute-start(f32[12,8,128]{2,1,0:T(8,128)S(1)} %add_add_fusion.1), channel_id=1, source_target_pairs={{0,16},{1,5},{2,18},{3,7},{4,20},{5,1},{6,22},{7,3},{8,24},{9,13},... | collective-permute-start | bytes 147464 | tf_op jit(solution)/shard_map/coefficients/ppermute | solution.py:44
  52.7 4.1 %collective-permute-start.15 = (f32[12,8,128]{2,1,0:T(8,128)S(1)}, f32[12,8,128]{2,1,0:T(8,128)S(1)}, u32[]{:S(2)}, u32[]{:S(2)}) collective-permute-start(f32[12,8,128]{2,1,0:T(8,128)S(1)} %add_add_fusion.1), channel_id=1, source_target_pairs={{0,8},{1,3},{2,10},{3,1},{4,12},{5,7},{6,14},{7,5},{8,0},{9,11},{1... | collective-permute-start | bytes 147464 | tf_op jit(solution)/shard_map/coefficients/ppermute | solution.py:44
  56.8 1.3 %collective-permute-start.18 = (f32[12,8,128]{2,1,0:T(8,128)S(1)}, f32[12,8,128]{2,1,0:T(8,128)S(1)}, u32[]{:S(2)}, u32[]{:S(2)}) collective-permute-start(f32[12,8,128]{2,1,0:T(8,128)S(1)} %add_add_fusion.mine), channel_id=1, source_target_pairs={{0,1},{1,0},{2,3},{3,2},{4,5},{5,4},{6,7},{7,6},{8,9},{9,8},{10,11... | collective-permute-start | bytes 147464 | tf_op jit(solution)/shard_map/coefficients/ppermute | solution.py:21
  59.7 1.2 %collective-permute-start.19 = (f32[24,128]{1,0:T(8,128)S(1)}, f32[24,128]{1,0:T(8,128)S(1)}, u32[]{:S(2)}, u32[]{:S(2)}) collective-permute-start(f32[24,128]{1,0:T(8,128)S(1)} %get-tuple-element.32), channel_id=1, source_target_pairs={{0,1},{1,0},{2,3},{3,2},{4,5},{5,4},{6,7},{7,6},{8,9},{9,8},{10,11... | collective-permute-start | bytes 36872 | tf_op jit(solution)/shard_map/gram/ppermute | solution.py:21
  61.0 4.6 %collective-permute-start.22 = (f32[24,128]{1,0:T(8,128)S(1)}, f32[24,128]{1,0:T(8,128)S(1)}, u32[]{:S(2)}, u32[]{:S(2)}) collective-permute-start(f32[24,128]{1,0:T(8,128)S(1)} %add.53), channel_id=1, source_target_pairs={{0,6},{1,7},{2,4},{3,5},{4,2},{5,3},{6,0},{7,1},{8,14},{9,15},{10,... | collective-permute-start | bytes 36872 | tf_op jit(solution)/shard_map/gram/ppermute | solution.py:21
  63.6 3.7 %collective-permute-start.21 = (f32[24,128]{1,0:T(8,128)S(1)}, f32[24,128]{1,0:T(8,128)S(1)}, u32[]{:S(2)}, u32[]{:S(2)}) collective-permute-start(f32[24,128]{1,0:T(8,128)S(1)} %add.53), channel_id=1, source_target_pairs={{0,4},{1,5},{2,6},{3,7},{4,0},{5,1},{6,2},{7,3},{8,12},{9,13},{10,... | collective-permute-start | bytes 36872 | tf_op jit(solution)/shard_map/gram/ppermute | solution.py:21
  64.4 3.7 %collective-permute-start.20 = (f32[24,128]{1,0:T(8,128)S(1)}, f32[24,128]{1,0:T(8,128)S(1)}, u32[]{:S(2)}, u32[]{:S(2)}) collective-permute-start(f32[24,128]{1,0:T(8,128)S(1)} %add.53), channel_id=1, source_target_pairs={{0,2},{1,3},{2,0},{3,1},{4,6},{5,7},{6,4},{7,5},{8,10},{9,11},{10,... | collective-permute-start | bytes 36872 | tf_op jit(solution)/shard_map/gram/ppermute | solution.py:21
  68.1 6.0 %collective-permute-start.25 = (f32[24,128]{1,0:T(8,128)S(1)}, f32[24,128]{1,0:T(8,128)S(1)}, u32[]{:S(2)}, u32[]{:S(2)}) collective-permute-start(f32[24,128]{1,0:T(8,128)S(1)} %add_add_fusion.3), channel_id=1, source_target_pairs={{0,24},{8,16},{16,8},{24,0},{1,25},{9,17},{17,9},{25,1},{2,26},{10... | collective-permute-start | bytes 36872 | tf_op jit(solution)/shard_map/gram/ppermute | solution.py:21
  70.4 4.6 %collective-permute-start.24 = (f32[24,128]{1,0:T(8,128)S(1)}, f32[24,128]{1,0:T(8,128)S(1)}, u32[]{:S(2)}, u32[]{:S(2)}) collective-permute-start(f32[24,128]{1,0:T(8,128)S(1)} %add_add_fusion.3), channel_id=1, source_target_pairs={{0,16},{8,24},{16,0},{24,8},{1,17},{9,25},{17,1},{25,9},{2,18},{10... | collective-permute-start | bytes 36872 | tf_op jit(solution)/shard_map/gram/ppermute | solution.py:21
  70.4 4.6 %collective-permute-start.23 = (f32[24,128]{1,0:T(8,128)S(1)}, f32[24,128]{1,0:T(8,128)S(1)}, u32[]{:S(2)}, u32[]{:S(2)}) collective-permute-start(f32[24,128]{1,0:T(8,128)S(1)} %add_add_fusion.3), channel_id=1, source_target_pairs={{0,8},{8,0},{16,24},{24,16},{1,9},{9,1},{17,25},{25,17},{2,10},{10... | collective-permute-start | bytes 36872 | tf_op jit(solution)/shard_map/gram/ppermute | solution.py:21

commit v14 on v13

--- a/solution.py
+++ b/solution.py
@@ -79,13 +79,13 @@
     tiles,
     own_panel,
     near_panel,
-    out,
+    plan,
     held,
     acc,
     panel_buf,
     rows,
     cols,
-    plan,
+    out,
     tile_sem,
     list_sem,
     panel_sem,
@@ -152,7 +152,10 @@
     phase = iota((bins, LANES), 1)
     edge = jnp.where(phase > 0, targets + (phase - 1) * slab_tiles, 0)
     inside = (iota((bins, LANES), 0) < edge).astype(f32).astype(bf16)
-    out[:, places:] = mm(sizes.astype(bf16), inside)[:1].astype(i32)
+    edges = mm(sizes.astype(bf16), inside)[:1].astype(i32)
+    lane = iota((1, LANES), 1)
+    edges = jnp.where(lane == LANES - 2, place[0], jnp.where(lane == LANES - 1, place[1], edges))
+    out[:, places:] = edges
     plan_copy = pltpu.make_async_copy(out, plan, list_sem.at[2])
     plan_copy.start()
     acc[...] = jnp.zeros_like(acc)
@@ -168,6 +171,14 @@
     @pl.loop(early_chunks, chunks)
     def _(k):
         tile_copy(k).wait()
+
+
+def row_of(plan):
+    return plan[0, plan.shape[1] - 2]
+
+
+def core_of(plan):
+    return plan[0, plan.shape[1] - 1] & 1
 
 
 def field(word, low, high):
@@ -210,28 +221,28 @@
         copy.wait()
 
 
-def first_late_kernel(masks, odd, place, plan, *refs):
+def first_late_kernel(masks, odd, plan, *refs):
     panels = dict(zip(odd, refs))
     tiles, early, _ = refs[len(odd) : len(odd) + 3]
     sends = refs[len(odd) + 3 : -3]
     panel_buf, acc, sem = refs[-3:]
     copies = load_panels(panels, panel_buf, sem)
     for mask, send in zip(masks, sends):
-        late_part(mask, place, plan, tiles, early, panel_buf, acc, copies)
+        late_part(mask, plan, tiles, early, panel_buf, acc, copies)
         put(send, acc)
         copies = ()
 
 
-def late_kernel(masks, place, plan, panel_buf, tiles, early, *refs):
+def late_kernel(masks, plan, panel_buf, tiles, early, *refs):
     sends, acc = refs[:-1], refs[-1]
     for i, (mask, send) in enumerate(zip(masks, sends)):
         if i == 0 or mask != masks[i - 1]:
-            late_part(mask, place, plan, tiles, early, panel_buf, acc, ())
+            late_part(mask, plan, tiles, early, panel_buf, acc, ())
         put(send, acc)
 
 
-def own_kernel(place, plan, panel_buf, tiles, early, current, previous, coupling, diag, base, acc):
-    late_part(0, place, plan, tiles, early, panel_buf, acc, ())
+def own_kernel(plan, panel_buf, tiles, early, current, previous, coupling, diag, base, acc):
+    late_part(0, plan, tiles, early, panel_buf, acc, ())
     put(base, acc)
     base[...] += diag[...] * current[...] - jnp.dot(
         coupling[...],
@@ -241,10 +252,10 @@
     )
 
 
-def late_part(mask, place, plan, tiles, early, panel_buf, acc, copies):
+def late_part(mask, plan, tiles, early, panel_buf, acc, copies):
     slab_tiles = acc.shape[0] - 1
     row_devs = (early.shape[0] - 1) // slab_tiles
-    first_row = (place[0] ^ mask) * slab_tiles
+    first_row = (row_of(plan) ^ mask) * slab_tiles
     for s in range(slab_tiles):
         acc[s] = early[first_row + s]
     for copy in copies:
@@ -257,14 +268,14 @@
         out[:, s * LANES : (s + 1) * LANES] = acc[s].astype(out.dtype)
 
 
-def coefficient_kernel(cells, received_count, relay, place, base, *refs):
+def coefficient_kernel(cells, received_count, relay, plan, base, *refs):
     received = refs[:received_count]
     mass, current, stored, recurrence, keep, give, halves = refs[received_count:]
     total = base[...]
     for i, ref in enumerate(received):
         value = ref[...].astype(jnp.float32)
         if relay and i == 0:
-            value = jnp.where((place[0] == 1) | (place[0] == 2), 0.0, value)
+            value = jnp.where((row_of(plan) == 1) | (row_of(plan) == 2), 0.0, value)
         total = total + value
     recurrence[...] = total
     weighted = total * (mass[...] * (1.0 / cells))
@@ -275,16 +286,16 @@
     halves[...] = jnp.zeros_like(halves)
     for p, (q, k) in enumerate(blocks(coef.shape)):
         halves[p // halves.shape[1], p % halves.shape[1]] = coef[q : q + 8, k : k + LANES]
-    core = place[1] & 1
+    core = core_of(plan)
     keep[...] = halves[core]
     give[...] = halves[1 - core]
 
 
 def residual_kernel(
-    cells, place, mine, other, recurrence, mass, current, stored, residual, coef_out, gram, halves, packed
+    cells, plan, mine, other, recurrence, mass, current, stored, residual, coef_out, gram, halves, packed
 ):
     width = recurrence.shape[0]
-    core = place[1] & 1
+    core = core_of(plan)
     halves[core] = mine[...]
     halves[1 - core] = other[...]
     for p, (q, k) in enumerate(blocks(packed.shape)):
@@ -382,17 +393,17 @@
         plan, held, early, gathered = pl.pallas_call(
             functools.partial(early_kernel, row_devs, col_devs, slab_tiles),
             out_shape=[
-                jax.ShapeDtypeStruct(plan_shape, jnp.int32),
+                pltpu.SMEM(plan_shape, jnp.int32),
                 pltpu.VMEM(tile_values.shape, bf16),
                 pltpu.VMEM(early_shape, f32),
                 pltpu.VMEM(panel_shape, bf16),
             ],
             in_specs=smem(2) + [pl.BlockSpec(memory_space=pltpu.HBM)] * 3 + anywhere * 2,
-            out_specs=vmem(4),
+            out_specs=smem(1) + vmem(3),
             scratch_shapes=[
                 pltpu.VMEM((1, slots), jnp.int32),
                 pltpu.VMEM((1, slots), jnp.int32),
-                pltpu.SMEM(plan_shape, jnp.int32),
+                pltpu.VMEM(plan_shape, jnp.int32),
                 pltpu.SemaphoreType.DMA((slots // CHUNK,)),
                 pltpu.SemaphoreType.DMA((3,)),
                 pltpu.SemaphoreType.DMA((2,)),
@@ -433,30 +444,30 @@
         first, gathered = pl.pallas_call(
             functools.partial(first_late_kernel, [first_mask], odd),
             out_shape=[part, pltpu.VMEM(panel_shape, bf16)],
-            in_specs=smem(2) + anywhere * len(odd) + vmem(3),
+            in_specs=smem(1) + anywhere * len(odd) + vmem(3),
             out_specs=vmem(2),
             scratch_shapes=[part_acc, pltpu.SemaphoreType.DMA((len(odd),))],
-            input_output_aliases={4 + len(odd): 1},
+            input_output_aliases={3 + len(odd): 1},
             compiler_params=limit(8),
             cost_estimate=cost(width),
-        )(place, plan, *[panels[m] for m in odd], held, early, gathered)
+        )(plan, *[panels[m] for m in odd], held, early, gathered)
         parts = pl.pallas_call(
             functools.partial(late_kernel, masks),
             out_shape=[part, slab, part] if relay else [part] * len(masks),
-            in_specs=smem(2) + vmem(3),
+            in_specs=smem(1) + vmem(3),
             out_specs=vmem(len(masks)),
             scratch_shapes=[part_acc],
             compiler_params=limit(8),
             cost_estimate=cost(width),
-        )(place, plan, gathered, held, early)
+        )(plan, gathered, held, early)
         if relay:
             first = lax.ppermute(first, "row", [(0, 1), (3, 2), (1, 3), (2, 0)])
             joined = (parts[1] + first.astype(f32)).astype(bf16)
             received = [
                 first,
+                lax.ppermute(parts[0], "row", [(0, 3), (3, 0)]),
+                lax.ppermute(joined, "row", [(1, 2), (2, 1)]),
                 swap(parts[2], "row", 1),
-                lax.ppermute(joined, "row", [(1, 2), (2, 1)]),
-                lax.ppermute(parts[0], "row", [(0, 3), (3, 0)]),
             ]
         else:
             received = [swap(first, "row", first_mask)]
@@ -464,12 +475,12 @@
         base = pl.pallas_call(
             own_kernel,
             out_shape=slab,
-            in_specs=smem(2) + vmem(7),
+            in_specs=smem(1) + vmem(7),
             out_specs=vmem(1)[0],
             scratch_shapes=[part_acc],
             compiler_params=limit(8),
             cost_estimate=cost(width),
-        )(place, plan, gathered, held, early, current_block, previous_block, previous_coupling, diag)
+        )(plan, gathered, held, early, current_block, previous_block, previous_coupling, diag)
 
     basis_rows = (stored_count + 1) * width
     padded = (width, -(-basis_rows // LANES) * LANES)
@@ -482,7 +493,7 @@
             out_specs=vmem(3),
             scratch_shapes=[pltpu.VMEM((2,) + half, f32)],
             compiler_params=limit(24),
-        )(place, base, *received, mass, current_block, stored)
+        )(plan, base, *received, mass, current_block, stored)
         mine = keep + swap(give, "col", 1)
         mine = total_by_core(mine)
         other = swap(mine, "col", 1)
@@ -499,7 +510,7 @@
             out_specs=vmem(3),
             scratch_shapes=[pltpu.VMEM((2,) + half, f32), pltpu.VMEM(padded, f32)],
             compiler_params=limit(24),
-        )(place, mine, other, recurrence, mass, current_block, stored)
+        )(plan, mine, other, recurrence, mass, current_block, stored)
         coefficients = coef.T.reshape(stored_count + 1, width, width)
 
     with jax.named_scope("gram"):

time: 75.1 us -> 72.2 us (0.961); the launches traced: 75.7 us -> 71.9 us
  starting transfers between devices: 30.5 us -> 28 us
  Pallas kernels: 15.3 us -> 13.8 us
    ppermute x17, starting transfers between devices: 17.1 us -> 13.6 us  [swap(): return lax.ppermute(value, axis, [(i, i ^ mask) for i in range(count)])]
    ppermute x17, waiting for transfers between devices: 12.7 us -> 14.9 us  [swap(): return lax.ppermute(value, axis, [(i, i ^ mask) for i in range(count)])]
    ppermute x1, starting transfers between devices: 2.43 us -> 4.08 us  [local(): lax.ppermute(parts[0], 'row', [(0, 3), (3, 0)])]
    ppermute x6, waiting for transfers between devices: 6.6 us -> 5.41 us  [total_by_core(): values.append(lax.ppermute(value, ('row', 'col'), trades))]
    ppermute x6, starting transfers between devices: 8.98 us -> 8 us  [total_by_core(): values.append(lax.ppermute(value, ('row', 'col'), trades))]
    ppermute x1, waiting for transfers between devices: 5.58 us -> 4.62 us  [local(): lax.ppermute(parts[0], 'row', [(0, 3), (3, 0)])]
    pallas_call x1, Pallas kernels: 2.67 us -> 1.75 us  [local(): pl.pallas_call(functools.partial(first_late_kernel, [first_mask], odd), o...]
  transfers between devices with their start and end apart: 26 -> 26, of which waited for: 18 -> 18; matrix products, arithmetic and copies ran while one was open for 2% -> 2% of each run, Pallas kernels for 12% -> 13%
where the time goes in v14:
time: 72.2 us; the launch traced here: 71.9 us
  starting transfers between devices  28 us (39%)
  waiting for transfers between devices  25.1 us (35%)
  Pallas kernels  13.8 us (19%)
  other arithmetic  1.81 us (3%)
  local copies, waits for them, and re-layouts  1.66 us (2%)
  between operations  1.49 us (2%)
    ppermute x17, waiting for transfers between devices, swap(): return lax.ppermute(value, axis, [(i, i ^ mask) for i in range(count)])  14.9 us
    ppermute x17, starting transfers between devices, swap(): return lax.ppermute(value, axis, [(i, i ^ mask) for i in range(count)])  13.6 us
    ppermute x6, starting transfers between devices, total_by_core(): values.append(lax.ppermute(value, ('row', 'col'), trades))  8 us
    ppermute x6, waiting for transfers between devices, total_by_core(): values.append(lax.ppermute(value, ('row', 'col'), trades))  5.41 us
    pallas_call x1, Pallas kernels, local(): pl.pallas_call(functools.partial(early_kernel, row_devs, col_devs, slab_t...  5.08 us
    ppermute x1, waiting for transfers between devices, local(): lax.ppermute(parts[0], 'row', [(0, 3), (3, 0)])  4.62 us
    ppermute x1, starting transfers between devices, local(): lax.ppermute(parts[0], 'row', [(0, 3), (3, 0)])  4.08 us
    pallas_call x1, Pallas kernels, local(): pl.pallas_call(functools.partial(late_kernel, masks), out_shape=[part, sl...  2.3 us
  transfers between devices with their start and end apart: 26, of which 18 were waited for; matrix products, arithmetic and copies ran while one was open for 2% of the time, Pallas kernels for 13%

profile of v14, /device:TPU:0, one launch (start us, length us, event | category | flops | bytes accessed | tf_op | source)
XLA Modules:
  0.0 71.9 jit_solution(18354684789917990922)
XLA Ops:
  0.6 1.0 %convert_element_type.9.own_panel = bf16[48,2048]{1,0:T(8,128)(2,1)S(1)} convert(f32[48,2048]{1,0:T(8,128)} %current.3) | non-fusion elementwise | flops 98304 | bytes 589824 | tf_op jit(solution)/shard_map/gather/convert_element_type | solution.py:384
  1.7 0.5 collective-permute-start
  2.2 2.6 %collective-permute-start.1 = (bf16[48,2048]{1,0:T(8,128)(2,1)S(1)}, bf16[48,2048]{1,0:T(8,128)(2,1)S(1)}, u32[]{:S(2)}, u32[]{:S(2)}) collective-permute-start(bf16[48,2048]{1,0:T(8,128)(2,1)S(1)} %convert_element_type.9.own_panel), channel_id=1, source_target_pairs={{0,2},{1,3},{2,0},{3,1},{4,6},{5,7},{6,4},{7,5},{8,10},{9,11},{10,... | collective-permute-start | bytes 589832 | tf_op jit(solution)/shard_map/gather/ppermute | solution.py:21
  4.7 1.5 %collective-permute-start.3 = (bf16[48,2048]{1,0:T(8,128)(2,1)S(1)}, bf16[48,2048]{1,0:T(8,128)(2,1)S(1)}, u32[]{:S(2)}, u32[]{:S(2)}) collective-permute-start(bf16[48,2048]{1,0:T(8,128)(2,1)S(1)} %convert_element_type.9.own_panel), channel_id=1, source_target_pairs={{0,4},{1,5},{2,6},{3,7},{4,0},{5,1},{6,2},{7,3},{8,12},{9,13},{10,... | collective-permute-start | bytes 589832 | tf_op jit(solution)/shard_map/gather/ppermute | solution.py:21
  6.3 0.0 collective-permute-start.5
  6.9 0.1 pad_add_fusion.place
  7.0 0.0 collective-permute-done.near_panel
  7.0 5.1 %early.1 = (s32[1,896]{1,0:T(1,128)S(4)}, bf16[512,128,128]{2,1,0:T(8,128)(2,1)S(1)}, f32[65,48,128]{2,1,0:T(8,128)S(1)}, bf16[9,48,2048]{2,1,0:T(8,128)(2,1)S(1)}) custom-call(s32[2]{0:T(128)S(1)} %pad_add_fusion.place, s32[1]{0:T(128)S(6)} %copy.26.counts, s32[1,512]{1,0:T(1,128)} %bitcast.16, s32[1,512]{1,0:T(1,128)} %bitcast.17, ...), custom_call_target="tpu_custom_call" | custom-call | flops 805306368 | bytes 16777216 | tf_op jit(solution)/shard_map/early/pallas_call | solution.py:393
  12.1 0.0 collective-permute-done.1.value
  12.1 0.2 collective-permute-start.2
  12.4 3.6 %collective-permute-done.3.value = bf16[48,2048]{1,0:T(8,128)(2,1)S(1)} collective-permute-done((bf16[48,2048]{1,0:T(8,128)(2,1)S(1)}, bf16[48,2048]{1,0:T(8,128)(2,1)S(1)}, u32[]{:S(2)}, u32[]{:S(2)}) %collective-permute-start.3) | collective-permute-done | bytes 196640 | tf_op jit(solution)/shard_map/gather/ppermute | solution.py:21
  15.9 0.0 collective-permute-start.4
  15.9 0.5 collective-permute-start.6
  16.4 0.8 %gather.7.refs_5_ = bf16[9,48,2048]{2,1,0:T(8,128)(2,1)S(1)} custom-call(bf16[48,2048]{1,0:T(8,128)(2,1)S(1)} %gather.4.refs_0_, bf16[48,2048]{1,0:T(8,128)(2,1)S(1)} %gather.5.refs_1_, bf16[48,2048]{1,0:T(8,128)(2,1)S(1)} %gather.6.refs_2_, bf16[9,48,2048]{2,1,0:T(8,128)(2,1)S(1)} %get-tuple-element.21.refs_3_), custom_call_target="tpu_custom_call", output_to_operand_aliasing={{}: (3, {})} | custom-call | flops 48 | bytes 1 | tf_op jit(solution)/shard_map/gather/pallas_call | solution.py:428
  17.2 0.2 collective-permute-done.4.refs_1_
  17.4 0.3 collective-permute-done.6.refs_2_
  17.6 1.8 %late.3 = (bf16[48,2048]{1,0:T(8,128)(2,1)S(1)}, bf16[9,48,2048]{2,1,0:T(8,128)(2,1)S(1)}) custom-call(s32[1,896]{1,0:T(1,128)S(4)} %get-tuple-element.18.plan, bf16[48,2048]{1,0:T(8,128)(2,1)S(1)} %collective-permute-done.2.refs_0_, bf16[48,2048]{1,0:T(8,128)(2,1)S(1)} %collective-permute-done.4.refs_1_, ...), custom_call_target="tpu_custom_call", output_to_operand_aliasing={{1}: (6, {})} | custom-call | flops 48 | bytes 1 | tf_op jit(solution)/shard_map/late/pallas_call | solution.py:444
  19.4 1.6 %collective-permute-start.7 = (bf16[48,2048]{1,0:T(8,128)(2,1)S(1)}, bf16[48,2048]{1,0:T(8,128)(2,1)S(1)}, u32[]{:S(2)}, u32[]{:S(2)}) collective-permute-start(bf16[48,2048]{1,0:T(8,128)(2,1)S(1)} %get-tuple-element.23), channel_id=1, source_target_pairs={{0,8},{24,16},{8,24},{16,0},{1,9},{25,17},{9,25},{17,1},{2,10},{26... | collective-permute-start | bytes 589832 | tf_op jit(solution)/shard_map/late/ppermute | solution.py:464
  21.0 2.3 %late.5 = (bf16[48,2048]{1,0:T(8,128)(2,1)S(1)}, f32[48,2048]{1,0:T(8,128)S(1)}, bf16[48,2048]{1,0:T(8,128)(2,1)S(1)}) custom-call(s32[1,896]{1,0:T(1,128)S(4)} %get-tuple-element.18.plan, bf16[9,48,2048]{2,1,0:T(8,128)(2,1)S(1)} %get-tuple-element.22.panel_buf, bf16[512,128,128]{2,1,0:T(8,128)(2,1)S(1)} %get-tuple-element.20.refs_3_.tiles, ...), custom_call_target="tpu_custom_call" | custom-call | flops 48 | bytes 1 | tf_op jit(solution)/shard_map/late/pallas_call | solution.py:454
  23.4 4.1 %collective-permute-start.8 = (bf16[48,2048]{1,0:T(8,128)(2,1)S(1)}, bf16[48,2048]{1,0:T(8,128)(2,1)S(1)}, u32[]{:S(2)}, u32[]{:S(2)}) collective-permute-start(bf16[48,2048]{1,0:T(8,128)(2,1)S(1)} %get-tuple-element.24), channel_id=1, source_target_pairs={{0,24},{24,0},{1,25},{25,1},{2,26},{26,2},{3,27},{27,3},{4,28},{28... | collective-permute-start | bytes 589832 | tf_op jit(solution)/shard_map/late/ppermute | solution.py:468
  27.4 0.1 collective-permute-start.10
  27.5 0.2 collective-permute-done.7.refs_0_
  27.7 0.1 add_convert_fusion
  27.8 0.7 collective-permute-start.9
  28.5 0.0 copy-start
  28.5 0.0 copy-start.3
  28.5 1.4 %late.4.base = f32[48,2048]{1,0:T(8,128)S(1)} custom-call(s32[1,896]{1,0:T(1,128)S(4)} %get-tuple-element.18.plan, bf16[9,48,2048]{2,1,0:T(8,128)(2,1)S(1)} %get-tuple-element.22.panel_buf, bf16[512,128,128]{2,1,0:T(8,128)(2,1)S(1)} %get-tuple-element.20.refs_3_.tiles, f32[65,48,128]{2,1,0:T(8,128)S(1)} %get-tuple-element.19.earlier.refs_4_.early, ...), custom_call_target="tpu_custom_call" | custom-call | flops 48 | bytes 1 | tf_op jit(solution)/shard_map/late/pallas_call | solution.py:475
  29.9 4.6 %collective-permute-done.8.refs_1_ = bf16[48,2048]{1,0:T(8,128)(2,1)S(1)} collective-permute-done((bf16[48,2048]{1,0:T(8,128)(2,1)S(1)}, bf16[48,2048]{1,0:T(8,128)(2,1)S(1)}, u32[]{:S(2)}, u32[]{:S(2)}) %collective-permute-start.8) | collective-permute-done | bytes 196640 | tf_op jit(solution)/shard_map/late/ppermute | solution.py:468
  34.6 3.5 %collective-permute-done.10.refs_3_ = bf16[48,2048]{1,0:T(8,128)(2,1)S(1)} collective-permute-done((bf16[48,2048]{1,0:T(8,128)(2,1)S(1)}, bf16[48,2048]{1,0:T(8,128)(2,1)S(1)}, u32[]{:S(2)}, u32[]{:S(2)}) %collective-permute-start.10) | collective-permute-done | bytes 196640 | tf_op jit(solution)/shard_map/late/ppermute | solution.py:21
  38.1 0.0 collective-permute-done.9.refs_2_
  38.1 1.3 %coefficients.1 = (f32[48,2048]{1,0:T(8,128)S(1)}, f32[12,8,128]{2,1,0:T(8,128)S(1)}, f32[12,8,128]{2,1,0:T(8,128)S(1)}) custom-call(s32[1,896]{1,0:T(1,128)S(4)} %get-tuple-element.18.plan, f32[48,2048]{1,0:T(8,128)S(1)} %late.4.base, bf16[48,2048]{1,0:T(8,128)(2,1)S(1)} %collective-permute-done.7.refs_0_, ...), custom_call_target="tpu_custom_call" | custom-call | tf_op jit(solution)/shard_map/coefficients/pallas_call | solution.py:489
  39.4 0.1 collective-permute-start.11
  39.5 1.2 %collective-permute-done.11 = f32[12,8,128]{2,1,0:T(8,128)S(1)} collective-permute-done((f32[12,8,128]{2,1,0:T(8,128)S(1)}, f32[12,8,128]{2,1,0:T(8,128)S(1)}, u32[]{:S(2)}, u32[]{:S(2)}) %collective-permute-start.11) | collective-permute-done | bytes 49184 | tf_op jit(solution)/shard_map/coefficients/ppermute | solution.py:21
  40.7 1.7 %collective-permute-start.14 = (f32[12,8,128]{2,1,0:T(8,128)S(1)}, f32[12,8,128]{2,1,0:T(8,128)S(1)}, u32[]{:S(2)}, u32[]{:S(2)}) collective-permute-start(f32[12,8,128]{2,1,0:T(8,128)S(1)} %add.46), channel_id=1, source_target_pairs={{0,6},{1,25},{2,4},{3,27},{4,2},{5,29},{6,0},{7,31},{8,14},{9,17},... | collective-permute-start | bytes 147464 | tf_op jit(solution)/shard_map/coefficients/ppermute | solution.py:44
  42.4 0.5 collective-permute-start.13
  42.9 1.3 %collective-permute-start.12 = (f32[12,8,128]{2,1,0:T(8,128)S(1)}, f32[12,8,128]{2,1,0:T(8,128)S(1)}, u32[]{:S(2)}, u32[]{:S(2)}) collective-permute-start(f32[12,8,128]{2,1,0:T(8,128)S(1)} %add.46), channel_id=1, source_target_pairs={{0,2},{1,9},{2,0},{3,11},{4,6},{5,13},{6,4},{7,15},{8,10},{9,1},{1... | collective-permute-start | bytes 147464 | tf_op jit(solution)/shard_map/coefficients/ppermute | solution.py:44
  44.2 1.5 %collective-permute-done.14 = f32[12,8,128]{2,1,0:T(8,128)S(1)} collective-permute-done((f32[12,8,128]{2,1,0:T(8,128)S(1)}, f32[12,8,128]{2,1,0:T(8,128)S(1)}, u32[]{:S(2)}, u32[]{:S(2)}) %collective-permute-start.14) | collective-permute-done | bytes 49184 | tf_op jit(solution)/shard_map/coefficients/ppermute | solution.py:44
  45.7 0.7 collective-permute-done.13
  46.4 0.5 collective-permute-done.12
  47.0 2.0 %collective-permute-start.17 = (f32[12,8,128]{2,1,0:T(8,128)S(1)}, f32[12,8,128]{2,1,0:T(8,128)S(1)}, u32[]{:S(2)}, u32[]{:S(2)}) collective-permute-start(f32[12,8,128]{2,1,0:T(8,128)S(1)} %add_add_fusion.1), channel_id=1, source_target_pairs={{0,24},{1,7},{2,26},{3,5},{4,28},{5,3},{6,30},{7,1},{8,16},{9,15},... | collective-permute-start | bytes 147464 | tf_op jit(solution)/shard_map/coefficients/ppermute | solution.py:44
  49.0 0.5 collective-permute-start.16
  49.5 2.0 %collective-permute-start.15 = (f32[12,8,128]{2,1,0:T(8,128)S(1)}, f32[12,8,128]{2,1,0:T(8,128)S(1)}, u32[]{:S(2)}, u32[]{:S(2)}) collective-permute-start(f32[12,8,128]{2,1,0:T(8,128)S(1)} %add_add_fusion.1), channel_id=1, source_target_pairs={{0,8},{1,3},{2,10},{3,1},{4,12},{5,7},{6,14},{7,5},{8,0},{9,11},{1... | collective-permute-start | bytes 147464 | tf_op jit(solution)/shard_map/coefficients/ppermute | solution.py:44
  51.4 1.5 %collective-permute-done.17 = f32[12,8,128]{2,1,0:T(8,128)S(1)} collective-permute-done((f32[12,8,128]{2,1,0:T(8,128)S(1)}, f32[12,8,128]{2,1,0:T(8,128)S(1)}, u32[]{:S(2)}, u32[]{:S(2)}) %collective-permute-start.17) | collective-permute-done | bytes 49184 | tf_op jit(solution)/shard_map/coefficients/ppermute | solution.py:44
  52.9 1.2 %collective-permute-done.16 = f32[12,8,128]{2,1,0:T(8,128)S(1)} collective-permute-done((f32[12,8,128]{2,1,0:T(8,128)S(1)}, f32[12,8,128]{2,1,0:T(8,128)S(1)}, u32[]{:S(2)}, u32[]{:S(2)}) %collective-permute-start.16) | collective-permute-done | bytes 49184 | tf_op jit(solution)/shard_map/coefficients/ppermute | solution.py:44
  54.1 0.0 collective-permute-done.15
  54.1 0.1 collective-permute-start.18
  54.2 1.2 %collective-permute-done.18.other = f32[12,8,128]{2,1,0:T(8,128)S(1)} collective-permute-done((f32[12,8,128]{2,1,0:T(8,128)S(1)}, f32[12,8,128]{2,1,0:T(8,128)S(1)}, u32[]{:S(2)}, u32[]{:S(2)}) %collective-permute-start.18) | collective-permute-done | bytes 49184 | tf_op jit(solution)/shard_map/coefficients/ppermute | solution.py:21
  55.4 1.2 %residual.1 = (f32[48,2048]{1,0:T(8,128)S(1)}, f32[48,432]{1,0:T(8,128)S(1)}, f32[24,128]{1,0:T(8,128)S(1)}) custom-call(s32[1,896]{1,0:T(1,128)S(4)} %get-tuple-element.18.plan, f32[12,8,128]{2,1,0:T(8,128)S(1)} %add_add_fusion.mine, f32[12,8,128]{2,1,0:T(8,128)S(1)} %collective-permute-done.18.other, f32[48,2048]{1,0:T(8,128)S(1)} %get-tuple-element.29.recurrence, ...), custom_call_target="tpu_custom_call" | custom-call | tf_op jit(solution)/shard_map/residual/pallas_call | solution.py:502
  56.6 0.2 collective-permute-start.19
  56.8 1.0 %collective-permute-done.19 = f32[24,128]{1,0:T(8,128)S(1)} collective-permute-done((f32[24,128]{1,0:T(8,128)S(1)}, f32[24,128]{1,0:T(8,128)S(1)}, u32[]{:S(2)}, u32[]{:S(2)}) %collective-permute-start.19) | collective-permute-done | bytes 12320 | tf_op jit(solution)/shard_map/gram/ppermute | solution.py:21
  57.8 2.2 %collective-permute-start.22 = (f32[24,128]{1,0:T(8,128)S(1)}, f32[24,128]{1,0:T(8,128)S(1)}, u32[]{:S(2)}, u32[]{:S(2)}) collective-permute-start(f32[24,128]{1,0:T(8,128)S(1)} %add.53), channel_id=1, source_target_pairs={{0,6},{1,7},{2,4},{3,5},{4,2},{5,3},{6,0},{7,1},{8,14},{9,15},{10,... | collective-permute-start | bytes 36872 | tf_op jit(solution)/shard_map/gram/ppermute | solution.py:21
  60.0 1.0 %collective-permute-start.21 = (f32[24,128]{1,0:T(8,128)S(1)}, f32[24,128]{1,0:T(8,128)S(1)}, u32[]{:S(2)}, u32[]{:S(2)}) collective-permute-start(f32[24,128]{1,0:T(8,128)S(1)} %add.53), channel_id=1, source_target_pairs={{0,4},{1,5},{2,6},{3,7},{4,0},{5,1},{6,2},{7,3},{8,12},{9,13},{10,... | collective-permute-start | bytes 36872 | tf_op jit(solution)/shard_map/gram/ppermute | solution.py:21
  61.1 0.2 collective-permute-start.20
  61.3 1.1 %collective-permute-done.22 = f32[24,128]{1,0:T(8,128)S(1)} collective-permute-done((f32[24,128]{1,0:T(8,128)S(1)}, f32[24,128]{1,0:T(8,128)S(1)}, u32[]{:S(2)}, u32[]{:S(2)}) %collective-permute-start.22) | collective-permute-done | bytes 12320 | tf_op jit(solution)/shard_map/gram/ppermute | solution.py:21
  62.4 1.3 %collective-permute-done.21 = f32[24,128]{1,0:T(8,128)S(1)} collective-permute-done((f32[24,128]{1,0:T(8,128)S(1)}, f32[24,128]{1,0:T(8,128)S(1)}, u32[]{:S(2)}, u32[]{:S(2)}) %collective-permute-start.21) | collective-permute-done | bytes 12320 | tf_op jit(solution)/shard_map/gram/ppermute | solution.py:21
  63.7 1.0 %collective-permute-done.20 = f32[24,128]{1,0:T(8,128)S(1)} collective-permute-done((f32[24,128]{1,0:T(8,128)S(1)}, f32[24,128]{1,0:T(8,128)S(1)}, u32[]{:S(2)}, u32[]{:S(2)}) %collective-permute-start.20) | collective-permute-done | bytes 12320 | tf_op jit(solution)/shard_map/gram/ppermute | solution.py:21
  64.8 1.8 %collective-permute-start.25 = (f32[24,128]{1,0:T(8,128)S(1)}, f32[24,128]{1,0:T(8,128)S(1)}, u32[]{:S(2)}, u32[]{:S(2)}) collective-permute-start(f32[24,128]{1,0:T(8,128)S(1)} %add_add_fusion.3), channel_id=1, source_target_pairs={{0,24},{8,16},{16,8},{24,0},{1,25},{9,17},{17,9},{25,1},{2,26},{10... | collective-permute-start | bytes 36872 | tf_op jit(solution)/shard_map/gram/ppermute | solution.py:21
  66.6 0.6 collective-permute-start.24
  67.2 2.0 %collective-permute-start.23 = (f32[24,128]{1,0:T(8,128)S(1)}, f32[24,128]{1,0:T(8,128)S(1)}, u32[]{:S(2)}, u32[]{:S(2)}) collective-permute-start(f32[24,128]{1,0:T(8,128)S(1)} %add_add_fusion.3), channel_id=1, source_target_pairs={{0,8},{8,0},{16,24},{24,16},{1,9},{9,1},{17,25},{25,17},{2,10},{10... | collective-permute-start | bytes 36872 | tf_op jit(solution)/shard_map/gram/ppermute | solution.py:21
  69.2 0.7 %copy.25 = f32[48,2048]{1,0:T(8,128)} copy(f32[48,2048]{1,0:T(8,128)S(1)} %get-tuple-element.38) | data formatting | bytes 786432
  69.9 0.8 %copy.19 = f32[432,48]{1,0:T(8,128)} copy(f32[432,48]{0,1:T(8,128)S(1)} %bitcast.11) | data formatting | bytes 165888 | tf_op jit(solution)/shard_map/residual/transpose | solution.py:514
  70.8 0.4 collective-permute-done.24
  71.2 0.1 fusion
  71.3 0.6 pad_maximum_fusion
  (23 shorter events, 0.1 us)
Async XLA Ops:
  1.7 5.4 %collective-permute-start = (bf16[48,2048]{1,0:T(8,128)(2,1)S(1)}, bf16[48,2048]{1,0:T(8,128)(2,1)S(1)}, u32[]{:S(2)}, u32[]{:S(2)}) collective-permute-start(bf16[48,2048]{1,0:T(8,128)(2,1)S(1)} %convert_element_type.9.own_panel), channel_id=1, source_target_pairs={{0,1},{1,0},{2,3},{3,2},{4,5},{5,4},{6,7},{7,6},{8,9},{9,8},{10,11... | collective-permute-start | bytes 589832 | tf_op jit(solution)/shard_map/gather/ppermute | solution.py:21
  2.2 9.9 %collective-permute-start.1 = (bf16[48,2048]{1,0:T(8,128)(2,1)S(1)}, bf16[48,2048]{1,0:T(8,128)(2,1)S(1)}, u32[]{:S(2)}, u32[]{:S(2)}) collective-permute-start(bf16[48,2048]{1,0:T(8,128)(2,1)S(1)} %convert_element_type.9.own_panel), channel_id=1, source_target_pairs={{0,2},{1,3},{2,0},{3,1},{4,6},{5,7},{6,4},{7,5},{8,10},{9,11},{10,... | collective-permute-start | bytes 589832 | tf_op jit(solution)/shard_map/gather/ppermute | solution.py:21
  4.7 11.2 %collective-permute-start.3 = (bf16[48,2048]{1,0:T(8,128)(2,1)S(1)}, bf16[48,2048]{1,0:T(8,128)(2,1)S(1)}, u32[]{:S(2)}, u32[]{:S(2)}) collective-permute-start(bf16[48,2048]{1,0:T(8,128)(2,1)S(1)} %convert_element_type.9.own_panel), channel_id=1, source_target_pairs={{0,4},{1,5},{2,6},{3,7},{4,0},{5,1},{6,2},{7,3},{8,12},{9,13},{10,... | collective-permute-start | bytes 589832 | tf_op jit(solution)/shard_map/gather/ppermute | solution.py:21
  6.3 9.7 %collective-permute-start.5 = (bf16[48,2048]{1,0:T(8,128)(2,1)S(1)}, bf16[48,2048]{1,0:T(8,128)(2,1)S(1)}, u32[]{:S(2)}, u32[]{:S(2)}) collective-permute-start(bf16[48,2048]{1,0:T(8,128)(2,1)S(1)} %convert_element_type.9.own_panel), channel_id=1, source_target_pairs={{0,6},{1,7},{2,4},{3,5},{4,2},{5,3},{6,0},{7,1},{8,14},{9,15},{10,... | collective-permute-start | bytes 589832 | tf_op jit(solution)/shard_map/gather/ppermute | solution.py:21
  12.1 5.1 %collective-permute-start.2 = (bf16[48,2048]{1,0:T(8,128)(2,1)S(1)}, bf16[48,2048]{1,0:T(8,128)(2,1)S(1)}, u32[]{:S(2)}, u32[]{:S(2)}) collective-permute-start(bf16[48,2048]{1,0:T(8,128)(2,1)S(1)} %gather.4.refs_0_), channel_id=1, source_target_pairs={{0,1},{1,0},{2,3},{3,2},{4,5},{5,4},{6,7},{7,6},{8,9},{9,8},{10,11... | collective-permute-start | bytes 589832 | tf_op jit(solution)/shard_map/gather/ppermute | solution.py:21
  15.9 1.4 %collective-permute-start.4 = (bf16[48,2048]{1,0:T(8,128)(2,1)S(1)}, bf16[48,2048]{1,0:T(8,128)(2,1)S(1)}, u32[]{:S(2)}, u32[]{:S(2)}) collective-permute-start(bf16[48,2048]{1,0:T(8,128)(2,1)S(1)} %gather.5.refs_1_), channel_id=1, source_target_pairs={{0,1},{1,0},{2,3},{3,2},{4,5},{5,4},{6,7},{7,6},{8,9},{9,8},{10,11... | collective-permute-start | bytes 589832 | tf_op jit(solution)/shard_map/gather/ppermute | solution.py:21
  15.9 1.7 %collective-permute-start.6 = (bf16[48,2048]{1,0:T(8,128)(2,1)S(1)}, bf16[48,2048]{1,0:T(8,128)(2,1)S(1)}, u32[]{:S(2)}, u32[]{:S(2)}) collective-permute-start(bf16[48,2048]{1,0:T(8,128)(2,1)S(1)} %gather.6.refs_2_), channel_id=1, source_target_pairs={{0,1},{1,0},{2,3},{3,2},{4,5},{5,4},{6,7},{7,6},{8,9},{9,8},{10,11... | collective-permute-start | bytes 589832 | tf_op jit(solution)/shard_map/gather/ppermute | solution.py:21
  19.4 8.3 %collective-permute-start.7 = (bf16[48,2048]{1,0:T(8,128)(2,1)S(1)}, bf16[48,2048]{1,0:T(8,128)(2,1)S(1)}, u32[]{:S(2)}, u32[]{:S(2)}) collective-permute-start(bf16[48,2048]{1,0:T(8,128)(2,1)S(1)} %get-tuple-element.23), channel_id=1, source_target_pairs={{0,8},{24,16},{8,24},{16,0},{1,9},{25,17},{9,25},{17,1},{2,10},{26... | collective-permute-start | bytes 589832 | tf_op jit(solution)/shard_map/late/ppermute | solution.py:464
  21.0 7.4 %copy-start.1 = (f32[48,2048]{1,0:T(8,128)S(1)}, f32[48,2048]{1,0:T(8,128)}, u32[]{:S(2)}) copy-start(f32[48,2048]{1,0:T(8,128)} %current.3) | copy-start | bytes 1179652
  21.0 7.4 %copy-start.2 = (f32[48,2048]{1,0:T(8,128)S(1)}, f32[48,2048]{1,0:T(8,128)}, u32[]{:S(2)}) copy-start(f32[48,2048]{1,0:T(8,128)} %previous.1) | copy-start | bytes 1179652
  21.0 7.4 %copy-start.4 = (f32[48,48]{1,0:T(8,128)S(1)}, f32[48,48]{1,0:T(8,128)}, u32[]{:S(2)}) copy-start(f32[48,48]{1,0:T(8,128)} %coupling.1) | copy-start | bytes 27652
  21.0 7.4 %copy-start.5 = (f32[2048]{0:T(1024)S(1)}, f32[2048]{0:T(1024)}, u32[]{:S(2)}) copy-start(f32[2048]{0:T(1024)} %param.14) | copy-start | bytes 24580
  23.4 11.2 %collective-permute-start.8 = (bf16[48,2048]{1,0:T(8,128)(2,1)S(1)}, bf16[48,2048]{1,0:T(8,128)(2,1)S(1)}, u32[]{:S(2)}, u32[]{:S(2)}) collective-permute-start(bf16[48,2048]{1,0:T(8,128)(2,1)S(1)} %get-tuple-element.24), channel_id=1, source_target_pairs={{0,24},{24,0},{1,25},{25,1},{2,26},{26,2},{3,27},{27,3},{4,28},{28... | collective-permute-start | bytes 589832 | tf_op jit(solution)/shard_map/late/ppermute | solution.py:468
  27.4 10.6 %collective-permute-start.10 = (bf16[48,2048]{1,0:T(8,128)(2,1)S(1)}, bf16[48,2048]{1,0:T(8,128)(2,1)S(1)}, u32[]{:S(2)}, u32[]{:S(2)}) collective-permute-start(bf16[48,2048]{1,0:T(8,128)(2,1)S(1)} %get-tuple-element.26), channel_id=1, source_target_pairs={{0,8},{8,0},{16,24},{24,16},{1,9},{9,1},{17,25},{25,17},{2,10},{10... | collective-permute-start | bytes 589832 | tf_op jit(solution)/shard_map/late/ppermute | solution.py:21
  27.8 10.3 %collective-permute-start.9 = (bf16[48,2048]{1,0:T(8,128)(2,1)S(1)}, bf16[48,2048]{1,0:T(8,128)(2,1)S(1)}, u32[]{:S(2)}, u32[]{:S(2)}) collective-permute-start(bf16[48,2048]{1,0:T(8,128)(2,1)S(1)} %add_convert_fusion), channel_id=1, source_target_pairs={{8,16},{16,8},{9,17},{17,9},{10,18},{18,10},{11,19},{19,11},{12,20... | collective-permute-start | bytes 589832 | tf_op jit(solution)/shard_map/late/ppermute | solution.py:469
  28.5 9.6 %copy-start = (f32[8,48,2048]{2,1,0:T(8,128)S(1)}, f32[8,48,2048]{2,1,0:T(8,128)}, u32[]{:S(2)}) copy-start(f32[8,48,2048]{2,1,0:T(8,128)} %param.13) | copy-start | bytes 9437188
  28.5 9.6 %copy-start.3 = (f32[2048]{0:T(1024)S(1)}, f32[2048]{0:T(1024)}, u32[]{:S(2)}) copy-start(f32[2048]{0:T(1024)} %param.15) | copy-start | bytes 24580
  39.4 1.3 %collective-permute-start.11 = (f32[12,8,128]{2,1,0:T(8,128)S(1)}, f32[12,8,128]{2,1,0:T(8,128)S(1)}, u32[]{:S(2)}, u32[]{:S(2)}) collective-permute-start(f32[12,8,128]{2,1,0:T(8,128)S(1)} %get-tuple-element.28), channel_id=1, source_target_pairs={{0,1},{1,0},{2,3},{3,2},{4,5},{5,4},{6,7},{7,6},{8,9},{9,8},{10,11... | collective-permute-start | bytes 147464 | tf_op jit(solution)/shard_map/coefficients/ppermute | solution.py:21
  40.7 5.0 %collective-permute-start.14 = (f32[12,8,128]{2,1,0:T(8,128)S(1)}, f32[12,8,128]{2,1,0:T(8,128)S(1)}, u32[]{:S(2)}, u32[]{:S(2)}) collective-permute-start(f32[12,8,128]{2,1,0:T(8,128)S(1)} %add.46), channel_id=1, source_target_pairs={{0,6},{1,25},{2,4},{3,27},{4,2},{5,29},{6,0},{7,31},{8,14},{9,17},... | collective-permute-start | bytes 147464 | tf_op jit(solution)/shard_map/coefficients/ppermute | solution.py:44
  42.4 4.1 %collective-permute-start.13 = (f32[12,8,128]{2,1,0:T(8,128)S(1)}, f32[12,8,128]{2,1,0:T(8,128)S(1)}, u32[]{:S(2)}, u32[]{:S(2)}) collective-permute-start(f32[12,8,128]{2,1,0:T(8,128)S(1)} %add.46), channel_id=1, source_target_pairs={{0,4},{1,17},{2,6},{3,19},{4,0},{5,21},{6,2},{7,23},{8,12},{9,25},... | collective-permute-start | bytes 147464 | tf_op jit(solution)/shard_map/coefficients/ppermute | solution.py:44
  42.9 4.1 %collective-permute-start.12 = (f32[12,8,128]{2,1,0:T(8,128)S(1)}, f32[12,8,128]{2,1,0:T(8,128)S(1)}, u32[]{:S(2)}, u32[]{:S(2)}) collective-permute-start(f32[12,8,128]{2,1,0:T(8,128)S(1)} %add.46), channel_id=1, source_target_pairs={{0,2},{1,9},{2,0},{3,11},{4,6},{5,13},{6,4},{7,15},{8,10},{9,1},{1... | collective-permute-start | bytes 147464 | tf_op jit(solution)/shard_map/coefficients/ppermute | solution.py:44
  47.0 6.0 %collective-permute-start.17 = (f32[12,8,128]{2,1,0:T(8,128)S(1)}, f32[12,8,128]{2,1,0:T(8,128)S(1)}, u32[]{:S(2)}, u32[]{:S(2)}) collective-permute-start(f32[12,8,128]{2,1,0:T(8,128)S(1)} %add_add_fusion.1), channel_id=1, source_target_pairs={{0,24},{1,7},{2,26},{3,5},{4,28},{5,3},{6,30},{7,1},{8,16},{9,15},... | collective-permute-start | bytes 147464 | tf_op jit(solution)/shard_map/coefficients/ppermute | solution.py:44
  49.0 5.1 %collective-permute-start.16 = (f32[12,8,128]{2,1,0:T(8,128)S(1)}, f32[12,8,128]{2,1,0:T(8,128)S(1)}, u32[]{:S(2)}, u32[]{:S(2)}) collective-permute-start(f32[12,8,128]{2,1,0:T(8,128)S(1)} %add_add_fusion.1), channel_id=1, source_target_pairs={{0,16},{1,5},{2,18},{3,7},{4,20},{5,1},{6,22},{7,3},{8,24},{9,13},... | collective-permute-start | bytes 147464 | tf_op jit(solution)/shard_map/coefficients/ppermute | solution.py:44
  49.5 4.6 %collective-permute-start.15 = (f32[12,8,128]{2,1,0:T(8,128)S(1)}, f32[12,8,128]{2,1,0:T(8,128)S(1)}, u32[]{:S(2)}, u32[]{:S(2)}) collective-permute-start(f32[12,8,128]{2,1,0:T(8,128)S(1)} %add_add_fusion.1), channel_id=1, source_target_pairs={{0,8},{1,3},{2,10},{3,1},{4,12},{5,7},{6,14},{7,5},{8,0},{9,11},{1... | collective-permute-start | bytes 147464 | tf_op jit(solution)/shard_map/coefficients/ppermute | solution.py:44
  54.1 1.3 %collective-permute-start.18 = (f32[12,8,128]{2,1,0:T(8,128)S(1)}, f32[12,8,128]{2,1,0:T(8,128)S(1)}, u32[]{:S(2)}, u32[]{:S(2)}) collective-permute-start(f32[12,8,128]{2,1,0:T(8,128)S(1)} %add_add_fusion.mine), channel_id=1, source_target_pairs={{0,1},{1,0},{2,3},{3,2},{4,5},{5,4},{6,7},{7,6},{8,9},{9,8},{10,11... | collective-permute-start | bytes 147464 | tf_op jit(solution)/shard_map/coefficients/ppermute | solution.py:21
  56.6 1.2 %collective-permute-start.19 = (f32[24,128]{1,0:T(8,128)S(1)}, f32[24,128]{1,0:T(8,128)S(1)}, u32[]{:S(2)}, u32[]{:S(2)}) collective-permute-start(f32[24,128]{1,0:T(8,128)S(1)} %get-tuple-element.32), channel_id=1, source_target_pairs={{0,1},{1,0},{2,3},{3,2},{4,5},{5,4},{6,7},{7,6},{8,9},{9,8},{10,11... | collective-permute-start | bytes 36872 | tf_op jit(solution)/shard_map/gram/ppermute | solution.py:21
  57.8 4.6 %collective-permute-start.22 = (f32[24,128]{1,0:T(8,128)S(1)}, f32[24,128]{1,0:T(8,128)S(1)}, u32[]{:S(2)}, u32[]{:S(2)}) collective-permute-start(f32[24,128]{1,0:T(8,128)S(1)} %add.53), channel_id=1, source_target_pairs={{0,6},{1,7},{2,4},{3,5},{4,2},{5,3},{6,0},{7,1},{8,14},{9,15},{10,... | collective-permute-start | bytes 36872 | tf_op jit(solution)/shard_map/gram/ppermute | solution.py:21
  60.0 3.7 %collective-permute-start.21 = (f32[24,128]{1,0:T(8,128)S(1)}, f32[24,128]{1,0:T(8,128)S(1)}, u32[]{:S(2)}, u32[]{:S(2)}) collective-permute-start(f32[24,128]{1,0:T(8,128)S(1)} %add.53), channel_id=1, source_target_pairs={{0,4},{1,5},{2,6},{3,7},{4,0},{5,1},{6,2},{7,3},{8,12},{9,13},{10,... | collective-permute-start | bytes 36872 | tf_op jit(solution)/shard_map/gram/ppermute | solution.py:21
  61.1 3.7 %collective-permute-start.20 = (f32[24,128]{1,0:T(8,128)S(1)}, f32[24,128]{1,0:T(8,128)S(1)}, u32[]{:S(2)}, u32[]{:S(2)}) collective-permute-start(f32[24,128]{1,0:T(8,128)S(1)} %add.53), channel_id=1, source_target_pairs={{0,2},{1,3},{2,0},{3,1},{4,6},{5,7},{6,4},{7,5},{8,10},{9,11},{10,... | collective-permute-start | bytes 36872 | tf_op jit(solution)/shard_map/gram/ppermute | solution.py:21
  64.8 6.0 %collective-permute-start.25 = (f32[24,128]{1,0:T(8,128)S(1)}, f32[24,128]{1,0:T(8,128)S(1)}, u32[]{:S(2)}, u32[]{:S(2)}) collective-permute-start(f32[24,128]{1,0:T(8,128)S(1)} %add_add_fusion.3), channel_id=1, source_target_pairs={{0,24},{8,16},{16,8},{24,0},{1,25},{9,17},{17,9},{25,1},{2,26},{10... | collective-permute-start | bytes 36872 | tf_op jit(solution)/shard_map/gram/ppermute | solution.py:21
  66.6 4.6 %collective-permute-start.24 = (f32[24,128]{1,0:T(8,128)S(1)}, f32[24,128]{1,0:T(8,128)S(1)}, u32[]{:S(2)}, u32[]{:S(2)}) collective-permute-start(f32[24,128]{1,0:T(8,128)S(1)} %add_add_fusion.3), channel_id=1, source_target_pairs={{0,16},{8,24},{16,0},{24,8},{1,17},{9,25},{17,1},{25,9},{2,18},{10... | collective-permute-start | bytes 36872 | tf_op jit(solution)/shard_map/gram/ppermute | solution.py:21
  67.2 4.0 %collective-permute-start.23 = (f32[24,128]{1,0:T(8,128)S(1)}, f32[24,128]{1,0:T(8,128)S(1)}, u32[]{:S(2)}, u32[]{:S(2)}) collective-permute-start(f32[24,128]{1,0:T(8,128)S(1)} %add_add_fusion.3), channel_id=1, source_target_pairs={{0,8},{8,0},{16,24},{24,16},{1,9},{9,1},{17,25},{25,17},{2,10},{10... | collective-permute-start | bytes 36872 | tf_op jit(solution)/shard_map/gram/ppermute | solution.py:21

commit v15 on v14

--- a/solution.py
+++ b/solution.py
@@ -22,13 +22,17 @@
 
 
 def tree_sum(values):
+    values = [values[m] for m in sorted(values)]
     while len(values) > 1:
         values = [values[i] + values[i + 1] for i in range(0, len(values), 2)]
     return values[0]
 
 
 def total(value, axis, step):
-    return tree_sum([value] + [swap(value, axis, m) for m in range(step, lax.axis_size(axis), step)])
+    values = {0: value}
+    for m in range(lax.axis_size(axis) - step, 0, -step):
+        values[m] = swap(value, axis, m)
+    return tree_sum(values)
 
 
 def total_by_core(value):
@@ -37,11 +41,11 @@
         return total(total(value, "col", 2), "row", 1)
     places = [(r, c) for r in range(row_devs) for c in range(col_devs)]
     for turn in range(2):
-        values = [value]
-        for m in range(1, row_devs):
+        values = {0: value}
+        for m in range(row_devs - 1, 0, -1):
             partners = [(r, c ^ (2 * m)) if c % 2 == turn else (r ^ m, c) for r, c in places]
             trades = [(i, r * col_devs + c) for i, (r, c) in enumerate(partners)]
-            values.append(lax.ppermute(value, ("row", "col"), trades))
+            values[m] = lax.ppermute(value, ("row", "col"), trades)
         value = tree_sum(values)
     return value
 
@@ -268,9 +272,28 @@
         out[:, s * LANES : (s + 1) * LANES] = acc[s].astype(out.dtype)
 
 
-def coefficient_kernel(cells, received_count, relay, plan, base, *refs):
+def half_basis(half, current, stored):
+    rows = (current.shape[0] + stored.shape[0]) // 2
+    cut = rows - current.shape[0]
+    return jnp.where(half == 0, jnp.concatenate([current[...], stored[:cut]], axis=0), stored[cut:])
+
+
+def pack(coef, out):
+    spare = -coef.shape[1] % LANES
+    coef = jnp.concatenate([coef, jnp.zeros((coef.shape[0], spare), jnp.float32)], axis=1)
+    for p, (q, k) in enumerate(blocks(coef.shape)):
+        out[p] = coef[q : q + 8, k : k + LANES]
+
+
+def unpack(pieces, width, columns):
+    groups = pieces.shape[0] * 8 // width
+    rows = [jnp.concatenate([pieces[p + g] for g in range(groups)], axis=1) for p in range(0, pieces.shape[0], groups)]
+    return jnp.concatenate(rows, axis=0)[:, :columns]
+
+
+def give_kernel(cells, received_count, relay, plan, base, *refs):
     received = refs[:received_count]
-    mass, current, stored, recurrence, keep, give, halves = refs[received_count:]
+    mass, current, stored, recurrence, give = refs[received_count:]
     total = base[...]
     for i, ref in enumerate(received):
         value = ref[...].astype(jnp.float32)
@@ -279,32 +302,29 @@
         total = total + value
     recurrence[...] = total
     weighted = total * (mass[...] * (1.0 / cells))
-    basis = jnp.concatenate([current[...], stored[...]], axis=0)
-    coef = dot_split(weighted, basis, NT)
-    spare = -coef.shape[1] % LANES
-    coef = jnp.concatenate([coef, jnp.zeros((coef.shape[0], spare), jnp.float32)], axis=1)
-    halves[...] = jnp.zeros_like(halves)
-    for p, (q, k) in enumerate(blocks(coef.shape)):
-        halves[p // halves.shape[1], p % halves.shape[1]] = coef[q : q + 8, k : k + LANES]
+    pack(dot_split(weighted, half_basis(1 - core_of(plan), current, stored), NT), give)
+
+
+def keep_kernel(cells, plan, recurrence, mass, current, stored, keep):
+    weighted = recurrence[...] * (mass[...] * (1.0 / cells))
+    pack(dot_split(weighted, half_basis(core_of(plan), current, stored), NT), keep)
+
+
+def less_kernel(plan, mine, recurrence, current, stored, less):
+    basis = half_basis(core_of(plan), current, stored)
+    less[...] = recurrence[...] - dot_split(unpack(mine, recurrence.shape[0], basis.shape[0]), basis)
+
+
+def residual_kernel(cells, plan, mine, other, less, mass, current, stored, residual, coef_out, gram):
+    width = less.shape[0]
     core = core_of(plan)
-    keep[...] = halves[core]
-    give[...] = halves[1 - core]
-
-
-def residual_kernel(
-    cells, plan, mine, other, recurrence, mass, current, stored, residual, coef_out, gram, halves, packed
-):
-    width = recurrence.shape[0]
-    core = core_of(plan)
-    halves[core] = mine[...]
-    halves[1 - core] = other[...]
-    for p, (q, k) in enumerate(blocks(packed.shape)):
-        packed[q : q + 8, k : k + LANES] = halves[p // halves.shape[1], p % halves.shape[1]]
-    coef = packed[...]
-    basis = jnp.concatenate([current[...], stored[...]], axis=0)
-    coef = coef[:, : basis.shape[0]]
-    coef_out[...] = coef
-    value = recurrence[...] - dot_split(coef, basis)
+    basis = half_basis(1 - core, current, stored)
+    own_coef = unpack(mine, width, basis.shape[0])
+    other_coef = unpack(other, width, basis.shape[0])
+    coef_out[...] = jnp.concatenate(
+        [jnp.where(core == 0, own_coef, other_coef), jnp.where(core == 0, other_coef, own_coef)], axis=1
+    )
+    value = less[...] - dot_split(other_coef, basis)
     residual[...] = value
     local = dot_split(value * (mass[...] * (1.0 / cells)), value, NT)
     half = width // 2
@@ -383,7 +403,7 @@
     with jax.named_scope("gather"):
         rounded = current_block.astype(bf16)
         panels = [rounded] + [None] * (col_devs - 1)
-        for m in range(col_devs - 2, 0, -2):
+        for m in range(2, col_devs, 2):
             panels[m] = swap(rounded, "col", m)
         panels[1] = swap(rounded, "col", 1)
 
@@ -421,7 +441,7 @@
         )
 
     with jax.named_scope("gather"):
-        for m in range(col_devs - 2, 0, -2):
+        for m in range(2, col_devs, 2):
             panels[m] = after(panels[m], early)
             panels[m + 1] = swap(panels[m], "col", 1)
         even, odd = list(range(2, col_devs, 2)), list(range(3, col_devs, 2))
@@ -483,22 +503,38 @@
         )(plan, gathered, held, early, current_block, previous_block, previous_coupling, diag)
 
     basis_rows = (stored_count + 1) * width
-    padded = (width, -(-basis_rows // LANES) * LANES)
-    half = (-(-len(blocks(padded)) // 2), 8, LANES)
+    half = (width // 8 * -(-basis_rows // 2 // LANES), 8, LANES)
+    half = jax.ShapeDtypeStruct(half, f32)
     with jax.named_scope("coefficients"):
-        recurrence, keep, give = pl.pallas_call(
-            functools.partial(coefficient_kernel, cells, len(received), relay),
-            out_shape=[slab] + [jax.ShapeDtypeStruct(half, f32)] * 2,
+        recurrence, give = pl.pallas_call(
+            functools.partial(give_kernel, cells, len(received), relay),
+            out_shape=[slab, half],
             in_specs=smem(1) + vmem(len(received) + 4),
-            out_specs=vmem(3),
-            scratch_shapes=[pltpu.VMEM((2,) + half, f32)],
-            compiler_params=limit(24),
+            out_specs=vmem(2),
+            compiler_params=limit(16),
+            cost_estimate=cost(width),
         )(plan, base, *received, mass, current_block, stored)
+        keep = pl.pallas_call(
+            functools.partial(keep_kernel, cells),
+            out_shape=half,
+            in_specs=smem(1) + vmem(4),
+            out_specs=vmem(1)[0],
+            compiler_params=limit(16),
+            cost_estimate=cost(width),
+        )(plan, recurrence, mass, current_block, stored)
         mine = keep + swap(give, "col", 1)
         mine = total_by_core(mine)
         other = swap(mine, "col", 1)
 
     with jax.named_scope("residual"):
+        less = pl.pallas_call(
+            less_kernel,
+            out_shape=slab,
+            in_specs=smem(1) + vmem(4),
+            out_specs=vmem(1)[0],
+            compiler_params=limit(16),
+            cost_estimate=cost(width),
+        )(plan, mine, recurrence, current_block, stored)
         residual_block, coef, gram = pl.pallas_call(
             functools.partial(residual_kernel, cells),
             out_shape=[
@@ -508,9 +544,9 @@
             ],
             in_specs=smem(1) + vmem(6),
             out_specs=vmem(3),
-            scratch_shapes=[pltpu.VMEM((2,) + half, f32), pltpu.VMEM(padded, f32)],
-            compiler_params=limit(24),
-        )(plan, mine, other, recurrence, mass, current_block, stored)
+            compiler_params=limit(16),
+            cost_estimate=cost(width),
+        )(plan, mine, other, less, mass, current_block, stored)
         coefficients = coef.T.reshape(stored_count + 1, width, width)
 
     with jax.named_scope("gram"):

time: 72.2 us -> 71.3 us (0.988)
  waiting for transfers between devices: 25.1 us -> 22.2 us
  starting transfers between devices: 28 us -> 30.5 us
    ppermute x17, waiting for transfers between devices: 14.9 us -> 11.9 us  [swap(): return lax.ppermute(value, axis, [(i, i ^ mask) for i in range(count)])]
    ppermute x1, starting transfers between devices: 4.08 us -> 6.12 us  [local(): lax.ppermute(parts[0], 'row', [(0, 3), (3, 0)])]
    ppermute x6, waiting for transfers between devices: 5.41 us -> 6.23 us  [total_by_core(): values[m] = lax.ppermute(value, ('row', 'col'), trades)]
    pallas_call x1 -> x3, Pallas kernels: 1.28 us -> 1.98 us  [the longest x1 0.7 us: local(): pl.pallas_call(functools.partial(keep_kernel, cells), out_shape=half, in_...]
  transfers between devices with their start and end apart: 26 -> 26, of which waited for: 18 -> 18; matrix products, arithmetic and copies ran while one was open for 2% -> 2% of each run, Pallas kernels for 13% -> 14%
where the time goes in v15:
time: 71.3 us; the launch traced here: 71 us
  starting transfers between devices  30.5 us (43%)
  waiting for transfers between devices  22.2 us (31%)
  Pallas kernels  13.3 us (19%)
  other arithmetic  1.8 us (3%)
  local copies, waits for them, and re-layouts  1.66 us (2%)
  between operations  1.53 us (2%)
    ppermute x17, starting transfers between devices, swap(): return lax.ppermute(value, axis, [(i, i ^ mask) for i in range(count)])  13.5 us
    ppermute x17, waiting for transfers between devices, swap(): return lax.ppermute(value, axis, [(i, i ^ mask) for i in range(count)])  11.9 us
    ppermute x6, starting transfers between devices, total_by_core(): values[m] = lax.ppermute(value, ('row', 'col'), trades)  8 us
    ppermute x6, waiting for transfers between devices, total_by_core(): values[m] = lax.ppermute(value, ('row', 'col'), trades)  6.23 us
    ppermute x1, starting transfers between devices, local(): lax.ppermute(parts[0], 'row', [(0, 3), (3, 0)])  6.12 us
    pallas_call x1, Pallas kernels, local(): pl.pallas_call(functools.partial(early_kernel, row_devs, col_devs, slab_t...  4.78 us
    ppermute x1, waiting for transfers between devices, local(): lax.ppermute(parts[0], 'row', [(0, 3), (3, 0)])  4.1 us
    pallas_call x1, Pallas kernels, local(): pl.pallas_call(functools.partial(late_kernel, masks), out_shape=[part, sl...  2.31 us
  transfers between devices with their start and end apart: 26, of which 18 were waited for; matrix products, arithmetic and copies ran while one was open for 2% of the time, Pallas kernels for 14%

profile of v15, /device:TPU:0, one launch (start us, length us, event | category | flops | bytes accessed | tf_op | source)
XLA Modules:
  0.0 71.0 jit_solution(8480663655226307865)
XLA Ops:
  0.6 1.0 %convert_element_type.9.own_panel = bf16[48,2048]{1,0:T(8,128)(2,1)S(1)} convert(f32[48,2048]{1,0:T(8,128)} %current.7) | non-fusion elementwise | flops 98304 | bytes 589824 | tf_op jit(solution)/shard_map/gather/convert_element_type | solution.py:404
  1.7 0.5 collective-permute-start
  2.2 2.6 %collective-permute-start.1 = (bf16[48,2048]{1,0:T(8,128)(2,1)S(1)}, bf16[48,2048]{1,0:T(8,128)(2,1)S(1)}, u32[]{:S(2)}, u32[]{:S(2)}) collective-permute-start(bf16[48,2048]{1,0:T(8,128)(2,1)S(1)} %convert_element_type.9.own_panel), channel_id=1, source_target_pairs={{0,2},{1,3},{2,0},{3,1},{4,6},{5,7},{6,4},{7,5},{8,10},{9,11},{10,... | collective-permute-start | bytes 589832 | tf_op jit(solution)/shard_map/gather/ppermute | solution.py:21
  4.7 1.5 %collective-permute-start.3 = (bf16[48,2048]{1,0:T(8,128)(2,1)S(1)}, bf16[48,2048]{1,0:T(8,128)(2,1)S(1)}, u32[]{:S(2)}, u32[]{:S(2)}) collective-permute-start(bf16[48,2048]{1,0:T(8,128)(2,1)S(1)} %convert_element_type.9.own_panel), channel_id=1, source_target_pairs={{0,4},{1,5},{2,6},{3,7},{4,0},{5,1},{6,2},{7,3},{8,12},{9,13},{10,... | collective-permute-start | bytes 589832 | tf_op jit(solution)/shard_map/gather/ppermute | solution.py:21
  6.3 0.0 collective-permute-start.5
  6.9 0.1 pad_add_fusion.place
  7.0 0.0 collective-permute-done.near_panel
  7.0 4.8 %early.1 = (s32[1,896]{1,0:T(1,128)S(4)}, bf16[512,128,128]{2,1,0:T(8,128)(2,1)S(1)}, f32[65,48,128]{2,1,0:T(8,128)S(1)}, bf16[9,48,2048]{2,1,0:T(8,128)(2,1)S(1)}) custom-call(s32[2]{0:T(128)S(1)} %pad_add_fusion.place, s32[1]{0:T(128)S(6)} %copy.26.counts, s32[1,512]{1,0:T(1,128)} %bitcast.19, s32[1,512]{1,0:T(1,128)} %bitcast.20, ...), custom_call_target="tpu_custom_call" | custom-call | flops 805306368 | bytes 16777216 | tf_op jit(solution)/shard_map/early/pallas_call | solution.py:413
  11.8 0.1 collective-permute-start.2
  11.9 4.0 %collective-permute-done.3.value = bf16[48,2048]{1,0:T(8,128)(2,1)S(1)} collective-permute-done((bf16[48,2048]{1,0:T(8,128)(2,1)S(1)}, bf16[48,2048]{1,0:T(8,128)(2,1)S(1)}, u32[]{:S(2)}, u32[]{:S(2)}) %collective-permute-start.3) | collective-permute-done | bytes 196640 | tf_op jit(solution)/shard_map/gather/ppermute | solution.py:21
  15.9 0.0 collective-permute-start.4
  15.9 0.0 collective-permute-done.5.value
  15.9 0.5 collective-permute-start.6
  16.4 0.8 %gather.7.refs_5_ = bf16[9,48,2048]{2,1,0:T(8,128)(2,1)S(1)} custom-call(bf16[48,2048]{1,0:T(8,128)(2,1)S(1)} %gather.4.refs_0_, bf16[48,2048]{1,0:T(8,128)(2,1)S(1)} %gather.5.refs_1_, bf16[48,2048]{1,0:T(8,128)(2,1)S(1)} %gather.6.refs_2_, bf16[9,48,2048]{2,1,0:T(8,128)(2,1)S(1)} %get-tuple-element.20.refs_3_), custom_call_target="tpu_custom_call", output_to_operand_aliasing={{}: (3, {})} | custom-call | flops 48 | bytes 1 | tf_op jit(solution)/shard_map/gather/pallas_call | solution.py:448
  17.2 0.0 collective-permute-done.2.refs_0_
  17.2 0.2 collective-permute-done.4.refs_1_
  17.4 0.3 collective-permute-done.6.refs_2_
  17.6 1.8 %late.3 = (bf16[48,2048]{1,0:T(8,128)(2,1)S(1)}, bf16[9,48,2048]{2,1,0:T(8,128)(2,1)S(1)}) custom-call(s32[1,896]{1,0:T(1,128)S(4)} %get-tuple-element.17.plan, bf16[48,2048]{1,0:T(8,128)(2,1)S(1)} %collective-permute-done.2.refs_0_, bf16[48,2048]{1,0:T(8,128)(2,1)S(1)} %collective-permute-done.4.refs_1_, ...), custom_call_target="tpu_custom_call", output_to_operand_aliasing={{1}: (6, {})} | custom-call | flops 48 | bytes 1 | tf_op jit(solution)/shard_map/late/pallas_call | solution.py:464
  19.4 2.2 %collective-permute-start.7 = (bf16[48,2048]{1,0:T(8,128)(2,1)S(1)}, bf16[48,2048]{1,0:T(8,128)(2,1)S(1)}, u32[]{:S(2)}, u32[]{:S(2)}) collective-permute-start(bf16[48,2048]{1,0:T(8,128)(2,1)S(1)} %get-tuple-element.22), channel_id=1, source_target_pairs={{0,8},{24,16},{8,24},{16,0},{1,9},{25,17},{9,25},{17,1},{2,10},{26... | collective-permute-start | bytes 589832 | tf_op jit(solution)/shard_map/late/ppermute | solution.py:484
  21.7 2.3 %late.5 = (bf16[48,2048]{1,0:T(8,128)(2,1)S(1)}, f32[48,2048]{1,0:T(8,128)S(1)}, bf16[48,2048]{1,0:T(8,128)(2,1)S(1)}) custom-call(s32[1,896]{1,0:T(1,128)S(4)} %get-tuple-element.17.plan, bf16[9,48,2048]{2,1,0:T(8,128)(2,1)S(1)} %get-tuple-element.21.panel_buf, bf16[512,128,128]{2,1,0:T(8,128)(2,1)S(1)} %get-tuple-element.19.refs_3_.tiles, ...), custom_call_target="tpu_custom_call" | custom-call | flops 48 | bytes 1 | tf_op jit(solution)/shard_map/late/pallas_call | solution.py:474
  24.0 6.1 %collective-permute-start.8 = (bf16[48,2048]{1,0:T(8,128)(2,1)S(1)}, bf16[48,2048]{1,0:T(8,128)(2,1)S(1)}, u32[]{:S(2)}, u32[]{:S(2)}) collective-permute-start(bf16[48,2048]{1,0:T(8,128)(2,1)S(1)} %get-tuple-element.23), channel_id=1, source_target_pairs={{0,24},{24,0},{1,25},{25,1},{2,26},{26,2},{3,27},{27,3},{4,28},{28... | collective-permute-start | bytes 589832 | tf_op jit(solution)/shard_map/late/ppermute | solution.py:488
  30.1 0.1 collective-permute-start.10
  30.2 0.7 collective-permute-start.9
  31.0 0.0 copy-start
  31.0 0.0 copy-start.3
  31.0 0.8 %late.4.base = f32[48,2048]{1,0:T(8,128)S(1)} custom-call(s32[1,896]{1,0:T(1,128)S(4)} %get-tuple-element.17.plan, bf16[9,48,2048]{2,1,0:T(8,128)(2,1)S(1)} %get-tuple-element.21.panel_buf, bf16[512,128,128]{2,1,0:T(8,128)(2,1)S(1)} %get-tuple-element.19.refs_3_.tiles, f32[65,48,128]{2,1,0:T(8,128)S(1)} %get-tuple-element.18.earlier.refs_4_.early, ...), custom_call_target="tpu_custom_call" | custom-call | flops 48 | bytes 1 | tf_op jit(solution)/shard_map/late/pallas_call | solution.py:495
  31.8 4.1 %collective-permute-done.8.refs_1_ = bf16[48,2048]{1,0:T(8,128)(2,1)S(1)} collective-permute-done((bf16[48,2048]{1,0:T(8,128)(2,1)S(1)}, bf16[48,2048]{1,0:T(8,128)(2,1)S(1)}, u32[]{:S(2)}, u32[]{:S(2)}) %collective-permute-start.8) | collective-permute-done | bytes 196640 | tf_op jit(solution)/shard_map/late/ppermute | solution.py:488
  35.9 2.1 %collective-permute-done.10.refs_3_ = bf16[48,2048]{1,0:T(8,128)(2,1)S(1)} collective-permute-done((bf16[48,2048]{1,0:T(8,128)(2,1)S(1)}, bf16[48,2048]{1,0:T(8,128)(2,1)S(1)}, u32[]{:S(2)}, u32[]{:S(2)}) %collective-permute-start.10) | collective-permute-done | bytes 196640 | tf_op jit(solution)/shard_map/late/ppermute | solution.py:21
  38.0 0.7 coefficients.2
  38.7 0.1 collective-permute-start.11
  38.8 0.7 coefficients.3
  39.5 0.5 collective-permute-done.11
  40.0 1.3 %collective-permute-start.14 = (f32[12,8,128]{2,1,0:T(8,128)S(1)}, f32[12,8,128]{2,1,0:T(8,128)S(1)}, u32[]{:S(2)}, u32[]{:S(2)}) collective-permute-start(f32[12,8,128]{2,1,0:T(8,128)S(1)} %add.46), channel_id=1, source_target_pairs={{0,6},{1,25},{2,4},{3,27},{4,2},{5,29},{6,0},{7,31},{8,14},{9,17},... | collective-permute-start | bytes 147464 | tf_op jit(solution)/shard_map/coefficients/ppermute | solution.py:48
  41.3 0.8 %collective-permute-start.13 = (f32[12,8,128]{2,1,0:T(8,128)S(1)}, f32[12,8,128]{2,1,0:T(8,128)S(1)}, u32[]{:S(2)}, u32[]{:S(2)}) collective-permute-start(f32[12,8,128]{2,1,0:T(8,128)S(1)} %add.46), channel_id=1, source_target_pairs={{0,4},{1,17},{2,6},{3,19},{4,0},{5,21},{6,2},{7,23},{8,12},{9,25},... | collective-permute-start | bytes 147464 | tf_op jit(solution)/shard_map/coefficients/ppermute | solution.py:48
  42.2 1.4 %collective-permute-start.12 = (f32[12,8,128]{2,1,0:T(8,128)S(1)}, f32[12,8,128]{2,1,0:T(8,128)S(1)}, u32[]{:S(2)}, u32[]{:S(2)}) collective-permute-start(f32[12,8,128]{2,1,0:T(8,128)S(1)} %add.46), channel_id=1, source_target_pairs={{0,2},{1,9},{2,0},{3,11},{4,6},{5,13},{6,4},{7,15},{8,10},{9,1},{1... | collective-permute-start | bytes 147464 | tf_op jit(solution)/shard_map/coefficients/ppermute | solution.py:48
  43.6 1.5 %collective-permute-done.14 = f32[12,8,128]{2,1,0:T(8,128)S(1)} collective-permute-done((f32[12,8,128]{2,1,0:T(8,128)S(1)}, f32[12,8,128]{2,1,0:T(8,128)S(1)}, u32[]{:S(2)}, u32[]{:S(2)}) %collective-permute-start.14) | collective-permute-done | bytes 49184 | tf_op jit(solution)/shard_map/coefficients/ppermute | solution.py:48
  45.1 0.5 collective-permute-done.13
  45.6 0.7 collective-permute-done.12
  46.3 2.1 %collective-permute-start.17 = (f32[12,8,128]{2,1,0:T(8,128)S(1)}, f32[12,8,128]{2,1,0:T(8,128)S(1)}, u32[]{:S(2)}, u32[]{:S(2)}) collective-permute-start(f32[12,8,128]{2,1,0:T(8,128)S(1)} %add_add_fusion.1), channel_id=1, source_target_pairs={{0,24},{1,7},{2,26},{3,5},{4,28},{5,3},{6,30},{7,1},{8,16},{9,15},... | collective-permute-start | bytes 147464 | tf_op jit(solution)/shard_map/coefficients/ppermute | solution.py:48
  48.4 1.5 %collective-permute-start.16 = (f32[12,8,128]{2,1,0:T(8,128)S(1)}, f32[12,8,128]{2,1,0:T(8,128)S(1)}, u32[]{:S(2)}, u32[]{:S(2)}) collective-permute-start(f32[12,8,128]{2,1,0:T(8,128)S(1)} %add_add_fusion.1), channel_id=1, source_target_pairs={{0,16},{1,5},{2,18},{3,7},{4,20},{5,1},{6,22},{7,3},{8,24},{9,13},... | collective-permute-start | bytes 147464 | tf_op jit(solution)/shard_map/coefficients/ppermute | solution.py:48
  49.9 0.9 %collective-permute-start.15 = (f32[12,8,128]{2,1,0:T(8,128)S(1)}, f32[12,8,128]{2,1,0:T(8,128)S(1)}, u32[]{:S(2)}, u32[]{:S(2)}) collective-permute-start(f32[12,8,128]{2,1,0:T(8,128)S(1)} %add_add_fusion.1), channel_id=1, source_target_pairs={{0,8},{1,3},{2,10},{3,1},{4,12},{5,7},{6,14},{7,5},{8,0},{9,11},{1... | collective-permute-start | bytes 147464 | tf_op jit(solution)/shard_map/coefficients/ppermute | solution.py:48
  50.8 1.6 %collective-permute-done.17 = f32[12,8,128]{2,1,0:T(8,128)S(1)} collective-permute-done((f32[12,8,128]{2,1,0:T(8,128)S(1)}, f32[12,8,128]{2,1,0:T(8,128)S(1)}, u32[]{:S(2)}, u32[]{:S(2)}) %collective-permute-start.17) | collective-permute-done | bytes 49184 | tf_op jit(solution)/shard_map/coefficients/ppermute | solution.py:48
  52.4 1.6 %collective-permute-done.16 = f32[12,8,128]{2,1,0:T(8,128)S(1)} collective-permute-done((f32[12,8,128]{2,1,0:T(8,128)S(1)}, f32[12,8,128]{2,1,0:T(8,128)S(1)}, u32[]{:S(2)}, u32[]{:S(2)}) %collective-permute-start.16) | collective-permute-done | bytes 49184 | tf_op jit(solution)/shard_map/coefficients/ppermute | solution.py:48
  54.0 0.3 collective-permute-done.15
  54.3 0.1 collective-permute-start.18
  54.4 0.6 residual.2.less
  55.0 0.6 collective-permute-done.18.other
  55.6 0.9 %residual.3 = (f32[48,2048]{1,0:T(8,128)S(1)}, f32[48,432]{1,0:T(8,128)S(1)}, f32[24,128]{1,0:T(8,128)S(1)}) custom-call(s32[1,896]{1,0:T(1,128)S(4)} %get-tuple-element.17.plan, f32[12,8,128]{2,1,0:T(8,128)S(1)} %add_add_fusion.mine, f32[12,8,128]{2,1,0:T(8,128)S(1)} %collective-permute-done.18.other, f32[48,2048]{1,0:T(8,128)S(1)} %residual.2.less, ...), custom_call_target="tpu_custom_call" | custom-call | flops 48 | bytes 1 | tf_op jit(solution)/shard_map/residual/pallas_call | solution.py:538
  56.5 0.2 collective-permute-start.19
  56.7 1.0 %collective-permute-done.19 = f32[24,128]{1,0:T(8,128)S(1)} collective-permute-done((f32[24,128]{1,0:T(8,128)S(1)}, f32[24,128]{1,0:T(8,128)S(1)}, u32[]{:S(2)}, u32[]{:S(2)}) %collective-permute-start.19) | collective-permute-done | bytes 12320 | tf_op jit(solution)/shard_map/gram/ppermute | solution.py:21
  57.7 2.3 %collective-permute-start.22 = (f32[24,128]{1,0:T(8,128)S(1)}, f32[24,128]{1,0:T(8,128)S(1)}, u32[]{:S(2)}, u32[]{:S(2)}) collective-permute-start(f32[24,128]{1,0:T(8,128)S(1)} %add.53), channel_id=1, source_target_pairs={{0,6},{1,7},{2,4},{3,5},{4,2},{5,3},{6,0},{7,1},{8,14},{9,15},{10,... | collective-permute-start | bytes 36872 | tf_op jit(solution)/shard_map/gram/ppermute | solution.py:21
  60.0 0.3 collective-permute-start.21
  60.3 0.9 %collective-permute-start.20 = (f32[24,128]{1,0:T(8,128)S(1)}, f32[24,128]{1,0:T(8,128)S(1)}, u32[]{:S(2)}, u32[]{:S(2)}) collective-permute-start(f32[24,128]{1,0:T(8,128)S(1)} %add.53), channel_id=1, source_target_pairs={{0,2},{1,3},{2,0},{3,1},{4,6},{5,7},{6,4},{7,5},{8,10},{9,11},{10,... | collective-permute-start | bytes 36872 | tf_op jit(solution)/shard_map/gram/ppermute | solution.py:21
  61.2 1.1 %collective-permute-done.22 = f32[24,128]{1,0:T(8,128)S(1)} collective-permute-done((f32[24,128]{1,0:T(8,128)S(1)}, f32[24,128]{1,0:T(8,128)S(1)}, u32[]{:S(2)}, u32[]{:S(2)}) %collective-permute-start.22) | collective-permute-done | bytes 12320 | tf_op jit(solution)/shard_map/gram/ppermute | solution.py:21
  62.3 1.4 %collective-permute-done.21 = f32[24,128]{1,0:T(8,128)S(1)} collective-permute-done((f32[24,128]{1,0:T(8,128)S(1)}, f32[24,128]{1,0:T(8,128)S(1)}, u32[]{:S(2)}, u32[]{:S(2)}) %collective-permute-start.21) | collective-permute-done | bytes 12320 | tf_op jit(solution)/shard_map/gram/ppermute | solution.py:21
  63.7 0.3 collective-permute-done.20
  64.0 1.7 %collective-permute-start.25 = (f32[24,128]{1,0:T(8,128)S(1)}, f32[24,128]{1,0:T(8,128)S(1)}, u32[]{:S(2)}, u32[]{:S(2)}) collective-permute-start(f32[24,128]{1,0:T(8,128)S(1)} %add_add_fusion.3), channel_id=1, source_target_pairs={{0,24},{8,16},{16,8},{24,0},{1,25},{9,17},{17,9},{25,1},{2,26},{10... | collective-permute-start | bytes 36872 | tf_op jit(solution)/shard_map/gram/ppermute | solution.py:21
  65.7 0.6 collective-permute-start.24
  66.3 2.1 %collective-permute-start.23 = (f32[24,128]{1,0:T(8,128)S(1)}, f32[24,128]{1,0:T(8,128)S(1)}, u32[]{:S(2)}, u32[]{:S(2)}) collective-permute-start(f32[24,128]{1,0:T(8,128)S(1)} %add_add_fusion.3), channel_id=1, source_target_pairs={{0,8},{8,0},{16,24},{24,16},{1,9},{9,1},{17,25},{25,17},{2,10},{10... | collective-permute-start | bytes 36872 | tf_op jit(solution)/shard_map/gram/ppermute | solution.py:21
  68.4 0.7 %copy.25 = f32[48,2048]{1,0:T(8,128)} copy(f32[48,2048]{1,0:T(8,128)S(1)} %get-tuple-element.36) | data formatting | bytes 786432
  69.2 0.8 %copy.19 = f32[432,48]{1,0:T(8,128)} copy(f32[432,48]{0,1:T(8,128)S(1)} %bitcast.13) | data formatting | bytes 165888 | tf_op jit(solution)/shard_map/residual/transpose | solution.py:550
  70.0 0.3 collective-permute-done.24
  70.3 0.1 fusion
  70.4 0.6 pad_maximum_fusion
  (25 shorter events, 0.1 us)
Async XLA Ops:
  1.7 5.4 %collective-permute-start = (bf16[48,2048]{1,0:T(8,128)(2,1)S(1)}, bf16[48,2048]{1,0:T(8,128)(2,1)S(1)}, u32[]{:S(2)}, u32[]{:S(2)}) collective-permute-start(bf16[48,2048]{1,0:T(8,128)(2,1)S(1)} %convert_element_type.9.own_panel), channel_id=1, source_target_pairs={{0,1},{1,0},{2,3},{3,2},{4,5},{5,4},{6,7},{7,6},{8,9},{9,8},{10,11... | collective-permute-start | bytes 589832 | tf_op jit(solution)/shard_map/gather/ppermute | solution.py:21
  2.2 9.6 %collective-permute-start.1 = (bf16[48,2048]{1,0:T(8,128)(2,1)S(1)}, bf16[48,2048]{1,0:T(8,128)(2,1)S(1)}, u32[]{:S(2)}, u32[]{:S(2)}) collective-permute-start(bf16[48,2048]{1,0:T(8,128)(2,1)S(1)} %convert_element_type.9.own_panel), channel_id=1, source_target_pairs={{0,2},{1,3},{2,0},{3,1},{4,6},{5,7},{6,4},{7,5},{8,10},{9,11},{10,... | collective-permute-start | bytes 589832 | tf_op jit(solution)/shard_map/gather/ppermute | solution.py:21
  4.7 11.2 %collective-permute-start.3 = (bf16[48,2048]{1,0:T(8,128)(2,1)S(1)}, bf16[48,2048]{1,0:T(8,128)(2,1)S(1)}, u32[]{:S(2)}, u32[]{:S(2)}) collective-permute-start(bf16[48,2048]{1,0:T(8,128)(2,1)S(1)} %convert_element_type.9.own_panel), channel_id=1, source_target_pairs={{0,4},{1,5},{2,6},{3,7},{4,0},{5,1},{6,2},{7,3},{8,12},{9,13},{10,... | collective-permute-start | bytes 589832 | tf_op jit(solution)/shard_map/gather/ppermute | solution.py:21
  6.3 9.7 %collective-permute-start.5 = (bf16[48,2048]{1,0:T(8,128)(2,1)S(1)}, bf16[48,2048]{1,0:T(8,128)(2,1)S(1)}, u32[]{:S(2)}, u32[]{:S(2)}) collective-permute-start(bf16[48,2048]{1,0:T(8,128)(2,1)S(1)} %convert_element_type.9.own_panel), channel_id=1, source_target_pairs={{0,6},{1,7},{2,4},{3,5},{4,2},{5,3},{6,0},{7,1},{8,14},{9,15},{10,... | collective-permute-start | bytes 589832 | tf_op jit(solution)/shard_map/gather/ppermute | solution.py:21
  11.8 5.4 %collective-permute-start.2 = (bf16[48,2048]{1,0:T(8,128)(2,1)S(1)}, bf16[48,2048]{1,0:T(8,128)(2,1)S(1)}, u32[]{:S(2)}, u32[]{:S(2)}) collective-permute-start(bf16[48,2048]{1,0:T(8,128)(2,1)S(1)} %gather.4.refs_0_), channel_id=1, source_target_pairs={{0,1},{1,0},{2,3},{3,2},{4,5},{5,4},{6,7},{7,6},{8,9},{9,8},{10,11... | collective-permute-start | bytes 589832 | tf_op jit(solution)/shard_map/gather/ppermute | solution.py:21
  15.9 1.4 %collective-permute-start.4 = (bf16[48,2048]{1,0:T(8,128)(2,1)S(1)}, bf16[48,2048]{1,0:T(8,128)(2,1)S(1)}, u32[]{:S(2)}, u32[]{:S(2)}) collective-permute-start(bf16[48,2048]{1,0:T(8,128)(2,1)S(1)} %gather.5.refs_1_), channel_id=1, source_target_pairs={{0,1},{1,0},{2,3},{3,2},{4,5},{5,4},{6,7},{7,6},{8,9},{9,8},{10,11... | collective-permute-start | bytes 589832 | tf_op jit(solution)/shard_map/gather/ppermute | solution.py:21
  15.9 1.7 %collective-permute-start.6 = (bf16[48,2048]{1,0:T(8,128)(2,1)S(1)}, bf16[48,2048]{1,0:T(8,128)(2,1)S(1)}, u32[]{:S(2)}, u32[]{:S(2)}) collective-permute-start(bf16[48,2048]{1,0:T(8,128)(2,1)S(1)} %gather.6.refs_2_), channel_id=1, source_target_pairs={{0,1},{1,0},{2,3},{3,2},{4,5},{5,4},{6,7},{7,6},{8,9},{9,8},{10,11... | collective-permute-start | bytes 589832 | tf_op jit(solution)/shard_map/gather/ppermute | solution.py:21
  19.4 10.8 %collective-permute-start.7 = (bf16[48,2048]{1,0:T(8,128)(2,1)S(1)}, bf16[48,2048]{1,0:T(8,128)(2,1)S(1)}, u32[]{:S(2)}, u32[]{:S(2)}) collective-permute-start(bf16[48,2048]{1,0:T(8,128)(2,1)S(1)} %get-tuple-element.22), channel_id=1, source_target_pairs={{0,8},{24,16},{8,24},{16,0},{1,9},{25,17},{9,25},{17,1},{2,10},{26... | collective-permute-start | bytes 589832 | tf_op jit(solution)/shard_map/late/ppermute | solution.py:484
  21.6 9.3 %copy-start.1 = (f32[48,2048]{1,0:T(8,128)S(1)}, f32[48,2048]{1,0:T(8,128)}, u32[]{:S(2)}) copy-start(f32[48,2048]{1,0:T(8,128)} %current.7) | copy-start | bytes 1179652
  21.6 9.3 %copy-start.2 = (f32[48,2048]{1,0:T(8,128)S(1)}, f32[48,2048]{1,0:T(8,128)}, u32[]{:S(2)}) copy-start(f32[48,2048]{1,0:T(8,128)} %previous.1) | copy-start | bytes 1179652
  21.7 9.3 %copy-start.4 = (f32[48,48]{1,0:T(8,128)S(1)}, f32[48,48]{1,0:T(8,128)}, u32[]{:S(2)}) copy-start(f32[48,48]{1,0:T(8,128)} %coupling.1) | copy-start | bytes 27652
  21.7 9.3 %copy-start.5 = (f32[2048]{0:T(1024)S(1)}, f32[2048]{0:T(1024)}, u32[]{:S(2)}) copy-start(f32[2048]{0:T(1024)} %param.14) | copy-start | bytes 24580
  24.0 11.9 %collective-permute-start.8 = (bf16[48,2048]{1,0:T(8,128)(2,1)S(1)}, bf16[48,2048]{1,0:T(8,128)(2,1)S(1)}, u32[]{:S(2)}, u32[]{:S(2)}) collective-permute-start(bf16[48,2048]{1,0:T(8,128)(2,1)S(1)} %get-tuple-element.23), channel_id=1, source_target_pairs={{0,24},{24,0},{1,25},{25,1},{2,26},{26,2},{3,27},{27,3},{4,28},{28... | collective-permute-start | bytes 589832 | tf_op jit(solution)/shard_map/late/ppermute | solution.py:488
  30.1 7.9 %collective-permute-start.10 = (bf16[48,2048]{1,0:T(8,128)(2,1)S(1)}, bf16[48,2048]{1,0:T(8,128)(2,1)S(1)}, u32[]{:S(2)}, u32[]{:S(2)}) collective-permute-start(bf16[48,2048]{1,0:T(8,128)(2,1)S(1)} %get-tuple-element.25), channel_id=1, source_target_pairs={{0,8},{8,0},{16,24},{24,16},{1,9},{9,1},{17,25},{25,17},{2,10},{10... | collective-permute-start | bytes 589832 | tf_op jit(solution)/shard_map/late/ppermute | solution.py:21
  30.2 7.8 %collective-permute-start.9 = (bf16[48,2048]{1,0:T(8,128)(2,1)S(1)}, bf16[48,2048]{1,0:T(8,128)(2,1)S(1)}, u32[]{:S(2)}, u32[]{:S(2)}) collective-permute-start(bf16[48,2048]{1,0:T(8,128)(2,1)S(1)} %add_convert_fusion), channel_id=1, source_target_pairs={{8,16},{16,8},{9,17},{17,9},{10,18},{18,10},{11,19},{19,11},{12,20... | collective-permute-start | bytes 589832 | tf_op jit(solution)/shard_map/late/ppermute | solution.py:489
  31.0 7.1 %copy-start = (f32[8,48,2048]{2,1,0:T(8,128)S(1)}, f32[8,48,2048]{2,1,0:T(8,128)}, u32[]{:S(2)}) copy-start(f32[8,48,2048]{2,1,0:T(8,128)} %param.13) | copy-start | bytes 9437188
  31.0 7.1 %copy-start.3 = (f32[2048]{0:T(1024)S(1)}, f32[2048]{0:T(1024)}, u32[]{:S(2)}) copy-start(f32[2048]{0:T(1024)} %param.15) | copy-start | bytes 24580
  38.7 1.3 %collective-permute-start.11 = (f32[12,8,128]{2,1,0:T(8,128)S(1)}, f32[12,8,128]{2,1,0:T(8,128)S(1)}, u32[]{:S(2)}, u32[]{:S(2)}) collective-permute-start(f32[12,8,128]{2,1,0:T(8,128)S(1)} %get-tuple-element.27), channel_id=1, source_target_pairs={{0,1},{1,0},{2,3},{3,2},{4,5},{5,4},{6,7},{7,6},{8,9},{9,8},{10,11... | collective-permute-start | bytes 147464 | tf_op jit(solution)/shard_map/coefficients/ppermute | solution.py:21
  40.0 5.1 %collective-permute-start.14 = (f32[12,8,128]{2,1,0:T(8,128)S(1)}, f32[12,8,128]{2,1,0:T(8,128)S(1)}, u32[]{:S(2)}, u32[]{:S(2)}) collective-permute-start(f32[12,8,128]{2,1,0:T(8,128)S(1)} %add.46), channel_id=1, source_target_pairs={{0,6},{1,25},{2,4},{3,27},{4,2},{5,29},{6,0},{7,31},{8,14},{9,17},... | collective-permute-start | bytes 147464 | tf_op jit(solution)/shard_map/coefficients/ppermute | solution.py:48
  41.3 4.3 %collective-permute-start.13 = (f32[12,8,128]{2,1,0:T(8,128)S(1)}, f32[12,8,128]{2,1,0:T(8,128)S(1)}, u32[]{:S(2)}, u32[]{:S(2)}) collective-permute-start(f32[12,8,128]{2,1,0:T(8,128)S(1)} %add.46), channel_id=1, source_target_pairs={{0,4},{1,17},{2,6},{3,19},{4,0},{5,21},{6,2},{7,23},{8,12},{9,25},... | collective-permute-start | bytes 147464 | tf_op jit(solution)/shard_map/coefficients/ppermute | solution.py:48
  42.2 4.1 %collective-permute-start.12 = (f32[12,8,128]{2,1,0:T(8,128)S(1)}, f32[12,8,128]{2,1,0:T(8,128)S(1)}, u32[]{:S(2)}, u32[]{:S(2)}) collective-permute-start(f32[12,8,128]{2,1,0:T(8,128)S(1)} %add.46), channel_id=1, source_target_pairs={{0,2},{1,9},{2,0},{3,11},{4,6},{5,13},{6,4},{7,15},{8,10},{9,1},{1... | collective-permute-start | bytes 147464 | tf_op jit(solution)/shard_map/coefficients/ppermute | solution.py:48
  46.3 6.1 %collective-permute-start.17 = (f32[12,8,128]{2,1,0:T(8,128)S(1)}, f32[12,8,128]{2,1,0:T(8,128)S(1)}, u32[]{:S(2)}, u32[]{:S(2)}) collective-permute-start(f32[12,8,128]{2,1,0:T(8,128)S(1)} %add_add_fusion.1), channel_id=1, source_target_pairs={{0,24},{1,7},{2,26},{3,5},{4,28},{5,3},{6,30},{7,1},{8,16},{9,15},... | collective-permute-start | bytes 147464 | tf_op jit(solution)/shard_map/coefficients/ppermute | solution.py:48
  48.4 5.6 %collective-permute-start.16 = (f32[12,8,128]{2,1,0:T(8,128)S(1)}, f32[12,8,128]{2,1,0:T(8,128)S(1)}, u32[]{:S(2)}, u32[]{:S(2)}) collective-permute-start(f32[12,8,128]{2,1,0:T(8,128)S(1)} %add_add_fusion.1), channel_id=1, source_target_pairs={{0,16},{1,5},{2,18},{3,7},{4,20},{5,1},{6,22},{7,3},{8,24},{9,13},... | collective-permute-start | bytes 147464 | tf_op jit(solution)/shard_map/coefficients/ppermute | solution.py:48
  49.9 4.4 %collective-permute-start.15 = (f32[12,8,128]{2,1,0:T(8,128)S(1)}, f32[12,8,128]{2,1,0:T(8,128)S(1)}, u32[]{:S(2)}, u32[]{:S(2)}) collective-permute-start(f32[12,8,128]{2,1,0:T(8,128)S(1)} %add_add_fusion.1), channel_id=1, source_target_pairs={{0,8},{1,3},{2,10},{3,1},{4,12},{5,7},{6,14},{7,5},{8,0},{9,11},{1... | collective-permute-start | bytes 147464 | tf_op jit(solution)/shard_map/coefficients/ppermute | solution.py:48
  54.3 1.3 %collective-permute-start.18 = (f32[12,8,128]{2,1,0:T(8,128)S(1)}, f32[12,8,128]{2,1,0:T(8,128)S(1)}, u32[]{:S(2)}, u32[]{:S(2)}) collective-permute-start(f32[12,8,128]{2,1,0:T(8,128)S(1)} %add_add_fusion.mine), channel_id=1, source_target_pairs={{0,1},{1,0},{2,3},{3,2},{4,5},{5,4},{6,7},{7,6},{8,9},{9,8},{10,11... | collective-permute-start | bytes 147464 | tf_op jit(solution)/shard_map/coefficients/ppermute | solution.py:21
  56.5 1.2 %collective-permute-start.19 = (f32[24,128]{1,0:T(8,128)S(1)}, f32[24,128]{1,0:T(8,128)S(1)}, u32[]{:S(2)}, u32[]{:S(2)}) collective-permute-start(f32[24,128]{1,0:T(8,128)S(1)} %get-tuple-element.30), channel_id=1, source_target_pairs={{0,1},{1,0},{2,3},{3,2},{4,5},{5,4},{6,7},{7,6},{8,9},{9,8},{10,11... | collective-permute-start | bytes 36872 | tf_op jit(solution)/shard_map/gram/ppermute | solution.py:21
  57.7 4.6 %collective-permute-start.22 = (f32[24,128]{1,0:T(8,128)S(1)}, f32[24,128]{1,0:T(8,128)S(1)}, u32[]{:S(2)}, u32[]{:S(2)}) collective-permute-start(f32[24,128]{1,0:T(8,128)S(1)} %add.53), channel_id=1, source_target_pairs={{0,6},{1,7},{2,4},{3,5},{4,2},{5,3},{6,0},{7,1},{8,14},{9,15},{10,... | collective-permute-start | bytes 36872 | tf_op jit(solution)/shard_map/gram/ppermute | solution.py:21
  60.0 3.7 %collective-permute-start.21 = (f32[24,128]{1,0:T(8,128)S(1)}, f32[24,128]{1,0:T(8,128)S(1)}, u32[]{:S(2)}, u32[]{:S(2)}) collective-permute-start(f32[24,128]{1,0:T(8,128)S(1)} %add.53), channel_id=1, source_target_pairs={{0,4},{1,5},{2,6},{3,7},{4,0},{5,1},{6,2},{7,3},{8,12},{9,13},{10,... | collective-permute-start | bytes 36872 | tf_op jit(solution)/shard_map/gram/ppermute | solution.py:21
  60.3 3.7 %collective-permute-start.20 = (f32[24,128]{1,0:T(8,128)S(1)}, f32[24,128]{1,0:T(8,128)S(1)}, u32[]{:S(2)}, u32[]{:S(2)}) collective-permute-start(f32[24,128]{1,0:T(8,128)S(1)} %add.53), channel_id=1, source_target_pairs={{0,2},{1,3},{2,0},{3,1},{4,6},{5,7},{6,4},{7,5},{8,10},{9,11},{10,... | collective-permute-start | bytes 36872 | tf_op jit(solution)/shard_map/gram/ppermute | solution.py:21
  64.0 6.0 %collective-permute-start.25 = (f32[24,128]{1,0:T(8,128)S(1)}, f32[24,128]{1,0:T(8,128)S(1)}, u32[]{:S(2)}, u32[]{:S(2)}) collective-permute-start(f32[24,128]{1,0:T(8,128)S(1)} %add_add_fusion.3), channel_id=1, source_target_pairs={{0,24},{8,16},{16,8},{24,0},{1,25},{9,17},{17,9},{25,1},{2,26},{10... | collective-permute-start | bytes 36872 | tf_op jit(solution)/shard_map/gram/ppermute | solution.py:21
  65.7 4.6 %collective-permute-start.24 = (f32[24,128]{1,0:T(8,128)S(1)}, f32[24,128]{1,0:T(8,128)S(1)}, u32[]{:S(2)}, u32[]{:S(2)}) collective-permute-start(f32[24,128]{1,0:T(8,128)S(1)} %add_add_fusion.3), channel_id=1, source_target_pairs={{0,16},{8,24},{16,0},{24,8},{1,17},{9,25},{17,1},{25,9},{2,18},{10... | collective-permute-start | bytes 36872 | tf_op jit(solution)/shard_map/gram/ppermute | solution.py:21
  66.3 4.0 %collective-permute-start.23 = (f32[24,128]{1,0:T(8,128)S(1)}, f32[24,128]{1,0:T(8,128)S(1)}, u32[]{:S(2)}, u32[]{:S(2)}) collective-permute-start(f32[24,128]{1,0:T(8,128)S(1)} %add_add_fusion.3), channel_id=1, source_target_pairs={{0,8},{8,0},{16,24},{24,16},{1,9},{9,1},{17,25},{25,17},{2,10},{10... | collective-permute-start | bytes 36872 | tf_op jit(solution)/shard_map/gram/ppermute | solution.py:21

commit v16 on v15

--- a/solution.py
+++ b/solution.py
@@ -315,16 +315,30 @@
     less[...] = recurrence[...] - dot_split(unpack(mine, recurrence.shape[0], basis.shape[0]), basis)
 
 
-def residual_kernel(cells, plan, mine, other, less, mass, current, stored, residual, coef_out, gram):
+def turned(pieces, width, rows):
+    value = unpack(pieces, width, pieces.shape[0] * 8 // width * LANES)
+    spare = jnp.zeros((LANES - width, value.shape[1]), jnp.float32)
+    return jnp.concatenate([value, spare], axis=0).T[:rows, :width]
+
+
+def coefficient_kernel(plan, mine, other, out):
+    rows = out.shape[0] // 2
+    core = core_of(plan)
+    own_half, other_half = turned(mine, out.shape[1], rows), turned(other, out.shape[1], rows)
+    out[:rows] = jnp.where(core == 0, own_half, other_half)
+    out[rows:] = jnp.where(core == 0, other_half, own_half)
+
+
+def store_kernel(value, out, sem):
+    copy = pltpu.make_async_copy(value, out, sem.at[0])
+    copy.start()
+    copy.wait()
+
+
+def residual_kernel(cells, plan, other, less, mass, current, stored, residual, gram):
     width = less.shape[0]
-    core = core_of(plan)
-    basis = half_basis(1 - core, current, stored)
-    own_coef = unpack(mine, width, basis.shape[0])
-    other_coef = unpack(other, width, basis.shape[0])
-    coef_out[...] = jnp.concatenate(
-        [jnp.where(core == 0, own_coef, other_coef), jnp.where(core == 0, other_coef, own_coef)], axis=1
-    )
-    value = less[...] - dot_split(other_coef, basis)
+    basis = half_basis(1 - core_of(plan), current, stored)
+    value = less[...] - dot_split(unpack(other, width, basis.shape[0]), basis)
     residual[...] = value
     local = dot_split(value * (mass[...] * (1.0 / cells)), value, NT)
     half = width // 2
@@ -333,20 +347,20 @@
     gram[:, LANES // 2 : LANES // 2 + width] = local[half:]
 
 
-def after_kernel(value, earlier, out):
+def after_kernel(*refs):
     pass
 
 
-def after(value, earlier):
+def after(value, *earlier):
     anywhere = pl.BlockSpec(memory_space=pl.ANY)
     return pl.pallas_call(
         after_kernel,
         out_shape=jax.ShapeDtypeStruct(value.shape, value.dtype),
-        in_specs=[anywhere, anywhere],
+        in_specs=[anywhere] * (1 + len(earlier)),
         out_specs=anywhere,
         input_output_aliases={0: 0},
         compiler_params=limit(1),
-    )(value, earlier)
+    )(value, *earlier)
 
 
 def in_hbm(value):
@@ -535,23 +549,40 @@
             compiler_params=limit(16),
             cost_estimate=cost(width),
         )(plan, mine, recurrence, current_block, stored)
-        residual_block, coef, gram = pl.pallas_call(
+        residual, gram = pl.pallas_call(
             functools.partial(residual_kernel, cells),
             out_shape=[
                 pltpu.VMEM((width, slab_len), f32),
-                jax.ShapeDtypeStruct((width, basis_rows), f32),
                 jax.ShapeDtypeStruct((width // 2, LANES), f32),
             ],
-            in_specs=smem(1) + vmem(6),
-            out_specs=vmem(3),
+            in_specs=smem(1) + vmem(5),
+            out_specs=vmem(2),
             compiler_params=limit(16),
             cost_estimate=cost(width),
-        )(plan, mine, other, less, mass, current_block, stored)
-        coefficients = coef.T.reshape(stored_count + 1, width, width)
+        )(plan, other, less, mass, current_block, stored)
+        residual_block = pl.pallas_call(
+            store_kernel,
+            out_shape=slab,
+            in_specs=vmem(1),
+            out_specs=anywhere[0],
+            scratch_shapes=[pltpu.SemaphoreType.DMA((1,))],
+            compiler_params=limit(1),
+            cost_estimate=cost(width),
+        )(residual)
+        coef = pl.pallas_call(
+            coefficient_kernel,
+            out_shape=jax.ShapeDtypeStruct((basis_rows, width), f32),
+            in_specs=smem(1) + vmem(2),
+            out_specs=vmem(1)[0],
+            compiler_params=limit(4),
+            cost_estimate=cost(width),
+        )(plan, mine, other)
+        coefficients = coef.reshape(stored_count + 1, width, width)
 
     with jax.named_scope("gram"):
         gram = gram + swap(gram, "col", 1)
-        gram = total(total(gram, "col", 2), "row", 1)
+        gram = after(total(gram, "col", 2), in_hbm(residual_block), in_hbm(coef))
+        gram = total(gram, "row", 1)
         gram = jnp.concatenate(
             [gram[:, :width], gram[:, LANES // 2 : LANES // 2 + width]], axis=0
         )

time: 71.3 us -> 70.9 us (level)
  starting transfers between devices: 30.5 us -> 27.6 us
  Pallas kernels: 13.3 us -> 16.1 us
  local copies, waits for them, and re-layouts: 1.66 us -> 0.1 us
  waiting for transfers between devices: 22.2 us -> 23.4 us
    ppermute x1, starting transfers between devices: 6.12 us -> 4.07 us  [local(): lax.ppermute(parts[0], 'row', [(0, 3), (3, 0)])]
    pallas_call x0 -> x2, Pallas kernels: none -> 1.57 us  [the longest x1 0.82 us: local(): pl.pallas_call(coefficient_kernel, out_shape=jax.ShapeDtypeStruct((basis_...]
    ppermute x1, starting transfers between devices: 2.23 us -> 1.32 us  [local(): first = lax.ppermute(first, 'row', [(0, 1), (3, 2), (1, 3), (2, 0)])]
    transpose x1 -> x0, local copies, waits for them, and re-layouts: 0.82 us -> none  [local(): coefficients = coef.T.reshape(stored_count + 1, width, width)]
    unnamed x13 -> x12, local copies, waits for them, and re-layouts: 0.77 us -> 0.03 us
  transfers between devices with their start and end apart: 26 -> 26, of which waited for: 18 -> 18; matrix products, arithmetic and copies ran while one was open for 2% -> 0% of each run, Pallas kernels for 14% -> 18%
where the time goes in v16:
time: 70.9 us; the launch traced here: 70.5 us
  starting transfers between devices  27.6 us (39%)
  waiting for transfers between devices  23.4 us (33%)
  Pallas kernels  16.1 us (23%)
  other arithmetic  1.8 us (3%)
  between operations  1.51 us (2%)
    ppermute x17, starting transfers between devices, swap(): return lax.ppermute(value, axis, [(i, i ^ mask) for i in range(count)])  13.6 us
    ppermute x17, waiting for transfers between devices, swap(): return lax.ppermute(value, axis, [(i, i ^ mask) for i in range(count)])  11.6 us
    ppermute x6, starting transfers between devices, total_by_core(): values[m] = lax.ppermute(value, ('row', 'col'), trades)  8 us
    ppermute x6, waiting for transfers between devices, total_by_core(): values[m] = lax.ppermute(value, ('row', 'col'), trades)  6.68 us
    pallas_call x1, Pallas kernels, local(): pl.pallas_call(functools.partial(early_kernel, row_devs, col_devs, slab_t...  5.38 us
    ppermute x1, waiting for transfers between devices, local(): lax.ppermute(parts[0], 'row', [(0, 3), (3, 0)])  4.64 us
    ppermute x1, starting transfers between devices, local(): lax.ppermute(parts[0], 'row', [(0, 3), (3, 0)])  4.07 us
    pallas_call x1, Pallas kernels, local(): pl.pallas_call(functools.partial(late_kernel, masks), out_shape=[part, sl...  2.31 us
  transfers between devices with their start and end apart: 26, of which 18 were waited for; matrix products, arithmetic and copies ran while one was open for 0% of the time, Pallas kernels for 18%

profile of v16, /device:TPU:0, one launch (start us, length us, event | category | flops | bytes accessed | tf_op | source)
XLA Modules:
  0.0 70.5 jit_solution(5271472961829755890)
XLA Ops:
  0.6 1.0 %convert_element_type.9.own_panel = bf16[48,2048]{1,0:T(8,128)(2,1)S(1)} convert(f32[48,2048]{1,0:T(8,128)} %current.7) | non-fusion elementwise | flops 98304 | bytes 589824 | tf_op jit(solution)/shard_map/gather/convert_element_type | solution.py:418
  1.7 0.5 collective-permute-start
  2.2 2.6 %collective-permute-start.1 = (bf16[48,2048]{1,0:T(8,128)(2,1)S(1)}, bf16[48,2048]{1,0:T(8,128)(2,1)S(1)}, u32[]{:S(2)}, u32[]{:S(2)}) collective-permute-start(bf16[48,2048]{1,0:T(8,128)(2,1)S(1)} %convert_element_type.9.own_panel), channel_id=1, source_target_pairs={{0,2},{1,3},{2,0},{3,1},{4,6},{5,7},{6,4},{7,5},{8,10},{9,11},{10,... | collective-permute-start | bytes 589832 | tf_op jit(solution)/shard_map/gather/ppermute | solution.py:21
  4.7 1.5 %collective-permute-start.3 = (bf16[48,2048]{1,0:T(8,128)(2,1)S(1)}, bf16[48,2048]{1,0:T(8,128)(2,1)S(1)}, u32[]{:S(2)}, u32[]{:S(2)}) collective-permute-start(bf16[48,2048]{1,0:T(8,128)(2,1)S(1)} %convert_element_type.9.own_panel), channel_id=1, source_target_pairs={{0,4},{1,5},{2,6},{3,7},{4,0},{5,1},{6,2},{7,3},{8,12},{9,13},{10,... | collective-permute-start | bytes 589832 | tf_op jit(solution)/shard_map/gather/ppermute | solution.py:21
  6.3 0.0 collective-permute-start.5
  6.9 0.1 pad_add_fusion.place
  7.0 0.0 collective-permute-done.near_panel
  7.0 5.4 %early.1 = (s32[1,896]{1,0:T(1,128)S(4)}, bf16[512,128,128]{2,1,0:T(8,128)(2,1)S(1)}, f32[65,48,128]{2,1,0:T(8,128)S(1)}, bf16[9,48,2048]{2,1,0:T(8,128)(2,1)S(1)}) custom-call(s32[2]{0:T(128)S(1)} %pad_add_fusion.place, s32[1]{0:T(128)S(6)} %copy.25.counts, s32[1,512]{1,0:T(1,128)} %bitcast.17, s32[1,512]{1,0:T(1,128)} %bitcast.18, ...), custom_call_target="tpu_custom_call" | custom-call | flops 805306368 | bytes 16777216 | tf_op jit(solution)/shard_map/early/pallas_call | solution.py:427
  12.4 0.0 collective-permute-done.1.refs_0_
  12.4 0.1 collective-permute-start.2
  12.5 3.4 %collective-permute-done.3.refs_0_ = bf16[48,2048]{1,0:T(8,128)(2,1)S(1)} collective-permute-done((bf16[48,2048]{1,0:T(8,128)(2,1)S(1)}, bf16[48,2048]{1,0:T(8,128)(2,1)S(1)}, u32[]{:S(2)}, u32[]{:S(2)}) %collective-permute-start.3) | collective-permute-done | bytes 196640 | tf_op jit(solution)/shard_map/gather/ppermute | solution.py:21
  15.9 0.0 collective-permute-start.4
  15.9 0.0 collective-permute-done.5.refs_0_
  15.9 0.5 collective-permute-start.6
  16.4 0.8 %gather.7.refs_5_ = bf16[9,48,2048]{2,1,0:T(8,128)(2,1)S(1)} custom-call(bf16[48,2048]{1,0:T(8,128)(2,1)S(1)} %gather.4.refs_0_, bf16[48,2048]{1,0:T(8,128)(2,1)S(1)} %gather.5.refs_1_, bf16[48,2048]{1,0:T(8,128)(2,1)S(1)} %gather.6.refs_2_, bf16[9,48,2048]{2,1,0:T(8,128)(2,1)S(1)} %get-tuple-element.19.refs_3_), custom_call_target="tpu_custom_call", output_to_operand_aliasing={{}: (3, {})} | custom-call | flops 48 | bytes 1 | tf_op jit(solution)/shard_map/gather/pallas_call | solution.py:462
  17.2 0.2 collective-permute-done.4.refs_1_
  17.4 0.3 collective-permute-done.6.refs_2_
  17.6 1.8 %late.3 = (bf16[48,2048]{1,0:T(8,128)(2,1)S(1)}, bf16[9,48,2048]{2,1,0:T(8,128)(2,1)S(1)}) custom-call(s32[1,896]{1,0:T(1,128)S(4)} %get-tuple-element.16.plan, bf16[48,2048]{1,0:T(8,128)(2,1)S(1)} %collective-permute-done.2.refs_0_, bf16[48,2048]{1,0:T(8,128)(2,1)S(1)} %collective-permute-done.4.refs_1_, ...), custom_call_target="tpu_custom_call", output_to_operand_aliasing={{1}: (6, {})} | custom-call | flops 48 | bytes 1 | tf_op jit(solution)/shard_map/late/pallas_call | solution.py:478
  19.4 1.3 %collective-permute-start.7 = (bf16[48,2048]{1,0:T(8,128)(2,1)S(1)}, bf16[48,2048]{1,0:T(8,128)(2,1)S(1)}, u32[]{:S(2)}, u32[]{:S(2)}) collective-permute-start(bf16[48,2048]{1,0:T(8,128)(2,1)S(1)} %get-tuple-element.21), channel_id=1, source_target_pairs={{0,8},{24,16},{8,24},{16,0},{1,9},{25,17},{9,25},{17,1},{2,10},{26... | collective-permute-start | bytes 589832 | tf_op jit(solution)/shard_map/late/ppermute | solution.py:498
  20.7 2.3 %late.5 = (bf16[48,2048]{1,0:T(8,128)(2,1)S(1)}, f32[48,2048]{1,0:T(8,128)S(1)}, bf16[48,2048]{1,0:T(8,128)(2,1)S(1)}) custom-call(s32[1,896]{1,0:T(1,128)S(4)} %get-tuple-element.16.plan, bf16[9,48,2048]{2,1,0:T(8,128)(2,1)S(1)} %get-tuple-element.20.panel_buf, bf16[512,128,128]{2,1,0:T(8,128)(2,1)S(1)} %get-tuple-element.18.refs_3_.tiles, ...), custom_call_target="tpu_custom_call" | custom-call | flops 48 | bytes 1 | tf_op jit(solution)/shard_map/late/pallas_call | solution.py:488
  23.1 4.1 %collective-permute-start.8 = (bf16[48,2048]{1,0:T(8,128)(2,1)S(1)}, bf16[48,2048]{1,0:T(8,128)(2,1)S(1)}, u32[]{:S(2)}, u32[]{:S(2)}) collective-permute-start(bf16[48,2048]{1,0:T(8,128)(2,1)S(1)} %get-tuple-element.22), channel_id=1, source_target_pairs={{0,24},{24,0},{1,25},{25,1},{2,26},{26,2},{3,27},{27,3},{4,28},{28... | collective-permute-start | bytes 589832 | tf_op jit(solution)/shard_map/late/ppermute | solution.py:502
  27.1 0.2 collective-permute-start.10
  27.3 0.4 collective-permute-done.7.refs_0_
  27.7 0.7 collective-permute-start.9
  28.5 0.0 copy-start
  28.5 0.0 copy-start.3
  28.5 1.4 %late.4.base = f32[48,2048]{1,0:T(8,128)S(1)} custom-call(s32[1,896]{1,0:T(1,128)S(4)} %get-tuple-element.16.plan, bf16[9,48,2048]{2,1,0:T(8,128)(2,1)S(1)} %get-tuple-element.20.panel_buf, bf16[512,128,128]{2,1,0:T(8,128)(2,1)S(1)} %get-tuple-element.18.refs_3_.tiles, f32[65,48,128]{2,1,0:T(8,128)S(1)} %get-tuple-element.17.refs_1_.refs_4_.early, ...), custom_call_target="tpu_custom_call" | custom-call | flops 48 | bytes 1 | tf_op jit(solution)/shard_map/late/pallas_call | solution.py:509
  29.9 4.6 %collective-permute-done.8.refs_1_ = bf16[48,2048]{1,0:T(8,128)(2,1)S(1)} collective-permute-done((bf16[48,2048]{1,0:T(8,128)(2,1)S(1)}, bf16[48,2048]{1,0:T(8,128)(2,1)S(1)}, u32[]{:S(2)}, u32[]{:S(2)}) %collective-permute-start.8) | collective-permute-done | bytes 196640 | tf_op jit(solution)/shard_map/late/ppermute | solution.py:502
  34.6 2.8 %collective-permute-done.10.refs_3_ = bf16[48,2048]{1,0:T(8,128)(2,1)S(1)} collective-permute-done((bf16[48,2048]{1,0:T(8,128)(2,1)S(1)}, bf16[48,2048]{1,0:T(8,128)(2,1)S(1)}, u32[]{:S(2)}, u32[]{:S(2)}) %collective-permute-start.10) | collective-permute-done | bytes 196640 | tf_op jit(solution)/shard_map/late/ppermute | solution.py:21
  37.4 0.7 coefficients.2
  38.1 0.1 collective-permute-start.11
  38.2 0.7 coefficients.3
  38.9 0.5 collective-permute-done.11
  39.4 1.9 %collective-permute-start.14 = (f32[12,8,128]{2,1,0:T(8,128)S(1)}, f32[12,8,128]{2,1,0:T(8,128)S(1)}, u32[]{:S(2)}, u32[]{:S(2)}) collective-permute-start(f32[12,8,128]{2,1,0:T(8,128)S(1)} %add.46), channel_id=1, source_target_pairs={{0,6},{1,25},{2,4},{3,27},{4,2},{5,29},{6,0},{7,31},{8,14},{9,17},... | collective-permute-start | bytes 147464 | tf_op jit(solution)/shard_map/coefficients/ppermute | solution.py:48
  41.3 0.9 %collective-permute-start.13 = (f32[12,8,128]{2,1,0:T(8,128)S(1)}, f32[12,8,128]{2,1,0:T(8,128)S(1)}, u32[]{:S(2)}, u32[]{:S(2)}) collective-permute-start(f32[12,8,128]{2,1,0:T(8,128)S(1)} %add.46), channel_id=1, source_target_pairs={{0,4},{1,17},{2,6},{3,19},{4,0},{5,21},{6,2},{7,23},{8,12},{9,25},... | collective-permute-start | bytes 147464 | tf_op jit(solution)/shard_map/coefficients/ppermute | solution.py:48
  42.2 0.8 %collective-permute-start.12 = (f32[12,8,128]{2,1,0:T(8,128)S(1)}, f32[12,8,128]{2,1,0:T(8,128)S(1)}, u32[]{:S(2)}, u32[]{:S(2)}) collective-permute-start(f32[12,8,128]{2,1,0:T(8,128)S(1)} %add.46), channel_id=1, source_target_pairs={{0,2},{1,9},{2,0},{3,11},{4,6},{5,13},{6,4},{7,15},{8,10},{9,1},{1... | collective-permute-start | bytes 147464 | tf_op jit(solution)/shard_map/coefficients/ppermute | solution.py:48
  43.0 1.5 %collective-permute-done.14 = f32[12,8,128]{2,1,0:T(8,128)S(1)} collective-permute-done((f32[12,8,128]{2,1,0:T(8,128)S(1)}, f32[12,8,128]{2,1,0:T(8,128)S(1)}, u32[]{:S(2)}, u32[]{:S(2)}) %collective-permute-start.14) | collective-permute-done | bytes 49184 | tf_op jit(solution)/shard_map/coefficients/ppermute | solution.py:48
  44.5 0.9 %collective-permute-done.13 = f32[12,8,128]{2,1,0:T(8,128)S(1)} collective-permute-done((f32[12,8,128]{2,1,0:T(8,128)S(1)}, f32[12,8,128]{2,1,0:T(8,128)S(1)}, u32[]{:S(2)}, u32[]{:S(2)}) %collective-permute-start.13) | collective-permute-done | bytes 49184 | tf_op jit(solution)/shard_map/coefficients/ppermute | solution.py:48
  45.4 0.9 %collective-permute-done.12 = f32[12,8,128]{2,1,0:T(8,128)S(1)} collective-permute-done((f32[12,8,128]{2,1,0:T(8,128)S(1)}, f32[12,8,128]{2,1,0:T(8,128)S(1)}, u32[]{:S(2)}, u32[]{:S(2)}) %collective-permute-start.12) | collective-permute-done | bytes 49184 | tf_op jit(solution)/shard_map/coefficients/ppermute | solution.py:48
  46.3 2.3 %collective-permute-start.17 = (f32[12,8,128]{2,1,0:T(8,128)S(1)}, f32[12,8,128]{2,1,0:T(8,128)S(1)}, u32[]{:S(2)}, u32[]{:S(2)}) collective-permute-start(f32[12,8,128]{2,1,0:T(8,128)S(1)} %add_add_fusion.1), channel_id=1, source_target_pairs={{0,24},{1,7},{2,26},{3,5},{4,28},{5,3},{6,30},{7,1},{8,16},{9,15},... | collective-permute-start | bytes 147464 | tf_op jit(solution)/shard_map/coefficients/ppermute | solution.py:48
  48.6 1.0 %collective-permute-start.16 = (f32[12,8,128]{2,1,0:T(8,128)S(1)}, f32[12,8,128]{2,1,0:T(8,128)S(1)}, u32[]{:S(2)}, u32[]{:S(2)}) collective-permute-start(f32[12,8,128]{2,1,0:T(8,128)S(1)} %add_add_fusion.1), channel_id=1, source_target_pairs={{0,16},{1,5},{2,18},{3,7},{4,20},{5,1},{6,22},{7,3},{8,24},{9,13},... | collective-permute-start | bytes 147464 | tf_op jit(solution)/shard_map/coefficients/ppermute | solution.py:48
  49.6 1.1 %collective-permute-start.15 = (f32[12,8,128]{2,1,0:T(8,128)S(1)}, f32[12,8,128]{2,1,0:T(8,128)S(1)}, u32[]{:S(2)}, u32[]{:S(2)}) collective-permute-start(f32[12,8,128]{2,1,0:T(8,128)S(1)} %add_add_fusion.1), channel_id=1, source_target_pairs={{0,8},{1,3},{2,10},{3,1},{4,12},{5,7},{6,14},{7,5},{8,0},{9,11},{1... | collective-permute-start | bytes 147464 | tf_op jit(solution)/shard_map/coefficients/ppermute | solution.py:48
  50.7 1.5 %collective-permute-done.17 = f32[12,8,128]{2,1,0:T(8,128)S(1)} collective-permute-done((f32[12,8,128]{2,1,0:T(8,128)S(1)}, f32[12,8,128]{2,1,0:T(8,128)S(1)}, u32[]{:S(2)}, u32[]{:S(2)}) %collective-permute-start.17) | collective-permute-done | bytes 49184 | tf_op jit(solution)/shard_map/coefficients/ppermute | solution.py:48
  52.2 1.9 %collective-permute-done.16 = f32[12,8,128]{2,1,0:T(8,128)S(1)} collective-permute-done((f32[12,8,128]{2,1,0:T(8,128)S(1)}, f32[12,8,128]{2,1,0:T(8,128)S(1)}, u32[]{:S(2)}, u32[]{:S(2)}) %collective-permute-start.16) | collective-permute-done | bytes 49184 | tf_op jit(solution)/shard_map/coefficients/ppermute | solution.py:48
  54.2 0.1 collective-permute-start.18
  54.2 0.6 residual.4.less
  54.8 0.6 collective-permute-done.18.other
  55.4 0.9 %residual.5 = (f32[48,2048]{1,0:T(8,128)S(1)}, f32[24,128]{1,0:T(8,128)S(1)}) custom-call(s32[1,896]{1,0:T(1,128)S(4)} %get-tuple-element.16.plan, f32[12,8,128]{2,1,0:T(8,128)S(1)} %collective-permute-done.18.other, f32[48,2048]{1,0:T(8,128)S(1)} %residual.4.less, f32[1,2048]{1,0:T(1,128)S(1)} %bitcast.14, f32[48,2048]{1,0:T(8,128)S(1)} %copy-done.1, ...), custom_call_target="tpu_custom_call" | custom-call | flops 48 | bytes 1 | tf_op jit(solution)/shard_map/residual/pallas_call | solution.py:552
  56.4 0.2 collective-permute-start.19
  56.6 1.0 %collective-permute-done.19 = f32[24,128]{1,0:T(8,128)S(1)} collective-permute-done((f32[24,128]{1,0:T(8,128)S(1)}, f32[24,128]{1,0:T(8,128)S(1)}, u32[]{:S(2)}, u32[]{:S(2)}) %collective-permute-start.19) | collective-permute-done | bytes 12320 | tf_op jit(solution)/shard_map/gram/ppermute | solution.py:21
  57.6 1.5 %collective-permute-start.22 = (f32[24,128]{1,0:T(8,128)S(1)}, f32[24,128]{1,0:T(8,128)S(1)}, u32[]{:S(2)}, u32[]{:S(2)}) collective-permute-start(f32[24,128]{1,0:T(8,128)S(1)} %add.53), channel_id=1, source_target_pairs={{0,6},{1,7},{2,4},{3,5},{4,2},{5,3},{6,0},{7,1},{8,14},{9,15},{10,... | collective-permute-start | bytes 36872 | tf_op jit(solution)/shard_map/gram/ppermute | solution.py:21
  59.1 0.4 collective-permute-start.21
  59.5 1.6 %collective-permute-start.20 = (f32[24,128]{1,0:T(8,128)S(1)}, f32[24,128]{1,0:T(8,128)S(1)}, u32[]{:S(2)}, u32[]{:S(2)}) collective-permute-start(f32[24,128]{1,0:T(8,128)S(1)} %add.53), channel_id=1, source_target_pairs={{0,2},{1,3},{2,0},{3,1},{4,6},{5,7},{6,4},{7,5},{8,10},{9,11},{10,... | collective-permute-start | bytes 36872 | tf_op jit(solution)/shard_map/gram/ppermute | solution.py:21
  61.1 0.8 %residual.6.refs_1_ = f32[48,2048]{1,0:T(8,128)} custom-call(f32[48,2048]{1,0:T(8,128)S(1)} %get-tuple-element.27.value), custom_call_target="tpu_custom_call" | custom-call | flops 48 | bytes 1 | tf_op jit(solution)/shard_map/residual/pallas_call | solution.py:563
  61.8 0.8 %residual.7.refs_2_ = f32[432,48]{1,0:T(8,128)} custom-call(s32[1,896]{1,0:T(1,128)S(4)} %get-tuple-element.16.plan, f32[12,8,128]{2,1,0:T(8,128)S(1)} %add_add_fusion.mine, f32[12,8,128]{2,1,0:T(8,128)S(1)} %collective-permute-done.18.other), custom_call_target="tpu_custom_call" | custom-call | flops 48 | bytes 1 | tf_op jit(solution)/shard_map/residual/pallas_call | solution.py:572
  62.7 0.1 collective-permute-done.21
  62.8 0.4 collective-permute-done.20
  63.2 2.0 %collective-permute-start.25 = (f32[24,128]{1,0:T(8,128)S(1)}, f32[24,128]{1,0:T(8,128)S(1)}, u32[]{:S(2)}, u32[]{:S(2)}) collective-permute-start(f32[24,128]{1,0:T(8,128)S(1)} %gram.1), channel_id=1, source_target_pairs={{0,24},{8,16},{16,8},{24,0},{1,25},{9,17},{17,9},{25,1},{2,26},{10... | collective-permute-start | bytes 36872 | tf_op jit(solution)/shard_map/gram/ppermute | solution.py:21
  65.2 0.5 collective-permute-start.24
  65.7 1.9 %collective-permute-start.23 = (f32[24,128]{1,0:T(8,128)S(1)}, f32[24,128]{1,0:T(8,128)S(1)}, u32[]{:S(2)}, u32[]{:S(2)}) collective-permute-start(f32[24,128]{1,0:T(8,128)S(1)} %gram.1), channel_id=1, source_target_pairs={{0,8},{8,0},{16,24},{24,16},{1,9},{9,1},{17,25},{25,17},{2,10},{10... | collective-permute-start | bytes 36872 | tf_op jit(solution)/shard_map/gram/ppermute | solution.py:21
  67.6 1.1 %collective-permute-done.25 = f32[24,128]{1,0:T(8,128)S(1)} collective-permute-done((f32[24,128]{1,0:T(8,128)S(1)}, f32[24,128]{1,0:T(8,128)S(1)}, u32[]{:S(2)}, u32[]{:S(2)}) %collective-permute-start.25) | collective-permute-done | bytes 12320 | tf_op jit(solution)/shard_map/gram/ppermute | solution.py:21
  68.7 1.1 %collective-permute-done.24 = f32[24,128]{1,0:T(8,128)S(1)} collective-permute-done((f32[24,128]{1,0:T(8,128)S(1)}, f32[24,128]{1,0:T(8,128)S(1)}, u32[]{:S(2)}, u32[]{:S(2)}) %collective-permute-start.24) | collective-permute-done | bytes 12320 | tf_op jit(solution)/shard_map/gram/ppermute | solution.py:21
  69.8 0.1 fusion
  69.9 0.6 pad_maximum_fusion
  (26 shorter events, 0.1 us)
Async XLA Ops:
  1.7 5.4 %collective-permute-start = (bf16[48,2048]{1,0:T(8,128)(2,1)S(1)}, bf16[48,2048]{1,0:T(8,128)(2,1)S(1)}, u32[]{:S(2)}, u32[]{:S(2)}) collective-permute-start(bf16[48,2048]{1,0:T(8,128)(2,1)S(1)} %convert_element_type.9.own_panel), channel_id=1, source_target_pairs={{0,1},{1,0},{2,3},{3,2},{4,5},{5,4},{6,7},{7,6},{8,9},{9,8},{10,11... | collective-permute-start | bytes 589832 | tf_op jit(solution)/shard_map/gather/ppermute | solution.py:21
  2.2 10.2 %collective-permute-start.1 = (bf16[48,2048]{1,0:T(8,128)(2,1)S(1)}, bf16[48,2048]{1,0:T(8,128)(2,1)S(1)}, u32[]{:S(2)}, u32[]{:S(2)}) collective-permute-start(bf16[48,2048]{1,0:T(8,128)(2,1)S(1)} %convert_element_type.9.own_panel), channel_id=1, source_target_pairs={{0,2},{1,3},{2,0},{3,1},{4,6},{5,7},{6,4},{7,5},{8,10},{9,11},{10,... | collective-permute-start | bytes 589832 | tf_op jit(solution)/shard_map/gather/ppermute | solution.py:21
  4.7 11.2 %collective-permute-start.3 = (bf16[48,2048]{1,0:T(8,128)(2,1)S(1)}, bf16[48,2048]{1,0:T(8,128)(2,1)S(1)}, u32[]{:S(2)}, u32[]{:S(2)}) collective-permute-start(bf16[48,2048]{1,0:T(8,128)(2,1)S(1)} %convert_element_type.9.own_panel), channel_id=1, source_target_pairs={{0,4},{1,5},{2,6},{3,7},{4,0},{5,1},{6,2},{7,3},{8,12},{9,13},{10,... | collective-permute-start | bytes 589832 | tf_op jit(solution)/shard_map/gather/ppermute | solution.py:21
  6.3 9.7 %collective-permute-start.5 = (bf16[48,2048]{1,0:T(8,128)(2,1)S(1)}, bf16[48,2048]{1,0:T(8,128)(2,1)S(1)}, u32[]{:S(2)}, u32[]{:S(2)}) collective-permute-start(bf16[48,2048]{1,0:T(8,128)(2,1)S(1)} %convert_element_type.9.own_panel), channel_id=1, source_target_pairs={{0,6},{1,7},{2,4},{3,5},{4,2},{5,3},{6,0},{7,1},{8,14},{9,15},{10,... | collective-permute-start | bytes 589832 | tf_op jit(solution)/shard_map/gather/ppermute | solution.py:21
  12.4 4.8 %collective-permute-start.2 = (bf16[48,2048]{1,0:T(8,128)(2,1)S(1)}, bf16[48,2048]{1,0:T(8,128)(2,1)S(1)}, u32[]{:S(2)}, u32[]{:S(2)}) collective-permute-start(bf16[48,2048]{1,0:T(8,128)(2,1)S(1)} %gather.4.refs_0_), channel_id=1, source_target_pairs={{0,1},{1,0},{2,3},{3,2},{4,5},{5,4},{6,7},{7,6},{8,9},{9,8},{10,11... | collective-permute-start | bytes 589832 | tf_op jit(solution)/shard_map/gather/ppermute | solution.py:21
  15.9 1.4 %collective-permute-start.4 = (bf16[48,2048]{1,0:T(8,128)(2,1)S(1)}, bf16[48,2048]{1,0:T(8,128)(2,1)S(1)}, u32[]{:S(2)}, u32[]{:S(2)}) collective-permute-start(bf16[48,2048]{1,0:T(8,128)(2,1)S(1)} %gather.5.refs_1_), channel_id=1, source_target_pairs={{0,1},{1,0},{2,3},{3,2},{4,5},{5,4},{6,7},{7,6},{8,9},{9,8},{10,11... | collective-permute-start | bytes 589832 | tf_op jit(solution)/shard_map/gather/ppermute | solution.py:21
  15.9 1.7 %collective-permute-start.6 = (bf16[48,2048]{1,0:T(8,128)(2,1)S(1)}, bf16[48,2048]{1,0:T(8,128)(2,1)S(1)}, u32[]{:S(2)}, u32[]{:S(2)}) collective-permute-start(bf16[48,2048]{1,0:T(8,128)(2,1)S(1)} %gather.6.refs_2_), channel_id=1, source_target_pairs={{0,1},{1,0},{2,3},{3,2},{4,5},{5,4},{6,7},{7,6},{8,9},{9,8},{10,11... | collective-permute-start | bytes 589832 | tf_op jit(solution)/shard_map/gather/ppermute | solution.py:21
  19.4 8.3 %collective-permute-start.7 = (bf16[48,2048]{1,0:T(8,128)(2,1)S(1)}, bf16[48,2048]{1,0:T(8,128)(2,1)S(1)}, u32[]{:S(2)}, u32[]{:S(2)}) collective-permute-start(bf16[48,2048]{1,0:T(8,128)(2,1)S(1)} %get-tuple-element.21), channel_id=1, source_target_pairs={{0,8},{24,16},{8,24},{16,0},{1,9},{25,17},{9,25},{17,1},{2,10},{26... | collective-permute-start | bytes 589832 | tf_op jit(solution)/shard_map/late/ppermute | solution.py:498
  20.7 7.7 %copy-start.1 = (f32[48,2048]{1,0:T(8,128)S(1)}, f32[48,2048]{1,0:T(8,128)}, u32[]{:S(2)}) copy-start(f32[48,2048]{1,0:T(8,128)} %current.7) | copy-start | bytes 1179652
  20.7 7.7 %copy-start.2 = (f32[48,2048]{1,0:T(8,128)S(1)}, f32[48,2048]{1,0:T(8,128)}, u32[]{:S(2)}) copy-start(f32[48,2048]{1,0:T(8,128)} %previous.1) | copy-start | bytes 1179652
  20.7 7.7 %copy-start.4 = (f32[48,48]{1,0:T(8,128)S(1)}, f32[48,48]{1,0:T(8,128)}, u32[]{:S(2)}) copy-start(f32[48,48]{1,0:T(8,128)} %coupling.1) | copy-start | bytes 27652
  20.7 7.7 %copy-start.5 = (f32[2048]{0:T(1024)S(1)}, f32[2048]{0:T(1024)}, u32[]{:S(2)}) copy-start(f32[2048]{0:T(1024)} %param.14) | copy-start | bytes 24580
  23.1 11.5 %collective-permute-start.8 = (bf16[48,2048]{1,0:T(8,128)(2,1)S(1)}, bf16[48,2048]{1,0:T(8,128)(2,1)S(1)}, u32[]{:S(2)}, u32[]{:S(2)}) collective-permute-start(bf16[48,2048]{1,0:T(8,128)(2,1)S(1)} %get-tuple-element.22), channel_id=1, source_target_pairs={{0,24},{24,0},{1,25},{25,1},{2,26},{26,2},{3,27},{27,3},{4,28},{28... | collective-permute-start | bytes 589832 | tf_op jit(solution)/shard_map/late/ppermute | solution.py:502
  27.1 10.3 %collective-permute-start.10 = (bf16[48,2048]{1,0:T(8,128)(2,1)S(1)}, bf16[48,2048]{1,0:T(8,128)(2,1)S(1)}, u32[]{:S(2)}, u32[]{:S(2)}) collective-permute-start(bf16[48,2048]{1,0:T(8,128)(2,1)S(1)} %get-tuple-element.24), channel_id=1, source_target_pairs={{0,8},{8,0},{16,24},{24,16},{1,9},{9,1},{17,25},{25,17},{2,10},{10... | collective-permute-start | bytes 589832 | tf_op jit(solution)/shard_map/late/ppermute | solution.py:21
  27.7 9.7 %collective-permute-start.9 = (bf16[48,2048]{1,0:T(8,128)(2,1)S(1)}, bf16[48,2048]{1,0:T(8,128)(2,1)S(1)}, u32[]{:S(2)}, u32[]{:S(2)}) collective-permute-start(bf16[48,2048]{1,0:T(8,128)(2,1)S(1)} %add_convert_fusion), channel_id=1, source_target_pairs={{8,16},{16,8},{9,17},{17,9},{10,18},{18,10},{11,19},{19,11},{12,20... | collective-permute-start | bytes 589832 | tf_op jit(solution)/shard_map/late/ppermute | solution.py:503
  28.5 8.9 %copy-start = (f32[8,48,2048]{2,1,0:T(8,128)S(1)}, f32[8,48,2048]{2,1,0:T(8,128)}, u32[]{:S(2)}) copy-start(f32[8,48,2048]{2,1,0:T(8,128)} %param.13) | copy-start | bytes 9437188
  28.5 8.9 %copy-start.3 = (f32[2048]{0:T(1024)S(1)}, f32[2048]{0:T(1024)}, u32[]{:S(2)}) copy-start(f32[2048]{0:T(1024)} %param.15) | copy-start | bytes 24580
  38.1 1.3 %collective-permute-start.11 = (f32[12,8,128]{2,1,0:T(8,128)S(1)}, f32[12,8,128]{2,1,0:T(8,128)S(1)}, u32[]{:S(2)}, u32[]{:S(2)}) collective-permute-start(f32[12,8,128]{2,1,0:T(8,128)S(1)} %get-tuple-element.26), channel_id=1, source_target_pairs={{0,1},{1,0},{2,3},{3,2},{4,5},{5,4},{6,7},{7,6},{8,9},{9,8},{10,11... | collective-permute-start | bytes 147464 | tf_op jit(solution)/shard_map/coefficients/ppermute | solution.py:21
  39.4 5.0 %collective-permute-start.14 = (f32[12,8,128]{2,1,0:T(8,128)S(1)}, f32[12,8,128]{2,1,0:T(8,128)S(1)}, u32[]{:S(2)}, u32[]{:S(2)}) collective-permute-start(f32[12,8,128]{2,1,0:T(8,128)S(1)} %add.46), channel_id=1, source_target_pairs={{0,6},{1,25},{2,4},{3,27},{4,2},{5,29},{6,0},{7,31},{8,14},{9,17},... | collective-permute-start | bytes 147464 | tf_op jit(solution)/shard_map/coefficients/ppermute | solution.py:48
  41.3 4.1 %collective-permute-start.13 = (f32[12,8,128]{2,1,0:T(8,128)S(1)}, f32[12,8,128]{2,1,0:T(8,128)S(1)}, u32[]{:S(2)}, u32[]{:S(2)}) collective-permute-start(f32[12,8,128]{2,1,0:T(8,128)S(1)} %add.46), channel_id=1, source_target_pairs={{0,4},{1,17},{2,6},{3,19},{4,0},{5,21},{6,2},{7,23},{8,12},{9,25},... | collective-permute-start | bytes 147464 | tf_op jit(solution)/shard_map/coefficients/ppermute | solution.py:48
  42.2 4.1 %collective-permute-start.12 = (f32[12,8,128]{2,1,0:T(8,128)S(1)}, f32[12,8,128]{2,1,0:T(8,128)S(1)}, u32[]{:S(2)}, u32[]{:S(2)}) collective-permute-start(f32[12,8,128]{2,1,0:T(8,128)S(1)} %add.46), channel_id=1, source_target_pairs={{0,2},{1,9},{2,0},{3,11},{4,6},{5,13},{6,4},{7,15},{8,10},{9,1},{1... | collective-permute-start | bytes 147464 | tf_op jit(solution)/shard_map/coefficients/ppermute | solution.py:48
  46.3 6.0 %collective-permute-start.17 = (f32[12,8,128]{2,1,0:T(8,128)S(1)}, f32[12,8,128]{2,1,0:T(8,128)S(1)}, u32[]{:S(2)}, u32[]{:S(2)}) collective-permute-start(f32[12,8,128]{2,1,0:T(8,128)S(1)} %add_add_fusion.1), channel_id=1, source_target_pairs={{0,24},{1,7},{2,26},{3,5},{4,28},{5,3},{6,30},{7,1},{8,16},{9,15},... | collective-permute-start | bytes 147464 | tf_op jit(solution)/shard_map/coefficients/ppermute | solution.py:48
  48.6 5.5 %collective-permute-start.16 = (f32[12,8,128]{2,1,0:T(8,128)S(1)}, f32[12,8,128]{2,1,0:T(8,128)S(1)}, u32[]{:S(2)}, u32[]{:S(2)}) collective-permute-start(f32[12,8,128]{2,1,0:T(8,128)S(1)} %add_add_fusion.1), channel_id=1, source_target_pairs={{0,16},{1,5},{2,18},{3,7},{4,20},{5,1},{6,22},{7,3},{8,24},{9,13},... | collective-permute-start | bytes 147464 | tf_op jit(solution)/shard_map/coefficients/ppermute | solution.py:48
  49.6 4.5 %collective-permute-start.15 = (f32[12,8,128]{2,1,0:T(8,128)S(1)}, f32[12,8,128]{2,1,0:T(8,128)S(1)}, u32[]{:S(2)}, u32[]{:S(2)}) collective-permute-start(f32[12,8,128]{2,1,0:T(8,128)S(1)} %add_add_fusion.1), channel_id=1, source_target_pairs={{0,8},{1,3},{2,10},{3,1},{4,12},{5,7},{6,14},{7,5},{8,0},{9,11},{1... | collective-permute-start | bytes 147464 | tf_op jit(solution)/shard_map/coefficients/ppermute | solution.py:48
  54.2 1.3 %collective-permute-start.18 = (f32[12,8,128]{2,1,0:T(8,128)S(1)}, f32[12,8,128]{2,1,0:T(8,128)S(1)}, u32[]{:S(2)}, u32[]{:S(2)}) collective-permute-start(f32[12,8,128]{2,1,0:T(8,128)S(1)} %add_add_fusion.mine), channel_id=1, source_target_pairs={{0,1},{1,0},{2,3},{3,2},{4,5},{5,4},{6,7},{7,6},{8,9},{9,8},{10,11... | collective-permute-start | bytes 147464 | tf_op jit(solution)/shard_map/coefficients/ppermute | solution.py:21
  56.4 1.2 %collective-permute-start.19 = (f32[24,128]{1,0:T(8,128)S(1)}, f32[24,128]{1,0:T(8,128)S(1)}, u32[]{:S(2)}, u32[]{:S(2)}) collective-permute-start(f32[24,128]{1,0:T(8,128)S(1)} %get-tuple-element.28), channel_id=1, source_target_pairs={{0,1},{1,0},{2,3},{3,2},{4,5},{5,4},{6,7},{7,6},{8,9},{9,8},{10,11... | collective-permute-start | bytes 36872 | tf_op jit(solution)/shard_map/gram/ppermute | solution.py:21
  57.6 5.1 %collective-permute-start.22 = (f32[24,128]{1,0:T(8,128)S(1)}, f32[24,128]{1,0:T(8,128)S(1)}, u32[]{:S(2)}, u32[]{:S(2)}) collective-permute-start(f32[24,128]{1,0:T(8,128)S(1)} %add.53), channel_id=1, source_target_pairs={{0,6},{1,7},{2,4},{3,5},{4,2},{5,3},{6,0},{7,1},{8,14},{9,15},{10,... | collective-permute-start | bytes 36872 | tf_op jit(solution)/shard_map/gram/ppermute | solution.py:21
  59.1 3.7 %collective-permute-start.21 = (f32[24,128]{1,0:T(8,128)S(1)}, f32[24,128]{1,0:T(8,128)S(1)}, u32[]{:S(2)}, u32[]{:S(2)}) collective-permute-start(f32[24,128]{1,0:T(8,128)S(1)} %add.53), channel_id=1, source_target_pairs={{0,4},{1,5},{2,6},{3,7},{4,0},{5,1},{6,2},{7,3},{8,12},{9,13},{10,... | collective-permute-start | bytes 36872 | tf_op jit(solution)/shard_map/gram/ppermute | solution.py:21
  59.5 3.7 %collective-permute-start.20 = (f32[24,128]{1,0:T(8,128)S(1)}, f32[24,128]{1,0:T(8,128)S(1)}, u32[]{:S(2)}, u32[]{:S(2)}) collective-permute-start(f32[24,128]{1,0:T(8,128)S(1)} %add.53), channel_id=1, source_target_pairs={{0,2},{1,3},{2,0},{3,1},{4,6},{5,7},{6,4},{7,5},{8,10},{9,11},{10,... | collective-permute-start | bytes 36872 | tf_op jit(solution)/shard_map/gram/ppermute | solution.py:21
  63.2 5.5 %collective-permute-start.25 = (f32[24,128]{1,0:T(8,128)S(1)}, f32[24,128]{1,0:T(8,128)S(1)}, u32[]{:S(2)}, u32[]{:S(2)}) collective-permute-start(f32[24,128]{1,0:T(8,128)S(1)} %gram.1), channel_id=1, source_target_pairs={{0,24},{8,16},{16,8},{24,0},{1,25},{9,17},{17,9},{25,1},{2,26},{10... | collective-permute-start | bytes 36872 | tf_op jit(solution)/shard_map/gram/ppermute | solution.py:21
  65.2 4.6 %collective-permute-start.24 = (f32[24,128]{1,0:T(8,128)S(1)}, f32[24,128]{1,0:T(8,128)S(1)}, u32[]{:S(2)}, u32[]{:S(2)}) collective-permute-start(f32[24,128]{1,0:T(8,128)S(1)} %gram.1), channel_id=1, source_target_pairs={{0,16},{8,24},{16,0},{24,8},{1,17},{9,25},{17,1},{25,9},{2,18},{10... | collective-permute-start | bytes 36872 | tf_op jit(solution)/shard_map/gram/ppermute | solution.py:21
  65.7 4.1 %collective-permute-start.23 = (f32[24,128]{1,0:T(8,128)S(1)}, f32[24,128]{1,0:T(8,128)S(1)}, u32[]{:S(2)}, u32[]{:S(2)}) collective-permute-start(f32[24,128]{1,0:T(8,128)S(1)} %gram.1), channel_id=1, source_target_pairs={{0,8},{8,0},{16,24},{24,16},{1,9},{9,1},{17,25},{25,17},{2,10},{10... | collective-permute-start | bytes 36872 | tf_op jit(solution)/shard_map/gram/ppermute | solution.py:21

commit v17 on v16

--- a/solution.py
+++ b/solution.py
@@ -33,6 +33,29 @@
     for m in range(lax.axis_size(axis) - step, 0, -step):
         values[m] = swap(value, axis, m)
     return tree_sum(values)
+
+
+def total_shared(value, axis, *earlier):
+    row_devs, col_devs = lax.axis_size("row"), lax.axis_size("col")
+    step = 2 if axis == "col" else 1
+    if lax.axis_size(axis) != 4 * step:
+        return after(total(value, axis, step), *earlier)
+
+    def trade(masks):
+        pairs = []
+        for r in range(row_devs):
+            for c in range(col_devs):
+                m = step * masks[c % 2]
+                there = (r, c ^ m) if axis == "col" else (r ^ m, c)
+                if m:
+                    pairs.append((r * col_devs + c, there[0] * col_devs + there[1]))
+        return lax.ppermute(value, ("row", "col"), pairs)
+
+    far, near = trade((1, 3)), trade((0, 2))
+    part = jnp.where(lax.axis_index("col") & 1 == 0, value, near) + far
+    if earlier:
+        part = after(part, *earlier)
+    return part + swap(part, "col", 1)
 
 
 def total_by_core(value):
@@ -581,8 +604,8 @@
 
     with jax.named_scope("gram"):
         gram = gram + swap(gram, "col", 1)
-        gram = after(total(gram, "col", 2), in_hbm(residual_block), in_hbm(coef))
-        gram = total(gram, "row", 1)
+        gram = total_shared(gram, "col", in_hbm(residual_block), in_hbm(coef))
+        gram = total_shared(gram, "row")
         gram = jnp.concatenate(
             [gram[:, :width], gram[:, LANES // 2 : LANES // 2 + width]], axis=0
         )

time: 70.9 us -> 73.8 us (1.041)
  starting transfers between devices: 27.6 us -> 34.7 us
  waiting for transfers between devices: 23.4 us -> 19.7 us
    ppermute x0 -> x4, starting transfers between devices: none -> 4.5 us  [trade(): return lax.ppermute(value, ('row', 'col'), pairs)]
    ppermute x1, waiting for transfers between devices: 4.64 us -> 2.66 us  [local(): lax.ppermute(parts[0], 'row', [(0, 3), (3, 0)])]
    ppermute x1, starting transfers between devices: 4.07 us -> 5.91 us  [local(): lax.ppermute(parts[0], 'row', [(0, 3), (3, 0)])]
    ppermute x6, waiting for transfers between devices: 6.68 us -> 4.98 us  [total_by_core(): values[m] = lax.ppermute(value, ('row', 'col'), trades)]
    ppermute x0 -> x4, waiting for transfers between devices: none -> 1.64 us  [trade(): return lax.ppermute(value, ('row', 'col'), pairs)]
    ppermute x17 -> x13, waiting for transfers between devices: 11.6 us -> 10.4 us  [swap(): return lax.ppermute(value, axis, [(i, i ^ mask) for i in range(count)])]
    ppermute x17 -> x13, starting transfers between devices: 13.6 us -> 14 us  [swap(): return lax.ppermute(value, axis, [(i, i ^ mask) for i in range(count)])]
  transfers between devices with their start and end apart: 26 -> 26, of which waited for: 18 -> 15; matrix products, arithmetic and copies ran while one was open for 0% -> 0% of each run, Pallas kernels for 18% -> 17%
where the time goes in v17:
time: 73.8 us; the launch traced here: 73.7 us
  starting transfers between devices  34.7 us (47%)
  waiting for transfers between devices  19.7 us (27%)
  Pallas kernels  15.8 us (21%)
  other arithmetic  1.8 us (2%)
  between operations  1.56 us (2%)
    ppermute x13, starting transfers between devices, swap(): return lax.ppermute(value, axis, [(i, i ^ mask) for i in range(count)])  14 us
    ppermute x13, waiting for transfers between devices, swap(): return lax.ppermute(value, axis, [(i, i ^ mask) for i in range(count)])  10.4 us
    ppermute x6, starting transfers between devices, total_by_core(): values[m] = lax.ppermute(value, ('row', 'col'), trades)  8 us
    ppermute x1, starting transfers between devices, local(): lax.ppermute(parts[0], 'row', [(0, 3), (3, 0)])  5.91 us
    pallas_call x1, Pallas kernels, local(): pl.pallas_call(functools.partial(early_kernel, row_devs, col_devs, slab_t...  5.38 us
    ppermute x6, waiting for transfers between devices, total_by_core(): values[m] = lax.ppermute(value, ('row', 'col'), trades)  4.98 us
    ppermute x4, starting transfers between devices, trade(): return lax.ppermute(value, ('row', 'col'), pairs)  4.5 us
    ppermute x1, waiting for transfers between devices, local(): lax.ppermute(parts[0], 'row', [(0, 3), (3, 0)])  2.66 us
  transfers between devices with their start and end apart: 26, of which 15 were waited for; matrix products, arithmetic and copies ran while one was open for 0% of the time, Pallas kernels for 17%

profile of v17, /device:TPU:0, one launch (start us, length us, event | category | flops | bytes accessed | tf_op | source)
XLA Modules:
  0.0 73.7 jit_solution(995362911522346492)
XLA Ops:
  0.6 1.0 %convert_element_type.9.own_panel = bf16[48,2048]{1,0:T(8,128)(2,1)S(1)} convert(f32[48,2048]{1,0:T(8,128)} %current.7) | non-fusion elementwise | flops 98304 | bytes 589824 | tf_op jit(solution)/shard_map/gather/convert_element_type | solution.py:441
  1.7 0.5 collective-permute-start
  2.2 2.6 %collective-permute-start.1 = (bf16[48,2048]{1,0:T(8,128)(2,1)S(1)}, bf16[48,2048]{1,0:T(8,128)(2,1)S(1)}, u32[]{:S(2)}, u32[]{:S(2)}) collective-permute-start(bf16[48,2048]{1,0:T(8,128)(2,1)S(1)} %convert_element_type.9.own_panel), channel_id=1, source_target_pairs={{0,2},{1,3},{2,0},{3,1},{4,6},{5,7},{6,4},{7,5},{8,10},{9,11},{10,... | collective-permute-start | bytes 589832 | tf_op jit(solution)/shard_map/gather/ppermute | solution.py:21
  4.7 1.5 %collective-permute-start.3 = (bf16[48,2048]{1,0:T(8,128)(2,1)S(1)}, bf16[48,2048]{1,0:T(8,128)(2,1)S(1)}, u32[]{:S(2)}, u32[]{:S(2)}) collective-permute-start(bf16[48,2048]{1,0:T(8,128)(2,1)S(1)} %convert_element_type.9.own_panel), channel_id=1, source_target_pairs={{0,4},{1,5},{2,6},{3,7},{4,0},{5,1},{6,2},{7,3},{8,12},{9,13},{10,... | collective-permute-start | bytes 589832 | tf_op jit(solution)/shard_map/gather/ppermute | solution.py:21
  6.3 0.0 collective-permute-start.5
  6.9 0.1 pad_add_fusion.place
  7.0 0.0 collective-permute-done.near_panel
  7.0 5.4 %early.1 = (s32[1,896]{1,0:T(1,128)S(4)}, bf16[512,128,128]{2,1,0:T(8,128)(2,1)S(1)}, f32[65,48,128]{2,1,0:T(8,128)S(1)}, bf16[9,48,2048]{2,1,0:T(8,128)(2,1)S(1)}) custom-call(s32[2]{0:T(128)S(1)} %pad_add_fusion.place, s32[1]{0:T(128)S(6)} %copy.25.counts, s32[1,512]{1,0:T(1,128)} %bitcast.17, s32[1,512]{1,0:T(1,128)} %bitcast.18, ...), custom_call_target="tpu_custom_call" | custom-call | flops 805306368 | bytes 16777216 | tf_op jit(solution)/shard_map/early/pallas_call | solution.py:450
  12.4 0.0 collective-permute-done.1.refs_0_
  12.4 2.1 %collective-permute-start.2 = (bf16[48,2048]{1,0:T(8,128)(2,1)S(1)}, bf16[48,2048]{1,0:T(8,128)(2,1)S(1)}, u32[]{:S(2)}, u32[]{:S(2)}) collective-permute-start(bf16[48,2048]{1,0:T(8,128)(2,1)S(1)} %gather.4.refs_0_), channel_id=1, source_target_pairs={{0,1},{1,0},{2,3},{3,2},{4,5},{5,4},{6,7},{7,6},{8,9},{9,8},{10,11... | collective-permute-start | bytes 589832 | tf_op jit(solution)/shard_map/gather/ppermute | solution.py:21
  14.5 1.4 %collective-permute-done.3.refs_0_ = bf16[48,2048]{1,0:T(8,128)(2,1)S(1)} collective-permute-done((bf16[48,2048]{1,0:T(8,128)(2,1)S(1)}, bf16[48,2048]{1,0:T(8,128)(2,1)S(1)}, u32[]{:S(2)}, u32[]{:S(2)}) %collective-permute-start.3) | collective-permute-done | bytes 196640 | tf_op jit(solution)/shard_map/gather/ppermute | solution.py:21
  15.9 0.5 collective-permute-start.6
  16.4 0.8 %gather.7.refs_5_ = bf16[9,48,2048]{2,1,0:T(8,128)(2,1)S(1)} custom-call(bf16[48,2048]{1,0:T(8,128)(2,1)S(1)} %gather.4.refs_0_, bf16[48,2048]{1,0:T(8,128)(2,1)S(1)} %gather.5.refs_1_, bf16[48,2048]{1,0:T(8,128)(2,1)S(1)} %gather.6.refs_2_, bf16[9,48,2048]{2,1,0:T(8,128)(2,1)S(1)} %get-tuple-element.19.refs_3_), custom_call_target="tpu_custom_call", output_to_operand_aliasing={{}: (3, {})} | custom-call | flops 48 | bytes 1 | tf_op jit(solution)/shard_map/gather/pallas_call | solution.py:485
  17.2 0.2 collective-permute-done.4.refs_1_
  17.4 0.3 collective-permute-done.6.refs_2_
  17.6 1.8 %late.3 = (bf16[48,2048]{1,0:T(8,128)(2,1)S(1)}, bf16[9,48,2048]{2,1,0:T(8,128)(2,1)S(1)}) custom-call(s32[1,896]{1,0:T(1,128)S(4)} %get-tuple-element.16.plan, bf16[48,2048]{1,0:T(8,128)(2,1)S(1)} %collective-permute-done.2.refs_0_, bf16[48,2048]{1,0:T(8,128)(2,1)S(1)} %collective-permute-done.4.refs_1_, ...), custom_call_target="tpu_custom_call", output_to_operand_aliasing={{1}: (6, {})} | custom-call | flops 48 | bytes 1 | tf_op jit(solution)/shard_map/late/pallas_call | solution.py:501
  19.4 1.6 %collective-permute-start.7 = (bf16[48,2048]{1,0:T(8,128)(2,1)S(1)}, bf16[48,2048]{1,0:T(8,128)(2,1)S(1)}, u32[]{:S(2)}, u32[]{:S(2)}) collective-permute-start(bf16[48,2048]{1,0:T(8,128)(2,1)S(1)} %get-tuple-element.21), channel_id=1, source_target_pairs={{0,8},{24,16},{8,24},{16,0},{1,9},{25,17},{9,25},{17,1},{2,10},{26... | collective-permute-start | bytes 589832 | tf_op jit(solution)/shard_map/late/ppermute | solution.py:521
  21.0 1.7 %late.5 = (bf16[48,2048]{1,0:T(8,128)(2,1)S(1)}, f32[48,2048]{1,0:T(8,128)S(1)}, bf16[48,2048]{1,0:T(8,128)(2,1)S(1)}) custom-call(s32[1,896]{1,0:T(1,128)S(4)} %get-tuple-element.16.plan, bf16[9,48,2048]{2,1,0:T(8,128)(2,1)S(1)} %get-tuple-element.20.panel_buf, bf16[512,128,128]{2,1,0:T(8,128)(2,1)S(1)} %get-tuple-element.18.refs_3_.tiles, ...), custom_call_target="tpu_custom_call" | custom-call | flops 48 | bytes 1 | tf_op jit(solution)/shard_map/late/pallas_call | solution.py:511
  22.7 5.9 %collective-permute-start.8 = (bf16[48,2048]{1,0:T(8,128)(2,1)S(1)}, bf16[48,2048]{1,0:T(8,128)(2,1)S(1)}, u32[]{:S(2)}, u32[]{:S(2)}) collective-permute-start(bf16[48,2048]{1,0:T(8,128)(2,1)S(1)} %get-tuple-element.22), channel_id=1, source_target_pairs={{0,24},{24,0},{1,25},{25,1},{2,26},{26,2},{3,27},{27,3},{4,28},{28... | collective-permute-start | bytes 589832 | tf_op jit(solution)/shard_map/late/ppermute | solution.py:525
  28.7 0.1 collective-permute-start.10
  28.8 0.0 collective-permute-done.7.refs_0_
  28.8 0.7 collective-permute-start.9
  29.5 0.0 copy-start
  29.5 0.0 copy-start.3
  29.6 1.7 %late.4.base = f32[48,2048]{1,0:T(8,128)S(1)} custom-call(s32[1,896]{1,0:T(1,128)S(4)} %get-tuple-element.16.plan, bf16[9,48,2048]{2,1,0:T(8,128)(2,1)S(1)} %get-tuple-element.20.panel_buf, bf16[512,128,128]{2,1,0:T(8,128)(2,1)S(1)} %get-tuple-element.18.refs_3_.tiles, f32[65,48,128]{2,1,0:T(8,128)S(1)} %get-tuple-element.17.refs_1_.refs_4_.early, ...), custom_call_target="tpu_custom_call" | custom-call | flops 48 | bytes 1 | tf_op jit(solution)/shard_map/late/pallas_call | solution.py:532
  31.3 2.7 %collective-permute-done.8.refs_1_ = bf16[48,2048]{1,0:T(8,128)(2,1)S(1)} collective-permute-done((bf16[48,2048]{1,0:T(8,128)(2,1)S(1)}, bf16[48,2048]{1,0:T(8,128)(2,1)S(1)}, u32[]{:S(2)}, u32[]{:S(2)}) %collective-permute-start.8) | collective-permute-done | bytes 196640 | tf_op jit(solution)/shard_map/late/ppermute | solution.py:525
  33.9 4.7 %collective-permute-done.10.refs_3_ = bf16[48,2048]{1,0:T(8,128)(2,1)S(1)} collective-permute-done((bf16[48,2048]{1,0:T(8,128)(2,1)S(1)}, bf16[48,2048]{1,0:T(8,128)(2,1)S(1)}, u32[]{:S(2)}, u32[]{:S(2)}) %collective-permute-start.10) | collective-permute-done | bytes 196640 | tf_op jit(solution)/shard_map/late/ppermute | solution.py:21
  38.6 0.7 coefficients.2
  39.3 0.1 collective-permute-start.11
  39.4 0.7 coefficients.3
  40.1 0.5 collective-permute-done.11
  40.6 1.0 %collective-permute-start.14 = (f32[12,8,128]{2,1,0:T(8,128)S(1)}, f32[12,8,128]{2,1,0:T(8,128)S(1)}, u32[]{:S(2)}, u32[]{:S(2)}) collective-permute-start(f32[12,8,128]{2,1,0:T(8,128)S(1)} %add.40), channel_id=1, source_target_pairs={{0,6},{1,25},{2,4},{3,27},{4,2},{5,29},{6,0},{7,31},{8,14},{9,17},... | collective-permute-start | bytes 147464 | tf_op jit(solution)/shard_map/coefficients/ppermute | solution.py:71
  41.6 0.5 collective-permute-start.13
  42.1 2.1 %collective-permute-start.12 = (f32[12,8,128]{2,1,0:T(8,128)S(1)}, f32[12,8,128]{2,1,0:T(8,128)S(1)}, u32[]{:S(2)}, u32[]{:S(2)}) collective-permute-start(f32[12,8,128]{2,1,0:T(8,128)S(1)} %add.40), channel_id=1, source_target_pairs={{0,2},{1,9},{2,0},{3,11},{4,6},{5,13},{6,4},{7,15},{8,10},{9,1},{1... | collective-permute-start | bytes 147464 | tf_op jit(solution)/shard_map/coefficients/ppermute | solution.py:71
  44.2 1.6 %collective-permute-done.14 = f32[12,8,128]{2,1,0:T(8,128)S(1)} collective-permute-done((f32[12,8,128]{2,1,0:T(8,128)S(1)}, f32[12,8,128]{2,1,0:T(8,128)S(1)}, u32[]{:S(2)}, u32[]{:S(2)}) %collective-permute-start.14) | collective-permute-done | bytes 49184 | tf_op jit(solution)/shard_map/coefficients/ppermute | solution.py:71
  45.8 0.4 collective-permute-done.13
  46.2 0.0 collective-permute-done.12
  46.3 1.8 %collective-permute-start.17 = (f32[12,8,128]{2,1,0:T(8,128)S(1)}, f32[12,8,128]{2,1,0:T(8,128)S(1)}, u32[]{:S(2)}, u32[]{:S(2)}) collective-permute-start(f32[12,8,128]{2,1,0:T(8,128)S(1)} %add_add_fusion.1), channel_id=1, source_target_pairs={{0,24},{1,7},{2,26},{3,5},{4,28},{5,3},{6,30},{7,1},{8,16},{9,15},... | collective-permute-start | bytes 147464 | tf_op jit(solution)/shard_map/coefficients/ppermute | solution.py:71
  48.1 0.7 collective-permute-start.16
  48.8 1.9 %collective-permute-start.15 = (f32[12,8,128]{2,1,0:T(8,128)S(1)}, f32[12,8,128]{2,1,0:T(8,128)S(1)}, u32[]{:S(2)}, u32[]{:S(2)}) collective-permute-start(f32[12,8,128]{2,1,0:T(8,128)S(1)} %add_add_fusion.1), channel_id=1, source_target_pairs={{0,8},{1,3},{2,10},{3,1},{4,12},{5,7},{6,14},{7,5},{8,0},{9,11},{1... | collective-permute-start | bytes 147464 | tf_op jit(solution)/shard_map/coefficients/ppermute | solution.py:71
  50.7 1.5 %collective-permute-done.17 = f32[12,8,128]{2,1,0:T(8,128)S(1)} collective-permute-done((f32[12,8,128]{2,1,0:T(8,128)S(1)}, f32[12,8,128]{2,1,0:T(8,128)S(1)}, u32[]{:S(2)}, u32[]{:S(2)}) %collective-permute-start.17) | collective-permute-done | bytes 49184 | tf_op jit(solution)/shard_map/coefficients/ppermute | solution.py:71
  52.2 1.4 %collective-permute-done.16 = f32[12,8,128]{2,1,0:T(8,128)S(1)} collective-permute-done((f32[12,8,128]{2,1,0:T(8,128)S(1)}, f32[12,8,128]{2,1,0:T(8,128)S(1)}, u32[]{:S(2)}, u32[]{:S(2)}) %collective-permute-start.16) | collective-permute-done | bytes 49184 | tf_op jit(solution)/shard_map/coefficients/ppermute | solution.py:71
  53.6 0.0 collective-permute-done.15
  53.7 0.1 collective-permute-start.18
  53.7 0.6 residual.4.less
  54.3 0.6 collective-permute-done.18.other
  55.0 0.9 %residual.5 = (f32[48,2048]{1,0:T(8,128)S(1)}, f32[24,128]{1,0:T(8,128)S(1)}) custom-call(s32[1,896]{1,0:T(1,128)S(4)} %get-tuple-element.16.plan, f32[12,8,128]{2,1,0:T(8,128)S(1)} %collective-permute-done.18.other, f32[48,2048]{1,0:T(8,128)S(1)} %residual.4.less, f32[1,2048]{1,0:T(1,128)S(1)} %bitcast.14, f32[48,2048]{1,0:T(8,128)S(1)} %copy-done.1, ...), custom_call_target="tpu_custom_call" | custom-call | flops 48 | bytes 1 | tf_op jit(solution)/shard_map/residual/pallas_call | solution.py:575
  55.9 0.2 collective-permute-start.19
  56.1 1.0 %collective-permute-done.19 = f32[24,128]{1,0:T(8,128)S(1)} collective-permute-done((f32[24,128]{1,0:T(8,128)S(1)}, f32[24,128]{1,0:T(8,128)S(1)}, u32[]{:S(2)}, u32[]{:S(2)}) %collective-permute-start.19) | collective-permute-done | bytes 12320 | tf_op jit(solution)/shard_map/gram/ppermute | solution.py:21
  57.1 1.8 %collective-permute-start.21 = (f32[24,128]{1,0:T(8,128)S(1)}, f32[24,128]{1,0:T(8,128)S(1)}, u32[]{:S(2)}, u32[]{:S(2)}) collective-permute-start(f32[24,128]{1,0:T(8,128)S(1)} %add.47), channel_id=1, source_target_pairs={{0,2},{1,7},{2,0},{3,5},{4,6},{5,3},{6,4},{7,1},{8,10},{9,15},{10,... | collective-permute-start | bytes 36872 | tf_op jit(solution)/shard_map/gram/ppermute | solution.py:52
  58.9 0.7 collective-permute-start.20
  59.6 0.8 %residual.6.refs_1_ = f32[48,2048]{1,0:T(8,128)} custom-call(f32[48,2048]{1,0:T(8,128)S(1)} %get-tuple-element.27.value), custom_call_target="tpu_custom_call" | custom-call | flops 48 | bytes 1 | tf_op jit(solution)/shard_map/residual/pallas_call | solution.py:586
  60.3 0.8 %residual.7.refs_2_ = f32[432,48]{1,0:T(8,128)} custom-call(s32[1,896]{1,0:T(1,128)S(4)} %get-tuple-element.16.plan, f32[12,8,128]{2,1,0:T(8,128)S(1)} %add_add_fusion.mine, f32[12,8,128]{2,1,0:T(8,128)S(1)} %collective-permute-done.18.other), custom_call_target="tpu_custom_call" | custom-call | flops 48 | bytes 1 | tf_op jit(solution)/shard_map/residual/pallas_call | solution.py:595
  61.1 0.0 collective-permute-done.21
  61.2 0.0 collective-permute-done.20
  61.2 2.4 %collective-permute-start.22 = (f32[24,128]{1,0:T(8,128)S(1)}, f32[24,128]{1,0:T(8,128)S(1)}, u32[]{:S(2)}, u32[]{:S(2)}) collective-permute-start(f32[24,128]{1,0:T(8,128)S(1)} %gram.1), channel_id=1, source_target_pairs={{0,1},{1,0},{2,3},{3,2},{4,5},{5,4},{6,7},{7,6},{8,9},{9,8},{10,11... | collective-permute-start | bytes 36872 | tf_op jit(solution)/shard_map/gram/ppermute | solution.py:21
  63.6 0.8 %collective-permute-done.22 = f32[24,128]{1,0:T(8,128)S(1)} collective-permute-done((f32[24,128]{1,0:T(8,128)S(1)}, f32[24,128]{1,0:T(8,128)S(1)}, u32[]{:S(2)}, u32[]{:S(2)}) %collective-permute-start.22) | collective-permute-done | bytes 12320 | tf_op jit(solution)/shard_map/gram/ppermute | solution.py:21
  64.4 1.4 %collective-permute-start.24 = (f32[24,128]{1,0:T(8,128)S(1)}, f32[24,128]{1,0:T(8,128)S(1)}, u32[]{:S(2)}, u32[]{:S(2)}) collective-permute-start(f32[24,128]{1,0:T(8,128)S(1)} %add.49), channel_id=1, source_target_pairs={{0,8},{1,25},{2,10},{3,27},{4,12},{5,29},{6,14},{7,31},{8,0},{9,17... | collective-permute-start | bytes 36872 | tf_op jit(solution)/shard_map/gram/ppermute | solution.py:52
  65.8 0.7 collective-permute-start.23
  66.5 1.6 %collective-permute-done.24 = f32[24,128]{1,0:T(8,128)S(1)} collective-permute-done((f32[24,128]{1,0:T(8,128)S(1)}, f32[24,128]{1,0:T(8,128)S(1)}, u32[]{:S(2)}, u32[]{:S(2)}) %collective-permute-start.24) | collective-permute-done | bytes 12320 | tf_op jit(solution)/shard_map/gram/ppermute | solution.py:52
  68.1 4.0 %collective-permute-start.25 = (f32[24,128]{1,0:T(8,128)S(1)}, f32[24,128]{1,0:T(8,128)S(1)}, u32[]{:S(2)}, u32[]{:S(2)}) collective-permute-start(f32[24,128]{1,0:T(8,128)S(1)} %select_add_fusion), channel_id=1, source_target_pairs={{0,1},{1,0},{2,3},{3,2},{4,5},{5,4},{6,7},{7,6},{8,9},{9,8},{10,11... | collective-permute-start | bytes 36872 | tf_op jit(solution)/shard_map/gram/ppermute | solution.py:21
  72.1 0.8 %collective-permute-done.25 = f32[24,128]{1,0:T(8,128)S(1)} collective-permute-done((f32[24,128]{1,0:T(8,128)S(1)}, f32[24,128]{1,0:T(8,128)S(1)}, u32[]{:S(2)}, u32[]{:S(2)}) %collective-permute-start.25) | collective-permute-done | bytes 12320 | tf_op jit(solution)/shard_map/gram/ppermute | solution.py:21
  73.0 0.1 fusion
  73.1 0.6 pad_maximum_fusion
  (28 shorter events, 0.1 us)
Async XLA Ops:
  1.7 5.4 %collective-permute-start = (bf16[48,2048]{1,0:T(8,128)(2,1)S(1)}, bf16[48,2048]{1,0:T(8,128)(2,1)S(1)}, u32[]{:S(2)}, u32[]{:S(2)}) collective-permute-start(bf16[48,2048]{1,0:T(8,128)(2,1)S(1)} %convert_element_type.9.own_panel), channel_id=1, source_target_pairs={{0,1},{1,0},{2,3},{3,2},{4,5},{5,4},{6,7},{7,6},{8,9},{9,8},{10,11... | collective-permute-start | bytes 589832 | tf_op jit(solution)/shard_map/gather/ppermute | solution.py:21
  2.2 10.2 %collective-permute-start.1 = (bf16[48,2048]{1,0:T(8,128)(2,1)S(1)}, bf16[48,2048]{1,0:T(8,128)(2,1)S(1)}, u32[]{:S(2)}, u32[]{:S(2)}) collective-permute-start(bf16[48,2048]{1,0:T(8,128)(2,1)S(1)} %convert_element_type.9.own_panel), channel_id=1, source_target_pairs={{0,2},{1,3},{2,0},{3,1},{4,6},{5,7},{6,4},{7,5},{8,10},{9,11},{10,... | collective-permute-start | bytes 589832 | tf_op jit(solution)/shard_map/gather/ppermute | solution.py:21
  4.7 11.2 %collective-permute-start.3 = (bf16[48,2048]{1,0:T(8,128)(2,1)S(1)}, bf16[48,2048]{1,0:T(8,128)(2,1)S(1)}, u32[]{:S(2)}, u32[]{:S(2)}) collective-permute-start(bf16[48,2048]{1,0:T(8,128)(2,1)S(1)} %convert_element_type.9.own_panel), channel_id=1, source_target_pairs={{0,4},{1,5},{2,6},{3,7},{4,0},{5,1},{6,2},{7,3},{8,12},{9,13},{10,... | collective-permute-start | bytes 589832 | tf_op jit(solution)/shard_map/gather/ppermute | solution.py:21
  6.3 9.7 %collective-permute-start.5 = (bf16[48,2048]{1,0:T(8,128)(2,1)S(1)}, bf16[48,2048]{1,0:T(8,128)(2,1)S(1)}, u32[]{:S(2)}, u32[]{:S(2)}) collective-permute-start(bf16[48,2048]{1,0:T(8,128)(2,1)S(1)} %convert_element_type.9.own_panel), channel_id=1, source_target_pairs={{0,6},{1,7},{2,4},{3,5},{4,2},{5,3},{6,0},{7,1},{8,14},{9,15},{10,... | collective-permute-start | bytes 589832 | tf_op jit(solution)/shard_map/gather/ppermute | solution.py:21
  12.4 4.8 %collective-permute-start.2 = (bf16[48,2048]{1,0:T(8,128)(2,1)S(1)}, bf16[48,2048]{1,0:T(8,128)(2,1)S(1)}, u32[]{:S(2)}, u32[]{:S(2)}) collective-permute-start(bf16[48,2048]{1,0:T(8,128)(2,1)S(1)} %gather.4.refs_0_), channel_id=1, source_target_pairs={{0,1},{1,0},{2,3},{3,2},{4,5},{5,4},{6,7},{7,6},{8,9},{9,8},{10,11... | collective-permute-start | bytes 589832 | tf_op jit(solution)/shard_map/gather/ppermute | solution.py:21
  15.9 1.4 %collective-permute-start.4 = (bf16[48,2048]{1,0:T(8,128)(2,1)S(1)}, bf16[48,2048]{1,0:T(8,128)(2,1)S(1)}, u32[]{:S(2)}, u32[]{:S(2)}) collective-permute-start(bf16[48,2048]{1,0:T(8,128)(2,1)S(1)} %gather.5.refs_1_), channel_id=1, source_target_pairs={{0,1},{1,0},{2,3},{3,2},{4,5},{5,4},{6,7},{7,6},{8,9},{9,8},{10,11... | collective-permute-start | bytes 589832 | tf_op jit(solution)/shard_map/gather/ppermute | solution.py:21
  15.9 1.7 %collective-permute-start.6 = (bf16[48,2048]{1,0:T(8,128)(2,1)S(1)}, bf16[48,2048]{1,0:T(8,128)(2,1)S(1)}, u32[]{:S(2)}, u32[]{:S(2)}) collective-permute-start(bf16[48,2048]{1,0:T(8,128)(2,1)S(1)} %gather.6.refs_2_), channel_id=1, source_target_pairs={{0,1},{1,0},{2,3},{3,2},{4,5},{5,4},{6,7},{7,6},{8,9},{9,8},{10,11... | collective-permute-start | bytes 589832 | tf_op jit(solution)/shard_map/gather/ppermute | solution.py:21
  19.4 9.3 %collective-permute-start.7 = (bf16[48,2048]{1,0:T(8,128)(2,1)S(1)}, bf16[48,2048]{1,0:T(8,128)(2,1)S(1)}, u32[]{:S(2)}, u32[]{:S(2)}) collective-permute-start(bf16[48,2048]{1,0:T(8,128)(2,1)S(1)} %get-tuple-element.21), channel_id=1, source_target_pairs={{0,8},{24,16},{8,24},{16,0},{1,9},{25,17},{9,25},{17,1},{2,10},{26... | collective-permute-start | bytes 589832 | tf_op jit(solution)/shard_map/late/ppermute | solution.py:521
  21.0 8.5 %copy-start.1 = (f32[48,2048]{1,0:T(8,128)S(1)}, f32[48,2048]{1,0:T(8,128)}, u32[]{:S(2)}) copy-start(f32[48,2048]{1,0:T(8,128)} %current.7) | copy-start | bytes 1179652
  21.0 8.5 %copy-start.2 = (f32[48,2048]{1,0:T(8,128)S(1)}, f32[48,2048]{1,0:T(8,128)}, u32[]{:S(2)}) copy-start(f32[48,2048]{1,0:T(8,128)} %previous.1) | copy-start | bytes 1179652
  21.0 8.5 %copy-start.4 = (f32[48,48]{1,0:T(8,128)S(1)}, f32[48,48]{1,0:T(8,128)}, u32[]{:S(2)}) copy-start(f32[48,48]{1,0:T(8,128)} %coupling.1) | copy-start | bytes 27652
  21.0 8.5 %copy-start.5 = (f32[2048]{0:T(1024)S(1)}, f32[2048]{0:T(1024)}, u32[]{:S(2)}) copy-start(f32[2048]{0:T(1024)} %param.14) | copy-start | bytes 24580
  22.7 11.2 %collective-permute-start.8 = (bf16[48,2048]{1,0:T(8,128)(2,1)S(1)}, bf16[48,2048]{1,0:T(8,128)(2,1)S(1)}, u32[]{:S(2)}, u32[]{:S(2)}) collective-permute-start(bf16[48,2048]{1,0:T(8,128)(2,1)S(1)} %get-tuple-element.22), channel_id=1, source_target_pairs={{0,24},{24,0},{1,25},{25,1},{2,26},{26,2},{3,27},{27,3},{4,28},{28... | collective-permute-start | bytes 589832 | tf_op jit(solution)/shard_map/late/ppermute | solution.py:525
  28.7 10.0 %collective-permute-start.10 = (bf16[48,2048]{1,0:T(8,128)(2,1)S(1)}, bf16[48,2048]{1,0:T(8,128)(2,1)S(1)}, u32[]{:S(2)}, u32[]{:S(2)}) collective-permute-start(bf16[48,2048]{1,0:T(8,128)(2,1)S(1)} %get-tuple-element.24), channel_id=1, source_target_pairs={{0,8},{8,0},{16,24},{24,16},{1,9},{9,1},{17,25},{25,17},{2,10},{10... | collective-permute-start | bytes 589832 | tf_op jit(solution)/shard_map/late/ppermute | solution.py:21
  28.8 9.8 %collective-permute-start.9 = (bf16[48,2048]{1,0:T(8,128)(2,1)S(1)}, bf16[48,2048]{1,0:T(8,128)(2,1)S(1)}, u32[]{:S(2)}, u32[]{:S(2)}) collective-permute-start(bf16[48,2048]{1,0:T(8,128)(2,1)S(1)} %add_convert_fusion), channel_id=1, source_target_pairs={{8,16},{16,8},{9,17},{17,9},{10,18},{18,10},{11,19},{19,11},{12,20... | collective-permute-start | bytes 589832 | tf_op jit(solution)/shard_map/late/ppermute | solution.py:526
  29.5 9.1 %copy-start = (f32[8,48,2048]{2,1,0:T(8,128)S(1)}, f32[8,48,2048]{2,1,0:T(8,128)}, u32[]{:S(2)}) copy-start(f32[8,48,2048]{2,1,0:T(8,128)} %param.13) | copy-start | bytes 9437188
  29.5 9.1 %copy-start.3 = (f32[2048]{0:T(1024)S(1)}, f32[2048]{0:T(1024)}, u32[]{:S(2)}) copy-start(f32[2048]{0:T(1024)} %param.15) | copy-start | bytes 24580
  39.3 1.3 %collective-permute-start.11 = (f32[12,8,128]{2,1,0:T(8,128)S(1)}, f32[12,8,128]{2,1,0:T(8,128)S(1)}, u32[]{:S(2)}, u32[]{:S(2)}) collective-permute-start(f32[12,8,128]{2,1,0:T(8,128)S(1)} %get-tuple-element.26), channel_id=1, source_target_pairs={{0,1},{1,0},{2,3},{3,2},{4,5},{5,4},{6,7},{7,6},{8,9},{9,8},{10,11... | collective-permute-start | bytes 147464 | tf_op jit(solution)/shard_map/coefficients/ppermute | solution.py:21
  40.6 5.2 %collective-permute-start.14 = (f32[12,8,128]{2,1,0:T(8,128)S(1)}, f32[12,8,128]{2,1,0:T(8,128)S(1)}, u32[]{:S(2)}, u32[]{:S(2)}) collective-permute-start(f32[12,8,128]{2,1,0:T(8,128)S(1)} %add.40), channel_id=1, source_target_pairs={{0,6},{1,25},{2,4},{3,27},{4,2},{5,29},{6,0},{7,31},{8,14},{9,17},... | collective-permute-start | bytes 147464 | tf_op jit(solution)/shard_map/coefficients/ppermute | solution.py:71
  41.6 4.6 %collective-permute-start.13 = (f32[12,8,128]{2,1,0:T(8,128)S(1)}, f32[12,8,128]{2,1,0:T(8,128)S(1)}, u32[]{:S(2)}, u32[]{:S(2)}) collective-permute-start(f32[12,8,128]{2,1,0:T(8,128)S(1)} %add.40), channel_id=1, source_target_pairs={{0,4},{1,17},{2,6},{3,19},{4,0},{5,21},{6,2},{7,23},{8,12},{9,25},... | collective-permute-start | bytes 147464 | tf_op jit(solution)/shard_map/coefficients/ppermute | solution.py:71
  42.1 4.1 %collective-permute-start.12 = (f32[12,8,128]{2,1,0:T(8,128)S(1)}, f32[12,8,128]{2,1,0:T(8,128)S(1)}, u32[]{:S(2)}, u32[]{:S(2)}) collective-permute-start(f32[12,8,128]{2,1,0:T(8,128)S(1)} %add.40), channel_id=1, source_target_pairs={{0,2},{1,9},{2,0},{3,11},{4,6},{5,13},{6,4},{7,15},{8,10},{9,1},{1... | collective-permute-start | bytes 147464 | tf_op jit(solution)/shard_map/coefficients/ppermute | solution.py:71
  46.3 6.0 %collective-permute-start.17 = (f32[12,8,128]{2,1,0:T(8,128)S(1)}, f32[12,8,128]{2,1,0:T(8,128)S(1)}, u32[]{:S(2)}, u32[]{:S(2)}) collective-permute-start(f32[12,8,128]{2,1,0:T(8,128)S(1)} %add_add_fusion.1), channel_id=1, source_target_pairs={{0,24},{1,7},{2,26},{3,5},{4,28},{5,3},{6,30},{7,1},{8,16},{9,15},... | collective-permute-start | bytes 147464 | tf_op jit(solution)/shard_map/coefficients/ppermute | solution.py:71
  48.1 5.5 %collective-permute-start.16 = (f32[12,8,128]{2,1,0:T(8,128)S(1)}, f32[12,8,128]{2,1,0:T(8,128)S(1)}, u32[]{:S(2)}, u32[]{:S(2)}) collective-permute-start(f32[12,8,128]{2,1,0:T(8,128)S(1)} %add_add_fusion.1), channel_id=1, source_target_pairs={{0,16},{1,5},{2,18},{3,7},{4,20},{5,1},{6,22},{7,3},{8,24},{9,13},... | collective-permute-start | bytes 147464 | tf_op jit(solution)/shard_map/coefficients/ppermute | solution.py:71
  48.8 4.8 %collective-permute-start.15 = (f32[12,8,128]{2,1,0:T(8,128)S(1)}, f32[12,8,128]{2,1,0:T(8,128)S(1)}, u32[]{:S(2)}, u32[]{:S(2)}) collective-permute-start(f32[12,8,128]{2,1,0:T(8,128)S(1)} %add_add_fusion.1), channel_id=1, source_target_pairs={{0,8},{1,3},{2,10},{3,1},{4,12},{5,7},{6,14},{7,5},{8,0},{9,11},{1... | collective-permute-start | bytes 147464 | tf_op jit(solution)/shard_map/coefficients/ppermute | solution.py:71
  53.7 1.3 %collective-permute-start.18 = (f32[12,8,128]{2,1,0:T(8,128)S(1)}, f32[12,8,128]{2,1,0:T(8,128)S(1)}, u32[]{:S(2)}, u32[]{:S(2)}) collective-permute-start(f32[12,8,128]{2,1,0:T(8,128)S(1)} %add_add_fusion.mine), channel_id=1, source_target_pairs={{0,1},{1,0},{2,3},{3,2},{4,5},{5,4},{6,7},{7,6},{8,9},{9,8},{10,11... | collective-permute-start | bytes 147464 | tf_op jit(solution)/shard_map/coefficients/ppermute | solution.py:21
  55.9 1.2 %collective-permute-start.19 = (f32[24,128]{1,0:T(8,128)S(1)}, f32[24,128]{1,0:T(8,128)S(1)}, u32[]{:S(2)}, u32[]{:S(2)}) collective-permute-start(f32[24,128]{1,0:T(8,128)S(1)} %get-tuple-element.28), channel_id=1, source_target_pairs={{0,1},{1,0},{2,3},{3,2},{4,5},{5,4},{6,7},{7,6},{8,9},{9,8},{10,11... | collective-permute-start | bytes 36872 | tf_op jit(solution)/shard_map/gram/ppermute | solution.py:21
  57.1 4.0 %collective-permute-start.21 = (f32[24,128]{1,0:T(8,128)S(1)}, f32[24,128]{1,0:T(8,128)S(1)}, u32[]{:S(2)}, u32[]{:S(2)}) collective-permute-start(f32[24,128]{1,0:T(8,128)S(1)} %add.47), channel_id=1, source_target_pairs={{0,2},{1,7},{2,0},{3,5},{4,6},{5,3},{6,4},{7,1},{8,10},{9,15},{10,... | collective-permute-start | bytes 36872 | tf_op jit(solution)/shard_map/gram/ppermute | solution.py:52
  58.9 2.3 %collective-permute-start.20 = (f32[24,128]{1,0:T(8,128)S(1)}, f32[24,128]{1,0:T(8,128)S(1)}, u32[]{:S(2)}, u32[]{:S(2)}) collective-permute-start(f32[24,128]{1,0:T(8,128)S(1)} %add.47), channel_id=1, source_target_pairs={{1,5},{3,7},{5,1},{7,3},{9,13},{11,15},{13,9},{15,11},{17,21},{19,... | collective-permute-start | bytes 36872 | tf_op jit(solution)/shard_map/gram/ppermute | solution.py:52
  61.2 3.2 %collective-permute-start.22 = (f32[24,128]{1,0:T(8,128)S(1)}, f32[24,128]{1,0:T(8,128)S(1)}, u32[]{:S(2)}, u32[]{:S(2)}) collective-permute-start(f32[24,128]{1,0:T(8,128)S(1)} %gram.1), channel_id=1, source_target_pairs={{0,1},{1,0},{2,3},{3,2},{4,5},{5,4},{6,7},{7,6},{8,9},{9,8},{10,11... | collective-permute-start | bytes 36872 | tf_op jit(solution)/shard_map/gram/ppermute | solution.py:21
  64.4 3.7 %collective-permute-start.24 = (f32[24,128]{1,0:T(8,128)S(1)}, f32[24,128]{1,0:T(8,128)S(1)}, u32[]{:S(2)}, u32[]{:S(2)}) collective-permute-start(f32[24,128]{1,0:T(8,128)S(1)} %add.49), channel_id=1, source_target_pairs={{0,8},{1,25},{2,10},{3,27},{4,12},{5,29},{6,14},{7,31},{8,0},{9,17... | collective-permute-start | bytes 36872 | tf_op jit(solution)/shard_map/gram/ppermute | solution.py:52
  65.8 2.3 %collective-permute-start.23 = (f32[24,128]{1,0:T(8,128)S(1)}, f32[24,128]{1,0:T(8,128)S(1)}, u32[]{:S(2)}, u32[]{:S(2)}) collective-permute-start(f32[24,128]{1,0:T(8,128)S(1)} %add.49), channel_id=1, source_target_pairs={{1,17},{3,19},{5,21},{7,23},{9,25},{11,27},{13,29},{15,31},{17,1},... | collective-permute-start | bytes 36872 | tf_op jit(solution)/shard_map/gram/ppermute | solution.py:52
  68.1 4.9 %collective-permute-start.25 = (f32[24,128]{1,0:T(8,128)S(1)}, f32[24,128]{1,0:T(8,128)S(1)}, u32[]{:S(2)}, u32[]{:S(2)}) collective-permute-start(f32[24,128]{1,0:T(8,128)S(1)} %select_add_fusion), channel_id=1, source_target_pairs={{0,1},{1,0},{2,3},{3,2},{4,5},{5,4},{6,7},{7,6},{8,9},{9,8},{10,11... | collective-permute-start | bytes 36872 | tf_op jit(solution)/shard_map/gram/ppermute | solution.py:21

commit v18 on v16

--- a/solution.py
+++ b/solution.py
@@ -19,6 +19,17 @@
 def swap(value, axis, mask):
     count = lax.axis_size(axis)
     return lax.ppermute(value, axis, [(i, i ^ mask) for i in range(count)])
+
+
+def trade_rows(value, pairs):
+    row_devs, col_devs = lax.axis_size("row"), lax.axis_size("col")
+    to = dict(pairs)
+    trades = []
+    for r in range(row_devs):
+        for c in range(col_devs):
+            partner = to[r] * col_devs + c if r in to else r * col_devs + (c ^ 1)
+            trades.append((r * col_devs + c, partner))
+    return lax.ppermute(value, ("row", "col"), trades)
 
 
 def tree_sum(values):
@@ -297,8 +308,9 @@
     total = base[...]
     for i, ref in enumerate(received):
         value = ref[...].astype(jnp.float32)
-        if relay and i == 0:
-            value = jnp.where((row_of(plan) == 1) | (row_of(plan) == 2), 0.0, value)
+        if relay and i < 3:
+            inner = (row_of(plan) == 1) | (row_of(plan) == 2)
+            value = jnp.where(inner if i < 2 else jnp.logical_not(inner), 0.0, value)
         total = total + value
     recurrence[...] = total
     weighted = total * (mass[...] * (1.0 / cells))
@@ -499,8 +511,8 @@
             joined = (parts[1] + first.astype(f32)).astype(bf16)
             received = [
                 first,
-                lax.ppermute(parts[0], "row", [(0, 3), (3, 0)]),
-                lax.ppermute(joined, "row", [(1, 2), (2, 1)]),
+                trade_rows(parts[0], [(0, 3), (3, 0)]),
+                trade_rows(joined, [(1, 2), (2, 1)]),
                 swap(parts[2], "row", 1),
             ]
         else:

time: 70.9 us -> 70 us (0.987)
  starting transfers between devices: 27.6 us -> 26.1 us
  waiting for transfers between devices: 23.4 us -> 24.3 us
    ppermute x1, waiting for transfers between devices: 0.4 us -> 6.6 us  [local(): first = lax.ppermute(first, 'row', [(0, 1), (3, 2), (1, 3), (2, 0)])]
    ppermute x2, waiting for transfers between devices: 4.65 us -> 0.01 us  [trade_rows(): return lax.ppermute(value, ('row', 'col'), trades)]
    ppermute x2, starting transfers between devices: 4.75 us -> 2.61 us  [trade_rows(): return lax.ppermute(value, ('row', 'col'), trades)]
    ppermute x6, waiting for transfers between devices: 6.68 us -> 5.59 us  [total_by_core(): values[m] = lax.ppermute(value, ('row', 'col'), trades)]
    ppermute x17, starting transfers between devices: 13.6 us -> 14.5 us  [swap(): return lax.ppermute(value, axis, [(i, i ^ mask) for i in range(count)])]
  transfers between devices with their start and end apart: 26 -> 26, of which waited for: 18 -> 16; matrix products, arithmetic and copies ran while one was open for 0% -> 0% of each run, Pallas kernels for 18% -> 17%
where the time goes in v18:
time: 70 us; the launch traced here: 69.9 us
  starting transfers between devices  26.1 us (37%)
  waiting for transfers between devices  24.3 us (35%)
  Pallas kernels  16.1 us (23%)
  other arithmetic  1.8 us (3%)
  between operations  1.51 us (2%)
    ppermute x17, starting transfers between devices, swap(): return lax.ppermute(value, axis, [(i, i ^ mask) for i in range(count)])  14.5 us
    ppermute x17, waiting for transfers between devices, swap(): return lax.ppermute(value, axis, [(i, i ^ mask) for i in range(count)])  12.1 us
    ppermute x6, starting transfers between devices, total_by_core(): values[m] = lax.ppermute(value, ('row', 'col'), trades)  8 us
    ppermute x1, waiting for transfers between devices, local(): first = lax.ppermute(first, 'row', [(0, 1), (3, 2), (1, 3), (2, 0)])  6.6 us
    ppermute x6, waiting for transfers between devices, total_by_core(): values[m] = lax.ppermute(value, ('row', 'col'), trades)  5.59 us
    pallas_call x1, Pallas kernels, local(): pl.pallas_call(functools.partial(early_kernel, row_devs, col_devs, slab_t...  5.39 us
    ppermute x2, starting transfers between devices, trade_rows(): return lax.ppermute(value, ('row', 'col'), trades)  2.61 us
    pallas_call x1, Pallas kernels, local(): pl.pallas_call(functools.partial(first_late_kernel, [first_mask], odd), o...  2.37 us
  transfers between devices with their start and end apart: 26, of which 16 were waited for; matrix products, arithmetic and copies ran while one was open for 0% of the time, Pallas kernels for 17%

profile of v18, /device:TPU:0, one launch (start us, length us, event | category | flops | bytes accessed | tf_op | source)
XLA Modules:
  0.0 69.9 jit_solution(7294362421392500909)
XLA Ops:
  0.6 1.0 %convert_element_type.9.own_panel = bf16[48,2048]{1,0:T(8,128)(2,1)S(1)} convert(f32[48,2048]{1,0:T(8,128)} %current.7) | non-fusion elementwise | flops 98304 | bytes 589824 | tf_op jit(solution)/shard_map/gather/convert_element_type | solution.py:430
  1.7 0.5 collective-permute-start
  2.2 2.6 %collective-permute-start.1 = (bf16[48,2048]{1,0:T(8,128)(2,1)S(1)}, bf16[48,2048]{1,0:T(8,128)(2,1)S(1)}, u32[]{:S(2)}, u32[]{:S(2)}) collective-permute-start(bf16[48,2048]{1,0:T(8,128)(2,1)S(1)} %convert_element_type.9.own_panel), channel_id=1, source_target_pairs={{0,2},{1,3},{2,0},{3,1},{4,6},{5,7},{6,4},{7,5},{8,10},{9,11},{10,... | collective-permute-start | bytes 589832 | tf_op jit(solution)/shard_map/gather/ppermute | solution.py:21
  4.7 1.5 %collective-permute-start.3 = (bf16[48,2048]{1,0:T(8,128)(2,1)S(1)}, bf16[48,2048]{1,0:T(8,128)(2,1)S(1)}, u32[]{:S(2)}, u32[]{:S(2)}) collective-permute-start(bf16[48,2048]{1,0:T(8,128)(2,1)S(1)} %convert_element_type.9.own_panel), channel_id=1, source_target_pairs={{0,4},{1,5},{2,6},{3,7},{4,0},{5,1},{6,2},{7,3},{8,12},{9,13},{10,... | collective-permute-start | bytes 589832 | tf_op jit(solution)/shard_map/gather/ppermute | solution.py:21
  6.3 0.0 collective-permute-start.5
  6.9 0.1 pad_add_fusion.place
  7.0 0.0 collective-permute-done.near_panel
  7.0 5.4 %early.1 = (s32[1,896]{1,0:T(1,128)S(4)}, bf16[512,128,128]{2,1,0:T(8,128)(2,1)S(1)}, f32[65,48,128]{2,1,0:T(8,128)S(1)}, bf16[9,48,2048]{2,1,0:T(8,128)(2,1)S(1)}) custom-call(s32[2]{0:T(128)S(1)} %pad_add_fusion.place, s32[1]{0:T(128)S(6)} %copy.25.counts, s32[1,512]{1,0:T(1,128)} %bitcast.17, s32[1,512]{1,0:T(1,128)} %bitcast.18, ...), custom_call_target="tpu_custom_call" | custom-call | flops 805306368 | bytes 16777216 | tf_op jit(solution)/shard_map/early/pallas_call | solution.py:439
  12.4 0.0 collective-permute-done.1.refs_0_
  12.4 0.2 collective-permute-start.2
  12.7 3.3 %collective-permute-done.3.refs_0_ = bf16[48,2048]{1,0:T(8,128)(2,1)S(1)} collective-permute-done((bf16[48,2048]{1,0:T(8,128)(2,1)S(1)}, bf16[48,2048]{1,0:T(8,128)(2,1)S(1)}, u32[]{:S(2)}, u32[]{:S(2)}) %collective-permute-start.3) | collective-permute-done | bytes 196640 | tf_op jit(solution)/shard_map/gather/ppermute | solution.py:21
  15.9 0.0 collective-permute-start.4
  15.9 0.5 collective-permute-start.6
  16.4 0.8 %gather.7.refs_5_ = bf16[9,48,2048]{2,1,0:T(8,128)(2,1)S(1)} custom-call(bf16[48,2048]{1,0:T(8,128)(2,1)S(1)} %gather.4.refs_0_, bf16[48,2048]{1,0:T(8,128)(2,1)S(1)} %gather.5.refs_1_, bf16[48,2048]{1,0:T(8,128)(2,1)S(1)} %gather.6.refs_2_, bf16[9,48,2048]{2,1,0:T(8,128)(2,1)S(1)} %get-tuple-element.19.refs_3_), custom_call_target="tpu_custom_call", output_to_operand_aliasing={{}: (3, {})} | custom-call | flops 48 | bytes 1 | tf_op jit(solution)/shard_map/gather/pallas_call | solution.py:474
  17.2 0.2 collective-permute-done.4.refs_1_
  17.4 0.3 collective-permute-done.6.refs_2_
  17.6 2.4 %late.3 = (bf16[48,2048]{1,0:T(8,128)(2,1)S(1)}, bf16[9,48,2048]{2,1,0:T(8,128)(2,1)S(1)}) custom-call(s32[1,896]{1,0:T(1,128)S(4)} %get-tuple-element.16.plan, bf16[48,2048]{1,0:T(8,128)(2,1)S(1)} %collective-permute-done.2.refs_0_, bf16[48,2048]{1,0:T(8,128)(2,1)S(1)} %collective-permute-done.4.refs_1_, ...), custom_call_target="tpu_custom_call", output_to_operand_aliasing={{1}: (6, {})} | custom-call | flops 48 | bytes 1 | tf_op jit(solution)/shard_map/late/pallas_call | solution.py:490
  20.0 1.0 %collective-permute-start.7 = (bf16[48,2048]{1,0:T(8,128)(2,1)S(1)}, bf16[48,2048]{1,0:T(8,128)(2,1)S(1)}, u32[]{:S(2)}, u32[]{:S(2)}) collective-permute-start(bf16[48,2048]{1,0:T(8,128)(2,1)S(1)} %get-tuple-element.21), channel_id=1, source_target_pairs={{0,8},{24,16},{8,24},{16,0},{1,9},{25,17},{9,25},{17,1},{2,10},{26... | collective-permute-start | bytes 589832 | tf_op jit(solution)/shard_map/late/ppermute | solution.py:510
  21.0 2.0 %late.5 = (bf16[48,2048]{1,0:T(8,128)(2,1)S(1)}, f32[48,2048]{1,0:T(8,128)S(1)}, bf16[48,2048]{1,0:T(8,128)(2,1)S(1)}) custom-call(s32[1,896]{1,0:T(1,128)S(4)} %get-tuple-element.16.plan, bf16[9,48,2048]{2,1,0:T(8,128)(2,1)S(1)} %get-tuple-element.20.panel_buf, bf16[512,128,128]{2,1,0:T(8,128)(2,1)S(1)} %get-tuple-element.18.refs_3_.tiles, ...), custom_call_target="tpu_custom_call" | custom-call | flops 48 | bytes 1 | tf_op jit(solution)/shard_map/late/pallas_call | solution.py:500
  23.1 2.5 %collective-permute-start.8 = (bf16[48,2048]{1,0:T(8,128)(2,1)S(1)}, bf16[48,2048]{1,0:T(8,128)(2,1)S(1)}, u32[]{:S(2)}, u32[]{:S(2)}) collective-permute-start(bf16[48,2048]{1,0:T(8,128)(2,1)S(1)} %get-tuple-element.22), channel_id=1, source_target_pairs={{0,24},{1,25},{2,26},{3,27},{4,28},{5,29},{6,30},{7,31},{8,9},{9,8... | collective-permute-start | bytes 589832 | tf_op jit(solution)/shard_map/late/ppermute | solution.py:32
  25.6 0.8 %collective-permute-start.10 = (bf16[48,2048]{1,0:T(8,128)(2,1)S(1)}, bf16[48,2048]{1,0:T(8,128)(2,1)S(1)}, u32[]{:S(2)}, u32[]{:S(2)}) collective-permute-start(bf16[48,2048]{1,0:T(8,128)(2,1)S(1)} %get-tuple-element.24), channel_id=1, source_target_pairs={{0,8},{8,0},{16,24},{24,16},{1,9},{9,1},{17,25},{25,17},{2,10},{10... | collective-permute-start | bytes 589832 | tf_op jit(solution)/shard_map/late/ppermute | solution.py:21
  26.4 6.6 %collective-permute-done.7.refs_0_ = bf16[48,2048]{1,0:T(8,128)(2,1)S(1)} collective-permute-done((bf16[48,2048]{1,0:T(8,128)(2,1)S(1)}, bf16[48,2048]{1,0:T(8,128)(2,1)S(1)}, u32[]{:S(2)}, u32[]{:S(2)}) %collective-permute-start.7) | collective-permute-done | bytes 196640 | tf_op jit(solution)/shard_map/late/ppermute | solution.py:510
  33.0 0.1 collective-permute-start.9
  33.2 0.0 copy-start
  33.2 0.0 copy-start.3
  33.2 1.1 %late.4.base = f32[48,2048]{1,0:T(8,128)S(1)} custom-call(s32[1,896]{1,0:T(1,128)S(4)} %get-tuple-element.16.plan, bf16[9,48,2048]{2,1,0:T(8,128)(2,1)S(1)} %get-tuple-element.20.panel_buf, bf16[512,128,128]{2,1,0:T(8,128)(2,1)S(1)} %get-tuple-element.18.refs_3_.tiles, f32[65,48,128]{2,1,0:T(8,128)S(1)} %get-tuple-element.17.refs_1_.refs_4_.early, ...), custom_call_target="tpu_custom_call" | custom-call | flops 48 | bytes 1 | tf_op jit(solution)/shard_map/late/pallas_call | solution.py:521
  34.3 0.0 collective-permute-done.8.refs_1_
  34.3 2.7 %collective-permute-done.10.refs_3_ = bf16[48,2048]{1,0:T(8,128)(2,1)S(1)} collective-permute-done((bf16[48,2048]{1,0:T(8,128)(2,1)S(1)}, bf16[48,2048]{1,0:T(8,128)(2,1)S(1)}, u32[]{:S(2)}, u32[]{:S(2)}) %collective-permute-start.10) | collective-permute-done | bytes 196640 | tf_op jit(solution)/shard_map/late/ppermute | solution.py:21
  37.1 0.7 coefficients.2
  37.8 0.1 collective-permute-start.11
  37.8 0.7 %coefficients.3 = f32[12,8,128]{2,1,0:T(8,128)S(1)} custom-call(s32[1,896]{1,0:T(1,128)S(4)} %get-tuple-element.16.plan, f32[48,2048]{1,0:T(8,128)S(1)} %get-tuple-element.25.recurrence, f32[1,2048]{1,0:T(1,128)S(1)} %bitcast.13, f32[48,2048]{1,0:T(8,128)S(1)} %copy-done.1, f32[384,2048]{1,0:T(8,128)S(1)} %bitcast.9), custom_call_target="tpu_custom_call" | custom-call | flops 48 | bytes 1 | tf_op jit(solution)/shard_map/coefficients/pallas_call | solution.py:543
  38.6 0.5 collective-permute-done.11
  39.1 1.2 %collective-permute-start.14 = (f32[12,8,128]{2,1,0:T(8,128)S(1)}, f32[12,8,128]{2,1,0:T(8,128)S(1)}, u32[]{:S(2)}, u32[]{:S(2)}) collective-permute-start(f32[12,8,128]{2,1,0:T(8,128)S(1)} %add.46), channel_id=1, source_target_pairs={{0,6},{1,25},{2,4},{3,27},{4,2},{5,29},{6,0},{7,31},{8,14},{9,17},... | collective-permute-start | bytes 147464 | tf_op jit(solution)/shard_map/coefficients/ppermute | solution.py:59
  40.3 0.8 %collective-permute-start.13 = (f32[12,8,128]{2,1,0:T(8,128)S(1)}, f32[12,8,128]{2,1,0:T(8,128)S(1)}, u32[]{:S(2)}, u32[]{:S(2)}) collective-permute-start(f32[12,8,128]{2,1,0:T(8,128)S(1)} %add.46), channel_id=1, source_target_pairs={{0,4},{1,17},{2,6},{3,19},{4,0},{5,21},{6,2},{7,23},{8,12},{9,25},... | collective-permute-start | bytes 147464 | tf_op jit(solution)/shard_map/coefficients/ppermute | solution.py:59
  41.1 1.5 %collective-permute-start.12 = (f32[12,8,128]{2,1,0:T(8,128)S(1)}, f32[12,8,128]{2,1,0:T(8,128)S(1)}, u32[]{:S(2)}, u32[]{:S(2)}) collective-permute-start(f32[12,8,128]{2,1,0:T(8,128)S(1)} %add.46), channel_id=1, source_target_pairs={{0,2},{1,9},{2,0},{3,11},{4,6},{5,13},{6,4},{7,15},{8,10},{9,1},{1... | collective-permute-start | bytes 147464 | tf_op jit(solution)/shard_map/coefficients/ppermute | solution.py:59
  42.6 1.5 %collective-permute-done.14 = f32[12,8,128]{2,1,0:T(8,128)S(1)} collective-permute-done((f32[12,8,128]{2,1,0:T(8,128)S(1)}, f32[12,8,128]{2,1,0:T(8,128)S(1)}, u32[]{:S(2)}, u32[]{:S(2)}) %collective-permute-start.14) | collective-permute-done | bytes 49184 | tf_op jit(solution)/shard_map/coefficients/ppermute | solution.py:59
  44.1 0.5 collective-permute-done.13
  44.6 0.6 collective-permute-done.12
  45.2 2.4 %collective-permute-start.17 = (f32[12,8,128]{2,1,0:T(8,128)S(1)}, f32[12,8,128]{2,1,0:T(8,128)S(1)}, u32[]{:S(2)}, u32[]{:S(2)}) collective-permute-start(f32[12,8,128]{2,1,0:T(8,128)S(1)} %add_add_fusion.1), channel_id=1, source_target_pairs={{0,24},{1,7},{2,26},{3,5},{4,28},{5,3},{6,30},{7,1},{8,16},{9,15},... | collective-permute-start | bytes 147464 | tf_op jit(solution)/shard_map/coefficients/ppermute | solution.py:59
  47.7 0.0 collective-permute-start.16
  47.7 2.0 %collective-permute-start.15 = (f32[12,8,128]{2,1,0:T(8,128)S(1)}, f32[12,8,128]{2,1,0:T(8,128)S(1)}, u32[]{:S(2)}, u32[]{:S(2)}) collective-permute-start(f32[12,8,128]{2,1,0:T(8,128)S(1)} %add_add_fusion.1), channel_id=1, source_target_pairs={{0,8},{1,3},{2,10},{3,1},{4,12},{5,7},{6,14},{7,5},{8,0},{9,11},{1... | collective-permute-start | bytes 147464 | tf_op jit(solution)/shard_map/coefficients/ppermute | solution.py:59
  49.7 1.5 %collective-permute-done.17 = f32[12,8,128]{2,1,0:T(8,128)S(1)} collective-permute-done((f32[12,8,128]{2,1,0:T(8,128)S(1)}, f32[12,8,128]{2,1,0:T(8,128)S(1)}, u32[]{:S(2)}, u32[]{:S(2)}) %collective-permute-start.17) | collective-permute-done | bytes 49184 | tf_op jit(solution)/shard_map/coefficients/ppermute | solution.py:59
  51.2 1.5 %collective-permute-done.16 = f32[12,8,128]{2,1,0:T(8,128)S(1)} collective-permute-done((f32[12,8,128]{2,1,0:T(8,128)S(1)}, f32[12,8,128]{2,1,0:T(8,128)S(1)}, u32[]{:S(2)}, u32[]{:S(2)}) %collective-permute-start.16) | collective-permute-done | bytes 49184 | tf_op jit(solution)/shard_map/coefficients/ppermute | solution.py:59
  52.7 0.1 collective-permute-start.18
  52.8 0.6 residual.4.less
  53.4 0.6 collective-permute-done.18.other
  54.0 0.9 %residual.5 = (f32[48,2048]{1,0:T(8,128)S(1)}, f32[24,128]{1,0:T(8,128)S(1)}) custom-call(s32[1,896]{1,0:T(1,128)S(4)} %get-tuple-element.16.plan, f32[12,8,128]{2,1,0:T(8,128)S(1)} %collective-permute-done.18.other, f32[48,2048]{1,0:T(8,128)S(1)} %residual.4.less, f32[1,2048]{1,0:T(1,128)S(1)} %bitcast.14, f32[48,2048]{1,0:T(8,128)S(1)} %copy-done.1, ...), custom_call_target="tpu_custom_call" | custom-call | flops 48 | bytes 1 | tf_op jit(solution)/shard_map/residual/pallas_call | solution.py:564
  54.9 0.2 collective-permute-start.19
  55.1 1.0 %collective-permute-done.19 = f32[24,128]{1,0:T(8,128)S(1)} collective-permute-done((f32[24,128]{1,0:T(8,128)S(1)}, f32[24,128]{1,0:T(8,128)S(1)}, u32[]{:S(2)}, u32[]{:S(2)}) %collective-permute-start.19) | collective-permute-done | bytes 12320 | tf_op jit(solution)/shard_map/gram/ppermute | solution.py:21
  56.1 2.6 %collective-permute-start.22 = (f32[24,128]{1,0:T(8,128)S(1)}, f32[24,128]{1,0:T(8,128)S(1)}, u32[]{:S(2)}, u32[]{:S(2)}) collective-permute-start(f32[24,128]{1,0:T(8,128)S(1)} %add.53), channel_id=1, source_target_pairs={{0,6},{1,7},{2,4},{3,5},{4,2},{5,3},{6,0},{7,1},{8,14},{9,15},{10,... | collective-permute-start | bytes 36872 | tf_op jit(solution)/shard_map/gram/ppermute | solution.py:21
  58.8 0.0 collective-permute-start.21
  58.8 0.8 %collective-permute-start.20 = (f32[24,128]{1,0:T(8,128)S(1)}, f32[24,128]{1,0:T(8,128)S(1)}, u32[]{:S(2)}, u32[]{:S(2)}) collective-permute-start(f32[24,128]{1,0:T(8,128)S(1)} %add.53), channel_id=1, source_target_pairs={{0,2},{1,3},{2,0},{3,1},{4,6},{5,7},{6,4},{7,5},{8,10},{9,11},{10,... | collective-permute-start | bytes 36872 | tf_op jit(solution)/shard_map/gram/ppermute | solution.py:21
  59.6 0.8 %residual.6.refs_1_ = f32[48,2048]{1,0:T(8,128)} custom-call(f32[48,2048]{1,0:T(8,128)S(1)} %get-tuple-element.27.value), custom_call_target="tpu_custom_call" | custom-call | flops 48 | bytes 1 | tf_op jit(solution)/shard_map/residual/pallas_call | solution.py:575
  60.4 0.8 %residual.7.refs_2_ = f32[432,48]{1,0:T(8,128)} custom-call(s32[1,896]{1,0:T(1,128)S(4)} %get-tuple-element.16.plan, f32[12,8,128]{2,1,0:T(8,128)S(1)} %add_add_fusion.mine, f32[12,8,128]{2,1,0:T(8,128)S(1)} %collective-permute-done.18.other), custom_call_target="tpu_custom_call" | custom-call | flops 48 | bytes 1 | tf_op jit(solution)/shard_map/residual/pallas_call | solution.py:584
  61.2 1.3 %collective-permute-done.21 = f32[24,128]{1,0:T(8,128)S(1)} collective-permute-done((f32[24,128]{1,0:T(8,128)S(1)}, f32[24,128]{1,0:T(8,128)S(1)}, u32[]{:S(2)}, u32[]{:S(2)}) %collective-permute-start.21) | collective-permute-done | bytes 12320 | tf_op jit(solution)/shard_map/gram/ppermute | solution.py:21
  62.5 0.0 collective-permute-done.20
  62.5 2.0 %collective-permute-start.25 = (f32[24,128]{1,0:T(8,128)S(1)}, f32[24,128]{1,0:T(8,128)S(1)}, u32[]{:S(2)}, u32[]{:S(2)}) collective-permute-start(f32[24,128]{1,0:T(8,128)S(1)} %gram.1), channel_id=1, source_target_pairs={{0,24},{8,16},{16,8},{24,0},{1,25},{9,17},{17,9},{25,1},{2,26},{10... | collective-permute-start | bytes 36872 | tf_op jit(solution)/shard_map/gram/ppermute | solution.py:21
  64.5 0.8 %collective-permute-start.24 = (f32[24,128]{1,0:T(8,128)S(1)}, f32[24,128]{1,0:T(8,128)S(1)}, u32[]{:S(2)}, u32[]{:S(2)}) collective-permute-start(f32[24,128]{1,0:T(8,128)S(1)} %gram.1), channel_id=1, source_target_pairs={{0,16},{8,24},{16,0},{24,8},{1,17},{9,25},{17,1},{25,9},{2,18},{10... | collective-permute-start | bytes 36872 | tf_op jit(solution)/shard_map/gram/ppermute | solution.py:21
  65.3 1.6 %collective-permute-start.23 = (f32[24,128]{1,0:T(8,128)S(1)}, f32[24,128]{1,0:T(8,128)S(1)}, u32[]{:S(2)}, u32[]{:S(2)}) collective-permute-start(f32[24,128]{1,0:T(8,128)S(1)} %gram.1), channel_id=1, source_target_pairs={{0,8},{8,0},{16,24},{24,16},{1,9},{9,1},{17,25},{25,17},{2,10},{10... | collective-permute-start | bytes 36872 | tf_op jit(solution)/shard_map/gram/ppermute | solution.py:21
  66.9 1.1 %collective-permute-done.25 = f32[24,128]{1,0:T(8,128)S(1)} collective-permute-done((f32[24,128]{1,0:T(8,128)S(1)}, f32[24,128]{1,0:T(8,128)S(1)}, u32[]{:S(2)}, u32[]{:S(2)}) %collective-permute-start.25) | collective-permute-done | bytes 12320 | tf_op jit(solution)/shard_map/gram/ppermute | solution.py:21
  68.0 1.1 %collective-permute-done.24 = f32[24,128]{1,0:T(8,128)S(1)} collective-permute-done((f32[24,128]{1,0:T(8,128)S(1)}, f32[24,128]{1,0:T(8,128)S(1)}, u32[]{:S(2)}, u32[]{:S(2)}) %collective-permute-start.24) | collective-permute-done | bytes 12320 | tf_op jit(solution)/shard_map/gram/ppermute | solution.py:21
  69.2 0.0 collective-permute-done.23
  69.2 0.1 fusion
  69.3 0.6 pad_maximum_fusion
  (26 shorter events, 0.1 us)
Async XLA Ops:
  1.7 5.4 %collective-permute-start = (bf16[48,2048]{1,0:T(8,128)(2,1)S(1)}, bf16[48,2048]{1,0:T(8,128)(2,1)S(1)}, u32[]{:S(2)}, u32[]{:S(2)}) collective-permute-start(bf16[48,2048]{1,0:T(8,128)(2,1)S(1)} %convert_element_type.9.own_panel), channel_id=1, source_target_pairs={{0,1},{1,0},{2,3},{3,2},{4,5},{5,4},{6,7},{7,6},{8,9},{9,8},{10,11... | collective-permute-start | bytes 589832 | tf_op jit(solution)/shard_map/gather/ppermute | solution.py:21
  2.2 10.2 %collective-permute-start.1 = (bf16[48,2048]{1,0:T(8,128)(2,1)S(1)}, bf16[48,2048]{1,0:T(8,128)(2,1)S(1)}, u32[]{:S(2)}, u32[]{:S(2)}) collective-permute-start(bf16[48,2048]{1,0:T(8,128)(2,1)S(1)} %convert_element_type.9.own_panel), channel_id=1, source_target_pairs={{0,2},{1,3},{2,0},{3,1},{4,6},{5,7},{6,4},{7,5},{8,10},{9,11},{10,... | collective-permute-start | bytes 589832 | tf_op jit(solution)/shard_map/gather/ppermute | solution.py:21
  4.7 11.2 %collective-permute-start.3 = (bf16[48,2048]{1,0:T(8,128)(2,1)S(1)}, bf16[48,2048]{1,0:T(8,128)(2,1)S(1)}, u32[]{:S(2)}, u32[]{:S(2)}) collective-permute-start(bf16[48,2048]{1,0:T(8,128)(2,1)S(1)} %convert_element_type.9.own_panel), channel_id=1, source_target_pairs={{0,4},{1,5},{2,6},{3,7},{4,0},{5,1},{6,2},{7,3},{8,12},{9,13},{10,... | collective-permute-start | bytes 589832 | tf_op jit(solution)/shard_map/gather/ppermute | solution.py:21
  6.3 9.7 %collective-permute-start.5 = (bf16[48,2048]{1,0:T(8,128)(2,1)S(1)}, bf16[48,2048]{1,0:T(8,128)(2,1)S(1)}, u32[]{:S(2)}, u32[]{:S(2)}) collective-permute-start(bf16[48,2048]{1,0:T(8,128)(2,1)S(1)} %convert_element_type.9.own_panel), channel_id=1, source_target_pairs={{0,6},{1,7},{2,4},{3,5},{4,2},{5,3},{6,0},{7,1},{8,14},{9,15},{10,... | collective-permute-start | bytes 589832 | tf_op jit(solution)/shard_map/gather/ppermute | solution.py:21
  12.4 4.8 %collective-permute-start.2 = (bf16[48,2048]{1,0:T(8,128)(2,1)S(1)}, bf16[48,2048]{1,0:T(8,128)(2,1)S(1)}, u32[]{:S(2)}, u32[]{:S(2)}) collective-permute-start(bf16[48,2048]{1,0:T(8,128)(2,1)S(1)} %gather.4.refs_0_), channel_id=1, source_target_pairs={{0,1},{1,0},{2,3},{3,2},{4,5},{5,4},{6,7},{7,6},{8,9},{9,8},{10,11... | collective-permute-start | bytes 589832 | tf_op jit(solution)/shard_map/gather/ppermute | solution.py:21
  15.9 1.4 %collective-permute-start.4 = (bf16[48,2048]{1,0:T(8,128)(2,1)S(1)}, bf16[48,2048]{1,0:T(8,128)(2,1)S(1)}, u32[]{:S(2)}, u32[]{:S(2)}) collective-permute-start(bf16[48,2048]{1,0:T(8,128)(2,1)S(1)} %gather.5.refs_1_), channel_id=1, source_target_pairs={{0,1},{1,0},{2,3},{3,2},{4,5},{5,4},{6,7},{7,6},{8,9},{9,8},{10,11... | collective-permute-start | bytes 589832 | tf_op jit(solution)/shard_map/gather/ppermute | solution.py:21
  15.9 1.7 %collective-permute-start.6 = (bf16[48,2048]{1,0:T(8,128)(2,1)S(1)}, bf16[48,2048]{1,0:T(8,128)(2,1)S(1)}, u32[]{:S(2)}, u32[]{:S(2)}) collective-permute-start(bf16[48,2048]{1,0:T(8,128)(2,1)S(1)} %gather.6.refs_2_), channel_id=1, source_target_pairs={{0,1},{1,0},{2,3},{3,2},{4,5},{5,4},{6,7},{7,6},{8,9},{9,8},{10,11... | collective-permute-start | bytes 589832 | tf_op jit(solution)/shard_map/gather/ppermute | solution.py:21
  20.0 13.0 %collective-permute-start.7 = (bf16[48,2048]{1,0:T(8,128)(2,1)S(1)}, bf16[48,2048]{1,0:T(8,128)(2,1)S(1)}, u32[]{:S(2)}, u32[]{:S(2)}) collective-permute-start(bf16[48,2048]{1,0:T(8,128)(2,1)S(1)} %get-tuple-element.21), channel_id=1, source_target_pairs={{0,8},{24,16},{8,24},{16,0},{1,9},{25,17},{9,25},{17,1},{2,10},{26... | collective-permute-start | bytes 589832 | tf_op jit(solution)/shard_map/late/ppermute | solution.py:510
  21.0 12.1 %copy-start.1 = (f32[48,2048]{1,0:T(8,128)S(1)}, f32[48,2048]{1,0:T(8,128)}, u32[]{:S(2)}) copy-start(f32[48,2048]{1,0:T(8,128)} %current.7) | copy-start | bytes 1179652
  21.0 12.1 %copy-start.2 = (f32[48,2048]{1,0:T(8,128)S(1)}, f32[48,2048]{1,0:T(8,128)}, u32[]{:S(2)}) copy-start(f32[48,2048]{1,0:T(8,128)} %previous.1) | copy-start | bytes 1179652
  21.0 12.1 %copy-start.4 = (f32[48,48]{1,0:T(8,128)S(1)}, f32[48,48]{1,0:T(8,128)}, u32[]{:S(2)}) copy-start(f32[48,48]{1,0:T(8,128)} %coupling.1) | copy-start | bytes 27652
  21.0 12.1 %copy-start.5 = (f32[2048]{0:T(1024)S(1)}, f32[2048]{0:T(1024)}, u32[]{:S(2)}) copy-start(f32[2048]{0:T(1024)} %param.14) | copy-start | bytes 24580
  23.1 11.3 %collective-permute-start.8 = (bf16[48,2048]{1,0:T(8,128)(2,1)S(1)}, bf16[48,2048]{1,0:T(8,128)(2,1)S(1)}, u32[]{:S(2)}, u32[]{:S(2)}) collective-permute-start(bf16[48,2048]{1,0:T(8,128)(2,1)S(1)} %get-tuple-element.22), channel_id=1, source_target_pairs={{0,24},{1,25},{2,26},{3,27},{4,28},{5,29},{6,30},{7,31},{8,9},{9,8... | collective-permute-start | bytes 589832 | tf_op jit(solution)/shard_map/late/ppermute | solution.py:32
  25.6 11.5 %collective-permute-start.10 = (bf16[48,2048]{1,0:T(8,128)(2,1)S(1)}, bf16[48,2048]{1,0:T(8,128)(2,1)S(1)}, u32[]{:S(2)}, u32[]{:S(2)}) collective-permute-start(bf16[48,2048]{1,0:T(8,128)(2,1)S(1)} %get-tuple-element.24), channel_id=1, source_target_pairs={{0,8},{8,0},{16,24},{24,16},{1,9},{9,1},{17,25},{25,17},{2,10},{10... | collective-permute-start | bytes 589832 | tf_op jit(solution)/shard_map/late/ppermute | solution.py:21
  33.0 4.0 %collective-permute-start.9 = (bf16[48,2048]{1,0:T(8,128)(2,1)S(1)}, bf16[48,2048]{1,0:T(8,128)(2,1)S(1)}, u32[]{:S(2)}, u32[]{:S(2)}) collective-permute-start(bf16[48,2048]{1,0:T(8,128)(2,1)S(1)} %add_convert_fusion), channel_id=1, source_target_pairs={{0,1},{1,0},{2,3},{3,2},{4,5},{5,4},{6,7},{7,6},{8,16},{9,17},{10,... | collective-permute-start | bytes 589832 | tf_op jit(solution)/shard_map/late/ppermute | solution.py:32
  33.2 3.9 %copy-start = (f32[8,48,2048]{2,1,0:T(8,128)S(1)}, f32[8,48,2048]{2,1,0:T(8,128)}, u32[]{:S(2)}) copy-start(f32[8,48,2048]{2,1,0:T(8,128)} %param.13) | copy-start | bytes 9437188
  33.2 3.9 %copy-start.3 = (f32[2048]{0:T(1024)S(1)}, f32[2048]{0:T(1024)}, u32[]{:S(2)}) copy-start(f32[2048]{0:T(1024)} %param.15) | copy-start | bytes 24580
  37.8 1.3 %collective-permute-start.11 = (f32[12,8,128]{2,1,0:T(8,128)S(1)}, f32[12,8,128]{2,1,0:T(8,128)S(1)}, u32[]{:S(2)}, u32[]{:S(2)}) collective-permute-start(f32[12,8,128]{2,1,0:T(8,128)S(1)} %get-tuple-element.26), channel_id=1, source_target_pairs={{0,1},{1,0},{2,3},{3,2},{4,5},{5,4},{6,7},{7,6},{8,9},{9,8},{10,11... | collective-permute-start | bytes 147464 | tf_op jit(solution)/shard_map/coefficients/ppermute | solution.py:21
  39.1 5.1 %collective-permute-start.14 = (f32[12,8,128]{2,1,0:T(8,128)S(1)}, f32[12,8,128]{2,1,0:T(8,128)S(1)}, u32[]{:S(2)}, u32[]{:S(2)}) collective-permute-start(f32[12,8,128]{2,1,0:T(8,128)S(1)} %add.46), channel_id=1, source_target_pairs={{0,6},{1,25},{2,4},{3,27},{4,2},{5,29},{6,0},{7,31},{8,14},{9,17},... | collective-permute-start | bytes 147464 | tf_op jit(solution)/shard_map/coefficients/ppermute | solution.py:59
  40.3 4.3 %collective-permute-start.13 = (f32[12,8,128]{2,1,0:T(8,128)S(1)}, f32[12,8,128]{2,1,0:T(8,128)S(1)}, u32[]{:S(2)}, u32[]{:S(2)}) collective-permute-start(f32[12,8,128]{2,1,0:T(8,128)S(1)} %add.46), channel_id=1, source_target_pairs={{0,4},{1,17},{2,6},{3,19},{4,0},{5,21},{6,2},{7,23},{8,12},{9,25},... | collective-permute-start | bytes 147464 | tf_op jit(solution)/shard_map/coefficients/ppermute | solution.py:59
  41.1 4.1 %collective-permute-start.12 = (f32[12,8,128]{2,1,0:T(8,128)S(1)}, f32[12,8,128]{2,1,0:T(8,128)S(1)}, u32[]{:S(2)}, u32[]{:S(2)}) collective-permute-start(f32[12,8,128]{2,1,0:T(8,128)S(1)} %add.46), channel_id=1, source_target_pairs={{0,2},{1,9},{2,0},{3,11},{4,6},{5,13},{6,4},{7,15},{8,10},{9,1},{1... | collective-permute-start | bytes 147464 | tf_op jit(solution)/shard_map/coefficients/ppermute | solution.py:59
  45.2 6.0 %collective-permute-start.17 = (f32[12,8,128]{2,1,0:T(8,128)S(1)}, f32[12,8,128]{2,1,0:T(8,128)S(1)}, u32[]{:S(2)}, u32[]{:S(2)}) collective-permute-start(f32[12,8,128]{2,1,0:T(8,128)S(1)} %add_add_fusion.1), channel_id=1, source_target_pairs={{0,24},{1,7},{2,26},{3,5},{4,28},{5,3},{6,30},{7,1},{8,16},{9,15},... | collective-permute-start | bytes 147464 | tf_op jit(solution)/shard_map/coefficients/ppermute | solution.py:59
  47.7 5.0 %collective-permute-start.16 = (f32[12,8,128]{2,1,0:T(8,128)S(1)}, f32[12,8,128]{2,1,0:T(8,128)S(1)}, u32[]{:S(2)}, u32[]{:S(2)}) collective-permute-start(f32[12,8,128]{2,1,0:T(8,128)S(1)} %add_add_fusion.1), channel_id=1, source_target_pairs={{0,16},{1,5},{2,18},{3,7},{4,20},{5,1},{6,22},{7,3},{8,24},{9,13},... | collective-permute-start | bytes 147464 | tf_op jit(solution)/shard_map/coefficients/ppermute | solution.py:59
  47.7 5.0 %collective-permute-start.15 = (f32[12,8,128]{2,1,0:T(8,128)S(1)}, f32[12,8,128]{2,1,0:T(8,128)S(1)}, u32[]{:S(2)}, u32[]{:S(2)}) collective-permute-start(f32[12,8,128]{2,1,0:T(8,128)S(1)} %add_add_fusion.1), channel_id=1, source_target_pairs={{0,8},{1,3},{2,10},{3,1},{4,12},{5,7},{6,14},{7,5},{8,0},{9,11},{1... | collective-permute-start | bytes 147464 | tf_op jit(solution)/shard_map/coefficients/ppermute | solution.py:59
  52.7 1.3 %collective-permute-start.18 = (f32[12,8,128]{2,1,0:T(8,128)S(1)}, f32[12,8,128]{2,1,0:T(8,128)S(1)}, u32[]{:S(2)}, u32[]{:S(2)}) collective-permute-start(f32[12,8,128]{2,1,0:T(8,128)S(1)} %add_add_fusion.mine), channel_id=1, source_target_pairs={{0,1},{1,0},{2,3},{3,2},{4,5},{5,4},{6,7},{7,6},{8,9},{9,8},{10,11... | collective-permute-start | bytes 147464 | tf_op jit(solution)/shard_map/coefficients/ppermute | solution.py:21
  54.9 1.2 %collective-permute-start.19 = (f32[24,128]{1,0:T(8,128)S(1)}, f32[24,128]{1,0:T(8,128)S(1)}, u32[]{:S(2)}, u32[]{:S(2)}) collective-permute-start(f32[24,128]{1,0:T(8,128)S(1)} %get-tuple-element.28), channel_id=1, source_target_pairs={{0,1},{1,0},{2,3},{3,2},{4,5},{5,4},{6,7},{7,6},{8,9},{9,8},{10,11... | collective-permute-start | bytes 36872 | tf_op jit(solution)/shard_map/gram/ppermute | solution.py:21
  56.1 5.1 %collective-permute-start.22 = (f32[24,128]{1,0:T(8,128)S(1)}, f32[24,128]{1,0:T(8,128)S(1)}, u32[]{:S(2)}, u32[]{:S(2)}) collective-permute-start(f32[24,128]{1,0:T(8,128)S(1)} %add.53), channel_id=1, source_target_pairs={{0,6},{1,7},{2,4},{3,5},{4,2},{5,3},{6,0},{7,1},{8,14},{9,15},{10,... | collective-permute-start | bytes 36872 | tf_op jit(solution)/shard_map/gram/ppermute | solution.py:21
  58.8 3.7 %collective-permute-start.21 = (f32[24,128]{1,0:T(8,128)S(1)}, f32[24,128]{1,0:T(8,128)S(1)}, u32[]{:S(2)}, u32[]{:S(2)}) collective-permute-start(f32[24,128]{1,0:T(8,128)S(1)} %add.53), channel_id=1, source_target_pairs={{0,4},{1,5},{2,6},{3,7},{4,0},{5,1},{6,2},{7,3},{8,12},{9,13},{10,... | collective-permute-start | bytes 36872 | tf_op jit(solution)/shard_map/gram/ppermute | solution.py:21
  58.8 3.7 %collective-permute-start.20 = (f32[24,128]{1,0:T(8,128)S(1)}, f32[24,128]{1,0:T(8,128)S(1)}, u32[]{:S(2)}, u32[]{:S(2)}) collective-permute-start(f32[24,128]{1,0:T(8,128)S(1)} %add.53), channel_id=1, source_target_pairs={{0,2},{1,3},{2,0},{3,1},{4,6},{5,7},{6,4},{7,5},{8,10},{9,11},{10,... | collective-permute-start | bytes 36872 | tf_op jit(solution)/shard_map/gram/ppermute | solution.py:21
  62.5 5.6 %collective-permute-start.25 = (f32[24,128]{1,0:T(8,128)S(1)}, f32[24,128]{1,0:T(8,128)S(1)}, u32[]{:S(2)}, u32[]{:S(2)}) collective-permute-start(f32[24,128]{1,0:T(8,128)S(1)} %gram.1), channel_id=1, source_target_pairs={{0,24},{8,16},{16,8},{24,0},{1,25},{9,17},{17,9},{25,1},{2,26},{10... | collective-permute-start | bytes 36872 | tf_op jit(solution)/shard_map/gram/ppermute | solution.py:21
  64.5 4.7 %collective-permute-start.24 = (f32[24,128]{1,0:T(8,128)S(1)}, f32[24,128]{1,0:T(8,128)S(1)}, u32[]{:S(2)}, u32[]{:S(2)}) collective-permute-start(f32[24,128]{1,0:T(8,128)S(1)} %gram.1), channel_id=1, source_target_pairs={{0,16},{8,24},{16,0},{24,8},{1,17},{9,25},{17,1},{25,9},{2,18},{10... | collective-permute-start | bytes 36872 | tf_op jit(solution)/shard_map/gram/ppermute | solution.py:21
  65.3 3.8 %collective-permute-start.23 = (f32[24,128]{1,0:T(8,128)S(1)}, f32[24,128]{1,0:T(8,128)S(1)}, u32[]{:S(2)}, u32[]{:S(2)}) collective-permute-start(f32[24,128]{1,0:T(8,128)S(1)} %gram.1), channel_id=1, source_target_pairs={{0,8},{8,0},{16,24},{24,16},{1,9},{9,1},{17,25},{25,17},{2,10},{10... | collective-permute-start | bytes 36872 | tf_op jit(solution)/shard_map/gram/ppermute | solution.py:21

commit v19 on v18

--- a/solution.py
+++ b/solution.py
@@ -513,7 +513,7 @@
                 first,
                 trade_rows(parts[0], [(0, 3), (3, 0)]),
                 trade_rows(joined, [(1, 2), (2, 1)]),
-                swap(parts[2], "row", 1),
+                swap(after(parts[2], joined), "row", 1),
             ]
         else:
             received = [swap(first, "row", first_mask)]

time: 70 us -> 72.2 us (1.031); the launches traced: 69.9 us -> 73.4 us
  starting transfers between devices: 26.1 us -> 34.5 us
  waiting for transfers between devices: 24.3 us -> 21 us
  Pallas kernels: 16.1 us -> 14.6 us
    ppermute x17, starting transfers between devices: 14.5 us -> 19.8 us  [swap(): return lax.ppermute(value, axis, [(i, i ^ mask) for i in range(count)])]
    ppermute x1, waiting for transfers between devices: 6.6 us -> 1.29 us  [local(): first = lax.ppermute(first, 'row', [(0, 1), (3, 2), (1, 3), (2, 0)])]
    ppermute x6, starting transfers between devices: 8 us -> 10.2 us  [total_by_core(): values[m] = lax.ppermute(value, ('row', 'col'), trades)]
    ppermute x6, waiting for transfers between devices: 5.59 us -> 6.83 us  [total_by_core(): values[m] = lax.ppermute(value, ('row', 'col'), trades)]
    pallas_call x1, Pallas kernels: 5.39 us -> 4.15 us  [local(): pl.pallas_call(functools.partial(early_kernel, row_devs, col_devs, slab_t...]
    ppermute x17, waiting for transfers between devices: 12.1 us -> 12.8 us  [swap(): return lax.ppermute(value, axis, [(i, i ^ mask) for i in range(count)])]
  transfers between devices with their start and end apart: 26 -> 26, of which waited for: 16 -> 17; matrix products, arithmetic and copies ran while one was open for 0% -> 0% of each run, Pallas kernels for 17% -> 15%
where the time goes in v19:
time: 72.2 us; the launch traced here: 73.4 us
  starting transfers between devices  34.5 us (48%)
  waiting for transfers between devices  21 us (29%)
  Pallas kernels  14.6 us (20%)
  other arithmetic  1.8 us (2%)
  between operations  1.51 us (2%)
    ppermute x17, starting transfers between devices, swap(): return lax.ppermute(value, axis, [(i, i ^ mask) for i in range(count)])  19.8 us
    ppermute x17, waiting for transfers between devices, swap(): return lax.ppermute(value, axis, [(i, i ^ mask) for i in range(count)])  12.8 us
    ppermute x6, starting transfers between devices, total_by_core(): values[m] = lax.ppermute(value, ('row', 'col'), trades)  10.2 us
    ppermute x6, waiting for transfers between devices, total_by_core(): values[m] = lax.ppermute(value, ('row', 'col'), trades)  6.83 us
    pallas_call x1, Pallas kernels, local(): pl.pallas_call(functools.partial(early_kernel, row_devs, col_devs, slab_t...  4.15 us
    ppermute x2, starting transfers between devices, trade_rows(): return lax.ppermute(value, ('row', 'col'), trades)  3.05 us
    pallas_call x1, Pallas kernels, local(): pl.pallas_call(functools.partial(late_kernel, masks), out_shape=[part, sl...  2.31 us
    pallas_call x1, Pallas kernels, local(): pl.pallas_call(functools.partial(first_late_kernel, [first_mask], odd), o...  1.75 us
  transfers between devices with their start and end apart: 26, of which 17 were waited for; matrix products, arithmetic and copies ran while one was open for 0% of the time, Pallas kernels for 15%

profile of v19, /device:TPU:0, one launch (start us, length us, event | category | flops | bytes accessed | tf_op | source)
XLA Modules:
  0.0 73.4 jit_solution(206919161138993341)
XLA Ops:
  0.6 1.0 %convert_element_type.9.own_panel = bf16[48,2048]{1,0:T(8,128)(2,1)S(1)} convert(f32[48,2048]{1,0:T(8,128)} %current.7) | non-fusion elementwise | flops 98304 | bytes 589824 | tf_op jit(solution)/shard_map/gather/convert_element_type | solution.py:430
  1.7 0.5 collective-permute-start
  2.2 2.6 %collective-permute-start.1 = (bf16[48,2048]{1,0:T(8,128)(2,1)S(1)}, bf16[48,2048]{1,0:T(8,128)(2,1)S(1)}, u32[]{:S(2)}, u32[]{:S(2)}) collective-permute-start(bf16[48,2048]{1,0:T(8,128)(2,1)S(1)} %convert_element_type.9.own_panel), channel_id=1, source_target_pairs={{0,2},{1,3},{2,0},{3,1},{4,6},{5,7},{6,4},{7,5},{8,10},{9,11},{10,... | collective-permute-start | bytes 589832 | tf_op jit(solution)/shard_map/gather/ppermute | solution.py:21
  4.7 1.5 %collective-permute-start.3 = (bf16[48,2048]{1,0:T(8,128)(2,1)S(1)}, bf16[48,2048]{1,0:T(8,128)(2,1)S(1)}, u32[]{:S(2)}, u32[]{:S(2)}) collective-permute-start(bf16[48,2048]{1,0:T(8,128)(2,1)S(1)} %convert_element_type.9.own_panel), channel_id=1, source_target_pairs={{0,4},{1,5},{2,6},{3,7},{4,0},{5,1},{6,2},{7,3},{8,12},{9,13},{10,... | collective-permute-start | bytes 589832 | tf_op jit(solution)/shard_map/gather/ppermute | solution.py:21
  6.3 0.0 collective-permute-start.5
  6.9 0.1 pad_add_fusion.place
  7.0 0.0 collective-permute-done.near_panel
  7.0 4.2 %early.1 = (s32[1,896]{1,0:T(1,128)S(4)}, bf16[512,128,128]{2,1,0:T(8,128)(2,1)S(1)}, f32[65,48,128]{2,1,0:T(8,128)S(1)}, bf16[9,48,2048]{2,1,0:T(8,128)(2,1)S(1)}) custom-call(s32[2]{0:T(128)S(1)} %pad_add_fusion.place, s32[1]{0:T(128)S(6)} %copy.27.counts, s32[1,512]{1,0:T(1,128)} %bitcast.17, s32[1,512]{1,0:T(1,128)} %bitcast.18, ...), custom_call_target="tpu_custom_call" | custom-call | flops 805306368 | bytes 16777216 | tf_op jit(solution)/shard_map/early/pallas_call | solution.py:439
  11.2 0.0 collective-permute-done.1.refs_0_
  11.2 1.5 %collective-permute-start.2 = (bf16[48,2048]{1,0:T(8,128)(2,1)S(1)}, bf16[48,2048]{1,0:T(8,128)(2,1)S(1)}, u32[]{:S(2)}, u32[]{:S(2)}) collective-permute-start(bf16[48,2048]{1,0:T(8,128)(2,1)S(1)} %gather.4.refs_0_), channel_id=1, source_target_pairs={{0,1},{1,0},{2,3},{3,2},{4,5},{5,4},{6,7},{7,6},{8,9},{9,8},{10,11... | collective-permute-start | bytes 589832 | tf_op jit(solution)/shard_map/gather/ppermute | solution.py:21
  12.6 3.3 %collective-permute-done.3.refs_0_ = bf16[48,2048]{1,0:T(8,128)(2,1)S(1)} collective-permute-done((bf16[48,2048]{1,0:T(8,128)(2,1)S(1)}, bf16[48,2048]{1,0:T(8,128)(2,1)S(1)}, u32[]{:S(2)}, u32[]{:S(2)}) %collective-permute-start.3) | collective-permute-done | bytes 196640 | tf_op jit(solution)/shard_map/gather/ppermute | solution.py:21
  15.9 0.0 collective-permute-start.4
  15.9 0.5 collective-permute-start.6
  16.4 0.8 %gather.7.refs_5_ = bf16[9,48,2048]{2,1,0:T(8,128)(2,1)S(1)} custom-call(bf16[48,2048]{1,0:T(8,128)(2,1)S(1)} %gather.4.refs_0_, bf16[48,2048]{1,0:T(8,128)(2,1)S(1)} %gather.5.refs_1_, bf16[48,2048]{1,0:T(8,128)(2,1)S(1)} %gather.6.refs_2_, bf16[9,48,2048]{2,1,0:T(8,128)(2,1)S(1)} %get-tuple-element.19.refs_3_), custom_call_target="tpu_custom_call", output_to_operand_aliasing={{}: (3, {})} | custom-call | flops 48 | bytes 1 | tf_op jit(solution)/shard_map/gather/pallas_call | solution.py:474
  17.2 0.2 collective-permute-done.4.refs_1_
  17.4 0.3 collective-permute-done.6.refs_2_
  17.6 1.8 %late.4 = (bf16[48,2048]{1,0:T(8,128)(2,1)S(1)}, bf16[9,48,2048]{2,1,0:T(8,128)(2,1)S(1)}) custom-call(s32[1,896]{1,0:T(1,128)S(4)} %get-tuple-element.16.plan, bf16[48,2048]{1,0:T(8,128)(2,1)S(1)} %collective-permute-done.2.refs_0_, bf16[48,2048]{1,0:T(8,128)(2,1)S(1)} %collective-permute-done.4.refs_1_, ...), custom_call_target="tpu_custom_call", output_to_operand_aliasing={{1}: (6, {})} | custom-call | flops 48 | bytes 1 | tf_op jit(solution)/shard_map/late/pallas_call | solution.py:490
  19.4 1.3 %collective-permute-start.7 = (bf16[48,2048]{1,0:T(8,128)(2,1)S(1)}, bf16[48,2048]{1,0:T(8,128)(2,1)S(1)}, u32[]{:S(2)}, u32[]{:S(2)}) collective-permute-start(bf16[48,2048]{1,0:T(8,128)(2,1)S(1)} %get-tuple-element.21), channel_id=1, source_target_pairs={{0,8},{24,16},{8,24},{16,0},{1,9},{25,17},{9,25},{17,1},{2,10},{26... | collective-permute-start | bytes 589832 | tf_op jit(solution)/shard_map/late/ppermute | solution.py:510
  20.7 2.3 %late.6 = (bf16[48,2048]{1,0:T(8,128)(2,1)S(1)}, f32[48,2048]{1,0:T(8,128)S(1)}, bf16[48,2048]{1,0:T(8,128)(2,1)S(1)}) custom-call(s32[1,896]{1,0:T(1,128)S(4)} %get-tuple-element.16.plan, bf16[9,48,2048]{2,1,0:T(8,128)(2,1)S(1)} %get-tuple-element.20.panel_buf, bf16[512,128,128]{2,1,0:T(8,128)(2,1)S(1)} %get-tuple-element.18.refs_3_.tiles, ...), custom_call_target="tpu_custom_call" | custom-call | flops 48 | bytes 1 | tf_op jit(solution)/shard_map/late/pallas_call | solution.py:500
  23.1 3.0 %collective-permute-start.8 = (bf16[48,2048]{1,0:T(8,128)(2,1)S(1)}, bf16[48,2048]{1,0:T(8,128)(2,1)S(1)}, u32[]{:S(2)}, u32[]{:S(2)}) collective-permute-start(bf16[48,2048]{1,0:T(8,128)(2,1)S(1)} %get-tuple-element.22), channel_id=1, source_target_pairs={{0,24},{1,25},{2,26},{3,27},{4,28},{5,29},{6,30},{7,31},{8,9},{9,8... | collective-permute-start | bytes 589832 | tf_op jit(solution)/shard_map/late/ppermute | solution.py:32
  26.1 1.3 %collective-permute-done.7.refs_0_ = bf16[48,2048]{1,0:T(8,128)(2,1)S(1)} collective-permute-done((bf16[48,2048]{1,0:T(8,128)(2,1)S(1)}, bf16[48,2048]{1,0:T(8,128)(2,1)S(1)}, u32[]{:S(2)}, u32[]{:S(2)}) %collective-permute-start.7) | collective-permute-done | bytes 196640 | tf_op jit(solution)/shard_map/late/ppermute | solution.py:510
  27.5 5.0 %collective-permute-start.10 = (bf16[48,2048]{1,0:T(8,128)(2,1)S(1)}, bf16[48,2048]{1,0:T(8,128)(2,1)S(1)}, u32[]{:S(2)}, u32[]{:S(2)}) collective-permute-start(bf16[48,2048]{1,0:T(8,128)(2,1)S(1)} %late.7), channel_id=1, source_target_pairs={{0,8},{8,0},{16,24},{24,16},{1,9},{9,1},{17,25},{25,17},{2,10},{10... | collective-permute-start | bytes 589832 | tf_op jit(solution)/shard_map/late/ppermute | solution.py:21
  32.4 0.0 collective-permute-start.9
  32.5 0.0 copy-start
  32.5 0.0 copy-start.3
  32.5 1.1 %late.5.base = f32[48,2048]{1,0:T(8,128)S(1)} custom-call(s32[1,896]{1,0:T(1,128)S(4)} %get-tuple-element.16.plan, bf16[9,48,2048]{2,1,0:T(8,128)(2,1)S(1)} %get-tuple-element.20.panel_buf, bf16[512,128,128]{2,1,0:T(8,128)(2,1)S(1)} %get-tuple-element.18.refs_3_.tiles, f32[65,48,128]{2,1,0:T(8,128)S(1)} %get-tuple-element.17.refs_1_.refs_4_.early, ...), custom_call_target="tpu_custom_call" | custom-call | flops 48 | bytes 1 | tf_op jit(solution)/shard_map/late/pallas_call | solution.py:521
  33.6 0.0 collective-permute-done.8.refs_1_
  33.6 3.5 %collective-permute-done.10.refs_3_ = bf16[48,2048]{1,0:T(8,128)(2,1)S(1)} collective-permute-done((bf16[48,2048]{1,0:T(8,128)(2,1)S(1)}, bf16[48,2048]{1,0:T(8,128)(2,1)S(1)}, u32[]{:S(2)}, u32[]{:S(2)}) %collective-permute-start.10) | collective-permute-done | bytes 196640 | tf_op jit(solution)/shard_map/late/ppermute | solution.py:21
  37.1 0.0 collective-permute-done.9.refs_2_
  37.1 0.7 coefficients.2
  37.8 0.1 collective-permute-start.11
  37.9 0.7 coefficients.3
  38.6 0.5 collective-permute-done.11
  39.1 1.9 %collective-permute-start.14 = (f32[12,8,128]{2,1,0:T(8,128)S(1)}, f32[12,8,128]{2,1,0:T(8,128)S(1)}, u32[]{:S(2)}, u32[]{:S(2)}) collective-permute-start(f32[12,8,128]{2,1,0:T(8,128)S(1)} %add.46), channel_id=1, source_target_pairs={{0,6},{1,25},{2,4},{3,27},{4,2},{5,29},{6,0},{7,31},{8,14},{9,17},... | collective-permute-start | bytes 147464 | tf_op jit(solution)/shard_map/coefficients/ppermute | solution.py:59
  41.0 1.0 %collective-permute-start.13 = (f32[12,8,128]{2,1,0:T(8,128)S(1)}, f32[12,8,128]{2,1,0:T(8,128)S(1)}, u32[]{:S(2)}, u32[]{:S(2)}) collective-permute-start(f32[12,8,128]{2,1,0:T(8,128)S(1)} %add.46), channel_id=1, source_target_pairs={{0,4},{1,17},{2,6},{3,19},{4,0},{5,21},{6,2},{7,23},{8,12},{9,25},... | collective-permute-start | bytes 147464 | tf_op jit(solution)/shard_map/coefficients/ppermute | solution.py:59
  41.9 1.4 %collective-permute-start.12 = (f32[12,8,128]{2,1,0:T(8,128)S(1)}, f32[12,8,128]{2,1,0:T(8,128)S(1)}, u32[]{:S(2)}, u32[]{:S(2)}) collective-permute-start(f32[12,8,128]{2,1,0:T(8,128)S(1)} %add.46), channel_id=1, source_target_pairs={{0,2},{1,9},{2,0},{3,11},{4,6},{5,13},{6,4},{7,15},{8,10},{9,1},{1... | collective-permute-start | bytes 147464 | tf_op jit(solution)/shard_map/coefficients/ppermute | solution.py:59
  43.3 0.8 %collective-permute-done.14 = f32[12,8,128]{2,1,0:T(8,128)S(1)} collective-permute-done((f32[12,8,128]{2,1,0:T(8,128)S(1)}, f32[12,8,128]{2,1,0:T(8,128)S(1)}, u32[]{:S(2)}, u32[]{:S(2)}) %collective-permute-start.14) | collective-permute-done | bytes 49184 | tf_op jit(solution)/shard_map/coefficients/ppermute | solution.py:59
  44.2 0.9 %collective-permute-done.13 = f32[12,8,128]{2,1,0:T(8,128)S(1)} collective-permute-done((f32[12,8,128]{2,1,0:T(8,128)S(1)}, f32[12,8,128]{2,1,0:T(8,128)S(1)}, u32[]{:S(2)}, u32[]{:S(2)}) %collective-permute-start.13) | collective-permute-done | bytes 49184 | tf_op jit(solution)/shard_map/coefficients/ppermute | solution.py:59
  45.1 1.0 %collective-permute-done.12 = f32[12,8,128]{2,1,0:T(8,128)S(1)} collective-permute-done((f32[12,8,128]{2,1,0:T(8,128)S(1)}, f32[12,8,128]{2,1,0:T(8,128)S(1)}, u32[]{:S(2)}, u32[]{:S(2)}) %collective-permute-start.12) | collective-permute-done | bytes 49184 | tf_op jit(solution)/shard_map/coefficients/ppermute | solution.py:59
  46.0 4.9 %collective-permute-start.17 = (f32[12,8,128]{2,1,0:T(8,128)S(1)}, f32[12,8,128]{2,1,0:T(8,128)S(1)}, u32[]{:S(2)}, u32[]{:S(2)}) collective-permute-start(f32[12,8,128]{2,1,0:T(8,128)S(1)} %add_add_fusion.1), channel_id=1, source_target_pairs={{0,24},{1,7},{2,26},{3,5},{4,28},{5,3},{6,30},{7,1},{8,16},{9,15},... | collective-permute-start | bytes 147464 | tf_op jit(solution)/shard_map/coefficients/ppermute | solution.py:59
  50.9 0.6 collective-permute-start.16
  51.6 0.5 collective-permute-start.15
  52.1 0.9 %collective-permute-done.17 = f32[12,8,128]{2,1,0:T(8,128)S(1)} collective-permute-done((f32[12,8,128]{2,1,0:T(8,128)S(1)}, f32[12,8,128]{2,1,0:T(8,128)S(1)}, u32[]{:S(2)}, u32[]{:S(2)}) %collective-permute-start.17) | collective-permute-done | bytes 49184 | tf_op jit(solution)/shard_map/coefficients/ppermute | solution.py:59
  53.0 3.0 %collective-permute-done.16 = f32[12,8,128]{2,1,0:T(8,128)S(1)} collective-permute-done((f32[12,8,128]{2,1,0:T(8,128)S(1)}, f32[12,8,128]{2,1,0:T(8,128)S(1)}, u32[]{:S(2)}, u32[]{:S(2)}) %collective-permute-start.16) | collective-permute-done | bytes 49184 | tf_op jit(solution)/shard_map/coefficients/ppermute | solution.py:59
  56.0 0.2 collective-permute-done.15
  56.2 0.1 collective-permute-start.18
  56.3 0.6 residual.4.less
  56.9 0.6 collective-permute-done.18.other
  57.5 0.9 %residual.5 = (f32[48,2048]{1,0:T(8,128)S(1)}, f32[24,128]{1,0:T(8,128)S(1)}) custom-call(s32[1,896]{1,0:T(1,128)S(4)} %get-tuple-element.16.plan, f32[12,8,128]{2,1,0:T(8,128)S(1)} %collective-permute-done.18.other, f32[48,2048]{1,0:T(8,128)S(1)} %residual.4.less, f32[1,2048]{1,0:T(1,128)S(1)} %bitcast.14, f32[48,2048]{1,0:T(8,128)S(1)} %copy-done.1, ...), custom_call_target="tpu_custom_call" | custom-call | flops 48 | bytes 1 | tf_op jit(solution)/shard_map/residual/pallas_call | solution.py:564
  58.4 0.2 collective-permute-start.19
  58.6 1.0 %collective-permute-done.19 = f32[24,128]{1,0:T(8,128)S(1)} collective-permute-done((f32[24,128]{1,0:T(8,128)S(1)}, f32[24,128]{1,0:T(8,128)S(1)}, u32[]{:S(2)}, u32[]{:S(2)}) %collective-permute-start.19) | collective-permute-done | bytes 12320 | tf_op jit(solution)/shard_map/gram/ppermute | solution.py:21
  59.7 2.8 %collective-permute-start.22 = (f32[24,128]{1,0:T(8,128)S(1)}, f32[24,128]{1,0:T(8,128)S(1)}, u32[]{:S(2)}, u32[]{:S(2)}) collective-permute-start(f32[24,128]{1,0:T(8,128)S(1)} %add.53), channel_id=1, source_target_pairs={{0,6},{1,7},{2,4},{3,5},{4,2},{5,3},{6,0},{7,1},{8,14},{9,15},{10,... | collective-permute-start | bytes 36872 | tf_op jit(solution)/shard_map/gram/ppermute | solution.py:21
  62.5 0.0 collective-permute-start.21
  62.5 0.7 collective-permute-start.20
  63.1 0.8 %residual.6.refs_1_ = f32[48,2048]{1,0:T(8,128)} custom-call(f32[48,2048]{1,0:T(8,128)S(1)} %get-tuple-element.27.value), custom_call_target="tpu_custom_call" | custom-call | flops 48 | bytes 1 | tf_op jit(solution)/shard_map/residual/pallas_call | solution.py:575
  63.9 0.8 %residual.7.refs_2_ = f32[432,48]{1,0:T(8,128)} custom-call(s32[1,896]{1,0:T(1,128)S(4)} %get-tuple-element.16.plan, f32[12,8,128]{2,1,0:T(8,128)S(1)} %add_add_fusion.mine, f32[12,8,128]{2,1,0:T(8,128)S(1)} %collective-permute-done.18.other), custom_call_target="tpu_custom_call" | custom-call | flops 48 | bytes 1 | tf_op jit(solution)/shard_map/residual/pallas_call | solution.py:584
  64.7 1.5 %collective-permute-done.21 = f32[24,128]{1,0:T(8,128)S(1)} collective-permute-done((f32[24,128]{1,0:T(8,128)S(1)}, f32[24,128]{1,0:T(8,128)S(1)}, u32[]{:S(2)}, u32[]{:S(2)}) %collective-permute-start.21) | collective-permute-done | bytes 12320 | tf_op jit(solution)/shard_map/gram/ppermute | solution.py:21
  66.2 1.9 %collective-permute-start.25 = (f32[24,128]{1,0:T(8,128)S(1)}, f32[24,128]{1,0:T(8,128)S(1)}, u32[]{:S(2)}, u32[]{:S(2)}) collective-permute-start(f32[24,128]{1,0:T(8,128)S(1)} %gram.1), channel_id=1, source_target_pairs={{0,24},{8,16},{16,8},{24,0},{1,25},{9,17},{17,9},{25,1},{2,26},{10... | collective-permute-start | bytes 36872 | tf_op jit(solution)/shard_map/gram/ppermute | solution.py:21
  68.1 0.0 collective-permute-start.24
  68.1 2.5 %collective-permute-start.23 = (f32[24,128]{1,0:T(8,128)S(1)}, f32[24,128]{1,0:T(8,128)S(1)}, u32[]{:S(2)}, u32[]{:S(2)}) collective-permute-start(f32[24,128]{1,0:T(8,128)S(1)} %gram.1), channel_id=1, source_target_pairs={{0,8},{8,0},{16,24},{24,16},{1,9},{9,1},{17,25},{25,17},{2,10},{10... | collective-permute-start | bytes 36872 | tf_op jit(solution)/shard_map/gram/ppermute | solution.py:21
  70.7 1.1 %collective-permute-done.25 = f32[24,128]{1,0:T(8,128)S(1)} collective-permute-done((f32[24,128]{1,0:T(8,128)S(1)}, f32[24,128]{1,0:T(8,128)S(1)}, u32[]{:S(2)}, u32[]{:S(2)}) %collective-permute-start.25) | collective-permute-done | bytes 12320 | tf_op jit(solution)/shard_map/gram/ppermute | solution.py:21
  71.8 0.9 %collective-permute-done.24 = f32[24,128]{1,0:T(8,128)S(1)} collective-permute-done((f32[24,128]{1,0:T(8,128)S(1)}, f32[24,128]{1,0:T(8,128)S(1)}, u32[]{:S(2)}, u32[]{:S(2)}) %collective-permute-start.24) | collective-permute-done | bytes 12320 | tf_op jit(solution)/shard_map/gram/ppermute | solution.py:21
  72.7 0.1 fusion
  72.8 0.6 pad_maximum_fusion
  (27 shorter events, 0.1 us)
Async XLA Ops:
  1.7 5.4 %collective-permute-start = (bf16[48,2048]{1,0:T(8,128)(2,1)S(1)}, bf16[48,2048]{1,0:T(8,128)(2,1)S(1)}, u32[]{:S(2)}, u32[]{:S(2)}) collective-permute-start(bf16[48,2048]{1,0:T(8,128)(2,1)S(1)} %convert_element_type.9.own_panel), channel_id=1, source_target_pairs={{0,1},{1,0},{2,3},{3,2},{4,5},{5,4},{6,7},{7,6},{8,9},{9,8},{10,11... | collective-permute-start | bytes 589832 | tf_op jit(solution)/shard_map/gather/ppermute | solution.py:21
  2.2 9.0 %collective-permute-start.1 = (bf16[48,2048]{1,0:T(8,128)(2,1)S(1)}, bf16[48,2048]{1,0:T(8,128)(2,1)S(1)}, u32[]{:S(2)}, u32[]{:S(2)}) collective-permute-start(bf16[48,2048]{1,0:T(8,128)(2,1)S(1)} %convert_element_type.9.own_panel), channel_id=1, source_target_pairs={{0,2},{1,3},{2,0},{3,1},{4,6},{5,7},{6,4},{7,5},{8,10},{9,11},{10,... | collective-permute-start | bytes 589832 | tf_op jit(solution)/shard_map/gather/ppermute | solution.py:21
  4.7 11.2 %collective-permute-start.3 = (bf16[48,2048]{1,0:T(8,128)(2,1)S(1)}, bf16[48,2048]{1,0:T(8,128)(2,1)S(1)}, u32[]{:S(2)}, u32[]{:S(2)}) collective-permute-start(bf16[48,2048]{1,0:T(8,128)(2,1)S(1)} %convert_element_type.9.own_panel), channel_id=1, source_target_pairs={{0,4},{1,5},{2,6},{3,7},{4,0},{5,1},{6,2},{7,3},{8,12},{9,13},{10,... | collective-permute-start | bytes 589832 | tf_op jit(solution)/shard_map/gather/ppermute | solution.py:21
  6.3 9.7 %collective-permute-start.5 = (bf16[48,2048]{1,0:T(8,128)(2,1)S(1)}, bf16[48,2048]{1,0:T(8,128)(2,1)S(1)}, u32[]{:S(2)}, u32[]{:S(2)}) collective-permute-start(bf16[48,2048]{1,0:T(8,128)(2,1)S(1)} %convert_element_type.9.own_panel), channel_id=1, source_target_pairs={{0,6},{1,7},{2,4},{3,5},{4,2},{5,3},{6,0},{7,1},{8,14},{9,15},{10,... | collective-permute-start | bytes 589832 | tf_op jit(solution)/shard_map/gather/ppermute | solution.py:21
  11.2 6.0 %collective-permute-start.2 = (bf16[48,2048]{1,0:T(8,128)(2,1)S(1)}, bf16[48,2048]{1,0:T(8,128)(2,1)S(1)}, u32[]{:S(2)}, u32[]{:S(2)}) collective-permute-start(bf16[48,2048]{1,0:T(8,128)(2,1)S(1)} %gather.4.refs_0_), channel_id=1, source_target_pairs={{0,1},{1,0},{2,3},{3,2},{4,5},{5,4},{6,7},{7,6},{8,9},{9,8},{10,11... | collective-permute-start | bytes 589832 | tf_op jit(solution)/shard_map/gather/ppermute | solution.py:21
  15.9 1.4 %collective-permute-start.4 = (bf16[48,2048]{1,0:T(8,128)(2,1)S(1)}, bf16[48,2048]{1,0:T(8,128)(2,1)S(1)}, u32[]{:S(2)}, u32[]{:S(2)}) collective-permute-start(bf16[48,2048]{1,0:T(8,128)(2,1)S(1)} %gather.5.refs_1_), channel_id=1, source_target_pairs={{0,1},{1,0},{2,3},{3,2},{4,5},{5,4},{6,7},{7,6},{8,9},{9,8},{10,11... | collective-permute-start | bytes 589832 | tf_op jit(solution)/shard_map/gather/ppermute | solution.py:21
  15.9 1.7 %collective-permute-start.6 = (bf16[48,2048]{1,0:T(8,128)(2,1)S(1)}, bf16[48,2048]{1,0:T(8,128)(2,1)S(1)}, u32[]{:S(2)}, u32[]{:S(2)}) collective-permute-start(bf16[48,2048]{1,0:T(8,128)(2,1)S(1)} %gather.6.refs_2_), channel_id=1, source_target_pairs={{0,1},{1,0},{2,3},{3,2},{4,5},{5,4},{6,7},{7,6},{8,9},{9,8},{10,11... | collective-permute-start | bytes 589832 | tf_op jit(solution)/shard_map/gather/ppermute | solution.py:21
  19.4 8.0 %collective-permute-start.7 = (bf16[48,2048]{1,0:T(8,128)(2,1)S(1)}, bf16[48,2048]{1,0:T(8,128)(2,1)S(1)}, u32[]{:S(2)}, u32[]{:S(2)}) collective-permute-start(bf16[48,2048]{1,0:T(8,128)(2,1)S(1)} %get-tuple-element.21), channel_id=1, source_target_pairs={{0,8},{24,16},{8,24},{16,0},{1,9},{25,17},{9,25},{17,1},{2,10},{26... | collective-permute-start | bytes 589832 | tf_op jit(solution)/shard_map/late/ppermute | solution.py:510
  20.7 11.7 %copy-start.1 = (f32[48,2048]{1,0:T(8,128)S(1)}, f32[48,2048]{1,0:T(8,128)}, u32[]{:S(2)}) copy-start(f32[48,2048]{1,0:T(8,128)} %current.7) | copy-start | bytes 1179652
  20.7 11.7 %copy-start.2 = (f32[48,2048]{1,0:T(8,128)S(1)}, f32[48,2048]{1,0:T(8,128)}, u32[]{:S(2)}) copy-start(f32[48,2048]{1,0:T(8,128)} %previous.1) | copy-start | bytes 1179652
  20.7 11.7 %copy-start.4 = (f32[48,48]{1,0:T(8,128)S(1)}, f32[48,48]{1,0:T(8,128)}, u32[]{:S(2)}) copy-start(f32[48,48]{1,0:T(8,128)} %coupling.1) | copy-start | bytes 27652
  20.7 11.7 %copy-start.5 = (f32[2048]{0:T(1024)S(1)}, f32[2048]{0:T(1024)}, u32[]{:S(2)}) copy-start(f32[2048]{0:T(1024)} %param.14) | copy-start | bytes 24580
  23.1 10.6 %collective-permute-start.8 = (bf16[48,2048]{1,0:T(8,128)(2,1)S(1)}, bf16[48,2048]{1,0:T(8,128)(2,1)S(1)}, u32[]{:S(2)}, u32[]{:S(2)}) collective-permute-start(bf16[48,2048]{1,0:T(8,128)(2,1)S(1)} %get-tuple-element.22), channel_id=1, source_target_pairs={{0,24},{1,25},{2,26},{3,27},{4,28},{5,29},{6,30},{7,31},{8,9},{9,8... | collective-permute-start | bytes 589832 | tf_op jit(solution)/shard_map/late/ppermute | solution.py:32
  27.5 9.6 %collective-permute-start.10 = (bf16[48,2048]{1,0:T(8,128)(2,1)S(1)}, bf16[48,2048]{1,0:T(8,128)(2,1)S(1)}, u32[]{:S(2)}, u32[]{:S(2)}) collective-permute-start(bf16[48,2048]{1,0:T(8,128)(2,1)S(1)} %late.7), channel_id=1, source_target_pairs={{0,8},{8,0},{16,24},{24,16},{1,9},{9,1},{17,25},{25,17},{2,10},{10... | collective-permute-start | bytes 589832 | tf_op jit(solution)/shard_map/late/ppermute | solution.py:21
  32.4 4.7 %collective-permute-start.9 = (bf16[48,2048]{1,0:T(8,128)(2,1)S(1)}, bf16[48,2048]{1,0:T(8,128)(2,1)S(1)}, u32[]{:S(2)}, u32[]{:S(2)}) collective-permute-start(bf16[48,2048]{1,0:T(8,128)(2,1)S(1)} %add_convert_fusion.refs_1_), channel_id=1, source_target_pairs={{0,1},{1,0},{2,3},{3,2},{4,5},{5,4},{6,7},{7,6},{8,16},{9,17},{10,... | collective-permute-start | bytes 589832 | tf_op jit(solution)/shard_map/late/ppermute | solution.py:32
  32.5 4.6 %copy-start = (f32[8,48,2048]{2,1,0:T(8,128)S(1)}, f32[8,48,2048]{2,1,0:T(8,128)}, u32[]{:S(2)}) copy-start(f32[8,48,2048]{2,1,0:T(8,128)} %param.13) | copy-start | bytes 9437188
  32.5 4.6 %copy-start.3 = (f32[2048]{0:T(1024)S(1)}, f32[2048]{0:T(1024)}, u32[]{:S(2)}) copy-start(f32[2048]{0:T(1024)} %param.15) | copy-start | bytes 24580
  37.8 1.3 %collective-permute-start.11 = (f32[12,8,128]{2,1,0:T(8,128)S(1)}, f32[12,8,128]{2,1,0:T(8,128)S(1)}, u32[]{:S(2)}, u32[]{:S(2)}) collective-permute-start(f32[12,8,128]{2,1,0:T(8,128)S(1)} %get-tuple-element.26), channel_id=1, source_target_pairs={{0,1},{1,0},{2,3},{3,2},{4,5},{5,4},{6,7},{7,6},{8,9},{9,8},{10,11... | collective-permute-start | bytes 147464 | tf_op jit(solution)/shard_map/coefficients/ppermute | solution.py:21
  39.1 5.0 %collective-permute-start.14 = (f32[12,8,128]{2,1,0:T(8,128)S(1)}, f32[12,8,128]{2,1,0:T(8,128)S(1)}, u32[]{:S(2)}, u32[]{:S(2)}) collective-permute-start(f32[12,8,128]{2,1,0:T(8,128)S(1)} %add.46), channel_id=1, source_target_pairs={{0,6},{1,25},{2,4},{3,27},{4,2},{5,29},{6,0},{7,31},{8,14},{9,17},... | collective-permute-start | bytes 147464 | tf_op jit(solution)/shard_map/coefficients/ppermute | solution.py:59
  41.0 4.1 %collective-permute-start.13 = (f32[12,8,128]{2,1,0:T(8,128)S(1)}, f32[12,8,128]{2,1,0:T(8,128)S(1)}, u32[]{:S(2)}, u32[]{:S(2)}) collective-permute-start(f32[12,8,128]{2,1,0:T(8,128)S(1)} %add.46), channel_id=1, source_target_pairs={{0,4},{1,17},{2,6},{3,19},{4,0},{5,21},{6,2},{7,23},{8,12},{9,25},... | collective-permute-start | bytes 147464 | tf_op jit(solution)/shard_map/coefficients/ppermute | solution.py:59
  41.9 4.1 %collective-permute-start.12 = (f32[12,8,128]{2,1,0:T(8,128)S(1)}, f32[12,8,128]{2,1,0:T(8,128)S(1)}, u32[]{:S(2)}, u32[]{:S(2)}) collective-permute-start(f32[12,8,128]{2,1,0:T(8,128)S(1)} %add.46), channel_id=1, source_target_pairs={{0,2},{1,9},{2,0},{3,11},{4,6},{5,13},{6,4},{7,15},{8,10},{9,1},{1... | collective-permute-start | bytes 147464 | tf_op jit(solution)/shard_map/coefficients/ppermute | solution.py:59
  46.0 7.0 %collective-permute-start.17 = (f32[12,8,128]{2,1,0:T(8,128)S(1)}, f32[12,8,128]{2,1,0:T(8,128)S(1)}, u32[]{:S(2)}, u32[]{:S(2)}) collective-permute-start(f32[12,8,128]{2,1,0:T(8,128)S(1)} %add_add_fusion.1), channel_id=1, source_target_pairs={{0,24},{1,7},{2,26},{3,5},{4,28},{5,3},{6,30},{7,1},{8,16},{9,15},... | collective-permute-start | bytes 147464 | tf_op jit(solution)/shard_map/coefficients/ppermute | solution.py:59
  50.9 5.1 %collective-permute-start.16 = (f32[12,8,128]{2,1,0:T(8,128)S(1)}, f32[12,8,128]{2,1,0:T(8,128)S(1)}, u32[]{:S(2)}, u32[]{:S(2)}) collective-permute-start(f32[12,8,128]{2,1,0:T(8,128)S(1)} %add_add_fusion.1), channel_id=1, source_target_pairs={{0,16},{1,5},{2,18},{3,7},{4,20},{5,1},{6,22},{7,3},{8,24},{9,13},... | collective-permute-start | bytes 147464 | tf_op jit(solution)/shard_map/coefficients/ppermute | solution.py:59
  51.6 4.6 %collective-permute-start.15 = (f32[12,8,128]{2,1,0:T(8,128)S(1)}, f32[12,8,128]{2,1,0:T(8,128)S(1)}, u32[]{:S(2)}, u32[]{:S(2)}) collective-permute-start(f32[12,8,128]{2,1,0:T(8,128)S(1)} %add_add_fusion.1), channel_id=1, source_target_pairs={{0,8},{1,3},{2,10},{3,1},{4,12},{5,7},{6,14},{7,5},{8,0},{9,11},{1... | collective-permute-start | bytes 147464 | tf_op jit(solution)/shard_map/coefficients/ppermute | solution.py:59
  56.2 1.3 %collective-permute-start.18 = (f32[12,8,128]{2,1,0:T(8,128)S(1)}, f32[12,8,128]{2,1,0:T(8,128)S(1)}, u32[]{:S(2)}, u32[]{:S(2)}) collective-permute-start(f32[12,8,128]{2,1,0:T(8,128)S(1)} %add_add_fusion.mine), channel_id=1, source_target_pairs={{0,1},{1,0},{2,3},{3,2},{4,5},{5,4},{6,7},{7,6},{8,9},{9,8},{10,11... | collective-permute-start | bytes 147464 | tf_op jit(solution)/shard_map/coefficients/ppermute | solution.py:21
  58.4 1.2 %collective-permute-start.19 = (f32[24,128]{1,0:T(8,128)S(1)}, f32[24,128]{1,0:T(8,128)S(1)}, u32[]{:S(2)}, u32[]{:S(2)}) collective-permute-start(f32[24,128]{1,0:T(8,128)S(1)} %get-tuple-element.28), channel_id=1, source_target_pairs={{0,1},{1,0},{2,3},{3,2},{4,5},{5,4},{6,7},{7,6},{8,9},{9,8},{10,11... | collective-permute-start | bytes 36872 | tf_op jit(solution)/shard_map/gram/ppermute | solution.py:21
  59.7 5.1 %collective-permute-start.22 = (f32[24,128]{1,0:T(8,128)S(1)}, f32[24,128]{1,0:T(8,128)S(1)}, u32[]{:S(2)}, u32[]{:S(2)}) collective-permute-start(f32[24,128]{1,0:T(8,128)S(1)} %add.53), channel_id=1, source_target_pairs={{0,6},{1,7},{2,4},{3,5},{4,2},{5,3},{6,0},{7,1},{8,14},{9,15},{10,... | collective-permute-start | bytes 36872 | tf_op jit(solution)/shard_map/gram/ppermute | solution.py:21
  62.5 3.7 %collective-permute-start.21 = (f32[24,128]{1,0:T(8,128)S(1)}, f32[24,128]{1,0:T(8,128)S(1)}, u32[]{:S(2)}, u32[]{:S(2)}) collective-permute-start(f32[24,128]{1,0:T(8,128)S(1)} %add.53), channel_id=1, source_target_pairs={{0,4},{1,5},{2,6},{3,7},{4,0},{5,1},{6,2},{7,3},{8,12},{9,13},{10,... | collective-permute-start | bytes 36872 | tf_op jit(solution)/shard_map/gram/ppermute | solution.py:21
  62.5 3.7 %collective-permute-start.20 = (f32[24,128]{1,0:T(8,128)S(1)}, f32[24,128]{1,0:T(8,128)S(1)}, u32[]{:S(2)}, u32[]{:S(2)}) collective-permute-start(f32[24,128]{1,0:T(8,128)S(1)} %add.53), channel_id=1, source_target_pairs={{0,2},{1,3},{2,0},{3,1},{4,6},{5,7},{6,4},{7,5},{8,10},{9,11},{10,... | collective-permute-start | bytes 36872 | tf_op jit(solution)/shard_map/gram/ppermute | solution.py:21
  66.2 5.6 %collective-permute-start.25 = (f32[24,128]{1,0:T(8,128)S(1)}, f32[24,128]{1,0:T(8,128)S(1)}, u32[]{:S(2)}, u32[]{:S(2)}) collective-permute-start(f32[24,128]{1,0:T(8,128)S(1)} %gram.1), channel_id=1, source_target_pairs={{0,24},{8,16},{16,8},{24,0},{1,25},{9,17},{17,9},{25,1},{2,26},{10... | collective-permute-start | bytes 36872 | tf_op jit(solution)/shard_map/gram/ppermute | solution.py:21
  68.1 4.6 %collective-permute-start.24 = (f32[24,128]{1,0:T(8,128)S(1)}, f32[24,128]{1,0:T(8,128)S(1)}, u32[]{:S(2)}, u32[]{:S(2)}) collective-permute-start(f32[24,128]{1,0:T(8,128)S(1)} %gram.1), channel_id=1, source_target_pairs={{0,16},{8,24},{16,0},{24,8},{1,17},{9,25},{17,1},{25,9},{2,18},{10... | collective-permute-start | bytes 36872 | tf_op jit(solution)/shard_map/gram/ppermute | solution.py:21
  68.1 4.6 %collective-permute-start.23 = (f32[24,128]{1,0:T(8,128)S(1)}, f32[24,128]{1,0:T(8,128)S(1)}, u32[]{:S(2)}, u32[]{:S(2)}) collective-permute-start(f32[24,128]{1,0:T(8,128)S(1)} %gram.1), channel_id=1, source_target_pairs={{0,8},{8,0},{16,24},{24,16},{1,9},{9,1},{17,25},{25,17},{2,10},{10... | collective-permute-start | bytes 36872 | tf_op jit(solution)/shard_map/gram/ppermute | solution.py:21

commit v20 on v18

--- a/solution.py
+++ b/solution.py
@@ -44,21 +44,6 @@
     for m in range(lax.axis_size(axis) - step, 0, -step):
         values[m] = swap(value, axis, m)
     return tree_sum(values)
-
-
-def total_by_core(value):
-    row_devs, col_devs = lax.axis_size("row"), lax.axis_size("col")
-    if col_devs != 2 * row_devs:
-        return total(total(value, "col", 2), "row", 1)
-    places = [(r, c) for r in range(row_devs) for c in range(col_devs)]
-    for turn in range(2):
-        values = {0: value}
-        for m in range(row_devs - 1, 0, -1):
-            partners = [(r, c ^ (2 * m)) if c % 2 == turn else (r ^ m, c) for r, c in places]
-            trades = [(i, r * col_devs + c) for i, (r, c) in enumerate(partners)]
-            values[m] = lax.ppermute(value, ("row", "col"), trades)
-        value = tree_sum(values)
-    return value
 
 
 def split(value):
@@ -549,7 +534,7 @@
             cost_estimate=cost(width),
         )(plan, recurrence, mass, current_block, stored)
         mine = keep + swap(give, "col", 1)
-        mine = total_by_core(mine)
+        mine = total(total(mine, "col", 2), "row", 1)
         other = swap(mine, "col", 1)
 
     with jax.named_scope("residual"):

time: 70 us -> 70 us (level)
  Pallas kernels: 16.1 us -> 14.9 us
    ppermute x6 -> x0, starting transfers between devices: 8 us -> none  [total_by_core(): values[m] = lax.ppermute(value, ('row', 'col'), trades)]
    ppermute x17 -> x23, starting transfers between devices: 14.5 us -> 22 us  [swap(): return lax.ppermute(value, axis, [(i, i ^ mask) for i in range(count)])]
    ppermute x17 -> x23, waiting for transfers between devices: 12.1 us -> 18.8 us  [swap(): return lax.ppermute(value, axis, [(i, i ^ mask) for i in range(count)])]
    ppermute x6 -> x0, waiting for transfers between devices: 5.59 us -> none  [total_by_core(): values[m] = lax.ppermute(value, ('row', 'col'), trades)]
    ppermute x1, waiting for transfers between devices: 6.6 us -> 1.3 us  [local(): first = lax.ppermute(first, 'row', [(0, 1), (3, 2), (1, 3), (2, 0)])]
    ppermute x2, waiting for transfers between devices: 0.01 us -> 4.82 us  [trade_rows(): return lax.ppermute(value, ('row', 'col'), trades)]
    ppermute x1, starting transfers between devices: 1.01 us -> 2.25 us  [local(): first = lax.ppermute(first, 'row', [(0, 1), (3, 2), (1, 3), (2, 0)])]
  transfers between devices with their start and end apart: 26 -> 26, of which waited for: 16 -> 17; matrix products, arithmetic and copies ran while one was open for 0% -> 0% of each run, Pallas kernels for 17% -> 16%
where the time goes in v20:
time: 70 us; the launch traced here: 69.8 us
  starting transfers between devices  26.6 us (38%)
  waiting for transfers between devices  24.9 us (36%)
  Pallas kernels  14.9 us (21%)
  other arithmetic  1.8 us (3%)
  between operations  1.51 us (2%)
    ppermute x23, starting transfers between devices, swap(): return lax.ppermute(value, axis, [(i, i ^ mask) for i in range(count)])  22 us
    ppermute x23, waiting for transfers between devices, swap(): return lax.ppermute(value, axis, [(i, i ^ mask) for i in range(count)])  18.8 us
    ppermute x2, waiting for transfers between devices, trade_rows(): return lax.ppermute(value, ('row', 'col'), trades)  4.82 us
    pallas_call x1, Pallas kernels, local(): pl.pallas_call(functools.partial(early_kernel, row_devs, col_devs, slab_t...  4.78 us
    ppermute x2, starting transfers between devices, trade_rows(): return lax.ppermute(value, ('row', 'col'), trades)  2.3 us
    ppermute x1, starting transfers between devices, local(): first = lax.ppermute(first, 'row', [(0, 1), (3, 2), (1, 3), (2, 0)])  2.25 us
    pallas_call x1, Pallas kernels, local(): pl.pallas_call(functools.partial(first_late_kernel, [first_mask], odd), o...  1.76 us
    pallas_call x1, Pallas kernels, local(): pl.pallas_call(functools.partial(late_kernel, masks), out_shape=[part, sl...  1.68 us
  transfers between devices with their start and end apart: 26, of which 17 were waited for; matrix products, arithmetic and copies ran while one was open for 0% of the time, Pallas kernels for 16%

profile of v20, /device:TPU:0, one launch (start us, length us, event | category | flops | bytes accessed | tf_op | source)
XLA Modules:
  0.0 69.8 jit_solution(7645224497435794008)
XLA Ops:
  0.6 1.0 %convert_element_type.9.own_panel = bf16[48,2048]{1,0:T(8,128)(2,1)S(1)} convert(f32[48,2048]{1,0:T(8,128)} %current.7) | non-fusion elementwise | flops 98304 | bytes 589824 | tf_op jit(solution)/shard_map/gather/convert_element_type | solution.py:415
  1.7 0.5 collective-permute-start
  2.2 2.6 %collective-permute-start.1 = (bf16[48,2048]{1,0:T(8,128)(2,1)S(1)}, bf16[48,2048]{1,0:T(8,128)(2,1)S(1)}, u32[]{:S(2)}, u32[]{:S(2)}) collective-permute-start(bf16[48,2048]{1,0:T(8,128)(2,1)S(1)} %convert_element_type.9.own_panel), channel_id=1, source_target_pairs={{0,2},{1,3},{2,0},{3,1},{4,6},{5,7},{6,4},{7,5},{8,10},{9,11},{10,... | collective-permute-start | bytes 589832 | tf_op jit(solution)/shard_map/gather/ppermute | solution.py:21
  4.7 1.5 %collective-permute-start.3 = (bf16[48,2048]{1,0:T(8,128)(2,1)S(1)}, bf16[48,2048]{1,0:T(8,128)(2,1)S(1)}, u32[]{:S(2)}, u32[]{:S(2)}) collective-permute-start(bf16[48,2048]{1,0:T(8,128)(2,1)S(1)} %convert_element_type.9.own_panel), channel_id=1, source_target_pairs={{0,4},{1,5},{2,6},{3,7},{4,0},{5,1},{6,2},{7,3},{8,12},{9,13},{10,... | collective-permute-start | bytes 589832 | tf_op jit(solution)/shard_map/gather/ppermute | solution.py:21
  6.3 0.0 collective-permute-start.5
  6.9 0.1 pad_add_fusion.place
  7.0 4.8 %early.1 = (s32[1,896]{1,0:T(1,128)S(4)}, bf16[512,128,128]{2,1,0:T(8,128)(2,1)S(1)}, f32[65,48,128]{2,1,0:T(8,128)S(1)}, bf16[9,48,2048]{2,1,0:T(8,128)(2,1)S(1)}) custom-call(s32[2]{0:T(128)S(1)} %pad_add_fusion.place, s32[1]{0:T(128)S(6)} %copy.25.counts, s32[1,512]{1,0:T(1,128)} %bitcast.17, s32[1,512]{1,0:T(1,128)} %bitcast.18, ...), custom_call_target="tpu_custom_call" | custom-call | flops 805306368 | bytes 16777216 | tf_op jit(solution)/shard_map/early/pallas_call | solution.py:424
  11.8 0.1 collective-permute-start.2
  11.9 4.0 %collective-permute-done.3.refs_0_ = bf16[48,2048]{1,0:T(8,128)(2,1)S(1)} collective-permute-done((bf16[48,2048]{1,0:T(8,128)(2,1)S(1)}, bf16[48,2048]{1,0:T(8,128)(2,1)S(1)}, u32[]{:S(2)}, u32[]{:S(2)}) %collective-permute-start.3) | collective-permute-done | bytes 196640 | tf_op jit(solution)/shard_map/gather/ppermute | solution.py:21
  15.9 0.0 collective-permute-start.4
  15.9 0.5 collective-permute-start.6
  16.4 0.8 %gather.7.refs_5_ = bf16[9,48,2048]{2,1,0:T(8,128)(2,1)S(1)} custom-call(bf16[48,2048]{1,0:T(8,128)(2,1)S(1)} %gather.4.refs_0_, bf16[48,2048]{1,0:T(8,128)(2,1)S(1)} %gather.5.refs_1_, bf16[48,2048]{1,0:T(8,128)(2,1)S(1)} %gather.6.refs_2_, bf16[9,48,2048]{2,1,0:T(8,128)(2,1)S(1)} %get-tuple-element.19.refs_3_), custom_call_target="tpu_custom_call", output_to_operand_aliasing={{}: (3, {})} | custom-call | flops 48 | bytes 1 | tf_op jit(solution)/shard_map/gather/pallas_call | solution.py:459
  17.2 0.0 collective-permute-done.2.refs_0_
  17.2 0.2 collective-permute-done.4.refs_1_
  17.4 0.3 collective-permute-done.6.refs_2_
  17.6 1.8 %late.3 = (bf16[48,2048]{1,0:T(8,128)(2,1)S(1)}, bf16[9,48,2048]{2,1,0:T(8,128)(2,1)S(1)}) custom-call(s32[1,896]{1,0:T(1,128)S(4)} %get-tuple-element.16.plan, bf16[48,2048]{1,0:T(8,128)(2,1)S(1)} %collective-permute-done.2.refs_0_, bf16[48,2048]{1,0:T(8,128)(2,1)S(1)} %collective-permute-done.4.refs_1_, ...), custom_call_target="tpu_custom_call", output_to_operand_aliasing={{1}: (6, {})} | custom-call | flops 48 | bytes 1 | tf_op jit(solution)/shard_map/late/pallas_call | solution.py:475
  19.4 2.2 %collective-permute-start.7 = (bf16[48,2048]{1,0:T(8,128)(2,1)S(1)}, bf16[48,2048]{1,0:T(8,128)(2,1)S(1)}, u32[]{:S(2)}, u32[]{:S(2)}) collective-permute-start(bf16[48,2048]{1,0:T(8,128)(2,1)S(1)} %get-tuple-element.21), channel_id=1, source_target_pairs={{0,8},{24,16},{8,24},{16,0},{1,9},{25,17},{9,25},{17,1},{2,10},{26... | collective-permute-start | bytes 589832 | tf_op jit(solution)/shard_map/late/ppermute | solution.py:495
  21.7 1.7 %late.5 = (bf16[48,2048]{1,0:T(8,128)(2,1)S(1)}, f32[48,2048]{1,0:T(8,128)S(1)}, bf16[48,2048]{1,0:T(8,128)(2,1)S(1)}) custom-call(s32[1,896]{1,0:T(1,128)S(4)} %get-tuple-element.16.plan, bf16[9,48,2048]{2,1,0:T(8,128)(2,1)S(1)} %get-tuple-element.20.panel_buf, bf16[512,128,128]{2,1,0:T(8,128)(2,1)S(1)} %get-tuple-element.18.refs_3_.tiles, ...), custom_call_target="tpu_custom_call" | custom-call | flops 48 | bytes 1 | tf_op jit(solution)/shard_map/late/pallas_call | solution.py:485
  23.4 2.2 %collective-permute-start.8 = (bf16[48,2048]{1,0:T(8,128)(2,1)S(1)}, bf16[48,2048]{1,0:T(8,128)(2,1)S(1)}, u32[]{:S(2)}, u32[]{:S(2)}) collective-permute-start(bf16[48,2048]{1,0:T(8,128)(2,1)S(1)} %get-tuple-element.22), channel_id=1, source_target_pairs={{0,24},{1,25},{2,26},{3,27},{4,28},{5,29},{6,30},{7,31},{8,9},{9,8... | collective-permute-start | bytes 589832 | tf_op jit(solution)/shard_map/late/ppermute | solution.py:32
  25.6 0.5 collective-permute-start.10
  26.1 1.3 %collective-permute-done.7.refs_0_ = bf16[48,2048]{1,0:T(8,128)(2,1)S(1)} collective-permute-done((bf16[48,2048]{1,0:T(8,128)(2,1)S(1)}, bf16[48,2048]{1,0:T(8,128)(2,1)S(1)}, u32[]{:S(2)}, u32[]{:S(2)}) %collective-permute-start.7) | collective-permute-done | bytes 196640 | tf_op jit(solution)/shard_map/late/ppermute | solution.py:495
  27.4 0.1 collective-permute-start.9
  27.6 0.0 copy-start
  27.6 0.0 copy-start.3
  27.6 1.4 %late.4.base = f32[48,2048]{1,0:T(8,128)S(1)} custom-call(s32[1,896]{1,0:T(1,128)S(4)} %get-tuple-element.16.plan, bf16[9,48,2048]{2,1,0:T(8,128)(2,1)S(1)} %get-tuple-element.20.panel_buf, bf16[512,128,128]{2,1,0:T(8,128)(2,1)S(1)} %get-tuple-element.18.refs_3_.tiles, f32[65,48,128]{2,1,0:T(8,128)S(1)} %get-tuple-element.17.refs_1_.refs_4_.early, ...), custom_call_target="tpu_custom_call" | custom-call | flops 48 | bytes 1 | tf_op jit(solution)/shard_map/late/pallas_call | solution.py:506
  29.0 4.8 %collective-permute-done.8.refs_1_ = bf16[48,2048]{1,0:T(8,128)(2,1)S(1)} collective-permute-done((bf16[48,2048]{1,0:T(8,128)(2,1)S(1)}, bf16[48,2048]{1,0:T(8,128)(2,1)S(1)}, u32[]{:S(2)}, u32[]{:S(2)}) %collective-permute-start.8) | collective-permute-done | bytes 196640 | tf_op jit(solution)/shard_map/late/ppermute | solution.py:32
  33.8 2.1 %collective-permute-done.10.refs_3_ = bf16[48,2048]{1,0:T(8,128)(2,1)S(1)} collective-permute-done((bf16[48,2048]{1,0:T(8,128)(2,1)S(1)}, bf16[48,2048]{1,0:T(8,128)(2,1)S(1)}, u32[]{:S(2)}, u32[]{:S(2)}) %collective-permute-start.10) | collective-permute-done | bytes 196640 | tf_op jit(solution)/shard_map/late/ppermute | solution.py:21
  35.9 0.0 collective-permute-done.9.refs_2_
  35.9 0.7 coefficients.2
  36.6 0.1 collective-permute-start.11
  36.7 0.7 %coefficients.3 = f32[12,8,128]{2,1,0:T(8,128)S(1)} custom-call(s32[1,896]{1,0:T(1,128)S(4)} %get-tuple-element.16.plan, f32[48,2048]{1,0:T(8,128)S(1)} %get-tuple-element.25.recurrence, f32[1,2048]{1,0:T(1,128)S(1)} %bitcast.13, f32[48,2048]{1,0:T(8,128)S(1)} %copy-done.1, f32[384,2048]{1,0:T(8,128)S(1)} %bitcast.9), custom_call_target="tpu_custom_call" | custom-call | flops 48 | bytes 1 | tf_op jit(solution)/shard_map/coefficients/pallas_call | solution.py:528
  37.4 0.5 collective-permute-done.11
  37.9 3.0 %collective-permute-start.14 = (f32[12,8,128]{2,1,0:T(8,128)S(1)}, f32[12,8,128]{2,1,0:T(8,128)S(1)}, u32[]{:S(2)}, u32[]{:S(2)}) collective-permute-start(f32[12,8,128]{2,1,0:T(8,128)S(1)} %add.46), channel_id=1, source_target_pairs={{0,6},{1,7},{2,4},{3,5},{4,2},{5,3},{6,0},{7,1},{8,14},{9,15},{10,... | collective-permute-start | bytes 147464 | tf_op jit(solution)/shard_map/coefficients/ppermute | solution.py:21
  41.0 0.0 collective-permute-start.13
  41.0 0.6 collective-permute-start.12
  41.6 1.4 %collective-permute-done.14 = f32[12,8,128]{2,1,0:T(8,128)S(1)} collective-permute-done((f32[12,8,128]{2,1,0:T(8,128)S(1)}, f32[12,8,128]{2,1,0:T(8,128)S(1)}, u32[]{:S(2)}, u32[]{:S(2)}) %collective-permute-start.14) | collective-permute-done | bytes 49184 | tf_op jit(solution)/shard_map/coefficients/ppermute | solution.py:21
  43.1 2.0 %collective-permute-done.13 = f32[12,8,128]{2,1,0:T(8,128)S(1)} collective-permute-done((f32[12,8,128]{2,1,0:T(8,128)S(1)}, f32[12,8,128]{2,1,0:T(8,128)S(1)}, u32[]{:S(2)}, u32[]{:S(2)}) %collective-permute-start.13) | collective-permute-done | bytes 49184 | tf_op jit(solution)/shard_map/coefficients/ppermute | solution.py:21
  45.1 0.0 collective-permute-done.12
  45.1 2.6 %collective-permute-start.17 = (f32[12,8,128]{2,1,0:T(8,128)S(1)}, f32[12,8,128]{2,1,0:T(8,128)S(1)}, u32[]{:S(2)}, u32[]{:S(2)}) collective-permute-start(f32[12,8,128]{2,1,0:T(8,128)S(1)} %add_add_fusion.1), channel_id=1, source_target_pairs={{0,24},{8,16},{16,8},{24,0},{1,25},{9,17},{17,9},{25,1},{2,26},{10... | collective-permute-start | bytes 147464 | tf_op jit(solution)/shard_map/coefficients/ppermute | solution.py:21
  47.7 0.0 collective-permute-start.16
  47.7 1.8 %collective-permute-start.15 = (f32[12,8,128]{2,1,0:T(8,128)S(1)}, f32[12,8,128]{2,1,0:T(8,128)S(1)}, u32[]{:S(2)}, u32[]{:S(2)}) collective-permute-start(f32[12,8,128]{2,1,0:T(8,128)S(1)} %add_add_fusion.1), channel_id=1, source_target_pairs={{0,8},{8,0},{16,24},{24,16},{1,9},{9,1},{17,25},{25,17},{2,10},{10... | collective-permute-start | bytes 147464 | tf_op jit(solution)/shard_map/coefficients/ppermute | solution.py:21
  49.6 1.5 %collective-permute-done.17 = f32[12,8,128]{2,1,0:T(8,128)S(1)} collective-permute-done((f32[12,8,128]{2,1,0:T(8,128)S(1)}, f32[12,8,128]{2,1,0:T(8,128)S(1)}, u32[]{:S(2)}, u32[]{:S(2)}) %collective-permute-start.17) | collective-permute-done | bytes 49184 | tf_op jit(solution)/shard_map/coefficients/ppermute | solution.py:21
  51.1 1.7 %collective-permute-done.16 = f32[12,8,128]{2,1,0:T(8,128)S(1)} collective-permute-done((f32[12,8,128]{2,1,0:T(8,128)S(1)}, f32[12,8,128]{2,1,0:T(8,128)S(1)}, u32[]{:S(2)}, u32[]{:S(2)}) %collective-permute-start.16) | collective-permute-done | bytes 49184 | tf_op jit(solution)/shard_map/coefficients/ppermute | solution.py:21
  52.8 0.0 collective-permute-done.15
  52.8 0.1 collective-permute-start.18
  52.9 0.6 residual.4.less
  53.5 0.6 collective-permute-done.18.other
  54.1 0.9 %residual.5 = (f32[48,2048]{1,0:T(8,128)S(1)}, f32[24,128]{1,0:T(8,128)S(1)}) custom-call(s32[1,896]{1,0:T(1,128)S(4)} %get-tuple-element.16.plan, f32[12,8,128]{2,1,0:T(8,128)S(1)} %collective-permute-done.18.other, f32[48,2048]{1,0:T(8,128)S(1)} %residual.4.less, f32[1,2048]{1,0:T(1,128)S(1)} %bitcast.14, f32[48,2048]{1,0:T(8,128)S(1)} %copy-done.1, ...), custom_call_target="tpu_custom_call" | custom-call | flops 48 | bytes 1 | tf_op jit(solution)/shard_map/residual/pallas_call | solution.py:549
  55.0 0.2 collective-permute-start.19
  55.2 1.0 %collective-permute-done.19 = f32[24,128]{1,0:T(8,128)S(1)} collective-permute-done((f32[24,128]{1,0:T(8,128)S(1)}, f32[24,128]{1,0:T(8,128)S(1)}, u32[]{:S(2)}, u32[]{:S(2)}) %collective-permute-start.19) | collective-permute-done | bytes 12320 | tf_op jit(solution)/shard_map/gram/ppermute | solution.py:21
  56.2 2.0 %collective-permute-start.22 = (f32[24,128]{1,0:T(8,128)S(1)}, f32[24,128]{1,0:T(8,128)S(1)}, u32[]{:S(2)}, u32[]{:S(2)}) collective-permute-start(f32[24,128]{1,0:T(8,128)S(1)} %add.53), channel_id=1, source_target_pairs={{0,6},{1,7},{2,4},{3,5},{4,2},{5,3},{6,0},{7,1},{8,14},{9,15},{10,... | collective-permute-start | bytes 36872 | tf_op jit(solution)/shard_map/gram/ppermute | solution.py:21
  58.3 0.9 %collective-permute-start.21 = (f32[24,128]{1,0:T(8,128)S(1)}, f32[24,128]{1,0:T(8,128)S(1)}, u32[]{:S(2)}, u32[]{:S(2)}) collective-permute-start(f32[24,128]{1,0:T(8,128)S(1)} %add.53), channel_id=1, source_target_pairs={{0,4},{1,5},{2,6},{3,7},{4,0},{5,1},{6,2},{7,3},{8,12},{9,13},{10,... | collective-permute-start | bytes 36872 | tf_op jit(solution)/shard_map/gram/ppermute | solution.py:21
  59.2 0.5 collective-permute-start.20
  59.7 0.8 %residual.6.refs_1_ = f32[48,2048]{1,0:T(8,128)} custom-call(f32[48,2048]{1,0:T(8,128)S(1)} %get-tuple-element.27.value), custom_call_target="tpu_custom_call" | custom-call | flops 48 | bytes 1 | tf_op jit(solution)/shard_map/residual/pallas_call | solution.py:560
  60.5 0.8 %residual.7.refs_2_ = f32[432,48]{1,0:T(8,128)} custom-call(s32[1,896]{1,0:T(1,128)S(4)} %get-tuple-element.16.plan, f32[12,8,128]{2,1,0:T(8,128)S(1)} %add_add_fusion.mine, f32[12,8,128]{2,1,0:T(8,128)S(1)} %collective-permute-done.18.other), custom_call_target="tpu_custom_call" | custom-call | flops 48 | bytes 1 | tf_op jit(solution)/shard_map/residual/pallas_call | solution.py:569
  61.3 0.7 collective-permute-done.21
  62.0 0.9 %collective-permute-done.20 = f32[24,128]{1,0:T(8,128)S(1)} collective-permute-done((f32[24,128]{1,0:T(8,128)S(1)}, f32[24,128]{1,0:T(8,128)S(1)}, u32[]{:S(2)}, u32[]{:S(2)}) %collective-permute-start.20) | collective-permute-done | bytes 12320 | tf_op jit(solution)/shard_map/gram/ppermute | solution.py:21
  62.9 1.5 %collective-permute-start.25 = (f32[24,128]{1,0:T(8,128)S(1)}, f32[24,128]{1,0:T(8,128)S(1)}, u32[]{:S(2)}, u32[]{:S(2)}) collective-permute-start(f32[24,128]{1,0:T(8,128)S(1)} %gram.1), channel_id=1, source_target_pairs={{0,24},{8,16},{16,8},{24,0},{1,25},{9,17},{17,9},{25,1},{2,26},{10... | collective-permute-start | bytes 36872 | tf_op jit(solution)/shard_map/gram/ppermute | solution.py:21
  64.4 0.2 collective-permute-start.24
  64.6 2.7 %collective-permute-start.23 = (f32[24,128]{1,0:T(8,128)S(1)}, f32[24,128]{1,0:T(8,128)S(1)}, u32[]{:S(2)}, u32[]{:S(2)}) collective-permute-start(f32[24,128]{1,0:T(8,128)S(1)} %gram.1), channel_id=1, source_target_pairs={{0,8},{8,0},{16,24},{24,16},{1,9},{9,1},{17,25},{25,17},{2,10},{10... | collective-permute-start | bytes 36872 | tf_op jit(solution)/shard_map/gram/ppermute | solution.py:21
  67.3 1.1 %collective-permute-done.25 = f32[24,128]{1,0:T(8,128)S(1)} collective-permute-done((f32[24,128]{1,0:T(8,128)S(1)}, f32[24,128]{1,0:T(8,128)S(1)}, u32[]{:S(2)}, u32[]{:S(2)}) %collective-permute-start.25) | collective-permute-done | bytes 12320 | tf_op jit(solution)/shard_map/gram/ppermute | solution.py:21
  68.4 0.7 %collective-permute-done.24 = f32[24,128]{1,0:T(8,128)S(1)} collective-permute-done((f32[24,128]{1,0:T(8,128)S(1)}, f32[24,128]{1,0:T(8,128)S(1)}, u32[]{:S(2)}, u32[]{:S(2)}) %collective-permute-start.24) | collective-permute-done | bytes 12320 | tf_op jit(solution)/shard_map/gram/ppermute | solution.py:21
  69.1 0.1 fusion
  69.2 0.6 pad_maximum_fusion
  (26 shorter events, 0.1 us)
Async XLA Ops:
  1.7 5.4 %collective-permute-start = (bf16[48,2048]{1,0:T(8,128)(2,1)S(1)}, bf16[48,2048]{1,0:T(8,128)(2,1)S(1)}, u32[]{:S(2)}, u32[]{:S(2)}) collective-permute-start(bf16[48,2048]{1,0:T(8,128)(2,1)S(1)} %convert_element_type.9.own_panel), channel_id=1, source_target_pairs={{0,1},{1,0},{2,3},{3,2},{4,5},{5,4},{6,7},{7,6},{8,9},{9,8},{10,11... | collective-permute-start | bytes 589832 | tf_op jit(solution)/shard_map/gather/ppermute | solution.py:21
  2.2 9.6 %collective-permute-start.1 = (bf16[48,2048]{1,0:T(8,128)(2,1)S(1)}, bf16[48,2048]{1,0:T(8,128)(2,1)S(1)}, u32[]{:S(2)}, u32[]{:S(2)}) collective-permute-start(bf16[48,2048]{1,0:T(8,128)(2,1)S(1)} %convert_element_type.9.own_panel), channel_id=1, source_target_pairs={{0,2},{1,3},{2,0},{3,1},{4,6},{5,7},{6,4},{7,5},{8,10},{9,11},{10,... | collective-permute-start | bytes 589832 | tf_op jit(solution)/shard_map/gather/ppermute | solution.py:21
  4.7 11.2 %collective-permute-start.3 = (bf16[48,2048]{1,0:T(8,128)(2,1)S(1)}, bf16[48,2048]{1,0:T(8,128)(2,1)S(1)}, u32[]{:S(2)}, u32[]{:S(2)}) collective-permute-start(bf16[48,2048]{1,0:T(8,128)(2,1)S(1)} %convert_element_type.9.own_panel), channel_id=1, source_target_pairs={{0,4},{1,5},{2,6},{3,7},{4,0},{5,1},{6,2},{7,3},{8,12},{9,13},{10,... | collective-permute-start | bytes 589832 | tf_op jit(solution)/shard_map/gather/ppermute | solution.py:21
  6.3 9.7 %collective-permute-start.5 = (bf16[48,2048]{1,0:T(8,128)(2,1)S(1)}, bf16[48,2048]{1,0:T(8,128)(2,1)S(1)}, u32[]{:S(2)}, u32[]{:S(2)}) collective-permute-start(bf16[48,2048]{1,0:T(8,128)(2,1)S(1)} %convert_element_type.9.own_panel), channel_id=1, source_target_pairs={{0,6},{1,7},{2,4},{3,5},{4,2},{5,3},{6,0},{7,1},{8,14},{9,15},{10,... | collective-permute-start | bytes 589832 | tf_op jit(solution)/shard_map/gather/ppermute | solution.py:21
  11.8 5.4 %collective-permute-start.2 = (bf16[48,2048]{1,0:T(8,128)(2,1)S(1)}, bf16[48,2048]{1,0:T(8,128)(2,1)S(1)}, u32[]{:S(2)}, u32[]{:S(2)}) collective-permute-start(bf16[48,2048]{1,0:T(8,128)(2,1)S(1)} %gather.4.refs_0_), channel_id=1, source_target_pairs={{0,1},{1,0},{2,3},{3,2},{4,5},{5,4},{6,7},{7,6},{8,9},{9,8},{10,11... | collective-permute-start | bytes 589832 | tf_op jit(solution)/shard_map/gather/ppermute | solution.py:21
  15.9 1.4 %collective-permute-start.4 = (bf16[48,2048]{1,0:T(8,128)(2,1)S(1)}, bf16[48,2048]{1,0:T(8,128)(2,1)S(1)}, u32[]{:S(2)}, u32[]{:S(2)}) collective-permute-start(bf16[48,2048]{1,0:T(8,128)(2,1)S(1)} %gather.5.refs_1_), channel_id=1, source_target_pairs={{0,1},{1,0},{2,3},{3,2},{4,5},{5,4},{6,7},{7,6},{8,9},{9,8},{10,11... | collective-permute-start | bytes 589832 | tf_op jit(solution)/shard_map/gather/ppermute | solution.py:21
  15.9 1.7 %collective-permute-start.6 = (bf16[48,2048]{1,0:T(8,128)(2,1)S(1)}, bf16[48,2048]{1,0:T(8,128)(2,1)S(1)}, u32[]{:S(2)}, u32[]{:S(2)}) collective-permute-start(bf16[48,2048]{1,0:T(8,128)(2,1)S(1)} %gather.6.refs_2_), channel_id=1, source_target_pairs={{0,1},{1,0},{2,3},{3,2},{4,5},{5,4},{6,7},{7,6},{8,9},{9,8},{10,11... | collective-permute-start | bytes 589832 | tf_op jit(solution)/shard_map/gather/ppermute | solution.py:21
  19.4 8.0 %collective-permute-start.7 = (bf16[48,2048]{1,0:T(8,128)(2,1)S(1)}, bf16[48,2048]{1,0:T(8,128)(2,1)S(1)}, u32[]{:S(2)}, u32[]{:S(2)}) collective-permute-start(bf16[48,2048]{1,0:T(8,128)(2,1)S(1)} %get-tuple-element.21), channel_id=1, source_target_pairs={{0,8},{24,16},{8,24},{16,0},{1,9},{25,17},{9,25},{17,1},{2,10},{26... | collective-permute-start | bytes 589832 | tf_op jit(solution)/shard_map/late/ppermute | solution.py:495
  21.7 5.9 %copy-start.1 = (f32[48,2048]{1,0:T(8,128)S(1)}, f32[48,2048]{1,0:T(8,128)}, u32[]{:S(2)}) copy-start(f32[48,2048]{1,0:T(8,128)} %current.7) | copy-start | bytes 1179652
  21.7 5.9 %copy-start.2 = (f32[48,2048]{1,0:T(8,128)S(1)}, f32[48,2048]{1,0:T(8,128)}, u32[]{:S(2)}) copy-start(f32[48,2048]{1,0:T(8,128)} %previous.1) | copy-start | bytes 1179652
  21.7 5.9 %copy-start.4 = (f32[48,48]{1,0:T(8,128)S(1)}, f32[48,48]{1,0:T(8,128)}, u32[]{:S(2)}) copy-start(f32[48,48]{1,0:T(8,128)} %coupling.1) | copy-start | bytes 27652
  21.7 5.9 %copy-start.5 = (f32[2048]{0:T(1024)S(1)}, f32[2048]{0:T(1024)}, u32[]{:S(2)}) copy-start(f32[2048]{0:T(1024)} %param.14) | copy-start | bytes 24580
  23.4 10.5 %collective-permute-start.8 = (bf16[48,2048]{1,0:T(8,128)(2,1)S(1)}, bf16[48,2048]{1,0:T(8,128)(2,1)S(1)}, u32[]{:S(2)}, u32[]{:S(2)}) collective-permute-start(bf16[48,2048]{1,0:T(8,128)(2,1)S(1)} %get-tuple-element.22), channel_id=1, source_target_pairs={{0,24},{1,25},{2,26},{3,27},{4,28},{5,29},{6,30},{7,31},{8,9},{9,8... | collective-permute-start | bytes 589832 | tf_op jit(solution)/shard_map/late/ppermute | solution.py:32
  25.6 10.3 %collective-permute-start.10 = (bf16[48,2048]{1,0:T(8,128)(2,1)S(1)}, bf16[48,2048]{1,0:T(8,128)(2,1)S(1)}, u32[]{:S(2)}, u32[]{:S(2)}) collective-permute-start(bf16[48,2048]{1,0:T(8,128)(2,1)S(1)} %get-tuple-element.24), channel_id=1, source_target_pairs={{0,8},{8,0},{16,24},{24,16},{1,9},{9,1},{17,25},{25,17},{2,10},{10... | collective-permute-start | bytes 589832 | tf_op jit(solution)/shard_map/late/ppermute | solution.py:21
  27.4 8.5 %collective-permute-start.9 = (bf16[48,2048]{1,0:T(8,128)(2,1)S(1)}, bf16[48,2048]{1,0:T(8,128)(2,1)S(1)}, u32[]{:S(2)}, u32[]{:S(2)}) collective-permute-start(bf16[48,2048]{1,0:T(8,128)(2,1)S(1)} %add_convert_fusion), channel_id=1, source_target_pairs={{0,1},{1,0},{2,3},{3,2},{4,5},{5,4},{6,7},{7,6},{8,16},{9,17},{10,... | collective-permute-start | bytes 589832 | tf_op jit(solution)/shard_map/late/ppermute | solution.py:32
  27.6 8.4 %copy-start = (f32[8,48,2048]{2,1,0:T(8,128)S(1)}, f32[8,48,2048]{2,1,0:T(8,128)}, u32[]{:S(2)}) copy-start(f32[8,48,2048]{2,1,0:T(8,128)} %param.13) | copy-start | bytes 9437188
  27.6 8.4 %copy-start.3 = (f32[2048]{0:T(1024)S(1)}, f32[2048]{0:T(1024)}, u32[]{:S(2)}) copy-start(f32[2048]{0:T(1024)} %param.15) | copy-start | bytes 24580
  36.6 1.3 %collective-permute-start.11 = (f32[12,8,128]{2,1,0:T(8,128)S(1)}, f32[12,8,128]{2,1,0:T(8,128)S(1)}, u32[]{:S(2)}, u32[]{:S(2)}) collective-permute-start(f32[12,8,128]{2,1,0:T(8,128)S(1)} %get-tuple-element.26), channel_id=1, source_target_pairs={{0,1},{1,0},{2,3},{3,2},{4,5},{5,4},{6,7},{7,6},{8,9},{9,8},{10,11... | collective-permute-start | bytes 147464 | tf_op jit(solution)/shard_map/coefficients/ppermute | solution.py:21
  37.9 5.1 %collective-permute-start.14 = (f32[12,8,128]{2,1,0:T(8,128)S(1)}, f32[12,8,128]{2,1,0:T(8,128)S(1)}, u32[]{:S(2)}, u32[]{:S(2)}) collective-permute-start(f32[12,8,128]{2,1,0:T(8,128)S(1)} %add.46), channel_id=1, source_target_pairs={{0,6},{1,7},{2,4},{3,5},{4,2},{5,3},{6,0},{7,1},{8,14},{9,15},{10,... | collective-permute-start | bytes 147464 | tf_op jit(solution)/shard_map/coefficients/ppermute | solution.py:21
  41.0 4.1 %collective-permute-start.13 = (f32[12,8,128]{2,1,0:T(8,128)S(1)}, f32[12,8,128]{2,1,0:T(8,128)S(1)}, u32[]{:S(2)}, u32[]{:S(2)}) collective-permute-start(f32[12,8,128]{2,1,0:T(8,128)S(1)} %add.46), channel_id=1, source_target_pairs={{0,4},{1,5},{2,6},{3,7},{4,0},{5,1},{6,2},{7,3},{8,12},{9,13},{10,... | collective-permute-start | bytes 147464 | tf_op jit(solution)/shard_map/coefficients/ppermute | solution.py:21
  41.0 4.1 %collective-permute-start.12 = (f32[12,8,128]{2,1,0:T(8,128)S(1)}, f32[12,8,128]{2,1,0:T(8,128)S(1)}, u32[]{:S(2)}, u32[]{:S(2)}) collective-permute-start(f32[12,8,128]{2,1,0:T(8,128)S(1)} %add.46), channel_id=1, source_target_pairs={{0,2},{1,3},{2,0},{3,1},{4,6},{5,7},{6,4},{7,5},{8,10},{9,11},{10,... | collective-permute-start | bytes 147464 | tf_op jit(solution)/shard_map/coefficients/ppermute | solution.py:21
  45.1 6.0 %collective-permute-start.17 = (f32[12,8,128]{2,1,0:T(8,128)S(1)}, f32[12,8,128]{2,1,0:T(8,128)S(1)}, u32[]{:S(2)}, u32[]{:S(2)}) collective-permute-start(f32[12,8,128]{2,1,0:T(8,128)S(1)} %add_add_fusion.1), channel_id=1, source_target_pairs={{0,24},{8,16},{16,8},{24,0},{1,25},{9,17},{17,9},{25,1},{2,26},{10... | collective-permute-start | bytes 147464 | tf_op jit(solution)/shard_map/coefficients/ppermute | solution.py:21
  47.7 5.1 %collective-permute-start.16 = (f32[12,8,128]{2,1,0:T(8,128)S(1)}, f32[12,8,128]{2,1,0:T(8,128)S(1)}, u32[]{:S(2)}, u32[]{:S(2)}) collective-permute-start(f32[12,8,128]{2,1,0:T(8,128)S(1)} %add_add_fusion.1), channel_id=1, source_target_pairs={{0,16},{8,24},{16,0},{24,8},{1,17},{9,25},{17,1},{25,9},{2,18},{10... | collective-permute-start | bytes 147464 | tf_op jit(solution)/shard_map/coefficients/ppermute | solution.py:21
  47.7 5.1 %collective-permute-start.15 = (f32[12,8,128]{2,1,0:T(8,128)S(1)}, f32[12,8,128]{2,1,0:T(8,128)S(1)}, u32[]{:S(2)}, u32[]{:S(2)}) collective-permute-start(f32[12,8,128]{2,1,0:T(8,128)S(1)} %add_add_fusion.1), channel_id=1, source_target_pairs={{0,8},{8,0},{16,24},{24,16},{1,9},{9,1},{17,25},{25,17},{2,10},{10... | collective-permute-start | bytes 147464 | tf_op jit(solution)/shard_map/coefficients/ppermute | solution.py:21
  52.8 1.3 %collective-permute-start.18 = (f32[12,8,128]{2,1,0:T(8,128)S(1)}, f32[12,8,128]{2,1,0:T(8,128)S(1)}, u32[]{:S(2)}, u32[]{:S(2)}) collective-permute-start(f32[12,8,128]{2,1,0:T(8,128)S(1)} %add_add_fusion.mine), channel_id=1, source_target_pairs={{0,1},{1,0},{2,3},{3,2},{4,5},{5,4},{6,7},{7,6},{8,9},{9,8},{10,11... | collective-permute-start | bytes 147464 | tf_op jit(solution)/shard_map/coefficients/ppermute | solution.py:21
  55.0 1.2 %collective-permute-start.19 = (f32[24,128]{1,0:T(8,128)S(1)}, f32[24,128]{1,0:T(8,128)S(1)}, u32[]{:S(2)}, u32[]{:S(2)}) collective-permute-start(f32[24,128]{1,0:T(8,128)S(1)} %get-tuple-element.28), channel_id=1, source_target_pairs={{0,1},{1,0},{2,3},{3,2},{4,5},{5,4},{6,7},{7,6},{8,9},{9,8},{10,11... | collective-permute-start | bytes 36872 | tf_op jit(solution)/shard_map/gram/ppermute | solution.py:21
  56.2 5.1 %collective-permute-start.22 = (f32[24,128]{1,0:T(8,128)S(1)}, f32[24,128]{1,0:T(8,128)S(1)}, u32[]{:S(2)}, u32[]{:S(2)}) collective-permute-start(f32[24,128]{1,0:T(8,128)S(1)} %add.53), channel_id=1, source_target_pairs={{0,6},{1,7},{2,4},{3,5},{4,2},{5,3},{6,0},{7,1},{8,14},{9,15},{10,... | collective-permute-start | bytes 36872 | tf_op jit(solution)/shard_map/gram/ppermute | solution.py:21
  58.3 3.7 %collective-permute-start.21 = (f32[24,128]{1,0:T(8,128)S(1)}, f32[24,128]{1,0:T(8,128)S(1)}, u32[]{:S(2)}, u32[]{:S(2)}) collective-permute-start(f32[24,128]{1,0:T(8,128)S(1)} %add.53), channel_id=1, source_target_pairs={{0,4},{1,5},{2,6},{3,7},{4,0},{5,1},{6,2},{7,3},{8,12},{9,13},{10,... | collective-permute-start | bytes 36872 | tf_op jit(solution)/shard_map/gram/ppermute | solution.py:21
  59.2 3.7 %collective-permute-start.20 = (f32[24,128]{1,0:T(8,128)S(1)}, f32[24,128]{1,0:T(8,128)S(1)}, u32[]{:S(2)}, u32[]{:S(2)}) collective-permute-start(f32[24,128]{1,0:T(8,128)S(1)} %add.53), channel_id=1, source_target_pairs={{0,2},{1,3},{2,0},{3,1},{4,6},{5,7},{6,4},{7,5},{8,10},{9,11},{10,... | collective-permute-start | bytes 36872 | tf_op jit(solution)/shard_map/gram/ppermute | solution.py:21
  62.9 5.5 %collective-permute-start.25 = (f32[24,128]{1,0:T(8,128)S(1)}, f32[24,128]{1,0:T(8,128)S(1)}, u32[]{:S(2)}, u32[]{:S(2)}) collective-permute-start(f32[24,128]{1,0:T(8,128)S(1)} %gram.1), channel_id=1, source_target_pairs={{0,24},{8,16},{16,8},{24,0},{1,25},{9,17},{17,9},{25,1},{2,26},{10... | collective-permute-start | bytes 36872 | tf_op jit(solution)/shard_map/gram/ppermute | solution.py:21
  64.4 4.7 %collective-permute-start.24 = (f32[24,128]{1,0:T(8,128)S(1)}, f32[24,128]{1,0:T(8,128)S(1)}, u32[]{:S(2)}, u32[]{:S(2)}) collective-permute-start(f32[24,128]{1,0:T(8,128)S(1)} %gram.1), channel_id=1, source_target_pairs={{0,16},{8,24},{16,0},{24,8},{1,17},{9,25},{17,1},{25,9},{2,18},{10... | collective-permute-start | bytes 36872 | tf_op jit(solution)/shard_map/gram/ppermute | solution.py:21
  64.6 4.5 %collective-permute-start.23 = (f32[24,128]{1,0:T(8,128)S(1)}, f32[24,128]{1,0:T(8,128)S(1)}, u32[]{:S(2)}, u32[]{:S(2)}) collective-permute-start(f32[24,128]{1,0:T(8,128)S(1)} %gram.1), channel_id=1, source_target_pairs={{0,8},{8,0},{16,24},{24,16},{1,9},{9,1},{17,25},{25,17},{2,10},{10... | collective-permute-start | bytes 36872 | tf_op jit(solution)/shard_map/gram/ppermute | solution.py:21

commit v21 on v20

--- a/solution.py
+++ b/solution.py
@@ -293,9 +293,9 @@
     total = base[...]
     for i, ref in enumerate(received):
         value = ref[...].astype(jnp.float32)
-        if relay and i < 3:
+        if relay and i != 1:
             inner = (row_of(plan) == 1) | (row_of(plan) == 2)
-            value = jnp.where(inner if i < 2 else jnp.logical_not(inner), 0.0, value)
+            value = jnp.where(jnp.logical_not(inner) if i == 2 else inner, 0.0, value)
         total = total + value
     recurrence[...] = total
     weighted = total * (mass[...] * (1.0 / cells))
@@ -496,9 +496,9 @@
             joined = (parts[1] + first.astype(f32)).astype(bf16)
             received = [
                 first,
+                swap(parts[2], "row", 1),
+                trade_rows(joined, [(1, 2), (2, 1)]),
                 trade_rows(parts[0], [(0, 3), (3, 0)]),
-                trade_rows(joined, [(1, 2), (2, 1)]),
-                swap(parts[2], "row", 1),
             ]
         else:
             received = [swap(first, "row", first_mask)]

time: 70 us -> 71.1 us (1.016)
  Pallas kernels: 14.9 us -> 16.7 us
  starting transfers between devices: 26.6 us -> 25.8 us
    ppermute x23, starting transfers between devices: 22 us -> 24.5 us  [swap(): return lax.ppermute(value, axis, [(i, i ^ mask) for i in range(count)])]
    ppermute x2, starting transfers between devices: 2.3 us -> 0.59 us  [trade_rows(): return lax.ppermute(value, ('row', 'col'), trades)]
    ppermute x1, starting transfers between devices: 2.25 us -> 0.71 us  [local(): first = lax.ppermute(first, 'row', [(0, 1), (3, 2), (1, 3), (2, 0)])]
    pallas_call x1, Pallas kernels: 4.78 us -> 5.69 us  [local(): pl.pallas_call(functools.partial(early_kernel, row_devs, col_devs, slab_t...]
  transfers between devices with their start and end apart: 26 -> 26, of which waited for: 17 -> 18; matrix products, arithmetic and copies ran while one was open for 0% -> 0% of each run, Pallas kernels for 16% -> 18%
where the time goes in v21:
time: 71.1 us; the launch traced here: 71.2 us
  starting transfers between devices  25.8 us (36%)
  waiting for transfers between devices  25.3 us (36%)
  Pallas kernels  16.7 us (23%)
  other arithmetic  1.8 us (3%)
  between operations  1.51 us (2%)
    ppermute x23, starting transfers between devices, swap(): return lax.ppermute(value, axis, [(i, i ^ mask) for i in range(count)])  24.5 us
    ppermute x23, waiting for transfers between devices, swap(): return lax.ppermute(value, axis, [(i, i ^ mask) for i in range(count)])  18.5 us
    pallas_call x1, Pallas kernels, local(): pl.pallas_call(functools.partial(early_kernel, row_devs, col_devs, slab_t...  5.69 us
    ppermute x2, waiting for transfers between devices, trade_rows(): return lax.ppermute(value, ('row', 'col'), trades)  5.28 us
    pallas_call x1, Pallas kernels, local(): pl.pallas_call(functools.partial(first_late_kernel, [first_mask], odd), o...  2.37 us
    pallas_call x1, Pallas kernels, local(): pl.pallas_call(functools.partial(late_kernel, masks), out_shape=[part, sl...  1.99 us
    ppermute x1, waiting for transfers between devices, local(): first = lax.ppermute(first, 'row', [(0, 1), (3, 2), (1, 3), (2, 0)])  1.54 us
    pallas_call x1, Pallas kernels, local(): pl.pallas_call(own_kernel, out_shape=slab, in_specs=smem(1) + vmem(7), ou...  1.42 us
  transfers between devices with their start and end apart: 26, of which 18 were waited for; matrix products, arithmetic and copies ran while one was open for 0% of the time, Pallas kernels for 18%

profile of v21, /device:TPU:0, one launch (start us, length us, event | category | flops | bytes accessed | tf_op | source)
XLA Modules:
  0.0 71.2 jit_solution(14786799544465657324)
XLA Ops:
  0.6 1.0 %convert_element_type.9.own_panel = bf16[48,2048]{1,0:T(8,128)(2,1)S(1)} convert(f32[48,2048]{1,0:T(8,128)} %current.7) | non-fusion elementwise | flops 98304 | bytes 589824 | tf_op jit(solution)/shard_map/gather/convert_element_type | solution.py:415
  1.7 0.5 collective-permute-start
  2.2 2.6 %collective-permute-start.1 = (bf16[48,2048]{1,0:T(8,128)(2,1)S(1)}, bf16[48,2048]{1,0:T(8,128)(2,1)S(1)}, u32[]{:S(2)}, u32[]{:S(2)}) collective-permute-start(bf16[48,2048]{1,0:T(8,128)(2,1)S(1)} %convert_element_type.9.own_panel), channel_id=1, source_target_pairs={{0,2},{1,3},{2,0},{3,1},{4,6},{5,7},{6,4},{7,5},{8,10},{9,11},{10,... | collective-permute-start | bytes 589832 | tf_op jit(solution)/shard_map/gather/ppermute | solution.py:21
  4.7 1.5 %collective-permute-start.3 = (bf16[48,2048]{1,0:T(8,128)(2,1)S(1)}, bf16[48,2048]{1,0:T(8,128)(2,1)S(1)}, u32[]{:S(2)}, u32[]{:S(2)}) collective-permute-start(bf16[48,2048]{1,0:T(8,128)(2,1)S(1)} %convert_element_type.9.own_panel), channel_id=1, source_target_pairs={{0,4},{1,5},{2,6},{3,7},{4,0},{5,1},{6,2},{7,3},{8,12},{9,13},{10,... | collective-permute-start | bytes 589832 | tf_op jit(solution)/shard_map/gather/ppermute | solution.py:21
  6.3 0.0 collective-permute-start.5
  6.9 0.1 pad_add_fusion.place
  7.0 5.7 %early.1 = (s32[1,896]{1,0:T(1,128)S(4)}, bf16[512,128,128]{2,1,0:T(8,128)(2,1)S(1)}, f32[65,48,128]{2,1,0:T(8,128)S(1)}, bf16[9,48,2048]{2,1,0:T(8,128)(2,1)S(1)}) custom-call(s32[2]{0:T(128)S(1)} %pad_add_fusion.place, s32[1]{0:T(128)S(6)} %copy.25.counts, s32[1,512]{1,0:T(1,128)} %bitcast.17, s32[1,512]{1,0:T(1,128)} %bitcast.18, ...), custom_call_target="tpu_custom_call" | custom-call | flops 805306368 | bytes 16777216 | tf_op jit(solution)/shard_map/early/pallas_call | solution.py:424
  12.7 0.0 collective-permute-done.1.refs_0_
  12.7 0.1 collective-permute-start.2
  12.8 3.1 %collective-permute-done.3.refs_0_ = bf16[48,2048]{1,0:T(8,128)(2,1)S(1)} collective-permute-done((bf16[48,2048]{1,0:T(8,128)(2,1)S(1)}, bf16[48,2048]{1,0:T(8,128)(2,1)S(1)}, u32[]{:S(2)}, u32[]{:S(2)}) %collective-permute-start.3) | collective-permute-done | bytes 196640 | tf_op jit(solution)/shard_map/gather/ppermute | solution.py:21
  15.9 0.5 collective-permute-start.6
  16.4 0.8 %gather.7.refs_5_ = bf16[9,48,2048]{2,1,0:T(8,128)(2,1)S(1)} custom-call(bf16[48,2048]{1,0:T(8,128)(2,1)S(1)} %gather.4.refs_0_, bf16[48,2048]{1,0:T(8,128)(2,1)S(1)} %gather.5.refs_1_, bf16[48,2048]{1,0:T(8,128)(2,1)S(1)} %gather.6.refs_2_, bf16[9,48,2048]{2,1,0:T(8,128)(2,1)S(1)} %get-tuple-element.19.refs_3_), custom_call_target="tpu_custom_call", output_to_operand_aliasing={{}: (3, {})} | custom-call | flops 48 | bytes 1 | tf_op jit(solution)/shard_map/gather/pallas_call | solution.py:459
  17.2 0.2 collective-permute-done.4.refs_1_
  17.4 0.3 collective-permute-done.6.refs_2_
  17.6 2.4 %late.3 = (bf16[48,2048]{1,0:T(8,128)(2,1)S(1)}, bf16[9,48,2048]{2,1,0:T(8,128)(2,1)S(1)}) custom-call(s32[1,896]{1,0:T(1,128)S(4)} %get-tuple-element.16.plan, bf16[48,2048]{1,0:T(8,128)(2,1)S(1)} %collective-permute-done.2.refs_0_, bf16[48,2048]{1,0:T(8,128)(2,1)S(1)} %collective-permute-done.4.refs_1_, ...), custom_call_target="tpu_custom_call", output_to_operand_aliasing={{1}: (6, {})} | custom-call | flops 48 | bytes 1 | tf_op jit(solution)/shard_map/late/pallas_call | solution.py:475
  20.0 0.7 %collective-permute-start.7 = (bf16[48,2048]{1,0:T(8,128)(2,1)S(1)}, bf16[48,2048]{1,0:T(8,128)(2,1)S(1)}, u32[]{:S(2)}, u32[]{:S(2)}) collective-permute-start(bf16[48,2048]{1,0:T(8,128)(2,1)S(1)} %get-tuple-element.21), channel_id=1, source_target_pairs={{0,8},{24,16},{8,24},{16,0},{1,9},{25,17},{9,25},{17,1},{2,10},{26... | collective-permute-start | bytes 589832 | tf_op jit(solution)/shard_map/late/ppermute | solution.py:495
  20.7 2.0 %late.5 = (bf16[48,2048]{1,0:T(8,128)(2,1)S(1)}, f32[48,2048]{1,0:T(8,128)S(1)}, bf16[48,2048]{1,0:T(8,128)(2,1)S(1)}) custom-call(s32[1,896]{1,0:T(1,128)S(4)} %get-tuple-element.16.plan, bf16[9,48,2048]{2,1,0:T(8,128)(2,1)S(1)} %get-tuple-element.20.panel_buf, bf16[512,128,128]{2,1,0:T(8,128)(2,1)S(1)} %get-tuple-element.18.refs_3_.tiles, ...), custom_call_target="tpu_custom_call" | custom-call | flops 48 | bytes 1 | tf_op jit(solution)/shard_map/late/pallas_call | solution.py:485
  22.7 3.0 %collective-permute-start.8 = (bf16[48,2048]{1,0:T(8,128)(2,1)S(1)}, bf16[48,2048]{1,0:T(8,128)(2,1)S(1)}, u32[]{:S(2)}, u32[]{:S(2)}) collective-permute-start(bf16[48,2048]{1,0:T(8,128)(2,1)S(1)} %get-tuple-element.22), channel_id=1, source_target_pairs={{0,8},{8,0},{16,24},{24,16},{1,9},{9,1},{17,25},{25,17},{2,10},{10... | collective-permute-start | bytes 589832 | tf_op jit(solution)/shard_map/late/ppermute | solution.py:21
  25.7 0.5 collective-permute-start.10
  26.2 1.5 %collective-permute-done.7.refs_0_ = bf16[48,2048]{1,0:T(8,128)(2,1)S(1)} collective-permute-done((bf16[48,2048]{1,0:T(8,128)(2,1)S(1)}, bf16[48,2048]{1,0:T(8,128)(2,1)S(1)}, u32[]{:S(2)}, u32[]{:S(2)}) %collective-permute-start.7) | collective-permute-done | bytes 196640 | tf_op jit(solution)/shard_map/late/ppermute | solution.py:495
  27.8 0.1 collective-permute-start.9
  27.9 0.0 copy-start
  27.9 0.0 copy-start.3
  28.0 1.4 %late.4.base = f32[48,2048]{1,0:T(8,128)S(1)} custom-call(s32[1,896]{1,0:T(1,128)S(4)} %get-tuple-element.16.plan, bf16[9,48,2048]{2,1,0:T(8,128)(2,1)S(1)} %get-tuple-element.20.panel_buf, bf16[512,128,128]{2,1,0:T(8,128)(2,1)S(1)} %get-tuple-element.18.refs_3_.tiles, f32[65,48,128]{2,1,0:T(8,128)S(1)} %get-tuple-element.17.refs_1_.refs_4_.early, ...), custom_call_target="tpu_custom_call" | custom-call | flops 48 | bytes 1 | tf_op jit(solution)/shard_map/late/pallas_call | solution.py:506
  29.4 2.5 %collective-permute-done.8.refs_1_ = bf16[48,2048]{1,0:T(8,128)(2,1)S(1)} collective-permute-done((bf16[48,2048]{1,0:T(8,128)(2,1)S(1)}, bf16[48,2048]{1,0:T(8,128)(2,1)S(1)}, u32[]{:S(2)}, u32[]{:S(2)}) %collective-permute-start.8) | collective-permute-done | bytes 196640 | tf_op jit(solution)/shard_map/late/ppermute | solution.py:21
  31.9 5.3 %collective-permute-done.10.refs_3_ = bf16[48,2048]{1,0:T(8,128)(2,1)S(1)} collective-permute-done((bf16[48,2048]{1,0:T(8,128)(2,1)S(1)}, bf16[48,2048]{1,0:T(8,128)(2,1)S(1)}, u32[]{:S(2)}, u32[]{:S(2)}) %collective-permute-start.10) | collective-permute-done | bytes 196640 | tf_op jit(solution)/shard_map/late/ppermute | solution.py:32
  37.2 0.7 coefficients.2
  37.9 0.1 collective-permute-start.11
  38.0 0.7 coefficients.3
  38.7 0.5 collective-permute-done.11
  39.2 1.1 %collective-permute-start.14 = (f32[12,8,128]{2,1,0:T(8,128)S(1)}, f32[12,8,128]{2,1,0:T(8,128)S(1)}, u32[]{:S(2)}, u32[]{:S(2)}) collective-permute-start(f32[12,8,128]{2,1,0:T(8,128)S(1)} %add.46), channel_id=1, source_target_pairs={{0,6},{1,7},{2,4},{3,5},{4,2},{5,3},{6,0},{7,1},{8,14},{9,15},{10,... | collective-permute-start | bytes 147464 | tf_op jit(solution)/shard_map/coefficients/ppermute | solution.py:21
  40.3 1.6 %collective-permute-start.13 = (f32[12,8,128]{2,1,0:T(8,128)S(1)}, f32[12,8,128]{2,1,0:T(8,128)S(1)}, u32[]{:S(2)}, u32[]{:S(2)}) collective-permute-start(f32[12,8,128]{2,1,0:T(8,128)S(1)} %add.46), channel_id=1, source_target_pairs={{0,4},{1,5},{2,6},{3,7},{4,0},{5,1},{6,2},{7,3},{8,12},{9,13},{10,... | collective-permute-start | bytes 147464 | tf_op jit(solution)/shard_map/coefficients/ppermute | solution.py:21
  42.0 0.8 %collective-permute-start.12 = (f32[12,8,128]{2,1,0:T(8,128)S(1)}, f32[12,8,128]{2,1,0:T(8,128)S(1)}, u32[]{:S(2)}, u32[]{:S(2)}) collective-permute-start(f32[12,8,128]{2,1,0:T(8,128)S(1)} %add.46), channel_id=1, source_target_pairs={{0,2},{1,3},{2,0},{3,1},{4,6},{5,7},{6,4},{7,5},{8,10},{9,11},{10,... | collective-permute-start | bytes 147464 | tf_op jit(solution)/shard_map/coefficients/ppermute | solution.py:21
  42.8 1.8 %collective-permute-done.14 = f32[12,8,128]{2,1,0:T(8,128)S(1)} collective-permute-done((f32[12,8,128]{2,1,0:T(8,128)S(1)}, f32[12,8,128]{2,1,0:T(8,128)S(1)}, u32[]{:S(2)}, u32[]{:S(2)}) %collective-permute-start.14) | collective-permute-done | bytes 49184 | tf_op jit(solution)/shard_map/coefficients/ppermute | solution.py:21
  44.6 0.2 collective-permute-done.13
  44.8 1.2 %collective-permute-done.12 = f32[12,8,128]{2,1,0:T(8,128)S(1)} collective-permute-done((f32[12,8,128]{2,1,0:T(8,128)S(1)}, f32[12,8,128]{2,1,0:T(8,128)S(1)}, u32[]{:S(2)}, u32[]{:S(2)}) %collective-permute-start.12) | collective-permute-done | bytes 49184 | tf_op jit(solution)/shard_map/coefficients/ppermute | solution.py:21
  46.1 2.6 %collective-permute-start.17 = (f32[12,8,128]{2,1,0:T(8,128)S(1)}, f32[12,8,128]{2,1,0:T(8,128)S(1)}, u32[]{:S(2)}, u32[]{:S(2)}) collective-permute-start(f32[12,8,128]{2,1,0:T(8,128)S(1)} %add_add_fusion.1), channel_id=1, source_target_pairs={{0,24},{8,16},{16,8},{24,0},{1,25},{9,17},{17,9},{25,1},{2,26},{10... | collective-permute-start | bytes 147464 | tf_op jit(solution)/shard_map/coefficients/ppermute | solution.py:21
  48.7 1.7 %collective-permute-start.16 = (f32[12,8,128]{2,1,0:T(8,128)S(1)}, f32[12,8,128]{2,1,0:T(8,128)S(1)}, u32[]{:S(2)}, u32[]{:S(2)}) collective-permute-start(f32[12,8,128]{2,1,0:T(8,128)S(1)} %add_add_fusion.1), channel_id=1, source_target_pairs={{0,16},{8,24},{16,0},{24,8},{1,17},{9,25},{17,1},{25,9},{2,18},{10... | collective-permute-start | bytes 147464 | tf_op jit(solution)/shard_map/coefficients/ppermute | solution.py:21
  50.4 0.3 collective-permute-start.15
  50.7 1.7 %collective-permute-done.17 = f32[12,8,128]{2,1,0:T(8,128)S(1)} collective-permute-done((f32[12,8,128]{2,1,0:T(8,128)S(1)}, f32[12,8,128]{2,1,0:T(8,128)S(1)}, u32[]{:S(2)}, u32[]{:S(2)}) %collective-permute-start.17) | collective-permute-done | bytes 49184 | tf_op jit(solution)/shard_map/coefficients/ppermute | solution.py:21
  52.4 1.3 %collective-permute-done.16 = f32[12,8,128]{2,1,0:T(8,128)S(1)} collective-permute-done((f32[12,8,128]{2,1,0:T(8,128)S(1)}, f32[12,8,128]{2,1,0:T(8,128)S(1)}, u32[]{:S(2)}, u32[]{:S(2)}) %collective-permute-start.16) | collective-permute-done | bytes 49184 | tf_op jit(solution)/shard_map/coefficients/ppermute | solution.py:21
  53.7 0.8 %collective-permute-done.15 = f32[12,8,128]{2,1,0:T(8,128)S(1)} collective-permute-done((f32[12,8,128]{2,1,0:T(8,128)S(1)}, f32[12,8,128]{2,1,0:T(8,128)S(1)}, u32[]{:S(2)}, u32[]{:S(2)}) %collective-permute-start.15) | collective-permute-done | bytes 49184 | tf_op jit(solution)/shard_map/coefficients/ppermute | solution.py:21
  54.5 0.1 collective-permute-start.18
  54.5 0.6 residual.4.less
  55.1 0.6 collective-permute-done.18.other
  55.8 0.9 %residual.5 = (f32[48,2048]{1,0:T(8,128)S(1)}, f32[24,128]{1,0:T(8,128)S(1)}) custom-call(s32[1,896]{1,0:T(1,128)S(4)} %get-tuple-element.16.plan, f32[12,8,128]{2,1,0:T(8,128)S(1)} %collective-permute-done.18.other, f32[48,2048]{1,0:T(8,128)S(1)} %residual.4.less, f32[1,2048]{1,0:T(1,128)S(1)} %bitcast.14, f32[48,2048]{1,0:T(8,128)S(1)} %copy-done.1, ...), custom_call_target="tpu_custom_call" | custom-call | flops 48 | bytes 1 | tf_op jit(solution)/shard_map/residual/pallas_call | solution.py:549
  56.7 0.2 collective-permute-start.19
  56.9 1.0 %collective-permute-done.19 = f32[24,128]{1,0:T(8,128)S(1)} collective-permute-done((f32[24,128]{1,0:T(8,128)S(1)}, f32[24,128]{1,0:T(8,128)S(1)}, u32[]{:S(2)}, u32[]{:S(2)}) %collective-permute-start.19) | collective-permute-done | bytes 12320 | tf_op jit(solution)/shard_map/gram/ppermute | solution.py:21
  57.9 1.2 %collective-permute-start.22 = (f32[24,128]{1,0:T(8,128)S(1)}, f32[24,128]{1,0:T(8,128)S(1)}, u32[]{:S(2)}, u32[]{:S(2)}) collective-permute-start(f32[24,128]{1,0:T(8,128)S(1)} %add.53), channel_id=1, source_target_pairs={{0,6},{1,7},{2,4},{3,5},{4,2},{5,3},{6,0},{7,1},{8,14},{9,15},{10,... | collective-permute-start | bytes 36872 | tf_op jit(solution)/shard_map/gram/ppermute | solution.py:21
  59.1 0.7 %collective-permute-start.21 = (f32[24,128]{1,0:T(8,128)S(1)}, f32[24,128]{1,0:T(8,128)S(1)}, u32[]{:S(2)}, u32[]{:S(2)}) collective-permute-start(f32[24,128]{1,0:T(8,128)S(1)} %add.53), channel_id=1, source_target_pairs={{0,4},{1,5},{2,6},{3,7},{4,0},{5,1},{6,2},{7,3},{8,12},{9,13},{10,... | collective-permute-start | bytes 36872 | tf_op jit(solution)/shard_map/gram/ppermute | solution.py:21
  59.8 1.6 %collective-permute-start.20 = (f32[24,128]{1,0:T(8,128)S(1)}, f32[24,128]{1,0:T(8,128)S(1)}, u32[]{:S(2)}, u32[]{:S(2)}) collective-permute-start(f32[24,128]{1,0:T(8,128)S(1)} %add.53), channel_id=1, source_target_pairs={{0,2},{1,3},{2,0},{3,1},{4,6},{5,7},{6,4},{7,5},{8,10},{9,11},{10,... | collective-permute-start | bytes 36872 | tf_op jit(solution)/shard_map/gram/ppermute | solution.py:21
  61.4 0.8 %residual.6.refs_1_ = f32[48,2048]{1,0:T(8,128)} custom-call(f32[48,2048]{1,0:T(8,128)S(1)} %get-tuple-element.27.value), custom_call_target="tpu_custom_call" | custom-call | flops 48 | bytes 1 | tf_op jit(solution)/shard_map/residual/pallas_call | solution.py:560
  62.2 0.8 %residual.7.refs_2_ = f32[432,48]{1,0:T(8,128)} custom-call(s32[1,896]{1,0:T(1,128)S(4)} %get-tuple-element.16.plan, f32[12,8,128]{2,1,0:T(8,128)S(1)} %add_add_fusion.mine, f32[12,8,128]{2,1,0:T(8,128)S(1)} %collective-permute-done.18.other), custom_call_target="tpu_custom_call" | custom-call | flops 48 | bytes 1 | tf_op jit(solution)/shard_map/residual/pallas_call | solution.py:569
  63.0 0.0 collective-permute-done.22
  63.0 0.0 collective-permute-done.21
  63.0 0.6 collective-permute-done.20
  63.5 2.4 %collective-permute-start.25 = (f32[24,128]{1,0:T(8,128)S(1)}, f32[24,128]{1,0:T(8,128)S(1)}, u32[]{:S(2)}, u32[]{:S(2)}) collective-permute-start(f32[24,128]{1,0:T(8,128)S(1)} %gram.1), channel_id=1, source_target_pairs={{0,24},{8,16},{16,8},{24,0},{1,25},{9,17},{17,9},{25,1},{2,26},{10... | collective-permute-start | bytes 36872 | tf_op jit(solution)/shard_map/gram/ppermute | solution.py:21
  65.9 0.0 collective-permute-start.24
  65.9 2.0 %collective-permute-start.23 = (f32[24,128]{1,0:T(8,128)S(1)}, f32[24,128]{1,0:T(8,128)S(1)}, u32[]{:S(2)}, u32[]{:S(2)}) collective-permute-start(f32[24,128]{1,0:T(8,128)S(1)} %gram.1), channel_id=1, source_target_pairs={{0,8},{8,0},{16,24},{24,16},{1,9},{9,1},{17,25},{25,17},{2,10},{10... | collective-permute-start | bytes 36872 | tf_op jit(solution)/shard_map/gram/ppermute | solution.py:21
  67.9 1.1 %collective-permute-done.25 = f32[24,128]{1,0:T(8,128)S(1)} collective-permute-done((f32[24,128]{1,0:T(8,128)S(1)}, f32[24,128]{1,0:T(8,128)S(1)}, u32[]{:S(2)}, u32[]{:S(2)}) %collective-permute-start.25) | collective-permute-done | bytes 12320 | tf_op jit(solution)/shard_map/gram/ppermute | solution.py:21
  69.0 1.5 %collective-permute-done.24 = f32[24,128]{1,0:T(8,128)S(1)} collective-permute-done((f32[24,128]{1,0:T(8,128)S(1)}, f32[24,128]{1,0:T(8,128)S(1)}, u32[]{:S(2)}, u32[]{:S(2)}) %collective-permute-start.24) | collective-permute-done | bytes 12320 | tf_op jit(solution)/shard_map/gram/ppermute | solution.py:21
  70.5 0.0 collective-permute-done.23
  70.5 0.1 fusion
  70.6 0.6 pad_maximum_fusion
  (26 shorter events, 0.1 us)
Async XLA Ops:
  1.7 5.4 %collective-permute-start = (bf16[48,2048]{1,0:T(8,128)(2,1)S(1)}, bf16[48,2048]{1,0:T(8,128)(2,1)S(1)}, u32[]{:S(2)}, u32[]{:S(2)}) collective-permute-start(bf16[48,2048]{1,0:T(8,128)(2,1)S(1)} %convert_element_type.9.own_panel), channel_id=1, source_target_pairs={{0,1},{1,0},{2,3},{3,2},{4,5},{5,4},{6,7},{7,6},{8,9},{9,8},{10,11... | collective-permute-start | bytes 589832 | tf_op jit(solution)/shard_map/gather/ppermute | solution.py:21
  2.2 10.5 %collective-permute-start.1 = (bf16[48,2048]{1,0:T(8,128)(2,1)S(1)}, bf16[48,2048]{1,0:T(8,128)(2,1)S(1)}, u32[]{:S(2)}, u32[]{:S(2)}) collective-permute-start(bf16[48,2048]{1,0:T(8,128)(2,1)S(1)} %convert_element_type.9.own_panel), channel_id=1, source_target_pairs={{0,2},{1,3},{2,0},{3,1},{4,6},{5,7},{6,4},{7,5},{8,10},{9,11},{10,... | collective-permute-start | bytes 589832 | tf_op jit(solution)/shard_map/gather/ppermute | solution.py:21
  4.7 11.2 %collective-permute-start.3 = (bf16[48,2048]{1,0:T(8,128)(2,1)S(1)}, bf16[48,2048]{1,0:T(8,128)(2,1)S(1)}, u32[]{:S(2)}, u32[]{:S(2)}) collective-permute-start(bf16[48,2048]{1,0:T(8,128)(2,1)S(1)} %convert_element_type.9.own_panel), channel_id=1, source_target_pairs={{0,4},{1,5},{2,6},{3,7},{4,0},{5,1},{6,2},{7,3},{8,12},{9,13},{10,... | collective-permute-start | bytes 589832 | tf_op jit(solution)/shard_map/gather/ppermute | solution.py:21
  6.3 9.7 %collective-permute-start.5 = (bf16[48,2048]{1,0:T(8,128)(2,1)S(1)}, bf16[48,2048]{1,0:T(8,128)(2,1)S(1)}, u32[]{:S(2)}, u32[]{:S(2)}) collective-permute-start(bf16[48,2048]{1,0:T(8,128)(2,1)S(1)} %convert_element_type.9.own_panel), channel_id=1, source_target_pairs={{0,6},{1,7},{2,4},{3,5},{4,2},{5,3},{6,0},{7,1},{8,14},{9,15},{10,... | collective-permute-start | bytes 589832 | tf_op jit(solution)/shard_map/gather/ppermute | solution.py:21
  12.7 4.5 %collective-permute-start.2 = (bf16[48,2048]{1,0:T(8,128)(2,1)S(1)}, bf16[48,2048]{1,0:T(8,128)(2,1)S(1)}, u32[]{:S(2)}, u32[]{:S(2)}) collective-permute-start(bf16[48,2048]{1,0:T(8,128)(2,1)S(1)} %gather.4.refs_0_), channel_id=1, source_target_pairs={{0,1},{1,0},{2,3},{3,2},{4,5},{5,4},{6,7},{7,6},{8,9},{9,8},{10,11... | collective-permute-start | bytes 589832 | tf_op jit(solution)/shard_map/gather/ppermute | solution.py:21
  15.9 1.4 %collective-permute-start.4 = (bf16[48,2048]{1,0:T(8,128)(2,1)S(1)}, bf16[48,2048]{1,0:T(8,128)(2,1)S(1)}, u32[]{:S(2)}, u32[]{:S(2)}) collective-permute-start(bf16[48,2048]{1,0:T(8,128)(2,1)S(1)} %gather.5.refs_1_), channel_id=1, source_target_pairs={{0,1},{1,0},{2,3},{3,2},{4,5},{5,4},{6,7},{7,6},{8,9},{9,8},{10,11... | collective-permute-start | bytes 589832 | tf_op jit(solution)/shard_map/gather/ppermute | solution.py:21
  15.9 1.7 %collective-permute-start.6 = (bf16[48,2048]{1,0:T(8,128)(2,1)S(1)}, bf16[48,2048]{1,0:T(8,128)(2,1)S(1)}, u32[]{:S(2)}, u32[]{:S(2)}) collective-permute-start(bf16[48,2048]{1,0:T(8,128)(2,1)S(1)} %gather.6.refs_2_), channel_id=1, source_target_pairs={{0,1},{1,0},{2,3},{3,2},{4,5},{5,4},{6,7},{7,6},{8,9},{9,8},{10,11... | collective-permute-start | bytes 589832 | tf_op jit(solution)/shard_map/gather/ppermute | solution.py:21
  20.0 7.8 %collective-permute-start.7 = (bf16[48,2048]{1,0:T(8,128)(2,1)S(1)}, bf16[48,2048]{1,0:T(8,128)(2,1)S(1)}, u32[]{:S(2)}, u32[]{:S(2)}) collective-permute-start(bf16[48,2048]{1,0:T(8,128)(2,1)S(1)} %get-tuple-element.21), channel_id=1, source_target_pairs={{0,8},{24,16},{8,24},{16,0},{1,9},{25,17},{9,25},{17,1},{2,10},{26... | collective-permute-start | bytes 589832 | tf_op jit(solution)/shard_map/late/ppermute | solution.py:495
  20.7 7.2 %copy-start.1 = (f32[48,2048]{1,0:T(8,128)S(1)}, f32[48,2048]{1,0:T(8,128)}, u32[]{:S(2)}) copy-start(f32[48,2048]{1,0:T(8,128)} %current.7) | copy-start | bytes 1179652
  20.7 7.2 %copy-start.2 = (f32[48,2048]{1,0:T(8,128)S(1)}, f32[48,2048]{1,0:T(8,128)}, u32[]{:S(2)}) copy-start(f32[48,2048]{1,0:T(8,128)} %previous.1) | copy-start | bytes 1179652
  20.7 7.2 %copy-start.4 = (f32[48,48]{1,0:T(8,128)S(1)}, f32[48,48]{1,0:T(8,128)}, u32[]{:S(2)}) copy-start(f32[48,48]{1,0:T(8,128)} %coupling.1) | copy-start | bytes 27652
  20.7 7.2 %copy-start.5 = (f32[2048]{0:T(1024)S(1)}, f32[2048]{0:T(1024)}, u32[]{:S(2)}) copy-start(f32[2048]{0:T(1024)} %param.14) | copy-start | bytes 24580
  22.7 9.2 %collective-permute-start.8 = (bf16[48,2048]{1,0:T(8,128)(2,1)S(1)}, bf16[48,2048]{1,0:T(8,128)(2,1)S(1)}, u32[]{:S(2)}, u32[]{:S(2)}) collective-permute-start(bf16[48,2048]{1,0:T(8,128)(2,1)S(1)} %get-tuple-element.22), channel_id=1, source_target_pairs={{0,8},{8,0},{16,24},{24,16},{1,9},{9,1},{17,25},{25,17},{2,10},{10... | collective-permute-start | bytes 589832 | tf_op jit(solution)/shard_map/late/ppermute | solution.py:21
  25.7 11.5 %collective-permute-start.10 = (bf16[48,2048]{1,0:T(8,128)(2,1)S(1)}, bf16[48,2048]{1,0:T(8,128)(2,1)S(1)}, u32[]{:S(2)}, u32[]{:S(2)}) collective-permute-start(bf16[48,2048]{1,0:T(8,128)(2,1)S(1)} %get-tuple-element.24), channel_id=1, source_target_pairs={{0,24},{1,25},{2,26},{3,27},{4,28},{5,29},{6,30},{7,31},{8,9},{9,8... | collective-permute-start | bytes 589832 | tf_op jit(solution)/shard_map/late/ppermute | solution.py:32
  27.8 9.4 %collective-permute-start.9 = (bf16[48,2048]{1,0:T(8,128)(2,1)S(1)}, bf16[48,2048]{1,0:T(8,128)(2,1)S(1)}, u32[]{:S(2)}, u32[]{:S(2)}) collective-permute-start(bf16[48,2048]{1,0:T(8,128)(2,1)S(1)} %add_convert_fusion), channel_id=1, source_target_pairs={{0,1},{1,0},{2,3},{3,2},{4,5},{5,4},{6,7},{7,6},{8,16},{9,17},{10,... | collective-permute-start | bytes 589832 | tf_op jit(solution)/shard_map/late/ppermute | solution.py:32
  27.9 9.3 %copy-start = (f32[8,48,2048]{2,1,0:T(8,128)S(1)}, f32[8,48,2048]{2,1,0:T(8,128)}, u32[]{:S(2)}) copy-start(f32[8,48,2048]{2,1,0:T(8,128)} %param.13) | copy-start | bytes 9437188
  27.9 9.3 %copy-start.3 = (f32[2048]{0:T(1024)S(1)}, f32[2048]{0:T(1024)}, u32[]{:S(2)}) copy-start(f32[2048]{0:T(1024)} %param.15) | copy-start | bytes 24580
  37.9 1.3 %collective-permute-start.11 = (f32[12,8,128]{2,1,0:T(8,128)S(1)}, f32[12,8,128]{2,1,0:T(8,128)S(1)}, u32[]{:S(2)}, u32[]{:S(2)}) collective-permute-start(f32[12,8,128]{2,1,0:T(8,128)S(1)} %get-tuple-element.26), channel_id=1, source_target_pairs={{0,1},{1,0},{2,3},{3,2},{4,5},{5,4},{6,7},{7,6},{8,9},{9,8},{10,11... | collective-permute-start | bytes 147464 | tf_op jit(solution)/shard_map/coefficients/ppermute | solution.py:21
  39.2 5.4 %collective-permute-start.14 = (f32[12,8,128]{2,1,0:T(8,128)S(1)}, f32[12,8,128]{2,1,0:T(8,128)S(1)}, u32[]{:S(2)}, u32[]{:S(2)}) collective-permute-start(f32[12,8,128]{2,1,0:T(8,128)S(1)} %add.46), channel_id=1, source_target_pairs={{0,6},{1,7},{2,4},{3,5},{4,2},{5,3},{6,0},{7,1},{8,14},{9,15},{10,... | collective-permute-start | bytes 147464 | tf_op jit(solution)/shard_map/coefficients/ppermute | solution.py:21
  40.3 4.5 %collective-permute-start.13 = (f32[12,8,128]{2,1,0:T(8,128)S(1)}, f32[12,8,128]{2,1,0:T(8,128)S(1)}, u32[]{:S(2)}, u32[]{:S(2)}) collective-permute-start(f32[12,8,128]{2,1,0:T(8,128)S(1)} %add.46), channel_id=1, source_target_pairs={{0,4},{1,5},{2,6},{3,7},{4,0},{5,1},{6,2},{7,3},{8,12},{9,13},{10,... | collective-permute-start | bytes 147464 | tf_op jit(solution)/shard_map/coefficients/ppermute | solution.py:21
  42.0 4.1 %collective-permute-start.12 = (f32[12,8,128]{2,1,0:T(8,128)S(1)}, f32[12,8,128]{2,1,0:T(8,128)S(1)}, u32[]{:S(2)}, u32[]{:S(2)}) collective-permute-start(f32[12,8,128]{2,1,0:T(8,128)S(1)} %add.46), channel_id=1, source_target_pairs={{0,2},{1,3},{2,0},{3,1},{4,6},{5,7},{6,4},{7,5},{8,10},{9,11},{10,... | collective-permute-start | bytes 147464 | tf_op jit(solution)/shard_map/coefficients/ppermute | solution.py:21
  46.1 6.3 %collective-permute-start.17 = (f32[12,8,128]{2,1,0:T(8,128)S(1)}, f32[12,8,128]{2,1,0:T(8,128)S(1)}, u32[]{:S(2)}, u32[]{:S(2)}) collective-permute-start(f32[12,8,128]{2,1,0:T(8,128)S(1)} %add_add_fusion.1), channel_id=1, source_target_pairs={{0,24},{8,16},{16,8},{24,0},{1,25},{9,17},{17,9},{25,1},{2,26},{10... | collective-permute-start | bytes 147464 | tf_op jit(solution)/shard_map/coefficients/ppermute | solution.py:21
  48.7 5.0 %collective-permute-start.16 = (f32[12,8,128]{2,1,0:T(8,128)S(1)}, f32[12,8,128]{2,1,0:T(8,128)S(1)}, u32[]{:S(2)}, u32[]{:S(2)}) collective-permute-start(f32[12,8,128]{2,1,0:T(8,128)S(1)} %add_add_fusion.1), channel_id=1, source_target_pairs={{0,16},{8,24},{16,0},{24,8},{1,17},{9,25},{17,1},{25,9},{2,18},{10... | collective-permute-start | bytes 147464 | tf_op jit(solution)/shard_map/coefficients/ppermute | solution.py:21
  50.4 4.1 %collective-permute-start.15 = (f32[12,8,128]{2,1,0:T(8,128)S(1)}, f32[12,8,128]{2,1,0:T(8,128)S(1)}, u32[]{:S(2)}, u32[]{:S(2)}) collective-permute-start(f32[12,8,128]{2,1,0:T(8,128)S(1)} %add_add_fusion.1), channel_id=1, source_target_pairs={{0,8},{8,0},{16,24},{24,16},{1,9},{9,1},{17,25},{25,17},{2,10},{10... | collective-permute-start | bytes 147464 | tf_op jit(solution)/shard_map/coefficients/ppermute | solution.py:21
  54.5 1.3 %collective-permute-start.18 = (f32[12,8,128]{2,1,0:T(8,128)S(1)}, f32[12,8,128]{2,1,0:T(8,128)S(1)}, u32[]{:S(2)}, u32[]{:S(2)}) collective-permute-start(f32[12,8,128]{2,1,0:T(8,128)S(1)} %add_add_fusion.mine), channel_id=1, source_target_pairs={{0,1},{1,0},{2,3},{3,2},{4,5},{5,4},{6,7},{7,6},{8,9},{9,8},{10,11... | collective-permute-start | bytes 147464 | tf_op jit(solution)/shard_map/coefficients/ppermute | solution.py:21
  56.7 1.2 %collective-permute-start.19 = (f32[24,128]{1,0:T(8,128)S(1)}, f32[24,128]{1,0:T(8,128)S(1)}, u32[]{:S(2)}, u32[]{:S(2)}) collective-permute-start(f32[24,128]{1,0:T(8,128)S(1)} %get-tuple-element.28), channel_id=1, source_target_pairs={{0,1},{1,0},{2,3},{3,2},{4,5},{5,4},{6,7},{7,6},{8,9},{9,8},{10,11... | collective-permute-start | bytes 36872 | tf_op jit(solution)/shard_map/gram/ppermute | solution.py:21
  57.9 5.1 %collective-permute-start.22 = (f32[24,128]{1,0:T(8,128)S(1)}, f32[24,128]{1,0:T(8,128)S(1)}, u32[]{:S(2)}, u32[]{:S(2)}) collective-permute-start(f32[24,128]{1,0:T(8,128)S(1)} %add.53), channel_id=1, source_target_pairs={{0,6},{1,7},{2,4},{3,5},{4,2},{5,3},{6,0},{7,1},{8,14},{9,15},{10,... | collective-permute-start | bytes 36872 | tf_op jit(solution)/shard_map/gram/ppermute | solution.py:21
  59.1 3.9 %collective-permute-start.21 = (f32[24,128]{1,0:T(8,128)S(1)}, f32[24,128]{1,0:T(8,128)S(1)}, u32[]{:S(2)}, u32[]{:S(2)}) collective-permute-start(f32[24,128]{1,0:T(8,128)S(1)} %add.53), channel_id=1, source_target_pairs={{0,4},{1,5},{2,6},{3,7},{4,0},{5,1},{6,2},{7,3},{8,12},{9,13},{10,... | collective-permute-start | bytes 36872 | tf_op jit(solution)/shard_map/gram/ppermute | solution.py:21
  59.8 3.7 %collective-permute-start.20 = (f32[24,128]{1,0:T(8,128)S(1)}, f32[24,128]{1,0:T(8,128)S(1)}, u32[]{:S(2)}, u32[]{:S(2)}) collective-permute-start(f32[24,128]{1,0:T(8,128)S(1)} %add.53), channel_id=1, source_target_pairs={{0,2},{1,3},{2,0},{3,1},{4,6},{5,7},{6,4},{7,5},{8,10},{9,11},{10,... | collective-permute-start | bytes 36872 | tf_op jit(solution)/shard_map/gram/ppermute | solution.py:21
  63.5 5.5 %collective-permute-start.25 = (f32[24,128]{1,0:T(8,128)S(1)}, f32[24,128]{1,0:T(8,128)S(1)}, u32[]{:S(2)}, u32[]{:S(2)}) collective-permute-start(f32[24,128]{1,0:T(8,128)S(1)} %gram.1), channel_id=1, source_target_pairs={{0,24},{8,16},{16,8},{24,0},{1,25},{9,17},{17,9},{25,1},{2,26},{10... | collective-permute-start | bytes 36872 | tf_op jit(solution)/shard_map/gram/ppermute | solution.py:21
  65.9 4.6 %collective-permute-start.24 = (f32[24,128]{1,0:T(8,128)S(1)}, f32[24,128]{1,0:T(8,128)S(1)}, u32[]{:S(2)}, u32[]{:S(2)}) collective-permute-start(f32[24,128]{1,0:T(8,128)S(1)} %gram.1), channel_id=1, source_target_pairs={{0,16},{8,24},{16,0},{24,8},{1,17},{9,25},{17,1},{25,9},{2,18},{10... | collective-permute-start | bytes 36872 | tf_op jit(solution)/shard_map/gram/ppermute | solution.py:21
  65.9 4.6 %collective-permute-start.23 = (f32[24,128]{1,0:T(8,128)S(1)}, f32[24,128]{1,0:T(8,128)S(1)}, u32[]{:S(2)}, u32[]{:S(2)}) collective-permute-start(f32[24,128]{1,0:T(8,128)S(1)} %gram.1), channel_id=1, source_target_pairs={{0,8},{8,0},{16,24},{24,16},{1,9},{9,1},{17,25},{25,17},{2,10},{10... | collective-permute-start | bytes 36872 | tf_op jit(solution)/shard_map/gram/ppermute | solution.py:21

commit v22 on v18

--- a/solution.py
+++ b/solution.py
@@ -10,7 +10,7 @@
 LANES = 128
 CHUNK = 32
 GROUP = 2
-UNROLL = 8
+UNROLL = 4
 TILE_BIT, SOURCE_BIT, ROW_BIT = 10, 15, 20
 NT = (((1,), (1,)), ((), ()))
 MIB = 1 << 20

time: 70 us -> 71.2 us (1.017)
  Pallas kernels: 16.1 us -> 19.4 us
  waiting for transfers between devices: 24.3 us -> 23.1 us
    ppermute x2, waiting for transfers between devices: 0.01 us -> 6.92 us  [trade_rows(): return lax.ppermute(value, ('row', 'col'), trades)]
    ppermute x1, waiting for transfers between devices: 6.6 us -> 0.43 us  [local(): first = lax.ppermute(first, 'row', [(0, 1), (3, 2), (1, 3), (2, 0)])]
    ppermute x17, waiting for transfers between devices: 12.1 us -> 8.76 us  [swap(): return lax.ppermute(value, axis, [(i, i ^ mask) for i in range(count)])]
    ppermute x2, starting transfers between devices: 2.61 us -> 0.14 us  [trade_rows(): return lax.ppermute(value, ('row', 'col'), trades)]
    pallas_call x1, Pallas kernels: 2 us -> 4.2 us  [local(): pl.pallas_call(functools.partial(late_kernel, masks), out_shape=[part, sl...]
    pallas_call x1, Pallas kernels: 5.39 us -> 6.92 us  [local(): pl.pallas_call(functools.partial(early_kernel, row_devs, col_devs, slab_t...]
    ppermute x1, starting transfers between devices: 1.01 us -> 2.48 us  [local(): first = lax.ppermute(first, 'row', [(0, 1), (3, 2), (1, 3), (2, 0)])]
    ppermute x6, waiting for transfers between devices: 5.59 us -> 6.97 us  [total_by_core(): values[m] = lax.ppermute(value, ('row', 'col'), trades)]
  transfers between devices with their start and end apart: 26 -> 26, of which waited for: 16 -> 20; matrix products, arithmetic and copies ran while one was open for 0% -> 0% of each run, Pallas kernels for 17% -> 23%
where the time goes in v22:
time: 71.2 us; the launch traced here: 71.3 us
  starting transfers between devices  25.4 us (36%)
  waiting for transfers between devices  23.1 us (32%)
  Pallas kernels  19.4 us (27%)
  other arithmetic  1.8 us (3%)
  between operations  1.52 us (2%)
    ppermute x17, starting transfers between devices, swap(): return lax.ppermute(value, axis, [(i, i ^ mask) for i in range(count)])  14.1 us
    ppermute x17, waiting for transfers between devices, swap(): return lax.ppermute(value, axis, [(i, i ^ mask) for i in range(count)])  8.76 us
    ppermute x6, starting transfers between devices, total_by_core(): values[m] = lax.ppermute(value, ('row', 'col'), trades)  8.63 us
    ppermute x6, waiting for transfers between devices, total_by_core(): values[m] = lax.ppermute(value, ('row', 'col'), trades)  6.97 us
    pallas_call x1, Pallas kernels, local(): pl.pallas_call(functools.partial(early_kernel, row_devs, col_devs, slab_t...  6.92 us
    ppermute x2, waiting for transfers between devices, trade_rows(): return lax.ppermute(value, ('row', 'col'), trades)  6.92 us
    pallas_call x1, Pallas kernels, local(): pl.pallas_call(functools.partial(late_kernel, masks), out_shape=[part, sl...  4.2 us
    ppermute x1, starting transfers between devices, local(): first = lax.ppermute(first, 'row', [(0, 1), (3, 2), (1, 3), (2, 0)])  2.48 us
  transfers between devices with their start and end apart: 26, of which 20 were waited for; matrix products, arithmetic and copies ran while one was open for 0% of the time, Pallas kernels for 23%

profile of v22, /device:TPU:0, one launch (start us, length us, event | category | flops | bytes accessed | tf_op | source)
XLA Modules:
  0.0 71.3 jit_solution(948148340428429074)
XLA Ops:
  0.6 1.0 %convert_element_type.9.own_panel = bf16[48,2048]{1,0:T(8,128)(2,1)S(1)} convert(f32[48,2048]{1,0:T(8,128)} %current.7) | non-fusion elementwise | flops 98304 | bytes 589824 | tf_op jit(solution)/shard_map/gather/convert_element_type | solution.py:430
  1.7 0.5 collective-permute-start
  2.2 2.6 %collective-permute-start.1 = (bf16[48,2048]{1,0:T(8,128)(2,1)S(1)}, bf16[48,2048]{1,0:T(8,128)(2,1)S(1)}, u32[]{:S(2)}, u32[]{:S(2)}) collective-permute-start(bf16[48,2048]{1,0:T(8,128)(2,1)S(1)} %convert_element_type.9.own_panel), channel_id=1, source_target_pairs={{0,2},{1,3},{2,0},{3,1},{4,6},{5,7},{6,4},{7,5},{8,10},{9,11},{10,... | collective-permute-start | bytes 589832 | tf_op jit(solution)/shard_map/gather/ppermute | solution.py:21
  4.7 1.5 %collective-permute-start.3 = (bf16[48,2048]{1,0:T(8,128)(2,1)S(1)}, bf16[48,2048]{1,0:T(8,128)(2,1)S(1)}, u32[]{:S(2)}, u32[]{:S(2)}) collective-permute-start(bf16[48,2048]{1,0:T(8,128)(2,1)S(1)} %convert_element_type.9.own_panel), channel_id=1, source_target_pairs={{0,4},{1,5},{2,6},{3,7},{4,0},{5,1},{6,2},{7,3},{8,12},{9,13},{10,... | collective-permute-start | bytes 589832 | tf_op jit(solution)/shard_map/gather/ppermute | solution.py:21
  6.3 0.0 collective-permute-start.5
  6.9 0.1 pad_add_fusion.place
  7.0 6.9 %early.1 = (s32[1,896]{1,0:T(1,128)S(4)}, bf16[512,128,128]{2,1,0:T(8,128)(2,1)S(1)}, f32[65,48,128]{2,1,0:T(8,128)S(1)}, bf16[9,48,2048]{2,1,0:T(8,128)(2,1)S(1)}) custom-call(s32[2]{0:T(128)S(1)} %pad_add_fusion.place, s32[1]{0:T(128)S(6)} %copy.25.counts, s32[1,512]{1,0:T(1,128)} %bitcast.17, s32[1,512]{1,0:T(1,128)} %bitcast.18, ...), custom_call_target="tpu_custom_call" | custom-call | flops 805306368 | bytes 16777216 | tf_op jit(solution)/shard_map/early/pallas_call | solution.py:439
  13.9 0.0 collective-permute-done.1.refs_0_
  14.0 0.1 collective-permute-start.2
  14.0 1.9 %collective-permute-done.3.refs_0_ = bf16[48,2048]{1,0:T(8,128)(2,1)S(1)} collective-permute-done((bf16[48,2048]{1,0:T(8,128)(2,1)S(1)}, bf16[48,2048]{1,0:T(8,128)(2,1)S(1)}, u32[]{:S(2)}, u32[]{:S(2)}) %collective-permute-start.3) | collective-permute-done | bytes 196640 | tf_op jit(solution)/shard_map/gather/ppermute | solution.py:21
  15.9 0.0 collective-permute-done.5.refs_0_
  15.9 0.5 collective-permute-start.6
  16.4 0.8 %gather.7.refs_5_ = bf16[9,48,2048]{2,1,0:T(8,128)(2,1)S(1)} custom-call(bf16[48,2048]{1,0:T(8,128)(2,1)S(1)} %gather.4.refs_0_, bf16[48,2048]{1,0:T(8,128)(2,1)S(1)} %gather.5.refs_1_, bf16[48,2048]{1,0:T(8,128)(2,1)S(1)} %gather.6.refs_2_, bf16[9,48,2048]{2,1,0:T(8,128)(2,1)S(1)} %get-tuple-element.19.refs_3_), custom_call_target="tpu_custom_call", output_to_operand_aliasing={{}: (3, {})} | custom-call | flops 48 | bytes 1 | tf_op jit(solution)/shard_map/gather/pallas_call | solution.py:474
  17.2 0.2 collective-permute-done.4.refs_1_
  17.4 0.3 collective-permute-done.6.refs_2_
  17.6 1.7 %late.3 = (bf16[48,2048]{1,0:T(8,128)(2,1)S(1)}, bf16[9,48,2048]{2,1,0:T(8,128)(2,1)S(1)}) custom-call(s32[1,896]{1,0:T(1,128)S(4)} %get-tuple-element.16.plan, bf16[48,2048]{1,0:T(8,128)(2,1)S(1)} %collective-permute-done.2.refs_0_, bf16[48,2048]{1,0:T(8,128)(2,1)S(1)} %collective-permute-done.4.refs_1_, ...), custom_call_target="tpu_custom_call", output_to_operand_aliasing={{1}: (6, {})} | custom-call | flops 48 | bytes 1 | tf_op jit(solution)/shard_map/late/pallas_call | solution.py:490
  19.3 2.5 %collective-permute-start.7 = (bf16[48,2048]{1,0:T(8,128)(2,1)S(1)}, bf16[48,2048]{1,0:T(8,128)(2,1)S(1)}, u32[]{:S(2)}, u32[]{:S(2)}) collective-permute-start(bf16[48,2048]{1,0:T(8,128)(2,1)S(1)} %get-tuple-element.21), channel_id=1, source_target_pairs={{0,8},{24,16},{8,24},{16,0},{1,9},{25,17},{9,25},{17,1},{2,10},{26... | collective-permute-start | bytes 589832 | tf_op jit(solution)/shard_map/late/ppermute | solution.py:510
  21.8 4.2 %late.5 = (bf16[48,2048]{1,0:T(8,128)(2,1)S(1)}, f32[48,2048]{1,0:T(8,128)S(1)}, bf16[48,2048]{1,0:T(8,128)(2,1)S(1)}) custom-call(s32[1,896]{1,0:T(1,128)S(4)} %get-tuple-element.16.plan, bf16[9,48,2048]{2,1,0:T(8,128)(2,1)S(1)} %get-tuple-element.20.panel_buf, bf16[512,128,128]{2,1,0:T(8,128)(2,1)S(1)} %get-tuple-element.18.refs_3_.tiles, ...), custom_call_target="tpu_custom_call" | custom-call | flops 48 | bytes 1 | tf_op jit(solution)/shard_map/late/pallas_call | solution.py:500
  26.0 0.1 collective-permute-start.8
  26.1 0.7 %collective-permute-start.10 = (bf16[48,2048]{1,0:T(8,128)(2,1)S(1)}, bf16[48,2048]{1,0:T(8,128)(2,1)S(1)}, u32[]{:S(2)}, u32[]{:S(2)}) collective-permute-start(bf16[48,2048]{1,0:T(8,128)(2,1)S(1)} %get-tuple-element.24), channel_id=1, source_target_pairs={{0,8},{8,0},{16,24},{24,16},{1,9},{9,1},{17,25},{25,17},{2,10},{10... | collective-permute-start | bytes 589832 | tf_op jit(solution)/shard_map/late/ppermute | solution.py:21
  26.9 0.4 collective-permute-done.7.refs_0_
  27.3 0.1 collective-permute-start.9
  27.4 0.0 copy-start
  27.5 0.0 copy-start.3
  27.5 1.4 %late.4.base = f32[48,2048]{1,0:T(8,128)S(1)} custom-call(s32[1,896]{1,0:T(1,128)S(4)} %get-tuple-element.16.plan, bf16[9,48,2048]{2,1,0:T(8,128)(2,1)S(1)} %get-tuple-element.20.panel_buf, bf16[512,128,128]{2,1,0:T(8,128)(2,1)S(1)} %get-tuple-element.18.refs_3_.tiles, f32[65,48,128]{2,1,0:T(8,128)S(1)} %get-tuple-element.17.refs_1_.refs_4_.early, ...), custom_call_target="tpu_custom_call" | custom-call | flops 48 | bytes 1 | tf_op jit(solution)/shard_map/late/pallas_call | solution.py:521
  28.8 6.9 %collective-permute-done.8.refs_1_ = bf16[48,2048]{1,0:T(8,128)(2,1)S(1)} collective-permute-done((bf16[48,2048]{1,0:T(8,128)(2,1)S(1)}, bf16[48,2048]{1,0:T(8,128)(2,1)S(1)}, u32[]{:S(2)}, u32[]{:S(2)}) %collective-permute-start.8) | collective-permute-done | bytes 196640 | tf_op jit(solution)/shard_map/late/ppermute | solution.py:32
  35.7 1.3 %collective-permute-done.10.refs_3_ = bf16[48,2048]{1,0:T(8,128)(2,1)S(1)} collective-permute-done((bf16[48,2048]{1,0:T(8,128)(2,1)S(1)}, bf16[48,2048]{1,0:T(8,128)(2,1)S(1)}, u32[]{:S(2)}, u32[]{:S(2)}) %collective-permute-start.10) | collective-permute-done | bytes 196640 | tf_op jit(solution)/shard_map/late/ppermute | solution.py:21
  37.0 0.7 coefficients.2
  37.7 0.1 collective-permute-start.11
  37.8 0.7 coefficients.3
  38.5 0.5 collective-permute-done.11
  39.0 2.3 %collective-permute-start.14 = (f32[12,8,128]{2,1,0:T(8,128)S(1)}, f32[12,8,128]{2,1,0:T(8,128)S(1)}, u32[]{:S(2)}, u32[]{:S(2)}) collective-permute-start(f32[12,8,128]{2,1,0:T(8,128)S(1)} %add.46), channel_id=1, source_target_pairs={{0,6},{1,25},{2,4},{3,27},{4,2},{5,29},{6,0},{7,31},{8,14},{9,17},... | collective-permute-start | bytes 147464 | tf_op jit(solution)/shard_map/coefficients/ppermute | solution.py:59
  41.4 0.5 collective-permute-start.13
  41.8 1.4 %collective-permute-start.12 = (f32[12,8,128]{2,1,0:T(8,128)S(1)}, f32[12,8,128]{2,1,0:T(8,128)S(1)}, u32[]{:S(2)}, u32[]{:S(2)}) collective-permute-start(f32[12,8,128]{2,1,0:T(8,128)S(1)} %add.46), channel_id=1, source_target_pairs={{0,2},{1,9},{2,0},{3,11},{4,6},{5,13},{6,4},{7,15},{8,10},{9,1},{1... | collective-permute-start | bytes 147464 | tf_op jit(solution)/shard_map/coefficients/ppermute | solution.py:59
  43.2 0.9 %collective-permute-done.14 = f32[12,8,128]{2,1,0:T(8,128)S(1)} collective-permute-done((f32[12,8,128]{2,1,0:T(8,128)S(1)}, f32[12,8,128]{2,1,0:T(8,128)S(1)}, u32[]{:S(2)}, u32[]{:S(2)}) %collective-permute-start.14) | collective-permute-done | bytes 49184 | tf_op jit(solution)/shard_map/coefficients/ppermute | solution.py:59
  44.1 1.4 %collective-permute-done.13 = f32[12,8,128]{2,1,0:T(8,128)S(1)} collective-permute-done((f32[12,8,128]{2,1,0:T(8,128)S(1)}, f32[12,8,128]{2,1,0:T(8,128)S(1)}, u32[]{:S(2)}, u32[]{:S(2)}) %collective-permute-start.13) | collective-permute-done | bytes 49184 | tf_op jit(solution)/shard_map/coefficients/ppermute | solution.py:59
  45.4 0.5 collective-permute-done.12
  45.9 3.2 %collective-permute-start.17 = (f32[12,8,128]{2,1,0:T(8,128)S(1)}, f32[12,8,128]{2,1,0:T(8,128)S(1)}, u32[]{:S(2)}, u32[]{:S(2)}) collective-permute-start(f32[12,8,128]{2,1,0:T(8,128)S(1)} %add_add_fusion.1), channel_id=1, source_target_pairs={{0,24},{1,7},{2,26},{3,5},{4,28},{5,3},{6,30},{7,1},{8,16},{9,15},... | collective-permute-start | bytes 147464 | tf_op jit(solution)/shard_map/coefficients/ppermute | solution.py:59
  49.1 0.9 %collective-permute-start.16 = (f32[12,8,128]{2,1,0:T(8,128)S(1)}, f32[12,8,128]{2,1,0:T(8,128)S(1)}, u32[]{:S(2)}, u32[]{:S(2)}) collective-permute-start(f32[12,8,128]{2,1,0:T(8,128)S(1)} %add_add_fusion.1), channel_id=1, source_target_pairs={{0,16},{1,5},{2,18},{3,7},{4,20},{5,1},{6,22},{7,3},{8,24},{9,13},... | collective-permute-start | bytes 147464 | tf_op jit(solution)/shard_map/coefficients/ppermute | solution.py:59
  50.0 0.3 collective-permute-start.15
  50.4 1.5 %collective-permute-done.17 = f32[12,8,128]{2,1,0:T(8,128)S(1)} collective-permute-done((f32[12,8,128]{2,1,0:T(8,128)S(1)}, f32[12,8,128]{2,1,0:T(8,128)S(1)}, u32[]{:S(2)}, u32[]{:S(2)}) %collective-permute-start.17) | collective-permute-done | bytes 49184 | tf_op jit(solution)/shard_map/coefficients/ppermute | solution.py:59
  51.9 2.3 %collective-permute-done.16 = f32[12,8,128]{2,1,0:T(8,128)S(1)} collective-permute-done((f32[12,8,128]{2,1,0:T(8,128)S(1)}, f32[12,8,128]{2,1,0:T(8,128)S(1)}, u32[]{:S(2)}, u32[]{:S(2)}) %collective-permute-start.16) | collective-permute-done | bytes 49184 | tf_op jit(solution)/shard_map/coefficients/ppermute | solution.py:59
  54.2 0.5 collective-permute-done.15
  54.7 0.1 collective-permute-start.18
  54.7 0.6 residual.4.less
  55.3 0.6 collective-permute-done.18.other
  56.0 0.9 %residual.5 = (f32[48,2048]{1,0:T(8,128)S(1)}, f32[24,128]{1,0:T(8,128)S(1)}) custom-call(s32[1,896]{1,0:T(1,128)S(4)} %get-tuple-element.16.plan, f32[12,8,128]{2,1,0:T(8,128)S(1)} %collective-permute-done.18.other, f32[48,2048]{1,0:T(8,128)S(1)} %residual.4.less, f32[1,2048]{1,0:T(1,128)S(1)} %bitcast.14, f32[48,2048]{1,0:T(8,128)S(1)} %copy-done.1, ...), custom_call_target="tpu_custom_call" | custom-call | flops 48 | bytes 1 | tf_op jit(solution)/shard_map/residual/pallas_call | solution.py:564
  56.9 0.2 collective-permute-start.19
  57.1 1.0 %collective-permute-done.19 = f32[24,128]{1,0:T(8,128)S(1)} collective-permute-done((f32[24,128]{1,0:T(8,128)S(1)}, f32[24,128]{1,0:T(8,128)S(1)}, u32[]{:S(2)}, u32[]{:S(2)}) %collective-permute-start.19) | collective-permute-done | bytes 12320 | tf_op jit(solution)/shard_map/gram/ppermute | solution.py:21
  58.1 1.6 %collective-permute-start.22 = (f32[24,128]{1,0:T(8,128)S(1)}, f32[24,128]{1,0:T(8,128)S(1)}, u32[]{:S(2)}, u32[]{:S(2)}) collective-permute-start(f32[24,128]{1,0:T(8,128)S(1)} %add.53), channel_id=1, source_target_pairs={{0,6},{1,7},{2,4},{3,5},{4,2},{5,3},{6,0},{7,1},{8,14},{9,15},{10,... | collective-permute-start | bytes 36872 | tf_op jit(solution)/shard_map/gram/ppermute | solution.py:21
  59.7 1.1 %collective-permute-start.21 = (f32[24,128]{1,0:T(8,128)S(1)}, f32[24,128]{1,0:T(8,128)S(1)}, u32[]{:S(2)}, u32[]{:S(2)}) collective-permute-start(f32[24,128]{1,0:T(8,128)S(1)} %add.53), channel_id=1, source_target_pairs={{0,4},{1,5},{2,6},{3,7},{4,0},{5,1},{6,2},{7,3},{8,12},{9,13},{10,... | collective-permute-start | bytes 36872 | tf_op jit(solution)/shard_map/gram/ppermute | solution.py:21
  60.8 0.8 %collective-permute-start.20 = (f32[24,128]{1,0:T(8,128)S(1)}, f32[24,128]{1,0:T(8,128)S(1)}, u32[]{:S(2)}, u32[]{:S(2)}) collective-permute-start(f32[24,128]{1,0:T(8,128)S(1)} %add.53), channel_id=1, source_target_pairs={{0,2},{1,3},{2,0},{3,1},{4,6},{5,7},{6,4},{7,5},{8,10},{9,11},{10,... | collective-permute-start | bytes 36872 | tf_op jit(solution)/shard_map/gram/ppermute | solution.py:21
  61.6 0.8 %residual.6.refs_1_ = f32[48,2048]{1,0:T(8,128)} custom-call(f32[48,2048]{1,0:T(8,128)S(1)} %get-tuple-element.27.value), custom_call_target="tpu_custom_call" | custom-call | flops 48 | bytes 1 | tf_op jit(solution)/shard_map/residual/pallas_call | solution.py:575
  62.3 0.8 %residual.7.refs_2_ = f32[432,48]{1,0:T(8,128)} custom-call(s32[1,896]{1,0:T(1,128)S(4)} %get-tuple-element.16.plan, f32[12,8,128]{2,1,0:T(8,128)S(1)} %add_add_fusion.mine, f32[12,8,128]{2,1,0:T(8,128)S(1)} %collective-permute-done.18.other), custom_call_target="tpu_custom_call" | custom-call | flops 48 | bytes 1 | tf_op jit(solution)/shard_map/residual/pallas_call | solution.py:584
  63.2 0.3 collective-permute-done.21
  63.4 1.1 %collective-permute-done.20 = f32[24,128]{1,0:T(8,128)S(1)} collective-permute-done((f32[24,128]{1,0:T(8,128)S(1)}, f32[24,128]{1,0:T(8,128)S(1)}, u32[]{:S(2)}, u32[]{:S(2)}) %collective-permute-start.20) | collective-permute-done | bytes 12320 | tf_op jit(solution)/shard_map/gram/ppermute | solution.py:21
  64.5 1.4 %collective-permute-start.25 = (f32[24,128]{1,0:T(8,128)S(1)}, f32[24,128]{1,0:T(8,128)S(1)}, u32[]{:S(2)}, u32[]{:S(2)}) collective-permute-start(f32[24,128]{1,0:T(8,128)S(1)} %gram.1), channel_id=1, source_target_pairs={{0,24},{8,16},{16,8},{24,0},{1,25},{9,17},{17,9},{25,1},{2,26},{10... | collective-permute-start | bytes 36872 | tf_op jit(solution)/shard_map/gram/ppermute | solution.py:21
  65.9 0.3 collective-permute-start.24
  66.1 2.7 %collective-permute-start.23 = (f32[24,128]{1,0:T(8,128)S(1)}, f32[24,128]{1,0:T(8,128)S(1)}, u32[]{:S(2)}, u32[]{:S(2)}) collective-permute-start(f32[24,128]{1,0:T(8,128)S(1)} %gram.1), channel_id=1, source_target_pairs={{0,8},{8,0},{16,24},{24,16},{1,9},{9,1},{17,25},{25,17},{2,10},{10... | collective-permute-start | bytes 36872 | tf_op jit(solution)/shard_map/gram/ppermute | solution.py:21
  68.9 1.1 %collective-permute-done.25 = f32[24,128]{1,0:T(8,128)S(1)} collective-permute-done((f32[24,128]{1,0:T(8,128)S(1)}, f32[24,128]{1,0:T(8,128)S(1)}, u32[]{:S(2)}, u32[]{:S(2)}) %collective-permute-start.25) | collective-permute-done | bytes 12320 | tf_op jit(solution)/shard_map/gram/ppermute | solution.py:21
  70.0 0.5 collective-permute-done.24
  70.5 0.1 collective-permute-done.23
  70.6 0.1 fusion
  70.7 0.6 pad_maximum_fusion
  (26 shorter events, 0.1 us)
Async XLA Ops:
  1.7 5.4 %collective-permute-start = (bf16[48,2048]{1,0:T(8,128)(2,1)S(1)}, bf16[48,2048]{1,0:T(8,128)(2,1)S(1)}, u32[]{:S(2)}, u32[]{:S(2)}) collective-permute-start(bf16[48,2048]{1,0:T(8,128)(2,1)S(1)} %convert_element_type.9.own_panel), channel_id=1, source_target_pairs={{0,1},{1,0},{2,3},{3,2},{4,5},{5,4},{6,7},{7,6},{8,9},{9,8},{10,11... | collective-permute-start | bytes 589832 | tf_op jit(solution)/shard_map/gather/ppermute | solution.py:21
  2.2 11.8 %collective-permute-start.1 = (bf16[48,2048]{1,0:T(8,128)(2,1)S(1)}, bf16[48,2048]{1,0:T(8,128)(2,1)S(1)}, u32[]{:S(2)}, u32[]{:S(2)}) collective-permute-start(bf16[48,2048]{1,0:T(8,128)(2,1)S(1)} %convert_element_type.9.own_panel), channel_id=1, source_target_pairs={{0,2},{1,3},{2,0},{3,1},{4,6},{5,7},{6,4},{7,5},{8,10},{9,11},{10,... | collective-permute-start | bytes 589832 | tf_op jit(solution)/shard_map/gather/ppermute | solution.py:21
  4.7 11.2 %collective-permute-start.3 = (bf16[48,2048]{1,0:T(8,128)(2,1)S(1)}, bf16[48,2048]{1,0:T(8,128)(2,1)S(1)}, u32[]{:S(2)}, u32[]{:S(2)}) collective-permute-start(bf16[48,2048]{1,0:T(8,128)(2,1)S(1)} %convert_element_type.9.own_panel), channel_id=1, source_target_pairs={{0,4},{1,5},{2,6},{3,7},{4,0},{5,1},{6,2},{7,3},{8,12},{9,13},{10,... | collective-permute-start | bytes 589832 | tf_op jit(solution)/shard_map/gather/ppermute | solution.py:21
  6.3 9.7 %collective-permute-start.5 = (bf16[48,2048]{1,0:T(8,128)(2,1)S(1)}, bf16[48,2048]{1,0:T(8,128)(2,1)S(1)}, u32[]{:S(2)}, u32[]{:S(2)}) collective-permute-start(bf16[48,2048]{1,0:T(8,128)(2,1)S(1)} %convert_element_type.9.own_panel), channel_id=1, source_target_pairs={{0,6},{1,7},{2,4},{3,5},{4,2},{5,3},{6,0},{7,1},{8,14},{9,15},{10,... | collective-permute-start | bytes 589832 | tf_op jit(solution)/shard_map/gather/ppermute | solution.py:21
  14.0 3.2 %collective-permute-start.2 = (bf16[48,2048]{1,0:T(8,128)(2,1)S(1)}, bf16[48,2048]{1,0:T(8,128)(2,1)S(1)}, u32[]{:S(2)}, u32[]{:S(2)}) collective-permute-start(bf16[48,2048]{1,0:T(8,128)(2,1)S(1)} %gather.4.refs_0_), channel_id=1, source_target_pairs={{0,1},{1,0},{2,3},{3,2},{4,5},{5,4},{6,7},{7,6},{8,9},{9,8},{10,11... | collective-permute-start | bytes 589832 | tf_op jit(solution)/shard_map/gather/ppermute | solution.py:21
  15.9 1.4 %collective-permute-start.4 = (bf16[48,2048]{1,0:T(8,128)(2,1)S(1)}, bf16[48,2048]{1,0:T(8,128)(2,1)S(1)}, u32[]{:S(2)}, u32[]{:S(2)}) collective-permute-start(bf16[48,2048]{1,0:T(8,128)(2,1)S(1)} %gather.5.refs_1_), channel_id=1, source_target_pairs={{0,1},{1,0},{2,3},{3,2},{4,5},{5,4},{6,7},{7,6},{8,9},{9,8},{10,11... | collective-permute-start | bytes 589832 | tf_op jit(solution)/shard_map/gather/ppermute | solution.py:21
  15.9 1.7 %collective-permute-start.6 = (bf16[48,2048]{1,0:T(8,128)(2,1)S(1)}, bf16[48,2048]{1,0:T(8,128)(2,1)S(1)}, u32[]{:S(2)}, u32[]{:S(2)}) collective-permute-start(bf16[48,2048]{1,0:T(8,128)(2,1)S(1)} %gather.6.refs_2_), channel_id=1, source_target_pairs={{0,1},{1,0},{2,3},{3,2},{4,5},{5,4},{6,7},{7,6},{8,9},{9,8},{10,11... | collective-permute-start | bytes 589832 | tf_op jit(solution)/shard_map/gather/ppermute | solution.py:21
  19.3 7.9 %collective-permute-start.7 = (bf16[48,2048]{1,0:T(8,128)(2,1)S(1)}, bf16[48,2048]{1,0:T(8,128)(2,1)S(1)}, u32[]{:S(2)}, u32[]{:S(2)}) collective-permute-start(bf16[48,2048]{1,0:T(8,128)(2,1)S(1)} %get-tuple-element.21), channel_id=1, source_target_pairs={{0,8},{24,16},{8,24},{16,0},{1,9},{25,17},{9,25},{17,1},{2,10},{26... | collective-permute-start | bytes 589832 | tf_op jit(solution)/shard_map/late/ppermute | solution.py:510
  21.8 5.6 %copy-start.1 = (f32[48,2048]{1,0:T(8,128)S(1)}, f32[48,2048]{1,0:T(8,128)}, u32[]{:S(2)}) copy-start(f32[48,2048]{1,0:T(8,128)} %current.7) | copy-start | bytes 1179652
  21.8 5.6 %copy-start.2 = (f32[48,2048]{1,0:T(8,128)S(1)}, f32[48,2048]{1,0:T(8,128)}, u32[]{:S(2)}) copy-start(f32[48,2048]{1,0:T(8,128)} %previous.1) | copy-start | bytes 1179652
  21.8 5.6 %copy-start.4 = (f32[48,48]{1,0:T(8,128)S(1)}, f32[48,48]{1,0:T(8,128)}, u32[]{:S(2)}) copy-start(f32[48,48]{1,0:T(8,128)} %coupling.1) | copy-start | bytes 27652
  21.8 5.6 %copy-start.5 = (f32[2048]{0:T(1024)S(1)}, f32[2048]{0:T(1024)}, u32[]{:S(2)}) copy-start(f32[2048]{0:T(1024)} %param.14) | copy-start | bytes 24580
  26.0 9.7 %collective-permute-start.8 = (bf16[48,2048]{1,0:T(8,128)(2,1)S(1)}, bf16[48,2048]{1,0:T(8,128)(2,1)S(1)}, u32[]{:S(2)}, u32[]{:S(2)}) collective-permute-start(bf16[48,2048]{1,0:T(8,128)(2,1)S(1)} %get-tuple-element.22), channel_id=1, source_target_pairs={{0,24},{1,25},{2,26},{3,27},{4,28},{5,29},{6,30},{7,31},{8,9},{9,8... | collective-permute-start | bytes 589832 | tf_op jit(solution)/shard_map/late/ppermute | solution.py:32
  26.1 10.9 %collective-permute-start.10 = (bf16[48,2048]{1,0:T(8,128)(2,1)S(1)}, bf16[48,2048]{1,0:T(8,128)(2,1)S(1)}, u32[]{:S(2)}, u32[]{:S(2)}) collective-permute-start(bf16[48,2048]{1,0:T(8,128)(2,1)S(1)} %get-tuple-element.24), channel_id=1, source_target_pairs={{0,8},{8,0},{16,24},{24,16},{1,9},{9,1},{17,25},{25,17},{2,10},{10... | collective-permute-start | bytes 589832 | tf_op jit(solution)/shard_map/late/ppermute | solution.py:21
  27.3 9.7 %collective-permute-start.9 = (bf16[48,2048]{1,0:T(8,128)(2,1)S(1)}, bf16[48,2048]{1,0:T(8,128)(2,1)S(1)}, u32[]{:S(2)}, u32[]{:S(2)}) collective-permute-start(bf16[48,2048]{1,0:T(8,128)(2,1)S(1)} %add_convert_fusion), channel_id=1, source_target_pairs={{0,1},{1,0},{2,3},{3,2},{4,5},{5,4},{6,7},{7,6},{8,16},{9,17},{10,... | collective-permute-start | bytes 589832 | tf_op jit(solution)/shard_map/late/ppermute | solution.py:32
  27.4 9.6 %copy-start = (f32[8,48,2048]{2,1,0:T(8,128)S(1)}, f32[8,48,2048]{2,1,0:T(8,128)}, u32[]{:S(2)}) copy-start(f32[8,48,2048]{2,1,0:T(8,128)} %param.13) | copy-start | bytes 9437188
  27.5 9.6 %copy-start.3 = (f32[2048]{0:T(1024)S(1)}, f32[2048]{0:T(1024)}, u32[]{:S(2)}) copy-start(f32[2048]{0:T(1024)} %param.15) | copy-start | bytes 24580
  37.7 1.3 %collective-permute-start.11 = (f32[12,8,128]{2,1,0:T(8,128)S(1)}, f32[12,8,128]{2,1,0:T(8,128)S(1)}, u32[]{:S(2)}, u32[]{:S(2)}) collective-permute-start(f32[12,8,128]{2,1,0:T(8,128)S(1)} %get-tuple-element.26), channel_id=1, source_target_pairs={{0,1},{1,0},{2,3},{3,2},{4,5},{5,4},{6,7},{7,6},{8,9},{9,8},{10,11... | collective-permute-start | bytes 147464 | tf_op jit(solution)/shard_map/coefficients/ppermute | solution.py:21
  39.0 5.0 %collective-permute-start.14 = (f32[12,8,128]{2,1,0:T(8,128)S(1)}, f32[12,8,128]{2,1,0:T(8,128)S(1)}, u32[]{:S(2)}, u32[]{:S(2)}) collective-permute-start(f32[12,8,128]{2,1,0:T(8,128)S(1)} %add.46), channel_id=1, source_target_pairs={{0,6},{1,25},{2,4},{3,27},{4,2},{5,29},{6,0},{7,31},{8,14},{9,17},... | collective-permute-start | bytes 147464 | tf_op jit(solution)/shard_map/coefficients/ppermute | solution.py:59
  41.4 4.1 %collective-permute-start.13 = (f32[12,8,128]{2,1,0:T(8,128)S(1)}, f32[12,8,128]{2,1,0:T(8,128)S(1)}, u32[]{:S(2)}, u32[]{:S(2)}) collective-permute-start(f32[12,8,128]{2,1,0:T(8,128)S(1)} %add.46), channel_id=1, source_target_pairs={{0,4},{1,17},{2,6},{3,19},{4,0},{5,21},{6,2},{7,23},{8,12},{9,25},... | collective-permute-start | bytes 147464 | tf_op jit(solution)/shard_map/coefficients/ppermute | solution.py:59
  41.8 4.1 %collective-permute-start.12 = (f32[12,8,128]{2,1,0:T(8,128)S(1)}, f32[12,8,128]{2,1,0:T(8,128)S(1)}, u32[]{:S(2)}, u32[]{:S(2)}) collective-permute-start(f32[12,8,128]{2,1,0:T(8,128)S(1)} %add.46), channel_id=1, source_target_pairs={{0,2},{1,9},{2,0},{3,11},{4,6},{5,13},{6,4},{7,15},{8,10},{9,1},{1... | collective-permute-start | bytes 147464 | tf_op jit(solution)/shard_map/coefficients/ppermute | solution.py:59
  45.9 6.0 %collective-permute-start.17 = (f32[12,8,128]{2,1,0:T(8,128)S(1)}, f32[12,8,128]{2,1,0:T(8,128)S(1)}, u32[]{:S(2)}, u32[]{:S(2)}) collective-permute-start(f32[12,8,128]{2,1,0:T(8,128)S(1)} %add_add_fusion.1), channel_id=1, source_target_pairs={{0,24},{1,7},{2,26},{3,5},{4,28},{5,3},{6,30},{7,1},{8,16},{9,15},... | collective-permute-start | bytes 147464 | tf_op jit(solution)/shard_map/coefficients/ppermute | solution.py:59
  49.1 5.0 %collective-permute-start.16 = (f32[12,8,128]{2,1,0:T(8,128)S(1)}, f32[12,8,128]{2,1,0:T(8,128)S(1)}, u32[]{:S(2)}, u32[]{:S(2)}) collective-permute-start(f32[12,8,128]{2,1,0:T(8,128)S(1)} %add_add_fusion.1), channel_id=1, source_target_pairs={{0,16},{1,5},{2,18},{3,7},{4,20},{5,1},{6,22},{7,3},{8,24},{9,13},... | collective-permute-start | bytes 147464 | tf_op jit(solution)/shard_map/coefficients/ppermute | solution.py:59
  50.0 4.6 %collective-permute-start.15 = (f32[12,8,128]{2,1,0:T(8,128)S(1)}, f32[12,8,128]{2,1,0:T(8,128)S(1)}, u32[]{:S(2)}, u32[]{:S(2)}) collective-permute-start(f32[12,8,128]{2,1,0:T(8,128)S(1)} %add_add_fusion.1), channel_id=1, source_target_pairs={{0,8},{1,3},{2,10},{3,1},{4,12},{5,7},{6,14},{7,5},{8,0},{9,11},{1... | collective-permute-start | bytes 147464 | tf_op jit(solution)/shard_map/coefficients/ppermute | solution.py:59
  54.7 1.3 %collective-permute-start.18 = (f32[12,8,128]{2,1,0:T(8,128)S(1)}, f32[12,8,128]{2,1,0:T(8,128)S(1)}, u32[]{:S(2)}, u32[]{:S(2)}) collective-permute-start(f32[12,8,128]{2,1,0:T(8,128)S(1)} %add_add_fusion.mine), channel_id=1, source_target_pairs={{0,1},{1,0},{2,3},{3,2},{4,5},{5,4},{6,7},{7,6},{8,9},{9,8},{10,11... | collective-permute-start | bytes 147464 | tf_op jit(solution)/shard_map/coefficients/ppermute | solution.py:21
  56.9 1.2 %collective-permute-start.19 = (f32[24,128]{1,0:T(8,128)S(1)}, f32[24,128]{1,0:T(8,128)S(1)}, u32[]{:S(2)}, u32[]{:S(2)}) collective-permute-start(f32[24,128]{1,0:T(8,128)S(1)} %get-tuple-element.28), channel_id=1, source_target_pairs={{0,1},{1,0},{2,3},{3,2},{4,5},{5,4},{6,7},{7,6},{8,9},{9,8},{10,11... | collective-permute-start | bytes 36872 | tf_op jit(solution)/shard_map/gram/ppermute | solution.py:21
  58.1 5.1 %collective-permute-start.22 = (f32[24,128]{1,0:T(8,128)S(1)}, f32[24,128]{1,0:T(8,128)S(1)}, u32[]{:S(2)}, u32[]{:S(2)}) collective-permute-start(f32[24,128]{1,0:T(8,128)S(1)} %add.53), channel_id=1, source_target_pairs={{0,6},{1,7},{2,4},{3,5},{4,2},{5,3},{6,0},{7,1},{8,14},{9,15},{10,... | collective-permute-start | bytes 36872 | tf_op jit(solution)/shard_map/gram/ppermute | solution.py:21
  59.7 3.7 %collective-permute-start.21 = (f32[24,128]{1,0:T(8,128)S(1)}, f32[24,128]{1,0:T(8,128)S(1)}, u32[]{:S(2)}, u32[]{:S(2)}) collective-permute-start(f32[24,128]{1,0:T(8,128)S(1)} %add.53), channel_id=1, source_target_pairs={{0,4},{1,5},{2,6},{3,7},{4,0},{5,1},{6,2},{7,3},{8,12},{9,13},{10,... | collective-permute-start | bytes 36872 | tf_op jit(solution)/shard_map/gram/ppermute | solution.py:21
  60.8 3.7 %collective-permute-start.20 = (f32[24,128]{1,0:T(8,128)S(1)}, f32[24,128]{1,0:T(8,128)S(1)}, u32[]{:S(2)}, u32[]{:S(2)}) collective-permute-start(f32[24,128]{1,0:T(8,128)S(1)} %add.53), channel_id=1, source_target_pairs={{0,2},{1,3},{2,0},{3,1},{4,6},{5,7},{6,4},{7,5},{8,10},{9,11},{10,... | collective-permute-start | bytes 36872 | tf_op jit(solution)/shard_map/gram/ppermute | solution.py:21
  64.5 5.5 %collective-permute-start.25 = (f32[24,128]{1,0:T(8,128)S(1)}, f32[24,128]{1,0:T(8,128)S(1)}, u32[]{:S(2)}, u32[]{:S(2)}) collective-permute-start(f32[24,128]{1,0:T(8,128)S(1)} %gram.1), channel_id=1, source_target_pairs={{0,24},{8,16},{16,8},{24,0},{1,25},{9,17},{17,9},{25,1},{2,26},{10... | collective-permute-start | bytes 36872 | tf_op jit(solution)/shard_map/gram/ppermute | solution.py:21
  65.9 4.6 %collective-permute-start.24 = (f32[24,128]{1,0:T(8,128)S(1)}, f32[24,128]{1,0:T(8,128)S(1)}, u32[]{:S(2)}, u32[]{:S(2)}) collective-permute-start(f32[24,128]{1,0:T(8,128)S(1)} %gram.1), channel_id=1, source_target_pairs={{0,16},{8,24},{16,0},{24,8},{1,17},{9,25},{17,1},{25,9},{2,18},{10... | collective-permute-start | bytes 36872 | tf_op jit(solution)/shard_map/gram/ppermute | solution.py:21
  66.1 4.4 %collective-permute-start.23 = (f32[24,128]{1,0:T(8,128)S(1)}, f32[24,128]{1,0:T(8,128)S(1)}, u32[]{:S(2)}, u32[]{:S(2)}) collective-permute-start(f32[24,128]{1,0:T(8,128)S(1)} %gram.1), channel_id=1, source_target_pairs={{0,8},{8,0},{16,24},{24,16},{1,9},{9,1},{17,25},{25,17},{2,10},{10... | collective-permute-start | bytes 36872 | tf_op jit(solution)/shard_map/gram/ppermute | solution.py:21
